TPU v7x, 32 devices: a whole 2x2x4 slice. The times are simulated.
32 devices in a mesh: grp: 2 (over x), dex: 16 (over z, y, core).
Axes of the slice: x: 2, y: 2, z: 4, core: 2. Of those that a mesh axis runs over, the one named last changes fastest.
Arguments:
- resident_state: float32 [512, 16, 16384], P('grp', None, 'dex'), parts along dimension 0, may hold values from -6 to 6
- resident_conv: float32 [512, 3, 16384], P('grp', None, 'dex'), parts along dimension 0, may hold values from -6 to 6
- prefilled_state: float32 [128, 16, 16384], P(('grp', 'dex')), parts along dimension 0, may hold values from -6 to 6
- prefilled_conv: float32 [128, 3, 16384], P(('grp', 'dex')), parts along dimension 0, may hold values from -6 to 6
- live_counts: int32 [32], P('grp'), parts along dimension 0, may hold values from 1 to 4, 32 in all
- batch_rows: int32 [128], P('grp'), parts along dimension 0, may hold values from 0 to 255, as said below
- step_x: bfloat16 [4, 512, 16384], P(None, 'grp', 'dex'), parts along dimension 1, may hold values from -6 to 6
- step_z: bfloat16 [4, 512, 16384], P(None, 'grp', 'dex'), parts along dimension 1, may hold values from -6 to 6
- conv_weight: float32 [4, 16384], P(None, 'dex'), may hold values from -3 to 3
- conv_bias: float32 [16384], P('dex'), may hold values from -0.5 to 0.5
- x_proj: bfloat16 [16384, 544], P('dex'), may hold values from -0.046875 to 0.046875
- norm_gain: float32 [544], replicated, may hold values from 0.1 to 1.9
- dt_proj: bfloat16 [512, 16384], P(None, 'dex'), may hold values from -0.25 to 0.25
- dt_bias: float32 [16384], P('dex'), may hold values from -4 to 0
- a_log: float32 [16, 16384], P(None, 'dex'), may hold values from 0 to 2.8
- d_skip: float32 [16384], P('dex'), may hold values from 0.5 to 1.5
- out_weight: bfloat16 [16384, 8192], P('dex'), may hold values from -0.046875 to 0.046875
Outputs:
- mixed: bfloat16 [512, 4, 8192], P(('grp', 'dex')), parts along dimension 0
There are 2 independent parts, one for each index of `grp`. A program takes and returns all parts, laid end to end along the dimension named above; an argument that names none is the same for every part. Nothing has to cross between parts.
Inputs may be any that keep to these rules, and one draw needn't show every extreme that they name: `live_counts`: each device's live prefilled requests fill its first slots; the counts add up to 4 * 16 / 2. `batch_rows`: all entries are distinct.
All inputs are finite; a program needn't handle non-finite values.
Results may differ from a plain program's by a relative error of at most 0.025.
Values may be sent and summed in bfloat16 or wider, within the bound.
No kernel may reach another device: no remote copies, remote signals or barrier semaphores. Data moves between devices by JAX's collectives and lax.ppermute only.
A program may use at most 256 MiB of HBM per device.

v0:
```python
import jax
import jax.numpy as jnp
from jax import lax
from jax.sharding import PartitionSpec as P

STATE = 16
DT_RANK = 512
STEPS = 4


RMS_EPS = 1e-06
BC_FLOOR = 0.2


def normalize(projected, norm_gain):
    dt_part = projected[:, :DT_RANK]
    dt_low = (
        dt_part
        * lax.rsqrt(jnp.mean(dt_part * dt_part, axis=1, keepdims=True) + RMS_EPS)
        * norm_gain[:DT_RANK]
    )
    b_part = projected[:, DT_RANK : DT_RANK + STATE]
    c_part = projected[:, DT_RANK + STATE :]
    b_coef = (
        b_part
        * lax.rsqrt(jnp.maximum(jnp.mean(b_part * b_part, axis=1, keepdims=True), BC_FLOOR))
        * norm_gain[DT_RANK : DT_RANK + STATE]
    )
    c_coef = (
        c_part
        * lax.rsqrt(jnp.maximum(jnp.mean(c_part * c_part, axis=1, keepdims=True), BC_FLOOR))
        * norm_gain[DT_RANK + STATE :]
    )
    return (dt_low, b_coef, c_coef)


def shards(
    resident_state,
    resident_conv,
    prefilled_state,
    prefilled_conv,
    live_counts,
    batch_rows,
    step_x,
    step_z,
    conv_weight,
    conv_bias,
    x_proj,
    norm_gain,
    dt_proj,
    dt_bias,
    a_log,
    d_skip,
    out_weight,
):
    moved_state, moved_conv = (
        lax.all_to_all(
            prefilled_state.astype(jnp.bfloat16), "dex", split_axis=2, concat_axis=0, tiled=True
        ).astype(prefilled_state.dtype),
        lax.all_to_all(
            prefilled_conv.astype(jnp.bfloat16), "dex", split_axis=2, concat_axis=0, tiled=True
        ).astype(prefilled_conv.dtype),
    )
    slots = prefilled_state.shape[0]
    is_live = (jnp.arange(slots, dtype=jnp.int32)[None, :] < live_counts[:, None]).reshape(-1)
    batch_size = resident_state.shape[0]
    target = jnp.where(is_live, batch_rows, batch_size)
    ssm_state = resident_state.at[target].set(moved_state, mode="drop")
    window = resident_conv.at[target].set(moved_conv, mode="drop")
    decay_rate = -jnp.exp(a_log)
    own_rows = batch_size // lax.axis_size("dex")
    outputs = []
    for step_index in range(STEPS):
        stacked = jnp.concatenate(
            [window, step_x[step_index].astype(jnp.float32)[:, None, :]], axis=1
        )
        conv_out = jax.nn.silu(jnp.sum(stacked * conv_weight[None], axis=1) + conv_bias)
        window = stacked[:, 1:, :]
        conv_low = conv_out.astype(jnp.bfloat16)
        partial_value = jnp.dot(conv_low, x_proj, preferred_element_type=jnp.float32)
        projected = lax.psum(partial_value.astype(jnp.bfloat16), "dex").astype(jnp.float32)
        dt_low, b_coef, c_coef = normalize(projected, norm_gain)
        step_size = jax.nn.softplus(
            jnp.dot(dt_low.astype(jnp.bfloat16), dt_proj, preferred_element_type=jnp.float32)
            + dt_bias
        )
        ssm_state = (
            jnp.exp(step_size[:, None, :] * decay_rate[None]) * ssm_state
            + (step_size * conv_out)[:, None, :] * b_coef[:, :, None]
        )
        gated = (
            (jnp.sum(ssm_state * c_coef[:, :, None], axis=1) + d_skip * conv_out)
            * jax.nn.silu(step_z[step_index].astype(jnp.float32))
        ).astype(jnp.bfloat16)

        def term_rows(first_row, row_count, source=gated):
            return jnp.dot(source, out_weight, preferred_element_type=jnp.float32)

        outputs.append(
            lax.psum_scatter(
                term_rows(jnp.int32(0), lax.axis_size("dex") * own_rows).astype(jnp.bfloat16),
                "dex",
                scatter_dimension=0,
                tiled=True,
            ).astype(jnp.float32)
        )
    mixed = jnp.stack(outputs, axis=1)
    return mixed.astype(jnp.bfloat16)


def solution(mesh):
    placed = (
        P("grp", None, "dex"),
        P("grp", None, "dex"),
        P(("grp", "dex"), None, None),
        P(("grp", "dex"), None, None),
        P("grp"),
        P("grp"),
        P(None, "grp", "dex"),
        P(None, "grp", "dex"),
        P(None, "dex"),
        P("dex"),
        P("dex", None),
        P(),
        P(None, "dex"),
        P("dex"),
        P(None, "dex"),
        P("dex"),
        P("dex", None),
    )
    return jax.shard_map(
        shards, mesh=mesh, in_specs=placed, out_specs=P(("grp", "dex"), None, None), check_vma=False
    )
```

profile of v0, /device:TPU:0, one launch (start us, length us, event | category | flops | bytes accessed | tf_op | source)
XLA Modules:
  0.0 725.9 jit_solution(11494329778212351606)
XLA Ops:
  6.5 4.1 copy.62
  10.6 11.8 %copy.61 = f32[256,16,1024]{2,1,0:T(8,128)} copy(f32[256,16,1024]{2,1,0:T(8,128)} %param.17) | data formatting | bytes 33554432
  22.6 16.2 %copy.40 = bf16[4,3,16384]{0,1,2:T(4,128)(2,1)} copy(bf16[4,3,16384]{2,0,1:T(4,128)(2,1)S(1)} %convert_element_type.183) | data formatting | bytes 786432 | tf_op jit(solution)/shard_map/convert_element_type | solution.py:61
  38.8 19.1 %reshape.219 = bf16[16,2,6144]{2,1,0:T(2,128)(2,1)} reshape(bf16[16384,3,4]{2,1,0:T(4,128)(2,1)} %bitcast.70) | data formatting | bytes 786432
  57.9 7.4 %all-to-all-start = ((bf16[16,2,6144]{2,1,0:T(2,128)(2,1)}), bf16[16,2,6144]{2,1,0:T(2,128)(2,1)}, u32[]{:S(2)}, u32[]{:S(2)}) async-start(bf16[16,2,6144]{2,1,0:T(2,128)(2,1)} %reshape.219), calls=%async_computation | async-start | bytes 786432 | tf_op jit(solution)/shard_map/all_to_all | solution.py:60
  65.6 3.3 bitcast_convert_fusion
  68.9 8.7 %all-to-all-done = bf16[16,2,6144]{2,1,0:T(2,128)(2,1)} async-done(((bf16[16,2,6144]{2,1,0:T(2,128)(2,1)}), bf16[16,2,6144]{2,1,0:T(2,128)(2,1)}, u32[]{:S(2)}, u32[]{:S(2)}) %all-to-all-start) | async-done | bytes 393248 | tf_op jit(solution)/shard_map/all_to_all | solution.py:60
  77.6 17.2 %reshape.220 = bf16[16384,3,4]{2,1,0:T(4,128)(2,1)} reshape(bf16[16,2,6144]{2,1,0:T(2,128)(2,1)} %all-to-all-done) | data formatting | bytes 786432
  94.9 15.9 %convert_bitcast_fusion.1 = f32[16,4,3,1024]{1,2,3,0:T(4,128)} fusion(bf16[4,3,16,1024]{0,1,3,2:T(4,128)(2,1)} %bitcast.67), kind=kLoop, calls=%fused_computation.3 | loop fusion | flops 196608 | bytes 1179648 | tf_op jit(solution)/shard_map/convert_element_type | solution.py:62
  110.8 26.3 %copy.41 = f32[16,4,3,1024]{3,1,0,2:T(4,128)} copy(f32[16,4,3,1024]{1,2,3,0:T(4,128)} %convert_bitcast_fusion.1) | data formatting | bytes 1572864 | tf_op jit(solution)/shard_map/convert_element_type | solution.py:62
  137.1 2.3 reshape.205
  139.4 15.2 %scatter_fusion = f32[256,3,1024]{2,0,1:T(8,128)} fusion(f32[256,3,1024]{2,0,1:T(8,128)} %copy.62, s32[64]{0:T(128)S(1)} %compare_select_fusion.4, f32[64,3,1024]{2,0,1:T(8,128)} %reshape.205), kind=kCustom, calls=%fused_computation | custom fusion | bytes 2359552 | tf_op jit(solution)/shard_map/scatter | solution.py:69
  154.6 1.8 fusion.9
  156.8 0.8 copy-done.3
  158.1 0.7 copy-done.2
  159.0 2.8 fusion.5
  161.9 1.8 convolution_convert_fusion.4
  163.7 1.3 convolution_convert_fusion.5
  165.1 1.3 convolution_convert_fusion.6
  166.4 1.3 convolution_convert_fusion.7
  167.7 2.4 convert_element_type.194
  170.1 15.8 %copy.42 = bf16[4,16,16384]{1,0,2:T(4,128)(2,1)} copy(bf16[4,16,16384]{2,1,0:T(8,128)(2,1)S(1)} %convert_element_type.194) | data formatting | bytes 4194304 | tf_op jit(solution)/shard_map/convert_element_type | solution.py:58
  185.9 20.8 %reshape.221 = bf16[16,2,32768]{2,1,0:T(2,128)(2,1)} reshape(bf16[16384,4,16]{2,1,0:T(4,128)(2,1)} %bitcast.69) | data formatting | bytes 4194304
  206.8 3.9 all-to-all-start.1
  211.7 0.6 exponential_negate_fusion
  212.3 67.2 %all-reduce.3.cloned.1.call-done = (bf16[256,544]{0,1:T(8,128)(2,1)}, bf16[256,544]{0,1:T(8,128)(2,1)}, bf16[256,544]{0,1:T(8,128)(2,1)}, bf16[256,544]{0,1:T(8,128)(2,1)}) async-done(((bf16[256,544]{0,1:T(8,128)(2,1)}, bf16[256,544]{0,1:T(8,128)(2,1)}, bf16[256,544]{0,1:T(8,128)(2,1)}, bf16[256,544]{0,1:T(8,128)(2,1)}), (bf16[256,544]{0,1:T(8,128)(2,1)}, bf16[256,544]{0,1:T(8,128)(2,1)}, ...) | async-done | bytes 1114128 | tf_op jit(solution)/shard_map/psum | solution.py:81
  279.5 1.0 convert_element_type.192
  280.5 1.2 convert_element_type.207
  281.7 1.2 convert_element_type.217
  282.9 1.0 convert_element_type.227
  284.1 0.7 multiply_multiply_fusion.3
  284.8 0.8 copy.45
  285.7 1.5 copy.46
  287.1 0.7 copy.47
  287.9 0.8 copy.48
  288.6 0.7 copy.49
  289.4 0.8 copy.50
  290.1 0.7 copy.51
  290.9 1.2 multiply_reduce_fusion.7
  292.1 1.1 multiply_reduce_fusion.6
  293.5 2.4 compare_select_fusion.3
  296.0 1.0 compare_select_fusion.2
  297.0 1.0 compare_select_fusion.1
  298.1 1.0 copy-done.45
  299.1 3.6 fusion.69
  302.7 14.3 %reshape.222 = bf16[16384,4,16]{2,1,0:T(4,128)(2,1)} reshape(bf16[16,2,32768]{2,1,0:T(2,128)(2,1)S(1)} %all-to-all-done.1) | data formatting | bytes 4194304
  316.9 15.9 %convert_bitcast_fusion = f32[16,4,16,1024]{2,1,3,0:T(4,128)} fusion(bf16[4,16,16,1024]{1,0,3,2:T(4,128)(2,1)} %bitcast.68), kind=kLoop, calls=%fused_computation.2 | loop fusion | flops 1048576 | bytes 6291456 | tf_op jit(solution)/shard_map/convert_element_type | solution.py:59
  332.8 27.7 %copy.43 = f32[16,4,16,1024]{3,2,1,0:T(8,128)} copy(f32[16,4,16,1024]{2,1,3,0:T(4,128)} %convert_bitcast_fusion) | data formatting | bytes 8388608 | tf_op jit(solution)/shard_map/convert_element_type | solution.py:59
  360.6 12.3 %scatter_fusion.1 = f32[256,16,1024]{2,1,0:T(8,128)} fusion(f32[256,16,1024]{2,1,0:T(8,128)} %copy.61, s32[64]{0:T(128)S(1)} %copy-done.32, f32[64,16,1024]{2,1,0:T(8,128)} %bitcast.71), kind=kCustom, calls=%fused_computation.1 | custom fusion | bytes 12583168 | tf_op jit(solution)/shard_map/scatter | solution.py:68
  373.0 30.9 %multiply_reduce_fusion.1 = (f32[256,1024]{1,0:T(8,128)}, f32[256,1024]{1,0:T(8,128)}, f32[256,1024]{1,0:T(8,128)}, f32[256,1024]{1,0:T(8,128)}) fusion(f32[256,16]{1,0:T(8,128)S(1)} %copy-done.24, f32[256,16]{1,0:T(8,128)S(1)} %copy-done.23, f32[256,1024]{1,0:T(8,128)} %get-tuple-element.38, f32[256,1024]{1,0:T(8,128)} %copy-done.45, ...), kind=kLoop, calls=%fused_computation.5 | loop fusion | flops 99614720 | bytes 29556736 | tf_op jit(solution)/shard_map/reduce_sum | solution.py:92
  403.9 13.0 %convolution_convert_fusion.3 = bf16[256,8192]{1,0:T(8,128)(2,1)} fusion(bf16[1024,8192]{1,0:T(8,128)(2,1)} %param.33, f32[256,1024]{1,0:T(8,128)} %get-tuple-element.8, bf16[4,256,1024]{2,1,0:T(8,128)(2,1)} %param.24, f32[1024]{0:T(1024)S(1)} %copy-done.40, f32[256,1024]{1,0:T(8,128)S(1)} %copy-done.19, f32[1024]{0:T(1024)S(1)} %copy-done.39), kind=kOutput, calls=%fused_computation.14 | convolution fusion | flops 4300734464 | bytes 23601152 | tf_op jit(solution)/shard_map/dot_general | solution.py:97
  417.0 1.1 copy-done.16
  418.1 0.7 copy-done.35
  418.8 13.3 %convolution_convert_fusion.2 = bf16[256,8192]{1,0:T(8,128)(2,1)} fusion(bf16[1024,8192]{1,0:T(8,128)(2,1)} %param.33, f32[256,1024]{1,0:T(8,128)} %get-tuple-element.7, bf16[4,256,1024]{2,1,0:T(8,128)(2,1)S(1)} %copy-done.35, f32[1024]{0:T(1024)S(1)} %copy-done.40, f32[256,1024]{1,0:T(8,128)S(1)} %copy-done.16, f32[1024]{0:T(1024)S(1)} %copy-done.39), kind=kOutput, calls=%fused_computation.13 | convolution fusion | flops 4300734464 | bytes 23601152 | tf_op jit(solution)/shard_map/dot_general | solution.py:97
  432.4 1.0 copy-done.13
  433.4 13.4 %convolution_convert_fusion.1 = bf16[256,8192]{1,0:T(8,128)(2,1)} fusion(bf16[1024,8192]{1,0:T(8,128)(2,1)} %param.33, f32[256,1024]{1,0:T(8,128)} %get-tuple-element.5, bf16[4,256,1024]{2,1,0:T(8,128)(2,1)S(1)} %copy-done.35, f32[1024]{0:T(1024)S(1)} %copy-done.40, f32[256,1024]{1,0:T(8,128)S(1)} %copy-done.13, f32[1024]{0:T(1024)S(1)} %copy-done.39), kind=kOutput, calls=%fused_computation.12 | convolution fusion | flops 4300734464 | bytes 23601152 | tf_op jit(solution)/shard_map/dot_general | solution.py:97
  446.9 1.2 copy-done.10
  448.1 12.9 %convolution_convert_fusion = bf16[256,8192]{1,0:T(8,128)(2,1)} fusion(bf16[1024,8192]{1,0:T(8,128)(2,1)} %param.33, f32[256,1024]{1,0:T(8,128)} %get-tuple-element.6, bf16[4,256,1024]{2,1,0:T(8,128)(2,1)S(1)} %copy-done.35, f32[1024]{0:T(1024)S(1)} %copy-done.40, f32[256,1024]{1,0:T(8,128)S(1)} %copy-done.10, f32[1024]{0:T(1024)S(1)} %copy-done.39), kind=kOutput, calls=%fused_computation.11 | convolution fusion | flops 4300734464 | bytes 23601152 | tf_op jit(solution)/shard_map/dot_general | solution.py:97
  461.0 28.4 %reduce-scatter.5.cloned.1.call-done = bf16[16,8192]{1,0:T(8,128)(2,1)} async-done(((bf16[256,8192]{1,0:T(8,128)(2,1)}), bf16[16,8192]{1,0:T(8,128)(2,1)}) %reduce-scatter.5.cloned.1.call-update) | async-done | bytes 262160 | tf_op jit(solution)/shard_map/reduce_scatter | solution.py:100
  489.4 75.8 %reduce-scatter.7.cloned.1.call-done = bf16[16,8192]{1,0:T(8,128)(2,1)} async-done(((bf16[256,8192]{1,0:T(8,128)(2,1)}), bf16[16,8192]{1,0:T(8,128)(2,1)}) %reduce-scatter.7.cloned.1.call-update) | async-done | bytes 262160 | tf_op jit(solution)/shard_map/reduce_scatter | solution.py:100
  565.2 75.2 %reduce-scatter.9.cloned.1.call-done = bf16[16,8192]{1,0:T(8,128)(2,1)} async-done(((bf16[256,8192]{1,0:T(8,128)(2,1)}), bf16[16,8192]{1,0:T(8,128)(2,1)}) %reduce-scatter.9.cloned.1.call-update) | async-done | bytes 262160 | tf_op jit(solution)/shard_map/reduce_scatter | solution.py:100
  640.4 75.7 %reduce-scatter.11.cloned.1.call-done = bf16[16,8192]{1,0:T(8,128)(2,1)} async-done(((bf16[256,8192]{1,0:T(8,128)(2,1)}), bf16[16,8192]{1,0:T(8,128)(2,1)}) %reduce-scatter.11.cloned.1.call-update) | async-done | bytes 262160 | tf_op jit(solution)/shard_map/reduce_scatter | solution.py:100
  716.1 1.3 pad_maximum_fusion.3
  717.4 1.8 copy.52
  (119 shorter events, 3.4 us)
Async XLA Ops:
  6.5 155.4 %copy-start = (bf16[1024,544]{0,1:T(8,128)(2,1)S(1)}, bf16[1024,544]{0,1:T(8,128)(2,1)}, u32[]{:S(2)}) copy-start(bf16[1024,544]{0,1:T(8,128)(2,1)} %param.27) | copy-start | bytes 3342340
  10.6 11.8 %copy-start.20 = (f32[4,3,16384]{2,0,1:T(4,128)S(1)}, f32[4,3,16384]{2,0,1:T(4,128)}, u32[]{:S(2)}) copy-start(f32[4,3,16384]{2,0,1:T(4,128)} %param.20) | copy-start | bytes 2359300
  38.8 26.6 %copy-start.34 = (s32[16]{0:T(128)S(1)}, s32[16]{0:T(128)}, u32[]{:S(2)}) copy-start(s32[16]{0:T(128)} %param.21) | copy-start | bytes 196
  38.8 26.8 %copy-start.41 = (s32[64]{0:T(128)S(1)}, s32[64]{0:T(128)}, u32[]{:S(2)}) copy-start(s32[64]{0:T(128)} %param.22) | copy-start | bytes 772
  57.9 19.7 %all-to-all-start = ((bf16[16,2,6144]{2,1,0:T(2,128)(2,1)}), bf16[16,2,6144]{2,1,0:T(2,128)(2,1)}, u32[]{:S(2)}, u32[]{:S(2)}) async-start(bf16[16,2,6144]{2,1,0:T(2,128)(2,1)} %reshape.219), calls=%async_computation | async-start | bytes 786432 | tf_op jit(solution)/shard_map/all_to_all | solution.py:60
  65.4 214.1 %all-reduce.3.cloned.1.call-start = ((), (), s32[]{:S(2)}) async-start(), calls=%async_computation.10 | async-start | bytes 2228224 | tf_op jit(solution)/shard_map/psum | solution.py:81
  65.6 73.7 %copy-start.31 = (s32[64]{0:T(128)}, s32[64]{0:T(128)S(1)}, u32[]{:S(2)}) copy-start(s32[64]{0:T(128)S(1)} %compare_select_fusion.4) | copy-start | bytes 772
  156.4 1.2 copy-start.3
  156.8 2.0 copy-start.2
  156.8 2.2 copy-start.4
  156.8 2.2 copy-start.29
  159.0 2.9 copy-start.38
  161.9 3.2 copy-start.8
  161.9 3.2 copy-start.11
  161.9 3.2 copy-start.14
  161.9 4.5 copy-start.17
  206.8 4.3 copy-start.30
  206.8 4.9 copy-start.27
  206.8 95.9 %all-to-all-start.1 = ((bf16[16,2,32768]{2,1,0:T(2,128)(2,1)}), bf16[16,2,32768]{2,1,0:T(2,128)(2,1)S(1)}, u32[]{:S(2)}, u32[]{:S(2)}) async-start(bf16[16,2,32768]{2,1,0:T(2,128)(2,1)} %reshape.221), calls=%async_computation.1 | async-start | bytes 4194304 | tf_op jit(solution)/shard_map/all_to_all | solution.py:57
  210.6 278.7 %reduce-scatter.5.cloned.1.call-start = ((), (), s32[]{:S(2)}) async-start(), calls=%async_computation.6 | async-start | bytes 4456448 | tf_op jit(solution)/shard_map/reduce_scatter | solution.py:100
  280.5 4.2 copy-start.7
  281.7 2.4 copy-start.5
  287.9 8.0 %copy-start.33 = (f32[512]{0:T(512)S(1)}, f32[512]{0:T(512)}, u32[]{:S(2)}) copy-start(f32[512]{0:T(512)} %slice.89) | copy-start | bytes 6148
  287.9 8.0 %copy-start.37 = (f32[1024]{0:T(1024)S(1)}, f32[1024]{0:T(1024)}, u32[]{:S(2)}) copy-start(f32[1024]{0:T(1024)} %param.30) | copy-start | bytes 12292
  290.9 5.0 copy-start.6
  290.9 5.0 copy-start.36
  295.9 2.1 copy-start.42
  295.9 3.2 copy-start.9
  295.9 3.2 copy-start.12
  295.9 3.2 copy-start.15
  296.0 3.1 copy-start.18
  296.0 3.1 copy-start.39
  297.0 1.0 copy-start.44
  298.0 1.0 copy-start.45
  332.8 27.7 %copy-start.32 = (s32[64]{0:T(128)S(1)}, s32[64]{0:T(128)}, u32[]{:S(2)}) copy-start(s32[64]{0:T(128)} %copy-done.31) | copy-start | bytes 772
  360.5 12.4 %copy-start.21 = (f32[256,16]{1,0:T(8,128)S(1)}, f32[256,16]{1,0:T(8,128)}, u32[]{:S(2)}) copy-start(f32[256,16]{1,0:T(8,128)} %copy.46) | copy-start | bytes 49156
  360.5 12.4 %copy-start.22 = (f32[256,16]{1,0:T(8,128)S(1)}, f32[256,16]{1,0:T(8,128)}, u32[]{:S(2)}) copy-start(f32[256,16]{1,0:T(8,128)} %copy.47) | copy-start | bytes 49156
  360.5 12.4 %copy-start.23 = (f32[256,16]{1,0:T(8,128)S(1)}, f32[256,16]{1,0:T(8,128)}, u32[]{:S(2)}) copy-start(f32[256,16]{1,0:T(8,128)} %copy.48) | copy-start | bytes 49156
  360.5 12.4 %copy-start.24 = (f32[256,16]{1,0:T(8,128)S(1)}, f32[256,16]{1,0:T(8,128)}, u32[]{:S(2)}) copy-start(f32[256,16]{1,0:T(8,128)} %copy.49) | copy-start | bytes 49156
  360.5 12.4 %copy-start.25 = (f32[256,16]{1,0:T(8,128)S(1)}, f32[256,16]{1,0:T(8,128)}, u32[]{:S(2)}) copy-start(f32[256,16]{1,0:T(8,128)} %copy.50) | copy-start | bytes 49156
  360.5 12.4 %copy-start.26 = (f32[256,16]{1,0:T(8,128)S(1)}, f32[256,16]{1,0:T(8,128)}, u32[]{:S(2)}) copy-start(f32[256,16]{1,0:T(8,128)} %copy.51) | copy-start | bytes 49156
  360.5 12.4 %copy-start.28 = (f32[16,1024]{1,0:T(8,128)S(1)}, f32[16,1024]{1,0:T(8,128)}, u32[]{:S(2)}) copy-start(f32[16,1024]{1,0:T(8,128)} %exponential_negate_fusion) | copy-start | bytes 196612
  360.6 12.4 %copy-start.43 = (f32[256,1024]{1,0:T(8,128)S(1)}, f32[256,1024]{1,0:T(8,128)}, u32[]{:S(2)}) copy-start(f32[256,1024]{1,0:T(8,128)} %copy-done.42) | copy-start | bytes 3145732
  373.0 30.9 %copy-start.19 = (f32[256,1024]{1,0:T(8,128)S(1)}, f32[256,1024]{1,0:T(8,128)}, u32[]{:S(2)}) copy-start(f32[256,1024]{1,0:T(8,128)} %copy-done.17) | copy-start | bytes 3145732
  373.0 30.9 %copy-start.40 = (f32[1024]{0:T(1024)S(1)}, f32[1024]{0:T(1024)}, u32[]{:S(2)}) copy-start(f32[1024]{0:T(1024)} %param.32) | copy-start | bytes 12292
  416.9 1.2 copy-start.16
  416.9 1.9 copy-start.35
  416.9 148.3 %reduce-scatter.7.cloned.1.call-start = ((), (), s32[]{:S(2)}) async-start(), calls=%async_computation.7 | async-start | bytes 4456448 | tf_op jit(solution)/shard_map/reduce_scatter | solution.py:100
  432.1 1.3 copy-start.13
  432.2 208.2 %reduce-scatter.9.cloned.1.call-start = ((), (), s32[]{:S(2)}) async-start(), calls=%async_computation.8 | async-start | bytes 4456448 | tf_op jit(solution)/shard_map/reduce_scatter | solution.py:100
  446.8 1.2 copy-start.10
  446.8 269.2 %reduce-scatter.11.cloned.1.call-start = ((), (), s32[]{:S(2)}) async-start(), calls=%async_computation.9 | async-start | bytes 4456448 | tf_op jit(solution)/shard_map/reduce_scatter | solution.py:100
  461.0 258.2 %copy-start.1 = (bf16[1024,544]{0,1:T(8,128)(2,1)S(1)}, bf16[1024,544]{0,1:T(8,128)(2,1)}, u32[]{:S(2)}) copy-start(bf16[1024,544]{0,1:T(8,128)(2,1)} %param.27) | copy-start | bytes 3342340
Sparse Core Ops, SparseCore 0:
  167.8 111.6 all-reduce.2
  417.1 72.2 reduce-scatter.4
  493.7 71.4 reduce-scatter.6
  568.9 71.4 reduce-scatter.8
  644.6 71.4 reduce-scatter.10
where the time goes:
time: 738 us; the launch traced here: 726 us
  waiting for transfers between devices  331 us (45%)
  local copies, waits for them, and re-layouts  219 us (30%)
  other arithmetic  83.6 us (11%)
  matrix products  66.4 us (9%)
  between operations  13.9 us (2%)
  starting transfers between devices  12 us (2%)
    reduce_scatter x4, waiting for transfers between devices, shards(): lax.psum_scatter(term_rows(jnp.int32(0), lax.axis_size('dex') * own_rows)...  255 us
    unnamed x98, local copies, waits for them, and re-layouts  94.4 us
    psum x1, waiting for transfers between devices, shards(): lax.psum(partial_value.astype(jnp.bfloat16), 'dex').astype(jnp.float32)  67.2 us
    convert_element_type x3, local copies, waits for them, and re-layouts, shards(): moved_state, moved_conv = (lax.all_to_all(prefilled_state.astype(jnp.bflo...  56.3 us
    dot_general x4, matrix products, term_rows(): return jnp.dot(source, out_weight, preferred_element_type=jnp.float32)  52.6 us
    convert_element_type x2, other arithmetic, shards(): moved_state, moved_conv = (lax.all_to_all(prefilled_state.astype(jnp.bflo...  31.8 us
    reduce_sum x1, other arithmetic, shards(): jnp.sum(ssm_state * c_coef[:, :, None], axis=1) + d_skip * conv_out  30.9 us
    convert_element_type x1, local copies, waits for them, and re-layouts, shards(): prefilled_conv.astype(jnp.bfloat16)  16.2 us
  transfers between devices with their start and end apart: 7, of which 6 were waited for; matrix products, arithmetic and copies ran while one was open for 14% of the time, Pallas kernels for 0%

commit v1 on v0

v1 whole, which is shorter than its diff:
```python
import functools

import jax
import jax.numpy as jnp
from jax import lax
from jax.experimental import pallas as pl
from jax.experimental.pallas import tpu as pltpu
from jax.sharding import PartitionSpec as P

STATE = 16
DT_RANK = 512
STEPS = 4
TAPS = 3
WIDE = DT_RANK + 128

RMS_EPS = 1e-06
BC_FLOOR = 0.2
LOG2E = 1.4426950408889634

BF16 = jnp.bfloat16
F32 = jnp.float32
VMEM_LIMIT = 56 * 1024 * 1024


def params(**kw):
    return pltpu.CompilerParams(vmem_limit_bytes=VMEM_LIMIT, **kw)


def swap(x, mask, n):
    return lax.ppermute(x, "dex", [(i, i ^ mask) for i in range(n)])


def sigmoid(x):
    return 1.0 / (1.0 + jnp.exp(-x))


def whole(shape):
    zeros = (0,) * len(shape)
    return pl.BlockSpec(shape, lambda *_: zeros)


def pack_conv_kernel(x_ref, o_ref):
    slots = x_ref.shape[1]
    for p in range(TAPS):
        o_ref[0, slots * p : slots * (p + 1), :] = x_ref[p].astype(BF16)
    o_ref[0, slots * TAPS :, :] = jnp.zeros_like(o_ref[0, slots * TAPS :, :])


def pack_conv(prefilled_conv, n):
    slots, _, inner = prefilled_conv.shape
    c = inner // n
    return pl.pallas_call(
        pack_conv_kernel,
        grid=(n,),
        in_specs=[pl.BlockSpec((TAPS, slots, c), lambda d: (0, 0, d))],
        out_specs=pl.BlockSpec((1, 4 * slots, c), lambda d: (d, 0, 0)),
        out_shape=jax.ShapeDtypeStruct((n, 4 * slots, c), BF16),
        compiler_params=params(),
        cost_estimate=pl.CostEstimate(flops=0, bytes_accessed=slots * 3 * inner * 6, transcendentals=0),
        name="pack_conv",
    )(jnp.transpose(prefilled_conv, (1, 0, 2)))


def pack_state_kernel(x_ref, o_ref):
    slots = x_ref.shape[0]
    for k in range(slots):
        o_ref[0, STATE * k : STATE * (k + 1), :] = x_ref[k].astype(BF16)


def pack_state(prefilled_state, n):
    slots, _, inner = prefilled_state.shape
    c = inner // n
    return pl.pallas_call(
        pack_state_kernel,
        grid=(n,),
        in_specs=[pl.BlockSpec((slots, STATE, c), lambda d: (0, 0, d))],
        out_specs=pl.BlockSpec((1, slots * STATE, c), lambda d: (d, 0, 0)),
        out_shape=jax.ShapeDtypeStruct((n, slots * STATE, c), BF16),
        compiler_params=params(),
        cost_estimate=pl.CostEstimate(
            flops=0, bytes_accessed=slots * STATE * inner * 6, transcendentals=0
        ),
        name="pack_state",
    )(prefilled_state)


def conv_kernel(steps, n, target_ref, old_ref, moved_ref, x_ref, w_ref, bias_ref, proj_ref, conv_ref, part_ref, win):
    rows, c = win.shape[1:]
    columns = target_ref.shape[1]
    row_id = lax.broadcasted_iota(jnp.int32, (rows, columns), 0)
    for p in range(TAPS):
        hot = row_id == target_ref[p : p + 1, :]
        taken = jnp.max(hot.astype(F32), axis=1, keepdims=True) > 0.0
        fresh = jnp.dot(hot.astype(BF16), moved_ref[...], preferred_element_type=F32)
        win[p] = jnp.where(taken, fresh, old_ref[p])
    for i, t in enumerate(steps):
        total = None
        for q in range(TAPS + 1):
            place = t + q
            value = win[place] if place < TAPS else x_ref[place - TAPS].astype(F32)
            term = value * w_ref[q : q + 1, :]
            total = term if total is None else total + term
        total = total + bias_ref[...]
        conv_out = total * sigmoid(total)
        conv_ref[i] = conv_out
        part = lax.dot_general(
            conv_out.astype(BF16), proj_ref[...], (((1,), (1,)), ((), ())), preferred_element_type=F32
        )
        for d in range(n):
            own = rows // n
            part_ref[d, i, :, : part.shape[1]] = part[d * own : (d + 1) * own, :].astype(BF16)
            part_ref[d, i, :, part.shape[1] :] = jnp.zeros((own, WIDE - part.shape[1]), BF16)


def conv_steps(steps, n, target, old, moved, step_x, conv_weight, conv_bias, proj):
    _, rows, c = old.shape
    s = len(steps)
    last = max(steps) + 1
    return pl.pallas_call(
        functools.partial(conv_kernel, steps, n),
        grid=(1,),
        in_specs=[
            whole(target.shape),
            whole(old.shape),
            whole(moved.shape),
            whole((last, rows, c)),
            whole(conv_weight.shape),
            whole((1, c)),
            whole(proj.shape),
        ],
        out_specs=[whole((s, rows, c)), whole((n, s, rows // n, WIDE))],
        out_shape=[
            jax.ShapeDtypeStruct((s, rows, c), F32),
            jax.ShapeDtypeStruct((n, s, rows // n, WIDE), BF16),
        ],
        scratch_shapes=[pltpu.VMEM((TAPS, rows, c), F32)],
        compiler_params=params(),
        cost_estimate=pl.CostEstimate(
            flops=2 * s * rows * c * 544,
            bytes_accessed=rows * c * (12 + 6 * s) + c * 1088,
            transcendentals=s * rows * c,
        ),
        name="conv_project",
    )(target, old, moved, step_x, conv_weight, conv_bias, proj)


def norm_kernel(n, part_ref, gain_ref, o_ref):
    total = part_ref[0].astype(F32)
    for d in range(1, n):
        total = total + part_ref[d].astype(F32)
    dt = total[:, :, :DT_RANK]
    dt = dt * lax.rsqrt(jnp.mean(dt * dt, axis=2, keepdims=True) + RMS_EPS) * gain_ref[:, :DT_RANK][None]
    tail = total[:, :, DT_RANK:]
    lane = lax.broadcasted_iota(jnp.int32, tail.shape, 2)
    square = tail * tail
    is_b = lane < STATE
    is_c = jnp.logical_and(lane >= STATE, lane < 2 * STATE)
    mean_b = jnp.sum(jnp.where(is_b, square, 0.0), axis=2, keepdims=True) / STATE
    mean_c = jnp.sum(jnp.where(is_c, square, 0.0), axis=2, keepdims=True) / STATE
    scale_b = lax.rsqrt(jnp.maximum(mean_b, BC_FLOOR))
    scale_c = lax.rsqrt(jnp.maximum(mean_c, BC_FLOOR))
    tail = tail * jnp.where(is_b, scale_b, scale_c) * gain_ref[:, DT_RANK:][None]
    tail = jnp.where(lane < 2 * STATE, tail, 0.0)
    dt = dt.astype(BF16)
    tail = tail.astype(BF16)
    for d in range(n):
        o_ref[d, :, :, :DT_RANK] = dt
        o_ref[d, :, :, DT_RANK:] = tail


def norm(part, gain, n):
    return pl.pallas_call(
        functools.partial(norm_kernel, n),
        grid=(1,),
        in_specs=[whole(part.shape), whole(gain.shape)],
        out_specs=whole(part.shape),
        out_shape=jax.ShapeDtypeStruct(part.shape, BF16),
        compiler_params=params(),
        cost_estimate=pl.CostEstimate(flops=part.size, bytes_accessed=part.size * 4, transcendentals=0),
        name="norm",
    )(part, gain)


def state_kernel(first, last, n, me_ref, slot_ref, *refs):
    if first:
        moved_ref, refs = refs[0], refs[1:]
    low_ref, conv_ref, z_ref, dtp_ref, dtb_ref, alog_ref, skip_ref, state_ref, *refs = refs
    if last:
        gated_ref, step_scr, bc_scr, decay_scr, y_scr = refs
        new_ref = None
    else:
        new_ref, gated_ref, step_scr, bc_scr, decay_scr, y_scr = refs
    block = pl.program_id(0)
    rows, c = step_scr.shape
    take = state_ref.shape[0]
    blocks = rows // take

    @pl.when(block == 0)
    def _():
        low = low_ref[...].reshape(rows, WIDE)
        pre = jnp.dot(low[:, :DT_RANK], dtp_ref[...], preferred_element_type=F32) + dtb_ref[...]
        step_scr[...] = jnp.maximum(pre, 0.0) + jnp.log(1.0 + jnp.exp(-jnp.abs(pre)))
        decay_scr[...] = jnp.exp(alog_ref[...]) * (-LOG2E)
        tail = low[:, DT_RANK:].astype(F32)
        per = 128 // take
        for h in range(rows // 128):
            turned = tail[128 * h : 128 * (h + 1), :].T
            for i in range(per):
                bc_scr[h * per + i, :, :take] = turned[: 2 * STATE, take * i : take * (i + 1)]

    base = block * take
    bc = bc_scr[block]
    from_ref = new_ref if first else state_ref
    lanes = 256
    for r in range(take):
        if first:
            slot = slot_ref[base + r]

            @pl.when(slot >= 0)
            def _(r=r, slot=slot):
                new_ref[r] = moved_ref[slot].astype(F32)

            @pl.when(slot < 0)
            def _(r=r):
                new_ref[r] = state_ref[r]

        b = bc[:STATE, r : r + 1]
        g = bc[STATE : 2 * STATE, r : r + 1]
        for l in range(0, c, lanes):
            cols = slice(l, l + lanes)
            step = step_scr[pl.ds(base + r, 1), cols]
            drive = step * conv_ref[pl.ds(r, 1), cols]
            state = jnp.exp2(step * decay_scr[:, cols]) * from_ref[r, :, cols] + drive * b
            if new_ref is not None:
                new_ref[r, :, cols] = state
            y_scr[pl.ds(r, 1), cols] = jnp.sum(state * g, axis=0, keepdims=True)
    z = z_ref[0].astype(F32)
    gated = (y_scr[...] + skip_ref[...] * conv_ref[...]) * (z * sigmoid(z))
    gated_ref[...] = gated.astype(BF16)


def state_step(t, index, me, slot_of_row, moved, low, conv, step_z, dt_proj, dt_bias, a_log, d_skip, state, n):
    rows, _, c = state.shape
    take = 2 * rows // n
    blocks = rows // take
    first, last = t == 0, t == STEPS - 1
    own = rows // n

    def placed(i, me_ref, slot_ref):
        z, y = i // 2, i % 2
        mine = (y == (me_ref[0] // 2) % 2).astype(jnp.int32)
        return (mine * (blocks // 2) + z, 0)

    in_specs = [
        pl.BlockSpec((n, None, own, WIDE), lambda i, *_: (0, index, 0, 0)),
        pl.BlockSpec((None, take, c), lambda i, *_: (index, i, 0)),
        pl.BlockSpec((1, take, c), lambda i, *_: (t, i, 0)),
        whole(dt_proj.shape),
        whole((1, c)),
        whole(a_log.shape),
        whole((1, c)),
        pl.BlockSpec((take, STATE, c), lambda i, *_: (i, 0, 0)),
    ]
    args = [low, conv, step_z, dt_proj, dt_bias, a_log, d_skip, state]
    if first:
        in_specs = [whole(moved.shape)] + in_specs
        args = [moved] + args
    out_specs = [pl.BlockSpec((take, c), placed)]
    out_shape = [jax.ShapeDtypeStruct((rows, c), BF16)]
    if not last:
        out_specs = [pl.BlockSpec((take, STATE, c), lambda i, *_: (i, 0, 0))] + out_specs
        out_shape = [jax.ShapeDtypeStruct(state.shape, F32)] + out_shape
    out = pl.pallas_call(
        functools.partial(state_kernel, first, last, n),
        grid_spec=pltpu.PrefetchScalarGridSpec(
            num_scalar_prefetch=2,
            grid=(blocks,),
            in_specs=in_specs,
            out_specs=out_specs,
            scratch_shapes=[
                pltpu.VMEM((rows, c), F32),
                pltpu.VMEM((blocks, 2 * STATE, 128), F32),
                pltpu.VMEM((STATE, c), F32),
                pltpu.VMEM((take, c), F32),
            ],
        ),
        out_shape=out_shape,
        compiler_params=params(),
        cost_estimate=pl.CostEstimate(
            flops=8 * state.size, bytes_accessed=8 * state.size, transcendentals=state.size
        ),
        name="state_step",
    )(me, slot_of_row, *args)
    return (None, out[0]) if last else (out[0], out[1])


def out_kernel(me_ref, own_ref, other_ref, wown_ref, wother_ref, send_ref, keep_ref):
    total = jnp.dot(own_ref[...], wown_ref[...], preferred_element_type=F32)
    total = total + jnp.dot(other_ref[...], wother_ref[...], preferred_element_type=F32)
    half = send_ref.shape[0]
    send_ref[...] = total[:half].astype(BF16)
    keep_ref[...] = total[half:].astype(BF16)


def out_project(me, own, other, out_weight, other_weight):
    rows, c = own.shape
    cols = other_weight.shape[1]
    tile = 512
    tiles = cols // tile
    half = jax.ShapeDtypeStruct((rows // 2, cols), BF16)
    return pl.pallas_call(
        out_kernel,
        grid_spec=pltpu.PrefetchScalarGridSpec(
            num_scalar_prefetch=1,
            grid=(tiles,),
            in_specs=[
                whole(own.shape),
                whole(other.shape),
                pl.BlockSpec((c, tile), lambda j, me_ref: (0, (me_ref[0] % 2) * tiles + j)),
                pl.BlockSpec((c, tile), lambda j, me_ref: (0, j)),
            ],
            out_specs=[pl.BlockSpec((rows // 2, tile), lambda j, me_ref: (0, j))] * 2,
        ),
        out_shape=[half, half],
        compiler_params=params(),
        cost_estimate=pl.CostEstimate(
            flops=4 * rows * c * cols, bytes_accessed=4 * c * cols + 2 * rows * cols, transcendentals=0
        ),
        name="out_project",
    )(me, own, other, out_weight, other_weight)


def pieces_kernel(zs, me_ref, keep_ref, got_ref, *o_refs):
    core = me_ref[0] % 2
    z = me_ref[0] // 4
    for m in range(zs):
        at = jnp.bitwise_xor(z, m)
        total = keep_ref[at].astype(F32) + got_ref[at].astype(F32)
        own = total.shape[0] // 2
        low, high = total[:own], total[own:]
        o_refs[2 * m][...] = jnp.where(core == 0, low, high).astype(BF16)
        o_refs[2 * m + 1][...] = jnp.where(core == 0, high, low).astype(BF16)


def sum_pieces(me, keep, got, n):
    half, cols = keep.shape
    zs = n // 4
    take = half // zs
    own = take // 2
    tile = 1024
    shape = jax.ShapeDtypeStruct((own, cols), BF16)
    return pl.pallas_call(
        functools.partial(pieces_kernel, zs),
        grid_spec=pltpu.PrefetchScalarGridSpec(
            num_scalar_prefetch=1,
            grid=(cols // tile,),
            in_specs=[pl.BlockSpec((zs, take, tile), lambda j, me_ref: (0, 0, j))] * 2,
            out_specs=[pl.BlockSpec((own, tile), lambda j, me_ref: (0, j))] * (2 * zs),
        ),
        out_shape=[shape] * (2 * zs),
        compiler_params=params(),
        cost_estimate=pl.CostEstimate(flops=half * cols, bytes_accessed=6 * half * cols, transcendentals=0),
        name="sum_pieces",
    )(me, keep.reshape(zs, take, cols), got.reshape(zs, take, cols))


def final_kernel(zs, me_ref, *refs):
    o_ref = refs[-1]
    pieces = refs[:-1]
    side = pl.program_id(0)
    own_half = side == me_ref[0] % 2
    for t in range(STEPS):
        at = 2 * zs * t
        mine = pieces[at][...].astype(F32)
        theirs = pieces[at + 1][...].astype(F32)
        for m in range(1, zs):
            mine = mine + pieces[at + 2 * m][...].astype(F32)
            theirs = theirs + pieces[at + 2 * m + 1][...].astype(F32)
        o_ref[:, t, :] = jnp.where(own_half, mine, theirs).astype(BF16)


def final_sum(me, pieces, n):
    own, cols = pieces[0].shape
    zs = n // 4
    tile = 1024
    tiles = cols // tile
    return pl.pallas_call(
        functools.partial(final_kernel, zs),
        grid_spec=pltpu.PrefetchScalarGridSpec(
            num_scalar_prefetch=1,
            grid=(2, tiles),
            in_specs=[pl.BlockSpec((own, tile), lambda s, j, me_ref: (0, j))] * len(pieces),
            out_specs=pl.BlockSpec((own, STEPS, tile), lambda s, j, me_ref: (0, 0, s * tiles + j)),
        ),
        out_shape=jax.ShapeDtypeStruct((own, STEPS, 2 * cols), BF16),
        compiler_params=params(),
        cost_estimate=pl.CostEstimate(
            flops=own * cols * len(pieces), bytes_accessed=own * cols * 2 * len(pieces), transcendentals=0
        ),
        name="final_sum",
    )(me, *pieces)


def shards(
    resident_state,
    resident_conv,
    prefilled_state,
    prefilled_conv,
    live_counts,
    batch_rows,
    step_x,
    step_z,
    conv_weight,
    conv_bias,
    x_proj,
    norm_gain,
    dt_proj,
    dt_bias,
    a_log,
    d_skip,
    out_weight,
):
    n = lax.axis_size("dex")
    rows = resident_state.shape[0]
    slots = prefilled_state.shape[0]
    c = resident_state.shape[2]
    me_scalar = lax.axis_index("dex").astype(jnp.int32)
    me = me_scalar.reshape(1)

    moved_conv = lax.all_to_all(pack_conv(prefilled_conv, n), "dex", 0, 0, tiled=True)
    moved_state = lax.all_to_all(pack_state(prefilled_state, n), "dex", 0, 0, tiled=True)

    cols = out_weight.shape[1] // 2
    core = me_scalar % 2
    other_weight = swap(lax.dynamic_slice_in_dim(out_weight, (1 - core) * cols, cols, 1), 1, n)

    is_live = jnp.arange(slots, dtype=jnp.int32)[None, :] < live_counts[:, None]
    target = jnp.where(is_live, batch_rows.reshape(n, slots), -1)
    spread = jnp.full((TAPS, n, 4, slots), -1, jnp.int32)
    place = jnp.arange(4, dtype=jnp.int32)[None, None, :, None]
    tap = jnp.arange(TAPS, dtype=jnp.int32)[:, None, None, None]
    spread = jnp.where(place == tap, target[None, :, None, :], spread).reshape(TAPS, n * 4 * slots)
    hit = target.reshape(1, n * slots) == jnp.arange(rows, dtype=jnp.int32)[:, None]
    slot_of_row = jnp.max(
        jnp.where(hit, jnp.arange(n * slots, dtype=jnp.int32)[None, :], -1), axis=1
    )
    gain = jnp.concatenate([norm_gain, jnp.zeros((WIDE - norm_gain.shape[0],), F32)]).reshape(1, WIDE)
    old = jnp.transpose(resident_conv, (1, 0, 2))
    proj = x_proj.T
    bias = conv_bias.reshape(1, c)
    moved_conv = moved_conv.reshape(n * 4 * slots, c)
    moved_state = moved_state.reshape(n * slots, STATE, c)

    lows = {}
    convs = {}
    for steps in ((0,), tuple(range(1, STEPS))):
        conv, part = conv_steps(steps, n, spread, old, moved_conv, step_x, conv_weight, bias, proj)
        part = lax.all_to_all(part, "dex", 0, 0, tiled=True)
        low = lax.all_to_all(norm(part, gain, n), "dex", 0, 0, tiled=True)
        for i, t in enumerate(steps):
            lows[t] = (low, i)
            convs[t] = conv

    state = resident_state
    pieces = []
    for t in range(STEPS):
        low, i = lows[t]
        state, gated = state_step(
            t, i, me, slot_of_row, moved_state, low, convs[t], step_z, dt_proj,
            dt_bias.reshape(1, c), a_log, d_skip.reshape(1, c), state, n,
        )
        send, keep = out_project(me, gated, swap(gated, 1, n), out_weight, other_weight)
        cut = sum_pieces(me, keep, swap(send, 2, n), n)
        for m in range(n // 4):
            for k in range(2):
                mask = 4 * m + k
                pieces.append(cut[2 * m + k] if mask == 0 else swap(cut[2 * m + k], mask, n))
    return final_sum(me, pieces, n)


def solution(mesh):
    placed = (
        P("grp", None, "dex"),
        P("grp", None, "dex"),
        P(("grp", "dex"), None, None),
        P(("grp", "dex"), None, None),
        P("grp"),
        P("grp"),
        P(None, "grp", "dex"),
        P(None, "grp", "dex"),
        P(None, "dex"),
        P("dex"),
        P("dex", None),
        P(),
        P(None, "dex"),
        P("dex"),
        P(None, "dex"),
        P("dex"),
        P("dex", None),
    )
    return jax.shard_map(
        shards, mesh=mesh, in_specs=placed, out_specs=P(("grp", "dex"), None, None), check_vma=False
    )
```

time: 738 us -> 448 us (0.61)
  local copies, waits for them, and re-layouts: 219 us -> 17.8 us
  Pallas kernels: 0 us -> 185 us
  waiting for transfers between devices: 331 us -> 150 us
  other arithmetic: 83.6 us -> 2.01 us
  starting transfers between devices: 12 us -> 85.8 us
  matrix products: 66.4 us -> 0 us
  between operations: 13.9 us -> 0.7 us
    reduce_scatter x4 -> x0, waiting for transfers between devices: 255 us -> none  [shards(): lax.psum_scatter(term_rows(jnp.int32(0), lax.axis_size('dex') * own_rows)...]
    pallas_call x0 -> x19, Pallas kernels: none -> 185 us  [the longest x4 82.4 us: state_step(): pl.pallas_call(functools.partial(state_kernel, first, last, n), grid_spec...]
    convert_element_type x5 -> x0, local copies, waits for them, and re-layouts: 88.3 us -> none  [the longest x3 56.3 us: shards(): moved_state, moved_conv = (lax.all_to_all(prefilled_state.astype(jnp.bflo...]
    unnamed x98 -> x94, local copies, waits for them, and re-layouts: 94.4 us -> 8.25 us
    ppermute x0 -> x37, waiting for transfers between devices: none -> 76.8 us  [swap(): return lax.ppermute(x, 'dex', [(i, i ^ mask) for i in range(n)])]
    psum x1 -> x0, waiting for transfers between devices: 67.2 us -> none  [shards(): lax.psum(partial_value.astype(jnp.bfloat16), 'dex').astype(jnp.float32)]
    dot_general x12 -> x0, matrix products: 66.4 us -> none  [the longest x4 52.6 us: term_rows(): return jnp.dot(source, out_weight, preferred_element_type=jnp.float32)]
    all_to_all x2 -> x6, waiting for transfers between devices: 8.69 us -> 73.3 us  [the longest x1 38.7 us: shards(): lax.all_to_all(pack_state(prefilled_state, n), 'dex', 0, 0, tiled=True)]
  transfers between devices with their start and end apart: 7 -> 43, of which waited for: 6 -> 14; matrix products, arithmetic and copies ran while one was open for 14% -> 3% of each run, Pallas kernels for 0% -> 37%
where the time goes in v1:
time: 448 us; the launch traced here: 441 us
  Pallas kernels  185 us (41%)
  waiting for transfers between devices  150 us (33%)
  starting transfers between devices  85.8 us (19%)
  local copies, waits for them, and re-layouts  17.8 us (4%)
    pallas_call x4, Pallas kernels, state_step(): pl.pallas_call(functools.partial(state_kernel, first, last, n), grid_spec...  82.4 us
    ppermute x37, waiting for transfers between devices, swap(): return lax.ppermute(x, 'dex', [(i, i ^ mask) for i in range(n)])  76.8 us
    ppermute x37, starting transfers between devices, swap(): return lax.ppermute(x, 'dex', [(i, i ^ mask) for i in range(n)])  47.1 us
    pallas_call x4, Pallas kernels, out_project(): pl.pallas_call(out_kernel, grid_spec=pltpu.PrefetchScalarGridSpec(num_sca...  45.9 us
    all_to_all x1, waiting for transfers between devices, shards(): lax.all_to_all(pack_state(prefilled_state, n), 'dex', 0, 0, tiled=True)  38.7 us
    all_to_all x2, waiting for transfers between devices, shards(): part = lax.all_to_all(part, 'dex', 0, 0, tiled=True)  22.5 us
    all_to_all x2, starting transfers between devices, shards(): low = lax.all_to_all(norm(part, gain, n), 'dex', 0, 0, tiled=True)  14.8 us
    pallas_call x4, Pallas kernels, sum_pieces(): pl.pallas_call(functools.partial(pieces_kernel, zs), grid_spec=pltpu.Pref...  14.5 us
  transfers between devices with their start and end apart: 43, of which 14 were waited for; matrix products, arithmetic and copies ran while one was open for 3% of the time, Pallas kernels for 37%

profile of v1, /device:TPU:0, one launch (start us, length us, event | category | flops | bytes accessed | tf_op | source)
XLA Modules:
  0.0 441.2 jit_solution(375982177890407480)
XLA Ops:
  0.0 8.5 %pack_conv.1 = bf16[16,16,1024]{2,1,0:T(8,128)(2,1)} custom-call(f32[3,4,16384]{2,1,0:T(4,128)} %bitcast.32), custom_call_target="tpu_custom_call" | custom-call | bytes 1179648 | tf_op jit(solution)/shard_map/pack_conv/pallas_call | solution.py:52
  8.5 7.4 %all-to-all-start.1 = ((bf16[16,16,1024]{2,1,0:T(8,128)(2,1)}), bf16[16,16,1024]{2,1,0:T(8,128)(2,1)S(1)}, u32[]{:S(2)}, u32[]{:S(2)}) async-start(bf16[16,16,1024]{2,1,0:T(8,128)(2,1)} %pack_conv.1), calls=%async_computation.1 | async-start | bytes 1048576 | tf_op jit(solution)/shard_map/all_to_all | solution.py:430
  18.3 12.1 %all-to-all-done.1 = bf16[16,16,1024]{2,1,0:T(8,128)(2,1)S(1)} async-done(((bf16[16,16,1024]{2,1,0:T(8,128)(2,1)}), bf16[16,16,1024]{2,1,0:T(8,128)(2,1)S(1)}, u32[]{:S(2)}, u32[]{:S(2)}) %all-to-all-start.1) | async-done | bytes 524320 | tf_op jit(solution)/shard_map/all_to_all | solution.py:430
  30.4 0.8 copy-done.2
  31.2 4.8 %conv_project.2 = (f32[1,256,1024]{2,1,0:T(8,128)}, bf16[16,1,16,640]{3,2,1,0:T(8,128)(2,1)}) custom-call(s32[3,256]{1,0:T(4,128)} %broadcast_select_fusion.1.target_ref, f32[3,256,1024]{2,1,0:T(8,128)} %bitcast.17, bf16[256,1024]{1,0:T(8,128)(2,1)} %bitcast.20, bf16[4,256,1024]{2,1,0:T(8,128)(2,1)} %x_ref.5, f32[4,1024]{1,0:T(4,128)} %w_ref.3, ...), custom_call_target="tpu_custom_call" | custom-call | flops 285212672 | bytes 5832704 | tf_op jit(solution)/shard_map/conv_project/pallas_call | solution.py:119
  36.0 4.1 all-to-all-start.2
  40.7 10.5 %all-to-all-done.2.part_ref = bf16[16,1,16,640]{3,2,1,0:T(8,128)(2,1)S(1)} async-done(((bf16[16,1,16,640]{3,2,1,0:T(8,128)(2,1)}), bf16[16,1,16,640]{3,2,1,0:T(8,128)(2,1)S(1)}, u32[]{:S(2)}, u32[]{:S(2)}) %all-to-all-start.2) | async-done | bytes 327712 | tf_op jit(solution)/shard_map/all_to_all | solution.py:458
  51.9 1.8 norm.2
  53.8 3.5 all-to-all-start.3
  57.3 7.8 %constant_dynamic-slice_fusion = bf16[1024,4096]{1,0:T(8,128)(2,1)} fusion(bf16[1024,8192]{1,0:T(8,128)(2,1)} %wown_ref.7, s32[]{:T(128)S(6)} %select_n.36), kind=kLoop, calls=%fused_computation.6 | loop fusion | bytes 16777220 | tf_op jit(solution)/shard_map/dynamic_slice | solution.py:435
  65.4 7.6 %conv_project.3 = (f32[3,256,1024]{2,1,0:T(8,128)}, bf16[16,3,16,640]{3,2,1,0:T(8,128)(2,1)}) custom-call(s32[3,256]{1,0:T(4,128)} %broadcast_select_fusion.1.target_ref, f32[3,256,1024]{2,1,0:T(8,128)} %bitcast.18, bf16[256,1024]{1,0:T(8,128)(2,1)} %bitcast.21, bf16[4,256,1024]{2,1,0:T(8,128)(2,1)} %x_ref.5, f32[4,1024]{1,0:T(4,128)} %w_ref.3, ...), custom_call_target="tpu_custom_call" | custom-call | flops 855638016 | bytes 8978432 | tf_op jit(solution)/shard_map/conv_project/pallas_call | solution.py:119
  73.0 5.9 %all-to-all-start.4 = ((bf16[16,3,16,640]{3,2,1,0:T(8,128)(2,1)}), bf16[16,3,16,640]{3,2,1,0:T(8,128)(2,1)S(1)}, u32[]{:S(2)}, u32[]{:S(2)}) async-start(bf16[16,3,16,640]{3,2,1,0:T(8,128)(2,1)} %get-tuple-element.68), calls=%async_computation.4 | async-start | bytes 1966080 | tf_op jit(solution)/shard_map/all_to_all | solution.py:458
  78.9 9.8 %pack_state.1 = bf16[16,64,1024]{2,1,0:T(8,128)(2,1)} custom-call(f32[4,16,16384]{2,1,0:T(8,128)} %x_ref.3), custom_call_target="tpu_custom_call" | custom-call | bytes 6291456 | tf_op jit(solution)/shard_map/pack_state/pallas_call | solution.py:73
  88.7 12.1 %all-to-all-done.4.part_ref = bf16[16,3,16,640]{3,2,1,0:T(8,128)(2,1)S(1)} async-done(((bf16[16,3,16,640]{3,2,1,0:T(8,128)(2,1)}), bf16[16,3,16,640]{3,2,1,0:T(8,128)(2,1)S(1)}, u32[]{:S(2)}, u32[]{:S(2)}) %all-to-all-start.4) | async-done | bytes 983072 | tf_op jit(solution)/shard_map/all_to_all | solution.py:458
  100.8 6.5 %all-to-all-start = ((bf16[16,64,1024]{2,1,0:T(8,128)(2,1)}), bf16[16,64,1024]{2,1,0:T(8,128)(2,1)S(1)}, u32[]{:S(2)}, u32[]{:S(2)}) async-start(bf16[16,64,1024]{2,1,0:T(8,128)(2,1)} %pack_state.1), calls=%async_computation | async-start | bytes 4194304 | tf_op jit(solution)/shard_map/all_to_all | solution.py:431
  107.3 2.4 norm.3
  109.7 38.7 %all-to-all-done = bf16[16,64,1024]{2,1,0:T(8,128)(2,1)S(1)} async-done(((bf16[16,64,1024]{2,1,0:T(8,128)(2,1)}), bf16[16,64,1024]{2,1,0:T(8,128)(2,1)S(1)}, u32[]{:S(2)}, u32[]{:S(2)}) %all-to-all-start) | async-done | bytes 2097184 | tf_op jit(solution)/shard_map/all_to_all | solution.py:431
  148.4 11.2 %all-to-all-start.5 = ((bf16[16,3,16,640]{3,2,1,0:T(8,128)(2,1)}), bf16[16,3,16,640]{3,2,1,0:T(8,128)(2,1)S(1)}, u32[]{:S(2)}, u32[]{:S(2)}) async-start(bf16[16,3,16,640]{3,2,1,0:T(8,128)(2,1)} %norm.3), calls=%async_computation.5 | async-start | bytes 1966080 | tf_op jit(solution)/shard_map/all_to_all | solution.py:459
  160.5 30.1 %state_step.4 = (f32[256,16,1024]{2,1,0:T(8,128)}, bf16[256,1024]{1,0:T(8,128)(2,1)}) custom-call(s32[1]{0:T(128)} %bitcast.me_ref, s32[256]{0:T(256)} %select_reduce_fusion.slot_ref, bf16[64,16,1024]{2,1,0:T(8,128)(2,1)} %bitcast.19, bf16[16,1,16,640]{3,2,1,0:T(8,128)(2,1)} %copy-done.5, f32[1,256,1024]{2,1,0:T(8,128)} %get-tuple-element.56.refs_2_, ...), custom_call_target="tpu_custom_call" | custom-call | flops 33554432 | bytes 33554432 | tf_op jit(solution)/shard_map/state_step/pallas_call | solution.py:273
  190.6 0.9 copy-done
  191.5 19.0 %state_step.5 = (f32[256,16,1024]{2,1,0:T(8,128)}, bf16[256,1024]{1,0:T(8,128)(2,1)}) custom-call(s32[1]{0:T(128)} %bitcast.me_ref, s32[256]{0:T(256)} %select_reduce_fusion.slot_ref, bf16[16,3,16,640]{3,2,1,0:T(8,128)(2,1)} %copy-done, f32[3,256,1024]{2,1,0:T(8,128)} %get-tuple-element.69.refs_1_, bf16[4,256,1024]{2,1,0:T(8,128)(2,1)} %refs_2_.5, ...), custom_call_target="tpu_custom_call" | custom-call | flops 33554432 | bytes 33554432 | tf_op jit(solution)/shard_map/state_step/pallas_call | solution.py:273
  210.6 19.0 %state_step.6 = (f32[256,16,1024]{2,1,0:T(8,128)}, bf16[256,1024]{1,0:T(8,128)(2,1)}) custom-call(s32[1]{0:T(128)} %bitcast.me_ref, s32[256]{0:T(256)} %select_reduce_fusion.slot_ref, bf16[16,3,16,640]{3,2,1,0:T(8,128)(2,1)} %copy-done, f32[3,256,1024]{2,1,0:T(8,128)} %get-tuple-element.69.refs_1_, bf16[4,256,1024]{2,1,0:T(8,128)(2,1)} %refs_2_.5, ...), custom_call_target="tpu_custom_call" | custom-call | flops 33554432 | bytes 33554432 | tf_op jit(solution)/shard_map/state_step/pallas_call | solution.py:273
  230.0 14.2 %state_step.7.own_ref = bf16[256,1024]{1,0:T(8,128)(2,1)} custom-call(s32[1]{0:T(128)} %bitcast.me_ref, s32[256]{0:T(256)} %select_reduce_fusion.slot_ref, bf16[16,3,16,640]{3,2,1,0:T(8,128)(2,1)} %copy-done, f32[3,256,1024]{2,1,0:T(8,128)} %get-tuple-element.69.refs_1_, bf16[4,256,1024]{2,1,0:T(8,128)(2,1)} %refs_2_.5, bf16[512,1024]{1,0:T(8,128)(2,1)} %refs_3_.7, ...), custom_call_target="tpu_custom_call" | custom-call | flops 33554432 | bytes 33554432 | tf_op jit(solution)/shard_map/state_step/pallas_call | solution.py:273
  245.6 11.5 %out_project.6 = (bf16[128,4096]{1,0:T(8,128)(2,1)}, bf16[128,4096]{1,0:T(8,128)(2,1)}) custom-call(s32[1]{0:T(128)} %bitcast.me_ref, bf16[256,1024]{1,0:T(8,128)(2,1)} %get-tuple-element.83.own_ref, bf16[256,1024]{1,0:T(8,128)(2,1)} %copy-done.15, bf16[1024,8192]{1,0:T(8,128)(2,1)} %wown_ref.7, bf16[1024,4096]{1,0:T(8,128)(2,1)} %collective-permute-done.1.wother_ref), custom_call_target="tpu_custom_call" | custom-call | flops 4294967296 | bytes 18874368 | tf_op jit(solution)/shard_map/out_project/pallas_call | solution.py:311
  257.1 1.9 collective-permute-start.20
  259.0 0.8 copy-done.14
  259.8 11.5 %out_project.7 = (bf16[128,4096]{1,0:T(8,128)(2,1)}, bf16[128,4096]{1,0:T(8,128)(2,1)}) custom-call(s32[1]{0:T(128)} %bitcast.me_ref, bf16[256,1024]{1,0:T(8,128)(2,1)} %state_step.7.own_ref, bf16[256,1024]{1,0:T(8,128)(2,1)} %copy-done.14, bf16[1024,8192]{1,0:T(8,128)(2,1)} %wown_ref.7, bf16[1024,4096]{1,0:T(8,128)(2,1)} %collective-permute-done.1.wother_ref), custom_call_target="tpu_custom_call" | custom-call | flops 4294967296 | bytes 18874368 | tf_op jit(solution)/shard_map/out_project/pallas_call | solution.py:311
  271.4 0.8 copy-done.13
  272.2 11.5 %out_project.5 = (bf16[128,4096]{1,0:T(8,128)(2,1)}, bf16[128,4096]{1,0:T(8,128)(2,1)}) custom-call(s32[1]{0:T(128)} %bitcast.me_ref, bf16[256,1024]{1,0:T(8,128)(2,1)} %get-tuple-element.71.own_ref, bf16[256,1024]{1,0:T(8,128)(2,1)} %copy-done.13, bf16[1024,8192]{1,0:T(8,128)(2,1)} %wown_ref.7, bf16[1024,4096]{1,0:T(8,128)(2,1)} %collective-permute-done.1.wother_ref), custom_call_target="tpu_custom_call" | custom-call | flops 4294967296 | bytes 18874368 | tf_op jit(solution)/shard_map/out_project/pallas_call | solution.py:311
  283.7 1.9 collective-permute-start.11
  285.5 0.8 copy-done.12
  286.4 11.5 %out_project.4 = (bf16[128,4096]{1,0:T(8,128)(2,1)}, bf16[128,4096]{1,0:T(8,128)(2,1)}) custom-call(s32[1]{0:T(128)} %bitcast.me_ref, bf16[256,1024]{1,0:T(8,128)(2,1)} %get-tuple-element.57.own_ref, bf16[256,1024]{1,0:T(8,128)(2,1)} %copy-done.12, bf16[1024,8192]{1,0:T(8,128)(2,1)} %wown_ref.7, bf16[1024,4096]{1,0:T(8,128)(2,1)} %collective-permute-done.1.wother_ref), custom_call_target="tpu_custom_call" | custom-call | flops 4294967296 | bytes 18874368 | tf_op jit(solution)/shard_map/out_project/pallas_call | solution.py:311
  298.0 1.1 copy-done.9
  299.1 3.6 sum_pieces.6
  302.7 2.0 collective-permute-start.22
  304.7 1.0 collective-permute-done.29
  305.8 0.9 copy-done.8
  306.7 3.7 sum_pieces.7
  310.4 17.8 %collective-permute-done.11 = bf16[128,4096]{1,0:T(8,128)(2,1)S(1)} collective-permute-done((bf16[128,4096]{1,0:T(8,128)(2,1)}, bf16[128,4096]{1,0:T(8,128)(2,1)S(1)}, u32[]{:S(2)}, u32[]{:S(2)}) %collective-permute-start.11) | collective-permute-done | bytes 1048608 | tf_op jit(solution)/shard_map/ppermute | solution.py:30
  328.2 2.9 collective-permute-start.24
  331.1 19.1 %collective-permute-done.2 = bf16[128,4096]{1,0:T(8,128)(2,1)S(1)} collective-permute-done((bf16[128,4096]{1,0:T(8,128)(2,1)}, bf16[128,4096]{1,0:T(8,128)(2,1)S(1)}, u32[]{:S(2)}, u32[]{:S(2)}) %collective-permute-start.2) | collective-permute-done | bytes 1048608 | tf_op jit(solution)/shard_map/ppermute | solution.py:30
  350.2 1.5 collective-permute-start.25
  351.7 2.1 collective-permute-start.26
  353.7 2.3 collective-permute-start.27
  356.1 9.3 %collective-permute-done.25.refs_21_ = bf16[16,4096]{1,0:T(8,128)(2,1)S(1)} collective-permute-done((bf16[16,4096]{1,0:T(8,128)(2,1)}, bf16[16,4096]{1,0:T(8,128)(2,1)S(1)}, u32[]{:S(2)}, u32[]{:S(2)}) %collective-permute-start.25) | collective-permute-done | bytes 131104 | tf_op jit(solution)/shard_map/ppermute | solution.py:30
  365.6 4.8 %collective-permute-start.33 = (bf16[16,4096]{1,0:T(8,128)(2,1)}, bf16[16,4096]{1,0:T(8,128)(2,1)S(1)}, u32[]{:S(2)}, u32[]{:S(2)}) collective-permute-start(bf16[16,4096]{1,0:T(8,128)(2,1)} %get-tuple-element.101), channel_id=1, source_target_pairs={{0,8},{1,9},{2,10},{3,11},{4,12},{5,13},{6,14},{7,15},{8,0},{9,1},... | collective-permute-start | bytes 393224 | tf_op jit(solution)/shard_map/ppermute | solution.py:30
  370.4 2.5 collective-permute-start.34
  373.7 3.6 sum_pieces.5
  377.3 3.0 collective-permute-start.36
  380.6 5.5 %collective-permute-done.33.refs_28_ = bf16[16,4096]{1,0:T(8,128)(2,1)S(1)} collective-permute-done((bf16[16,4096]{1,0:T(8,128)(2,1)}, bf16[16,4096]{1,0:T(8,128)(2,1)S(1)}, u32[]{:S(2)}, u32[]{:S(2)}) %collective-permute-start.33) | collective-permute-done | bytes 131104 | tf_op jit(solution)/shard_map/ppermute | solution.py:30
  386.1 2.0 collective-permute-done.34.refs_29_
  388.2 4.8 %collective-permute-start.15 = (bf16[16,4096]{1,0:T(8,128)(2,1)}, bf16[16,4096]{1,0:T(8,128)(2,1)S(1)}, u32[]{:S(2)}, u32[]{:S(2)}) collective-permute-start(bf16[16,4096]{1,0:T(8,128)(2,1)} %get-tuple-element.78), channel_id=1, source_target_pairs={{0,8},{1,9},{2,10},{3,11},{4,12},{5,13},{6,14},{7,15},{8,0},{9,1},... | collective-permute-start | bytes 393224 | tf_op jit(solution)/shard_map/ppermute | solution.py:30
  393.0 3.6 sum_pieces.4
  396.7 1.7 collective-permute-start.17
  398.4 1.5 collective-permute-start.18
  400.7 7.7 %collective-permute-done.15.refs_12_ = bf16[16,4096]{1,0:T(8,128)(2,1)S(1)} collective-permute-done((bf16[16,4096]{1,0:T(8,128)(2,1)}, bf16[16,4096]{1,0:T(8,128)(2,1)S(1)}, u32[]{:S(2)}, u32[]{:S(2)}) %collective-permute-start.15) | collective-permute-done | bytes 131104 | tf_op jit(solution)/shard_map/ppermute | solution.py:30
  408.4 2.6 collective-permute-done.16.refs_13_
  411.1 4.4 %collective-permute-start.6 = (bf16[16,4096]{1,0:T(8,128)(2,1)}, bf16[16,4096]{1,0:T(8,128)(2,1)S(1)}, u32[]{:S(2)}, u32[]{:S(2)}) collective-permute-start(bf16[16,4096]{1,0:T(8,128)(2,1)} %get-tuple-element.64), channel_id=1, source_target_pairs={{0,8},{1,9},{2,10},{3,11},{4,12},{5,13},{6,14},{7,15},{8,0},{9,1},... | collective-permute-start | bytes 393224 | tf_op jit(solution)/shard_map/ppermute | solution.py:30
  415.5 2.5 collective-permute-start.7
  418.0 1.2 collective-permute-start.8
  419.2 2.4 collective-permute-start.9
  421.7 9.5 %collective-permute-done.6.refs_4_ = bf16[16,4096]{1,0:T(8,128)(2,1)S(1)} collective-permute-done((bf16[16,4096]{1,0:T(8,128)(2,1)}, bf16[16,4096]{1,0:T(8,128)(2,1)S(1)}, u32[]{:S(2)}, u32[]{:S(2)}) %collective-permute-start.6) | collective-permute-done | bytes 131104 | tf_op jit(solution)/shard_map/ppermute | solution.py:30
  431.2 2.0 collective-permute-done.7.refs_5_
  433.9 7.1 %final_sum.1 = bf16[16,4,8192]{2,1,0:T(4,128)(2,1)} custom-call(s32[1]{0:T(128)} %bitcast.me_ref, bf16[16,4096]{1,0:T(8,128)(2,1)} %get-tuple-element.60.refs_0_, bf16[16,4096]{1,0:T(8,128)(2,1)} %copy-done.37, bf16[16,4096]{1,0:T(8,128)(2,1)} %copy-done.38, bf16[16,4096]{1,0:T(8,128)(2,1)} %copy-done.39, bf16[16,4096]{1,0:T(8,128)(2,1)} %copy-done.40, ...), custom_call_target="tpu_custom_call" | custom-call | flops 2097152 | bytes 4194304 | tf_op jit(solution)/shard_map/final_sum/pallas_call | solution.py:387
  (150 shorter events, 9.8 us)
Async XLA Ops:
  0.0 40.1 %copy-start.44 = (f32[544]{0:T(1024)S(1)}, f32[544]{0:T(1024)}, u32[]{:S(2)}) copy-start(f32[544]{0:T(1024)} %param.28) | copy-start | bytes 6532
  8.5 21.9 %all-to-all-start.1 = ((bf16[16,16,1024]{2,1,0:T(8,128)(2,1)}), bf16[16,16,1024]{2,1,0:T(8,128)(2,1)S(1)}, u32[]{:S(2)}, u32[]{:S(2)}) async-start(bf16[16,16,1024]{2,1,0:T(8,128)(2,1)} %pack_conv.1), calls=%async_computation.1 | async-start | bytes 1048576 | tf_op jit(solution)/shard_map/all_to_all | solution.py:430
  36.0 15.2 %all-to-all-start.2 = ((bf16[16,1,16,640]{3,2,1,0:T(8,128)(2,1)}), bf16[16,1,16,640]{3,2,1,0:T(8,128)(2,1)S(1)}, u32[]{:S(2)}, u32[]{:S(2)}) async-start(bf16[16,1,16,640]{3,2,1,0:T(8,128)(2,1)} %get-tuple-element.55), calls=%async_computation.2 | async-start | bytes 655360 | tf_op jit(solution)/shard_map/all_to_all | solution.py:458
  53.8 19.2 %all-to-all-start.3 = ((bf16[16,1,16,640]{3,2,1,0:T(8,128)(2,1)}), bf16[16,1,16,640]{3,2,1,0:T(8,128)(2,1)S(1)}, u32[]{:S(2)}, u32[]{:S(2)}) async-start(bf16[16,1,16,640]{3,2,1,0:T(8,128)(2,1)} %norm.2), calls=%async_computation.3 | async-start | bytes 655360 | tf_op jit(solution)/shard_map/all_to_all | solution.py:459
  65.1 179.7 %collective-permute-start.1 = (bf16[1024,4096]{1,0:T(8,128)(2,1)}, bf16[1024,4096]{1,0:T(8,128)(2,1)}, u32[]{:S(2)}, u32[]{:S(2)}) collective-permute-start(bf16[1024,4096]{1,0:T(8,128)(2,1)} %constant_dynamic-slice_fusion), channel_id=1, source_target_pairs={{0,1},{1,0},{2,3},{3,2},{4,5},{5,4},{6,7},{7,6},{8,9},{9,8},{10,11... | collective-permute-start | bytes 25165832 | tf_op jit(solution)/shard_map/ppermute | solution.py:30
  73.0 86.6 %copy-start.45 = (s32[16]{0:T(128)S(1)}, s32[16]{0:T(128)}, u32[]{:S(2)}) copy-start(s32[16]{0:T(128)} %param.21) | copy-start | bytes 196
  73.0 86.8 %copy-start.46 = (s32[64]{0:T(128)S(1)}, s32[64]{0:T(128)}, u32[]{:S(2)}) copy-start(s32[64]{0:T(128)} %param.22) | copy-start | bytes 772
  73.0 87.4 %copy-start.5 = (bf16[16,1,16,640]{3,2,1,0:T(8,128)(2,1)}, bf16[16,1,16,640]{3,2,1,0:T(8,128)(2,1)S(1)}, u32[]{:S(2)}) copy-start(bf16[16,1,16,640]{3,2,1,0:T(8,128)(2,1)S(1)} %all-to-all-done.3.refs_1_) | copy-start | bytes 983044
  73.0 27.7 %all-to-all-start.4 = ((bf16[16,3,16,640]{3,2,1,0:T(8,128)(2,1)}), bf16[16,3,16,640]{3,2,1,0:T(8,128)(2,1)S(1)}, u32[]{:S(2)}, u32[]{:S(2)}) async-start(bf16[16,3,16,640]{3,2,1,0:T(8,128)(2,1)} %get-tuple-element.68), calls=%async_computation.4 | async-start | bytes 1966080 | tf_op jit(solution)/shard_map/all_to_all | solution.py:458
  100.8 47.6 %all-to-all-start = ((bf16[16,64,1024]{2,1,0:T(8,128)(2,1)}), bf16[16,64,1024]{2,1,0:T(8,128)(2,1)S(1)}, u32[]{:S(2)}, u32[]{:S(2)}) async-start(bf16[16,64,1024]{2,1,0:T(8,128)(2,1)} %pack_state.1), calls=%async_computation | async-start | bytes 4194304 | tf_op jit(solution)/shard_map/all_to_all | solution.py:431
  148.4 42.2 %all-to-all-start.5 = ((bf16[16,3,16,640]{3,2,1,0:T(8,128)(2,1)}), bf16[16,3,16,640]{3,2,1,0:T(8,128)(2,1)S(1)}, u32[]{:S(2)}, u32[]{:S(2)}) async-start(bf16[16,3,16,640]{3,2,1,0:T(8,128)(2,1)} %norm.3), calls=%async_computation.5 | async-start | bytes 1966080 | tf_op jit(solution)/shard_map/all_to_all | solution.py:459
  229.6 15.2 %collective-permute-start.19 = (bf16[256,1024]{1,0:T(8,128)(2,1)}, bf16[256,1024]{1,0:T(8,128)(2,1)S(1)}, u32[]{:S(2)}, u32[]{:S(2)}) collective-permute-start(bf16[256,1024]{1,0:T(8,128)(2,1)} %get-tuple-element.83.own_ref), channel_id=1, source_target_pairs={{0,1},{1,0},{2,3},{3,2},{4,5},{5,4},{6,7},{7,6},{8,9},{9,8},{10,11... | collective-permute-start | bytes 1572872 | tf_op jit(solution)/shard_map/ppermute | solution.py:30
  244.2 14.8 %collective-permute-start.28 = (bf16[256,1024]{1,0:T(8,128)(2,1)}, bf16[256,1024]{1,0:T(8,128)(2,1)S(1)}, u32[]{:S(2)}, u32[]{:S(2)}) collective-permute-start(bf16[256,1024]{1,0:T(8,128)(2,1)} %state_step.7.own_ref), channel_id=1, source_target_pairs={{0,1},{1,0},{2,3},{3,2},{4,5},{5,4},{6,7},{7,6},{8,9},{9,8},{10,11... | collective-permute-start | bytes 1572872 | tf_op jit(solution)/shard_map/ppermute | solution.py:30
  244.3 41.2 %collective-permute-start = (bf16[256,1024]{1,0:T(8,128)(2,1)S(1)}, bf16[256,1024]{1,0:T(8,128)(2,1)S(1)}, u32[]{:S(2)}, u32[]{:S(2)}) collective-permute-start(bf16[256,1024]{1,0:T(8,128)(2,1)S(1)} %copy-done.10), channel_id=1, source_target_pairs={{0,1},{1,0},{2,3},{3,2},{4,5},{5,4},{6,7},{7,6},{8,9},{9,8},{10,11... | collective-permute-start | bytes 1572872 | tf_op jit(solution)/shard_map/ppermute | solution.py:30
  244.7 26.7 %collective-permute-start.10 = (bf16[256,1024]{1,0:T(8,128)(2,1)S(1)}, bf16[256,1024]{1,0:T(8,128)(2,1)S(1)}, u32[]{:S(2)}, u32[]{:S(2)}) collective-permute-start(bf16[256,1024]{1,0:T(8,128)(2,1)S(1)} %copy-done.11), channel_id=1, source_target_pairs={{0,1},{1,0},{2,3},{3,2},{4,5},{5,4},{6,7},{7,6},{8,9},{9,8},{10,11... | collective-permute-start | bytes 1572872 | tf_op jit(solution)/shard_map/ppermute | solution.py:30
  257.1 40.9 %collective-permute-start.20 = (bf16[128,4096]{1,0:T(8,128)(2,1)}, bf16[128,4096]{1,0:T(8,128)(2,1)S(1)}, u32[]{:S(2)}, u32[]{:S(2)}) collective-permute-start(bf16[128,4096]{1,0:T(8,128)(2,1)} %get-tuple-element.85), channel_id=1, source_target_pairs={{0,2},{1,3},{2,0},{3,1},{4,6},{5,7},{6,4},{7,5},{8,10},{9,11},{10,... | collective-permute-start | bytes 3145736 | tf_op jit(solution)/shard_map/ppermute | solution.py:30
  271.3 34.5 %collective-permute-start.29 = (bf16[128,4096]{1,0:T(8,128)(2,1)}, bf16[128,4096]{1,0:T(8,128)(2,1)S(1)}, u32[]{:S(2)}, u32[]{:S(2)}) collective-permute-start(bf16[128,4096]{1,0:T(8,128)(2,1)} %get-tuple-element.96), channel_id=1, source_target_pairs={{0,2},{1,3},{2,0},{3,1},{4,6},{5,7},{6,4},{7,5},{8,10},{9,11},{10,... | collective-permute-start | bytes 3145736 | tf_op jit(solution)/shard_map/ppermute | solution.py:30
  283.7 44.6 %collective-permute-start.11 = (bf16[128,4096]{1,0:T(8,128)(2,1)}, bf16[128,4096]{1,0:T(8,128)(2,1)S(1)}, u32[]{:S(2)}, u32[]{:S(2)}) collective-permute-start(bf16[128,4096]{1,0:T(8,128)(2,1)} %get-tuple-element.73), channel_id=1, source_target_pairs={{0,2},{1,3},{2,0},{3,1},{4,6},{5,7},{6,4},{7,5},{8,10},{9,11},{10,... | collective-permute-start | bytes 3145736 | tf_op jit(solution)/shard_map/ppermute | solution.py:30
  297.8 52.4 %collective-permute-start.2 = (bf16[128,4096]{1,0:T(8,128)(2,1)}, bf16[128,4096]{1,0:T(8,128)(2,1)S(1)}, u32[]{:S(2)}, u32[]{:S(2)}) collective-permute-start(bf16[128,4096]{1,0:T(8,128)(2,1)} %get-tuple-element.59), channel_id=1, source_target_pairs={{0,2},{1,3},{2,0},{3,1},{4,6},{5,7},{6,4},{7,5},{8,10},{9,11},{10,... | collective-permute-start | bytes 3145736 | tf_op jit(solution)/shard_map/ppermute | solution.py:30
  302.7 49.0 %collective-permute-start.21 = (bf16[16,4096]{1,0:T(8,128)(2,1)}, bf16[16,4096]{1,0:T(8,128)(2,1)S(1)}, u32[]{:S(2)}, u32[]{:S(2)}) collective-permute-start(bf16[16,4096]{1,0:T(8,128)(2,1)} %get-tuple-element.87), channel_id=1, source_target_pairs={{0,1},{1,0},{2,3},{3,2},{4,5},{5,4},{6,7},{7,6},{8,9},{9,8},{10,11... | collective-permute-start | bytes 393224 | tf_op jit(solution)/shard_map/ppermute | solution.py:30
  302.7 51.0 %collective-permute-start.22 = (bf16[16,4096]{1,0:T(8,128)(2,1)}, bf16[16,4096]{1,0:T(8,128)(2,1)S(1)}, u32[]{:S(2)}, u32[]{:S(2)}) collective-permute-start(bf16[16,4096]{1,0:T(8,128)(2,1)} %get-tuple-element.88), channel_id=1, source_target_pairs={{0,4},{1,5},{2,6},{3,7},{4,0},{5,1},{6,2},{7,3},{8,12},{9,13},{10,... | collective-permute-start | bytes 393224 | tf_op jit(solution)/shard_map/ppermute | solution.py:30
  305.8 50.3 %collective-permute-start.23 = (bf16[16,4096]{1,0:T(8,128)(2,1)}, bf16[16,4096]{1,0:T(8,128)(2,1)S(1)}, u32[]{:S(2)}, u32[]{:S(2)}) collective-permute-start(bf16[16,4096]{1,0:T(8,128)(2,1)} %get-tuple-element.89), channel_id=1, source_target_pairs={{0,5},{1,4},{2,7},{3,6},{4,1},{5,0},{6,3},{7,2},{8,13},{9,12},{10,... | collective-permute-start | bytes 393224 | tf_op jit(solution)/shard_map/ppermute | solution.py:30
  328.2 45.5 %copy-start.7 = (bf16[128,4096]{1,0:T(8,128)(2,1)}, bf16[128,4096]{1,0:T(8,128)(2,1)S(1)}, u32[]{:S(2)}) copy-start(bf16[128,4096]{1,0:T(8,128)(2,1)S(1)} %collective-permute-done.11) | copy-start | bytes 3145732
  328.2 27.8 %collective-permute-start.24 = (bf16[16,4096]{1,0:T(8,128)(2,1)}, bf16[16,4096]{1,0:T(8,128)(2,1)S(1)}, u32[]{:S(2)}, u32[]{:S(2)}) collective-permute-start(bf16[16,4096]{1,0:T(8,128)(2,1)} %get-tuple-element.90), channel_id=1, source_target_pairs={{0,8},{1,9},{2,10},{3,11},{4,12},{5,13},{6,14},{7,15},{8,0},{9,1},... | collective-permute-start | bytes 393224 | tf_op jit(solution)/shard_map/ppermute | solution.py:30
  350.2 42.7 %copy-start.6 = (bf16[128,4096]{1,0:T(8,128)(2,1)}, bf16[128,4096]{1,0:T(8,128)(2,1)S(1)}, u32[]{:S(2)}) copy-start(bf16[128,4096]{1,0:T(8,128)(2,1)S(1)} %collective-permute-done.2) | copy-start | bytes 3145732
  350.2 15.2 %collective-permute-start.25 = (bf16[16,4096]{1,0:T(8,128)(2,1)}, bf16[16,4096]{1,0:T(8,128)(2,1)S(1)}, u32[]{:S(2)}, u32[]{:S(2)}) collective-permute-start(bf16[16,4096]{1,0:T(8,128)(2,1)} %get-tuple-element.91), channel_id=1, source_target_pairs={{0,9},{1,8},{2,11},{3,10},{4,13},{5,12},{6,15},{7,14},{8,1},{9,0},... | collective-permute-start | bytes 393224 | tf_op jit(solution)/shard_map/ppermute | solution.py:30
  351.7 81.5 %copy-start.16 = (bf16[16,4096]{1,0:T(8,128)(2,1)}, bf16[16,4096]{1,0:T(8,128)(2,1)S(1)}, u32[]{:S(2)}) copy-start(bf16[16,4096]{1,0:T(8,128)(2,1)S(1)} %collective-permute-done.21.refs_17_) | copy-start | bytes 393220
  351.7 13.9 %collective-permute-start.26 = (bf16[16,4096]{1,0:T(8,128)(2,1)}, bf16[16,4096]{1,0:T(8,128)(2,1)S(1)}, u32[]{:S(2)}, u32[]{:S(2)}) collective-permute-start(bf16[16,4096]{1,0:T(8,128)(2,1)} %get-tuple-element.92), channel_id=1, source_target_pairs={{0,12},{1,13},{2,14},{3,15},{4,8},{5,9},{6,10},{7,11},{8,4},{9,5},... | collective-permute-start | bytes 393224 | tf_op jit(solution)/shard_map/ppermute | solution.py:30
  353.7 79.5 %copy-start.17 = (bf16[16,4096]{1,0:T(8,128)(2,1)}, bf16[16,4096]{1,0:T(8,128)(2,1)S(1)}, u32[]{:S(2)}) copy-start(bf16[16,4096]{1,0:T(8,128)(2,1)S(1)} %collective-permute-done.22.refs_18_) | copy-start | bytes 393220
  353.7 16.7 %collective-permute-start.27 = (bf16[16,4096]{1,0:T(8,128)(2,1)}, bf16[16,4096]{1,0:T(8,128)(2,1)S(1)}, u32[]{:S(2)}, u32[]{:S(2)}) collective-permute-start(bf16[16,4096]{1,0:T(8,128)(2,1)} %get-tuple-element.93), channel_id=1, source_target_pairs={{0,13},{1,12},{2,15},{3,14},{4,9},{5,8},{6,11},{7,10},{8,5},{9,4},... | collective-permute-start | bytes 393224 | tf_op jit(solution)/shard_map/ppermute | solution.py:30
  356.0 77.2 %copy-start.18 = (bf16[16,4096]{1,0:T(8,128)(2,1)}, bf16[16,4096]{1,0:T(8,128)(2,1)S(1)}, u32[]{:S(2)}) copy-start(bf16[16,4096]{1,0:T(8,128)(2,1)S(1)} %collective-permute-done.23.refs_19_) | copy-start | bytes 393220
  356.0 16.9 %collective-permute-start.30 = (bf16[16,4096]{1,0:T(8,128)(2,1)}, bf16[16,4096]{1,0:T(8,128)(2,1)S(1)}, u32[]{:S(2)}, u32[]{:S(2)}) collective-permute-start(bf16[16,4096]{1,0:T(8,128)(2,1)} %get-tuple-element.98), channel_id=1, source_target_pairs={{0,1},{1,0},{2,3},{3,2},{4,5},{5,4},{6,7},{7,6},{8,9},{9,8},{10,11... | collective-permute-start | bytes 393224 | tf_op jit(solution)/shard_map/ppermute | solution.py:30
  356.1 77.2 %copy-start.19 = (bf16[16,4096]{1,0:T(8,128)(2,1)}, bf16[16,4096]{1,0:T(8,128)(2,1)S(1)}, u32[]{:S(2)}) copy-start(bf16[16,4096]{1,0:T(8,128)(2,1)S(1)} %collective-permute-done.24.refs_20_) | copy-start | bytes 393220
  356.1 21.2 %collective-permute-start.31 = (bf16[16,4096]{1,0:T(8,128)(2,1)}, bf16[16,4096]{1,0:T(8,128)(2,1)S(1)}, u32[]{:S(2)}, u32[]{:S(2)}) collective-permute-start(bf16[16,4096]{1,0:T(8,128)(2,1)} %get-tuple-element.99), channel_id=1, source_target_pairs={{0,4},{1,5},{2,6},{3,7},{4,0},{5,1},{6,2},{7,3},{8,12},{9,13},{10,... | collective-permute-start | bytes 393224 | tf_op jit(solution)/shard_map/ppermute | solution.py:30
  365.5 67.8 %copy-start.20 = (bf16[16,4096]{1,0:T(8,128)(2,1)}, bf16[16,4096]{1,0:T(8,128)(2,1)S(1)}, u32[]{:S(2)}) copy-start(bf16[16,4096]{1,0:T(8,128)(2,1)S(1)} %collective-permute-done.25.refs_21_) | copy-start | bytes 393220
  365.5 14.8 %collective-permute-start.32 = (bf16[16,4096]{1,0:T(8,128)(2,1)}, bf16[16,4096]{1,0:T(8,128)(2,1)S(1)}, u32[]{:S(2)}, u32[]{:S(2)}) collective-permute-start(bf16[16,4096]{1,0:T(8,128)(2,1)} %get-tuple-element.100), channel_id=1, source_target_pairs={{0,5},{1,4},{2,7},{3,6},{4,1},{5,0},{6,3},{7,2},{8,13},{9,12},{10,... | collective-permute-start | bytes 393224 | tf_op jit(solution)/shard_map/ppermute | solution.py:30
  365.6 67.7 %copy-start.21 = (bf16[16,4096]{1,0:T(8,128)(2,1)}, bf16[16,4096]{1,0:T(8,128)(2,1)S(1)}, u32[]{:S(2)}) copy-start(bf16[16,4096]{1,0:T(8,128)(2,1)S(1)} %collective-permute-done.26.refs_22_) | copy-start | bytes 393220
  365.6 20.5 %collective-permute-start.33 = (bf16[16,4096]{1,0:T(8,128)(2,1)}, bf16[16,4096]{1,0:T(8,128)(2,1)S(1)}, u32[]{:S(2)}, u32[]{:S(2)}) collective-permute-start(bf16[16,4096]{1,0:T(8,128)(2,1)} %get-tuple-element.101), channel_id=1, source_target_pairs={{0,8},{1,9},{2,10},{3,11},{4,12},{5,13},{6,14},{7,15},{8,0},{9,1},... | collective-permute-start | bytes 393224 | tf_op jit(solution)/shard_map/ppermute | solution.py:30
  370.4 62.9 %copy-start.22 = (bf16[16,4096]{1,0:T(8,128)(2,1)}, bf16[16,4096]{1,0:T(8,128)(2,1)S(1)}, u32[]{:S(2)}) copy-start(bf16[16,4096]{1,0:T(8,128)(2,1)S(1)} %collective-permute-done.27.refs_23_) | copy-start | bytes 393220
  370.4 17.7 %collective-permute-start.34 = (bf16[16,4096]{1,0:T(8,128)(2,1)}, bf16[16,4096]{1,0:T(8,128)(2,1)S(1)}, u32[]{:S(2)}, u32[]{:S(2)}) collective-permute-start(bf16[16,4096]{1,0:T(8,128)(2,1)} %get-tuple-element.102), channel_id=1, source_target_pairs={{0,9},{1,8},{2,11},{3,10},{4,13},{5,12},{6,15},{7,14},{8,1},{9,0},... | collective-permute-start | bytes 393224 | tf_op jit(solution)/shard_map/ppermute | solution.py:30
  372.9 60.4 %copy-start.23 = (bf16[16,4096]{1,0:T(8,128)(2,1)}, bf16[16,4096]{1,0:T(8,128)(2,1)S(1)}, u32[]{:S(2)}) copy-start(bf16[16,4096]{1,0:T(8,128)(2,1)S(1)} %collective-permute-done.30.refs_25_) | copy-start | bytes 393220
  372.9 15.2 %collective-permute-start.35 = (bf16[16,4096]{1,0:T(8,128)(2,1)}, bf16[16,4096]{1,0:T(8,128)(2,1)S(1)}, u32[]{:S(2)}, u32[]{:S(2)}) collective-permute-start(bf16[16,4096]{1,0:T(8,128)(2,1)} %get-tuple-element.103), channel_id=1, source_target_pairs={{0,12},{1,13},{2,14},{3,15},{4,8},{5,9},{6,10},{7,11},{8,4},{9,5},... | collective-permute-start | bytes 393224 | tf_op jit(solution)/shard_map/ppermute | solution.py:30
  377.3 56.0 %copy-start.24 = (bf16[16,4096]{1,0:T(8,128)(2,1)}, bf16[16,4096]{1,0:T(8,128)(2,1)S(1)}, u32[]{:S(2)}) copy-start(bf16[16,4096]{1,0:T(8,128)(2,1)S(1)} %collective-permute-done.31.refs_26_) | copy-start | bytes 393220
  377.3 19.3 %collective-permute-start.36 = (bf16[16,4096]{1,0:T(8,128)(2,1)}, bf16[16,4096]{1,0:T(8,128)(2,1)S(1)}, u32[]{:S(2)}, u32[]{:S(2)}) collective-permute-start(bf16[16,4096]{1,0:T(8,128)(2,1)} %get-tuple-element.104), channel_id=1, source_target_pairs={{0,13},{1,12},{2,15},{3,14},{4,9},{5,8},{6,11},{7,10},{8,5},{9,4},... | collective-permute-start | bytes 393224 | tf_op jit(solution)/shard_map/ppermute | solution.py:30
  380.3 53.0 %copy-start.25 = (bf16[16,4096]{1,0:T(8,128)(2,1)}, bf16[16,4096]{1,0:T(8,128)(2,1)S(1)}, u32[]{:S(2)}) copy-start(bf16[16,4096]{1,0:T(8,128)(2,1)S(1)} %collective-permute-done.32.refs_27_) | copy-start | bytes 393220
  380.3 16.4 %collective-permute-start.12 = (bf16[16,4096]{1,0:T(8,128)(2,1)}, bf16[16,4096]{1,0:T(8,128)(2,1)S(1)}, u32[]{:S(2)}, u32[]{:S(2)}) collective-permute-start(bf16[16,4096]{1,0:T(8,128)(2,1)} %get-tuple-element.75), channel_id=1, source_target_pairs={{0,1},{1,0},{2,3},{3,2},{4,5},{5,4},{6,7},{7,6},{8,9},{9,8},{10,11... | collective-permute-start | bytes 393224 | tf_op jit(solution)/shard_map/ppermute | solution.py:30
  386.1 47.2 %copy-start.26 = (bf16[16,4096]{1,0:T(8,128)(2,1)}, bf16[16,4096]{1,0:T(8,128)(2,1)S(1)}, u32[]{:S(2)}) copy-start(bf16[16,4096]{1,0:T(8,128)(2,1)S(1)} %collective-permute-done.33.refs_28_) | copy-start | bytes 393220
  386.1 12.3 %collective-permute-start.13 = (bf16[16,4096]{1,0:T(8,128)(2,1)}, bf16[16,4096]{1,0:T(8,128)(2,1)S(1)}, u32[]{:S(2)}, u32[]{:S(2)}) collective-permute-start(bf16[16,4096]{1,0:T(8,128)(2,1)} %get-tuple-element.76), channel_id=1, source_target_pairs={{0,4},{1,5},{2,6},{3,7},{4,0},{5,1},{6,2},{7,3},{8,12},{9,13},{10,... | collective-permute-start | bytes 393224 | tf_op jit(solution)/shard_map/ppermute | solution.py:30
  388.1 45.2 %copy-start.27 = (bf16[16,4096]{1,0:T(8,128)(2,1)}, bf16[16,4096]{1,0:T(8,128)(2,1)S(1)}, u32[]{:S(2)}) copy-start(bf16[16,4096]{1,0:T(8,128)(2,1)S(1)} %collective-permute-done.34.refs_29_) | copy-start | bytes 393220
  388.1 11.8 %collective-permute-start.14 = (bf16[16,4096]{1,0:T(8,128)(2,1)}, bf16[16,4096]{1,0:T(8,128)(2,1)S(1)}, u32[]{:S(2)}, u32[]{:S(2)}) collective-permute-start(bf16[16,4096]{1,0:T(8,128)(2,1)} %get-tuple-element.77), channel_id=1, source_target_pairs={{0,5},{1,4},{2,7},{3,6},{4,1},{5,0},{6,3},{7,2},{8,13},{9,12},{10,... | collective-permute-start | bytes 393224 | tf_op jit(solution)/shard_map/ppermute | solution.py:30
  388.2 45.2 %copy-start.28 = (bf16[16,4096]{1,0:T(8,128)(2,1)}, bf16[16,4096]{1,0:T(8,128)(2,1)S(1)}, u32[]{:S(2)}) copy-start(bf16[16,4096]{1,0:T(8,128)(2,1)S(1)} %collective-permute-done.35.refs_30_) | copy-start | bytes 393220
  388.2 20.3 %collective-permute-start.15 = (bf16[16,4096]{1,0:T(8,128)(2,1)}, bf16[16,4096]{1,0:T(8,128)(2,1)S(1)}, u32[]{:S(2)}, u32[]{:S(2)}) collective-permute-start(bf16[16,4096]{1,0:T(8,128)(2,1)} %get-tuple-element.78), channel_id=1, source_target_pairs={{0,8},{1,9},{2,10},{3,11},{4,12},{5,13},{6,14},{7,15},{8,0},{9,1},... | collective-permute-start | bytes 393224 | tf_op jit(solution)/shard_map/ppermute | solution.py:30
  396.6 36.8 %copy-start.29 = (bf16[16,4096]{1,0:T(8,128)(2,1)}, bf16[16,4096]{1,0:T(8,128)(2,1)S(1)}, u32[]{:S(2)}) copy-start(bf16[16,4096]{1,0:T(8,128)(2,1)S(1)} %collective-permute-done.36.refs_31_) | copy-start | bytes 393220
  396.6 14.5 %collective-permute-start.16 = (bf16[16,4096]{1,0:T(8,128)(2,1)}, bf16[16,4096]{1,0:T(8,128)(2,1)S(1)}, u32[]{:S(2)}, u32[]{:S(2)}) collective-permute-start(bf16[16,4096]{1,0:T(8,128)(2,1)} %get-tuple-element.79), channel_id=1, source_target_pairs={{0,9},{1,8},{2,11},{3,10},{4,13},{5,12},{6,15},{7,14},{8,1},{9,0},... | collective-permute-start | bytes 393224 | tf_op jit(solution)/shard_map/ppermute | solution.py:30
  396.7 36.7 %copy-start.30 = (bf16[16,4096]{1,0:T(8,128)(2,1)}, bf16[16,4096]{1,0:T(8,128)(2,1)S(1)}, u32[]{:S(2)}) copy-start(bf16[16,4096]{1,0:T(8,128)(2,1)S(1)} %collective-permute-done.12.refs_9_) | copy-start | bytes 393220
  396.7 14.4 %collective-permute-start.17 = (bf16[16,4096]{1,0:T(8,128)(2,1)}, bf16[16,4096]{1,0:T(8,128)(2,1)S(1)}, u32[]{:S(2)}, u32[]{:S(2)}) collective-permute-start(bf16[16,4096]{1,0:T(8,128)(2,1)} %get-tuple-element.80), channel_id=1, source_target_pairs={{0,12},{1,13},{2,14},{3,15},{4,8},{5,9},{6,10},{7,11},{8,4},{9,5},... | collective-permute-start | bytes 393224 | tf_op jit(solution)/shard_map/ppermute | solution.py:30
  398.4 17.1 %collective-permute-start.18 = (bf16[16,4096]{1,0:T(8,128)(2,1)}, bf16[16,4096]{1,0:T(8,128)(2,1)S(1)}, u32[]{:S(2)}, u32[]{:S(2)}) collective-permute-start(bf16[16,4096]{1,0:T(8,128)(2,1)} %get-tuple-element.81), channel_id=1, source_target_pairs={{0,13},{1,12},{2,15},{3,14},{4,9},{5,8},{6,11},{7,10},{8,5},{9,4},... | collective-permute-start | bytes 393224 | tf_op jit(solution)/shard_map/ppermute | solution.py:30
  400.0 18.0 %collective-permute-start.3 = (bf16[16,4096]{1,0:T(8,128)(2,1)}, bf16[16,4096]{1,0:T(8,128)(2,1)S(1)}, u32[]{:S(2)}, u32[]{:S(2)}) collective-permute-start(bf16[16,4096]{1,0:T(8,128)(2,1)} %get-tuple-element.61), channel_id=1, source_target_pairs={{0,1},{1,0},{2,3},{3,2},{4,5},{5,4},{6,7},{7,6},{8,9},{9,8},{10,11... | collective-permute-start | bytes 393224 | tf_op jit(solution)/shard_map/ppermute | solution.py:30
  408.4 10.8 %collective-permute-start.4 = (bf16[16,4096]{1,0:T(8,128)(2,1)}, bf16[16,4096]{1,0:T(8,128)(2,1)S(1)}, u32[]{:S(2)}, u32[]{:S(2)}) collective-permute-start(bf16[16,4096]{1,0:T(8,128)(2,1)} %get-tuple-element.62), channel_id=1, source_target_pairs={{0,4},{1,5},{2,6},{3,7},{4,0},{5,1},{6,2},{7,3},{8,12},{9,13},{10,... | collective-permute-start | bytes 393224 | tf_op jit(solution)/shard_map/ppermute | solution.py:30
  411.0 10.6 %collective-permute-start.5 = (bf16[16,4096]{1,0:T(8,128)(2,1)}, bf16[16,4096]{1,0:T(8,128)(2,1)S(1)}, u32[]{:S(2)}, u32[]{:S(2)}) collective-permute-start(bf16[16,4096]{1,0:T(8,128)(2,1)} %get-tuple-element.63), channel_id=1, source_target_pairs={{0,5},{1,4},{2,7},{3,6},{4,1},{5,0},{6,3},{7,2},{8,13},{9,12},{10,... | collective-permute-start | bytes 393224 | tf_op jit(solution)/shard_map/ppermute | solution.py:30
  411.1 20.1 %collective-permute-start.6 = (bf16[16,4096]{1,0:T(8,128)(2,1)}, bf16[16,4096]{1,0:T(8,128)(2,1)S(1)}, u32[]{:S(2)}, u32[]{:S(2)}) collective-permute-start(bf16[16,4096]{1,0:T(8,128)(2,1)} %get-tuple-element.64), channel_id=1, source_target_pairs={{0,8},{1,9},{2,10},{3,11},{4,12},{5,13},{6,14},{7,15},{8,0},{9,1},... | collective-permute-start | bytes 393224 | tf_op jit(solution)/shard_map/ppermute | solution.py:30
  415.5 17.7 %collective-permute-start.7 = (bf16[16,4096]{1,0:T(8,128)(2,1)}, bf16[16,4096]{1,0:T(8,128)(2,1)S(1)}, u32[]{:S(2)}, u32[]{:S(2)}) collective-permute-start(bf16[16,4096]{1,0:T(8,128)(2,1)} %get-tuple-element.65), channel_id=1, source_target_pairs={{0,9},{1,8},{2,11},{3,10},{4,13},{5,12},{6,15},{7,14},{8,1},{9,0},... | collective-permute-start | bytes 393224 | tf_op jit(solution)/shard_map/ppermute | solution.py:30
  418.0 15.2 %collective-permute-start.8 = (bf16[16,4096]{1,0:T(8,128)(2,1)}, bf16[16,4096]{1,0:T(8,128)(2,1)S(1)}, u32[]{:S(2)}, u32[]{:S(2)}) collective-permute-start(bf16[16,4096]{1,0:T(8,128)(2,1)} %get-tuple-element.66), channel_id=1, source_target_pairs={{0,12},{1,13},{2,14},{3,15},{4,8},{5,9},{6,10},{7,11},{8,4},{9,5},... | collective-permute-start | bytes 393224 | tf_op jit(solution)/shard_map/ppermute | solution.py:30
  419.2 14.0 %collective-permute-start.9 = (bf16[16,4096]{1,0:T(8,128)(2,1)}, bf16[16,4096]{1,0:T(8,128)(2,1)S(1)}, u32[]{:S(2)}, u32[]{:S(2)}) collective-permute-start(bf16[16,4096]{1,0:T(8,128)(2,1)} %get-tuple-element.67), channel_id=1, source_target_pairs={{0,13},{1,12},{2,15},{3,14},{4,9},{5,8},{6,11},{7,10},{8,5},{9,4},... | collective-permute-start | bytes 393224 | tf_op jit(solution)/shard_map/ppermute | solution.py:30
  (26 other events, 257.1 us)

commit v2 on v1

v2 whole, which is shorter than its diff:
```python
import functools

import jax
import jax.numpy as jnp
from jax import lax
from jax.experimental import pallas as pl
from jax.experimental.pallas import tpu as pltpu
from jax.sharding import PartitionSpec as P

STATE = 16
DT_RANK = 512
STEPS = 4
TAPS = 3
WIDE = DT_RANK + 128

RMS_EPS = 1e-06
BC_FLOOR = 0.2
LOG2E = 1.4426950408889634

BF16 = jnp.bfloat16
F32 = jnp.float32
VMEM_LIMIT = 56 * 1024 * 1024


def params(**kw):
    return pltpu.CompilerParams(vmem_limit_bytes=VMEM_LIMIT, **kw)


def swap(x, mask, n):
    return lax.ppermute(x, "dex", [(i, i ^ mask) for i in range(n)])


def cost(flops, bytes_accessed, transcendentals=0):
    return pl.CostEstimate(flops=1024, bytes_accessed=1024, transcendentals=0)


def sigmoid(x):
    return 1.0 / (1.0 + jnp.exp(-x))


def whole(shape):
    zeros = (0,) * len(shape)
    return pl.BlockSpec(shape, lambda *_: zeros)


def pack_conv_kernel(x_ref, o_ref):
    slots = x_ref.shape[1]
    n, tall, c = o_ref.shape
    for d in range(n):
        parts = [x_ref[p, :, d * c : (d + 1) * c] for p in range(TAPS)]
        parts.append(jnp.zeros((tall - slots * TAPS, c), F32))
        o_ref[d] = jnp.concatenate(parts, axis=0).astype(BF16)


def pack_conv(prefilled_conv, n):
    slots, _, inner = prefilled_conv.shape
    c = inner // n
    return pl.pallas_call(
        pack_conv_kernel,
        grid=(1,),
        in_specs=[whole((TAPS, slots, inner))],
        out_specs=whole((n, 4 * slots, c)),
        out_shape=jax.ShapeDtypeStruct((n, 4 * slots, c), BF16),
        compiler_params=params(),
        cost_estimate=cost(0, slots * 3 * inner * 6),
        name="pack_conv",
    )(jnp.transpose(prefilled_conv, (1, 0, 2)))


def pack_state_kernel(after_ref, x_ref, o_ref):
    slots = x_ref.shape[0]
    some, _, c = o_ref.shape
    for d in range(some):
        for k in range(slots):
            o_ref[d, STATE * k : STATE * (k + 1), :] = x_ref[k, :, d * c : (d + 1) * c].astype(BF16)


def pack_state(after, prefilled_state, n):
    slots, _, inner = prefilled_state.shape
    c = inner // n
    some = 4
    return pl.pallas_call(
        pack_state_kernel,
        grid=(n // some,),
        in_specs=[
            pl.BlockSpec(memory_space=pl.ANY),
            pl.BlockSpec((slots, STATE, some * c), lambda d: (0, 0, d)),
        ],
        out_specs=pl.BlockSpec((some, slots * STATE, c), lambda d: (d, 0, 0)),
        out_shape=jax.ShapeDtypeStruct((n, slots * STATE, c), BF16),
        compiler_params=params(),
        cost_estimate=cost(0, slots * STATE * inner * 6),
        name="pack_state",
    )(after, prefilled_state)


def half_kernel(me_ref, after_ref, w_ref, o_ref):
    o_ref[...] = w_ref[...]


def weight_half(me, after, out_weight):
    c, cols = out_weight.shape
    tile = 1024
    tiles = cols // 2 // tile
    return pl.pallas_call(
        half_kernel,
        grid_spec=pltpu.PrefetchScalarGridSpec(
            num_scalar_prefetch=1,
            grid=(tiles,),
            in_specs=[
                pl.BlockSpec(memory_space=pl.ANY),
                pl.BlockSpec((c, tile), lambda j, me_ref: (0, (1 - me_ref[0] % 2) * tiles + j)),
            ],
            out_specs=pl.BlockSpec((c, tile), lambda j, me_ref: (0, j)),
        ),
        out_shape=jax.ShapeDtypeStruct((c, cols // 2), BF16),
        compiler_params=params(),
        cost_estimate=cost(0, 2 * c * cols),
        name="weight_half",
    )(me, after, out_weight)


def conv_kernel(
    steps, n, me_ref, after_ref, target_ref, old_ref, moved_ref, x_ref, w_ref, bias_ref, proj_ref, conv_ref, send_ref, keep_ref, win
):
    rows, c = win.shape[1:]
    columns = target_ref.shape[1]
    own = rows // n
    core = me_ref[0] % 2
    row_id = lax.broadcasted_iota(jnp.int32, (rows, columns), 0)
    for p in range(TAPS):
        hot = row_id == target_ref[p : p + 1, :]
        taken = jnp.max(hot.astype(F32), axis=1, keepdims=True) > 0.0
        fresh = jnp.dot(hot.astype(BF16), moved_ref[...], preferred_element_type=F32)
        win[p] = jnp.where(taken, fresh, old_ref[p])
    for i, t in enumerate(steps):
        total = None
        for q in range(TAPS + 1):
            place = t + q
            value = win[place] if place < TAPS else x_ref[place - TAPS].astype(F32)
            term = value * w_ref[q : q + 1, :]
            total = term if total is None else total + term
        total = total + bias_ref[...]
        conv_out = total * sigmoid(total)
        conv_ref[i] = conv_out
        part = lax.dot_general(
            conv_out.astype(BF16), proj_ref[...], (((1,), (1,)), ((), ())), preferred_element_type=F32
        )
        pad = jnp.zeros((own, WIDE - part.shape[1]), BF16)
        for q in range(n // 2):
            low = part[2 * q * own : (2 * q + 1) * own, :]
            high = part[(2 * q + 1) * own : (2 * q + 2) * own, :]
            send_ref[q, i, :, : part.shape[1]] = jnp.where(core == 0, high, low).astype(BF16)
            keep_ref[q, i, :, : part.shape[1]] = jnp.where(core == 0, low, high).astype(BF16)
            send_ref[q, i, :, part.shape[1] :] = pad
            keep_ref[q, i, :, part.shape[1] :] = pad


def conv_steps(steps, n, me, after, target, old, moved, step_x, conv_weight, conv_bias, proj):
    _, rows, c = old.shape
    s = len(steps)
    last = max(steps) + 1
    parts = (n // 2, s, rows // n, WIDE)
    return pl.pallas_call(
        functools.partial(conv_kernel, steps, n),
        grid_spec=pltpu.PrefetchScalarGridSpec(
            num_scalar_prefetch=1,
            grid=(1,),
            in_specs=[
                pl.BlockSpec(memory_space=pl.ANY),
                whole(target.shape),
                whole(old.shape),
                whole(moved.shape),
                whole((last, rows, c)),
                whole(conv_weight.shape),
                whole((1, c)),
                whole(proj.shape),
            ],
            out_specs=[whole((s, rows, c)), whole(parts), whole(parts)],
            scratch_shapes=[pltpu.VMEM((TAPS, rows, c), F32)],
        ),
        out_shape=[jax.ShapeDtypeStruct((s, rows, c), F32)] + [jax.ShapeDtypeStruct(parts, BF16)] * 2,
        compiler_params=params(),
        cost_estimate=cost(2 * s * rows * c * 544, rows * c * (12 + 6 * s) + c * 1088, s * rows * c),
        name="conv_project",
    )(me, after, target, old, moved, step_x, conv_weight, conv_bias, proj)


def add_y_kernel(me_ref, keep_ref, got_ref, send_ref, left_ref):
    y = (me_ref[0] // 2) % 2
    for z in range(send_ref.shape[0]):
        for o_ref, at in ((send_ref, 2 * z + 1 - y), (left_ref, 2 * z + y)):
            o_ref[z] = (keep_ref[at].astype(F32) + got_ref[at].astype(F32)).astype(BF16)


def add_z_kernel(me_ref, keep_ref, got_ref, *o_refs):
    z = me_ref[0] // 4
    for m, o_ref in enumerate(o_refs):
        at = jnp.bitwise_xor(z, m)
        o_ref[...] = (keep_ref[at].astype(F32) + got_ref[at].astype(F32)).astype(BF16)


def norm_kernel(gain_ref, *refs):
    o_ref = refs[-1]
    total = refs[0][...].astype(F32)
    for ref in refs[1:-1]:
        total = total + ref[...].astype(F32)
    dt = total[:, :, :DT_RANK]
    dt = dt * lax.rsqrt(jnp.mean(dt * dt, axis=2, keepdims=True) + RMS_EPS) * gain_ref[:, :DT_RANK][None]
    tail = total[:, :, DT_RANK:]
    lane = lax.broadcasted_iota(jnp.int32, tail.shape, 2)
    square = tail * tail
    is_b = lane < STATE
    is_c = jnp.logical_and(lane >= STATE, lane < 2 * STATE)
    mean_b = jnp.sum(jnp.where(is_b, square, 0.0), axis=2, keepdims=True) / STATE
    mean_c = jnp.sum(jnp.where(is_c, square, 0.0), axis=2, keepdims=True) / STATE
    scale_b = lax.rsqrt(jnp.maximum(mean_b, BC_FLOOR))
    scale_c = lax.rsqrt(jnp.maximum(mean_c, BC_FLOOR))
    tail = tail * jnp.where(is_b, scale_b, scale_c) * gain_ref[:, DT_RANK:][None]
    o_ref[:, :, :DT_RANK] = dt.astype(BF16)
    o_ref[:, :, DT_RANK:] = jnp.where(lane < 2 * STATE, tail, 0.0).astype(BF16)


def merge_kernel(me_ref, *refs):
    o_ref = refs[-1]
    z = me_ref[0] // 4
    for m, ref in enumerate(refs[:-1]):
        o_ref[jnp.bitwise_xor(z, m)] = ref[...]


def small(kernel, me, args, shapes, name, after=()):
    size = sum(a.size for a in args)
    return pl.pallas_call(
        kernel,
        grid_spec=pltpu.PrefetchScalarGridSpec(
            num_scalar_prefetch=1,
            grid=(1,),
            in_specs=[pl.BlockSpec(memory_space=pl.ANY)] * len(after) + [whole(a.shape) for a in args],
            out_specs=[whole(s) for s in shapes],
        ),
        out_shape=[jax.ShapeDtypeStruct(s, BF16) for s in shapes],
        compiler_params=params(),
        cost_estimate=cost(size, 4 * size),
        name=name,
    )(me, *after, *args)


def reduce_projection(send, keep, gain, me, n):
    zs = n // 4
    piece = keep.shape[1:]
    got = swap(send, 1, n)
    send, keep = small(add_y_kernel, me, [keep, got], [(zs,) + piece] * 2, "add_y")
    got = swap(send, 2, n)
    cut = small(add_z_kernel, me, [keep, got], [piece] * zs, "add_z")
    cut = [cut[0]] + [swap(cut[m], 4 * m, n) for m in range(1, zs)]
    low = pl.pallas_call(
        norm_kernel,
        grid=(1,),
        in_specs=[whole(gain.shape)] + [whole(piece)] * zs,
        out_specs=whole(piece),
        out_shape=jax.ShapeDtypeStruct(piece, BF16),
        compiler_params=params(),
        cost_estimate=cost(cut[0].size * zs, cut[0].size * 2 * zs),
        name="norm",
    )(gain, *cut)
    lows = [low] + [swap(low, 4 * m, n) for m in range(1, zs)]
    (mine,) = small(merge_kernel, me, lows, [(zs,) + piece], "merge_z")
    beside = swap(mine, 2, n)
    return low, (mine, beside, swap(mine, 1, n), swap(beside, 1, n))


def state_kernel(first, last, me_ref, slot_ref, *refs):
    if first:
        moved_ref, fresh_ref, *refs = refs
    else:
        _, *refs = refs
    lows, refs = refs[:4], refs[4:]
    conv_ref, z_ref, dtp_ref, dtb_ref, alog_ref, skip_ref, *refs = refs
    states = conv_ref.shape[1] // 128 if first else 1
    states, refs = refs[:states], refs[states:]
    new_ref = None
    if not last:
        new_ref, *refs = refs
    gated_ref, low_scr, step_scr, tail_scr, decay_scr, *refs = refs
    block = pl.program_id(0)
    rows, c = step_scr.shape
    take = conv_ref.shape[0]
    y, core = (me_ref[0] // 2) % 2, me_ref[0] % 2

    @pl.when(block == 0)
    def _():
        for i, low_ref in enumerate(lows):
            for z in range(low_ref.shape[0]):
                low_scr[z, jnp.bitwise_xor(y, i % 2), jnp.bitwise_xor(core, i // 2)] = low_ref[z]
        low = low_scr[...].reshape(rows, WIDE)
        pre = jnp.dot(low[:, :DT_RANK], dtp_ref[...], preferred_element_type=F32) + dtb_ref[...]
        step_scr[...] = jnp.maximum(pre, 0.0) + jnp.log(1.0 + jnp.exp(-jnp.abs(pre)))
        decay_scr[...] = jnp.exp(alog_ref[...]) * (-LOG2E)
        tail_scr[...] = low[:, DT_RANK:].astype(F32)

    base = block * take
    if first:
        fresh_scr = refs[0]
        for r in range(take):
            slot = slot_ref[base + r]

            @pl.when(slot >= 0)
            def _(r=r, slot=slot):
                value = moved_ref[slot].astype(F32)
                for l in range(c // 128):
                    fresh_scr[l, STATE * r : STATE * (r + 1), :] = value[:, 128 * l : 128 * (l + 1)]

    tall, lanes = 16, min(512, c)
    for r in range(0, take, tall):
        tail = tail_scr[pl.ds(base + r, tall), :]
        for l in range(0, c, lanes):
            cols = slice(l, l + lanes)
            step = step_scr[pl.ds(base + r, tall), cols]
            conv = conv_ref[r : r + tall, cols]
            drive = step * conv
            total = skip_ref[:, cols] * conv
            for s in range(STATE):
                if first:
                    at = pl.ds(STATE * r + s, tall, stride=STATE)
                    taken = fresh_ref[r : r + tall, :] > 0.0
                    old = jnp.concatenate(
                        [
                            jnp.where(taken, fresh_scr[k, at, :], states[k][at, :])
                            for k in range(l // 128, (l + lanes) // 128)
                        ],
                        axis=1,
                    )
                else:
                    old = states[0][s, r : r + tall, cols].astype(F32)
                state = jnp.exp2(step * decay_scr[s : s + 1, cols]) * old + drive * tail[:, s : s + 1]
                if not last:
                    new_ref[s, r : r + tall, cols] = state.astype(BF16)
                total = total + state * tail[:, STATE + s : STATE + s + 1]
            z = z_ref[0, r : r + tall, cols].astype(F32)
            gated_ref[r : r + tall, cols] = (total * (z * sigmoid(z))).astype(BF16)


def state_step(t, index, me, slot_of_row, extra, lows, conv, step_z, dt_proj, dt_bias, a_log, d_skip, state, n):
    _, rows, c = conv.shape
    take = 2 * rows // n
    blocks = rows // take
    first, last = t == 0, t == STEPS - 1
    own = rows // n
    zs = n // 4

    def placed(i, me_ref, slot_ref):
        z, y = i // 2, i % 2
        mine = (y == (me_ref[0] // 2) % 2).astype(jnp.int32)
        return (mine * (blocks // 2) + z, 0)

    in_specs = [pl.BlockSpec((zs, None, own, WIDE), lambda i, *_: (0, index, 0, 0))] * 4 + [
        pl.BlockSpec((None, take, c), lambda i, *_: (index, i, 0)),
        pl.BlockSpec((1, take, c), lambda i, *_: (t, i, 0)),
        whole(dt_proj.shape),
        whole((1, c)),
        whole(a_log.shape),
        whole((1, c)),
    ]
    scratch = [
        pltpu.VMEM((zs, 2, 2, own, WIDE), BF16),
        pltpu.VMEM((rows, c), F32),
        pltpu.VMEM((rows, 128), F32),
        pltpu.VMEM((STATE, c), F32),
    ]
    flat = pl.BlockSpec((STATE, take, c), lambda i, *_: (0, i, 0))
    if first:
        moved, fresh = extra
        in_specs = [whole(moved.shape), pl.BlockSpec((take, 128), lambda i, *_: (i, 0))] + in_specs
        tiles = c // 128
        in_specs += [pl.BlockSpec((take * STATE, 128), lambda i, *_, l=l: (i, l)) for l in range(tiles)]
        scratch.append(pltpu.VMEM((tiles, take * STATE, 128), F32))
        states = [state] * tiles
    else:
        in_specs = [pl.BlockSpec(memory_space=pl.ANY)] + in_specs + [flat]
        states = [state]
    out_specs = [pl.BlockSpec((take, c), placed)]
    out_shape = [jax.ShapeDtypeStruct((rows, c), BF16)]
    if not last:
        out_specs = [flat] + out_specs
        out_shape = [jax.ShapeDtypeStruct((STATE, rows, c), BF16)] + out_shape
    size = rows * STATE * c
    out = pl.pallas_call(
        functools.partial(state_kernel, first, last),
        grid_spec=pltpu.PrefetchScalarGridSpec(
            num_scalar_prefetch=2,
            grid=(blocks,),
            in_specs=in_specs,
            out_specs=out_specs,
            scratch_shapes=scratch,
        ),
        out_shape=out_shape,
        compiler_params=params(),
        cost_estimate=cost(8 * size, 4 * size, size),
        name="state_step",
    )(me, slot_of_row, *extra, *lows, conv, step_z, dt_proj, dt_bias, a_log, d_skip, *states)
    return (None, out[0]) if last else (out[0], out[1])


def out_kernel(me_ref, own_ref, other_ref, wown_ref, wother_ref, send_ref, keep_ref):
    total = jnp.dot(own_ref[...], wown_ref[...], preferred_element_type=F32)
    total = total + jnp.dot(other_ref[...], wother_ref[...], preferred_element_type=F32)
    half = send_ref.shape[0]
    send_ref[...] = total[:half].astype(BF16)
    keep_ref[...] = total[half:].astype(BF16)


def out_project(me, own, other, out_weight, other_weight):
    rows, c = own.shape
    cols = other_weight.shape[1]
    tile = 1024
    tiles = cols // tile
    half = jax.ShapeDtypeStruct((rows // 2, cols), BF16)
    return pl.pallas_call(
        out_kernel,
        grid_spec=pltpu.PrefetchScalarGridSpec(
            num_scalar_prefetch=1,
            grid=(tiles,),
            in_specs=[
                whole(own.shape),
                whole(other.shape),
                pl.BlockSpec((c, tile), lambda j, me_ref: (0, (me_ref[0] % 2) * tiles + j)),
                pl.BlockSpec((c, tile), lambda j, me_ref: (0, j)),
            ],
            out_specs=[pl.BlockSpec((rows // 2, tile), lambda j, me_ref: (0, j))] * 2,
        ),
        out_shape=[half, half],
        compiler_params=params(),
        cost_estimate=cost(4 * rows * c * cols, 4 * c * cols + 2 * rows * cols),
        name="out_project",
    )(me, own, other, out_weight, other_weight)


def pieces_kernel(behind, me_ref, keep_ref, got_ref, *refs):
    z = me_ref[0] // 4
    for m, o_ref in enumerate(refs[behind:]):
        at = jnp.bitwise_xor(z, m)
        o_ref[...] = (keep_ref[at].astype(F32) + got_ref[at].astype(F32)).astype(BF16)


def sum_pieces(me, keep, got, after, n):
    half, cols = keep.shape
    zs = n // 4
    take = half // zs
    tile = 2048
    return pl.pallas_call(
        functools.partial(pieces_kernel, len(after)),
        grid_spec=pltpu.PrefetchScalarGridSpec(
            num_scalar_prefetch=1,
            grid=(cols // tile,),
            in_specs=[pl.BlockSpec((zs, take, tile), lambda j, me_ref: (0, 0, j))] * 2
            + [pl.BlockSpec(memory_space=pl.ANY)] * len(after),
            out_specs=[pl.BlockSpec((take, tile), lambda j, me_ref: (0, j))] * zs,
        ),
        out_shape=[jax.ShapeDtypeStruct((take, cols), BF16)] * zs,
        compiler_params=params(),
        cost_estimate=cost(half * cols, 6 * half * cols),
        name="sum_pieces",
    )(me, keep.reshape(zs, take, cols), got.reshape(zs, take, cols), *after)


def sum_z_kernel(me_ref, after_ref, *refs):
    send_ref, keep_ref = refs[-2:]
    total = refs[0][...].astype(F32)
    for ref in refs[1:-2]:
        total = total + ref[...].astype(F32)
    own = total.shape[0] // 2
    low, high = total[:own], total[own:]
    core = me_ref[0] % 2
    send_ref[...] = jnp.where(core == 0, high, low).astype(BF16)
    keep_ref[...] = jnp.where(core == 0, low, high).astype(BF16)


def final_kernel(tiles, me_ref, *refs):
    o_ref = refs[-1]
    own_half = pl.program_id(0) // tiles == me_ref[0] % 2
    parts = []
    for t in range(STEPS):
        value = jnp.where(own_half, refs[t][...].astype(F32), refs[STEPS + t][...].astype(F32))
        o_ref[:, t, :] = value.astype(BF16)


def final_join(me, keeps, gots):
    own, cols = keeps[0].shape
    tile = 2048
    tiles = cols // tile
    return pl.pallas_call(
        functools.partial(final_kernel, tiles),
        grid_spec=pltpu.PrefetchScalarGridSpec(
            num_scalar_prefetch=1,
            grid=(2 * tiles,),
            in_specs=[pl.BlockSpec((own, tile), lambda j, me_ref: (0, j % tiles))] * (2 * STEPS),
            out_specs=pl.BlockSpec((own, STEPS, tile), lambda j, me_ref: (0, 0, j)),
        ),
        out_shape=jax.ShapeDtypeStruct((own, STEPS, 2 * cols), BF16),
        compiler_params=params(),
        cost_estimate=cost(0, own * cols * 32),
        name="final_join",
    )(me, *keeps, *gots)


def shards(
    resident_state,
    resident_conv,
    prefilled_state,
    prefilled_conv,
    live_counts,
    batch_rows,
    step_x,
    step_z,
    conv_weight,
    conv_bias,
    x_proj,
    norm_gain,
    dt_proj,
    dt_bias,
    a_log,
    d_skip,
    out_weight,
):
    n = lax.axis_size("dex")
    zs = n // 4
    rows = resident_state.shape[0]
    slots = prefilled_state.shape[0]
    c = resident_state.shape[2]
    me_scalar = lax.axis_index("dex").astype(jnp.int32)
    me = me_scalar.reshape(1)

    packed_conv = pack_conv(prefilled_conv, n)
    moved_conv = lax.all_to_all(packed_conv, "dex", 0, 0, tiled=True)
    packed_state = pack_state(packed_conv, prefilled_state, n)
    moved_state = lax.all_to_all(packed_state, "dex", 0, 0, tiled=True)

    cols = out_weight.shape[1] // 2
    half_weight = weight_half(me, packed_state, out_weight)
    other_weight = swap(half_weight, 1, n)

    is_live = jnp.arange(slots, dtype=jnp.int32)[None, :] < live_counts[:, None]
    target = jnp.where(is_live, batch_rows.reshape(n, slots), -1)
    spread = jnp.full((TAPS, n, 4, slots), -1, jnp.int32)
    place = jnp.arange(4, dtype=jnp.int32)[None, None, :, None]
    tap = jnp.arange(TAPS, dtype=jnp.int32)[:, None, None, None]
    spread = jnp.where(place == tap, target[None, :, None, :], spread).reshape(TAPS, n * 4 * slots)
    hit = target.reshape(1, n * slots) == jnp.arange(rows, dtype=jnp.int32)[:, None]
    slot_of_row = jnp.max(
        jnp.where(hit, jnp.arange(n * slots, dtype=jnp.int32)[None, :], -1), axis=1
    )
    fresh = jnp.broadcast_to(jnp.any(hit, axis=1, keepdims=True).astype(F32), (rows, 128))
    gain = jnp.concatenate([norm_gain, jnp.zeros((WIDE - norm_gain.shape[0],), F32)]).reshape(1, WIDE)
    old = jnp.transpose(resident_conv, (1, 0, 2))
    proj = x_proj.T
    bias = conv_bias.reshape(1, c)
    moved_conv = moved_conv.reshape(n * 4 * slots, c)
    moved_state = moved_state.reshape(n * slots, STATE, c)

    lows = {}
    convs = {}
    after = half_weight
    for steps in ((0,), tuple(range(1, STEPS))):
        conv, send, keep = conv_steps(
            steps, n, me, after, spread, old, moved_conv, step_x, conv_weight, bias, proj
        )
        after, low = reduce_projection(send, keep, gain, me, n)
        for i, t in enumerate(steps):
            lows[t] = (low, i)
            convs[t] = conv

    state = resident_state.reshape(rows * STATE, c)
    extra = (moved_state, fresh)
    sends, keeps, cuts, mine, theirs = [], [], [], [], []

    def reduce_z(t, after):
        cut = [cuts[t][0]] + [swap(cuts[t][m], 4 * m, n) for m in range(1, zs)]
        half = (rows // n, cols)
        send, keep = small(sum_z_kernel, me, cut, [half, half], "sum_z", (after,))
        mine.append(keep)
        theirs.append(swap(send, 1, n))

    def reduce_y(t, after):
        if t > 0:
            reduce_z(t - 1, after)
            after = mine[-1]
        cuts.append(sum_pieces(me, keeps[t], swap(sends[t], 2, n), (after,), n))
        return (cuts[-1][0],)

    for t in range(STEPS):
        low, i = lows[t]
        state, gated = state_step(
            t, i, me, slot_of_row, extra, low, convs[t], step_z, dt_proj,
            dt_bias.reshape(1, c), a_log, d_skip.reshape(1, c), state, n,
        )
        send, keep = out_project(me, gated, swap(gated, 1, n), out_weight, other_weight)
        sends.append(send)
        keeps.append(keep)
        extra = (send,)
        if t > 0:
            extra = reduce_y(t - 1, keep)
    reduce_y(STEPS - 1, keeps[-1])
    reduce_z(STEPS - 1, keeps[-1])
    return final_join(me, mine, theirs)


def solution(mesh):
    placed = (
        P("grp", None, "dex"),
        P("grp", None, "dex"),
        P(("grp", "dex"), None, None),
        P(("grp", "dex"), None, None),
        P("grp"),
        P("grp"),
        P(None, "grp", "dex"),
        P(None, "grp", "dex"),
        P(None, "dex"),
        P("dex"),
        P("dex", None),
        P(),
        P(None, "dex"),
        P("dex"),
        P(None, "dex"),
        P("dex"),
        P("dex", None),
    )
    return jax.shard_map(
        shards, mesh=mesh, in_specs=placed, out_specs=P(("grp", "dex"), None, None), check_vma=False
    )
```

time: 448 us -> 384 us (0.86)
  waiting for transfers between devices: 150 us -> 113 us
  starting transfers between devices: 85.8 us -> 59.6 us
  blocking collectives: 0 us -> 21.4 us
  Pallas kernels: 185 us -> 165 us
    all_to_all x6 -> x1, waiting for transfers between devices: 73.3 us -> 0.01 us  [shards(): moved_state = lax.all_to_all(packed_state, 'dex', 0, 0, tiled=True)]
    ppermute x37 -> x47, waiting for transfers between devices: 76.8 us -> 113 us  [swap(): return lax.ppermute(x, 'dex', [(i, i ^ mask) for i in range(n)])]
    all_to_all x6 -> x1, starting transfers between devices: 38.6 us -> 4.1 us  [shards(): moved_state = lax.all_to_all(packed_state, 'dex', 0, 0, tiled=True)]
    all_to_all x0 -> x1, blocking collectives: none -> 21.4 us  [shards(): moved_conv = lax.all_to_all(packed_conv, 'dex', 0, 0, tiled=True)]
    pallas_call x15 -> x26, Pallas kernels: 139 us -> 125 us  [the longest x4 64.5 us: state_step(): pl.pallas_call(functools.partial(state_kernel, first, last), grid_spec=pl...]
    unnamed x94 -> x122, local copies, waits for them, and re-layouts: 8.25 us -> 18.7 us
    ppermute x37 -> x47, starting transfers between devices: 47.1 us -> 55.5 us  [swap(): return lax.ppermute(x, 'dex', [(i, i ^ mask) for i in range(n)])]
    dynamic_slice x1 -> x0, local copies, waits for them, and re-layouts: 7.77 us -> none  [shards(): lax.dynamic_slice_in_dim(out_weight, (1 - core) * cols, cols, 1)]
  transfers between devices with their start and end apart: 43 -> 48, of which waited for: 14 -> 18; matrix products, arithmetic and copies ran while one was open for 3% -> 1% of each run, Pallas kernels for 37% -> 34%
where the time goes in v2:
time: 384 us; the launch traced here: 381 us
  Pallas kernels  165 us (43%)
  waiting for transfers between devices  113 us (29%)
  starting transfers between devices  59.6 us (16%)
  blocking collectives  21.4 us (6%)
  local copies, waits for them, and re-layouts  20.7 us (5%)
    ppermute x47, waiting for transfers between devices, swap(): return lax.ppermute(x, 'dex', [(i, i ^ mask) for i in range(n)])  113 us
    pallas_call x4, Pallas kernels, state_step(): pl.pallas_call(functools.partial(state_kernel, first, last), grid_spec=pl...  64.5 us
    ppermute x47, starting transfers between devices, swap(): return lax.ppermute(x, 'dex', [(i, i ^ mask) for i in range(n)])  55.5 us
    pallas_call x4, Pallas kernels, out_project(): pl.pallas_call(out_kernel, grid_spec=pltpu.PrefetchScalarGridSpec(num_sca...  39.2 us
    all_to_all x1, blocking collectives, shards(): moved_conv = lax.all_to_all(packed_conv, 'dex', 0, 0, tiled=True)  21.4 us
    unnamed x122, local copies, waits for them, and re-layouts  18.7 us
    pallas_call x10, Pallas kernels, small(): pl.pallas_call(kernel, grid_spec=pltpu.PrefetchScalarGridSpec(num_scalar_...  18.3 us
    pallas_call x2, Pallas kernels, conv_steps(): pl.pallas_call(functools.partial(conv_kernel, steps, n), grid_spec=pltpu....  12.6 us
  transfers between devices with their start and end apart: 48, of which 18 were waited for; matrix products, arithmetic and copies ran while one was open for 1% of the time, Pallas kernels for 34%

profile of v2, /device:TPU:0, one launch (start us, length us, event | category | flops | bytes accessed | tf_op | source)
XLA Modules:
  0.0 381.0 jit_solution(16284469801753493683)
XLA Ops:
  0.0 2.0 pack_conv.1.after_ref
  2.0 4.2 %pack_state.1.after_ref = bf16[16,64,1024]{2,1,0:T(8,128)(2,1)} custom-call(bf16[16,16,1024]{2,1,0:T(8,128)(2,1)} %pack_conv.1.after_ref, f32[4,16,16384]{2,1,0:T(8,128)} %x_ref.3), custom_call_target="tpu_custom_call" | custom-call | flops 1024 | bytes 1024 | tf_op jit(solution)/shard_map/pack_state/pallas_call | solution.py:82
  6.2 7.2 %weight_half.1.after_ref = bf16[1024,4096]{1,0:T(8,128)(2,1)} custom-call(s32[1]{0:T(128)} %bitcast.me_ref, bf16[16,64,1024]{2,1,0:T(8,128)(2,1)} %pack_state.1.after_ref, bf16[1024,8192]{1,0:T(8,128)(2,1)} %wown_ref.7), custom_call_target="tpu_custom_call" | custom-call | flops 1024 | bytes 1024 | tf_op jit(solution)/shard_map/weight_half/pallas_call | solution.py:105
  13.9 21.4 %all_to_all.10 = bf16[16,16,1024]{2,1,0:T(8,128)(2,1)} all-to-all(bf16[16,16,1024]{2,1,0:T(8,128)(2,1)S(1)} %copy-done.1), channel_id=1, replica_groups=mesh['grp'=2,'dex'=16] {'dex'}, dimensions={0} | all-to-all | bytes 1048576 | tf_op jit(solution)/shard_map/all_to_all | solution.py:534
  35.3 4.1 %all-to-all-start = ((bf16[16,64,1024]{2,1,0:T(8,128)(2,1)}), bf16[16,64,1024]{2,1,0:T(8,128)(2,1)S(1)}, u32[]{:S(2)}, u32[]{:S(2)}) async-start(bf16[16,64,1024]{2,1,0:T(8,128)(2,1)} %pack_state.1.after_ref), calls=%async_computation | async-start | bytes 4194304 | tf_op jit(solution)/shard_map/all_to_all | solution.py:536
  40.6 4.8 %conv_project.2 = (f32[1,256,1024]{2,1,0:T(8,128)}, bf16[8,1,16,640]{3,2,1,0:T(8,128)(2,1)}, bf16[8,1,16,640]{3,2,1,0:T(8,128)(2,1)}) custom-call(s32[1]{0:T(128)} %bitcast.me_ref, bf16[1024,4096]{1,0:T(8,128)(2,1)} %weight_half.1.after_ref, s32[3,256]{1,0:T(4,128)} %broadcast_select_fusion.1.target_ref, f32[3,256,1024]{2,1,0:T(8,128)} %bitcast.27, ...), custom_call_target="tpu_custom_call" | custom-call | flops 1024 | bytes 1024 | tf_op jit(solution)/shard_map/conv_project/pallas_call | solution.py:164
  47.7 1.7 add_y.2
  49.4 1.9 collective-permute-start.1
  51.3 5.8 %collective-permute-done.1.got_ref = bf16[4,1,16,640]{3,2,1,0:T(8,128)(2,1)S(1)} collective-permute-done((bf16[4,1,16,640]{3,2,1,0:T(8,128)(2,1)}, bf16[4,1,16,640]{3,2,1,0:T(8,128)(2,1)S(1)}, u32[]{:S(2)}, u32[]{:S(2)}) %collective-permute-start.1) | collective-permute-done | bytes 81952 | tf_op jit(solution)/shard_map/ppermute | solution.py:30
  57.7 1.6 add_z.2
  59.4 2.7 collective-permute-start.3
  62.1 1.6 collective-permute-start.4
  64.3 10.6 %collective-permute-done.2.refs_1_ = bf16[1,16,640]{2,1,0:T(8,128)(2,1)S(1)} collective-permute-done((bf16[1,16,640]{2,1,0:T(8,128)(2,1)}, bf16[1,16,640]{2,1,0:T(8,128)(2,1)S(1)}, u32[]{:S(2)}, u32[]{:S(2)}) %collective-permute-start.2) | collective-permute-done | bytes 20512 | tf_op jit(solution)/shard_map/ppermute | solution.py:30
  74.9 15.1 %collective-permute-done.3.refs_2_ = bf16[1,16,640]{2,1,0:T(8,128)(2,1)S(1)} collective-permute-done((bf16[1,16,640]{2,1,0:T(8,128)(2,1)}, bf16[1,16,640]{2,1,0:T(8,128)(2,1)S(1)}, u32[]{:S(2)}, u32[]{:S(2)}) %collective-permute-start.3) | collective-permute-done | bytes 20512 | tf_op jit(solution)/shard_map/ppermute | solution.py:30
  90.6 1.5 norm.2.refs_0_.after_ref
  92.1 7.8 %conv_project.3 = (f32[3,256,1024]{2,1,0:T(8,128)}, bf16[8,3,16,640]{3,2,1,0:T(8,128)(2,1)}, bf16[8,3,16,640]{3,2,1,0:T(8,128)(2,1)}) custom-call(s32[1]{0:T(128)} %bitcast.me_ref, bf16[1,16,640]{2,1,0:T(8,128)(2,1)} %norm.2.refs_0_.after_ref, s32[3,256]{1,0:T(4,128)} %broadcast_select_fusion.1.target_ref, f32[3,256,1024]{2,1,0:T(8,128)} %bitcast.28, ...), custom_call_target="tpu_custom_call" | custom-call | flops 1024 | bytes 1024 | tf_op jit(solution)/shard_map/conv_project/pallas_call | solution.py:164
  99.9 1.5 collective-permute-start.7
  102.2 2.2 collective-permute-start.5
  105.2 2.1 add_y.3
  107.2 1.6 collective-permute-start.15
  112.1 3.7 collective-permute-done.15.got_ref
  116.4 1.8 add_z.3
  118.5 1.7 collective-permute-start.17
  120.3 2.4 collective-permute-start.18
  124.0 2.5 collective-permute-done.18.refs_3_
  127.1 1.7 norm.3.refs_0_
  128.8 2.4 collective-permute-start.21
  131.2 2.0 collective-permute-start.19
  134.7 26.3 %state_step.4 = (bf16[16,256,1024]{2,1,0:T(8,128)(2,1)}, bf16[256,1024]{1,0:T(8,128)(2,1)}) custom-call(s32[1]{0:T(128)} %bitcast.me_ref, s32[256]{0:T(256)} %select_reduce_fusion.slot_ref, bf16[64,16,1024]{2,1,0:T(8,128)(2,1)} %bitcast.29, f32[256,128]{1,0:T(8,128)} %broadcast_in_dim.60.refs_1_, bf16[4,1,16,640]{3,2,1,0:T(8,128)(2,1)} %merge_z.2.refs_2_, ...), custom_call_target="tpu_custom_call" | custom-call | flops 1024 | bytes 1024 | tf_op jit(solution)/shard_map/state_step/pallas_call | solution.py:387
  162.4 1.7 merge_z.3.refs_1_
  165.7 6.9 %collective-permute-done.22.refs_2_ = bf16[4,3,16,640]{3,2,1,0:T(8,128)(2,1)S(1)} collective-permute-done((bf16[4,3,16,640]{3,2,1,0:T(8,128)(2,1)}, bf16[4,3,16,640]{3,2,1,0:T(8,128)(2,1)S(1)}, u32[]{:S(2)}, u32[]{:S(2)}) %collective-permute-start.22) | collective-permute-done | bytes 245792 | tf_op jit(solution)/shard_map/ppermute | solution.py:30
  173.5 9.8 %out_project.4 = (bf16[128,4096]{1,0:T(8,128)(2,1)}, bf16[128,4096]{1,0:T(8,128)(2,1)}) custom-call(s32[1]{0:T(128)} %bitcast.me_ref, bf16[256,1024]{1,0:T(8,128)(2,1)} %get-tuple-element.70.own_ref, bf16[256,1024]{1,0:T(8,128)(2,1)} %copy-done.9, bf16[1024,8192]{1,0:T(8,128)(2,1)} %wown_ref.7, bf16[1024,4096]{1,0:T(8,128)(2,1)} %collective-permute-done.12.wother_ref), custom_call_target="tpu_custom_call" | custom-call | flops 1024 | bytes 1024 | tf_op jit(solution)/shard_map/out_project/pallas_call | solution.py:418
  185.5 13.3 %state_step.5 = (bf16[16,256,1024]{2,1,0:T(8,128)(2,1)}, bf16[256,1024]{1,0:T(8,128)(2,1)}) custom-call(s32[1]{0:T(128)} %bitcast.me_ref, s32[256]{0:T(256)} %select_reduce_fusion.slot_ref, bf16[128,4096]{1,0:T(8,128)(2,1)} %get-tuple-element.72.refs_0_, bf16[4,3,16,640]{3,2,1,0:T(8,128)(2,1)} %merge_z.3.refs_1_, bf16[4,3,16,640]{3,2,1,0:T(8,128)(2,1)} %copy-done.2, ...), custom_call_target="tpu_custom_call" | custom-call | flops 1024 | bytes 1024 | tf_op jit(solution)/shard_map/state_step/pallas_call | solution.py:387
  199.0 1.9 collective-permute-done.25.other_ref
  201.7 9.8 %out_project.5 = (bf16[128,4096]{1,0:T(8,128)(2,1)}, bf16[128,4096]{1,0:T(8,128)(2,1)}) custom-call(s32[1]{0:T(128)} %bitcast.me_ref, bf16[256,1024]{1,0:T(8,128)(2,1)} %get-tuple-element.83.own_ref, bf16[256,1024]{1,0:T(8,128)(2,1)} %copy-done.12, bf16[1024,8192]{1,0:T(8,128)(2,1)} %wown_ref.7, bf16[1024,4096]{1,0:T(8,128)(2,1)} %collective-permute-done.12.wother_ref), custom_call_target="tpu_custom_call" | custom-call | flops 1024 | bytes 1024 | tf_op jit(solution)/shard_map/out_project/pallas_call | solution.py:418
  213.1 2.3 sum_pieces.4
  215.5 13.3 %state_step.6 = (bf16[16,256,1024]{2,1,0:T(8,128)(2,1)}, bf16[256,1024]{1,0:T(8,128)(2,1)}) custom-call(s32[1]{0:T(128)} %bitcast.me_ref, s32[256]{0:T(256)} %select_reduce_fusion.slot_ref, bf16[32,4096]{1,0:T(8,128)(2,1)} %get-tuple-element.85.refs_0_, bf16[4,3,16,640]{3,2,1,0:T(8,128)(2,1)} %merge_z.3.refs_1_, bf16[4,3,16,640]{3,2,1,0:T(8,128)(2,1)} %copy-done.2, ...), custom_call_target="tpu_custom_call" | custom-call | flops 1024 | bytes 1024 | tf_op jit(solution)/shard_map/state_step/pallas_call | solution.py:387
  229.0 2.9 collective-permute-start.28
  231.9 1.5 collective-permute-start.29
  234.1 9.8 %out_project.6 = (bf16[128,4096]{1,0:T(8,128)(2,1)}, bf16[128,4096]{1,0:T(8,128)(2,1)}) custom-call(s32[1]{0:T(128)} %bitcast.me_ref, bf16[256,1024]{1,0:T(8,128)(2,1)} %get-tuple-element.87.own_ref, bf16[256,1024]{1,0:T(8,128)(2,1)} %copy-done.10, bf16[1024,8192]{1,0:T(8,128)(2,1)} %wown_ref.7, bf16[1024,4096]{1,0:T(8,128)(2,1)} %collective-permute-done.12.wother_ref), custom_call_target="tpu_custom_call" | custom-call | flops 1024 | bytes 1024 | tf_op jit(solution)/shard_map/out_project/pallas_call | solution.py:418
  243.9 6.4 %collective-permute-done.28.refs_2_ = bf16[32,4096]{1,0:T(8,128)(2,1)S(1)} collective-permute-done((bf16[32,4096]{1,0:T(8,128)(2,1)S(1)}, bf16[32,4096]{1,0:T(8,128)(2,1)S(1)}, u32[]{:S(2)}, u32[]{:S(2)}) %collective-permute-start.28) | collective-permute-done | bytes 262176 | tf_op jit(solution)/shard_map/ppermute | solution.py:30
  251.1 2.0 sum_z.4
  254.1 2.4 sum_pieces.5
  256.5 11.5 %state_step.7.own_ref = bf16[256,1024]{1,0:T(8,128)(2,1)} custom-call(s32[1]{0:T(128)} %bitcast.me_ref, s32[256]{0:T(256)} %select_reduce_fusion.slot_ref, bf16[32,4096]{1,0:T(8,128)(2,1)} %get-tuple-element.94.refs_0_, bf16[4,3,16,640]{3,2,1,0:T(8,128)(2,1)} %merge_z.3.refs_1_, bf16[4,3,16,640]{3,2,1,0:T(8,128)(2,1)} %copy-done.2, ...), custom_call_target="tpu_custom_call" | custom-call | flops 1024 | bytes 1024 | tf_op jit(solution)/shard_map/state_step/pallas_call | solution.py:387
  268.0 1.6 collective-permute-start.35
  270.9 9.8 %out_project.7 = (bf16[128,4096]{1,0:T(8,128)(2,1)}, bf16[128,4096]{1,0:T(8,128)(2,1)}) custom-call(s32[1]{0:T(128)} %bitcast.me_ref, bf16[256,1024]{1,0:T(8,128)(2,1)} %state_step.7.own_ref, bf16[256,1024]{1,0:T(8,128)(2,1)} %copy-done.11, bf16[1024,8192]{1,0:T(8,128)(2,1)} %wown_ref.7, bf16[1024,4096]{1,0:T(8,128)(2,1)} %collective-permute-done.12.wother_ref), custom_call_target="tpu_custom_call" | custom-call | flops 1024 | bytes 1024 | tf_op jit(solution)/shard_map/out_project/pallas_call | solution.py:418
  280.6 1.5 collective-permute-start.39
  282.2 5.5 %collective-permute-start.32 = (bf16[32,4096]{1,0:T(8,128)(2,1)S(1)}, bf16[32,4096]{1,0:T(8,128)(2,1)S(1)}, u32[]{:S(2)}, u32[]{:S(2)}) collective-permute-start(bf16[32,4096]{1,0:T(8,128)(2,1)S(1)} %copy-done.55), channel_id=1, source_target_pairs={{0,4},{1,5},{2,6},{3,7},{4,0},{5,1},{6,2},{7,3},{8,12},{9,13},{10,... | collective-permute-start | bytes 786440 | tf_op jit(solution)/shard_map/ppermute | solution.py:30
  288.7 1.5 collective-permute-start.34
  290.2 8.7 %collective-permute-done.32.refs_1_ = bf16[32,4096]{1,0:T(8,128)(2,1)S(1)} collective-permute-done((bf16[32,4096]{1,0:T(8,128)(2,1)S(1)}, bf16[32,4096]{1,0:T(8,128)(2,1)S(1)}, u32[]{:S(2)}, u32[]{:S(2)}) %collective-permute-start.32) | collective-permute-done | bytes 262176 | tf_op jit(solution)/shard_map/ppermute | solution.py:30
  298.9 10.2 %collective-permute-done.33.refs_2_ = bf16[32,4096]{1,0:T(8,128)(2,1)S(1)} collective-permute-done((bf16[32,4096]{1,0:T(8,128)(2,1)S(1)}, bf16[32,4096]{1,0:T(8,128)(2,1)S(1)}, u32[]{:S(2)}, u32[]{:S(2)}) %collective-permute-start.33) | collective-permute-done | bytes 262176 | tf_op jit(solution)/shard_map/ppermute | solution.py:30
  309.9 2.1 sum_z.5
  312.9 2.4 sum_pieces.6
  315.3 4.7 %collective-permute-start.36 = (bf16[32,4096]{1,0:T(8,128)(2,1)}, bf16[32,4096]{1,0:T(8,128)(2,1)S(1)}, u32[]{:S(2)}, u32[]{:S(2)}) collective-permute-start(bf16[32,4096]{1,0:T(8,128)(2,1)} %get-tuple-element.103), channel_id=1, source_target_pairs={{0,4},{1,5},{2,6},{3,7},{4,0},{5,1},{6,2},{7,3},{8,12},{9,13},{10,... | collective-permute-start | bytes 786440 | tf_op jit(solution)/shard_map/ppermute | solution.py:30
  322.4 7.1 %collective-permute-done.36.refs_1_ = bf16[32,4096]{1,0:T(8,128)(2,1)S(1)} collective-permute-done((bf16[32,4096]{1,0:T(8,128)(2,1)}, bf16[32,4096]{1,0:T(8,128)(2,1)S(1)}, u32[]{:S(2)}, u32[]{:S(2)}) %collective-permute-start.36) | collective-permute-done | bytes 262176 | tf_op jit(solution)/shard_map/ppermute | solution.py:30
  329.6 12.0 %collective-permute-done.37.refs_2_ = bf16[32,4096]{1,0:T(8,128)(2,1)S(1)} collective-permute-done((bf16[32,4096]{1,0:T(8,128)(2,1)}, bf16[32,4096]{1,0:T(8,128)(2,1)S(1)}, u32[]{:S(2)}, u32[]{:S(2)}) %collective-permute-start.37) | collective-permute-done | bytes 262176 | tf_op jit(solution)/shard_map/ppermute | solution.py:30
  342.4 2.0 sum_z.6
  345.4 2.4 sum_pieces.7
  347.8 3.5 collective-permute-start.40
  354.3 4.9 %collective-permute-done.40.refs_1_ = bf16[32,4096]{1,0:T(8,128)(2,1)S(1)} collective-permute-done((bf16[32,4096]{1,0:T(8,128)(2,1)}, bf16[32,4096]{1,0:T(8,128)(2,1)S(1)}, u32[]{:S(2)}, u32[]{:S(2)}) %collective-permute-start.40) | collective-permute-done | bytes 262176 | tf_op jit(solution)/shard_map/ppermute | solution.py:30
  359.2 12.9 %collective-permute-done.41.refs_2_ = bf16[32,4096]{1,0:T(8,128)(2,1)S(1)} collective-permute-done((bf16[32,4096]{1,0:T(8,128)(2,1)}, bf16[32,4096]{1,0:T(8,128)(2,1)S(1)}, u32[]{:S(2)}, u32[]{:S(2)}) %collective-permute-start.41) | collective-permute-done | bytes 262176 | tf_op jit(solution)/shard_map/ppermute | solution.py:30
  372.8 2.0 sum_z.7
  374.9 1.5 collective-permute-done.46.refs_7_
  377.1 3.9 %final_join.1 = bf16[16,4,8192]{2,1,0:T(4,128)(2,1)} custom-call(s32[1]{0:T(128)} %bitcast.me_ref, bf16[16,4096]{1,0:T(8,128)(2,1)} %get-tuple-element.92.refs_0_, bf16[16,4096]{1,0:T(8,128)(2,1)} %get-tuple-element.100.refs_0_.refs_1_, bf16[16,4096]{1,0:T(8,128)(2,1)} %get-tuple-element.106.refs_0_.refs_2_, bf16[16,4096]{1,0:T(8,128)(2,1)} %get-tuple-element.112.refs_3_, ...), custom_call_target="tpu_custom_call" | custom-call | flops 1024 | bytes 1024 | tf_op jit(solution)/shard_map/final_join/pallas_call | solution.py:491
  (202 shorter events, 39.1 us)
Async XLA Ops:
  13.5 26.0 %copy-start.51 = (s32[64]{0:T(128)S(1)}, s32[64]{0:T(128)}, u32[]{:S(2)}) copy-start(s32[64]{0:T(128)} %param.22) | copy-start | bytes 772
  13.5 26.3 %copy-start.50 = (s32[16]{0:T(128)S(1)}, s32[16]{0:T(128)}, u32[]{:S(2)}) copy-start(s32[16]{0:T(128)} %param.21) | copy-start | bytes 196
  13.5 159.2 %collective-permute-start.12 = (bf16[1024,4096]{1,0:T(8,128)(2,1)}, bf16[1024,4096]{1,0:T(8,128)(2,1)}, u32[]{:S(2)}, u32[]{:S(2)}) collective-permute-start(bf16[1024,4096]{1,0:T(8,128)(2,1)} %weight_half.1.after_ref), channel_id=1, source_target_pairs={{0,1},{1,0},{2,3},{3,2},{4,5},{5,4},{6,7},{7,6},{8,9},{9,8},{10,11... | collective-permute-start | bytes 25165832 | tf_op jit(solution)/shard_map/ppermute | solution.py:30
  35.3 98.0 %all-to-all-start = ((bf16[16,64,1024]{2,1,0:T(8,128)(2,1)}), bf16[16,64,1024]{2,1,0:T(8,128)(2,1)S(1)}, u32[]{:S(2)}, u32[]{:S(2)}) async-start(bf16[16,64,1024]{2,1,0:T(8,128)(2,1)} %pack_state.1.after_ref), calls=%async_computation | async-start | bytes 4194304 | tf_op jit(solution)/shard_map/all_to_all | solution.py:536
  40.5 23.2 %copy-start.49 = (f32[544]{0:T(1024)S(1)}, f32[544]{0:T(1024)}, u32[]{:S(2)}) copy-start(f32[544]{0:T(1024)} %param.28) | copy-start | bytes 6532
  45.4 1.6 collective-permute-start
  49.4 7.7 %collective-permute-start.1 = (bf16[4,1,16,640]{3,2,1,0:T(8,128)(2,1)}, bf16[4,1,16,640]{3,2,1,0:T(8,128)(2,1)S(1)}, u32[]{:S(2)}, u32[]{:S(2)}) collective-permute-start(bf16[4,1,16,640]{3,2,1,0:T(8,128)(2,1)} %get-tuple-element.64), channel_id=1, source_target_pairs={{0,2},{1,3},{2,0},{3,1},{4,6},{5,7},{6,4},{7,5},{8,10},{9,11},{10,... | collective-permute-start | bytes 245768 | tf_op jit(solution)/shard_map/ppermute | solution.py:30
  59.3 15.6 %collective-permute-start.2 = (bf16[1,16,640]{2,1,0:T(8,128)(2,1)}, bf16[1,16,640]{2,1,0:T(8,128)(2,1)S(1)}, u32[]{:S(2)}, u32[]{:S(2)}) collective-permute-start(bf16[1,16,640]{2,1,0:T(8,128)(2,1)} %get-tuple-element.66), channel_id=1, source_target_pairs={{0,4},{1,5},{2,6},{3,7},{4,0},{5,1},{6,2},{7,3},{8,12},{9,13},{10,... | collective-permute-start | bytes 61448 | tf_op jit(solution)/shard_map/ppermute | solution.py:30
  59.4 30.6 %collective-permute-start.3 = (bf16[1,16,640]{2,1,0:T(8,128)(2,1)}, bf16[1,16,640]{2,1,0:T(8,128)(2,1)S(1)}, u32[]{:S(2)}, u32[]{:S(2)}) collective-permute-start(bf16[1,16,640]{2,1,0:T(8,128)(2,1)} %get-tuple-element.67), channel_id=1, source_target_pairs={{0,8},{1,9},{2,10},{3,11},{4,12},{5,13},{6,14},{7,15},{8,0},{9,1},... | collective-permute-start | bytes 61448 | tf_op jit(solution)/shard_map/ppermute | solution.py:30
  62.1 27.9 %collective-permute-start.4 = (bf16[1,16,640]{2,1,0:T(8,128)(2,1)}, bf16[1,16,640]{2,1,0:T(8,128)(2,1)S(1)}, u32[]{:S(2)}, u32[]{:S(2)}) collective-permute-start(bf16[1,16,640]{2,1,0:T(8,128)(2,1)} %get-tuple-element.68), channel_id=1, source_target_pairs={{0,12},{1,13},{2,14},{3,15},{4,8},{5,9},{6,10},{7,11},{8,4},{9,5},... | collective-permute-start | bytes 61448 | tf_op jit(solution)/shard_map/ppermute | solution.py:30
  74.9 15.1 %copy-start.46 = (bf16[1,16,640]{2,1,0:T(8,128)(2,1)}, bf16[1,16,640]{2,1,0:T(8,128)(2,1)S(1)}, u32[]{:S(2)}) copy-start(bf16[1,16,640]{2,1,0:T(8,128)(2,1)S(1)} %collective-permute-done.2.refs_1_) | copy-start | bytes 61444
  99.9 4.5 %collective-permute-start.14 = (bf16[8,3,16,640]{3,2,1,0:T(8,128)(2,1)}, bf16[8,3,16,640]{3,2,1,0:T(8,128)(2,1)S(1)}, u32[]{:S(2)}, u32[]{:S(2)}) collective-permute-start(bf16[8,3,16,640]{3,2,1,0:T(8,128)(2,1)} %get-tuple-element.74), channel_id=1, source_target_pairs={{0,1},{1,0},{2,3},{3,2},{4,5},{5,4},{6,7},{7,6},{8,9},{9,8},{10,11... | collective-permute-start | bytes 1474568 | tf_op jit(solution)/shard_map/ppermute | solution.py:30
  99.9 9.0 %collective-permute-start.7 = (bf16[1,16,640]{2,1,0:T(8,128)(2,1)S(1)}, bf16[1,16,640]{2,1,0:T(8,128)(2,1)S(1)}, u32[]{:S(2)}, u32[]{:S(2)}) collective-permute-start(bf16[1,16,640]{2,1,0:T(8,128)(2,1)S(1)} %copy-done.27), channel_id=1, source_target_pairs={{0,12},{1,13},{2,14},{3,15},{4,8},{5,9},{6,10},{7,11},{8,4},{9,5},... | collective-permute-start | bytes 61448 | tf_op jit(solution)/shard_map/ppermute | solution.py:30
  101.4 7.5 %collective-permute-start.6 = (bf16[1,16,640]{2,1,0:T(8,128)(2,1)S(1)}, bf16[1,16,640]{2,1,0:T(8,128)(2,1)S(1)}, u32[]{:S(2)}, u32[]{:S(2)}) collective-permute-start(bf16[1,16,640]{2,1,0:T(8,128)(2,1)S(1)} %copy-done.27), channel_id=1, source_target_pairs={{0,8},{1,9},{2,10},{3,11},{4,12},{5,13},{6,14},{7,15},{8,0},{9,1},... | collective-permute-start | bytes 61448 | tf_op jit(solution)/shard_map/ppermute | solution.py:30
  102.2 6.8 %collective-permute-start.5 = (bf16[1,16,640]{2,1,0:T(8,128)(2,1)S(1)}, bf16[1,16,640]{2,1,0:T(8,128)(2,1)S(1)}, u32[]{:S(2)}, u32[]{:S(2)}) collective-permute-start(bf16[1,16,640]{2,1,0:T(8,128)(2,1)S(1)} %copy-done.27), channel_id=1, source_target_pairs={{0,4},{1,5},{2,6},{3,7},{4,0},{5,1},{6,2},{7,3},{8,12},{9,13},{10,... | collective-permute-start | bytes 61448 | tf_op jit(solution)/shard_map/ppermute | solution.py:30
  107.2 8.5 %collective-permute-start.15 = (bf16[4,3,16,640]{3,2,1,0:T(8,128)(2,1)}, bf16[4,3,16,640]{3,2,1,0:T(8,128)(2,1)S(1)}, u32[]{:S(2)}, u32[]{:S(2)}) collective-permute-start(bf16[4,3,16,640]{3,2,1,0:T(8,128)(2,1)} %get-tuple-element.76), channel_id=1, source_target_pairs={{0,2},{1,3},{2,0},{3,1},{4,6},{5,7},{6,4},{7,5},{8,10},{9,11},{10,... | collective-permute-start | bytes 737288 | tf_op jit(solution)/shard_map/ppermute | solution.py:30
  111.6 8.7 %collective-permute-start.8 = (bf16[4,1,16,640]{3,2,1,0:T(8,128)(2,1)}, bf16[4,1,16,640]{3,2,1,0:T(8,128)(2,1)S(1)}, u32[]{:S(2)}, u32[]{:S(2)}) collective-permute-start(bf16[4,1,16,640]{3,2,1,0:T(8,128)(2,1)} %merge_z.2.refs_2_), channel_id=1, source_target_pairs={{0,2},{1,3},{2,0},{3,1},{4,6},{5,7},{6,4},{7,5},{8,10},{9,11},{10,... | collective-permute-start | bytes 245768 | tf_op jit(solution)/shard_map/ppermute | solution.py:30
  112.1 19.1 %collective-permute-start.9 = (bf16[4,1,16,640]{3,2,1,0:T(8,128)(2,1)}, bf16[4,1,16,640]{3,2,1,0:T(8,128)(2,1)S(1)}, u32[]{:S(2)}, u32[]{:S(2)}) collective-permute-start(bf16[4,1,16,640]{3,2,1,0:T(8,128)(2,1)} %merge_z.2.refs_2_), channel_id=1, source_target_pairs={{0,1},{1,0},{2,3},{3,2},{4,5},{5,4},{6,7},{7,6},{8,9},{9,8},{10,11... | collective-permute-start | bytes 245768 | tf_op jit(solution)/shard_map/ppermute | solution.py:30
  118.2 5.7 %collective-permute-start.16 = (bf16[3,16,640]{2,1,0:T(8,128)(2,1)}, bf16[3,16,640]{2,1,0:T(8,128)(2,1)S(1)}, u32[]{:S(2)}, u32[]{:S(2)}) collective-permute-start(bf16[3,16,640]{2,1,0:T(8,128)(2,1)} %get-tuple-element.78), channel_id=1, source_target_pairs={{0,4},{1,5},{2,6},{3,7},{4,0},{5,1},{6,2},{7,3},{8,12},{9,13},{10,... | collective-permute-start | bytes 184328 | tf_op jit(solution)/shard_map/ppermute | solution.py:30
  118.5 5.5 %collective-permute-start.17 = (bf16[3,16,640]{2,1,0:T(8,128)(2,1)}, bf16[3,16,640]{2,1,0:T(8,128)(2,1)S(1)}, u32[]{:S(2)}, u32[]{:S(2)}) collective-permute-start(bf16[3,16,640]{2,1,0:T(8,128)(2,1)} %get-tuple-element.79), channel_id=1, source_target_pairs={{0,8},{1,9},{2,10},{3,11},{4,12},{5,13},{6,14},{7,15},{8,0},{9,1},... | collective-permute-start | bytes 184328 | tf_op jit(solution)/shard_map/ppermute | solution.py:30
  120.3 14.0 %copy-start.33 = (bf16[4,1,16,640]{3,2,1,0:T(8,128)(2,1)}, bf16[4,1,16,640]{3,2,1,0:T(8,128)(2,1)S(1)}, u32[]{:S(2)}) copy-start(bf16[4,1,16,640]{3,2,1,0:T(8,128)(2,1)S(1)} %collective-permute-done.8.refs_3_) | copy-start | bytes 245764
  120.3 6.2 %collective-permute-start.18 = (bf16[3,16,640]{2,1,0:T(8,128)(2,1)}, bf16[3,16,640]{2,1,0:T(8,128)(2,1)S(1)}, u32[]{:S(2)}, u32[]{:S(2)}) collective-permute-start(bf16[3,16,640]{2,1,0:T(8,128)(2,1)} %get-tuple-element.80), channel_id=1, source_target_pairs={{0,12},{1,13},{2,14},{3,15},{4,8},{5,9},{6,10},{7,11},{8,4},{9,5},... | collective-permute-start | bytes 184328 | tf_op jit(solution)/shard_map/ppermute | solution.py:30
  124.0 9.3 %collective-permute-start.10 = (bf16[4,1,16,640]{3,2,1,0:T(8,128)(2,1)S(1)}, bf16[4,1,16,640]{3,2,1,0:T(8,128)(2,1)S(1)}, u32[]{:S(2)}, u32[]{:S(2)}) collective-permute-start(bf16[4,1,16,640]{3,2,1,0:T(8,128)(2,1)S(1)} %collective-permute-done.8.refs_3_), channel_id=1, source_target_pairs={{0,1},{1,0},{2,3},{3,2},{4,5},{5,4},{6,7},{7,6},{8,9},{9,8},{10,11... | collective-permute-start | bytes 245768 | tf_op jit(solution)/shard_map/ppermute | solution.py:30
  128.8 32.3 %collective-permute-start.21 = (bf16[3,16,640]{2,1,0:T(8,128)(2,1)}, bf16[3,16,640]{2,1,0:T(8,128)(2,1)S(1)}, u32[]{:S(2)}, u32[]{:S(2)}) collective-permute-start(bf16[3,16,640]{2,1,0:T(8,128)(2,1)} %norm.3.refs_0_), channel_id=1, source_target_pairs={{0,12},{1,13},{2,14},{3,15},{4,8},{5,9},{6,10},{7,11},{8,4},{9,5},... | collective-permute-start | bytes 184328 | tf_op jit(solution)/shard_map/ppermute | solution.py:30
  131.2 30.0 %collective-permute-start.20 = (bf16[3,16,640]{2,1,0:T(8,128)(2,1)}, bf16[3,16,640]{2,1,0:T(8,128)(2,1)S(1)}, u32[]{:S(2)}, u32[]{:S(2)}) collective-permute-start(bf16[3,16,640]{2,1,0:T(8,128)(2,1)} %norm.3.refs_0_), channel_id=1, source_target_pairs={{0,8},{1,9},{2,10},{3,11},{4,12},{5,13},{6,14},{7,15},{8,0},{9,1},... | collective-permute-start | bytes 184328 | tf_op jit(solution)/shard_map/ppermute | solution.py:30
  131.2 30.0 %collective-permute-start.19 = (bf16[3,16,640]{2,1,0:T(8,128)(2,1)}, bf16[3,16,640]{2,1,0:T(8,128)(2,1)S(1)}, u32[]{:S(2)}, u32[]{:S(2)}) collective-permute-start(bf16[3,16,640]{2,1,0:T(8,128)(2,1)} %norm.3.refs_0_), channel_id=1, source_target_pairs={{0,4},{1,5},{2,6},{3,7},{4,0},{5,1},{6,2},{7,3},{8,12},{9,13},{10,... | collective-permute-start | bytes 184328 | tf_op jit(solution)/shard_map/ppermute | solution.py:30
  161.0 11.6 %collective-permute-start.11 = (bf16[256,1024]{1,0:T(8,128)(2,1)}, bf16[256,1024]{1,0:T(8,128)(2,1)S(1)}, u32[]{:S(2)}, u32[]{:S(2)}) collective-permute-start(bf16[256,1024]{1,0:T(8,128)(2,1)} %get-tuple-element.70.own_ref), channel_id=1, source_target_pairs={{0,1},{1,0},{2,3},{3,2},{4,5},{5,4},{6,7},{7,6},{8,9},{9,8},{10,11... | collective-permute-start | bytes 1572872 | tf_op jit(solution)/shard_map/ppermute | solution.py:30
  164.0 8.6 %collective-permute-start.22 = (bf16[4,3,16,640]{3,2,1,0:T(8,128)(2,1)}, bf16[4,3,16,640]{3,2,1,0:T(8,128)(2,1)S(1)}, u32[]{:S(2)}, u32[]{:S(2)}) collective-permute-start(bf16[4,3,16,640]{3,2,1,0:T(8,128)(2,1)} %merge_z.3.refs_1_), channel_id=1, source_target_pairs={{0,2},{1,3},{2,0},{3,1},{4,6},{5,7},{6,4},{7,5},{8,10},{9,11},{10,... | collective-permute-start | bytes 737288 | tf_op jit(solution)/shard_map/ppermute | solution.py:30
  165.4 19.3 %collective-permute-start.23 = (bf16[4,3,16,640]{3,2,1,0:T(8,128)(2,1)}, bf16[4,3,16,640]{3,2,1,0:T(8,128)(2,1)S(1)}, u32[]{:S(2)}, u32[]{:S(2)}) collective-permute-start(bf16[4,3,16,640]{3,2,1,0:T(8,128)(2,1)} %merge_z.3.refs_1_), channel_id=1, source_target_pairs={{0,1},{1,0},{2,3},{3,2},{4,5},{5,4},{6,7},{7,6},{8,9},{9,8},{10,11... | collective-permute-start | bytes 737288 | tf_op jit(solution)/shard_map/ppermute | solution.py:30
  172.6 12.1 %collective-permute-start.24 = (bf16[4,3,16,640]{3,2,1,0:T(8,128)(2,1)S(1)}, bf16[4,3,16,640]{3,2,1,0:T(8,128)(2,1)S(1)}, u32[]{:S(2)}, u32[]{:S(2)}) collective-permute-start(bf16[4,3,16,640]{3,2,1,0:T(8,128)(2,1)S(1)} %collective-permute-done.22.refs_2_), channel_id=1, source_target_pairs={{0,1},{1,0},{2,3},{3,2},{4,5},{5,4},{6,7},{7,6},{8,9},{9,8},{10,11... | collective-permute-start | bytes 737288 | tf_op jit(solution)/shard_map/ppermute | solution.py:30
  183.3 28.9 %collective-permute-start.13 = (bf16[128,4096]{1,0:T(8,128)(2,1)}, bf16[128,4096]{1,0:T(8,128)(2,1)S(1)}, u32[]{:S(2)}, u32[]{:S(2)}) collective-permute-start(bf16[128,4096]{1,0:T(8,128)(2,1)} %get-tuple-element.72.refs_0_), channel_id=1, source_target_pairs={{0,2},{1,3},{2,0},{3,1},{4,6},{5,7},{6,4},{7,5},{8,10},{9,11},{10,... | collective-permute-start | bytes 3145736 | tf_op jit(solution)/shard_map/ppermute | solution.py:30
  198.8 2.1 collective-permute-start.25
  211.5 41.6 %collective-permute-start.30 = (bf16[128,4096]{1,0:T(8,128)(2,1)}, bf16[128,4096]{1,0:T(8,128)(2,1)S(1)}, u32[]{:S(2)}, u32[]{:S(2)}) collective-permute-start(bf16[128,4096]{1,0:T(8,128)(2,1)} %get-tuple-element.93), channel_id=1, source_target_pairs={{0,2},{1,3},{2,0},{3,1},{4,6},{5,7},{6,4},{7,5},{8,10},{9,11},{10,... | collective-permute-start | bytes 3145736 | tf_op jit(solution)/shard_map/ppermute | solution.py:30
  215.5 13.4 %copy-start.58 = (bf16[32,4096]{1,0:T(8,128)(2,1)S(1)}, bf16[32,4096]{1,0:T(8,128)(2,1)}, u32[]{:S(2)}) copy-start(bf16[32,4096]{1,0:T(8,128)(2,1)} %get-tuple-element.89) | copy-start | bytes 786436
  215.5 13.5 %copy-start.57 = (bf16[32,4096]{1,0:T(8,128)(2,1)S(1)}, bf16[32,4096]{1,0:T(8,128)(2,1)}, u32[]{:S(2)}) copy-start(bf16[32,4096]{1,0:T(8,128)(2,1)} %get-tuple-element.90) | copy-start | bytes 786436
  215.5 16.4 %copy-start.56 = (bf16[32,4096]{1,0:T(8,128)(2,1)S(1)}, bf16[32,4096]{1,0:T(8,128)(2,1)}, u32[]{:S(2)}) copy-start(bf16[32,4096]{1,0:T(8,128)(2,1)} %get-tuple-element.91) | copy-start | bytes 786436
  228.8 4.5 %collective-permute-start.26 = (bf16[256,1024]{1,0:T(8,128)(2,1)}, bf16[256,1024]{1,0:T(8,128)(2,1)S(1)}, u32[]{:S(2)}, u32[]{:S(2)}) collective-permute-start(bf16[256,1024]{1,0:T(8,128)(2,1)} %get-tuple-element.87.own_ref), channel_id=1, source_target_pairs={{0,1},{1,0},{2,3},{3,2},{4,5},{5,4},{6,7},{7,6},{8,9},{9,8},{10,11... | collective-permute-start | bytes 1572872 | tf_op jit(solution)/shard_map/ppermute | solution.py:30
  228.9 15.1 %collective-permute-start.27 = (bf16[32,4096]{1,0:T(8,128)(2,1)S(1)}, bf16[32,4096]{1,0:T(8,128)(2,1)S(1)}, u32[]{:S(2)}, u32[]{:S(2)}) collective-permute-start(bf16[32,4096]{1,0:T(8,128)(2,1)S(1)} %copy-done.58), channel_id=1, source_target_pairs={{0,4},{1,5},{2,6},{3,7},{4,0},{5,1},{6,2},{7,3},{8,12},{9,13},{10,... | collective-permute-start | bytes 786440 | tf_op jit(solution)/shard_map/ppermute | solution.py:30
  229.0 21.3 %collective-permute-start.28 = (bf16[32,4096]{1,0:T(8,128)(2,1)S(1)}, bf16[32,4096]{1,0:T(8,128)(2,1)S(1)}, u32[]{:S(2)}, u32[]{:S(2)}) collective-permute-start(bf16[32,4096]{1,0:T(8,128)(2,1)S(1)} %copy-done.57), channel_id=1, source_target_pairs={{0,8},{1,9},{2,10},{3,11},{4,12},{5,13},{6,14},{7,15},{8,0},{9,1},... | collective-permute-start | bytes 786440 | tf_op jit(solution)/shard_map/ppermute | solution.py:30
  231.9 18.4 %collective-permute-start.29 = (bf16[32,4096]{1,0:T(8,128)(2,1)S(1)}, bf16[32,4096]{1,0:T(8,128)(2,1)S(1)}, u32[]{:S(2)}, u32[]{:S(2)}) collective-permute-start(bf16[32,4096]{1,0:T(8,128)(2,1)S(1)} %copy-done.56), channel_id=1, source_target_pairs={{0,12},{1,13},{2,14},{3,15},{4,8},{5,9},{6,10},{7,11},{8,4},{9,5},... | collective-permute-start | bytes 786440 | tf_op jit(solution)/shard_map/ppermute | solution.py:30
  256.5 11.5 %copy-start.52 = (bf16[128,4096]{1,0:T(8,128)(2,1)S(1)}, bf16[128,4096]{1,0:T(8,128)(2,1)}, u32[]{:S(2)}) copy-start(bf16[128,4096]{1,0:T(8,128)(2,1)} %get-tuple-element.101) | copy-start | bytes 3145732
  268.0 2.1 collective-permute-start.31
  268.0 14.2 %copy-start.55 = (bf16[32,4096]{1,0:T(8,128)(2,1)S(1)}, bf16[32,4096]{1,0:T(8,128)(2,1)}, u32[]{:S(2)}) copy-start(bf16[32,4096]{1,0:T(8,128)(2,1)} %get-tuple-element.97) | copy-start | bytes 786436
  268.0 19.7 %copy-start.54 = (bf16[32,4096]{1,0:T(8,128)(2,1)S(1)}, bf16[32,4096]{1,0:T(8,128)(2,1)}, u32[]{:S(2)}) copy-start(bf16[32,4096]{1,0:T(8,128)(2,1)} %get-tuple-element.98) | copy-start | bytes 786436
  268.0 20.7 %copy-start.53 = (bf16[32,4096]{1,0:T(8,128)(2,1)S(1)}, bf16[32,4096]{1,0:T(8,128)(2,1)}, u32[]{:S(2)}) copy-start(bf16[32,4096]{1,0:T(8,128)(2,1)} %get-tuple-element.99) | copy-start | bytes 786436
  268.0 43.9 %collective-permute-start.35 = (bf16[128,4096]{1,0:T(8,128)(2,1)S(1)}, bf16[128,4096]{1,0:T(8,128)(2,1)S(1)}, u32[]{:S(2)}, u32[]{:S(2)}) collective-permute-start(bf16[128,4096]{1,0:T(8,128)(2,1)S(1)} %copy-done.52), channel_id=1, source_target_pairs={{0,2},{1,3},{2,0},{3,1},{4,6},{5,7},{6,4},{7,5},{8,10},{9,11},{10,... | collective-permute-start | bytes 3145736 | tf_op jit(solution)/shard_map/ppermute | solution.py:30
  280.6 63.8 %collective-permute-start.39 = (bf16[128,4096]{1,0:T(8,128)(2,1)}, bf16[128,4096]{1,0:T(8,128)(2,1)S(1)}, u32[]{:S(2)}, u32[]{:S(2)}) collective-permute-start(bf16[128,4096]{1,0:T(8,128)(2,1)} %get-tuple-element.107), channel_id=1, source_target_pairs={{0,2},{1,3},{2,0},{3,1},{4,6},{5,7},{6,4},{7,5},{8,10},{9,11},{10,... | collective-permute-start | bytes 3145736 | tf_op jit(solution)/shard_map/ppermute | solution.py:30
  282.2 16.7 %collective-permute-start.32 = (bf16[32,4096]{1,0:T(8,128)(2,1)S(1)}, bf16[32,4096]{1,0:T(8,128)(2,1)S(1)}, u32[]{:S(2)}, u32[]{:S(2)}) collective-permute-start(bf16[32,4096]{1,0:T(8,128)(2,1)S(1)} %copy-done.55), channel_id=1, source_target_pairs={{0,4},{1,5},{2,6},{3,7},{4,0},{5,1},{6,2},{7,3},{8,12},{9,13},{10,... | collective-permute-start | bytes 786440 | tf_op jit(solution)/shard_map/ppermute | solution.py:30
  287.7 21.4 %collective-permute-start.33 = (bf16[32,4096]{1,0:T(8,128)(2,1)S(1)}, bf16[32,4096]{1,0:T(8,128)(2,1)S(1)}, u32[]{:S(2)}, u32[]{:S(2)}) collective-permute-start(bf16[32,4096]{1,0:T(8,128)(2,1)S(1)} %copy-done.54), channel_id=1, source_target_pairs={{0,8},{1,9},{2,10},{3,11},{4,12},{5,13},{6,14},{7,15},{8,0},{9,1},... | collective-permute-start | bytes 786440 | tf_op jit(solution)/shard_map/ppermute | solution.py:30
  288.7 20.3 %collective-permute-start.34 = (bf16[32,4096]{1,0:T(8,128)(2,1)S(1)}, bf16[32,4096]{1,0:T(8,128)(2,1)S(1)}, u32[]{:S(2)}, u32[]{:S(2)}) collective-permute-start(bf16[32,4096]{1,0:T(8,128)(2,1)S(1)} %copy-done.53), channel_id=1, source_target_pairs={{0,12},{1,13},{2,14},{3,15},{4,8},{5,9},{6,10},{7,11},{8,4},{9,5},... | collective-permute-start | bytes 786440 | tf_op jit(solution)/shard_map/ppermute | solution.py:30
  309.9 43.9 %copy-start.59 = (bf16[16,4096]{1,0:T(8,128)(2,1)S(1)}, bf16[16,4096]{1,0:T(8,128)(2,1)}, u32[]{:S(2)}) copy-start(bf16[16,4096]{1,0:T(8,128)(2,1)} %get-tuple-element.113) | copy-start | bytes 393220
  311.9 41.9 %copy-start.60 = (bf16[16,4096]{1,0:T(8,128)(2,1)S(1)}, bf16[16,4096]{1,0:T(8,128)(2,1)}, u32[]{:S(2)}) copy-start(bf16[16,4096]{1,0:T(8,128)(2,1)} %get-tuple-element.114) | copy-start | bytes 393220
  315.3 14.2 %collective-permute-start.36 = (bf16[32,4096]{1,0:T(8,128)(2,1)}, bf16[32,4096]{1,0:T(8,128)(2,1)S(1)}, u32[]{:S(2)}, u32[]{:S(2)}) collective-permute-start(bf16[32,4096]{1,0:T(8,128)(2,1)} %get-tuple-element.103), channel_id=1, source_target_pairs={{0,4},{1,5},{2,6},{3,7},{4,0},{5,1},{6,2},{7,3},{8,12},{9,13},{10,... | collective-permute-start | bytes 786440 | tf_op jit(solution)/shard_map/ppermute | solution.py:30
  320.0 21.6 %collective-permute-start.37 = (bf16[32,4096]{1,0:T(8,128)(2,1)}, bf16[32,4096]{1,0:T(8,128)(2,1)S(1)}, u32[]{:S(2)}, u32[]{:S(2)}) collective-permute-start(bf16[32,4096]{1,0:T(8,128)(2,1)} %get-tuple-element.104), channel_id=1, source_target_pairs={{0,8},{1,9},{2,10},{3,11},{4,12},{5,13},{6,14},{7,15},{8,0},{9,1},... | collective-permute-start | bytes 786440 | tf_op jit(solution)/shard_map/ppermute | solution.py:30
  321.0 20.6 %collective-permute-start.38 = (bf16[32,4096]{1,0:T(8,128)(2,1)}, bf16[32,4096]{1,0:T(8,128)(2,1)S(1)}, u32[]{:S(2)}, u32[]{:S(2)}) collective-permute-start(bf16[32,4096]{1,0:T(8,128)(2,1)} %get-tuple-element.105), channel_id=1, source_target_pairs={{0,12},{1,13},{2,14},{3,15},{4,8},{5,9},{6,10},{7,11},{8,4},{9,5},... | collective-permute-start | bytes 786440 | tf_op jit(solution)/shard_map/ppermute | solution.py:30
  329.6 12.1 %copy-start.21 = (bf16[32,4096]{1,0:T(8,128)(2,1)}, bf16[32,4096]{1,0:T(8,128)(2,1)S(1)}, u32[]{:S(2)}) copy-start(bf16[32,4096]{1,0:T(8,128)(2,1)S(1)} %collective-permute-done.36.refs_1_) | copy-start | bytes 786436
  347.8 11.3 %collective-permute-start.40 = (bf16[32,4096]{1,0:T(8,128)(2,1)}, bf16[32,4096]{1,0:T(8,128)(2,1)S(1)}, u32[]{:S(2)}, u32[]{:S(2)}) collective-permute-start(bf16[32,4096]{1,0:T(8,128)(2,1)} %get-tuple-element.109), channel_id=1, source_target_pairs={{0,4},{1,5},{2,6},{3,7},{4,0},{5,1},{6,2},{7,3},{8,12},{9,13},{10,... | collective-permute-start | bytes 786440 | tf_op jit(solution)/shard_map/ppermute | solution.py:30
  351.3 20.7 %collective-permute-start.41 = (bf16[32,4096]{1,0:T(8,128)(2,1)}, bf16[32,4096]{1,0:T(8,128)(2,1)S(1)}, u32[]{:S(2)}, u32[]{:S(2)}) collective-permute-start(bf16[32,4096]{1,0:T(8,128)(2,1)} %get-tuple-element.110), channel_id=1, source_target_pairs={{0,8},{1,9},{2,10},{3,11},{4,12},{5,13},{6,14},{7,15},{8,0},{9,1},... | collective-permute-start | bytes 786440 | tf_op jit(solution)/shard_map/ppermute | solution.py:30
  352.4 19.7 %collective-permute-start.42 = (bf16[32,4096]{1,0:T(8,128)(2,1)}, bf16[32,4096]{1,0:T(8,128)(2,1)S(1)}, u32[]{:S(2)}, u32[]{:S(2)}) collective-permute-start(bf16[32,4096]{1,0:T(8,128)(2,1)} %get-tuple-element.111), channel_id=1, source_target_pairs={{0,12},{1,13},{2,14},{3,15},{4,8},{5,9},{6,10},{7,11},{8,4},{9,5},... | collective-permute-start | bytes 786440 | tf_op jit(solution)/shard_map/ppermute | solution.py:30
  353.8 21.1 %collective-permute-start.43 = (bf16[16,4096]{1,0:T(8,128)(2,1)S(1)}, bf16[16,4096]{1,0:T(8,128)(2,1)S(1)}, u32[]{:S(2)}, u32[]{:S(2)}) collective-permute-start(bf16[16,4096]{1,0:T(8,128)(2,1)S(1)} %copy-done.59), channel_id=1, source_target_pairs={{0,1},{1,0},{2,3},{3,2},{4,5},{5,4},{6,7},{7,6},{8,9},{9,8},{10,11... | collective-permute-start | bytes 393224 | tf_op jit(solution)/shard_map/ppermute | solution.py:30
  353.8 21.1 %collective-permute-start.44 = (bf16[16,4096]{1,0:T(8,128)(2,1)S(1)}, bf16[16,4096]{1,0:T(8,128)(2,1)S(1)}, u32[]{:S(2)}, u32[]{:S(2)}) collective-permute-start(bf16[16,4096]{1,0:T(8,128)(2,1)S(1)} %copy-done.60), channel_id=1, source_target_pairs={{0,1},{1,0},{2,3},{3,2},{4,5},{5,4},{6,7},{7,6},{8,9},{9,8},{10,11... | collective-permute-start | bytes 393224 | tf_op jit(solution)/shard_map/ppermute | solution.py:30
  359.1 12.9 %copy-start.14 = (bf16[32,4096]{1,0:T(8,128)(2,1)}, bf16[32,4096]{1,0:T(8,128)(2,1)S(1)}, u32[]{:S(2)}) copy-start(bf16[32,4096]{1,0:T(8,128)(2,1)S(1)} %collective-permute-done.40.refs_1_) | copy-start | bytes 786436
  359.1 15.8 %collective-permute-start.45 = (bf16[16,4096]{1,0:T(8,128)(2,1)}, bf16[16,4096]{1,0:T(8,128)(2,1)S(1)}, u32[]{:S(2)}, u32[]{:S(2)}) collective-permute-start(bf16[16,4096]{1,0:T(8,128)(2,1)} %get-tuple-element.115), channel_id=1, source_target_pairs={{0,1},{1,0},{2,3},{3,2},{4,5},{5,4},{6,7},{7,6},{8,9},{9,8},{10,11... | collective-permute-start | bytes 393224 | tf_op jit(solution)/shard_map/ppermute | solution.py:30
  374.9 1.6 collective-permute-start.46
  (45 other events, 81.3 us)

commit v3 on v2

--- a/solution.py
+++ b/solution.py
@@ -15,15 +15,13 @@
 
 RMS_EPS = 1e-06
 BC_FLOOR = 0.2
-LOG2E = 1.4426950408889634
 
 BF16 = jnp.bfloat16
 F32 = jnp.float32
-VMEM_LIMIT = 56 * 1024 * 1024
-
-
-def params(**kw):
-    return pltpu.CompilerParams(vmem_limit_bytes=VMEM_LIMIT, **kw)
+
+
+def params(mib):
+    return pltpu.CompilerParams(vmem_limit_bytes=mib * 1024 * 1024)
 
 
 def swap(x, mask, n):
@@ -43,28 +41,55 @@
     return pl.BlockSpec(shape, lambda *_: zeros)
 
 
-def pack_conv_kernel(x_ref, o_ref):
-    slots = x_ref.shape[1]
-    n, tall, c = o_ref.shape
-    for d in range(n):
-        parts = [x_ref[p, :, d * c : (d + 1) * c] for p in range(TAPS)]
-        parts.append(jnp.zeros((tall - slots * TAPS, c), F32))
-        o_ref[d] = jnp.concatenate(parts, axis=0).astype(BF16)
-
-
-def pack_conv(prefilled_conv, n):
+def small(kernel, me, args, shapes, name, after=()):
+    size = sum(a.size for a in args)
+    return pl.pallas_call(
+        kernel,
+        grid_spec=pltpu.PrefetchScalarGridSpec(
+            num_scalar_prefetch=1,
+            grid=(1,),
+            in_specs=[pl.BlockSpec(memory_space=pl.ANY)] * len(after) + [whole(a.shape) for a in args],
+            out_specs=[whole(s) for s in shapes],
+        ),
+        out_shape=[jax.ShapeDtypeStruct(s, BF16) for s in shapes],
+        compiler_params=params(8),
+        cost_estimate=cost(size, 4 * size),
+        name=name,
+    )(me, *after, *args)
+
+
+def pack_conv_kernel(me_ref, x_ref, *o_refs):
+    zs, _, wide = o_refs[0].shape
+    y, core = (me_ref[0] // 2) % 2, me_ref[0] % 2
+    c = wide * (TAPS + 1) // TAPS
+    for i, o_ref in enumerate(o_refs):
+        for z in range(zs):
+            dest = 4 * z + 2 * jnp.bitwise_xor(y, i % 2) + jnp.bitwise_xor(core, i // 2)
+            x = x_ref[:, :, pl.ds(pl.multiple_of(dest * c, 128), c)]
+            parts = [x[p, :, :wide] for p in range(TAPS)]
+            parts.append(jnp.concatenate([x[p, :, wide:] for p in range(TAPS)], axis=1))
+            o_ref[z] = jnp.concatenate(parts, axis=0).astype(BF16)
+
+
+def cut_conv_kernel(me_ref, after_ref, *refs):
+    zs = refs[0].shape[0]
+    z, y, core = me_ref[0] // 4, (me_ref[0] // 2) % 2, me_ref[0] % 2
+    for m in range(zs):
+        for i in range(4):
+            at = 2 * jnp.bitwise_xor(y, i % 2) + jnp.bitwise_xor(core, i // 2)
+            refs[4 + m][at] = refs[i][jnp.bitwise_xor(z, m)]
+
+
+def exchange_conv(prefilled_conv, prefilled_state, me, n):
     slots, _, inner = prefilled_conv.shape
-    c = inner // n
-    return pl.pallas_call(
-        pack_conv_kernel,
-        grid=(1,),
-        in_specs=[whole((TAPS, slots, inner))],
-        out_specs=whole((n, 4 * slots, c)),
-        out_shape=jax.ShapeDtypeStruct((n, 4 * slots, c), BF16),
-        compiler_params=params(),
-        cost_estimate=cost(0, slots * 3 * inner * 6),
-        name="pack_conv",
-    )(jnp.transpose(prefilled_conv, (1, 0, 2)))
+    zs = n // 4
+    piece = ((TAPS + 1) * slots, inner // n * TAPS // (TAPS + 1))
+    packed = small(pack_conv_kernel, me, [jnp.transpose(prefilled_conv, (1, 0, 2))], [(zs,) + piece] * 4, "pack_conv")
+    packed_state = pack_state(packed[0], prefilled_state, n)
+    near, far = swap(packed[2], 1, n), swap(packed[3], 1, n)
+    got = [packed[0], swap(packed[1], 2, n), near, swap(far, 2, n)]
+    cut = small(cut_conv_kernel, me, got, [(4,) + piece] * zs, "cut_conv", (packed_state,))
+    return packed_state, [cut[0]] + [swap(cut[m], 4 * m, n) for m in range(1, zs)]
 
 
 def pack_state_kernel(after_ref, x_ref, o_ref):
@@ -88,51 +113,31 @@
         ],
         out_specs=pl.BlockSpec((some, slots * STATE, c), lambda d: (d, 0, 0)),
         out_shape=jax.ShapeDtypeStruct((n, slots * STATE, c), BF16),
-        compiler_params=params(),
+        compiler_params=params(24),
         cost_estimate=cost(0, slots * STATE * inner * 6),
         name="pack_state",
     )(after, prefilled_state)
 
 
-def half_kernel(me_ref, after_ref, w_ref, o_ref):
-    o_ref[...] = w_ref[...]
-
-
-def weight_half(me, after, out_weight):
-    c, cols = out_weight.shape
-    tile = 1024
-    tiles = cols // 2 // tile
-    return pl.pallas_call(
-        half_kernel,
-        grid_spec=pltpu.PrefetchScalarGridSpec(
-            num_scalar_prefetch=1,
-            grid=(tiles,),
-            in_specs=[
-                pl.BlockSpec(memory_space=pl.ANY),
-                pl.BlockSpec((c, tile), lambda j, me_ref: (0, (1 - me_ref[0] % 2) * tiles + j)),
-            ],
-            out_specs=pl.BlockSpec((c, tile), lambda j, me_ref: (0, j)),
-        ),
-        out_shape=jax.ShapeDtypeStruct((c, cols // 2), BF16),
-        compiler_params=params(),
-        cost_estimate=cost(0, 2 * c * cols),
-        name="weight_half",
-    )(me, after, out_weight)
-
-
-def conv_kernel(
-    steps, n, me_ref, after_ref, target_ref, old_ref, moved_ref, x_ref, w_ref, bias_ref, proj_ref, conv_ref, send_ref, keep_ref, win
-):
+def conv_kernel(steps, n, me_ref, target_ref, old_ref, x_ref, w_ref, bias_ref, proj_ref, *refs):
+    zs = n // 4
+    moved, (conv_ref, send_ref, keep_ref, moved_scr, win) = refs[:zs], refs[-5:]
     rows, c = win.shape[1:]
     columns = target_ref.shape[1]
     own = rows // n
-    core = me_ref[0] % 2
+    core, my_z = me_ref[0] % 2, me_ref[0] // 4
+    for m in range(zs):
+        moved_scr[jnp.bitwise_xor(my_z, m)] = moved[m][...]
+    fresh = moved_scr[...].reshape(columns, moved_scr.shape[3])
+    wide = fresh.shape[1]
     row_id = lax.broadcasted_iota(jnp.int32, (rows, columns), 0)
+    hots = [row_id == target_ref[p : p + 1, :] for p in range(TAPS + 1)]
+    taken = jnp.max(hots[0].astype(F32), axis=1, keepdims=True) > 0.0
+    fresh = [jnp.dot(hot.astype(BF16), fresh, preferred_element_type=F32) for hot in hots]
     for p in range(TAPS):
-        hot = row_id == target_ref[p : p + 1, :]
-        taken = jnp.max(hot.astype(F32), axis=1, keepdims=True) > 0.0
-        fresh = jnp.dot(hot.astype(BF16), moved_ref[...], preferred_element_type=F32)
-        win[p] = jnp.where(taken, fresh, old_ref[p])
+        part = (c - wide) * p
+        win[p, :, :wide] = jnp.where(taken, fresh[p], old_ref[p, :, :wide])
+        win[p, :, wide:] = jnp.where(taken, fresh[TAPS][:, part : part + c - wide], old_ref[p, :, wide:])
     for i, t in enumerate(steps):
         total = None
         for q in range(TAPS + 1):
@@ -167,23 +172,26 @@
             num_scalar_prefetch=1,
             grid=(1,),
             in_specs=[
-                pl.BlockSpec(memory_space=pl.ANY),
                 whole(target.shape),
                 whole(old.shape),
-                whole(moved.shape),
                 whole((last, rows, c)),
                 whole(conv_weight.shape),
                 whole((1, c)),
                 whole(proj.shape),
+            ]
+            + [whole(moved[0].shape)] * len(moved)
+            + [pl.BlockSpec(memory_space=pl.ANY)] * len(after),
+            out_specs=[whole((s, rows, c)), whole(parts), whole(parts)],
+            scratch_shapes=[
+                pltpu.VMEM((len(moved),) + moved[0].shape, BF16),
+                pltpu.VMEM((TAPS, rows, c), F32),
             ],
-            out_specs=[whole((s, rows, c)), whole(parts), whole(parts)],
-            scratch_shapes=[pltpu.VMEM((TAPS, rows, c), F32)],
         ),
         out_shape=[jax.ShapeDtypeStruct((s, rows, c), F32)] + [jax.ShapeDtypeStruct(parts, BF16)] * 2,
-        compiler_params=params(),
+        compiler_params=params(40),
         cost_estimate=cost(2 * s * rows * c * 544, rows * c * (12 + 6 * s) + c * 1088, s * rows * c),
         name="conv_project",
-    )(me, after, target, old, moved, step_x, conv_weight, conv_bias, proj)
+    )(me, target, old, step_x, conv_weight, conv_bias, proj, *moved, *after)
 
 
 def add_y_kernel(me_ref, keep_ref, got_ref, send_ref, left_ref):
@@ -228,23 +236,6 @@
         o_ref[jnp.bitwise_xor(z, m)] = ref[...]
 
 
-def small(kernel, me, args, shapes, name, after=()):
-    size = sum(a.size for a in args)
-    return pl.pallas_call(
-        kernel,
-        grid_spec=pltpu.PrefetchScalarGridSpec(
-            num_scalar_prefetch=1,
-            grid=(1,),
-            in_specs=[pl.BlockSpec(memory_space=pl.ANY)] * len(after) + [whole(a.shape) for a in args],
-            out_specs=[whole(s) for s in shapes],
-        ),
-        out_shape=[jax.ShapeDtypeStruct(s, BF16) for s in shapes],
-        compiler_params=params(),
-        cost_estimate=cost(size, 4 * size),
-        name=name,
-    )(me, *after, *args)
-
-
 def reduce_projection(send, keep, gain, me, n):
     zs = n // 4
     piece = keep.shape[1:]
@@ -259,7 +250,7 @@
         in_specs=[whole(gain.shape)] + [whole(piece)] * zs,
         out_specs=whole(piece),
         out_shape=jax.ShapeDtypeStruct(piece, BF16),
-        compiler_params=params(),
+        compiler_params=params(8),
         cost_estimate=cost(cut[0].size * zs, cut[0].size * 2 * zs),
         name="norm",
     )(gain, *cut)
@@ -269,15 +260,13 @@
     return low, (mine, beside, swap(mine, 1, n), swap(beside, 1, n))
 
 
-def state_kernel(first, last, me_ref, slot_ref, *refs):
+def state_kernel(first, last, me_ref, live_ref, *refs):
     if first:
-        moved_ref, fresh_ref, *refs = refs
+        moved_ref, *refs = refs
     else:
         _, *refs = refs
     lows, refs = refs[:4], refs[4:]
-    conv_ref, z_ref, dtp_ref, dtb_ref, alog_ref, skip_ref, *refs = refs
-    states = conv_ref.shape[1] // 128 if first else 1
-    states, refs = refs[:states], refs[states:]
+    conv_ref, z_ref, dtp_ref, dtb_ref, alog_ref, skip_ref, state_ref, *refs = refs
     new_ref = None
     if not last:
         new_ref, *refs = refs
@@ -285,7 +274,34 @@
     block = pl.program_id(0)
     rows, c = step_scr.shape
     take = conv_ref.shape[0]
+    blocks = rows // take
     y, core = (me_ref[0] // 2) % 2, me_ref[0] % 2
+
+    if first:
+        buf, sems = refs
+
+        def fetch(at, slot):
+            first_row = pl.multiple_of(at * (take * STATE), take * STATE)
+            return [
+                pltpu.make_async_copy(
+                    state_ref.at[pl.ds(first_row, take * STATE), 128 * l : 128 * (l + 1)],
+                    buf.at[slot, l],
+                    sems.at[slot, l],
+                )
+                for l in range(c // 128)
+            ]
+
+        now = lax.rem(block, 2)
+
+        @pl.when(block == 0)
+        def _():
+            for copy in fetch(0, 0):
+                copy.start()
+
+        @pl.when(block + 1 < blocks)
+        def _():
+            for copy in fetch(block + 1, 1 - now):
+                copy.start()
 
     @pl.when(block == 0)
     def _():
@@ -295,20 +311,22 @@
         low = low_scr[...].reshape(rows, WIDE)
         pre = jnp.dot(low[:, :DT_RANK], dtp_ref[...], preferred_element_type=F32) + dtb_ref[...]
         step_scr[...] = jnp.maximum(pre, 0.0) + jnp.log(1.0 + jnp.exp(-jnp.abs(pre)))
-        decay_scr[...] = jnp.exp(alog_ref[...]) * (-LOG2E)
+        decay_scr[...] = -jnp.exp(alog_ref[...])
         tail_scr[...] = low[:, DT_RANK:].astype(F32)
 
     base = block * take
     if first:
-        fresh_scr = refs[0]
-        for r in range(take):
-            slot = slot_ref[base + r]
-
-            @pl.when(slot >= 0)
-            def _(r=r, slot=slot):
-                value = moved_ref[slot].astype(F32)
-                for l in range(c // 128):
-                    fresh_scr[l, STATE * r : STATE * (r + 1), :] = value[:, 128 * l : 128 * (l + 1)]
+        for copy in fetch(block, now):
+            copy.wait()
+
+        def replace(i, carry):
+            at = pl.multiple_of((live_ref[1, i] - base) * STATE, STATE)
+            value = moved_ref[live_ref[2, i]].astype(F32)
+            for l in range(c // 128):
+                buf[now, l, pl.ds(at, STATE), :] = value[:, 128 * l : 128 * (l + 1)]
+            return carry
+
+        lax.fori_loop(live_ref[0, block], live_ref[0, block + 1], replace, 0)
 
     tall, lanes = 16, min(512, c)
     for r in range(0, take, tall):
@@ -322,17 +340,11 @@
             for s in range(STATE):
                 if first:
                     at = pl.ds(STATE * r + s, tall, stride=STATE)
-                    taken = fresh_ref[r : r + tall, :] > 0.0
-                    old = jnp.concatenate(
-                        [
-                            jnp.where(taken, fresh_scr[k, at, :], states[k][at, :])
-                            for k in range(l // 128, (l + lanes) // 128)
-                        ],
-                        axis=1,
-                    )
+                    tiles = range(l // 128, (l + lanes) // 128)
+                    old = jnp.concatenate([buf[now, k, at, :] for k in tiles], axis=1)
                 else:
-                    old = states[0][s, r : r + tall, cols].astype(F32)
-                state = jnp.exp2(step * decay_scr[s : s + 1, cols]) * old + drive * tail[:, s : s + 1]
+                    old = state_ref[s, r : r + tall, cols].astype(F32)
+                state = jnp.exp(step * decay_scr[s : s + 1, cols]) * old + drive * tail[:, s : s + 1]
                 if not last:
                     new_ref[s, r : r + tall, cols] = state.astype(BF16)
                 total = total + state * tail[:, STATE + s : STATE + s + 1]
@@ -340,7 +352,7 @@
             gated_ref[r : r + tall, cols] = (total * (z * sigmoid(z))).astype(BF16)
 
 
-def state_step(t, index, me, slot_of_row, extra, lows, conv, step_z, dt_proj, dt_bias, a_log, d_skip, state, n):
+def state_step(t, index, me, live, extra, lows, conv, step_z, dt_proj, dt_bias, a_log, d_skip, state, n):
     _, rows, c = conv.shape
     take = 2 * rows // n
     blocks = rows // take
@@ -348,7 +360,7 @@
     own = rows // n
     zs = n // 4
 
-    def placed(i, me_ref, slot_ref):
+    def placed(i, me_ref, live_ref):
         z, y = i // 2, i % 2
         mine = (y == (me_ref[0] // 2) % 2).astype(jnp.int32)
         return (mine * (blocks // 2) + z, 0)
@@ -369,15 +381,13 @@
     ]
     flat = pl.BlockSpec((STATE, take, c), lambda i, *_: (0, i, 0))
     if first:
-        moved, fresh = extra
-        in_specs = [whole(moved.shape), pl.BlockSpec((take, 128), lambda i, *_: (i, 0))] + in_specs
-        tiles = c // 128
-        in_specs += [pl.BlockSpec((take * STATE, 128), lambda i, *_, l=l: (i, l)) for l in range(tiles)]
-        scratch.append(pltpu.VMEM((tiles, take * STATE, 128), F32))
-        states = [state] * tiles
+        in_specs = [whole(extra[0].shape)] + in_specs + [pl.BlockSpec(memory_space=pl.ANY)]
+        scratch += [
+            pltpu.VMEM((2, c // 128, take * STATE, 128), F32),
+            pltpu.SemaphoreType.DMA((2, c // 128)),
+        ]
     else:
         in_specs = [pl.BlockSpec(memory_space=pl.ANY)] + in_specs + [flat]
-        states = [state]
     out_specs = [pl.BlockSpec((take, c), placed)]
     out_shape = [jax.ShapeDtypeStruct((rows, c), BF16)]
     if not last:
@@ -394,14 +404,15 @@
             scratch_shapes=scratch,
         ),
         out_shape=out_shape,
-        compiler_params=params(),
+        compiler_params=params(32),
         cost_estimate=cost(8 * size, 4 * size, size),
         name="state_step",
-    )(me, slot_of_row, *extra, *lows, conv, step_z, dt_proj, dt_bias, a_log, d_skip, *states)
+    )(me, live, *extra, *lows, conv, step_z, dt_proj, dt_bias, a_log, d_skip, state)
     return (None, out[0]) if last else (out[0], out[1])
 
 
-def out_kernel(me_ref, own_ref, other_ref, wown_ref, wother_ref, send_ref, keep_ref):
+def out_kernel(me_ref, own_ref, other_ref, wown_ref, wother_ref, *refs):
+    send_ref, keep_ref = refs[-2:]
     total = jnp.dot(own_ref[...], wown_ref[...], preferred_element_type=F32)
     total = total + jnp.dot(other_ref[...], wother_ref[...], preferred_element_type=F32)
     half = send_ref.shape[0]
@@ -409,9 +420,9 @@
     keep_ref[...] = total[half:].astype(BF16)
 
 
-def out_project(me, own, other, out_weight, other_weight):
+def out_project(me, own, other, out_weight, other_weight, after):
     rows, c = own.shape
-    cols = other_weight.shape[1]
+    cols = out_weight.shape[1] // 2
     tile = 1024
     tiles = cols // tile
     half = jax.ShapeDtypeStruct((rows // 2, cols), BF16)
@@ -424,15 +435,16 @@
                 whole(own.shape),
                 whole(other.shape),
                 pl.BlockSpec((c, tile), lambda j, me_ref: (0, (me_ref[0] % 2) * tiles + j)),
-                pl.BlockSpec((c, tile), lambda j, me_ref: (0, j)),
-            ],
+                pl.BlockSpec((c, tile), lambda j, me_ref: (0, (me_ref[0] % 2) * tiles + j)),
+            ]
+            + [pl.BlockSpec(memory_space=pl.ANY)] * len(after),
             out_specs=[pl.BlockSpec((rows // 2, tile), lambda j, me_ref: (0, j))] * 2,
         ),
         out_shape=[half, half],
-        compiler_params=params(),
+        compiler_params=params(24),
         cost_estimate=cost(4 * rows * c * cols, 4 * c * cols + 2 * rows * cols),
         name="out_project",
-    )(me, own, other, out_weight, other_weight)
+    )(me, own, other, out_weight, other_weight, *after)
 
 
 def pieces_kernel(behind, me_ref, keep_ref, got_ref, *refs):
@@ -457,7 +469,7 @@
             out_specs=[pl.BlockSpec((take, tile), lambda j, me_ref: (0, j))] * zs,
         ),
         out_shape=[jax.ShapeDtypeStruct((take, cols), BF16)] * zs,
-        compiler_params=params(),
+        compiler_params=params(16),
         cost_estimate=cost(half * cols, 6 * half * cols),
         name="sum_pieces",
     )(me, keep.reshape(zs, take, cols), got.reshape(zs, take, cols), *after)
@@ -497,7 +509,7 @@
             out_specs=pl.BlockSpec((own, STEPS, tile), lambda j, me_ref: (0, 0, j)),
         ),
         out_shape=jax.ShapeDtypeStruct((own, STEPS, 2 * cols), BF16),
-        compiler_params=params(),
+        compiler_params=params(16),
         cost_estimate=cost(0, own * cols * 32),
         name="final_join",
     )(me, *keeps, *gots)
@@ -530,78 +542,88 @@
     me_scalar = lax.axis_index("dex").astype(jnp.int32)
     me = me_scalar.reshape(1)
 
-    packed_conv = pack_conv(prefilled_conv, n)
-    moved_conv = lax.all_to_all(packed_conv, "dex", 0, 0, tiled=True)
-    packed_state = pack_state(packed_conv, prefilled_state, n)
+    packed_state, moved_conv = exchange_conv(prefilled_conv, prefilled_state, me, n)
     moved_state = lax.all_to_all(packed_state, "dex", 0, 0, tiled=True)
-
+    other_weight = swap(out_weight, 1, n)
     cols = out_weight.shape[1] // 2
-    half_weight = weight_half(me, packed_state, out_weight)
-    other_weight = swap(half_weight, 1, n)
 
     is_live = jnp.arange(slots, dtype=jnp.int32)[None, :] < live_counts[:, None]
     target = jnp.where(is_live, batch_rows.reshape(n, slots), -1)
-    spread = jnp.full((TAPS, n, 4, slots), -1, jnp.int32)
-    place = jnp.arange(4, dtype=jnp.int32)[None, None, :, None]
-    tap = jnp.arange(TAPS, dtype=jnp.int32)[:, None, None, None]
-    spread = jnp.where(place == tap, target[None, :, None, :], spread).reshape(TAPS, n * 4 * slots)
-    hit = target.reshape(1, n * slots) == jnp.arange(rows, dtype=jnp.int32)[:, None]
-    slot_of_row = jnp.max(
-        jnp.where(hit, jnp.arange(n * slots, dtype=jnp.int32)[None, :], -1), axis=1
+    place = jnp.arange(TAPS + 1, dtype=jnp.int32)
+    mine = place[None, None, :, None] == place[:, None, None, None]
+    spread = jnp.where(mine, target[None, :, None, :], -1).reshape(TAPS + 1, n * (TAPS + 1) * slots)
+    flat = target.reshape(-1)
+    count = n * slots
+    number = jnp.arange(count, dtype=jnp.int32)
+    key = jnp.where(flat < 0, rows + number, flat)
+    before = jnp.sum((key[None, :] < key[:, None]).astype(jnp.int32), axis=1)
+    hit = before[None, :] == number[:, None]
+    bounds = jnp.arange(count, dtype=jnp.int32) * (2 * rows // n)
+    live = jnp.stack(
+        [
+            jnp.sum((key[None, :] < jnp.minimum(bounds, rows)[:, None]).astype(jnp.int32), axis=1),
+            jnp.sum(jnp.where(hit, key[None, :], 0), axis=1),
+            jnp.sum(jnp.where(hit, number[None, :], 0), axis=1),
+        ]
     )
-    fresh = jnp.broadcast_to(jnp.any(hit, axis=1, keepdims=True).astype(F32), (rows, 128))
     gain = jnp.concatenate([norm_gain, jnp.zeros((WIDE - norm_gain.shape[0],), F32)]).reshape(1, WIDE)
     old = jnp.transpose(resident_conv, (1, 0, 2))
     proj = x_proj.T
     bias = conv_bias.reshape(1, c)
-    moved_conv = moved_conv.reshape(n * 4 * slots, c)
     moved_state = moved_state.reshape(n * slots, STATE, c)
 
     lows = {}
     convs = {}
-    after = half_weight
+    after = ()
     for steps in ((0,), tuple(range(1, STEPS))):
         conv, send, keep = conv_steps(
             steps, n, me, after, spread, old, moved_conv, step_x, conv_weight, bias, proj
         )
-        after, low = reduce_projection(send, keep, gain, me, n)
+        low_rows, low = reduce_projection(send, keep, gain, me, n)
+        after = (low_rows,)
         for i, t in enumerate(steps):
             lows[t] = (low, i)
             convs[t] = conv
 
     state = resident_state.reshape(rows * STATE, c)
-    extra = (moved_state, fresh)
-    sends, keeps, cuts, mine, theirs = [], [], [], [], []
-
-    def reduce_z(t, after):
-        cut = [cuts[t][0]] + [swap(cuts[t][m], 4 * m, n) for m in range(1, zs)]
-        half = (rows // n, cols)
-        send, keep = small(sum_z_kernel, me, cut, [half, half], "sum_z", (after,))
-        mine.append(keep)
-        theirs.append(swap(send, 1, n))
-
-    def reduce_y(t, after):
-        if t > 0:
-            reduce_z(t - 1, after)
-            after = mine[-1]
-        cuts.append(sum_pieces(me, keeps[t], swap(sends[t], 2, n), (after,), n))
-        return (cuts[-1][0],)
-
-    for t in range(STEPS):
+    sends, keeps, cuts, sums, gated = {}, {}, {}, {}, {}
+
+    def s_step(t, extra):
+        nonlocal state
         low, i = lows[t]
-        state, gated = state_step(
-            t, i, me, slot_of_row, extra, low, convs[t], step_z, dt_proj,
+        state, gated[t] = state_step(
+            t, i, me, live, extra, low, convs[t], step_z, dt_proj,
             dt_bias.reshape(1, c), a_log, d_skip.reshape(1, c), state, n,
         )
-        send, keep = out_project(me, gated, swap(gated, 1, n), out_weight, other_weight)
-        sends.append(send)
-        keeps.append(keep)
-        extra = (send,)
-        if t > 0:
-            extra = reduce_y(t - 1, keep)
-    reduce_y(STEPS - 1, keeps[-1])
-    reduce_z(STEPS - 1, keeps[-1])
-    return final_join(me, mine, theirs)
+
+    def project(t, after):
+        sends[t], keeps[t] = out_project(me, gated[t], swap(gated[t], 1, n), out_weight, other_weight, after)
+
+    def reduce_y(t, after):
+        cuts[t] = sum_pieces(me, keeps[t], swap(sends[t], 2, n), after, n)
+
+    def reduce_z(t, after):
+        parts = [cuts[t][0]] + [swap(cuts[t][m], 4 * m, n) for m in range(1, zs)]
+        send, keep = small(sum_z_kernel, me, parts, [(rows // n, cols)] * 2, "sum_z", after)
+        sums[t] = (keep, swap(send, 1, n))
+
+    s_step(0, (moved_state,))
+    s_step(1, (gated[0],))
+    project(0, (gated[1],))
+    s_step(2, (sends[0],))
+    project(1, (gated[2],))
+    reduce_y(0, (keeps[1],))
+    s_step(3, (cuts[0][0],))
+    project(2, (gated[3],))
+    reduce_y(1, (keeps[2],))
+    reduce_z(0, (cuts[1][0],))
+    project(3, (sums[0][0],))
+    reduce_y(2, (keeps[3],))
+    reduce_z(1, (cuts[2][0],))
+    reduce_y(3, (sums[1][0],))
+    reduce_z(2, (cuts[3][0],))
+    reduce_z(3, (sums[2][0],))
+    return final_join(me, [sums[t][0] for t in range(STEPS)], [sums[t][1] for t in range(STEPS)])
 
 
 def solution(mesh):

time: 384 us -> 357 us (0.930)
  Pallas kernels: 165 us -> 96 us
  local copies, waits for them, and re-layouts: 20.7 us -> 59.2 us
  starting transfers between devices: 59.6 us -> 87.3 us
  blocking collectives: 21.4 us -> 0 us
  waiting for transfers between devices: 113 us -> 108 us
    unnamed x122 -> x118, local copies, waits for them, and re-layouts: 18.7 us -> 53.5 us
    ppermute x47 -> x54, starting transfers between devices: 55.5 us -> 80 us  [swap(): return lax.ppermute(x, 'dex', [(i, i ^ mask) for i in range(n)])]
    all_to_all x1 -> x0, blocking collectives: 21.4 us -> none  [shards(): moved_conv = lax.all_to_all(packed_conv, 'dex', 0, 0, tiled=True)]
    pallas_call x4, Pallas kernels: 64.5 us -> 46.6 us  [state_step(): pl.pallas_call(functools.partial(state_kernel, first, last), grid_spec=pl...]
    pallas_call x10 -> x12, Pallas kernels: 18.3 us -> 2.26 us  [small(): pl.pallas_call(kernel, grid_spec=pltpu.PrefetchScalarGridSpec(num_scalar_...]
    pallas_call x2 -> x0, Pallas kernels: 9.23 us -> none  [the longest x1 7.22 us: weight_half(): pl.pallas_call(half_kernel, grid_spec=pltpu.PrefetchScalarGridSpec(num_sc...]
    pallas_call x2, Pallas kernels: 12.6 us -> 4.85 us  [conv_steps(): pl.pallas_call(functools.partial(conv_kernel, steps, n), grid_spec=pltpu....]
    pallas_call x4, Pallas kernels: 39.2 us -> 33.4 us  [out_project(): pl.pallas_call(out_kernel, grid_spec=pltpu.PrefetchScalarGridSpec(num_sca...]
  transfers between devices with their start and end apart: 48 -> 55, of which waited for: 18 -> 24; matrix products, arithmetic and copies ran while one was open for 1% -> 2% of each run, Pallas kernels for 34% -> 27%
where the time goes in v3:
time: 357 us; the launch traced here: 354 us
  waiting for transfers between devices  108 us (30%)
  Pallas kernels  96 us (27%)
  starting transfers between devices  87.3 us (24%)
  local copies, waits for them, and re-layouts  59.2 us (17%)
    ppermute x54, waiting for transfers between devices, swap(): return lax.ppermute(x, 'dex', [(i, i ^ mask) for i in range(n)])  108 us
    ppermute x54, starting transfers between devices, swap(): return lax.ppermute(x, 'dex', [(i, i ^ mask) for i in range(n)])  80 us
    unnamed x118, local copies, waits for them, and re-layouts  53.5 us
    pallas_call x4, Pallas kernels, state_step(): pl.pallas_call(functools.partial(state_kernel, first, last), grid_spec=pl...  46.6 us
    pallas_call x4, Pallas kernels, out_project(): pl.pallas_call(out_kernel, grid_spec=pltpu.PrefetchScalarGridSpec(num_sca...  33.4 us
    all_to_all x1, starting transfers between devices, shards(): moved_state = lax.all_to_all(packed_state, 'dex', 0, 0, tiled=True)  7.36 us
  transfers between devices with their start and end apart: 55, of which 24 were waited for; matrix products, arithmetic and copies ran while one was open for 2% of the time, Pallas kernels for 27%

profile of v3, /device:TPU:0, one launch (start us, length us, event | category | flops | bytes accessed | tf_op | source)
XLA Modules:
  0.0 353.6 jit_solution(9846234451354953708)
XLA Ops:
  2.3 2.2 copy-done.17
  4.5 2.1 pack_state.1.after_ref
  6.6 7.4 %all-to-all-start = ((bf16[16,64,1024]{2,1,0:T(8,128)(2,1)}), bf16[16,64,1024]{2,1,0:T(8,128)(2,1)}, u32[]{:S(2)}, u32[]{:S(2)}) async-start(bf16[16,64,1024]{2,1,0:T(8,128)(2,1)} %pack_state.1.after_ref), calls=%async_computation | async-start | bytes 4194304 | tf_op jit(solution)/shard_map/all_to_all | solution.py:546
  14.4 1.7 collective-permute-start
  20.3 5.5 %collective-permute-done.2 = bf16[4,16,768]{2,1,0:T(8,128)(2,1)} collective-permute-done((bf16[4,16,768]{2,1,0:T(8,128)(2,1)S(1)}, bf16[4,16,768]{2,1,0:T(8,128)(2,1)}, u32[]{:S(2)}, u32[]{:S(2)}) %collective-permute-start.2) | collective-permute-done | bytes 98336 | tf_op jit(solution)/shard_map/ppermute | solution.py:28
  25.8 2.9 collective-permute-start.3
  31.9 5.3 %collective-permute-done.3.refs_3_ = bf16[4,16,768]{2,1,0:T(8,128)(2,1)S(1)} collective-permute-done((bf16[4,16,768]{2,1,0:T(8,128)(2,1)}, bf16[4,16,768]{2,1,0:T(8,128)(2,1)S(1)}, u32[]{:S(2)}, u32[]{:S(2)}) %collective-permute-start.3) | collective-permute-done | bytes 98336 | tf_op jit(solution)/shard_map/ppermute | solution.py:28
  39.3 1.8 collective-permute-start.5
  41.1 2.2 collective-permute-start.6
  43.9 7.2 %collective-permute-done.4.refs_1_ = bf16[4,16,768]{2,1,0:T(8,128)(2,1)S(1)} collective-permute-done((bf16[4,16,768]{2,1,0:T(8,128)(2,1)S(1)}, bf16[4,16,768]{2,1,0:T(8,128)(2,1)S(1)}, u32[]{:S(2)}, u32[]{:S(2)}) %collective-permute-start.4) | collective-permute-done | bytes 98336 | tf_op jit(solution)/shard_map/ppermute | solution.py:28
  51.2 18.6 %collective-permute-done.5.refs_2_ = bf16[4,16,768]{2,1,0:T(8,128)(2,1)S(1)} collective-permute-done((bf16[4,16,768]{2,1,0:T(8,128)(2,1)S(1)}, bf16[4,16,768]{2,1,0:T(8,128)(2,1)S(1)}, u32[]{:S(2)}, u32[]{:S(2)}) %collective-permute-start.5) | collective-permute-done | bytes 98336 | tf_op jit(solution)/shard_map/ppermute | solution.py:28
  69.8 1.6 copy-done.15
  73.3 1.6 conv_project.2
  77.4 1.6 collective-permute-start.8
  79.0 2.9 collective-permute-done.8.got_ref
  82.0 2.3 collective-permute-start.10
  84.3 2.3 collective-permute-start.11
  86.9 2.9 collective-permute-done.11.refs_3_
  90.5 3.2 conv_project.3
  93.8 1.7 copy-done.4
  95.5 1.9 collective-permute-done.18.got_ref
  97.5 1.6 collective-permute-start.19
  99.1 6.4 %collective-permute-done.19.got_ref = bf16[4,3,16,640]{3,2,1,0:T(8,128)(2,1)S(1)} collective-permute-done((bf16[4,3,16,640]{3,2,1,0:T(8,128)(2,1)S(1)}, bf16[4,3,16,640]{3,2,1,0:T(8,128)(2,1)S(1)}, u32[]{:S(2)}, u32[]{:S(2)}) %collective-permute-start.19) | collective-permute-done | bytes 245792 | tf_op jit(solution)/shard_map/ppermute | solution.py:28
  106.5 2.1 collective-permute-start.21
  108.6 2.0 collective-permute-start.22
  110.8 2.4 collective-permute-done.21.refs_2_
  114.9 2.6 collective-permute-start.24
  117.4 1.8 collective-permute-start.25
  119.9 2.6 collective-permute-start.13
  122.5 1.8 collective-permute-start.14
  124.3 1.6 collective-permute-start.26
  126.2 1.9 collective-permute-done.14.refs_3_
  128.8 1.6 collective-permute-start.15
  130.7 2.6 collective-permute-done.15.refs_2_
  140.6 15.8 %state_step.4 = (bf16[16,256,1024]{2,1,0:T(8,128)(2,1)S(1)}, bf16[256,1024]{1,0:T(8,128)(2,1)S(1)}) custom-call(s32[1]{0:T(128)} %bitcast.me_ref, s32[3,64]{1,0:T(4,128)S(1)} %pad_add_fusion.live_ref, bf16[64,16,1024]{2,1,0:T(8,128)(2,1)} %bitcast.5.refs_0_, bf16[4,1,16,640]{3,2,1,0:T(8,128)(2,1)S(1)} %merge_z.2.refs_1_, ...), custom_call_target="tpu_custom_call" | custom-call | flops 1024 | bytes 1024 | tf_op jit(solution)/shard_map/state_step/pallas_call | solution.py:397
  156.4 3.3 copy-done.13
  160.7 1.7 collective-permute-done.27.refs_3_
  162.7 10.6 %state_step.5 = (bf16[16,256,1024]{2,1,0:T(8,128)(2,1)S(1)}, bf16[256,1024]{1,0:T(8,128)(2,1)S(1)}) custom-call(s32[1]{0:T(128)} %bitcast.me_ref, s32[3,64]{1,0:T(4,128)S(1)} %pad_add_fusion.live_ref, bf16[256,1024]{1,0:T(8,128)(2,1)S(1)} %get-tuple-element.86.refs_0_.own_ref, bf16[4,3,16,640]{3,2,1,0:T(8,128)(2,1)S(1)} %merge_z.3.refs_1_, ...), custom_call_target="tpu_custom_call" | custom-call | flops 1024 | bytes 1024 | tf_op jit(solution)/shard_map/state_step/pallas_call | solution.py:397
  173.3 3.3 copy-done.14
  177.0 5.8 %copy-done = bf16[1024,8192]{1,0:T(8,128)(2,1)S(1)} copy-done((bf16[1024,8192]{1,0:T(8,128)(2,1)S(1)}, bf16[1024,8192]{1,0:T(8,128)(2,1)}, u32[]{:S(2)}) %copy-start) | copy-done | bytes 16777240
  182.8 8.1 %out_project.4 = (bf16[128,4096]{1,0:T(8,128)(2,1)}, bf16[128,4096]{1,0:T(8,128)(2,1)S(1)}) custom-call(s32[1]{0:T(128)} %bitcast.me_ref, bf16[256,1024]{1,0:T(8,128)(2,1)S(1)} %get-tuple-element.86.refs_0_.own_ref, bf16[256,1024]{1,0:T(8,128)(2,1)S(1)} %collective-permute-done.31.other_ref, bf16[1024,8192]{1,0:T(8,128)(2,1)S(1)} %copy-done, ...), custom_call_target="tpu_custom_call" | custom-call | flops 1024 | bytes 1024 | tf_op jit(solution)/shard_map/out_project/pallas_call | solution.py:429
  193.5 11.3 %state_step.6 = (bf16[16,256,1024]{2,1,0:T(8,128)(2,1)S(1)}, bf16[256,1024]{1,0:T(8,128)(2,1)}) custom-call(s32[1]{0:T(128)} %bitcast.me_ref, s32[3,64]{1,0:T(4,128)S(1)} %pad_add_fusion.live_ref, bf16[128,4096]{1,0:T(8,128)(2,1)} %get-tuple-element.98.refs_0_, bf16[4,3,16,640]{3,2,1,0:T(8,128)(2,1)S(1)} %merge_z.3.refs_1_, ...), custom_call_target="tpu_custom_call" | custom-call | flops 1024 | bytes 1024 | tf_op jit(solution)/shard_map/state_step/pallas_call | solution.py:397
  204.7 3.3 copy-done.11
  208.9 5.8 %copy-done.1 = bf16[1024,8192]{1,0:T(8,128)(2,1)S(1)} copy-done((bf16[1024,8192]{1,0:T(8,128)(2,1)S(1)}, bf16[1024,8192]{1,0:T(8,128)(2,1)}, u32[]{:S(2)}) %copy-start.1) | copy-done | bytes 16777240
  215.7 9.8 %out_project.5 = (bf16[128,4096]{1,0:T(8,128)(2,1)}, bf16[128,4096]{1,0:T(8,128)(2,1)S(1)}) custom-call(s32[1]{0:T(128)} %bitcast.me_ref, bf16[256,1024]{1,0:T(8,128)(2,1)S(1)} %get-tuple-element.97.refs_0_.own_ref, bf16[256,1024]{1,0:T(8,128)(2,1)S(1)} %copy-done.33, bf16[1024,8192]{1,0:T(8,128)(2,1)S(1)} %copy-done.1, ...), custom_call_target="tpu_custom_call" | custom-call | flops 1024 | bytes 1024 | tf_op jit(solution)/shard_map/out_project/pallas_call | solution.py:429
  226.0 1.9 sum_pieces.4
  228.8 1.9 copy-done.6
  231.9 3.4 copy-done.12
  238.1 8.9 %state_step.7.refs_0_.own_ref = bf16[256,1024]{1,0:T(8,128)(2,1)S(1)} custom-call(s32[1]{0:T(128)} %bitcast.me_ref, s32[3,64]{1,0:T(4,128)S(1)} %pad_add_fusion.live_ref, bf16[32,4096]{1,0:T(8,128)(2,1)S(1)} %get-tuple-element.104.refs_0_, bf16[4,3,16,640]{3,2,1,0:T(8,128)(2,1)S(1)} %copy-done.21, bf16[4,3,16,640]{3,2,1,0:T(8,128)(2,1)} %collective-permute-done.26.refs_2_, ...), custom_call_target="tpu_custom_call" | custom-call | flops 1024 | bytes 1024 | tf_op jit(solution)/shard_map/state_step/pallas_call | solution.py:397
  247.1 2.4 collective-permute-start.36
  249.5 2.0 collective-permute-start.37
  251.5 7.8 %out_project.6 = (bf16[128,4096]{1,0:T(8,128)(2,1)S(1)}, bf16[128,4096]{1,0:T(8,128)(2,1)S(1)}) custom-call(s32[1]{0:T(128)} %bitcast.me_ref, bf16[256,1024]{1,0:T(8,128)(2,1)} %get-tuple-element.100.refs_0_.own_ref, bf16[256,1024]{1,0:T(8,128)(2,1)} %collective-permute-done.33.other_ref, bf16[1024,8192]{1,0:T(8,128)(2,1)S(1)} %bitcast.21, ...), custom_call_target="tpu_custom_call" | custom-call | flops 1024 | bytes 1024 | tf_op jit(solution)/shard_map/out_project/pallas_call | solution.py:429
  262.4 6.3 %collective-permute-done.36.refs_2_ = bf16[32,4096]{1,0:T(8,128)(2,1)S(1)} collective-permute-done((bf16[32,4096]{1,0:T(8,128)(2,1)}, bf16[32,4096]{1,0:T(8,128)(2,1)S(1)}, u32[]{:S(2)}, u32[]{:S(2)}) %collective-permute-start.36) | collective-permute-done | bytes 262176 | tf_op jit(solution)/shard_map/ppermute | solution.py:28
  268.9 7.6 %out_project.7 = (bf16[128,4096]{1,0:T(8,128)(2,1)S(1)}, bf16[128,4096]{1,0:T(8,128)(2,1)S(1)}) custom-call(s32[1]{0:T(128)} %bitcast.me_ref, bf16[256,1024]{1,0:T(8,128)(2,1)S(1)} %state_step.7.refs_0_.own_ref, bf16[256,1024]{1,0:T(8,128)(2,1)S(1)} %collective-permute-done.39.other_ref, bf16[1024,8192]{1,0:T(8,128)(2,1)S(1)} %bitcast.21, ...), custom_call_target="tpu_custom_call" | custom-call | flops 1024 | bytes 1024 | tf_op jit(solution)/shard_map/out_project/pallas_call | solution.py:429
  278.0 5.4 %collective-permute-start.40 = (bf16[32,4096]{1,0:T(8,128)(2,1)S(1)}, bf16[32,4096]{1,0:T(8,128)(2,1)S(1)}, u32[]{:S(2)}, u32[]{:S(2)}) collective-permute-start(bf16[32,4096]{1,0:T(8,128)(2,1)S(1)} %get-tuple-element.115), channel_id=1, source_target_pairs={{0,4},{1,5},{2,6},{3,7},{4,0},{5,1},{6,2},{7,3},{8,12},{9,13},{10,... | collective-permute-start | bytes 786440 | tf_op jit(solution)/shard_map/ppermute | solution.py:28
  283.7 2.0 collective-permute-start.42
  287.5 7.8 %collective-permute-done.40.refs_1_ = bf16[32,4096]{1,0:T(8,128)(2,1)S(1)} collective-permute-done((bf16[32,4096]{1,0:T(8,128)(2,1)S(1)}, bf16[32,4096]{1,0:T(8,128)(2,1)S(1)}, u32[]{:S(2)}, u32[]{:S(2)}) %collective-permute-start.40) | collective-permute-done | bytes 262176 | tf_op jit(solution)/shard_map/ppermute | solution.py:28
  295.3 9.5 %collective-permute-done.41.refs_2_ = bf16[32,4096]{1,0:T(8,128)(2,1)S(1)} collective-permute-done((bf16[32,4096]{1,0:T(8,128)(2,1)S(1)}, bf16[32,4096]{1,0:T(8,128)(2,1)S(1)}, u32[]{:S(2)}, u32[]{:S(2)}) %collective-permute-start.41) | collective-permute-done | bytes 262176 | tf_op jit(solution)/shard_map/ppermute | solution.py:28
  304.8 1.8 collective-permute-start.46
  307.3 20.8 %collective-permute-start.47 = (bf16[32,4096]{1,0:T(8,128)(2,1)S(1)}, bf16[32,4096]{1,0:T(8,128)(2,1)S(1)}, u32[]{:S(2)}, u32[]{:S(2)}) collective-permute-start(bf16[32,4096]{1,0:T(8,128)(2,1)S(1)} %get-tuple-element.125), channel_id=1, source_target_pairs={{0,4},{1,5},{2,6},{3,7},{4,0},{5,1},{6,2},{7,3},{8,12},{9,13},{10,... | collective-permute-start | bytes 786440 | tf_op jit(solution)/shard_map/ppermute | solution.py:28
  328.2 2.4 collective-permute-start.49
  330.6 7.9 %collective-permute-done.45.refs_2_ = bf16[32,4096]{1,0:T(8,128)(2,1)S(1)} collective-permute-done((bf16[32,4096]{1,0:T(8,128)(2,1)S(1)}, bf16[32,4096]{1,0:T(8,128)(2,1)S(1)}, u32[]{:S(2)}, u32[]{:S(2)}) %collective-permute-start.45) | collective-permute-done | bytes 262176 | tf_op jit(solution)/shard_map/ppermute | solution.py:28
  339.3 10.5 %collective-permute-done.48.refs_2_ = bf16[32,4096]{1,0:T(8,128)(2,1)S(1)} collective-permute-done((bf16[32,4096]{1,0:T(8,128)(2,1)S(1)}, bf16[32,4096]{1,0:T(8,128)(2,1)S(1)}, u32[]{:S(2)}, u32[]{:S(2)}) %collective-permute-start.48) | collective-permute-done | bytes 262176 | tf_op jit(solution)/shard_map/ppermute | solution.py:28
  351.3 2.2 final_join.1
  (211 shorter events, 51.3 us)
Async XLA Ops:
  0.0 177.0 %collective-permute-start.30 = (bf16[1024,8192]{1,0:T(8,128)(2,1)}, bf16[1024,8192]{1,0:T(8,128)(2,1)}, u32[]{:S(2)}, u32[]{:S(2)}) collective-permute-start(bf16[1024,8192]{1,0:T(8,128)(2,1)} %wown_ref.7), channel_id=1, source_target_pairs={{0,1},{1,0},{2,3},{3,2},{4,5},{5,4},{6,7},{7,6},{8,9},{9,8},{10,11... | collective-permute-start | bytes 50331656 | tf_op jit(solution)/shard_map/ppermute | solution.py:28
  6.6 63.2 %copy-start.9 = (f32[256,3,1024]{2,0,1:T(8,128)S(1)}, f32[256,3,1024]{2,0,1:T(8,128)}, u32[]{:S(2)}) copy-start(f32[256,3,1024]{2,0,1:T(8,128)} %param.18) | copy-start | bytes 9437188
  6.6 63.2 %copy-start.44 = (f32[4,1024]{1,0:T(4,128)S(1)}, f32[4,1024]{1,0:T(4,128)}, u32[]{:S(2)}) copy-start(f32[4,1024]{1,0:T(4,128)} %w_ref.3) | copy-start | bytes 49156
  6.6 128.6 %all-to-all-start = ((bf16[16,64,1024]{2,1,0:T(8,128)(2,1)}), bf16[16,64,1024]{2,1,0:T(8,128)(2,1)}, u32[]{:S(2)}, u32[]{:S(2)}) async-start(bf16[16,64,1024]{2,1,0:T(8,128)(2,1)} %pack_state.1.after_ref), calls=%async_computation | async-start | bytes 4194304 | tf_op jit(solution)/shard_map/all_to_all | solution.py:546
  14.0 11.8 %collective-permute-start.2 = (bf16[4,16,768]{2,1,0:T(8,128)(2,1)S(1)}, bf16[4,16,768]{2,1,0:T(8,128)(2,1)}, u32[]{:S(2)}, u32[]{:S(2)}) collective-permute-start(bf16[4,16,768]{2,1,0:T(8,128)(2,1)S(1)} %get-tuple-element.72), channel_id=1, source_target_pairs={{0,1},{1,0},{2,3},{3,2},{4,5},{5,4},{6,7},{7,6},{8,9},{9,8},{10,11... | collective-permute-start | bytes 294920 | tf_op jit(solution)/shard_map/ppermute | solution.py:28
  14.4 17.6 %collective-permute-start = (bf16[4,16,768]{2,1,0:T(8,128)(2,1)}, bf16[4,16,768]{2,1,0:T(8,128)(2,1)S(1)}, u32[]{:S(2)}, u32[]{:S(2)}) collective-permute-start(bf16[4,16,768]{2,1,0:T(8,128)(2,1)} %get-tuple-element.70), channel_id=1, source_target_pairs={{0,2},{1,3},{2,0},{3,1},{4,6},{5,7},{6,4},{7,5},{8,10},{9,11},{10,... | collective-permute-start | bytes 294920 | tf_op jit(solution)/shard_map/ppermute | solution.py:28
  16.0 15.9 %collective-permute-start.1 = (bf16[4,16,768]{2,1,0:T(8,128)(2,1)}, bf16[4,16,768]{2,1,0:T(8,128)(2,1)S(1)}, u32[]{:S(2)}, u32[]{:S(2)}) collective-permute-start(bf16[4,16,768]{2,1,0:T(8,128)(2,1)} %get-tuple-element.71), channel_id=1, source_target_pairs={{0,1},{1,0},{2,3},{3,2},{4,5},{5,4},{6,7},{7,6},{8,9},{9,8},{10,11... | collective-permute-start | bytes 294920 | tf_op jit(solution)/shard_map/ppermute | solution.py:28
  25.8 11.4 %collective-permute-start.3 = (bf16[4,16,768]{2,1,0:T(8,128)(2,1)}, bf16[4,16,768]{2,1,0:T(8,128)(2,1)S(1)}, u32[]{:S(2)}, u32[]{:S(2)}) collective-permute-start(bf16[4,16,768]{2,1,0:T(8,128)(2,1)} %collective-permute-done.2), channel_id=1, source_target_pairs={{0,2},{1,3},{2,0},{3,1},{4,6},{5,7},{6,4},{7,5},{8,10},{9,11},{10,... | collective-permute-start | bytes 294920 | tf_op jit(solution)/shard_map/ppermute | solution.py:28
  38.8 47.8 %copy-start.53 = (f32[544]{0:T(1024)S(1)}, f32[544]{0:T(1024)}, u32[]{:S(2)}) copy-start(f32[544]{0:T(1024)} %param.28) | copy-start | bytes 6532
  38.8 51.7 %copy-start.10 = (f32[256,3,1024]{2,0,1:T(8,128)S(1)}, f32[256,3,1024]{2,0,1:T(8,128)}, u32[]{:S(2)}) copy-start(f32[256,3,1024]{2,0,1:T(8,128)} %param.18) | copy-start | bytes 9437188
  38.8 12.4 %collective-permute-start.4 = (bf16[4,16,768]{2,1,0:T(8,128)(2,1)S(1)}, bf16[4,16,768]{2,1,0:T(8,128)(2,1)S(1)}, u32[]{:S(2)}, u32[]{:S(2)}) collective-permute-start(bf16[4,16,768]{2,1,0:T(8,128)(2,1)S(1)} %get-tuple-element.74), channel_id=1, source_target_pairs={{0,4},{1,5},{2,6},{3,7},{4,0},{5,1},{6,2},{7,3},{8,12},{9,13},{10,... | collective-permute-start | bytes 294920 | tf_op jit(solution)/shard_map/ppermute | solution.py:28
  39.3 30.5 %collective-permute-start.5 = (bf16[4,16,768]{2,1,0:T(8,128)(2,1)S(1)}, bf16[4,16,768]{2,1,0:T(8,128)(2,1)S(1)}, u32[]{:S(2)}, u32[]{:S(2)}) collective-permute-start(bf16[4,16,768]{2,1,0:T(8,128)(2,1)S(1)} %get-tuple-element.75), channel_id=1, source_target_pairs={{0,8},{1,9},{2,10},{3,11},{4,12},{5,13},{6,14},{7,15},{8,0},{9,1},... | collective-permute-start | bytes 294920 | tf_op jit(solution)/shard_map/ppermute | solution.py:28
  41.1 28.7 %collective-permute-start.6 = (bf16[4,16,768]{2,1,0:T(8,128)(2,1)S(1)}, bf16[4,16,768]{2,1,0:T(8,128)(2,1)S(1)}, u32[]{:S(2)}, u32[]{:S(2)}) collective-permute-start(bf16[4,16,768]{2,1,0:T(8,128)(2,1)S(1)} %get-tuple-element.76), channel_id=1, source_target_pairs={{0,12},{1,13},{2,14},{3,15},{4,8},{5,9},{6,10},{7,11},{8,4},{9,5},... | collective-permute-start | bytes 294920 | tf_op jit(solution)/shard_map/ppermute | solution.py:28
  75.9 1.4 collective-permute-start.7
  77.4 4.6 %collective-permute-start.8 = (bf16[4,1,16,640]{3,2,1,0:T(8,128)(2,1)S(1)}, bf16[4,1,16,640]{3,2,1,0:T(8,128)(2,1)S(1)}, u32[]{:S(2)}, u32[]{:S(2)}) collective-permute-start(bf16[4,1,16,640]{3,2,1,0:T(8,128)(2,1)S(1)} %get-tuple-element.80), channel_id=1, source_target_pairs={{0,2},{1,3},{2,0},{3,1},{4,6},{5,7},{6,4},{7,5},{8,10},{9,11},{10,... | collective-permute-start | bytes 245768 | tf_op jit(solution)/shard_map/ppermute | solution.py:28
  82.0 4.9 %collective-permute-start.10 = (bf16[1,16,640]{2,1,0:T(8,128)(2,1)S(1)}, bf16[1,16,640]{2,1,0:T(8,128)(2,1)S(1)}, u32[]{:S(2)}, u32[]{:S(2)}) collective-permute-start(bf16[1,16,640]{2,1,0:T(8,128)(2,1)S(1)} %get-tuple-element.83), channel_id=1, source_target_pairs={{0,8},{1,9},{2,10},{3,11},{4,12},{5,13},{6,14},{7,15},{8,0},{9,1},... | collective-permute-start | bytes 61448 | tf_op jit(solution)/shard_map/ppermute | solution.py:28
  84.3 5.6 %collective-permute-start.11 = (bf16[1,16,640]{2,1,0:T(8,128)(2,1)S(1)}, bf16[1,16,640]{2,1,0:T(8,128)(2,1)S(1)}, u32[]{:S(2)}, u32[]{:S(2)}) collective-permute-start(bf16[1,16,640]{2,1,0:T(8,128)(2,1)S(1)} %get-tuple-element.84), channel_id=1, source_target_pairs={{0,12},{1,13},{2,14},{3,15},{4,8},{5,9},{6,10},{7,11},{8,4},{9,5},... | collective-permute-start | bytes 61448 | tf_op jit(solution)/shard_map/ppermute | solution.py:28
  86.6 3.8 %collective-permute-start.9 = (bf16[1,16,640]{2,1,0:T(8,128)(2,1)S(1)}, bf16[1,16,640]{2,1,0:T(8,128)(2,1)S(1)}, u32[]{:S(2)}, u32[]{:S(2)}) collective-permute-start(bf16[1,16,640]{2,1,0:T(8,128)(2,1)S(1)} %get-tuple-element.82), channel_id=1, source_target_pairs={{0,4},{1,5},{2,6},{3,7},{4,0},{5,1},{6,2},{7,3},{8,12},{9,13},{10,... | collective-permute-start | bytes 61448 | tf_op jit(solution)/shard_map/ppermute | solution.py:28
  90.5 44.8 %copy-start.2 = (bf16[4,256,1024]{2,1,0:T(8,128)(2,1)S(1)}, bf16[4,256,1024]{2,1,0:T(8,128)(2,1)}, u32[]{:S(2)}) copy-start(bf16[4,256,1024]{2,1,0:T(8,128)(2,1)} %refs_6_.7) | copy-start | bytes 6291460
  90.5 44.8 %copy-start.7 = (bf16[512,1024]{1,0:T(8,128)(2,1)S(1)}, bf16[512,1024]{1,0:T(8,128)(2,1)}, u32[]{:S(2)}) copy-start(bf16[512,1024]{1,0:T(8,128)(2,1)} %refs_7_.7) | copy-start | bytes 3145732
  90.5 44.8 %copy-start.26 = (f32[16,1024]{1,0:T(8,128)S(1)}, f32[16,1024]{1,0:T(8,128)}, u32[]{:S(2)}) copy-start(f32[16,1024]{1,0:T(8,128)} %refs_9_.7) | copy-start | bytes 196612
  95.5 1.9 collective-permute-start.18
  97.5 8.1 %collective-permute-start.19 = (bf16[4,3,16,640]{3,2,1,0:T(8,128)(2,1)S(1)}, bf16[4,3,16,640]{3,2,1,0:T(8,128)(2,1)S(1)}, u32[]{:S(2)}, u32[]{:S(2)}) collective-permute-start(bf16[4,3,16,640]{3,2,1,0:T(8,128)(2,1)S(1)} %get-tuple-element.90), channel_id=1, source_target_pairs={{0,2},{1,3},{2,0},{3,1},{4,6},{5,7},{6,4},{7,5},{8,10},{9,11},{10,... | collective-permute-start | bytes 737288 | tf_op jit(solution)/shard_map/ppermute | solution.py:28
  106.3 4.6 %collective-permute-start.20 = (bf16[3,16,640]{2,1,0:T(8,128)(2,1)}, bf16[3,16,640]{2,1,0:T(8,128)(2,1)S(1)}, u32[]{:S(2)}, u32[]{:S(2)}) collective-permute-start(bf16[3,16,640]{2,1,0:T(8,128)(2,1)} %get-tuple-element.92), channel_id=1, source_target_pairs={{0,4},{1,5},{2,6},{3,7},{4,0},{5,1},{6,2},{7,3},{8,12},{9,13},{10,... | collective-permute-start | bytes 184328 | tf_op jit(solution)/shard_map/ppermute | solution.py:28
  106.5 6.7 %collective-permute-start.21 = (bf16[3,16,640]{2,1,0:T(8,128)(2,1)}, bf16[3,16,640]{2,1,0:T(8,128)(2,1)S(1)}, u32[]{:S(2)}, u32[]{:S(2)}) collective-permute-start(bf16[3,16,640]{2,1,0:T(8,128)(2,1)} %get-tuple-element.93), channel_id=1, source_target_pairs={{0,8},{1,9},{2,10},{3,11},{4,12},{5,13},{6,14},{7,15},{8,0},{9,1},... | collective-permute-start | bytes 184328 | tf_op jit(solution)/shard_map/ppermute | solution.py:28
  108.6 6.0 %collective-permute-start.22 = (bf16[3,16,640]{2,1,0:T(8,128)(2,1)S(1)}, bf16[3,16,640]{2,1,0:T(8,128)(2,1)S(1)}, u32[]{:S(2)}, u32[]{:S(2)}) collective-permute-start(bf16[3,16,640]{2,1,0:T(8,128)(2,1)S(1)} %get-tuple-element.94), channel_id=1, source_target_pairs={{0,12},{1,13},{2,14},{3,15},{4,8},{5,9},{6,10},{7,11},{8,4},{9,5},... | collective-permute-start | bytes 184328 | tf_op jit(solution)/shard_map/ppermute | solution.py:28
  114.8 5.1 %collective-permute-start.23 = (bf16[3,16,640]{2,1,0:T(8,128)(2,1)S(1)}, bf16[3,16,640]{2,1,0:T(8,128)(2,1)S(1)}, u32[]{:S(2)}, u32[]{:S(2)}) collective-permute-start(bf16[3,16,640]{2,1,0:T(8,128)(2,1)S(1)} %norm.3.refs_0_), channel_id=1, source_target_pairs={{0,4},{1,5},{2,6},{3,7},{4,0},{5,1},{6,2},{7,3},{8,12},{9,13},{10,... | collective-permute-start | bytes 184328 | tf_op jit(solution)/shard_map/ppermute | solution.py:28
  114.9 7.6 %collective-permute-start.24 = (bf16[3,16,640]{2,1,0:T(8,128)(2,1)S(1)}, bf16[3,16,640]{2,1,0:T(8,128)(2,1)S(1)}, u32[]{:S(2)}, u32[]{:S(2)}) collective-permute-start(bf16[3,16,640]{2,1,0:T(8,128)(2,1)S(1)} %norm.3.refs_0_), channel_id=1, source_target_pairs={{0,8},{1,9},{2,10},{3,11},{4,12},{5,13},{6,14},{7,15},{8,0},{9,1},... | collective-permute-start | bytes 184328 | tf_op jit(solution)/shard_map/ppermute | solution.py:28
  117.4 6.9 %collective-permute-start.25 = (bf16[3,16,640]{2,1,0:T(8,128)(2,1)S(1)}, bf16[3,16,640]{2,1,0:T(8,128)(2,1)S(1)}, u32[]{:S(2)}, u32[]{:S(2)}) collective-permute-start(bf16[3,16,640]{2,1,0:T(8,128)(2,1)S(1)} %norm.3.refs_0_), channel_id=1, source_target_pairs={{0,12},{1,13},{2,14},{3,15},{4,8},{5,9},{6,10},{7,11},{8,4},{9,5},... | collective-permute-start | bytes 184328 | tf_op jit(solution)/shard_map/ppermute | solution.py:28
  119.9 6.2 %collective-permute-start.12 = (bf16[1,16,640]{2,1,0:T(8,128)(2,1)S(1)}, bf16[1,16,640]{2,1,0:T(8,128)(2,1)S(1)}, u32[]{:S(2)}, u32[]{:S(2)}) collective-permute-start(bf16[1,16,640]{2,1,0:T(8,128)(2,1)S(1)} %norm.2.refs_0_.refs_4_), channel_id=1, source_target_pairs={{0,4},{1,5},{2,6},{3,7},{4,0},{5,1},{6,2},{7,3},{8,12},{9,13},{10,... | collective-permute-start | bytes 61448 | tf_op jit(solution)/shard_map/ppermute | solution.py:28
  119.9 6.2 %collective-permute-start.13 = (bf16[1,16,640]{2,1,0:T(8,128)(2,1)S(1)}, bf16[1,16,640]{2,1,0:T(8,128)(2,1)S(1)}, u32[]{:S(2)}, u32[]{:S(2)}) collective-permute-start(bf16[1,16,640]{2,1,0:T(8,128)(2,1)S(1)} %norm.2.refs_0_.refs_4_), channel_id=1, source_target_pairs={{0,8},{1,9},{2,10},{3,11},{4,12},{5,13},{6,14},{7,15},{8,0},{9,1},... | collective-permute-start | bytes 61448 | tf_op jit(solution)/shard_map/ppermute | solution.py:28
  122.5 5.6 %collective-permute-start.14 = (bf16[1,16,640]{2,1,0:T(8,128)(2,1)S(1)}, bf16[1,16,640]{2,1,0:T(8,128)(2,1)S(1)}, u32[]{:S(2)}, u32[]{:S(2)}) collective-permute-start(bf16[1,16,640]{2,1,0:T(8,128)(2,1)S(1)} %norm.2.refs_0_.refs_4_), channel_id=1, source_target_pairs={{0,12},{1,13},{2,14},{3,15},{4,8},{5,9},{6,10},{7,11},{8,4},{9,5},... | collective-permute-start | bytes 61448 | tf_op jit(solution)/shard_map/ppermute | solution.py:28
  124.3 69.1 %copy-start.20 = (bf16[4,3,16,640]{3,2,1,0:T(8,128)(2,1)}, bf16[4,3,16,640]{3,2,1,0:T(8,128)(2,1)S(1)}, u32[]{:S(2)}) copy-start(bf16[4,3,16,640]{3,2,1,0:T(8,128)(2,1)S(1)} %merge_z.3.refs_1_) | copy-start | bytes 737284
  124.3 35.9 %collective-permute-start.26 = (bf16[4,3,16,640]{3,2,1,0:T(8,128)(2,1)S(1)}, bf16[4,3,16,640]{3,2,1,0:T(8,128)(2,1)}, u32[]{:S(2)}, u32[]{:S(2)}) collective-permute-start(bf16[4,3,16,640]{3,2,1,0:T(8,128)(2,1)S(1)} %merge_z.3.refs_1_), channel_id=1, source_target_pairs={{0,2},{1,3},{2,0},{3,1},{4,6},{5,7},{6,4},{7,5},{8,10},{9,11},{10,... | collective-permute-start | bytes 737288 | tf_op jit(solution)/shard_map/ppermute | solution.py:28
  128.8 4.5 %collective-permute-start.15 = (bf16[4,1,16,640]{3,2,1,0:T(8,128)(2,1)S(1)}, bf16[4,1,16,640]{3,2,1,0:T(8,128)(2,1)S(1)}, u32[]{:S(2)}, u32[]{:S(2)}) collective-permute-start(bf16[4,1,16,640]{3,2,1,0:T(8,128)(2,1)S(1)} %merge_z.2.refs_1_), channel_id=1, source_target_pairs={{0,2},{1,3},{2,0},{3,1},{4,6},{5,7},{6,4},{7,5},{8,10},{9,11},{10,... | collective-permute-start | bytes 245768 | tf_op jit(solution)/shard_map/ppermute | solution.py:28
  130.6 3.3 collective-permute-start.16
  133.3 1.3 collective-permute-start.17
  159.7 17.3 %collective-permute-start.31 = (bf16[256,1024]{1,0:T(8,128)(2,1)S(1)}, bf16[256,1024]{1,0:T(8,128)(2,1)S(1)}, u32[]{:S(2)}, u32[]{:S(2)}) collective-permute-start(bf16[256,1024]{1,0:T(8,128)(2,1)S(1)} %get-tuple-element.86.refs_0_.own_ref), channel_id=1, source_target_pairs={{0,1},{1,0},{2,3},{3,2},{4,5},{5,4},{6,7},{7,6},{8,9},{9,8},{10,11... | collective-permute-start | bytes 1572872 | tf_op jit(solution)/shard_map/ppermute | solution.py:28
  160.2 2.2 collective-permute-start.27
  160.2 2.4 collective-permute-start.28
  176.6 31.5 %collective-permute-start.29 = (bf16[256,1024]{1,0:T(8,128)(2,1)S(1)}, bf16[256,1024]{1,0:T(8,128)(2,1)S(1)}, u32[]{:S(2)}, u32[]{:S(2)}) collective-permute-start(bf16[256,1024]{1,0:T(8,128)(2,1)S(1)} %get-tuple-element.97.refs_0_.own_ref), channel_id=1, source_target_pairs={{0,1},{1,0},{2,3},{3,2},{4,5},{5,4},{6,7},{7,6},{8,9},{9,8},{10,11... | collective-permute-start | bytes 1572872 | tf_op jit(solution)/shard_map/ppermute | solution.py:28
  191.9 34.0 %collective-permute-start.34 = (bf16[128,4096]{1,0:T(8,128)(2,1)}, bf16[128,4096]{1,0:T(8,128)(2,1)}, u32[]{:S(2)}, u32[]{:S(2)}) collective-permute-start(bf16[128,4096]{1,0:T(8,128)(2,1)} %get-tuple-element.98.refs_0_), channel_id=1, source_target_pairs={{0,2},{1,3},{2,0},{3,1},{4,6},{5,7},{6,4},{7,5},{8,10},{9,11},{10,... | collective-permute-start | bytes 3145736 | tf_op jit(solution)/shard_map/ppermute | solution.py:28
  215.7 35.8 %slice-start.2 = ((s8[16777216]{0:T(1024)(128)(4,1)}), s8[4194304]{0:T(1024)(128)(4,1)S(1)}, s32[]{:S(2)}) async-start(s8[16777216]{0:T(1024)(128)(4,1)} %bitcast.20), calls=%async_computation.3 | async-start | bytes 8388608
  225.5 33.9 %collective-permute-start.32 = (bf16[128,4096]{1,0:T(8,128)(2,1)}, bf16[128,4096]{1,0:T(8,128)(2,1)}, u32[]{:S(2)}, u32[]{:S(2)}) collective-permute-start(bf16[128,4096]{1,0:T(8,128)(2,1)} %get-tuple-element.102), channel_id=1, source_target_pairs={{0,2},{1,3},{2,0},{3,1},{4,6},{5,7},{6,4},{7,5},{8,10},{9,11},{10,... | collective-permute-start | bytes 3145736 | tf_op jit(solution)/shard_map/ppermute | solution.py:28
  225.9 23.6 %collective-permute-start.33 = (bf16[256,1024]{1,0:T(8,128)(2,1)}, bf16[256,1024]{1,0:T(8,128)(2,1)}, u32[]{:S(2)}, u32[]{:S(2)}) collective-permute-start(bf16[256,1024]{1,0:T(8,128)(2,1)} %get-tuple-element.100.refs_0_.own_ref), channel_id=1, source_target_pairs={{0,1},{1,0},{2,3},{3,2},{4,5},{5,4},{6,7},{7,6},{8,9},{9,8},{10,11... | collective-permute-start | bytes 1572872 | tf_op jit(solution)/shard_map/ppermute | solution.py:28
  247.0 21.9 %collective-permute-start.39 = (bf16[256,1024]{1,0:T(8,128)(2,1)S(1)}, bf16[256,1024]{1,0:T(8,128)(2,1)S(1)}, u32[]{:S(2)}, u32[]{:S(2)}) collective-permute-start(bf16[256,1024]{1,0:T(8,128)(2,1)S(1)} %state_step.7.refs_0_.own_ref), channel_id=1, source_target_pairs={{0,1},{1,0},{2,3},{3,2},{4,5},{5,4},{6,7},{7,6},{8,9},{9,8},{10,11... | collective-permute-start | bytes 1572872 | tf_op jit(solution)/shard_map/ppermute | solution.py:28
  247.1 15.3 %collective-permute-start.35 = (bf16[32,4096]{1,0:T(8,128)(2,1)}, bf16[32,4096]{1,0:T(8,128)(2,1)S(1)}, u32[]{:S(2)}, u32[]{:S(2)}) collective-permute-start(bf16[32,4096]{1,0:T(8,128)(2,1)} %copy-done.52), channel_id=1, source_target_pairs={{0,4},{1,5},{2,6},{3,7},{4,0},{5,1},{6,2},{7,3},{8,12},{9,13},{10,... | collective-permute-start | bytes 786440 | tf_op jit(solution)/shard_map/ppermute | solution.py:28
  247.1 21.6 %collective-permute-start.36 = (bf16[32,4096]{1,0:T(8,128)(2,1)}, bf16[32,4096]{1,0:T(8,128)(2,1)S(1)}, u32[]{:S(2)}, u32[]{:S(2)}) collective-permute-start(bf16[32,4096]{1,0:T(8,128)(2,1)} %copy-done.51), channel_id=1, source_target_pairs={{0,8},{1,9},{2,10},{3,11},{4,12},{5,13},{6,14},{7,15},{8,0},{9,1},... | collective-permute-start | bytes 786440 | tf_op jit(solution)/shard_map/ppermute | solution.py:28
  249.5 19.2 %collective-permute-start.37 = (bf16[32,4096]{1,0:T(8,128)(2,1)}, bf16[32,4096]{1,0:T(8,128)(2,1)S(1)}, u32[]{:S(2)}, u32[]{:S(2)}) collective-permute-start(bf16[32,4096]{1,0:T(8,128)(2,1)} %copy-done.50), channel_id=1, source_target_pairs={{0,12},{1,13},{2,14},{3,15},{4,8},{5,9},{6,10},{7,11},{8,4},{9,5},... | collective-permute-start | bytes 786440 | tf_op jit(solution)/shard_map/ppermute | solution.py:28
  259.4 26.4 %collective-permute-start.38 = (bf16[128,4096]{1,0:T(8,128)(2,1)S(1)}, bf16[128,4096]{1,0:T(8,128)(2,1)S(1)}, u32[]{:S(2)}, u32[]{:S(2)}) collective-permute-start(bf16[128,4096]{1,0:T(8,128)(2,1)S(1)} %get-tuple-element.112), channel_id=1, source_target_pairs={{0,2},{1,3},{2,0},{3,1},{4,6},{5,7},{6,4},{7,5},{8,10},{9,11},{10,... | collective-permute-start | bytes 3145736 | tf_op jit(solution)/shard_map/ppermute | solution.py:28
  276.5 30.3 %collective-permute-start.43 = (bf16[128,4096]{1,0:T(8,128)(2,1)S(1)}, bf16[128,4096]{1,0:T(8,128)(2,1)S(1)}, u32[]{:S(2)}, u32[]{:S(2)}) collective-permute-start(bf16[128,4096]{1,0:T(8,128)(2,1)S(1)} %get-tuple-element.119), channel_id=1, source_target_pairs={{0,2},{1,3},{2,0},{3,1},{4,6},{5,7},{6,4},{7,5},{8,10},{9,11},{10,... | collective-permute-start | bytes 3145736 | tf_op jit(solution)/shard_map/ppermute | solution.py:28
  278.0 17.3 %collective-permute-start.40 = (bf16[32,4096]{1,0:T(8,128)(2,1)S(1)}, bf16[32,4096]{1,0:T(8,128)(2,1)S(1)}, u32[]{:S(2)}, u32[]{:S(2)}) collective-permute-start(bf16[32,4096]{1,0:T(8,128)(2,1)S(1)} %get-tuple-element.115), channel_id=1, source_target_pairs={{0,4},{1,5},{2,6},{3,7},{4,0},{5,1},{6,2},{7,3},{8,12},{9,13},{10,... | collective-permute-start | bytes 786440 | tf_op jit(solution)/shard_map/ppermute | solution.py:28
  283.4 21.4 %collective-permute-start.41 = (bf16[32,4096]{1,0:T(8,128)(2,1)S(1)}, bf16[32,4096]{1,0:T(8,128)(2,1)S(1)}, u32[]{:S(2)}, u32[]{:S(2)}) collective-permute-start(bf16[32,4096]{1,0:T(8,128)(2,1)S(1)} %get-tuple-element.116), channel_id=1, source_target_pairs={{0,8},{1,9},{2,10},{3,11},{4,12},{5,13},{6,14},{7,15},{8,0},{9,1},... | collective-permute-start | bytes 786440 | tf_op jit(solution)/shard_map/ppermute | solution.py:28
  283.7 22.9 %collective-permute-start.42 = (bf16[32,4096]{1,0:T(8,128)(2,1)S(1)}, bf16[32,4096]{1,0:T(8,128)(2,1)S(1)}, u32[]{:S(2)}, u32[]{:S(2)}) collective-permute-start(bf16[32,4096]{1,0:T(8,128)(2,1)S(1)} %get-tuple-element.117), channel_id=1, source_target_pairs={{0,12},{1,13},{2,14},{3,15},{4,8},{5,9},{6,10},{7,11},{8,4},{9,5},... | collective-permute-start | bytes 786440 | tf_op jit(solution)/shard_map/ppermute | solution.py:28
  286.3 41.9 %collective-permute-start.44 = (bf16[32,4096]{1,0:T(8,128)(2,1)S(1)}, bf16[32,4096]{1,0:T(8,128)(2,1)S(1)}, u32[]{:S(2)}, u32[]{:S(2)}) collective-permute-start(bf16[32,4096]{1,0:T(8,128)(2,1)S(1)} %get-tuple-element.121), channel_id=1, source_target_pairs={{0,4},{1,5},{2,6},{3,7},{4,0},{5,1},{6,2},{7,3},{8,12},{9,13},{10,... | collective-permute-start | bytes 786440 | tf_op jit(solution)/shard_map/ppermute | solution.py:28
  295.3 43.2 %collective-permute-start.45 = (bf16[32,4096]{1,0:T(8,128)(2,1)S(1)}, bf16[32,4096]{1,0:T(8,128)(2,1)S(1)}, u32[]{:S(2)}, u32[]{:S(2)}) collective-permute-start(bf16[32,4096]{1,0:T(8,128)(2,1)S(1)} %get-tuple-element.122), channel_id=1, source_target_pairs={{0,8},{1,9},{2,10},{3,11},{4,12},{5,13},{6,14},{7,15},{8,0},{9,1},... | collective-permute-start | bytes 786440 | tf_op jit(solution)/shard_map/ppermute | solution.py:28
  304.8 33.7 %collective-permute-start.46 = (bf16[32,4096]{1,0:T(8,128)(2,1)S(1)}, bf16[32,4096]{1,0:T(8,128)(2,1)S(1)}, u32[]{:S(2)}, u32[]{:S(2)}) collective-permute-start(bf16[32,4096]{1,0:T(8,128)(2,1)S(1)} %get-tuple-element.123), channel_id=1, source_target_pairs={{0,12},{1,13},{2,14},{3,15},{4,8},{5,9},{6,10},{7,11},{8,4},{9,5},... | collective-permute-start | bytes 786440 | tf_op jit(solution)/shard_map/ppermute | solution.py:28
  307.3 31.9 %collective-permute-start.47 = (bf16[32,4096]{1,0:T(8,128)(2,1)S(1)}, bf16[32,4096]{1,0:T(8,128)(2,1)S(1)}, u32[]{:S(2)}, u32[]{:S(2)}) collective-permute-start(bf16[32,4096]{1,0:T(8,128)(2,1)S(1)} %get-tuple-element.125), channel_id=1, source_target_pairs={{0,4},{1,5},{2,6},{3,7},{4,0},{5,1},{6,2},{7,3},{8,12},{9,13},{10,... | collective-permute-start | bytes 786440 | tf_op jit(solution)/shard_map/ppermute | solution.py:28
  328.2 21.6 %collective-permute-start.48 = (bf16[32,4096]{1,0:T(8,128)(2,1)S(1)}, bf16[32,4096]{1,0:T(8,128)(2,1)S(1)}, u32[]{:S(2)}, u32[]{:S(2)}) collective-permute-start(bf16[32,4096]{1,0:T(8,128)(2,1)S(1)} %get-tuple-element.126), channel_id=1, source_target_pairs={{0,8},{1,9},{2,10},{3,11},{4,12},{5,13},{6,14},{7,15},{8,0},{9,1},... | collective-permute-start | bytes 786440 | tf_op jit(solution)/shard_map/ppermute | solution.py:28
  328.2 21.6 %collective-permute-start.49 = (bf16[32,4096]{1,0:T(8,128)(2,1)S(1)}, bf16[32,4096]{1,0:T(8,128)(2,1)S(1)}, u32[]{:S(2)}, u32[]{:S(2)}) collective-permute-start(bf16[32,4096]{1,0:T(8,128)(2,1)S(1)} %get-tuple-element.127), channel_id=1, source_target_pairs={{0,12},{1,13},{2,14},{3,15},{4,8},{5,9},{6,10},{7,11},{8,4},{9,5},... | collective-permute-start | bytes 786440 | tf_op jit(solution)/shard_map/ppermute | solution.py:28
  338.5 11.5 %collective-permute-start.50 = (bf16[16,4096]{1,0:T(8,128)(2,1)S(1)}, bf16[16,4096]{1,0:T(8,128)(2,1)S(1)}, u32[]{:S(2)}, u32[]{:S(2)}) collective-permute-start(bf16[16,4096]{1,0:T(8,128)(2,1)S(1)} %get-tuple-element.129), channel_id=1, source_target_pairs={{0,1},{1,0},{2,3},{3,2},{4,5},{5,4},{6,7},{7,6},{8,9},{9,8},{10,11... | collective-permute-start | bytes 393224 | tf_op jit(solution)/shard_map/ppermute | solution.py:28
  338.5 11.5 %collective-permute-start.51 = (bf16[16,4096]{1,0:T(8,128)(2,1)S(1)}, bf16[16,4096]{1,0:T(8,128)(2,1)S(1)}, u32[]{:S(2)}, u32[]{:S(2)}) collective-permute-start(bf16[16,4096]{1,0:T(8,128)(2,1)S(1)} %get-tuple-element.130), channel_id=1, source_target_pairs={{0,1},{1,0},{2,3},{3,2},{4,5},{5,4},{6,7},{7,6},{8,9},{9,8},{10,11... | collective-permute-start | bytes 393224 | tf_op jit(solution)/shard_map/ppermute | solution.py:28
  339.2 10.8 %collective-permute-start.52 = (bf16[16,4096]{1,0:T(8,128)(2,1)S(1)}, bf16[16,4096]{1,0:T(8,128)(2,1)S(1)}, u32[]{:S(2)}, u32[]{:S(2)}) collective-permute-start(bf16[16,4096]{1,0:T(8,128)(2,1)S(1)} %get-tuple-element.131), channel_id=1, source_target_pairs={{0,1},{1,0},{2,3},{3,2},{4,5},{5,4},{6,7},{7,6},{8,9},{9,8},{10,11... | collective-permute-start | bytes 393224 | tf_op jit(solution)/shard_map/ppermute | solution.py:28
  349.9 1.4 collective-permute-start.53
  (50 other events, 348.1 us)

commit v4 on v3

--- a/solution.py
+++ b/solution.py
@@ -43,14 +43,13 @@
 
 def small(kernel, me, args, shapes, name, after=()):
     size = sum(a.size for a in args)
+    vmem = pl.BlockSpec(memory_space=pltpu.VMEM)
     return pl.pallas_call(
         kernel,
-        grid_spec=pltpu.PrefetchScalarGridSpec(
-            num_scalar_prefetch=1,
-            grid=(1,),
-            in_specs=[pl.BlockSpec(memory_space=pl.ANY)] * len(after) + [whole(a.shape) for a in args],
-            out_specs=[whole(s) for s in shapes],
-        ),
+        in_specs=[pl.BlockSpec(memory_space=pltpu.SMEM)]
+        + [pl.BlockSpec(memory_space=pl.ANY)] * len(after)
+        + [vmem] * len(args),
+        out_specs=[vmem] * len(shapes),
         out_shape=[jax.ShapeDtypeStruct(s, BF16) for s in shapes],
         compiler_params=params(8),
         cost_estimate=cost(size, 4 * size),
@@ -58,7 +57,7 @@
     )(me, *after, *args)
 
 
-def pack_conv_kernel(me_ref, x_ref, *o_refs):
+def pack_conv_kernel(me_ref, after_ref, x_ref, *o_refs):
     zs, _, wide = o_refs[0].shape
     y, core = (me_ref[0] // 2) % 2, me_ref[0] % 2
     c = wide * (TAPS + 1) // TAPS
@@ -71,7 +70,7 @@
             o_ref[z] = jnp.concatenate(parts, axis=0).astype(BF16)
 
 
-def cut_conv_kernel(me_ref, after_ref, *refs):
+def cut_conv_kernel(me_ref, *refs):
     zs = refs[0].shape[0]
     z, y, core = me_ref[0] // 4, (me_ref[0] // 2) % 2, me_ref[0] % 2
     for m in range(zs):
@@ -80,19 +79,19 @@
             refs[4 + m][at] = refs[i][jnp.bitwise_xor(z, m)]
 
 
-def exchange_conv(prefilled_conv, prefilled_state, me, n):
+def exchange_conv(prefilled_conv, packed_state, me, n):
     slots, _, inner = prefilled_conv.shape
     zs = n // 4
     piece = ((TAPS + 1) * slots, inner // n * TAPS // (TAPS + 1))
-    packed = small(pack_conv_kernel, me, [jnp.transpose(prefilled_conv, (1, 0, 2))], [(zs,) + piece] * 4, "pack_conv")
-    packed_state = pack_state(packed[0], prefilled_state, n)
+    conv = jnp.transpose(prefilled_conv, (1, 0, 2))
+    packed = small(pack_conv_kernel, me, [conv], [(zs,) + piece] * 4, "pack_conv", (packed_state,))
     near, far = swap(packed[2], 1, n), swap(packed[3], 1, n)
     got = [packed[0], swap(packed[1], 2, n), near, swap(far, 2, n)]
-    cut = small(cut_conv_kernel, me, got, [(4,) + piece] * zs, "cut_conv", (packed_state,))
-    return packed_state, [cut[0]] + [swap(cut[m], 4 * m, n) for m in range(1, zs)]
-
-
-def pack_state_kernel(after_ref, x_ref, o_ref):
+    cut = small(cut_conv_kernel, me, got, [(4,) + piece] * zs, "cut_conv")
+    return [cut[0]] + [swap(cut[m], 4 * m, n) for m in range(1, zs)]
+
+
+def pack_state_kernel(x_ref, o_ref):
     slots = x_ref.shape[0]
     some, _, c = o_ref.shape
     for d in range(some):
@@ -100,23 +99,20 @@
             o_ref[d, STATE * k : STATE * (k + 1), :] = x_ref[k, :, d * c : (d + 1) * c].astype(BF16)
 
 
-def pack_state(after, prefilled_state, n):
+def pack_state(prefilled_state, n):
     slots, _, inner = prefilled_state.shape
     c = inner // n
     some = 4
     return pl.pallas_call(
         pack_state_kernel,
         grid=(n // some,),
-        in_specs=[
-            pl.BlockSpec(memory_space=pl.ANY),
-            pl.BlockSpec((slots, STATE, some * c), lambda d: (0, 0, d)),
-        ],
+        in_specs=[pl.BlockSpec((slots, STATE, some * c), lambda d: (0, 0, d))],
         out_specs=pl.BlockSpec((some, slots * STATE, c), lambda d: (d, 0, 0)),
         out_shape=jax.ShapeDtypeStruct((n, slots * STATE, c), BF16),
         compiler_params=params(24),
         cost_estimate=cost(0, slots * STATE * inner * 6),
         name="pack_state",
-    )(after, prefilled_state)
+    )(prefilled_state)
 
 
 def conv_kernel(steps, n, me_ref, target_ref, old_ref, x_ref, w_ref, bias_ref, proj_ref, *refs):
@@ -194,21 +190,23 @@
     )(me, target, old, step_x, conv_weight, conv_bias, proj, *moved, *after)
 
 
-def add_y_kernel(me_ref, keep_ref, got_ref, send_ref, left_ref):
+def add_y_kernel(me_ref, *refs):
+    keep_ref, got_ref, send_ref, left_ref = refs[-4:]
     y = (me_ref[0] // 2) % 2
     for z in range(send_ref.shape[0]):
         for o_ref, at in ((send_ref, 2 * z + 1 - y), (left_ref, 2 * z + y)):
             o_ref[z] = (keep_ref[at].astype(F32) + got_ref[at].astype(F32)).astype(BF16)
 
 
-def add_z_kernel(me_ref, keep_ref, got_ref, *o_refs):
+def add_z_kernel(zs, me_ref, *refs):
+    keep_ref, got_ref, *o_refs = refs[-2 - zs :]
     z = me_ref[0] // 4
     for m, o_ref in enumerate(o_refs):
         at = jnp.bitwise_xor(z, m)
         o_ref[...] = (keep_ref[at].astype(F32) + got_ref[at].astype(F32)).astype(BF16)
 
 
-def norm_kernel(gain_ref, *refs):
+def norm_kernel(me_ref, gain_ref, *refs):
     o_ref = refs[-1]
     total = refs[0][...].astype(F32)
     for ref in refs[1:-1]:
@@ -236,28 +234,19 @@
         o_ref[jnp.bitwise_xor(z, m)] = ref[...]
 
 
-def reduce_projection(send, keep, gain, me, n):
+def reduce_projection(send, keep, gain, me, after_y, after_z, n):
     zs = n // 4
     piece = keep.shape[1:]
     got = swap(send, 1, n)
-    send, keep = small(add_y_kernel, me, [keep, got], [(zs,) + piece] * 2, "add_y")
+    send, keep = small(add_y_kernel, me, [keep, got], [(zs,) + piece] * 2, "add_y", after_y)
     got = swap(send, 2, n)
-    cut = small(add_z_kernel, me, [keep, got], [piece] * zs, "add_z")
+    cut = small(functools.partial(add_z_kernel, zs), me, [keep, got], [piece] * zs, "add_z", after_z)
     cut = [cut[0]] + [swap(cut[m], 4 * m, n) for m in range(1, zs)]
-    low = pl.pallas_call(
-        norm_kernel,
-        grid=(1,),
-        in_specs=[whole(gain.shape)] + [whole(piece)] * zs,
-        out_specs=whole(piece),
-        out_shape=jax.ShapeDtypeStruct(piece, BF16),
-        compiler_params=params(8),
-        cost_estimate=cost(cut[0].size * zs, cut[0].size * 2 * zs),
-        name="norm",
-    )(gain, *cut)
+    (low,) = small(norm_kernel, me, [gain] + cut, [piece], "norm")
     lows = [low] + [swap(low, 4 * m, n) for m in range(1, zs)]
     (mine,) = small(merge_kernel, me, lows, [(zs,) + piece], "merge_z")
     beside = swap(mine, 2, n)
-    return low, (mine, beside, swap(mine, 1, n), swap(beside, 1, n))
+    return mine, (mine, beside, swap(mine, 1, n), swap(beside, 1, n))
 
 
 def state_kernel(first, last, me_ref, live_ref, *refs):
@@ -404,7 +393,7 @@
             scratch_shapes=scratch,
         ),
         out_shape=out_shape,
-        compiler_params=params(32),
+        compiler_params=params(56),
         cost_estimate=cost(8 * size, 4 * size, size),
         name="state_step",
     )(me, live, *extra, *lows, conv, step_z, dt_proj, dt_bias, a_log, d_skip, state)
@@ -441,50 +430,26 @@
             out_specs=[pl.BlockSpec((rows // 2, tile), lambda j, me_ref: (0, j))] * 2,
         ),
         out_shape=[half, half],
-        compiler_params=params(24),
+        compiler_params=params(56),
         cost_estimate=cost(4 * rows * c * cols, 4 * c * cols + 2 * rows * cols),
         name="out_project",
     )(me, own, other, out_weight, other_weight, *after)
 
 
-def pieces_kernel(behind, me_ref, keep_ref, got_ref, *refs):
-    z = me_ref[0] // 4
-    for m, o_ref in enumerate(refs[behind:]):
-        at = jnp.bitwise_xor(z, m)
-        o_ref[...] = (keep_ref[at].astype(F32) + got_ref[at].astype(F32)).astype(BF16)
-
-
-def sum_pieces(me, keep, got, after, n):
-    half, cols = keep.shape
-    zs = n // 4
-    take = half // zs
-    tile = 2048
-    return pl.pallas_call(
-        functools.partial(pieces_kernel, len(after)),
-        grid_spec=pltpu.PrefetchScalarGridSpec(
-            num_scalar_prefetch=1,
-            grid=(cols // tile,),
-            in_specs=[pl.BlockSpec((zs, take, tile), lambda j, me_ref: (0, 0, j))] * 2
-            + [pl.BlockSpec(memory_space=pl.ANY)] * len(after),
-            out_specs=[pl.BlockSpec((take, tile), lambda j, me_ref: (0, j))] * zs,
-        ),
-        out_shape=[jax.ShapeDtypeStruct((take, cols), BF16)] * zs,
-        compiler_params=params(16),
-        cost_estimate=cost(half * cols, 6 * half * cols),
-        name="sum_pieces",
-    )(me, keep.reshape(zs, take, cols), got.reshape(zs, take, cols), *after)
-
-
-def sum_z_kernel(me_ref, after_ref, *refs):
-    send_ref, keep_ref = refs[-2:]
-    total = refs[0][...].astype(F32)
-    for ref in refs[1:-2]:
-        total = total + ref[...].astype(F32)
+def halve_kernel(stage, me_ref, after_ref, keep_ref, got_ref, send_ref, left_ref):
+    bit = (me_ref[0] >> (2 + stage)) & 1
+    for i in range(send_ref.shape[0]):
+        for o_ref, at in ((send_ref, 2 * i + 1 - bit), (left_ref, 2 * i + bit)):
+            o_ref[i] = (keep_ref[at].astype(F32) + got_ref[at].astype(F32)).astype(BF16)
+
+
+def sum_z_kernel(me_ref, after_ref, keep_ref, got_ref, send_ref, left_ref):
+    total = keep_ref[0].astype(F32) + got_ref[0].astype(F32)
     own = total.shape[0] // 2
     low, high = total[:own], total[own:]
     core = me_ref[0] % 2
     send_ref[...] = jnp.where(core == 0, high, low).astype(BF16)
-    keep_ref[...] = jnp.where(core == 0, low, high).astype(BF16)
+    left_ref[...] = jnp.where(core == 0, low, high).astype(BF16)
 
 
 def final_kernel(tiles, me_ref, *refs):
@@ -542,7 +507,8 @@
     me_scalar = lax.axis_index("dex").astype(jnp.int32)
     me = me_scalar.reshape(1)
 
-    packed_state, moved_conv = exchange_conv(prefilled_conv, prefilled_state, me, n)
+    packed_state = pack_state(prefilled_state, n)
+    moved_conv = exchange_conv(prefilled_conv, packed_state, me, n)
     moved_state = lax.all_to_all(packed_state, "dex", 0, 0, tiled=True)
     other_weight = swap(out_weight, 1, n)
     cols = out_weight.shape[1] // 2
@@ -574,19 +540,21 @@
 
     lows = {}
     convs = {}
-    after = ()
-    for steps in ((0,), tuple(range(1, STEPS))):
+
+    def low_rows(steps, after, after_y, after_z):
         conv, send, keep = conv_steps(
             steps, n, me, after, spread, old, moved_conv, step_x, conv_weight, bias, proj
         )
-        low_rows, low = reduce_projection(send, keep, gain, me, n)
-        after = (low_rows,)
+        merged, low = reduce_projection(send, keep, gain, me, after_y, after_z, n)
         for i, t in enumerate(steps):
             lows[t] = (low, i)
             convs[t] = conv
+        return merged
 
     state = resident_state.reshape(rows * STATE, c)
-    sends, keeps, cuts, sums, gated = {}, {}, {}, {}, {}
+    sends, keeps, gated = {}, {}, {}
+    stages = zs.bit_length() - 1
+    take = 2 * rows // n
 
     def s_step(t, extra):
         nonlocal state
@@ -595,35 +563,52 @@
             t, i, me, live, extra, low, convs[t], step_z, dt_proj,
             dt_bias.reshape(1, c), a_log, d_skip.reshape(1, c), state, n,
         )
+        return gated[t]
 
     def project(t, after):
-        sends[t], keeps[t] = out_project(me, gated[t], swap(gated[t], 1, n), out_weight, other_weight, after)
-
-    def reduce_y(t, after):
-        cuts[t] = sum_pieces(me, keeps[t], swap(sends[t], 2, n), after, n)
-
-    def reduce_z(t, after):
-        parts = [cuts[t][0]] + [swap(cuts[t][m], 4 * m, n) for m in range(1, zs)]
-        send, keep = small(sum_z_kernel, me, parts, [(rows // n, cols)] * 2, "sum_z", after)
-        sums[t] = (keep, swap(send, 1, n))
-
-    s_step(0, (moved_state,))
-    s_step(1, (gated[0],))
-    project(0, (gated[1],))
-    s_step(2, (sends[0],))
-    project(1, (gated[2],))
-    reduce_y(0, (keeps[1],))
-    s_step(3, (cuts[0][0],))
-    project(2, (gated[3],))
-    reduce_y(1, (keeps[2],))
-    reduce_z(0, (cuts[1][0],))
-    project(3, (sums[0][0],))
-    reduce_y(2, (keeps[3],))
-    reduce_z(1, (cuts[2][0],))
-    reduce_y(3, (sums[1][0],))
-    reduce_z(2, (cuts[3][0],))
-    reduce_z(3, (sums[2][0],))
-    return final_join(me, [sums[t][0] for t in range(STEPS)], [sums[t][1] for t in range(STEPS)])
+        sends[t], keeps[t] = out_project(me, gated[t], swap(gated[t], 1, n), out_weight, other_weight, (after,))
+        return keeps[t]
+
+    def reduce(t, stage, after):
+        if stage == 0:
+            keep, got = keeps[t].reshape(zs, take, cols), swap(sends[t], 2, n).reshape(zs, take, cols)
+        else:
+            keep, got = keeps[t], swap(sends[t], 2 << stage, n)
+        if stage < stages:
+            kernel, shape = functools.partial(halve_kernel, stage), (keep.shape[0] // 2, take, cols)
+        else:
+            kernel, shape = sum_z_kernel, (take // 2, cols)
+        sends[t], keeps[t] = small(kernel, me, [keep, got], [shape] * 2, "reduce_%d" % stage, (after,))
+        if stage == stages:
+            sends[t] = swap(sends[t], 1, n)
+        return keeps[t]
+
+    merged = low_rows((0,), (), (), ())
+    last = s_step(0, (moved_state,))
+    low_rows(tuple(range(1, STEPS)), (merged,), (lows[0][0][3],), (last,))
+    last = project(0, last)
+    last = s_step(1, (last,))
+    last = reduce(0, 0, last)
+    last = project(1, last)
+    last = s_step(2, (last,))
+    for stage in range(1, stages):
+        last = reduce(0, stage, last)
+    last = project(2, last)
+    last = reduce(1, 0, last)
+    last = s_step(3, (last,))
+    for stage in range(1, stages):
+        last = reduce(1, stage, last)
+    last = project(3, last)
+    last = reduce(2, 0, last)
+    last = reduce(0, stages, last)
+    for stage in range(1, stages):
+        last = reduce(2, stage, last)
+    last = reduce(3, 0, last)
+    last = reduce(1, stages, last)
+    last = reduce(2, stages, last)
+    for stage in range(1, stages + 1):
+        last = reduce(3, stage, last)
+    return final_join(me, [keeps[t] for t in range(STEPS)], [sends[t] for t in range(STEPS)])
 
 
 def solution(mesh):

time: 357 us -> 353 us (0.989)
  waiting for transfers between devices: 108 us -> 144 us
  starting transfers between devices: 87.3 us -> 56.2 us
  local copies, waits for them, and re-layouts: 59.2 us -> 36.4 us
  Pallas kernels: 96 us -> 111 us
    ppermute x54 -> x50, waiting for transfers between devices: 108 us -> 144 us  [swap(): return lax.ppermute(x, 'dex', [(i, i ^ mask) for i in range(n)])]
    ppermute x54 -> x50, starting transfers between devices: 80 us -> 48.8 us  [swap(): return lax.ppermute(x, 'dex', [(i, i ^ mask) for i in range(n)])]
    unnamed x118 -> x116, local copies, waits for them, and re-layouts: 53.5 us -> 34.7 us
    pallas_call x4, Pallas kernels: 46.6 us -> 57.6 us  [state_step(): pl.pallas_call(functools.partial(state_kernel, first, last), grid_spec=pl...]
    pallas_call x4, Pallas kernels: 33.4 us -> 39.4 us  [out_project(): pl.pallas_call(out_kernel, grid_spec=pltpu.PrefetchScalarGridSpec(num_sca...]
  transfers between devices with their start and end apart: 55 -> 51, of which waited for: 24 -> 27; matrix products, arithmetic and copies ran while one was open for 2% -> 1% of each run, Pallas kernels for 27% -> 28%
where the time goes in v4:
time: 353 us; the launch traced here: 351 us
  waiting for transfers between devices  144 us (41%)
  Pallas kernels  111 us (31%)
  starting transfers between devices  56.2 us (16%)
  local copies, waits for them, and re-layouts  36.4 us (10%)
    ppermute x50, waiting for transfers between devices, swap(): return lax.ppermute(x, 'dex', [(i, i ^ mask) for i in range(n)])  144 us
    pallas_call x4, Pallas kernels, state_step(): pl.pallas_call(functools.partial(state_kernel, first, last), grid_spec=pl...  57.6 us
    ppermute x50, starting transfers between devices, swap(): return lax.ppermute(x, 'dex', [(i, i ^ mask) for i in range(n)])  48.8 us
    pallas_call x4, Pallas kernels, out_project(): pl.pallas_call(out_kernel, grid_spec=pltpu.PrefetchScalarGridSpec(num_sca...  39.4 us
    unnamed x116, local copies, waits for them, and re-layouts  34.7 us
    all_to_all x1, starting transfers between devices, shards(): moved_state = lax.all_to_all(packed_state, 'dex', 0, 0, tiled=True)  7.37 us
  transfers between devices with their start and end apart: 51, of which 27 were waited for; matrix products, arithmetic and copies ran while one was open for 1% of the time, Pallas kernels for 28%

profile of v4, /device:TPU:0, one launch (start us, length us, event | category | flops | bytes accessed | tf_op | source)
XLA Modules:
  0.0 350.8 jit_solution(6575771735903203392)
XLA Ops:
  0.5 2.2 copy-done.10
  2.6 2.1 pack_state.1.after_ref
  4.8 7.4 %all-to-all-start = ((bf16[16,64,1024]{2,1,0:T(8,128)(2,1)}), bf16[16,64,1024]{2,1,0:T(8,128)(2,1)}, u32[]{:S(2)}, u32[]{:S(2)}) async-start(bf16[16,64,1024]{2,1,0:T(8,128)(2,1)} %pack_state.1.after_ref), calls=%async_computation | async-start | bytes 4194304 | tf_op jit(solution)/shard_map/all_to_all | solution.py:512
  12.2 1.1 copy-done.27
  14.0 1.9 collective-permute-start
  16.7 9.3 %collective-permute-done.2 = bf16[4,16,768]{2,1,0:T(8,128)(2,1)} collective-permute-done((bf16[4,16,768]{2,1,0:T(8,128)(2,1)}, bf16[4,16,768]{2,1,0:T(8,128)(2,1)}, u32[]{:S(2)}, u32[]{:S(2)}) %collective-permute-start.2) | collective-permute-done | bytes 98336 | tf_op jit(solution)/shard_map/ppermute | solution.py:28
  26.0 2.9 collective-permute-start.3
  30.4 5.7 %collective-permute-done.3.refs_3_ = bf16[4,16,768]{2,1,0:T(8,128)(2,1)} collective-permute-done((bf16[4,16,768]{2,1,0:T(8,128)(2,1)}, bf16[4,16,768]{2,1,0:T(8,128)(2,1)}, u32[]{:S(2)}, u32[]{:S(2)}) %collective-permute-start.3) | collective-permute-done | bytes 98336 | tf_op jit(solution)/shard_map/ppermute | solution.py:28
  38.8 1.3 collective-permute-start.5
  40.1 2.3 collective-permute-start.6
  43.1 6.3 %collective-permute-done.4.refs_1_ = bf16[4,16,768]{2,1,0:T(8,128)(2,1)S(1)} collective-permute-done((bf16[4,16,768]{2,1,0:T(8,128)(2,1)S(1)}, bf16[4,16,768]{2,1,0:T(8,128)(2,1)S(1)}, u32[]{:S(2)}, u32[]{:S(2)}) %collective-permute-start.4) | collective-permute-done | bytes 98336 | tf_op jit(solution)/shard_map/ppermute | solution.py:28
  49.3 18.6 %collective-permute-done.5.refs_2_ = bf16[4,16,768]{2,1,0:T(8,128)(2,1)S(1)} collective-permute-done((bf16[4,16,768]{2,1,0:T(8,128)(2,1)S(1)}, bf16[4,16,768]{2,1,0:T(8,128)(2,1)S(1)}, u32[]{:S(2)}, u32[]{:S(2)}) %collective-permute-start.5) | collective-permute-done | bytes 98336 | tf_op jit(solution)/shard_map/ppermute | solution.py:28
  68.0 1.6 copy-done.2
  69.6 1.2 copy-done.6
  70.9 1.6 conv_project.2
  73.4 1.4 collective-permute-done.7.refs_1_
  74.9 1.6 collective-permute-start.8
  76.5 2.9 collective-permute-done.8.refs_1_
  79.4 2.3 collective-permute-start.9
  81.8 2.3 collective-permute-start.11
  84.2 2.2 collective-permute-done.10.refs_2_
  87.5 2.4 collective-permute-start.14
  89.9 2.1 collective-permute-start.12
  98.7 1.6 copy-done.3
  100.3 1.2 copy-done.7
  103.1 3.8 %conv_project.3 = (f32[3,256,1024]{2,1,0:T(8,128)S(1)}, bf16[8,3,16,640]{3,2,1,0:T(8,128)(2,1)}, bf16[8,3,16,640]{3,2,1,0:T(8,128)(2,1)S(1)}) custom-call(s32[1]{0:T(128)} %bitcast.me_ref, s32[4,256]{1,0:T(4,128)S(1)} %broadcast_select_fusion.1.target_ref, f32[3,256,1024]{2,1,0:T(8,128)S(1)} %bitcast.21, bf16[4,256,1024]{2,1,0:T(8,128)(2,1)S(1)} %copy-done.3, ...), custom_call_target="tpu_custom_call" | custom-call | flops 1024 | bytes 1024 | tf_op jit(solution)/shard_map/conv_project/pallas_call | solution.py:165
  107.0 1.7 copy-done
  109.6 1.6 collective-permute-start.15
  111.8 2.8 collective-permute-done.15.refs_2_
  116.5 18.5 %state_step.4 = (bf16[16,256,1024]{2,1,0:T(8,128)(2,1)}, bf16[256,1024]{1,0:T(8,128)(2,1)}) custom-call(s32[1]{0:T(128)} %bitcast.me_ref, s32[3,64]{1,0:T(4,128)} %pad_add_fusion.live_ref, bf16[64,16,1024]{2,1,0:T(8,128)(2,1)} %bitcast.4.refs_0_, bf16[4,1,16,640]{3,2,1,0:T(8,128)(2,1)} %copy-done.28, bf16[4,1,16,640]{3,2,1,0:T(8,128)(2,1)} %copy-done.53, ...), custom_call_target="tpu_custom_call" | custom-call | flops 1024 | bytes 1024 | tf_op jit(solution)/shard_map/state_step/pallas_call | solution.py:386
  136.3 1.6 collective-permute-start.21
  137.9 6.6 %collective-permute-done.21.refs_2_ = bf16[4,3,16,640]{3,2,1,0:T(8,128)(2,1)S(1)} collective-permute-done((bf16[4,3,16,640]{3,2,1,0:T(8,128)(2,1)S(1)}, bf16[4,3,16,640]{3,2,1,0:T(8,128)(2,1)S(1)}, u32[]{:S(2)}, u32[]{:S(2)}) %collective-permute-start.21) | collective-permute-done | bytes 245792 | tf_op jit(solution)/shard_map/ppermute | solution.py:28
  146.3 1.7 collective-permute-start.23
  148.0 2.1 collective-permute-start.24
  150.4 2.9 collective-permute-done.23.refs_2_
  154.3 2.2 collective-permute-start.27
  156.8 1.9 collective-permute-start.25
  159.6 9.8 %out_project.4 = (bf16[128,4096]{1,0:T(8,128)(2,1)}, bf16[128,4096]{1,0:T(8,128)(2,1)}) custom-call(s32[1]{0:T(128)} %bitcast.me_ref, bf16[256,1024]{1,0:T(8,128)(2,1)} %get-tuple-element.86.own_ref.refs_0_, bf16[256,1024]{1,0:T(8,128)(2,1)} %copy-done.49, bf16[1024,8192]{1,0:T(8,128)(2,1)} %wown_ref.7, ...), custom_call_target="tpu_custom_call" | custom-call | flops 1024 | bytes 1024 | tf_op jit(solution)/shard_map/out_project/pallas_call | solution.py:418
  169.3 1.6 collective-permute-start.32
  171.5 25.8 %collective-permute-done.28.refs_2_ = bf16[4,3,16,640]{3,2,1,0:T(8,128)(2,1)S(1)} collective-permute-done((bf16[4,3,16,640]{3,2,1,0:T(8,128)(2,1)S(1)}, bf16[4,3,16,640]{3,2,1,0:T(8,128)(2,1)S(1)}, u32[]{:S(2)}, u32[]{:S(2)}) %collective-permute-start.28) | collective-permute-done | bytes 245792 | tf_op jit(solution)/shard_map/ppermute | solution.py:28
  197.3 1.5 collective-permute-done.30.refs_4_
  199.5 13.7 %state_step.5 = (bf16[16,256,1024]{2,1,0:T(8,128)(2,1)}, bf16[256,1024]{1,0:T(8,128)(2,1)}) custom-call(s32[1]{0:T(128)} %bitcast.me_ref, s32[3,64]{1,0:T(4,128)} %pad_add_fusion.live_ref, bf16[128,4096]{1,0:T(8,128)(2,1)} %get-tuple-element.87.refs_0_, bf16[4,3,16,640]{3,2,1,0:T(8,128)(2,1)} %copy-done.15, bf16[4,3,16,640]{3,2,1,0:T(8,128)(2,1)} %copy-done.46, ...), custom_call_target="tpu_custom_call" | custom-call | flops 1024 | bytes 1024 | tf_op jit(solution)/shard_map/state_step/pallas_call | solution.py:386
  213.4 1.0 copy-done.19
  216.2 9.8 %out_project.5 = (bf16[128,4096]{1,0:T(8,128)(2,1)}, bf16[128,4096]{1,0:T(8,128)(2,1)}) custom-call(s32[1]{0:T(128)} %bitcast.me_ref, bf16[256,1024]{1,0:T(8,128)(2,1)} %get-tuple-element.98.after_ref.own_ref, bf16[256,1024]{1,0:T(8,128)(2,1)} %copy-done.51, bf16[1024,8192]{1,0:T(8,128)(2,1)} %wown_ref.7, ...), custom_call_target="tpu_custom_call" | custom-call | flops 1024 | bytes 1024 | tf_op jit(solution)/shard_map/out_project/pallas_call | solution.py:418
  226.0 1.6 collective-permute-start.35
  227.9 13.5 %state_step.6 = (bf16[16,256,1024]{2,1,0:T(8,128)(2,1)}, bf16[256,1024]{1,0:T(8,128)(2,1)}) custom-call(s32[1]{0:T(128)} %bitcast.me_ref, s32[3,64]{1,0:T(4,128)} %pad_add_fusion.live_ref, bf16[128,4096]{1,0:T(8,128)(2,1)} %get-tuple-element.101.refs_0_, bf16[4,3,16,640]{3,2,1,0:T(8,128)(2,1)} %copy-done.15, bf16[4,3,16,640]{3,2,1,0:T(8,128)(2,1)} %copy-done.46, ...), custom_call_target="tpu_custom_call" | custom-call | flops 1024 | bytes 1024 | tf_op jit(solution)/shard_map/state_step/pallas_call | solution.py:386
  244.3 9.9 %out_project.6 = (bf16[128,4096]{1,0:T(8,128)(2,1)}, bf16[128,4096]{1,0:T(8,128)(2,1)}) custom-call(s32[1]{0:T(128)} %bitcast.me_ref, bf16[256,1024]{1,0:T(8,128)(2,1)} %get-tuple-element.103.after_ref.own_ref, bf16[256,1024]{1,0:T(8,128)(2,1)} %copy-done.52, bf16[1024,8192]{1,0:T(8,128)(2,1)} %wown_ref.7, ...), custom_call_target="tpu_custom_call" | custom-call | flops 1024 | bytes 1024 | tf_op jit(solution)/shard_map/out_project/pallas_call | solution.py:418
  254.8 1.2 copy-done.13
  257.1 1.7 collective-permute-start.37
  258.8 11.8 %state_step.7.after_ref.own_ref = bf16[256,1024]{1,0:T(8,128)(2,1)} custom-call(s32[1]{0:T(128)} %bitcast.me_ref, s32[3,64]{1,0:T(4,128)} %pad_add_fusion.live_ref, bf16[2,32,4096]{2,1,0:T(8,128)(2,1)} %copy-done.20, bf16[4,3,16,640]{3,2,1,0:T(8,128)(2,1)} %copy-done.15, bf16[4,3,16,640]{3,2,1,0:T(8,128)(2,1)} %copy-done.46, ...), custom_call_target="tpu_custom_call" | custom-call | flops 1024 | bytes 1024 | tf_op jit(solution)/shard_map/state_step/pallas_call | solution.py:386
  270.9 1.0 copy-done.5
  273.6 9.9 %out_project.7 = (bf16[128,4096]{1,0:T(8,128)(2,1)}, bf16[128,4096]{1,0:T(8,128)(2,1)}) custom-call(s32[1]{0:T(128)} %bitcast.me_ref, bf16[256,1024]{1,0:T(8,128)(2,1)} %state_step.7.after_ref.own_ref, bf16[256,1024]{1,0:T(8,128)(2,1)} %copy-done.50, bf16[1024,8192]{1,0:T(8,128)(2,1)} %wown_ref.7, bf16[1024,8192]{1,0:T(8,128)(2,1)} %collective-permute-done.19.wother_ref, ...), custom_call_target="tpu_custom_call" | custom-call | flops 1024 | bytes 1024 | tf_op jit(solution)/shard_map/out_project/pallas_call | solution.py:418
  283.5 1.5 collective-permute-start.41
  285.0 1.2 copy-done.11
  286.5 1.8 collective-permute-start.40
  289.2 14.9 %collective-permute-done.39.got_ref = bf16[1,32,4096]{2,1,0:T(8,128)(2,1)S(1)} collective-permute-done((bf16[1,32,4096]{2,1,0:T(8,128)(2,1)S(1)}, bf16[1,32,4096]{2,1,0:T(8,128)(2,1)S(1)}, u32[]{:S(2)}, u32[]{:S(2)}) %collective-permute-start.39) | collective-permute-done | bytes 262176 | tf_op jit(solution)/shard_map/ppermute | solution.py:28
  304.2 1.7 collective-permute-done.40.got_ref
  306.0 2.9 collective-permute-done.41
  309.9 2.0 collective-permute-start.42
  312.9 15.1 %collective-permute-done.42.got_ref = bf16[1,32,4096]{2,1,0:T(8,128)(2,1)S(1)} collective-permute-done((bf16[1,32,4096]{2,1,0:T(8,128)(2,1)S(1)}, bf16[1,32,4096]{2,1,0:T(8,128)(2,1)S(1)}, u32[]{:S(2)}, u32[]{:S(2)}) %collective-permute-start.42) | collective-permute-done | bytes 262176 | tf_op jit(solution)/shard_map/ppermute | solution.py:28
  328.1 6.6 %collective-permute-done.43.got_ref = bf16[1,32,4096]{2,1,0:T(8,128)(2,1)S(1)} collective-permute-done((bf16[1,32,4096]{2,1,0:T(8,128)(2,1)S(1)}, bf16[1,32,4096]{2,1,0:T(8,128)(2,1)S(1)}, u32[]{:S(2)}, u32[]{:S(2)}) %collective-permute-start.43) | collective-permute-done | bytes 262176 | tf_op jit(solution)/shard_map/ppermute | solution.py:28
  335.8 11.3 %collective-permute-done.45.got_ref = bf16[1,32,4096]{2,1,0:T(8,128)(2,1)S(1)} collective-permute-done((bf16[1,32,4096]{2,1,0:T(8,128)(2,1)S(1)}, bf16[1,32,4096]{2,1,0:T(8,128)(2,1)S(1)}, u32[]{:S(2)}, u32[]{:S(2)}) %collective-permute-start.45) | collective-permute-done | bytes 262176 | tf_op jit(solution)/shard_map/ppermute | solution.py:28
  347.3 1.3 collective-permute-done.49.refs_7_
  348.6 2.2 final_join.1
  (204 shorter events, 40.8 us)
Async XLA Ops:
  0.0 158.7 %collective-permute-start.19 = (bf16[1024,8192]{1,0:T(8,128)(2,1)}, bf16[1024,8192]{1,0:T(8,128)(2,1)}, u32[]{:S(2)}, u32[]{:S(2)}) collective-permute-start(bf16[1024,8192]{1,0:T(8,128)(2,1)} %wown_ref.7), channel_id=1, source_target_pairs={{0,1},{1,0},{2,3},{3,2},{4,5},{5,4},{6,7},{7,6},{8,9},{9,8},{10,11... | collective-permute-start | bytes 50331656 | tf_op jit(solution)/shard_map/ppermute | solution.py:28
  4.8 63.2 %copy-start.1 = (f32[256,3,1024]{2,0,1:T(8,128)S(1)}, f32[256,3,1024]{2,0,1:T(8,128)}, u32[]{:S(2)}) copy-start(f32[256,3,1024]{2,0,1:T(8,128)} %param.18) | copy-start | bytes 9437188
  4.8 63.2 %copy-start.37 = (f32[4,1024]{1,0:T(4,128)S(1)}, f32[4,1024]{1,0:T(4,128)}, u32[]{:S(2)}) copy-start(f32[4,1024]{1,0:T(4,128)} %w_ref.3) | copy-start | bytes 49156
  4.8 63.2 %copy-start.45 = (f32[1024]{0:T(1024)S(1)}, f32[1024]{0:T(1024)}, u32[]{:S(2)}) copy-start(f32[1024]{0:T(1024)} %param.26) | copy-start | bytes 12292
  4.8 111.1 %all-to-all-start = ((bf16[16,64,1024]{2,1,0:T(8,128)(2,1)}), bf16[16,64,1024]{2,1,0:T(8,128)(2,1)}, u32[]{:S(2)}, u32[]{:S(2)}) async-start(bf16[16,64,1024]{2,1,0:T(8,128)(2,1)} %pack_state.1.after_ref), calls=%async_computation | async-start | bytes 4194304 | tf_op jit(solution)/shard_map/all_to_all | solution.py:512
  14.0 70.1 %copy-start.55 = (f32[544]{0:T(1024)S(1)}, f32[544]{0:T(1024)}, u32[]{:S(2)}) copy-start(f32[544]{0:T(1024)} %param.28) | copy-start | bytes 6532
  14.0 15.7 %collective-permute-start = (bf16[4,16,768]{2,1,0:T(8,128)(2,1)}, bf16[4,16,768]{2,1,0:T(8,128)(2,1)S(1)}, u32[]{:S(2)}, u32[]{:S(2)}) collective-permute-start(bf16[4,16,768]{2,1,0:T(8,128)(2,1)} %get-tuple-element.70), channel_id=1, source_target_pairs={{0,2},{1,3},{2,0},{3,1},{4,6},{5,7},{6,4},{7,5},{8,10},{9,11},{10,... | collective-permute-start | bytes 294920 | tf_op jit(solution)/shard_map/ppermute | solution.py:28
  15.9 13.9 %collective-permute-start.1 = (bf16[4,16,768]{2,1,0:T(8,128)(2,1)}, bf16[4,16,768]{2,1,0:T(8,128)(2,1)S(1)}, u32[]{:S(2)}, u32[]{:S(2)}) collective-permute-start(bf16[4,16,768]{2,1,0:T(8,128)(2,1)} %get-tuple-element.71), channel_id=1, source_target_pairs={{0,1},{1,0},{2,3},{3,2},{4,5},{5,4},{6,7},{7,6},{8,9},{9,8},{10,11... | collective-permute-start | bytes 294920 | tf_op jit(solution)/shard_map/ppermute | solution.py:28
  15.9 10.1 %collective-permute-start.2 = (bf16[4,16,768]{2,1,0:T(8,128)(2,1)}, bf16[4,16,768]{2,1,0:T(8,128)(2,1)}, u32[]{:S(2)}, u32[]{:S(2)}) collective-permute-start(bf16[4,16,768]{2,1,0:T(8,128)(2,1)} %get-tuple-element.72), channel_id=1, source_target_pairs={{0,1},{1,0},{2,3},{3,2},{4,5},{5,4},{6,7},{7,6},{8,9},{9,8},{10,11... | collective-permute-start | bytes 294920 | tf_op jit(solution)/shard_map/ppermute | solution.py:28
  26.0 10.1 %collective-permute-start.3 = (bf16[4,16,768]{2,1,0:T(8,128)(2,1)}, bf16[4,16,768]{2,1,0:T(8,128)(2,1)}, u32[]{:S(2)}, u32[]{:S(2)}) collective-permute-start(bf16[4,16,768]{2,1,0:T(8,128)(2,1)} %collective-permute-done.2), channel_id=1, source_target_pairs={{0,2},{1,3},{2,0},{3,1},{4,6},{5,7},{6,4},{7,5},{8,10},{9,11},{10,... | collective-permute-start | bytes 294920 | tf_op jit(solution)/shard_map/ppermute | solution.py:28
  37.9 11.4 %collective-permute-start.4 = (bf16[4,16,768]{2,1,0:T(8,128)(2,1)S(1)}, bf16[4,16,768]{2,1,0:T(8,128)(2,1)S(1)}, u32[]{:S(2)}, u32[]{:S(2)}) collective-permute-start(bf16[4,16,768]{2,1,0:T(8,128)(2,1)S(1)} %get-tuple-element.74), channel_id=1, source_target_pairs={{0,4},{1,5},{2,6},{3,7},{4,0},{5,1},{6,2},{7,3},{8,12},{9,13},{10,... | collective-permute-start | bytes 294920 | tf_op jit(solution)/shard_map/ppermute | solution.py:28
  38.8 29.2 %collective-permute-start.5 = (bf16[4,16,768]{2,1,0:T(8,128)(2,1)S(1)}, bf16[4,16,768]{2,1,0:T(8,128)(2,1)S(1)}, u32[]{:S(2)}, u32[]{:S(2)}) collective-permute-start(bf16[4,16,768]{2,1,0:T(8,128)(2,1)S(1)} %get-tuple-element.75), channel_id=1, source_target_pairs={{0,8},{1,9},{2,10},{3,11},{4,12},{5,13},{6,14},{7,15},{8,0},{9,1},... | collective-permute-start | bytes 294920 | tf_op jit(solution)/shard_map/ppermute | solution.py:28
  40.1 27.9 %collective-permute-start.6 = (bf16[4,16,768]{2,1,0:T(8,128)(2,1)S(1)}, bf16[4,16,768]{2,1,0:T(8,128)(2,1)S(1)}, u32[]{:S(2)}, u32[]{:S(2)}) collective-permute-start(bf16[4,16,768]{2,1,0:T(8,128)(2,1)S(1)} %get-tuple-element.76), channel_id=1, source_target_pairs={{0,12},{1,13},{2,14},{3,15},{4,8},{5,9},{6,10},{7,11},{8,4},{9,5},... | collective-permute-start | bytes 294920 | tf_op jit(solution)/shard_map/ppermute | solution.py:28
  73.4 1.4 collective-permute-start.7
  74.9 4.6 %collective-permute-start.8 = (bf16[4,1,16,640]{3,2,1,0:T(8,128)(2,1)S(1)}, bf16[4,1,16,640]{3,2,1,0:T(8,128)(2,1)S(1)}, u32[]{:S(2)}, u32[]{:S(2)}) collective-permute-start(bf16[4,1,16,640]{3,2,1,0:T(8,128)(2,1)S(1)} %get-tuple-element.80), channel_id=1, source_target_pairs={{0,2},{1,3},{2,0},{3,1},{4,6},{5,7},{6,4},{7,5},{8,10},{9,11},{10,... | collective-permute-start | bytes 245768 | tf_op jit(solution)/shard_map/ppermute | solution.py:28
  79.4 4.7 %collective-permute-start.9 = (bf16[1,16,640]{2,1,0:T(8,128)(2,1)S(1)}, bf16[1,16,640]{2,1,0:T(8,128)(2,1)S(1)}, u32[]{:S(2)}, u32[]{:S(2)}) collective-permute-start(bf16[1,16,640]{2,1,0:T(8,128)(2,1)S(1)} %get-tuple-element.82), channel_id=1, source_target_pairs={{0,4},{1,5},{2,6},{3,7},{4,0},{5,1},{6,2},{7,3},{8,12},{9,13},{10,... | collective-permute-start | bytes 61448 | tf_op jit(solution)/shard_map/ppermute | solution.py:28
  81.7 4.7 %collective-permute-start.10 = (bf16[1,16,640]{2,1,0:T(8,128)(2,1)S(1)}, bf16[1,16,640]{2,1,0:T(8,128)(2,1)S(1)}, u32[]{:S(2)}, u32[]{:S(2)}) collective-permute-start(bf16[1,16,640]{2,1,0:T(8,128)(2,1)S(1)} %get-tuple-element.83), channel_id=1, source_target_pairs={{0,8},{1,9},{2,10},{3,11},{4,12},{5,13},{6,14},{7,15},{8,0},{9,1},... | collective-permute-start | bytes 61448 | tf_op jit(solution)/shard_map/ppermute | solution.py:28
  81.8 5.6 %collective-permute-start.11 = (bf16[1,16,640]{2,1,0:T(8,128)(2,1)S(1)}, bf16[1,16,640]{2,1,0:T(8,128)(2,1)S(1)}, u32[]{:S(2)}, u32[]{:S(2)}) collective-permute-start(bf16[1,16,640]{2,1,0:T(8,128)(2,1)S(1)} %get-tuple-element.84), channel_id=1, source_target_pairs={{0,12},{1,13},{2,14},{3,15},{4,8},{5,9},{6,10},{7,11},{8,4},{9,5},... | collective-permute-start | bytes 61448 | tf_op jit(solution)/shard_map/ppermute | solution.py:28
  87.5 5.9 %collective-permute-start.14 = (bf16[1,16,640]{2,1,0:T(8,128)(2,1)S(1)}, bf16[1,16,640]{2,1,0:T(8,128)(2,1)S(1)}, u32[]{:S(2)}, u32[]{:S(2)}) collective-permute-start(bf16[1,16,640]{2,1,0:T(8,128)(2,1)S(1)} %norm.2.refs_0_), channel_id=1, source_target_pairs={{0,12},{1,13},{2,14},{3,15},{4,8},{5,9},{6,10},{7,11},{8,4},{9,5},... | collective-permute-start | bytes 61448 | tf_op jit(solution)/shard_map/ppermute | solution.py:28
  89.9 4.7 %collective-permute-start.13 = (bf16[1,16,640]{2,1,0:T(8,128)(2,1)S(1)}, bf16[1,16,640]{2,1,0:T(8,128)(2,1)S(1)}, u32[]{:S(2)}, u32[]{:S(2)}) collective-permute-start(bf16[1,16,640]{2,1,0:T(8,128)(2,1)S(1)} %norm.2.refs_0_), channel_id=1, source_target_pairs={{0,8},{1,9},{2,10},{3,11},{4,12},{5,13},{6,14},{7,15},{8,0},{9,1},... | collective-permute-start | bytes 61448 | tf_op jit(solution)/shard_map/ppermute | solution.py:28
  89.9 5.3 %collective-permute-start.12 = (bf16[1,16,640]{2,1,0:T(8,128)(2,1)S(1)}, bf16[1,16,640]{2,1,0:T(8,128)(2,1)S(1)}, u32[]{:S(2)}, u32[]{:S(2)}) collective-permute-start(bf16[1,16,640]{2,1,0:T(8,128)(2,1)S(1)} %norm.2.refs_0_), channel_id=1, source_target_pairs={{0,4},{1,5},{2,6},{3,7},{4,0},{5,1},{6,2},{7,3},{8,12},{9,13},{10,... | collective-permute-start | bytes 61448 | tf_op jit(solution)/shard_map/ppermute | solution.py:28
  98.0 17.9 %copy-start.28 = (bf16[4,1,16,640]{3,2,1,0:T(8,128)(2,1)}, bf16[4,1,16,640]{3,2,1,0:T(8,128)(2,1)S(1)}, u32[]{:S(2)}) copy-start(bf16[4,1,16,640]{3,2,1,0:T(8,128)(2,1)S(1)} %merge_z.2.refs_1_.refs_4_) | copy-start | bytes 245764
  109.5 25.8 %collective-permute-start.20 = (bf16[8,3,16,640]{3,2,1,0:T(8,128)(2,1)}, bf16[8,3,16,640]{3,2,1,0:T(8,128)(2,1)S(1)}, u32[]{:S(2)}, u32[]{:S(2)}) collective-permute-start(bf16[8,3,16,640]{3,2,1,0:T(8,128)(2,1)} %get-tuple-element.89), channel_id=1, source_target_pairs={{0,1},{1,0},{2,3},{3,2},{4,5},{5,4},{6,7},{7,6},{8,9},{9,8},{10,11... | collective-permute-start | bytes 1474568 | tf_op jit(solution)/shard_map/ppermute | solution.py:28
  109.6 4.9 %collective-permute-start.15 = (bf16[4,1,16,640]{3,2,1,0:T(8,128)(2,1)S(1)}, bf16[4,1,16,640]{3,2,1,0:T(8,128)(2,1)S(1)}, u32[]{:S(2)}, u32[]{:S(2)}) collective-permute-start(bf16[4,1,16,640]{3,2,1,0:T(8,128)(2,1)S(1)} %merge_z.2.refs_1_.refs_4_), channel_id=1, source_target_pairs={{0,2},{1,3},{2,0},{3,1},{4,6},{5,7},{6,4},{7,5},{8,10},{9,11},{10,... | collective-permute-start | bytes 245768 | tf_op jit(solution)/shard_map/ppermute | solution.py:28
  111.5 3.7 %collective-permute-start.16 = (bf16[4,1,16,640]{3,2,1,0:T(8,128)(2,1)S(1)}, bf16[4,1,16,640]{3,2,1,0:T(8,128)(2,1)S(1)}, u32[]{:S(2)}, u32[]{:S(2)}) collective-permute-start(bf16[4,1,16,640]{3,2,1,0:T(8,128)(2,1)S(1)} %merge_z.2.refs_1_.refs_4_), channel_id=1, source_target_pairs={{0,1},{1,0},{2,3},{3,2},{4,5},{5,4},{6,7},{7,6},{8,9},{9,8},{10,11... | collective-permute-start | bytes 245768 | tf_op jit(solution)/shard_map/ppermute | solution.py:28
  114.6 1.3 collective-permute-start.17
  116.5 18.8 %copy-start.30 = (bf16[8,3,16,640]{3,2,1,0:T(8,128)(2,1)S(1)}, bf16[8,3,16,640]{3,2,1,0:T(8,128)(2,1)}, u32[]{:S(2)}) copy-start(bf16[8,3,16,640]{3,2,1,0:T(8,128)(2,1)} %copy-done.29) | copy-start | bytes 1474564
  135.0 23.7 %collective-permute-start.18 = (bf16[256,1024]{1,0:T(8,128)(2,1)}, bf16[256,1024]{1,0:T(8,128)(2,1)S(1)}, u32[]{:S(2)}, u32[]{:S(2)}) collective-permute-start(bf16[256,1024]{1,0:T(8,128)(2,1)} %get-tuple-element.86.own_ref.refs_0_), channel_id=1, source_target_pairs={{0,1},{1,0},{2,3},{3,2},{4,5},{5,4},{6,7},{7,6},{8,9},{9,8},{10,11... | collective-permute-start | bytes 1572872 | tf_op jit(solution)/shard_map/ppermute | solution.py:28
  136.3 8.3 %collective-permute-start.21 = (bf16[4,3,16,640]{3,2,1,0:T(8,128)(2,1)S(1)}, bf16[4,3,16,640]{3,2,1,0:T(8,128)(2,1)S(1)}, u32[]{:S(2)}, u32[]{:S(2)}) collective-permute-start(bf16[4,3,16,640]{3,2,1,0:T(8,128)(2,1)S(1)} %get-tuple-element.91), channel_id=1, source_target_pairs={{0,2},{1,3},{2,0},{3,1},{4,6},{5,7},{6,4},{7,5},{8,10},{9,11},{10,... | collective-permute-start | bytes 737288 | tf_op jit(solution)/shard_map/ppermute | solution.py:28
  145.7 4.7 %collective-permute-start.22 = (bf16[3,16,640]{2,1,0:T(8,128)(2,1)S(1)}, bf16[3,16,640]{2,1,0:T(8,128)(2,1)S(1)}, u32[]{:S(2)}, u32[]{:S(2)}) collective-permute-start(bf16[3,16,640]{2,1,0:T(8,128)(2,1)S(1)} %get-tuple-element.93), channel_id=1, source_target_pairs={{0,4},{1,5},{2,6},{3,7},{4,0},{5,1},{6,2},{7,3},{8,12},{9,13},{10,... | collective-permute-start | bytes 184328 | tf_op jit(solution)/shard_map/ppermute | solution.py:28
  146.3 7.0 %collective-permute-start.23 = (bf16[3,16,640]{2,1,0:T(8,128)(2,1)S(1)}, bf16[3,16,640]{2,1,0:T(8,128)(2,1)S(1)}, u32[]{:S(2)}, u32[]{:S(2)}) collective-permute-start(bf16[3,16,640]{2,1,0:T(8,128)(2,1)S(1)} %get-tuple-element.94), channel_id=1, source_target_pairs={{0,8},{1,9},{2,10},{3,11},{4,12},{5,13},{6,14},{7,15},{8,0},{9,1},... | collective-permute-start | bytes 184328 | tf_op jit(solution)/shard_map/ppermute | solution.py:28
  148.0 6.1 %collective-permute-start.24 = (bf16[3,16,640]{2,1,0:T(8,128)(2,1)S(1)}, bf16[3,16,640]{2,1,0:T(8,128)(2,1)S(1)}, u32[]{:S(2)}, u32[]{:S(2)}) collective-permute-start(bf16[3,16,640]{2,1,0:T(8,128)(2,1)S(1)} %get-tuple-element.95), channel_id=1, source_target_pairs={{0,12},{1,13},{2,14},{3,15},{4,8},{5,9},{6,10},{7,11},{8,4},{9,5},... | collective-permute-start | bytes 184328 | tf_op jit(solution)/shard_map/ppermute | solution.py:28
  154.3 16.6 %collective-permute-start.27 = (bf16[3,16,640]{2,1,0:T(8,128)(2,1)S(1)}, bf16[3,16,640]{2,1,0:T(8,128)(2,1)S(1)}, u32[]{:S(2)}, u32[]{:S(2)}) collective-permute-start(bf16[3,16,640]{2,1,0:T(8,128)(2,1)S(1)} %norm.3.refs_0_), channel_id=1, source_target_pairs={{0,12},{1,13},{2,14},{3,15},{4,8},{5,9},{6,10},{7,11},{8,4},{9,5},... | collective-permute-start | bytes 184328 | tf_op jit(solution)/shard_map/ppermute | solution.py:28
  156.4 14.5 %collective-permute-start.26 = (bf16[3,16,640]{2,1,0:T(8,128)(2,1)S(1)}, bf16[3,16,640]{2,1,0:T(8,128)(2,1)S(1)}, u32[]{:S(2)}, u32[]{:S(2)}) collective-permute-start(bf16[3,16,640]{2,1,0:T(8,128)(2,1)S(1)} %norm.3.refs_0_), channel_id=1, source_target_pairs={{0,8},{1,9},{2,10},{3,11},{4,12},{5,13},{6,14},{7,15},{8,0},{9,1},... | collective-permute-start | bytes 184328 | tf_op jit(solution)/shard_map/ppermute | solution.py:28
  156.8 14.1 %collective-permute-start.25 = (bf16[3,16,640]{2,1,0:T(8,128)(2,1)S(1)}, bf16[3,16,640]{2,1,0:T(8,128)(2,1)S(1)}, u32[]{:S(2)}, u32[]{:S(2)}) collective-permute-start(bf16[3,16,640]{2,1,0:T(8,128)(2,1)S(1)} %norm.3.refs_0_), channel_id=1, source_target_pairs={{0,4},{1,5},{2,6},{3,7},{4,0},{5,1},{6,2},{7,3},{8,12},{9,13},{10,... | collective-permute-start | bytes 184328 | tf_op jit(solution)/shard_map/ppermute | solution.py:28
  169.3 44.0 %collective-permute-start.32 = (bf16[128,4096]{1,0:T(8,128)(2,1)}, bf16[128,4096]{1,0:T(8,128)(2,1)S(1)}, u32[]{:S(2)}, u32[]{:S(2)}) collective-permute-start(bf16[128,4096]{1,0:T(8,128)(2,1)} %get-tuple-element.99), channel_id=1, source_target_pairs={{0,2},{1,3},{2,0},{3,1},{4,6},{5,7},{6,4},{7,5},{8,10},{9,11},{10,... | collective-permute-start | bytes 3145736 | tf_op jit(solution)/shard_map/ppermute | solution.py:28
  171.0 27.9 %copy-start.15 = (bf16[4,3,16,640]{3,2,1,0:T(8,128)(2,1)}, bf16[4,3,16,640]{3,2,1,0:T(8,128)(2,1)S(1)}, u32[]{:S(2)}) copy-start(bf16[4,3,16,640]{3,2,1,0:T(8,128)(2,1)S(1)} %merge_z.3.refs_1_) | copy-start | bytes 737284
  171.0 26.3 %collective-permute-start.28 = (bf16[4,3,16,640]{3,2,1,0:T(8,128)(2,1)S(1)}, bf16[4,3,16,640]{3,2,1,0:T(8,128)(2,1)S(1)}, u32[]{:S(2)}, u32[]{:S(2)}) collective-permute-start(bf16[4,3,16,640]{3,2,1,0:T(8,128)(2,1)S(1)} %merge_z.3.refs_1_), channel_id=1, source_target_pairs={{0,2},{1,3},{2,0},{3,1},{4,6},{5,7},{6,4},{7,5},{8,10},{9,11},{10,... | collective-permute-start | bytes 737288 | tf_op jit(solution)/shard_map/ppermute | solution.py:28
  171.5 25.8 %collective-permute-start.29 = (bf16[4,3,16,640]{3,2,1,0:T(8,128)(2,1)S(1)}, bf16[4,3,16,640]{3,2,1,0:T(8,128)(2,1)S(1)}, u32[]{:S(2)}, u32[]{:S(2)}) collective-permute-start(bf16[4,3,16,640]{3,2,1,0:T(8,128)(2,1)S(1)} %merge_z.3.refs_1_), channel_id=1, source_target_pairs={{0,1},{1,0},{2,3},{3,2},{4,5},{5,4},{6,7},{7,6},{8,9},{9,8},{10,11... | collective-permute-start | bytes 737288 | tf_op jit(solution)/shard_map/ppermute | solution.py:28
  197.3 1.5 collective-permute-start.30
  199.5 13.8 %copy-start.8 = (bf16[128,4096]{1,0:T(8,128)(2,1)S(1)}, bf16[128,4096]{1,0:T(8,128)(2,1)}, u32[]{:S(2)}) copy-start(bf16[128,4096]{1,0:T(8,128)(2,1)} %get-tuple-element.87.refs_0_) | copy-start | bytes 3145732
  213.2 2.2 collective-permute-start.31
  226.0 28.8 %collective-permute-start.35 = (bf16[128,4096]{1,0:T(8,128)(2,1)}, bf16[128,4096]{1,0:T(8,128)(2,1)S(1)}, u32[]{:S(2)}, u32[]{:S(2)}) collective-permute-start(bf16[128,4096]{1,0:T(8,128)(2,1)} %get-tuple-element.107), channel_id=1, source_target_pairs={{0,2},{1,3},{2,0},{3,1},{4,6},{5,7},{6,4},{7,5},{8,10},{9,11},{10,... | collective-permute-start | bytes 3145736 | tf_op jit(solution)/shard_map/ppermute | solution.py:28
  227.6 13.9 %collective-permute-start.34 = (bf16[2,32,4096]{2,1,0:T(8,128)(2,1)S(1)}, bf16[2,32,4096]{2,1,0:T(8,128)(2,1)S(1)}, u32[]{:S(2)}, u32[]{:S(2)}) collective-permute-start(bf16[2,32,4096]{2,1,0:T(8,128)(2,1)S(1)} %get-tuple-element.104), channel_id=1, source_target_pairs={{0,4},{1,5},{2,6},{3,7},{4,0},{5,1},{6,2},{7,3},{8,12},{9,13},{10,... | collective-permute-start | bytes 1572872 | tf_op jit(solution)/shard_map/ppermute | solution.py:28
  227.9 13.6 %copy-start.17 = (bf16[2,32,4096]{2,1,0:T(8,128)(2,1)S(1)}, bf16[2,32,4096]{2,1,0:T(8,128)(2,1)}, u32[]{:S(2)}) copy-start(bf16[2,32,4096]{2,1,0:T(8,128)(2,1)} %copy-done.16) | copy-start | bytes 1572868
  241.4 2.1 collective-permute-start.33
  254.3 30.7 %collective-permute-start.38 = (bf16[128,4096]{1,0:T(8,128)(2,1)}, bf16[128,4096]{1,0:T(8,128)(2,1)S(1)}, u32[]{:S(2)}, u32[]{:S(2)}) collective-permute-start(bf16[128,4096]{1,0:T(8,128)(2,1)} %get-tuple-element.113), channel_id=1, source_target_pairs={{0,2},{1,3},{2,0},{3,1},{4,6},{5,7},{6,4},{7,5},{8,10},{9,11},{10,... | collective-permute-start | bytes 3145736 | tf_op jit(solution)/shard_map/ppermute | solution.py:28
  257.1 13.8 %collective-permute-start.37 = (bf16[2,32,4096]{2,1,0:T(8,128)(2,1)S(1)}, bf16[2,32,4096]{2,1,0:T(8,128)(2,1)S(1)}, u32[]{:S(2)}, u32[]{:S(2)}) collective-permute-start(bf16[2,32,4096]{2,1,0:T(8,128)(2,1)S(1)} %get-tuple-element.110), channel_id=1, source_target_pairs={{0,4},{1,5},{2,6},{3,7},{4,0},{5,1},{6,2},{7,3},{8,12},{9,13},{10,... | collective-permute-start | bytes 1572872 | tf_op jit(solution)/shard_map/ppermute | solution.py:28
  258.8 12.1 %copy-start.21 = (bf16[2,32,4096]{2,1,0:T(8,128)(2,1)S(1)}, bf16[2,32,4096]{2,1,0:T(8,128)(2,1)}, u32[]{:S(2)}) copy-start(bf16[2,32,4096]{2,1,0:T(8,128)(2,1)} %copy-done.20) | copy-start | bytes 1572868
  270.6 2.2 collective-permute-start.36
  273.6 30.6 %copy-start.23 = (bf16[1,32,4096]{2,1,0:T(8,128)(2,1)S(1)}, bf16[1,32,4096]{2,1,0:T(8,128)(2,1)}, u32[]{:S(2)}) copy-start(bf16[1,32,4096]{2,1,0:T(8,128)(2,1)} %copy-done.22) | copy-start | bytes 786436
  273.6 54.4 %copy-start.25 = (bf16[1,32,4096]{2,1,0:T(8,128)(2,1)S(1)}, bf16[1,32,4096]{2,1,0:T(8,128)(2,1)}, u32[]{:S(2)}) copy-start(bf16[1,32,4096]{2,1,0:T(8,128)(2,1)} %copy-done.24) | copy-start | bytes 786436
  283.5 25.4 %collective-permute-start.41 = (bf16[128,4096]{1,0:T(8,128)(2,1)}, bf16[128,4096]{1,0:T(8,128)(2,1)S(1)}, u32[]{:S(2)}, u32[]{:S(2)}) collective-permute-start(bf16[128,4096]{1,0:T(8,128)(2,1)} %get-tuple-element.119), channel_id=1, source_target_pairs={{0,2},{1,3},{2,0},{3,1},{4,6},{5,7},{6,4},{7,5},{8,10},{9,11},{10,... | collective-permute-start | bytes 3145736 | tf_op jit(solution)/shard_map/ppermute | solution.py:28
  286.2 22.7 %copy-start.12 = (bf16[128,4096]{1,0:T(8,128)(2,1)S(1)}, bf16[128,4096]{1,0:T(8,128)(2,1)}, u32[]{:S(2)}) copy-start(bf16[128,4096]{1,0:T(8,128)(2,1)} %get-tuple-element.112.after_ref) | copy-start | bytes 3145732
  286.5 19.4 %collective-permute-start.40 = (bf16[2,32,4096]{2,1,0:T(8,128)(2,1)S(1)}, bf16[2,32,4096]{2,1,0:T(8,128)(2,1)S(1)}, u32[]{:S(2)}, u32[]{:S(2)}) collective-permute-start(bf16[2,32,4096]{2,1,0:T(8,128)(2,1)S(1)} %get-tuple-element.117), channel_id=1, source_target_pairs={{0,4},{1,5},{2,6},{3,7},{4,0},{5,1},{6,2},{7,3},{8,12},{9,13},{10,... | collective-permute-start | bytes 1572872 | tf_op jit(solution)/shard_map/ppermute | solution.py:28
  288.3 15.8 %collective-permute-start.39 = (bf16[1,32,4096]{2,1,0:T(8,128)(2,1)S(1)}, bf16[1,32,4096]{2,1,0:T(8,128)(2,1)S(1)}, u32[]{:S(2)}, u32[]{:S(2)}) collective-permute-start(bf16[1,32,4096]{2,1,0:T(8,128)(2,1)S(1)} %get-tuple-element.115), channel_id=1, source_target_pairs={{0,8},{1,9},{2,10},{3,11},{4,12},{5,13},{6,14},{7,15},{8,0},{9,1},... | collective-permute-start | bytes 786440 | tf_op jit(solution)/shard_map/ppermute | solution.py:28
  309.2 25.6 %collective-permute-start.44 = (bf16[2,32,4096]{2,1,0:T(8,128)(2,1)S(1)}, bf16[2,32,4096]{2,1,0:T(8,128)(2,1)S(1)}, u32[]{:S(2)}, u32[]{:S(2)}) collective-permute-start(bf16[2,32,4096]{2,1,0:T(8,128)(2,1)S(1)} %get-tuple-element.125), channel_id=1, source_target_pairs={{0,4},{1,5},{2,6},{3,7},{4,0},{5,1},{6,2},{7,3},{8,12},{9,13},{10,... | collective-permute-start | bytes 1572872 | tf_op jit(solution)/shard_map/ppermute | solution.py:28
  309.9 18.0 %collective-permute-start.42 = (bf16[1,32,4096]{2,1,0:T(8,128)(2,1)S(1)}, bf16[1,32,4096]{2,1,0:T(8,128)(2,1)S(1)}, u32[]{:S(2)}, u32[]{:S(2)}) collective-permute-start(bf16[1,32,4096]{2,1,0:T(8,128)(2,1)S(1)} %get-tuple-element.121), channel_id=1, source_target_pairs={{0,8},{1,9},{2,10},{3,11},{4,12},{5,13},{6,14},{7,15},{8,0},{9,1},... | collective-permute-start | bytes 786440 | tf_op jit(solution)/shard_map/ppermute | solution.py:28
  312.0 22.7 %collective-permute-start.43 = (bf16[1,32,4096]{2,1,0:T(8,128)(2,1)S(1)}, bf16[1,32,4096]{2,1,0:T(8,128)(2,1)S(1)}, u32[]{:S(2)}, u32[]{:S(2)}) collective-permute-start(bf16[1,32,4096]{2,1,0:T(8,128)(2,1)S(1)} %get-tuple-element.123), channel_id=1, source_target_pairs={{0,8},{1,9},{2,10},{3,11},{4,12},{5,13},{6,14},{7,15},{8,0},{9,1},... | collective-permute-start | bytes 786440 | tf_op jit(solution)/shard_map/ppermute | solution.py:28
  334.9 12.1 %collective-permute-start.45 = (bf16[1,32,4096]{2,1,0:T(8,128)(2,1)S(1)}, bf16[1,32,4096]{2,1,0:T(8,128)(2,1)S(1)}, u32[]{:S(2)}, u32[]{:S(2)}) collective-permute-start(bf16[1,32,4096]{2,1,0:T(8,128)(2,1)S(1)} %get-tuple-element.127), channel_id=1, source_target_pairs={{0,8},{1,9},{2,10},{3,11},{4,12},{5,13},{6,14},{7,15},{8,0},{9,1},... | collective-permute-start | bytes 786440 | tf_op jit(solution)/shard_map/ppermute | solution.py:28
  335.2 12.0 %collective-permute-start.46 = (bf16[16,4096]{1,0:T(8,128)(2,1)S(1)}, bf16[16,4096]{1,0:T(8,128)(2,1)S(1)}, u32[]{:S(2)}, u32[]{:S(2)}) collective-permute-start(bf16[16,4096]{1,0:T(8,128)(2,1)S(1)} %get-tuple-element.129), channel_id=1, source_target_pairs={{0,1},{1,0},{2,3},{3,2},{4,5},{5,4},{6,7},{7,6},{8,9},{9,8},{10,11... | collective-permute-start | bytes 393224 | tf_op jit(solution)/shard_map/ppermute | solution.py:28
  335.3 12.0 %collective-permute-start.48 = (bf16[16,4096]{1,0:T(8,128)(2,1)S(1)}, bf16[16,4096]{1,0:T(8,128)(2,1)S(1)}, u32[]{:S(2)}, u32[]{:S(2)}) collective-permute-start(bf16[16,4096]{1,0:T(8,128)(2,1)S(1)} %get-tuple-element.131), channel_id=1, source_target_pairs={{0,1},{1,0},{2,3},{3,2},{4,5},{5,4},{6,7},{7,6},{8,9},{9,8},{10,11... | collective-permute-start | bytes 393224 | tf_op jit(solution)/shard_map/ppermute | solution.py:28
  335.8 11.5 %collective-permute-start.47 = (bf16[16,4096]{1,0:T(8,128)(2,1)S(1)}, bf16[16,4096]{1,0:T(8,128)(2,1)S(1)}, u32[]{:S(2)}, u32[]{:S(2)}) collective-permute-start(bf16[16,4096]{1,0:T(8,128)(2,1)S(1)} %get-tuple-element.130), channel_id=1, source_target_pairs={{0,1},{1,0},{2,3},{3,2},{4,5},{5,4},{6,7},{7,6},{8,9},{9,8},{10,11... | collective-permute-start | bytes 393224 | tf_op jit(solution)/shard_map/ppermute | solution.py:28
  347.1 1.4 collective-permute-start.49
  (45 other events, 89.5 us)

commit v5 on v4

--- a/solution.py
+++ b/solution.py
@@ -41,7 +41,7 @@
     return pl.BlockSpec(shape, lambda *_: zeros)
 
 
-def small(kernel, me, args, shapes, name, after=()):
+def small(kernel, me, args, shapes, name, after=(), dtype=BF16, scratch=(), mib=8):
     size = sum(a.size for a in args)
     vmem = pl.BlockSpec(memory_space=pltpu.VMEM)
     return pl.pallas_call(
@@ -50,14 +50,15 @@
         + [pl.BlockSpec(memory_space=pl.ANY)] * len(after)
         + [vmem] * len(args),
         out_specs=[vmem] * len(shapes),
-        out_shape=[jax.ShapeDtypeStruct(s, BF16) for s in shapes],
-        compiler_params=params(8),
+        out_shape=[jax.ShapeDtypeStruct(s, dtype) for s in shapes],
+        scratch_shapes=list(scratch),
+        compiler_params=params(mib),
         cost_estimate=cost(size, 4 * size),
         name=name,
     )(me, *after, *args)
 
 
-def pack_conv_kernel(me_ref, after_ref, x_ref, *o_refs):
+def pack_conv_kernel(me_ref, x_ref, *o_refs):
     zs, _, wide = o_refs[0].shape
     y, core = (me_ref[0] // 2) % 2, me_ref[0] % 2
     c = wide * (TAPS + 1) // TAPS
@@ -79,19 +80,19 @@
             refs[4 + m][at] = refs[i][jnp.bitwise_xor(z, m)]
 
 
-def exchange_conv(prefilled_conv, packed_state, me, n):
+def exchange_conv(prefilled_conv, me, n):
     slots, _, inner = prefilled_conv.shape
     zs = n // 4
     piece = ((TAPS + 1) * slots, inner // n * TAPS // (TAPS + 1))
     conv = jnp.transpose(prefilled_conv, (1, 0, 2))
-    packed = small(pack_conv_kernel, me, [conv], [(zs,) + piece] * 4, "pack_conv", (packed_state,))
+    packed = small(pack_conv_kernel, me, [conv], [(zs,) + piece] * 4, "pack_conv")
     near, far = swap(packed[2], 1, n), swap(packed[3], 1, n)
     got = [packed[0], swap(packed[1], 2, n), near, swap(far, 2, n)]
     cut = small(cut_conv_kernel, me, got, [(4,) + piece] * zs, "cut_conv")
     return [cut[0]] + [swap(cut[m], 4 * m, n) for m in range(1, zs)]
 
 
-def pack_state_kernel(x_ref, o_ref):
+def pack_state_kernel(after_ref, x_ref, o_ref):
     slots = x_ref.shape[0]
     some, _, c = o_ref.shape
     for d in range(some):
@@ -99,20 +100,24 @@
             o_ref[d, STATE * k : STATE * (k + 1), :] = x_ref[k, :, d * c : (d + 1) * c].astype(BF16)
 
 
-def pack_state(prefilled_state, n):
+def pack_state(part, after, prefilled_state, n):
     slots, _, inner = prefilled_state.shape
+    slots //= 2
     c = inner // n
     some = 4
     return pl.pallas_call(
         pack_state_kernel,
         grid=(n // some,),
-        in_specs=[pl.BlockSpec((slots, STATE, some * c), lambda d: (0, 0, d))],
+        in_specs=[
+            pl.BlockSpec(memory_space=pl.ANY),
+            pl.BlockSpec((slots, STATE, some * c), lambda d: (part, 0, d)),
+        ],
         out_specs=pl.BlockSpec((some, slots * STATE, c), lambda d: (d, 0, 0)),
         out_shape=jax.ShapeDtypeStruct((n, slots * STATE, c), BF16),
         compiler_params=params(24),
         cost_estimate=cost(0, slots * STATE * inner * 6),
         name="pack_state",
-    )(prefilled_state)
+    )(after, prefilled_state)
 
 
 def conv_kernel(steps, n, me_ref, target_ref, old_ref, x_ref, w_ref, bias_ref, proj_ref, *refs):
@@ -249,11 +254,21 @@
     return mine, (mine, beside, swap(mine, 1, n), swap(beside, 1, n))
 
 
-def state_kernel(first, last, me_ref, live_ref, *refs):
-    if first:
-        moved_ref, *refs = refs
-    else:
-        _, *refs = refs
+def assemble_low(lows, index, low_scr, me_ref):
+    y, core = (me_ref[0] // 2) % 2, me_ref[0] % 2
+    for i, low_ref in enumerate(lows):
+        for z in range(low_ref.shape[0]):
+            low_scr[z, jnp.bitwise_xor(y, i % 2), jnp.bitwise_xor(core, i // 2)] = low_ref[z] if index is None else low_ref[z, index]
+    return low_scr[...].reshape(-1, WIDE)
+
+
+def step_sizes(low, dtp_ref, dtb_ref):
+    pre = jnp.dot(low[:, :DT_RANK], dtp_ref[...], preferred_element_type=F32) + dtb_ref[...]
+    return jnp.maximum(pre, 0.0) + jnp.log(1.0 + jnp.exp(-jnp.abs(pre)))
+
+
+def state_kernel(first, last, behind, me_ref, *refs):
+    refs = refs[behind:]
     lows, refs = refs[:4], refs[4:]
     conv_ref, z_ref, dtp_ref, dtb_ref, alog_ref, skip_ref, state_ref, *refs = refs
     new_ref = None
@@ -264,7 +279,6 @@
     rows, c = step_scr.shape
     take = conv_ref.shape[0]
     blocks = rows // take
-    y, core = (me_ref[0] // 2) % 2, me_ref[0] % 2
 
     if first:
         buf, sems = refs
@@ -294,12 +308,8 @@
 
     @pl.when(block == 0)
     def _():
-        for i, low_ref in enumerate(lows):
-            for z in range(low_ref.shape[0]):
-                low_scr[z, jnp.bitwise_xor(y, i % 2), jnp.bitwise_xor(core, i // 2)] = low_ref[z]
-        low = low_scr[...].reshape(rows, WIDE)
-        pre = jnp.dot(low[:, :DT_RANK], dtp_ref[...], preferred_element_type=F32) + dtb_ref[...]
-        step_scr[...] = jnp.maximum(pre, 0.0) + jnp.log(1.0 + jnp.exp(-jnp.abs(pre)))
+        low = assemble_low(lows, None, low_scr, me_ref)
+        step_scr[...] = step_sizes(low, dtp_ref, dtb_ref)
         decay_scr[...] = -jnp.exp(alog_ref[...])
         tail_scr[...] = low[:, DT_RANK:].astype(F32)
 
@@ -307,15 +317,6 @@
     if first:
         for copy in fetch(block, now):
             copy.wait()
-
-        def replace(i, carry):
-            at = pl.multiple_of((live_ref[1, i] - base) * STATE, STATE)
-            value = moved_ref[live_ref[2, i]].astype(F32)
-            for l in range(c // 128):
-                buf[now, l, pl.ds(at, STATE), :] = value[:, 128 * l : 128 * (l + 1)]
-            return carry
-
-        lax.fori_loop(live_ref[0, block], live_ref[0, block + 1], replace, 0)
 
     tall, lanes = 16, min(512, c)
     for r in range(0, take, tall):
@@ -341,7 +342,7 @@
             gated_ref[r : r + tall, cols] = (total * (z * sigmoid(z))).astype(BF16)
 
 
-def state_step(t, index, me, live, extra, lows, conv, step_z, dt_proj, dt_bias, a_log, d_skip, state, n):
+def state_step(t, me, after, lows, conv, step_z, dt_proj, dt_bias, a_log, d_skip, state, n):
     _, rows, c = conv.shape
     take = 2 * rows // n
     blocks = rows // take
@@ -349,13 +350,13 @@
     own = rows // n
     zs = n // 4
 
-    def placed(i, me_ref, live_ref):
+    def placed(i, me_ref):
         z, y = i // 2, i % 2
         mine = (y == (me_ref[0] // 2) % 2).astype(jnp.int32)
         return (mine * (blocks // 2) + z, 0)
 
-    in_specs = [pl.BlockSpec((zs, None, own, WIDE), lambda i, *_: (0, index, 0, 0))] * 4 + [
-        pl.BlockSpec((None, take, c), lambda i, *_: (index, i, 0)),
+    in_specs = [pl.BlockSpec((zs, None, own, WIDE), lambda i, *_: (0, t, 0, 0))] * 4 + [
+        pl.BlockSpec((None, take, c), lambda i, *_: (t, i, 0)),
         pl.BlockSpec((1, take, c), lambda i, *_: (t, i, 0)),
         whole(dt_proj.shape),
         whole((1, c)),
@@ -370,13 +371,14 @@
     ]
     flat = pl.BlockSpec((STATE, take, c), lambda i, *_: (0, i, 0))
     if first:
-        in_specs = [whole(extra[0].shape)] + in_specs + [pl.BlockSpec(memory_space=pl.ANY)]
+        in_specs = in_specs + [pl.BlockSpec(memory_space=pl.ANY)]
         scratch += [
             pltpu.VMEM((2, c // 128, take * STATE, 128), F32),
             pltpu.SemaphoreType.DMA((2, c // 128)),
         ]
     else:
-        in_specs = [pl.BlockSpec(memory_space=pl.ANY)] + in_specs + [flat]
+        in_specs = in_specs + [flat]
+    in_specs = [pl.BlockSpec(memory_space=pl.ANY)] * len(after) + in_specs
     out_specs = [pl.BlockSpec((take, c), placed)]
     out_shape = [jax.ShapeDtypeStruct((rows, c), BF16)]
     if not last:
@@ -384,9 +386,9 @@
         out_shape = [jax.ShapeDtypeStruct((STATE, rows, c), BF16)] + out_shape
     size = rows * STATE * c
     out = pl.pallas_call(
-        functools.partial(state_kernel, first, last),
+        functools.partial(state_kernel, first, last, len(after)),
         grid_spec=pltpu.PrefetchScalarGridSpec(
-            num_scalar_prefetch=2,
+            num_scalar_prefetch=1,
             grid=(blocks,),
             in_specs=in_specs,
             out_specs=out_specs,
@@ -396,8 +398,121 @@
         compiler_params=params(56),
         cost_estimate=cost(8 * size, 4 * size, size),
         name="state_step",
-    )(me, live, *extra, *lows, conv, step_z, dt_proj, dt_bias, a_log, d_skip, state)
+    )(me, *after, *lows, conv, step_z, dt_proj, dt_bias, a_log, d_skip, state)
     return (None, out[0]) if last else (out[0], out[1])
+
+
+def gather_kernel(me_ref, after_ref, row_ref, *refs):
+    lows, refs = refs[:4], refs[4:]
+    conv_ref, z_ref, dtp_ref, dtb_ref, step_ref, live_conv_ref, gate_ref, tail_ref, low_scr = refs
+    count = step_ref.shape[1]
+    rows = conv_ref.shape[1]
+    hot = (row_ref[:, :1] == lax.broadcasted_iota(jnp.int32, (count, rows), 1)).astype(F32).astype(BF16)
+    for t in range(STEPS):
+        low = jnp.dot(hot, assemble_low(lows, t, low_scr, me_ref), preferred_element_type=F32)
+        step_ref[t] = step_sizes(low.astype(BF16), dtp_ref, dtb_ref)
+        tail_ref[t, :, :128] = low[:, DT_RANK:]
+        conv = conv_ref[t]
+        high = conv.astype(BF16)
+        rest = (conv - high.astype(F32)).astype(BF16)
+        live_conv_ref[t] = jnp.dot(hot, high, preferred_element_type=F32) + jnp.dot(
+            hot, rest, preferred_element_type=F32
+        )
+        z = jnp.dot(hot, z_ref[t], preferred_element_type=F32)
+        gate_ref[t] = z * sigmoid(z)
+
+
+def gather_live(me, after, row_of_live, lows, conv, step_z, dt_proj, dt_bias, n):
+    _, rows, c = conv.shape
+    count = row_of_live.shape[0]
+    wide = (STEPS, count, c)
+    return small(
+        gather_kernel,
+        me,
+        [row_of_live, *lows, conv, step_z, dt_proj, dt_bias],
+        [wide, wide, wide, (STEPS, count, 128)],
+        "gather_live",
+        after,
+        F32,
+        [pltpu.VMEM((n // 4, 2, 2, rows // n, WIDE), BF16)],
+        40,
+    )
+
+
+def live_kernel(slot_ref, after_ref, low_ref, high_ref, step_ref, conv_ref, gate_ref, tail_ref, alog_ref, skip_ref, o_ref, buf, state_scr):
+    _, count, c = o_ref.shape
+    half = low_ref.shape[1] // STATE
+
+    def place(i, carry):
+        source, slot = slot_ref[0, i], slot_ref[1, i]
+        at = pl.multiple_of(i * STATE, STATE)
+        for side, moved_ref in ((0, low_ref), (1, high_ref)):
+
+            @pl.when((slot >= half) == bool(side))
+            def _(side=side, moved_ref=moved_ref):
+                from_row = pl.multiple_of((slot - half * side) * STATE, STATE)
+                value = moved_ref[source, pl.ds(from_row, STATE), :].astype(F32)
+                for l in range(c // 128):
+                    buf[l, pl.ds(at, STATE), :] = value[:, 128 * l : 128 * (l + 1)]
+
+        return carry
+
+    lax.fori_loop(0, count, place, 0)
+    for s in range(STATE):
+        for l in range(c // 128):
+            state_scr[s, :, 128 * l : 128 * (l + 1)] = buf[l, pl.ds(s, count, stride=STATE), :]
+    tall, lanes = 16, min(512, c)
+
+    def step_all(t, carry):
+        for r in range(0, count, tall):
+            tail = tail_ref[t, r : r + tall, :]
+            for l in range(0, c, lanes):
+                cols = slice(l, l + lanes)
+                step = step_ref[t, r : r + tall, cols]
+                conv = conv_ref[t, r : r + tall, cols]
+                drive = step * conv
+                total = skip_ref[:, cols] * conv
+                for s in range(STATE):
+                    rate = -jnp.exp(alog_ref[s : s + 1, cols])
+                    old = state_scr[s, r : r + tall, cols]
+                    state = jnp.exp(step * rate) * old + drive * tail[:, s : s + 1]
+                    state_scr[s, r : r + tall, cols] = state
+                    total = total + state * tail[:, STATE + s : STATE + s + 1]
+                o_ref[t, r : r + tall, cols] = (total * gate_ref[t, r : r + tall, cols]).astype(BF16)
+        return carry
+
+    lax.fori_loop(0, STEPS, step_all, 0)
+
+
+def live_steps(slot_of_live, after, moved, gathered, a_log, d_skip):
+    _, count, c = gathered[0].shape
+    (out,) = small(
+        live_kernel,
+        slot_of_live,
+        [*moved, *gathered, a_log, d_skip],
+        [(STEPS, count, c)],
+        "live_steps",
+        after,
+        BF16,
+        [pltpu.VMEM((c // 128, count * STATE, 128), F32), pltpu.VMEM((STATE, count, c), F32)],
+        32,
+    )
+    return out
+
+
+def fix_kernel(t, take, me_ref, after_ref, row_ref, gated_ref, live_ref, o_ref):
+    rows = gated_ref.shape[0]
+    count = live_ref.shape[1]
+    shift = take.bit_length() - 1
+    place = lax.broadcasted_iota(jnp.int32, (rows, count), 0)
+    mine = place >= rows // 2
+    within = place - jnp.where(mine, rows // 2, 0)
+    y = (me_ref[0] // 2) % 2
+    row = ((2 * (within >> shift) + jnp.where(mine, y, 1 - y)) << shift) + (within & (take - 1))
+    hot = (row == row_ref[...]).astype(F32)
+    taken = jnp.max(hot, axis=1, keepdims=True) > 0.0
+    live = jnp.dot(hot.astype(BF16), live_ref[t], preferred_element_type=F32)
+    o_ref[...] = jnp.where(taken, live, gated_ref[...].astype(F32)).astype(BF16)
 
 
 def out_kernel(me_ref, own_ref, other_ref, wown_ref, wother_ref, *refs):
@@ -507,9 +622,9 @@
     me_scalar = lax.axis_index("dex").astype(jnp.int32)
     me = me_scalar.reshape(1)
 
-    packed_state = pack_state(prefilled_state, n)
-    moved_conv = exchange_conv(prefilled_conv, packed_state, me, n)
-    moved_state = lax.all_to_all(packed_state, "dex", 0, 0, tiled=True)
+    moved_conv = exchange_conv(prefilled_conv, me, n)
+    packed = pack_state(0, moved_conv[0], prefilled_state, n)
+    moved_low = lax.all_to_all(packed, "dex", 0, 0, tiled=True)
     other_weight = swap(out_weight, 1, n)
     cols = out_weight.shape[1] // 2
 
@@ -519,50 +634,43 @@
     mine = place[None, None, :, None] == place[:, None, None, None]
     spread = jnp.where(mine, target[None, :, None, :], -1).reshape(TAPS + 1, n * (TAPS + 1) * slots)
     flat = target.reshape(-1)
-    count = n * slots
-    number = jnp.arange(count, dtype=jnp.int32)
-    key = jnp.where(flat < 0, rows + number, flat)
-    before = jnp.sum((key[None, :] < key[:, None]).astype(jnp.int32), axis=1)
-    hit = before[None, :] == number[:, None]
-    bounds = jnp.arange(count, dtype=jnp.int32) * (2 * rows // n)
-    live = jnp.stack(
-        [
-            jnp.sum((key[None, :] < jnp.minimum(bounds, rows)[:, None]).astype(jnp.int32), axis=1),
-            jnp.sum(jnp.where(hit, key[None, :], 0), axis=1),
-            jnp.sum(jnp.where(hit, number[None, :], 0), axis=1),
-        ]
-    )
+    number = jnp.arange(n * slots, dtype=jnp.int32)
+    count = n * slots // 2
+    rank = jnp.sum(((flat >= 0)[None, :] & (number[None, :] < number[:, None])).astype(jnp.int32), axis=1)
+    hit = (rank[None, :] == number[:count, None]) & (flat >= 0)[None, :]
+    live_slot = jnp.sum(jnp.where(hit, number[None, :], 0), axis=1)
+    live_row = jnp.sum(jnp.where(hit, flat[None, :], 0), axis=1)
+    slot_of_live = jnp.stack([live_slot // slots, live_slot % slots])
+    row_of_live = jnp.broadcast_to(live_row[:, None], (count, 128))
+    live_row = live_row.reshape(1, count)
     gain = jnp.concatenate([norm_gain, jnp.zeros((WIDE - norm_gain.shape[0],), F32)]).reshape(1, WIDE)
     old = jnp.transpose(resident_conv, (1, 0, 2))
     proj = x_proj.T
     bias = conv_bias.reshape(1, c)
-    moved_state = moved_state.reshape(n * slots, STATE, c)
-
-    lows = {}
-    convs = {}
-
-    def low_rows(steps, after, after_y, after_z):
-        conv, send, keep = conv_steps(
-            steps, n, me, after, spread, old, moved_conv, step_x, conv_weight, bias, proj
-        )
-        merged, low = reduce_projection(send, keep, gain, me, after_y, after_z, n)
-        for i, t in enumerate(steps):
-            lows[t] = (low, i)
-            convs[t] = conv
-        return merged
+    conv, send, keep = conv_steps(
+        tuple(range(STEPS)), n, me, (), spread, old, moved_conv, step_x, conv_weight, bias, proj
+    )
+    merged, lows = reduce_projection(send, keep, gain, me, (), (), n)
+    packed = pack_state(1, merged, prefilled_state, n)
+    moved_high = lax.all_to_all(packed, "dex", 0, 0, tiled=True)
 
     state = resident_state.reshape(rows * STATE, c)
     sends, keeps, gated = {}, {}, {}
     stages = zs.bit_length() - 1
     take = 2 * rows // n
 
-    def s_step(t, extra):
+    rate_bias, skip = dt_bias.reshape(1, c), d_skip.reshape(1, c)
+
+    def s_step(t, after):
         nonlocal state
-        low, i = lows[t]
         state, gated[t] = state_step(
-            t, i, me, live, extra, low, convs[t], step_z, dt_proj,
-            dt_bias.reshape(1, c), a_log, d_skip.reshape(1, c), state, n,
+            t, me, (after,), lows, conv, step_z, dt_proj, rate_bias, a_log, skip, state, n
         )
+        return gated[t]
+
+    def fix(t, after):
+        kernel = functools.partial(fix_kernel, t, take)
+        (gated[t],) = small(kernel, me, [live_row, gated[t], live_gated], [(rows, c)], "fix", (after,))
         return gated[t]
 
     def project(t, after):
@@ -583,23 +691,27 @@
             sends[t] = swap(sends[t], 1, n)
         return keeps[t]
 
-    merged = low_rows((0,), (), (), ())
-    last = s_step(0, (moved_state,))
-    low_rows(tuple(range(1, STEPS)), (merged,), (lows[0][0][3],), (last,))
+    last = s_step(0, packed)
+    gathered = gather_live(me, (last,), row_of_live, lows, conv, step_z, dt_proj, rate_bias, n)
+    last = s_step(1, gathered[0])
+    live_gated = live_steps(slot_of_live, (last,), [moved_low, moved_high], gathered, a_log, skip)
+    last = fix(0, live_gated)
+    last = fix(1, last)
     last = project(0, last)
-    last = s_step(1, (last,))
+    last = project(1, last)
+    last = s_step(2, last)
+    last = fix(2, last)
     last = reduce(0, 0, last)
-    last = project(1, last)
-    last = s_step(2, (last,))
+    last = project(2, last)
+    last = s_step(3, last)
+    last = fix(3, last)
     for stage in range(1, stages):
         last = reduce(0, stage, last)
-    last = project(2, last)
     last = reduce(1, 0, last)
-    last = s_step(3, (last,))
+    last = project(3, last)
+    last = reduce(2, 0, last)
     for stage in range(1, stages):
         last = reduce(1, stage, last)
-    last = project(3, last)
-    last = reduce(2, 0, last)
     last = reduce(0, stages, last)
     for stage in range(1, stages):
         last = reduce(2, stage, last)

time: 353 us -> 343 us (0.972)
  local copies, waits for them, and re-layouts: 36.4 us -> 28.1 us
  starting transfers between devices: 56.2 us -> 51.8 us
  Pallas kernels: 111 us -> 115 us
    ppermute x50 -> x39, starting transfers between devices: 48.8 us -> 41.1 us  [swap(): return lax.ppermute(x, 'dex', [(i, i ^ mask) for i in range(n)])]
    pallas_call x22 -> x24, Pallas kernels: 3.96 us -> 11.6 us  [small(): pl.pallas_call(kernel, in_specs=[pl.BlockSpec(memory_space=pltpu.SMEM)] +...]
    unnamed x116, local copies, waits for them, and re-layouts: 34.7 us -> 27.5 us
    all_to_all x1 -> x2, starting transfers between devices: 7.37 us -> 10.7 us  [the longest x1 6.16 us: shards(): moved_low = lax.all_to_all(packed, 'dex', 0, 0, tiled=True)]
    ppermute x50 -> x39, waiting for transfers between devices: 144 us -> 145 us  [swap(): return lax.ppermute(x, 'dex', [(i, i ^ mask) for i in range(n)])]
  transfers between devices with their start and end apart: 51 -> 41, of which waited for: 27 -> 22; matrix products, arithmetic and copies ran while one was open for 1% -> 0% of each run, Pallas kernels for 28% -> 33%
where the time goes in v5:
time: 343 us; the launch traced here: 342 us
  waiting for transfers between devices  145 us (42%)
  Pallas kernels  115 us (34%)
  starting transfers between devices  51.8 us (15%)
  local copies, waits for them, and re-layouts  28.1 us (8%)
    ppermute x39, waiting for transfers between devices, swap(): return lax.ppermute(x, 'dex', [(i, i ^ mask) for i in range(n)])  145 us
    pallas_call x4, Pallas kernels, state_step(): pl.pallas_call(functools.partial(state_kernel, first, last, len(after)),...  54.6 us
    ppermute x39, starting transfers between devices, swap(): return lax.ppermute(x, 'dex', [(i, i ^ mask) for i in range(n)])  41.1 us
    pallas_call x4, Pallas kernels, out_project(): pl.pallas_call(out_kernel, grid_spec=pltpu.PrefetchScalarGridSpec(num_sca...  39.4 us
    unnamed x116, local copies, waits for them, and re-layouts  27.5 us
    pallas_call x24, Pallas kernels, small(): pl.pallas_call(kernel, in_specs=[pl.BlockSpec(memory_space=pltpu.SMEM)] +...  11.6 us
  transfers between devices with their start and end apart: 41, of which 22 were waited for; matrix products, arithmetic and copies ran while one was open for 0% of the time, Pallas kernels for 33%

profile of v5, /device:TPU:0, one launch (start us, length us, event | category | flops | bytes accessed | tf_op | source)
XLA Modules:
  0.0 341.5 jit_solution(13468439633237642259)
XLA Ops:
  0.5 1.1 copy-done.40
  1.8 3.0 collective-permute-start
  4.8 14.4 %collective-permute-done.2 = bf16[4,16,768]{2,1,0:T(8,128)(2,1)S(1)} collective-permute-done((bf16[4,16,768]{2,1,0:T(8,128)(2,1)S(1)}, bf16[4,16,768]{2,1,0:T(8,128)(2,1)S(1)}, u32[]{:S(2)}, u32[]{:S(2)}) %collective-permute-start.2) | collective-permute-done | bytes 98336 | tf_op jit(solution)/shard_map/ppermute | solution.py:28
  19.3 2.7 collective-permute-start.3
  21.9 3.3 collective-permute-done.3.refs_3_
  25.9 2.2 copy-done.4
  28.1 1.7 pack_state.3
  29.8 6.2 %all-to-all-start = ((bf16[16,32,1024]{2,1,0:T(8,128)(2,1)}), bf16[16,32,1024]{2,1,0:T(8,128)(2,1)S(1)}, u32[]{:S(2)}, u32[]{:S(2)}) async-start(bf16[16,32,1024]{2,1,0:T(8,128)(2,1)} %pack_state.3), calls=%async_computation | async-start | bytes 2097152 | tf_op jit(solution)/shard_map/all_to_all | solution.py:627
  36.5 2.0 collective-permute-start.4
  38.5 2.4 collective-permute-start.5
  41.0 15.4 %collective-permute-done.4.refs_1_ = bf16[4,16,768]{2,1,0:T(8,128)(2,1)S(1)} collective-permute-done((bf16[4,16,768]{2,1,0:T(8,128)(2,1)}, bf16[4,16,768]{2,1,0:T(8,128)(2,1)S(1)}, u32[]{:S(2)}, u32[]{:S(2)}) %collective-permute-start.4) | collective-permute-done | bytes 98336 | tf_op jit(solution)/shard_map/ppermute | solution.py:28
  56.4 12.9 %collective-permute-done.5.refs_2_ = bf16[4,16,768]{2,1,0:T(8,128)(2,1)S(1)} collective-permute-done((bf16[4,16,768]{2,1,0:T(8,128)(2,1)S(1)}, bf16[4,16,768]{2,1,0:T(8,128)(2,1)S(1)}, u32[]{:S(2)}, u32[]{:S(2)}) %collective-permute-start.5) | collective-permute-done | bytes 98336 | tf_op jit(solution)/shard_map/ppermute | solution.py:28
  69.3 1.9 copy-done.26
  71.2 1.2 copy-done.39
  72.5 3.9 %conv_project.1 = (f32[4,256,1024]{2,1,0:T(8,128)S(1)}, bf16[8,4,16,640]{3,2,1,0:T(8,128)(2,1)S(1)}, bf16[8,4,16,640]{3,2,1,0:T(8,128)(2,1)S(1)}) custom-call(s32[1]{0:T(128)} %bitcast.me_ref, s32[4,256]{1,0:T(4,128)S(1)} %broadcast_select_fusion.1.target_ref, f32[3,256,1024]{2,1,0:T(8,128)S(1)} %bitcast.37, bf16[4,256,1024]{2,1,0:T(8,128)(2,1)S(1)} %copy-done.37, ...), custom_call_target="tpu_custom_call" | custom-call | flops 1024 | bytes 1024 | tf_op jit(solution)/shard_map/conv_project/pallas_call | solution.py:170
  76.4 1.9 copy-done
  78.3 2.1 collective-permute-done.7.refs_1_
  80.6 1.5 collective-permute-start.8
  82.1 8.3 %collective-permute-done.8.refs_1_ = bf16[4,4,16,640]{3,2,1,0:T(8,128)(2,1)S(1)} collective-permute-done((bf16[4,4,16,640]{3,2,1,0:T(8,128)(2,1)S(1)}, bf16[4,4,16,640]{3,2,1,0:T(8,128)(2,1)S(1)}, u32[]{:S(2)}, u32[]{:S(2)}) %collective-permute-start.8) | collective-permute-done | bytes 327712 | tf_op jit(solution)/shard_map/ppermute | solution.py:28
  90.5 2.3 collective-permute-start.9
  92.8 2.4 collective-permute-start.11
  95.3 5.8 %collective-permute-done.10.refs_2_ = bf16[4,16,640]{2,1,0:T(8,128)(2,1)S(1)} collective-permute-done((bf16[4,16,640]{2,1,0:T(8,128)(2,1)S(1)}, bf16[4,16,640]{2,1,0:T(8,128)(2,1)S(1)}, u32[]{:S(2)}, u32[]{:S(2)}) %collective-permute-start.10) | collective-permute-done | bytes 81952 | tf_op jit(solution)/shard_map/ppermute | solution.py:28
  101.3 1.8 collective-permute-start.14
  103.1 1.2 collective-permute-start.13
  104.3 1.5 collective-permute-start.12
  105.8 2.1 collective-permute-done.14.refs_3_
  107.9 3.3 collective-permute-done.13.refs_2_
  111.2 1.7 pack_state.2.refs_0_
  112.9 4.5 %all-to-all-start.1 = ((bf16[16,32,1024]{2,1,0:T(8,128)(2,1)}), bf16[16,32,1024]{2,1,0:T(8,128)(2,1)}, u32[]{:S(2)}, u32[]{:S(2)}) async-start(bf16[16,32,1024]{2,1,0:T(8,128)(2,1)} %pack_state.2.refs_0_), calls=%async_computation.1 | async-start | bytes 2097152 | tf_op jit(solution)/shard_map/all_to_all | solution.py:655
  117.6 1.6 collective-permute-start.15
  119.7 16.0 %collective-permute-done.15.refs_2_.refs_1_ = bf16[4,4,16,640]{3,2,1,0:T(8,128)(2,1)S(1)} collective-permute-done((bf16[4,4,16,640]{3,2,1,0:T(8,128)(2,1)S(1)}, bf16[4,4,16,640]{3,2,1,0:T(8,128)(2,1)S(1)}, u32[]{:S(2)}, u32[]{:S(2)}) %collective-permute-start.15) | collective-permute-done | bytes 327712 | tf_op jit(solution)/shard_map/ppermute | solution.py:28
  135.7 1.6 collective-permute-done.17.refs_4_.refs_3_
  138.1 17.8 %state_step.4 = (bf16[16,256,1024]{2,1,0:T(8,128)(2,1)}, bf16[256,1024]{1,0:T(8,128)(2,1)}) custom-call(s32[1]{0:T(128)} %bitcast.me_ref, bf16[16,32,1024]{2,1,0:T(8,128)(2,1)} %pack_state.2.refs_0_, bf16[4,4,16,640]{3,2,1,0:T(8,128)(2,1)} %copy-done.6, bf16[4,4,16,640]{3,2,1,0:T(8,128)(2,1)} %copy-done.8, bf16[4,4,16,640]{3,2,1,0:T(8,128)(2,1)} %copy-done.10, ...), custom_call_target="tpu_custom_call" | custom-call | flops 1024 | bytes 1024 | tf_op jit(solution)/shard_map/state_step/pallas_call | solution.py:388
  159.9 1.0 copy-done.35
  161.0 2.6 gather_live.1
  166.0 12.8 %state_step.5 = (bf16[16,256,1024]{2,1,0:T(8,128)(2,1)}, bf16[256,1024]{1,0:T(8,128)(2,1)}) custom-call(s32[1]{0:T(128)} %bitcast.me_ref, f32[4,32,1024]{2,1,0:T(8,128)} %copy-done.32, bf16[4,4,16,640]{3,2,1,0:T(8,128)(2,1)} %copy-done.6, bf16[4,4,16,640]{3,2,1,0:T(8,128)(2,1)} %copy-done.8, bf16[4,4,16,640]{3,2,1,0:T(8,128)(2,1)} %copy-done.10, ...), custom_call_target="tpu_custom_call" | custom-call | flops 1024 | bytes 1024 | tf_op jit(solution)/shard_map/state_step/pallas_call | solution.py:388
  178.9 1.0 copy-done.31
  179.9 5.6 %live_steps.1.after_ref.live_ref = bf16[4,32,1024]{2,1,0:T(8,128)(2,1)S(1)} custom-call(s32[2,32]{1,0:T(2,128)S(1)} %pad_add_fusion.slot_ref, bf16[256,1024]{1,0:T(8,128)(2,1)S(1)} %copy-done.31, bf16[16,32,1024]{2,1,0:T(8,128)(2,1)S(1)} %copy-done.25, bf16[16,32,1024]{2,1,0:T(8,128)(2,1)} %all-to-all-done.1.high_ref, f32[4,32,1024]{2,1,0:T(8,128)S(1)} %copy-done.33, ...), custom_call_target="tpu_custom_call" | custom-call | flops 1024 | bytes 1024 | tf_op jit(solution)/shard_map/live_steps/pallas_call | solution.py:47
  186.8 1.0 collective-permute-done.20.other_ref
  188.6 9.8 %out_project.4 = (bf16[128,4096]{1,0:T(8,128)(2,1)}, bf16[128,4096]{1,0:T(8,128)(2,1)}) custom-call(s32[1]{0:T(128)} %bitcast.me_ref, bf16[256,1024]{1,0:T(8,128)(2,1)} %copy-done.17, bf16[256,1024]{1,0:T(8,128)(2,1)} %copy-done.53, bf16[1024,8192]{1,0:T(8,128)(2,1)} %wown_ref.7, bf16[1024,8192]{1,0:T(8,128)(2,1)} %collective-permute-done.19.wother_ref, ...), custom_call_target="tpu_custom_call" | custom-call | flops 1024 | bytes 1024 | tf_op jit(solution)/shard_map/out_project/pallas_call | solution.py:533
  198.4 1.8 collective-permute-start.22
  201.0 9.9 %out_project.5 = (bf16[128,4096]{1,0:T(8,128)(2,1)}, bf16[128,4096]{1,0:T(8,128)(2,1)}) custom-call(s32[1]{0:T(128)} %bitcast.me_ref, bf16[256,1024]{1,0:T(8,128)(2,1)} %copy-done.14, bf16[256,1024]{1,0:T(8,128)(2,1)} %copy-done.52, bf16[1024,8192]{1,0:T(8,128)(2,1)} %wown_ref.7, bf16[1024,8192]{1,0:T(8,128)(2,1)} %collective-permute-done.19.wother_ref, ...), custom_call_target="tpu_custom_call" | custom-call | flops 1024 | bytes 1024 | tf_op jit(solution)/shard_map/out_project/pallas_call | solution.py:533
  210.9 12.8 %state_step.6 = (bf16[16,256,1024]{2,1,0:T(8,128)(2,1)}, bf16[256,1024]{1,0:T(8,128)(2,1)}) custom-call(s32[1]{0:T(128)} %bitcast.me_ref, bf16[128,4096]{1,0:T(8,128)(2,1)} %get-tuple-element.89.refs_0_, bf16[4,4,16,640]{3,2,1,0:T(8,128)(2,1)} %copy-done.6, bf16[4,4,16,640]{3,2,1,0:T(8,128)(2,1)} %copy-done.8, bf16[4,4,16,640]{3,2,1,0:T(8,128)(2,1)} %copy-done.10, ...), custom_call_target="tpu_custom_call" | custom-call | flops 1024 | bytes 1024 | tf_op jit(solution)/shard_map/state_step/pallas_call | solution.py:388
  223.7 1.0 copy-done.34
  226.5 1.9 collective-permute-start.24
  229.2 9.8 %out_project.6 = (bf16[128,4096]{1,0:T(8,128)(2,1)}, bf16[128,4096]{1,0:T(8,128)(2,1)}) custom-call(s32[1]{0:T(128)} %bitcast.me_ref, bf16[256,1024]{1,0:T(8,128)(2,1)} %copy-done.16, bf16[256,1024]{1,0:T(8,128)(2,1)} %copy-done.50, bf16[1024,8192]{1,0:T(8,128)(2,1)} %wown_ref.7, bf16[1024,8192]{1,0:T(8,128)(2,1)} %collective-permute-done.19.wother_ref, ...), custom_call_target="tpu_custom_call" | custom-call | flops 1024 | bytes 1024 | tf_op jit(solution)/shard_map/out_project/pallas_call | solution.py:533
  239.1 11.0 %state_step.7.after_ref.gated_ref = bf16[256,1024]{1,0:T(8,128)(2,1)} custom-call(s32[1]{0:T(128)} %bitcast.me_ref, bf16[128,4096]{1,0:T(8,128)(2,1)} %get-tuple-element.94.refs_0_, bf16[4,4,16,640]{3,2,1,0:T(8,128)(2,1)} %copy-done.6, bf16[4,4,16,640]{3,2,1,0:T(8,128)(2,1)} %copy-done.8, bf16[4,4,16,640]{3,2,1,0:T(8,128)(2,1)} %copy-done.10, ...), custom_call_target="tpu_custom_call" | custom-call | flops 1024 | bytes 1024 | tf_op jit(solution)/shard_map/state_step/pallas_call | solution.py:388
  250.1 1.0 copy-done.18
  254.3 9.9 %out_project.7 = (bf16[128,4096]{1,0:T(8,128)(2,1)}, bf16[128,4096]{1,0:T(8,128)(2,1)}) custom-call(s32[1]{0:T(128)} %bitcast.me_ref, bf16[256,1024]{1,0:T(8,128)(2,1)} %copy-done.15, bf16[256,1024]{1,0:T(8,128)(2,1)} %copy-done.51, bf16[1024,8192]{1,0:T(8,128)(2,1)} %wown_ref.7, bf16[1024,8192]{1,0:T(8,128)(2,1)} %collective-permute-done.19.wother_ref, ...), custom_call_target="tpu_custom_call" | custom-call | flops 1024 | bytes 1024 | tf_op jit(solution)/shard_map/out_project/pallas_call | solution.py:533
  264.2 1.9 collective-permute-start.30
  266.2 7.4 %collective-permute-done.26 = bf16[128,4096]{1,0:T(8,128)(2,1)S(1)} collective-permute-done((bf16[128,4096]{1,0:T(8,128)(2,1)}, bf16[128,4096]{1,0:T(8,128)(2,1)S(1)}, u32[]{:S(2)}, u32[]{:S(2)}) %collective-permute-start.26) | collective-permute-done | bytes 1048608 | tf_op jit(solution)/shard_map/ppermute | solution.py:28
  273.7 1.2 copy-done.22
  275.4 3.4 %collective-permute-start.28 = (bf16[1,32,4096]{2,1,0:T(8,128)(2,1)S(1)}, bf16[1,32,4096]{2,1,0:T(8,128)(2,1)S(1)}, u32[]{:S(2)}, u32[]{:S(2)}) collective-permute-start(bf16[1,32,4096]{2,1,0:T(8,128)(2,1)S(1)} %get-tuple-element.105), channel_id=1, source_target_pairs={{0,8},{1,9},{2,10},{3,11},{4,12},{5,13},{6,14},{7,15},{8,0},{9,1},... | collective-permute-start | bytes 786440 | tf_op jit(solution)/shard_map/ppermute | solution.py:28
  278.8 7.8 %collective-permute-done.27.got_ref = bf16[2,32,4096]{2,1,0:T(8,128)(2,1)S(1)} collective-permute-done((bf16[2,32,4096]{2,1,0:T(8,128)(2,1)S(1)}, bf16[2,32,4096]{2,1,0:T(8,128)(2,1)S(1)}, u32[]{:S(2)}, u32[]{:S(2)}) %collective-permute-start.27) | collective-permute-done | bytes 524320 | tf_op jit(solution)/shard_map/ppermute | solution.py:28
  286.7 7.8 %collective-permute-done.28.got_ref = bf16[1,32,4096]{2,1,0:T(8,128)(2,1)S(1)} collective-permute-done((bf16[1,32,4096]{2,1,0:T(8,128)(2,1)S(1)}, bf16[1,32,4096]{2,1,0:T(8,128)(2,1)S(1)}, u32[]{:S(2)}, u32[]{:S(2)}) %collective-permute-start.28) | collective-permute-done | bytes 262176 | tf_op jit(solution)/shard_map/ppermute | solution.py:28
  294.5 2.1 collective-permute-done.29.got_ref
  296.8 1.2 copy-done.23
  298.3 3.6 %collective-permute-start.33 = (bf16[2,32,4096]{2,1,0:T(8,128)(2,1)S(1)}, bf16[2,32,4096]{2,1,0:T(8,128)(2,1)S(1)}, u32[]{:S(2)}, u32[]{:S(2)}) collective-permute-start(bf16[2,32,4096]{2,1,0:T(8,128)(2,1)S(1)} %get-tuple-element.115), channel_id=1, source_target_pairs={{0,4},{1,5},{2,6},{3,7},{4,0},{5,1},{6,2},{7,3},{8,12},{9,13},{10,... | collective-permute-start | bytes 1572872 | tf_op jit(solution)/shard_map/ppermute | solution.py:28
  302.0 2.8 collective-permute-start.32
  304.8 15.1 %collective-permute-done.31.got_ref = bf16[1,32,4096]{2,1,0:T(8,128)(2,1)S(1)} collective-permute-done((bf16[1,32,4096]{2,1,0:T(8,128)(2,1)S(1)}, bf16[1,32,4096]{2,1,0:T(8,128)(2,1)S(1)}, u32[]{:S(2)}, u32[]{:S(2)}) %collective-permute-start.31) | collective-permute-done | bytes 262176 | tf_op jit(solution)/shard_map/ppermute | solution.py:28
  319.9 6.6 %collective-permute-done.32.got_ref = bf16[1,32,4096]{2,1,0:T(8,128)(2,1)S(1)} collective-permute-done((bf16[1,32,4096]{2,1,0:T(8,128)(2,1)S(1)}, bf16[1,32,4096]{2,1,0:T(8,128)(2,1)S(1)}, u32[]{:S(2)}, u32[]{:S(2)}) %collective-permute-start.32) | collective-permute-done | bytes 262176 | tf_op jit(solution)/shard_map/ppermute | solution.py:28
  327.6 10.2 %collective-permute-done.34.got_ref = bf16[1,32,4096]{2,1,0:T(8,128)(2,1)S(1)} collective-permute-done((bf16[1,32,4096]{2,1,0:T(8,128)(2,1)S(1)}, bf16[1,32,4096]{2,1,0:T(8,128)(2,1)S(1)}, u32[]{:S(2)}, u32[]{:S(2)}) %collective-permute-start.34) | collective-permute-done | bytes 262176 | tf_op jit(solution)/shard_map/ppermute | solution.py:28
  338.0 1.3 collective-permute-done.38.refs_7_
  339.3 2.2 final_join.1
  (189 shorter events, 21.4 us)
Async XLA Ops:
  0.0 36.0 %copy-start.56 = (s32[64]{0:T(128)S(1)}, s32[64]{0:T(128)}, u32[]{:S(2)}) copy-start(s32[64]{0:T(128)} %param.22) | copy-start | bytes 772
  0.0 36.0 %copy-start.55 = (s32[16]{0:T(128)S(1)}, s32[16]{0:T(128)}, u32[]{:S(2)}) copy-start(s32[16]{0:T(128)} %param.21) | copy-start | bytes 196
  0.0 69.3 %copy-start.48 = (f32[1024]{0:T(1024)S(1)}, f32[1024]{0:T(1024)}, u32[]{:S(2)}) copy-start(f32[1024]{0:T(1024)} %param.26) | copy-start | bytes 12292
  0.0 187.8 %collective-permute-start.19 = (bf16[1024,8192]{1,0:T(8,128)(2,1)}, bf16[1024,8192]{1,0:T(8,128)(2,1)}, u32[]{:S(2)}, u32[]{:S(2)}) collective-permute-start(bf16[1024,8192]{1,0:T(8,128)(2,1)} %wown_ref.7), channel_id=1, source_target_pairs={{0,1},{1,0},{2,3},{3,2},{4,5},{5,4},{6,7},{7,6},{8,9},{9,8},{10,11... | collective-permute-start | bytes 50331656 | tf_op jit(solution)/shard_map/ppermute | solution.py:28
  1.7 67.6 %copy-start.47 = (f32[4,1024]{1,0:T(4,128)S(1)}, f32[4,1024]{1,0:T(4,128)}, u32[]{:S(2)}) copy-start(f32[4,1024]{1,0:T(4,128)} %w_ref.1) | copy-start | bytes 49156
  1.7 17.5 %collective-permute-start.2 = (bf16[4,16,768]{2,1,0:T(8,128)(2,1)S(1)}, bf16[4,16,768]{2,1,0:T(8,128)(2,1)S(1)}, u32[]{:S(2)}, u32[]{:S(2)}) collective-permute-start(bf16[4,16,768]{2,1,0:T(8,128)(2,1)S(1)} %get-tuple-element.67), channel_id=1, source_target_pairs={{0,1},{1,0},{2,3},{3,2},{4,5},{5,4},{6,7},{7,6},{8,9},{9,8},{10,11... | collective-permute-start | bytes 294920 | tf_op jit(solution)/shard_map/ppermute | solution.py:28
  1.8 20.1 %collective-permute-start = (bf16[4,16,768]{2,1,0:T(8,128)(2,1)S(1)}, bf16[4,16,768]{2,1,0:T(8,128)(2,1)S(1)}, u32[]{:S(2)}, u32[]{:S(2)}) collective-permute-start(bf16[4,16,768]{2,1,0:T(8,128)(2,1)S(1)} %get-tuple-element.65), channel_id=1, source_target_pairs={{0,2},{1,3},{2,0},{3,1},{4,6},{5,7},{6,4},{7,5},{8,10},{9,11},{10,... | collective-permute-start | bytes 294920 | tf_op jit(solution)/shard_map/ppermute | solution.py:28
  4.8 17.1 %collective-permute-start.1 = (bf16[4,16,768]{2,1,0:T(8,128)(2,1)S(1)}, bf16[4,16,768]{2,1,0:T(8,128)(2,1)S(1)}, u32[]{:S(2)}, u32[]{:S(2)}) collective-permute-start(bf16[4,16,768]{2,1,0:T(8,128)(2,1)S(1)} %get-tuple-element.66), channel_id=1, source_target_pairs={{0,1},{1,0},{2,3},{3,2},{4,5},{5,4},{6,7},{7,6},{8,9},{9,8},{10,11... | collective-permute-start | bytes 294920 | tf_op jit(solution)/shard_map/ppermute | solution.py:28
  19.3 6.0 %collective-permute-start.3 = (bf16[4,16,768]{2,1,0:T(8,128)(2,1)S(1)}, bf16[4,16,768]{2,1,0:T(8,128)(2,1)S(1)}, u32[]{:S(2)}, u32[]{:S(2)}) collective-permute-start(bf16[4,16,768]{2,1,0:T(8,128)(2,1)S(1)} %collective-permute-done.2), channel_id=1, source_target_pairs={{0,2},{1,3},{2,0},{3,1},{4,6},{5,7},{6,4},{7,5},{8,10},{9,11},{10,... | collective-permute-start | bytes 294920 | tf_op jit(solution)/shard_map/ppermute | solution.py:28
  25.2 69.9 %copy-start.54 = (f32[544]{0:T(1024)S(1)}, f32[544]{0:T(1024)}, u32[]{:S(2)}) copy-start(f32[544]{0:T(1024)} %param.28) | copy-start | bytes 6532
  28.1 41.2 %copy-start.37 = (bf16[4,256,1024]{2,1,0:T(8,128)(2,1)S(1)}, bf16[4,256,1024]{2,1,0:T(8,128)(2,1)}, u32[]{:S(2)}) copy-start(bf16[4,256,1024]{2,1,0:T(8,128)(2,1)} %x_ref.3) | copy-start | bytes 6291460
  29.8 83.1 %all-to-all-start = ((bf16[16,32,1024]{2,1,0:T(8,128)(2,1)}), bf16[16,32,1024]{2,1,0:T(8,128)(2,1)S(1)}, u32[]{:S(2)}, u32[]{:S(2)}) async-start(bf16[16,32,1024]{2,1,0:T(8,128)(2,1)} %pack_state.3), calls=%async_computation | async-start | bytes 2097152 | tf_op jit(solution)/shard_map/all_to_all | solution.py:627
  36.5 74.7 %copy-start.5 = (f32[4,16,16384]{2,1,0:T(8,128)S(1)}, f32[4,16,16384]{2,1,0:T(8,128)}, u32[]{:S(2)}) copy-start(f32[4,16,16384]{2,1,0:T(8,128)} %x_ref.5) | copy-start | bytes 12582916
  36.5 19.9 %collective-permute-start.4 = (bf16[4,16,768]{2,1,0:T(8,128)(2,1)}, bf16[4,16,768]{2,1,0:T(8,128)(2,1)S(1)}, u32[]{:S(2)}, u32[]{:S(2)}) collective-permute-start(bf16[4,16,768]{2,1,0:T(8,128)(2,1)} %copy-done.49), channel_id=1, source_target_pairs={{0,4},{1,5},{2,6},{3,7},{4,0},{5,1},{6,2},{7,3},{8,12},{9,13},{10,... | collective-permute-start | bytes 294920 | tf_op jit(solution)/shard_map/ppermute | solution.py:28
  38.5 30.8 %collective-permute-start.5 = (bf16[4,16,768]{2,1,0:T(8,128)(2,1)S(1)}, bf16[4,16,768]{2,1,0:T(8,128)(2,1)S(1)}, u32[]{:S(2)}, u32[]{:S(2)}) collective-permute-start(bf16[4,16,768]{2,1,0:T(8,128)(2,1)S(1)} %get-tuple-element.70), channel_id=1, source_target_pairs={{0,8},{1,9},{2,10},{3,11},{4,12},{5,13},{6,14},{7,15},{8,0},{9,1},... | collective-permute-start | bytes 294920 | tf_op jit(solution)/shard_map/ppermute | solution.py:28
  40.9 28.4 %collective-permute-start.6 = (bf16[4,16,768]{2,1,0:T(8,128)(2,1)S(1)}, bf16[4,16,768]{2,1,0:T(8,128)(2,1)S(1)}, u32[]{:S(2)}, u32[]{:S(2)}) collective-permute-start(bf16[4,16,768]{2,1,0:T(8,128)(2,1)S(1)} %get-tuple-element.71), channel_id=1, source_target_pairs={{0,12},{1,13},{2,14},{3,15},{4,8},{5,9},{6,10},{7,11},{8,4},{9,5},... | collective-permute-start | bytes 294920 | tf_op jit(solution)/shard_map/ppermute | solution.py:28
  78.3 2.1 collective-permute-start.7
  80.6 9.8 %collective-permute-start.8 = (bf16[4,4,16,640]{3,2,1,0:T(8,128)(2,1)S(1)}, bf16[4,4,16,640]{3,2,1,0:T(8,128)(2,1)S(1)}, u32[]{:S(2)}, u32[]{:S(2)}) collective-permute-start(bf16[4,4,16,640]{3,2,1,0:T(8,128)(2,1)S(1)} %get-tuple-element.75), channel_id=1, source_target_pairs={{0,2},{1,3},{2,0},{3,1},{4,6},{5,7},{6,4},{7,5},{8,10},{9,11},{10,... | collective-permute-start | bytes 983048 | tf_op jit(solution)/shard_map/ppermute | solution.py:28
  90.5 4.9 %collective-permute-start.9 = (bf16[4,16,640]{2,1,0:T(8,128)(2,1)S(1)}, bf16[4,16,640]{2,1,0:T(8,128)(2,1)S(1)}, u32[]{:S(2)}, u32[]{:S(2)}) collective-permute-start(bf16[4,16,640]{2,1,0:T(8,128)(2,1)S(1)} %get-tuple-element.77), channel_id=1, source_target_pairs={{0,4},{1,5},{2,6},{3,7},{4,0},{5,1},{6,2},{7,3},{8,12},{9,13},{10,... | collective-permute-start | bytes 245768 | tf_op jit(solution)/shard_map/ppermute | solution.py:28
  92.7 8.4 %collective-permute-start.10 = (bf16[4,16,640]{2,1,0:T(8,128)(2,1)S(1)}, bf16[4,16,640]{2,1,0:T(8,128)(2,1)S(1)}, u32[]{:S(2)}, u32[]{:S(2)}) collective-permute-start(bf16[4,16,640]{2,1,0:T(8,128)(2,1)S(1)} %get-tuple-element.78), channel_id=1, source_target_pairs={{0,8},{1,9},{2,10},{3,11},{4,12},{5,13},{6,14},{7,15},{8,0},{9,1},... | collective-permute-start | bytes 245768 | tf_op jit(solution)/shard_map/ppermute | solution.py:28
  92.8 8.4 %collective-permute-start.11 = (bf16[4,16,640]{2,1,0:T(8,128)(2,1)S(1)}, bf16[4,16,640]{2,1,0:T(8,128)(2,1)S(1)}, u32[]{:S(2)}, u32[]{:S(2)}) collective-permute-start(bf16[4,16,640]{2,1,0:T(8,128)(2,1)S(1)} %get-tuple-element.79), channel_id=1, source_target_pairs={{0,12},{1,13},{2,14},{3,15},{4,8},{5,9},{6,10},{7,11},{8,4},{9,5},... | collective-permute-start | bytes 245768 | tf_op jit(solution)/shard_map/ppermute | solution.py:28
  101.3 6.5 %collective-permute-start.14 = (bf16[4,16,640]{2,1,0:T(8,128)(2,1)S(1)}, bf16[4,16,640]{2,1,0:T(8,128)(2,1)S(1)}, u32[]{:S(2)}, u32[]{:S(2)}) collective-permute-start(bf16[4,16,640]{2,1,0:T(8,128)(2,1)S(1)} %norm.1.refs_0_), channel_id=1, source_target_pairs={{0,12},{1,13},{2,14},{3,15},{4,8},{5,9},{6,10},{7,11},{8,4},{9,5},... | collective-permute-start | bytes 245768 | tf_op jit(solution)/shard_map/ppermute | solution.py:28
  103.1 8.1 %collective-permute-start.13 = (bf16[4,16,640]{2,1,0:T(8,128)(2,1)S(1)}, bf16[4,16,640]{2,1,0:T(8,128)(2,1)S(1)}, u32[]{:S(2)}, u32[]{:S(2)}) collective-permute-start(bf16[4,16,640]{2,1,0:T(8,128)(2,1)S(1)} %norm.1.refs_0_), channel_id=1, source_target_pairs={{0,8},{1,9},{2,10},{3,11},{4,12},{5,13},{6,14},{7,15},{8,0},{9,1},... | collective-permute-start | bytes 245768 | tf_op jit(solution)/shard_map/ppermute | solution.py:28
  104.3 6.9 %collective-permute-start.12 = (bf16[4,16,640]{2,1,0:T(8,128)(2,1)S(1)}, bf16[4,16,640]{2,1,0:T(8,128)(2,1)S(1)}, u32[]{:S(2)}, u32[]{:S(2)}) collective-permute-start(bf16[4,16,640]{2,1,0:T(8,128)(2,1)S(1)} %norm.1.refs_0_), channel_id=1, source_target_pairs={{0,4},{1,5},{2,6},{3,7},{4,0},{5,1},{6,2},{7,3},{8,12},{9,13},{10,... | collective-permute-start | bytes 245768 | tf_op jit(solution)/shard_map/ppermute | solution.py:28
  111.2 26.8 %copy-start.6 = (bf16[4,4,16,640]{3,2,1,0:T(8,128)(2,1)}, bf16[4,4,16,640]{3,2,1,0:T(8,128)(2,1)S(1)}, u32[]{:S(2)}) copy-start(bf16[4,4,16,640]{3,2,1,0:T(8,128)(2,1)S(1)} %merge_z.1.after_ref.refs_1_.refs_0_) | copy-start | bytes 983044
  112.9 65.9 %all-to-all-start.1 = ((bf16[16,32,1024]{2,1,0:T(8,128)(2,1)}), bf16[16,32,1024]{2,1,0:T(8,128)(2,1)}, u32[]{:S(2)}, u32[]{:S(2)}) async-start(bf16[16,32,1024]{2,1,0:T(8,128)(2,1)} %pack_state.2.refs_0_), calls=%async_computation.1 | async-start | bytes 2097152 | tf_op jit(solution)/shard_map/all_to_all | solution.py:655
  117.6 18.0 %collective-permute-start.15 = (bf16[4,4,16,640]{3,2,1,0:T(8,128)(2,1)S(1)}, bf16[4,4,16,640]{3,2,1,0:T(8,128)(2,1)S(1)}, u32[]{:S(2)}, u32[]{:S(2)}) collective-permute-start(bf16[4,4,16,640]{3,2,1,0:T(8,128)(2,1)S(1)} %merge_z.1.after_ref.refs_1_.refs_0_), channel_id=1, source_target_pairs={{0,2},{1,3},{2,0},{3,1},{4,6},{5,7},{6,4},{7,5},{8,10},{9,11},{10,... | collective-permute-start | bytes 983048 | tf_op jit(solution)/shard_map/ppermute | solution.py:28
  119.6 16.1 %collective-permute-start.16 = (bf16[4,4,16,640]{3,2,1,0:T(8,128)(2,1)S(1)}, bf16[4,4,16,640]{3,2,1,0:T(8,128)(2,1)S(1)}, u32[]{:S(2)}, u32[]{:S(2)}) collective-permute-start(bf16[4,4,16,640]{3,2,1,0:T(8,128)(2,1)S(1)} %merge_z.1.after_ref.refs_1_.refs_0_), channel_id=1, source_target_pairs={{0,1},{1,0},{2,3},{3,2},{4,5},{5,4},{6,7},{7,6},{8,9},{9,8},{10,11... | collective-permute-start | bytes 983048 | tf_op jit(solution)/shard_map/ppermute | solution.py:28
  135.7 1.6 collective-permute-start.17
  138.0 18.0 %copy-start.1 = (f32[4,256,1024]{2,1,0:T(8,128)S(1)}, f32[4,256,1024]{2,1,0:T(8,128)}, u32[]{:S(2)}) copy-start(f32[4,256,1024]{2,1,0:T(8,128)} %copy-done) | copy-start | bytes 12582916
  138.1 18.0 %copy-start.2 = (bf16[4,256,1024]{2,1,0:T(8,128)(2,1)S(1)}, bf16[4,256,1024]{2,1,0:T(8,128)(2,1)}, u32[]{:S(2)}) copy-start(bf16[4,256,1024]{2,1,0:T(8,128)(2,1)} %refs_6_.9) | copy-start | bytes 6291460
  138.1 18.0 %copy-start.3 = (bf16[512,1024]{1,0:T(8,128)(2,1)S(1)}, bf16[512,1024]{1,0:T(8,128)(2,1)}, u32[]{:S(2)}) copy-start(bf16[512,1024]{1,0:T(8,128)(2,1)} %refs_7_.7) | copy-start | bytes 3145732
  138.1 17.9 %copy-start.45 = (f32[1024]{0:T(1024)S(1)}, f32[1024]{0:T(1024)}, u32[]{:S(2)}) copy-start(f32[1024]{0:T(1024)} %param.30) | copy-start | bytes 12292
  165.9 12.9 %copy-start.25 = (bf16[16,32,1024]{2,1,0:T(8,128)(2,1)S(1)}, bf16[16,32,1024]{2,1,0:T(8,128)(2,1)}, u32[]{:S(2)}) copy-start(bf16[16,32,1024]{2,1,0:T(8,128)(2,1)} %copy-done.24) | copy-start | bytes 3145732
  165.9 12.9 %copy-start.33 = (f32[4,32,1024]{2,1,0:T(8,128)S(1)}, f32[4,32,1024]{2,1,0:T(8,128)}, u32[]{:S(2)}) copy-start(f32[4,32,1024]{2,1,0:T(8,128)} %copy-done.32) | copy-start | bytes 1572868
  165.9 12.9 %copy-start.38 = (f32[16,1024]{1,0:T(8,128)S(1)}, f32[16,1024]{1,0:T(8,128)}, u32[]{:S(2)}) copy-start(f32[16,1024]{1,0:T(8,128)} %refs_9_.7) | copy-start | bytes 196612
  165.9 12.9 %copy-start.42 = (f32[4,32,1024]{2,1,0:T(8,128)S(1)}, f32[4,32,1024]{2,1,0:T(8,128)}, u32[]{:S(2)}) copy-start(f32[4,32,1024]{2,1,0:T(8,128)} %copy-done.41) | copy-start | bytes 1572868
  165.9 12.9 %copy-start.44 = (f32[4,32,1024]{2,1,0:T(8,128)S(1)}, f32[4,32,1024]{2,1,0:T(8,128)}, u32[]{:S(2)}) copy-start(f32[4,32,1024]{2,1,0:T(8,128)} %copy-done.43) | copy-start | bytes 1572868
  165.9 12.9 %copy-start.46 = (f32[1024]{0:T(1024)S(1)}, f32[1024]{0:T(1024)}, u32[]{:S(2)}) copy-start(f32[1024]{0:T(1024)} %param.32) | copy-start | bytes 12292
  166.0 19.6 %copy-start.36 = (bf16[256,1024]{1,0:T(8,128)(2,1)S(1)}, bf16[256,1024]{1,0:T(8,128)(2,1)}, u32[]{:S(2)}) copy-start(bf16[256,1024]{1,0:T(8,128)(2,1)} %get-tuple-element.81.after_ref.gated_ref) | copy-start | bytes 1572868
  185.8 2.0 collective-permute-start.20
  186.4 13.9 %collective-permute-start.18 = (bf16[256,1024]{1,0:T(8,128)(2,1)S(1)}, bf16[256,1024]{1,0:T(8,128)(2,1)S(1)}, u32[]{:S(2)}, u32[]{:S(2)}) collective-permute-start(bf16[256,1024]{1,0:T(8,128)(2,1)S(1)} %fix.5.refs_0_.own_ref), channel_id=1, source_target_pairs={{0,1},{1,0},{2,3},{3,2},{4,5},{5,4},{6,7},{7,6},{8,9},{9,8},{10,11... | collective-permute-start | bytes 1572872 | tf_op jit(solution)/shard_map/ppermute | solution.py:28
  198.4 27.0 %collective-permute-start.22 = (bf16[128,4096]{1,0:T(8,128)(2,1)}, bf16[128,4096]{1,0:T(8,128)(2,1)S(1)}, u32[]{:S(2)}, u32[]{:S(2)}) collective-permute-start(bf16[128,4096]{1,0:T(8,128)(2,1)} %get-tuple-element.92), channel_id=1, source_target_pairs={{0,2},{1,3},{2,0},{3,1},{4,6},{5,7},{6,4},{7,5},{8,10},{9,11},{10,... | collective-permute-start | bytes 3145736 | tf_op jit(solution)/shard_map/ppermute | solution.py:28
  210.9 14.3 %copy-start.57 = (bf16[128,4096]{1,0:T(8,128)(2,1)S(1)}, bf16[128,4096]{1,0:T(8,128)(2,1)}, u32[]{:S(2)}) copy-start(bf16[128,4096]{1,0:T(8,128)(2,1)} %get-tuple-element.98) | copy-start | bytes 3145732
  210.9 14.6 %copy-start.21 = (bf16[128,4096]{1,0:T(8,128)(2,1)S(1)}, bf16[128,4096]{1,0:T(8,128)(2,1)}, u32[]{:S(2)}) copy-start(bf16[128,4096]{1,0:T(8,128)(2,1)} %get-tuple-element.88.refs_0_) | copy-start | bytes 3145732
  225.1 3.3 collective-permute-start.21
  225.2 26.5 %collective-permute-start.25 = (bf16[128,4096]{1,0:T(8,128)(2,1)S(1)}, bf16[128,4096]{1,0:T(8,128)(2,1)S(1)}, u32[]{:S(2)}, u32[]{:S(2)}) collective-permute-start(bf16[128,4096]{1,0:T(8,128)(2,1)S(1)} %copy-done.57), channel_id=1, source_target_pairs={{0,2},{1,3},{2,0},{3,1},{4,6},{5,7},{6,4},{7,5},{8,10},{9,11},{10,... | collective-permute-start | bytes 3145736 | tf_op jit(solution)/shard_map/ppermute | solution.py:28
  226.5 25.0 %collective-permute-start.24 = (bf16[2,32,4096]{2,1,0:T(8,128)(2,1)S(1)}, bf16[2,32,4096]{2,1,0:T(8,128)(2,1)S(1)}, u32[]{:S(2)}, u32[]{:S(2)}) collective-permute-start(bf16[2,32,4096]{2,1,0:T(8,128)(2,1)S(1)} %get-tuple-element.96), channel_id=1, source_target_pairs={{0,4},{1,5},{2,6},{3,7},{4,0},{5,1},{6,2},{7,3},{8,12},{9,13},{10,... | collective-permute-start | bytes 1572872 | tf_op jit(solution)/shard_map/ppermute | solution.py:28
  239.0 34.7 %collective-permute-start.26 = (bf16[128,4096]{1,0:T(8,128)(2,1)}, bf16[128,4096]{1,0:T(8,128)(2,1)S(1)}, u32[]{:S(2)}, u32[]{:S(2)}) collective-permute-start(bf16[128,4096]{1,0:T(8,128)(2,1)} %get-tuple-element.101), channel_id=1, source_target_pairs={{0,2},{1,3},{2,0},{3,1},{4,6},{5,7},{6,4},{7,5},{8,10},{9,11},{10,... | collective-permute-start | bytes 3145736 | tf_op jit(solution)/shard_map/ppermute | solution.py:28
  251.5 2.0 collective-permute-start.23
  254.3 19.4 %copy-start.20 = (bf16[128,4096]{1,0:T(8,128)(2,1)S(1)}, bf16[128,4096]{1,0:T(8,128)(2,1)}, u32[]{:S(2)}) copy-start(bf16[128,4096]{1,0:T(8,128)(2,1)} %get-tuple-element.94.refs_0_) | copy-start | bytes 3145732
  254.3 32.3 %copy-start.28 = (bf16[2,32,4096]{2,1,0:T(8,128)(2,1)S(1)}, bf16[2,32,4096]{2,1,0:T(8,128)(2,1)}, u32[]{:S(2)}) copy-start(bf16[2,32,4096]{2,1,0:T(8,128)(2,1)} %copy-done.27) | copy-start | bytes 1572868
  264.2 32.6 %collective-permute-start.30 = (bf16[128,4096]{1,0:T(8,128)(2,1)}, bf16[128,4096]{1,0:T(8,128)(2,1)S(1)}, u32[]{:S(2)}, u32[]{:S(2)}) collective-permute-start(bf16[128,4096]{1,0:T(8,128)(2,1)} %get-tuple-element.109), channel_id=1, source_target_pairs={{0,2},{1,3},{2,0},{3,1},{4,6},{5,7},{6,4},{7,5},{8,10},{9,11},{10,... | collective-permute-start | bytes 3145736 | tf_op jit(solution)/shard_map/ppermute | solution.py:28
  266.1 20.4 %collective-permute-start.27 = (bf16[2,32,4096]{2,1,0:T(8,128)(2,1)S(1)}, bf16[2,32,4096]{2,1,0:T(8,128)(2,1)S(1)}, u32[]{:S(2)}, u32[]{:S(2)}) collective-permute-start(bf16[2,32,4096]{2,1,0:T(8,128)(2,1)S(1)} %get-tuple-element.103), channel_id=1, source_target_pairs={{0,4},{1,5},{2,6},{3,7},{4,0},{5,1},{6,2},{7,3},{8,12},{9,13},{10,... | collective-permute-start | bytes 1572872 | tf_op jit(solution)/shard_map/ppermute | solution.py:28
  275.1 21.5 %collective-permute-start.29 = (bf16[2,32,4096]{2,1,0:T(8,128)(2,1)S(1)}, bf16[2,32,4096]{2,1,0:T(8,128)(2,1)S(1)}, u32[]{:S(2)}, u32[]{:S(2)}) collective-permute-start(bf16[2,32,4096]{2,1,0:T(8,128)(2,1)S(1)} %get-tuple-element.107), channel_id=1, source_target_pairs={{0,4},{1,5},{2,6},{3,7},{4,0},{5,1},{6,2},{7,3},{8,12},{9,13},{10,... | collective-permute-start | bytes 1572872 | tf_op jit(solution)/shard_map/ppermute | solution.py:28
  275.4 19.1 %collective-permute-start.28 = (bf16[1,32,4096]{2,1,0:T(8,128)(2,1)S(1)}, bf16[1,32,4096]{2,1,0:T(8,128)(2,1)S(1)}, u32[]{:S(2)}, u32[]{:S(2)}) collective-permute-start(bf16[1,32,4096]{2,1,0:T(8,128)(2,1)S(1)} %get-tuple-element.105), channel_id=1, source_target_pairs={{0,8},{1,9},{2,10},{3,11},{4,12},{5,13},{6,14},{7,15},{8,0},{9,1},... | collective-permute-start | bytes 786440 | tf_op jit(solution)/shard_map/ppermute | solution.py:28
  298.3 28.4 %collective-permute-start.33 = (bf16[2,32,4096]{2,1,0:T(8,128)(2,1)S(1)}, bf16[2,32,4096]{2,1,0:T(8,128)(2,1)S(1)}, u32[]{:S(2)}, u32[]{:S(2)}) collective-permute-start(bf16[2,32,4096]{2,1,0:T(8,128)(2,1)S(1)} %get-tuple-element.115), channel_id=1, source_target_pairs={{0,4},{1,5},{2,6},{3,7},{4,0},{5,1},{6,2},{7,3},{8,12},{9,13},{10,... | collective-permute-start | bytes 1572872 | tf_op jit(solution)/shard_map/ppermute | solution.py:28
  301.9 18.0 %collective-permute-start.31 = (bf16[1,32,4096]{2,1,0:T(8,128)(2,1)S(1)}, bf16[1,32,4096]{2,1,0:T(8,128)(2,1)S(1)}, u32[]{:S(2)}, u32[]{:S(2)}) collective-permute-start(bf16[1,32,4096]{2,1,0:T(8,128)(2,1)S(1)} %get-tuple-element.111), channel_id=1, source_target_pairs={{0,8},{1,9},{2,10},{3,11},{4,12},{5,13},{6,14},{7,15},{8,0},{9,1},... | collective-permute-start | bytes 786440 | tf_op jit(solution)/shard_map/ppermute | solution.py:28
  302.0 24.5 %collective-permute-start.32 = (bf16[1,32,4096]{2,1,0:T(8,128)(2,1)S(1)}, bf16[1,32,4096]{2,1,0:T(8,128)(2,1)S(1)}, u32[]{:S(2)}, u32[]{:S(2)}) collective-permute-start(bf16[1,32,4096]{2,1,0:T(8,128)(2,1)S(1)} %get-tuple-element.113), channel_id=1, source_target_pairs={{0,8},{1,9},{2,10},{3,11},{4,12},{5,13},{6,14},{7,15},{8,0},{9,1},... | collective-permute-start | bytes 786440 | tf_op jit(solution)/shard_map/ppermute | solution.py:28
  326.8 11.0 %collective-permute-start.34 = (bf16[1,32,4096]{2,1,0:T(8,128)(2,1)S(1)}, bf16[1,32,4096]{2,1,0:T(8,128)(2,1)S(1)}, u32[]{:S(2)}, u32[]{:S(2)}) collective-permute-start(bf16[1,32,4096]{2,1,0:T(8,128)(2,1)S(1)} %get-tuple-element.117), channel_id=1, source_target_pairs={{0,8},{1,9},{2,10},{3,11},{4,12},{5,13},{6,14},{7,15},{8,0},{9,1},... | collective-permute-start | bytes 786440 | tf_op jit(solution)/shard_map/ppermute | solution.py:28
  327.1 10.9 %collective-permute-start.35 = (bf16[16,4096]{1,0:T(8,128)(2,1)S(1)}, bf16[16,4096]{1,0:T(8,128)(2,1)S(1)}, u32[]{:S(2)}, u32[]{:S(2)}) collective-permute-start(bf16[16,4096]{1,0:T(8,128)(2,1)S(1)} %get-tuple-element.119), channel_id=1, source_target_pairs={{0,1},{1,0},{2,3},{3,2},{4,5},{5,4},{6,7},{7,6},{8,9},{9,8},{10,11... | collective-permute-start | bytes 393224 | tf_op jit(solution)/shard_map/ppermute | solution.py:28
  327.1 10.9 %collective-permute-start.36 = (bf16[16,4096]{1,0:T(8,128)(2,1)S(1)}, bf16[16,4096]{1,0:T(8,128)(2,1)S(1)}, u32[]{:S(2)}, u32[]{:S(2)}) collective-permute-start(bf16[16,4096]{1,0:T(8,128)(2,1)S(1)} %get-tuple-element.120), channel_id=1, source_target_pairs={{0,1},{1,0},{2,3},{3,2},{4,5},{5,4},{6,7},{7,6},{8,9},{9,8},{10,11... | collective-permute-start | bytes 393224 | tf_op jit(solution)/shard_map/ppermute | solution.py:28
  327.6 10.4 %collective-permute-start.37 = (bf16[16,4096]{1,0:T(8,128)(2,1)S(1)}, bf16[16,4096]{1,0:T(8,128)(2,1)S(1)}, u32[]{:S(2)}, u32[]{:S(2)}) collective-permute-start(bf16[16,4096]{1,0:T(8,128)(2,1)S(1)} %get-tuple-element.121), channel_id=1, source_target_pairs={{0,1},{1,0},{2,3},{3,2},{4,5},{5,4},{6,7},{7,6},{8,9},{9,8},{10,11... | collective-permute-start | bytes 393224 | tf_op jit(solution)/shard_map/ppermute | solution.py:28
  337.9 1.4 collective-permute-start.38
  (35 other events, 71.9 us)

commit v6 on v4

--- a/solution.py
+++ b/solution.py
@@ -41,7 +41,7 @@
     return pl.BlockSpec(shape, lambda *_: zeros)
 
 
-def small(kernel, me, args, shapes, name, after=()):
+def small(kernel, me, args, shapes, name, after=(), dtype=BF16, scratch=(), mib=8):
     size = sum(a.size for a in args)
     vmem = pl.BlockSpec(memory_space=pltpu.VMEM)
     return pl.pallas_call(
@@ -50,14 +50,15 @@
         + [pl.BlockSpec(memory_space=pl.ANY)] * len(after)
         + [vmem] * len(args),
         out_specs=[vmem] * len(shapes),
-        out_shape=[jax.ShapeDtypeStruct(s, BF16) for s in shapes],
-        compiler_params=params(8),
+        out_shape=[jax.ShapeDtypeStruct(s, dtype) for s in shapes],
+        scratch_shapes=list(scratch),
+        compiler_params=params(mib),
         cost_estimate=cost(size, 4 * size),
         name=name,
     )(me, *after, *args)
 
 
-def pack_conv_kernel(me_ref, after_ref, x_ref, *o_refs):
+def pack_conv_kernel(me_ref, x_ref, *o_refs):
     zs, _, wide = o_refs[0].shape
     y, core = (me_ref[0] // 2) % 2, me_ref[0] % 2
     c = wide * (TAPS + 1) // TAPS
@@ -79,19 +80,20 @@
             refs[4 + m][at] = refs[i][jnp.bitwise_xor(z, m)]
 
 
-def exchange_conv(prefilled_conv, packed_state, me, n):
+def exchange_conv(prefilled_conv, me, n):
     slots, _, inner = prefilled_conv.shape
     zs = n // 4
     piece = ((TAPS + 1) * slots, inner // n * TAPS // (TAPS + 1))
     conv = jnp.transpose(prefilled_conv, (1, 0, 2))
-    packed = small(pack_conv_kernel, me, [conv], [(zs,) + piece] * 4, "pack_conv", (packed_state,))
+    packed = small(pack_conv_kernel, me, [conv], [(zs,) + piece] * 4, "pack_conv")
     near, far = swap(packed[2], 1, n), swap(packed[3], 1, n)
     got = [packed[0], swap(packed[1], 2, n), near, swap(far, 2, n)]
     cut = small(cut_conv_kernel, me, got, [(4,) + piece] * zs, "cut_conv")
     return [cut[0]] + [swap(cut[m], 4 * m, n) for m in range(1, zs)]
 
 
-def pack_state_kernel(x_ref, o_ref):
+def pack_state_kernel(x_ref, *refs):
+    o_ref = refs[-1]
     slots = x_ref.shape[0]
     some, _, c = o_ref.shape
     for d in range(some):
@@ -99,20 +101,47 @@
             o_ref[d, STATE * k : STATE * (k + 1), :] = x_ref[k, :, d * c : (d + 1) * c].astype(BF16)
 
 
-def pack_state(prefilled_state, n):
+def pack_state(after, prefilled_state, n):
     slots, _, inner = prefilled_state.shape
     c = inner // n
     some = 4
     return pl.pallas_call(
         pack_state_kernel,
         grid=(n // some,),
-        in_specs=[pl.BlockSpec((slots, STATE, some * c), lambda d: (0, 0, d))],
+        in_specs=[pl.BlockSpec((slots, STATE, some * c), lambda d: (0, 0, d))]
+        + [pl.BlockSpec(memory_space=pl.ANY)] * len(after),
         out_specs=pl.BlockSpec((some, slots * STATE, c), lambda d: (d, 0, 0)),
         out_shape=jax.ShapeDtypeStruct((n, slots * STATE, c), BF16),
         compiler_params=params(24),
         cost_estimate=cost(0, slots * STATE * inner * 6),
         name="pack_state",
-    )(prefilled_state)
+    )(prefilled_state, *after)
+
+
+def half_kernel(me_ref, after_ref, w_ref, o_ref):
+    o_ref[...] = w_ref[...]
+
+
+def weight_half(me, after, out_weight):
+    c, cols = out_weight.shape
+    tile = 1024
+    tiles = cols // 2 // tile
+    return pl.pallas_call(
+        half_kernel,
+        grid_spec=pltpu.PrefetchScalarGridSpec(
+            num_scalar_prefetch=1,
+            grid=(tiles,),
+            in_specs=[
+                pl.BlockSpec(memory_space=pl.ANY),
+                pl.BlockSpec((c, tile), lambda j, me_ref: (0, (1 - me_ref[0] % 2) * tiles + j)),
+            ],
+            out_specs=pl.BlockSpec((c, tile), lambda j, me_ref: (0, j)),
+        ),
+        out_shape=jax.ShapeDtypeStruct((c, cols // 2), BF16),
+        compiler_params=params(56),
+        cost_estimate=cost(0, 2 * c * cols),
+        name="weight_half",
+    )(me, after, out_weight)
 
 
 def conv_kernel(steps, n, me_ref, target_ref, old_ref, x_ref, w_ref, bias_ref, proj_ref, *refs):
@@ -246,14 +275,27 @@
     lows = [low] + [swap(low, 4 * m, n) for m in range(1, zs)]
     (mine,) = small(merge_kernel, me, lows, [(zs,) + piece], "merge_z")
     beside = swap(mine, 2, n)
-    return mine, (mine, beside, swap(mine, 1, n), swap(beside, 1, n))
-
-
-def state_kernel(first, last, me_ref, live_ref, *refs):
+    return keep, (mine, beside, swap(mine, 1, n), swap(beside, 1, n))
+
+
+def assemble_low(lows, index, low_scr, me_ref):
+    y, core = (me_ref[0] // 2) % 2, me_ref[0] % 2
+    for i, low_ref in enumerate(lows):
+        for z in range(low_ref.shape[0]):
+            low_scr[z, jnp.bitwise_xor(y, i % 2), jnp.bitwise_xor(core, i // 2)] = low_ref[z, index]
+    return low_scr[...].reshape(-1, WIDE)
+
+
+def step_sizes(low, dtp_ref, dtb_ref):
+    pre = jnp.dot(low[:, :DT_RANK], dtp_ref[...], preferred_element_type=F32) + dtb_ref[...]
+    return jnp.maximum(pre, 0.0) + jnp.log(1.0 + jnp.exp(-jnp.abs(pre)))
+
+
+def state_kernel(t, behind, me_ref, live_ref, *refs):
+    first, last = t == 0, t == STEPS - 1
+    refs = refs[behind:]
     if first:
         moved_ref, *refs = refs
-    else:
-        _, *refs = refs
     lows, refs = refs[:4], refs[4:]
     conv_ref, z_ref, dtp_ref, dtb_ref, alog_ref, skip_ref, state_ref, *refs = refs
     new_ref = None
@@ -264,7 +306,6 @@
     rows, c = step_scr.shape
     take = conv_ref.shape[0]
     blocks = rows // take
-    y, core = (me_ref[0] // 2) % 2, me_ref[0] % 2
 
     if first:
         buf, sems = refs
@@ -294,12 +335,8 @@
 
     @pl.when(block == 0)
     def _():
-        for i, low_ref in enumerate(lows):
-            for z in range(low_ref.shape[0]):
-                low_scr[z, jnp.bitwise_xor(y, i % 2), jnp.bitwise_xor(core, i // 2)] = low_ref[z]
-        low = low_scr[...].reshape(rows, WIDE)
-        pre = jnp.dot(low[:, :DT_RANK], dtp_ref[...], preferred_element_type=F32) + dtb_ref[...]
-        step_scr[...] = jnp.maximum(pre, 0.0) + jnp.log(1.0 + jnp.exp(-jnp.abs(pre)))
+        low = assemble_low(lows, t, low_scr, me_ref)
+        step_scr[...] = step_sizes(low, dtp_ref, dtb_ref)
         decay_scr[...] = -jnp.exp(alog_ref[...])
         tail_scr[...] = low[:, DT_RANK:].astype(F32)
 
@@ -341,7 +378,7 @@
             gated_ref[r : r + tall, cols] = (total * (z * sigmoid(z))).astype(BF16)
 
 
-def state_step(t, index, me, live, extra, lows, conv, step_z, dt_proj, dt_bias, a_log, d_skip, state, n):
+def state_step(t, me, live, moved, after, lows, conv, step_z, dt_proj, dt_bias, a_log, d_skip, state, n):
     _, rows, c = conv.shape
     take = 2 * rows // n
     blocks = rows // take
@@ -354,8 +391,9 @@
         mine = (y == (me_ref[0] // 2) % 2).astype(jnp.int32)
         return (mine * (blocks // 2) + z, 0)
 
-    in_specs = [pl.BlockSpec((zs, None, own, WIDE), lambda i, *_: (0, index, 0, 0))] * 4 + [
-        pl.BlockSpec((None, take, c), lambda i, *_: (index, i, 0)),
+    vmem = pl.BlockSpec(memory_space=pltpu.VMEM)
+    in_specs = [vmem] * len(moved) + [vmem] * 4 + [
+        pl.BlockSpec((None, take, c), lambda i, *_: (t, i, 0)),
         pl.BlockSpec((1, take, c), lambda i, *_: (t, i, 0)),
         whole(dt_proj.shape),
         whole((1, c)),
@@ -370,13 +408,14 @@
     ]
     flat = pl.BlockSpec((STATE, take, c), lambda i, *_: (0, i, 0))
     if first:
-        in_specs = [whole(extra[0].shape)] + in_specs + [pl.BlockSpec(memory_space=pl.ANY)]
+        in_specs = in_specs + [pl.BlockSpec(memory_space=pl.ANY)]
         scratch += [
             pltpu.VMEM((2, c // 128, take * STATE, 128), F32),
             pltpu.SemaphoreType.DMA((2, c // 128)),
         ]
     else:
-        in_specs = [pl.BlockSpec(memory_space=pl.ANY)] + in_specs + [flat]
+        in_specs = in_specs + [flat]
+    in_specs = [pl.BlockSpec(memory_space=pl.ANY)] * len(after) + in_specs
     out_specs = [pl.BlockSpec((take, c), placed)]
     out_shape = [jax.ShapeDtypeStruct((rows, c), BF16)]
     if not last:
@@ -384,7 +423,7 @@
         out_shape = [jax.ShapeDtypeStruct((STATE, rows, c), BF16)] + out_shape
     size = rows * STATE * c
     out = pl.pallas_call(
-        functools.partial(state_kernel, first, last),
+        functools.partial(state_kernel, t, len(after)),
         grid_spec=pltpu.PrefetchScalarGridSpec(
             num_scalar_prefetch=2,
             grid=(blocks,),
@@ -393,10 +432,10 @@
             scratch_shapes=scratch,
         ),
         out_shape=out_shape,
-        compiler_params=params(56),
+        compiler_params=params(48),
         cost_estimate=cost(8 * size, 4 * size, size),
         name="state_step",
-    )(me, live, *extra, *lows, conv, step_z, dt_proj, dt_bias, a_log, d_skip, state)
+    )(me, live, *after, *moved, *lows, conv, step_z, dt_proj, dt_bias, a_log, d_skip, state)
     return (None, out[0]) if last else (out[0], out[1])
 
 
@@ -421,16 +460,16 @@
             num_scalar_prefetch=1,
             grid=(tiles,),
             in_specs=[
-                whole(own.shape),
-                whole(other.shape),
+                pl.BlockSpec(memory_space=pltpu.VMEM),
+                pl.BlockSpec(memory_space=pltpu.VMEM),
                 pl.BlockSpec((c, tile), lambda j, me_ref: (0, (me_ref[0] % 2) * tiles + j)),
-                pl.BlockSpec((c, tile), lambda j, me_ref: (0, (me_ref[0] % 2) * tiles + j)),
+                pl.BlockSpec((c, tile), lambda j, me_ref: (0, j)),
             ]
             + [pl.BlockSpec(memory_space=pl.ANY)] * len(after),
             out_specs=[pl.BlockSpec((rows // 2, tile), lambda j, me_ref: (0, j))] * 2,
         ),
         out_shape=[half, half],
-        compiler_params=params(56),
+        compiler_params=params(48),
         cost_estimate=cost(4 * rows * c * cols, 4 * c * cols + 2 * rows * cols),
         name="out_project",
     )(me, own, other, out_weight, other_weight, *after)
@@ -507,10 +546,9 @@
     me_scalar = lax.axis_index("dex").astype(jnp.int32)
     me = me_scalar.reshape(1)
 
-    packed_state = pack_state(prefilled_state, n)
-    moved_conv = exchange_conv(prefilled_conv, packed_state, me, n)
-    moved_state = lax.all_to_all(packed_state, "dex", 0, 0, tiled=True)
-    other_weight = swap(out_weight, 1, n)
+    moved_conv = exchange_conv(prefilled_conv, me, n)
+    packed = pack_state(tuple(moved_conv[1:]), prefilled_state, n)
+    moved_state = lax.all_to_all(packed, "dex", 0, 0, tiled=True).reshape(n * slots, STATE, c)
     cols = out_weight.shape[1] // 2
 
     is_live = jnp.arange(slots, dtype=jnp.int32)[None, :] < live_counts[:, None]
@@ -536,32 +574,23 @@
     old = jnp.transpose(resident_conv, (1, 0, 2))
     proj = x_proj.T
     bias = conv_bias.reshape(1, c)
-    moved_state = moved_state.reshape(n * slots, STATE, c)
-
-    lows = {}
-    convs = {}
-
-    def low_rows(steps, after, after_y, after_z):
-        conv, send, keep = conv_steps(
-            steps, n, me, after, spread, old, moved_conv, step_x, conv_weight, bias, proj
-        )
-        merged, low = reduce_projection(send, keep, gain, me, after_y, after_z, n)
-        for i, t in enumerate(steps):
-            lows[t] = (low, i)
-            convs[t] = conv
-        return merged
+    conv, send, keep = conv_steps(
+        tuple(range(STEPS)), n, me, (packed,), spread, old, moved_conv, step_x, conv_weight, bias, proj
+    )
+    behind, lows = reduce_projection(send, keep, gain, me, (), (), n)
+    other_weight = swap(weight_half(me, behind, out_weight), 1, n)
 
     state = resident_state.reshape(rows * STATE, c)
     sends, keeps, gated = {}, {}, {}
     stages = zs.bit_length() - 1
     take = 2 * rows // n
 
-    def s_step(t, extra):
+    rate_bias, skip = dt_bias.reshape(1, c), d_skip.reshape(1, c)
+
+    def s_step(t, after):
         nonlocal state
-        low, i = lows[t]
         state, gated[t] = state_step(
-            t, i, me, live, extra, low, convs[t], step_z, dt_proj,
-            dt_bias.reshape(1, c), a_log, d_skip.reshape(1, c), state, n,
+            t, me, live, (moved_state,) if t == 0 else (), after, lows, conv, step_z, dt_proj, rate_bias, a_log, skip, state, n
         )
         return gated[t]
 
@@ -583,31 +612,22 @@
             sends[t] = swap(sends[t], 1, n)
         return keeps[t]
 
-    merged = low_rows((0,), (), (), ())
-    last = s_step(0, (moved_state,))
-    low_rows(tuple(range(1, STEPS)), (merged,), (lows[0][0][3],), (last,))
+    last = s_step(0, ())
     last = project(0, last)
-    last = s_step(1, (last,))
-    last = reduce(0, 0, last)
-    last = project(1, last)
-    last = s_step(2, (last,))
-    for stage in range(1, stages):
-        last = reduce(0, stage, last)
-    last = project(2, last)
-    last = reduce(1, 0, last)
-    last = s_step(3, (last,))
-    for stage in range(1, stages):
-        last = reduce(1, stage, last)
-    last = project(3, last)
-    last = reduce(2, 0, last)
-    last = reduce(0, stages, last)
-    for stage in range(1, stages):
-        last = reduce(2, stage, last)
-    last = reduce(3, 0, last)
-    last = reduce(1, stages, last)
-    last = reduce(2, stages, last)
-    for stage in range(1, stages + 1):
-        last = reduce(3, stage, last)
+    for t in range(1, STEPS):
+        last = s_step(t, (last,))
+        if t > 1:
+            for stage in range(1, stages):
+                last = reduce(t - 2, stage, last)
+        last = project(t, last)
+        if t > 1:
+            last = reduce(t - 2, stages, last)
+        last = reduce(t - 1, 0, last)
+    for t in (STEPS - 2, STEPS - 1):
+        if t == STEPS - 1:
+            last = reduce(t, 0, last)
+        for stage in range(1, stages + 1):
+            last = reduce(t, stage, last)
     return final_join(me, [keeps[t] for t in range(STEPS)], [sends[t] for t in range(STEPS)])
 
 

time: 353 us -> 295 us (0.84)
  local copies, waits for them, and re-layouts: 36.4 us -> 12.7 us
  starting transfers between devices: 56.2 us -> 36.6 us
  waiting for transfers between devices: 144 us -> 136 us
  Pallas kernels: 111 us -> 104 us
    unnamed x116 -> x48, local copies, waits for them, and re-layouts: 34.7 us -> 11.5 us
    ppermute x50 -> x39, starting transfers between devices: 48.8 us -> 32.4 us  [swap(): return lax.ppermute(x, 'dex', [(i, i ^ mask) for i in range(n)])]
    ppermute x50 -> x39, waiting for transfers between devices: 144 us -> 136 us  [swap(): return lax.ppermute(x, 'dex', [(i, i ^ mask) for i in range(n)])]
    pallas_call x4, Pallas kernels: 39.4 us -> 34.2 us  [out_project(): pl.pallas_call(out_kernel, grid_spec=pltpu.PrefetchScalarGridSpec(num_sca...]
    pallas_call x4 -> x5, Pallas kernels: 57.6 us -> 59.6 us  [the longest x4 52.4 us: state_step(): pl.pallas_call(functools.partial(state_kernel, t, len(after)), grid_spec=...]
  transfers between devices with their start and end apart: 51 -> 40, of which waited for: 27 -> 24; matrix products, arithmetic and copies ran while one was open for 1% -> 1% of each run, Pallas kernels for 28% -> 27%
where the time goes in v6:
time: 295 us; the launch traced here: 292 us
  waiting for transfers between devices  136 us (46%)
  Pallas kernels  104 us (35%)
  starting transfers between devices  36.6 us (12%)
  local copies, waits for them, and re-layouts  12.7 us (4%)
    ppermute x39, waiting for transfers between devices, swap(): return lax.ppermute(x, 'dex', [(i, i ^ mask) for i in range(n)])  136 us
    pallas_call x4, Pallas kernels, state_step(): pl.pallas_call(functools.partial(state_kernel, t, len(after)), grid_spec=...  52.4 us
    pallas_call x4, Pallas kernels, out_project(): pl.pallas_call(out_kernel, grid_spec=pltpu.PrefetchScalarGridSpec(num_sca...  34.2 us
    ppermute x39, starting transfers between devices, swap(): return lax.ppermute(x, 'dex', [(i, i ^ mask) for i in range(n)])  32.4 us
    unnamed x48, local copies, waits for them, and re-layouts  11.5 us
    pallas_call x1, Pallas kernels, weight_half(): pl.pallas_call(half_kernel, grid_spec=pltpu.PrefetchScalarGridSpec(num_sc...  7.11 us
  transfers between devices with their start and end apart: 40, of which 24 were waited for; matrix products, arithmetic and copies ran while one was open for 1% of the time, Pallas kernels for 27%

profile of v6, /device:TPU:0, one launch (start us, length us, event | category | flops | bytes accessed | tf_op | source)
XLA Modules:
  0.0 291.8 jit_solution(8941071829777192160)
XLA Ops:
  0.0 1.2 copy-done.16
  1.3 3.0 %collective-permute-start = (bf16[4,16,768]{2,1,0:T(8,128)(2,1)S(1)}, bf16[4,16,768]{2,1,0:T(8,128)(2,1)S(1)}, u32[]{:S(2)}, u32[]{:S(2)}) collective-permute-start(bf16[4,16,768]{2,1,0:T(8,128)(2,1)S(1)} %get-tuple-element.61), channel_id=1, source_target_pairs={{0,2},{1,3},{2,0},{3,1},{4,6},{5,7},{6,4},{7,5},{8,10},{9,11},{10,... | collective-permute-start | bytes 294920 | tf_op jit(solution)/shard_map/ppermute | solution.py:28
  4.9 0.7 reshape.103
  5.6 0.7 broadcast_select_fusion
  7.1 4.1 %collective-permute-done.3.refs_3_ = bf16[4,16,768]{2,1,0:T(8,128)(2,1)S(1)} collective-permute-done((bf16[4,16,768]{2,1,0:T(8,128)(2,1)S(1)}, bf16[4,16,768]{2,1,0:T(8,128)(2,1)S(1)}, u32[]{:S(2)}, u32[]{:S(2)}) %collective-permute-start.3) | collective-permute-done | bytes 98336 | tf_op jit(solution)/shard_map/ppermute | solution.py:28
  11.3 1.6 collective-permute-start.4
  12.9 2.6 collective-permute-start.5
  15.7 1.2 collective-permute-done.4.refs_0_.refs_1_
  16.9 5.7 %collective-permute-done.5.refs_1_.refs_2_ = bf16[4,16,768]{2,1,0:T(8,128)(2,1)S(1)} collective-permute-done((bf16[4,16,768]{2,1,0:T(8,128)(2,1)S(1)}, bf16[4,16,768]{2,1,0:T(8,128)(2,1)S(1)}, u32[]{:S(2)}, u32[]{:S(2)}) %collective-permute-start.5) | collective-permute-done | bytes 98336 | tf_op jit(solution)/shard_map/ppermute | solution.py:28
  22.6 2.2 copy-done.9
  24.8 2.1 pack_state.1.refs_4_
  27.5 0.7 copy-done.11
  28.1 3.8 %conv_project.1 = (f32[4,256,1024]{2,1,0:T(8,128)S(1)}, bf16[8,4,16,640]{3,2,1,0:T(8,128)(2,1)S(1)}, bf16[8,4,16,640]{3,2,1,0:T(8,128)(2,1)S(1)}) custom-call(s32[1]{0:T(128)} %bitcast.me_ref, s32[4,256]{1,0:T(4,128)S(1)} %broadcast_select_fusion.1.target_ref, f32[3,256,1024]{2,1,0:T(8,128)S(1)} %bitcast.25, bf16[4,256,1024]{2,1,0:T(8,128)(2,1)S(1)} %copy-done.11, ...), custom_call_target="tpu_custom_call" | custom-call | flops 1024 | bytes 1024 | tf_op jit(solution)/shard_map/conv_project/pallas_call | solution.py:194
  31.9 2.1 copy-done
  34.0 2.1 collective-permute-done.7.refs_1_
  36.3 0.7 copy-done.12
  37.0 0.7 copy-done.21
  37.7 7.1 %weight_half.1 = bf16[1024,4096]{1,0:T(8,128)(2,1)} custom-call(s32[1]{0:T(128)} %bitcast.me_ref, bf16[4,4,16,640]{3,2,1,0:T(8,128)(2,1)} %copy-done.12, bf16[1024,8192]{1,0:T(8,128)(2,1)} %wown_ref.7), custom_call_target="tpu_custom_call" | custom-call | flops 1024 | bytes 1024 | tf_op jit(solution)/shard_map/weight_half/pallas_call | solution.py:129
  45.1 4.2 %all-to-all-start = ((bf16[16,64,1024]{2,1,0:T(8,128)(2,1)}), bf16[16,64,1024]{2,1,0:T(8,128)(2,1)S(1)}, u32[]{:S(2)}, u32[]{:S(2)}) async-start(bf16[16,64,1024]{2,1,0:T(8,128)(2,1)} %pack_state.1.refs_4_), calls=%async_computation | async-start | bytes 4194304 | tf_op jit(solution)/shard_map/all_to_all | solution.py:551
  49.3 2.0 collective-permute-start.8
  51.3 24.9 %collective-permute-done.8.refs_1_ = bf16[4,4,16,640]{3,2,1,0:T(8,128)(2,1)S(1)} collective-permute-done((bf16[4,4,16,640]{3,2,1,0:T(8,128)(2,1)}, bf16[4,4,16,640]{3,2,1,0:T(8,128)(2,1)S(1)}, u32[]{:S(2)}, u32[]{:S(2)}) %collective-permute-start.8) | collective-permute-done | bytes 327712 | tf_op jit(solution)/shard_map/ppermute | solution.py:28
  76.3 3.9 %collective-permute-start.10 = (bf16[4,16,640]{2,1,0:T(8,128)(2,1)S(1)}, bf16[4,16,640]{2,1,0:T(8,128)(2,1)S(1)}, u32[]{:S(2)}, u32[]{:S(2)}) collective-permute-start(bf16[4,16,640]{2,1,0:T(8,128)(2,1)S(1)} %get-tuple-element.74), channel_id=1, source_target_pairs={{0,8},{1,9},{2,10},{3,11},{4,12},{5,13},{6,14},{7,15},{8,0},{9,1},... | collective-permute-start | bytes 245768 | tf_op jit(solution)/shard_map/ppermute | solution.py:28
  80.7 5.5 %collective-permute-done.9.refs_1_ = bf16[4,16,640]{2,1,0:T(8,128)(2,1)S(1)} collective-permute-done((bf16[4,16,640]{2,1,0:T(8,128)(2,1)S(1)}, bf16[4,16,640]{2,1,0:T(8,128)(2,1)S(1)}, u32[]{:S(2)}, u32[]{:S(2)}) %collective-permute-start.9) | collective-permute-done | bytes 81952 | tf_op jit(solution)/shard_map/ppermute | solution.py:28
  86.2 17.9 %collective-permute-done.10.refs_2_ = bf16[4,16,640]{2,1,0:T(8,128)(2,1)S(1)} collective-permute-done((bf16[4,16,640]{2,1,0:T(8,128)(2,1)S(1)}, bf16[4,16,640]{2,1,0:T(8,128)(2,1)S(1)}, u32[]{:S(2)}, u32[]{:S(2)}) %collective-permute-start.10) | collective-permute-done | bytes 81952 | tf_op jit(solution)/shard_map/ppermute | solution.py:28
  104.2 1.6 collective-permute-start.14
  105.9 1.7 collective-permute-start.13
  107.6 1.1 collective-permute-start.12
  108.7 2.7 collective-permute-done.14.refs_3_
  111.3 3.5 %collective-permute-done.13.refs_2_ = bf16[4,16,640]{2,1,0:T(8,128)(2,1)S(1)} collective-permute-done((bf16[4,16,640]{2,1,0:T(8,128)(2,1)S(1)}, bf16[4,16,640]{2,1,0:T(8,128)(2,1)S(1)}, u32[]{:S(2)}, u32[]{:S(2)}) %collective-permute-start.13) | collective-permute-done | bytes 81952 | tf_op jit(solution)/shard_map/ppermute | solution.py:28
  114.9 1.6 collective-permute-start.15
  116.7 0.7 compare_select_fusion
  117.3 7.1 %collective-permute-done.15.refs_2_ = bf16[4,4,16,640]{3,2,1,0:T(8,128)(2,1)} collective-permute-done((bf16[4,4,16,640]{3,2,1,0:T(8,128)(2,1)S(1)}, bf16[4,4,16,640]{3,2,1,0:T(8,128)(2,1)}, u32[]{:S(2)}, u32[]{:S(2)}) %collective-permute-start.15) | collective-permute-done | bytes 327712 | tf_op jit(solution)/shard_map/ppermute | solution.py:28
  124.8 0.7 copy-done.3
  125.5 0.7 collective-permute-done.17.refs_4_
  126.2 0.7 copy-done.6
  127.0 1.0 copy-done.4
  128.0 1.0 copy-done.7
  128.9 17.1 %state_step.4 = (bf16[16,256,1024]{2,1,0:T(8,128)(2,1)}, bf16[256,1024]{1,0:T(8,128)(2,1)S(1)}) custom-call(s32[1]{0:T(128)} %bitcast.me_ref, s32[3,64]{1,0:T(4,128)S(1)} %pad_add_fusion.live_ref, bf16[64,16,1024]{2,1,0:T(8,128)(2,1)S(1)} %bitcast.20, bf16[4,4,16,640]{3,2,1,0:T(8,128)(2,1)S(1)} %merge_z.1.refs_1_, ...), custom_call_target="tpu_custom_call" | custom-call | flops 1024 | bytes 1024 | tf_op jit(solution)/shard_map/state_step/pallas_call | solution.py:425
  146.3 1.8 collective-permute-done.18.other_ref
  148.1 8.5 %out_project.4 = (bf16[128,4096]{1,0:T(8,128)(2,1)S(1)}, bf16[128,4096]{1,0:T(8,128)(2,1)S(1)}) custom-call(s32[1]{0:T(128)} %bitcast.me_ref, bf16[256,1024]{1,0:T(8,128)(2,1)S(1)} %get-tuple-element.77.own_ref.refs_0_, bf16[256,1024]{1,0:T(8,128)(2,1)S(1)} %collective-permute-done.18.other_ref, bf16[1024,8192]{1,0:T(8,128)(2,1)} %wown_ref.7, ...), custom_call_target="tpu_custom_call" | custom-call | flops 1024 | bytes 1024 | tf_op jit(solution)/shard_map/out_project/pallas_call | solution.py:457
  156.6 1.8 collective-permute-start.21
  158.4 12.5 %state_step.5 = (bf16[16,256,1024]{2,1,0:T(8,128)(2,1)}, bf16[256,1024]{1,0:T(8,128)(2,1)S(1)}) custom-call(s32[1]{0:T(128)} %bitcast.me_ref, s32[3,64]{1,0:T(4,128)S(1)} %pad_add_fusion.live_ref, bf16[128,4096]{1,0:T(8,128)(2,1)S(1)} %get-tuple-element.78.refs_0_, bf16[4,4,16,640]{3,2,1,0:T(8,128)(2,1)S(1)} %merge_z.1.refs_1_, ...), custom_call_target="tpu_custom_call" | custom-call | flops 1024 | bytes 1024 | tf_op jit(solution)/shard_map/state_step/pallas_call | solution.py:425
  171.0 1.9 collective-permute-done.20.other_ref
  172.9 8.5 %out_project.5 = (bf16[128,4096]{1,0:T(8,128)(2,1)S(1)}, bf16[128,4096]{1,0:T(8,128)(2,1)S(1)}) custom-call(s32[1]{0:T(128)} %bitcast.me_ref, bf16[256,1024]{1,0:T(8,128)(2,1)S(1)} %get-tuple-element.80.own_ref.refs_0_, bf16[256,1024]{1,0:T(8,128)(2,1)S(1)} %collective-permute-done.20.other_ref, bf16[1024,8192]{1,0:T(8,128)(2,1)} %wown_ref.7, ...), custom_call_target="tpu_custom_call" | custom-call | flops 1024 | bytes 1024 | tf_op jit(solution)/shard_map/out_project/pallas_call | solution.py:457
  182.2 12.6 %state_step.6 = (bf16[16,256,1024]{2,1,0:T(8,128)(2,1)}, bf16[256,1024]{1,0:T(8,128)(2,1)S(1)}) custom-call(s32[1]{0:T(128)} %bitcast.me_ref, s32[3,64]{1,0:T(4,128)S(1)} %pad_add_fusion.live_ref, bf16[2,32,4096]{2,1,0:T(8,128)(2,1)S(1)} %get-tuple-element.83.refs_0_.keep_ref, bf16[4,4,16,640]{3,2,1,0:T(8,128)(2,1)S(1)} %merge_z.1.refs_1_, ...), custom_call_target="tpu_custom_call" | custom-call | flops 1024 | bytes 1024 | tf_op jit(solution)/shard_map/state_step/pallas_call | solution.py:425
  194.8 1.0 collective-permute-done.23.got_ref
  195.9 1.1 collective-permute-start.24
  197.0 8.5 %out_project.6 = (bf16[128,4096]{1,0:T(8,128)(2,1)S(1)}, bf16[128,4096]{1,0:T(8,128)(2,1)S(1)}) custom-call(s32[1]{0:T(128)} %bitcast.me_ref, bf16[256,1024]{1,0:T(8,128)(2,1)S(1)} %get-tuple-element.85.after_ref.own_ref, bf16[256,1024]{1,0:T(8,128)(2,1)S(1)} %collective-permute-done.22.other_ref, bf16[1024,8192]{1,0:T(8,128)(2,1)} %wown_ref.7, ...), custom_call_target="tpu_custom_call" | custom-call | flops 1024 | bytes 1024 | tf_op jit(solution)/shard_map/out_project/pallas_call | solution.py:457
  205.5 1.5 collective-permute-start.29
  207.0 3.2 %collective-permute-done.24.got_ref = bf16[1,32,4096]{2,1,0:T(8,128)(2,1)S(1)} collective-permute-done((bf16[1,32,4096]{2,1,0:T(8,128)(2,1)S(1)}, bf16[1,32,4096]{2,1,0:T(8,128)(2,1)S(1)}, u32[]{:S(2)}, u32[]{:S(2)}) %collective-permute-start.24) | collective-permute-done | bytes 262176 | tf_op jit(solution)/shard_map/ppermute | solution.py:28
  210.6 10.2 %state_step.7.after_ref.own_ref = bf16[256,1024]{1,0:T(8,128)(2,1)S(1)} custom-call(s32[1]{0:T(128)} %bitcast.me_ref, s32[3,64]{1,0:T(4,128)S(1)} %pad_add_fusion.live_ref, bf16[2,32,4096]{2,1,0:T(8,128)(2,1)S(1)} %get-tuple-element.92.refs_0_.keep_ref, bf16[4,4,16,640]{3,2,1,0:T(8,128)(2,1)S(1)} %merge_z.1.refs_1_, ...), custom_call_target="tpu_custom_call" | custom-call | flops 1024 | bytes 1024 | tf_op jit(solution)/shard_map/state_step/pallas_call | solution.py:425
  220.9 2.1 collective-permute-done.27.got_ref
  223.2 1.0 collective-permute-start.28
  224.1 8.5 %out_project.7 = (bf16[128,4096]{1,0:T(8,128)(2,1)S(1)}, bf16[128,4096]{1,0:T(8,128)(2,1)S(1)}) custom-call(s32[1]{0:T(128)} %bitcast.me_ref, bf16[256,1024]{1,0:T(8,128)(2,1)S(1)} %state_step.7.after_ref.own_ref, bf16[256,1024]{1,0:T(8,128)(2,1)S(1)} %collective-permute-done.26.other_ref, bf16[1024,8192]{1,0:T(8,128)(2,1)} %wown_ref.7, ...), custom_call_target="tpu_custom_call" | custom-call | flops 1024 | bytes 1024 | tf_op jit(solution)/shard_map/out_project/pallas_call | solution.py:457
  232.7 2.3 collective-permute-start.32
  235.0 1.4 collective-permute-done.28.got_ref
  237.1 12.0 %collective-permute-done.30.got_ref = bf16[2,32,4096]{2,1,0:T(8,128)(2,1)S(1)} collective-permute-done((bf16[2,32,4096]{2,1,0:T(8,128)(2,1)S(1)}, bf16[2,32,4096]{2,1,0:T(8,128)(2,1)S(1)}, u32[]{:S(2)}, u32[]{:S(2)}) %collective-permute-start.30) | collective-permute-done | bytes 524320 | tf_op jit(solution)/shard_map/ppermute | solution.py:28
  249.2 0.6 collective-permute-start.31
  249.8 11.4 %collective-permute-done.31.got_ref = bf16[1,32,4096]{2,1,0:T(8,128)(2,1)S(1)} collective-permute-done((bf16[1,32,4096]{2,1,0:T(8,128)(2,1)S(1)}, bf16[1,32,4096]{2,1,0:T(8,128)(2,1)S(1)}, u32[]{:S(2)}, u32[]{:S(2)}) %collective-permute-start.31) | collective-permute-done | bytes 262176 | tf_op jit(solution)/shard_map/ppermute | solution.py:28
  261.7 13.1 %collective-permute-done.33.got_ref = bf16[2,32,4096]{2,1,0:T(8,128)(2,1)S(1)} collective-permute-done((bf16[2,32,4096]{2,1,0:T(8,128)(2,1)S(1)}, bf16[2,32,4096]{2,1,0:T(8,128)(2,1)S(1)}, u32[]{:S(2)}, u32[]{:S(2)}) %collective-permute-start.33) | collective-permute-done | bytes 524320 | tf_op jit(solution)/shard_map/ppermute | solution.py:28
  274.9 1.5 collective-permute-start.34
  276.9 11.2 %collective-permute-done.34.got_ref = bf16[1,32,4096]{2,1,0:T(8,128)(2,1)S(1)} collective-permute-done((bf16[1,32,4096]{2,1,0:T(8,128)(2,1)S(1)}, bf16[1,32,4096]{2,1,0:T(8,128)(2,1)S(1)}, u32[]{:S(2)}, u32[]{:S(2)}) %collective-permute-start.34) | collective-permute-done | bytes 262176 | tf_op jit(solution)/shard_map/ppermute | solution.py:28
  288.3 1.3 collective-permute-done.38.refs_7_
  289.6 2.2 final_join.1
  (110 shorter events, 7.7 us)
Async XLA Ops:
  0.0 27.0 %copy-start.14 = (bf16[1024,544]{0,1:T(8,128)(2,1)S(1)}, bf16[1024,544]{0,1:T(8,128)(2,1)}, u32[]{:S(2)}) copy-start(bf16[1024,544]{0,1:T(8,128)(2,1)} %param.27) | copy-start | bytes 3342340
  0.0 1.2 copy-start.16
  1.2 25.7 %copy-start.19 = (f32[4,1024]{1,0:T(4,128)S(1)}, f32[4,1024]{1,0:T(4,128)}, u32[]{:S(2)}) copy-start(f32[4,1024]{1,0:T(4,128)} %w_ref.2) | copy-start | bytes 49156
  1.2 25.7 %copy-start.20 = (f32[1024]{0:T(1024)S(1)}, f32[1024]{0:T(1024)}, u32[]{:S(2)}) copy-start(f32[1024]{0:T(1024)} %param.26) | copy-start | bytes 12292
  1.3 5.8 %collective-permute-start = (bf16[4,16,768]{2,1,0:T(8,128)(2,1)S(1)}, bf16[4,16,768]{2,1,0:T(8,128)(2,1)S(1)}, u32[]{:S(2)}, u32[]{:S(2)}) collective-permute-start(bf16[4,16,768]{2,1,0:T(8,128)(2,1)S(1)} %get-tuple-element.61), channel_id=1, source_target_pairs={{0,2},{1,3},{2,0},{3,1},{4,6},{5,7},{6,4},{7,5},{8,10},{9,11},{10,... | collective-permute-start | bytes 294920 | tf_op jit(solution)/shard_map/ppermute | solution.py:28
  4.3 2.8 collective-permute-start.1
  4.3 2.1 collective-permute-start.2
  6.5 4.8 %collective-permute-start.3 = (bf16[4,16,768]{2,1,0:T(8,128)(2,1)S(1)}, bf16[4,16,768]{2,1,0:T(8,128)(2,1)S(1)}, u32[]{:S(2)}, u32[]{:S(2)}) collective-permute-start(bf16[4,16,768]{2,1,0:T(8,128)(2,1)S(1)} %collective-permute-done.2), channel_id=1, source_target_pairs={{0,2},{1,3},{2,0},{3,1},{4,6},{5,7},{6,4},{7,5},{8,10},{9,11},{10,... | collective-permute-start | bytes 294920 | tf_op jit(solution)/shard_map/ppermute | solution.py:28
  11.3 5.7 %collective-permute-start.4 = (bf16[4,16,768]{2,1,0:T(8,128)(2,1)S(1)}, bf16[4,16,768]{2,1,0:T(8,128)(2,1)S(1)}, u32[]{:S(2)}, u32[]{:S(2)}) collective-permute-start(bf16[4,16,768]{2,1,0:T(8,128)(2,1)S(1)} %get-tuple-element.64), channel_id=1, source_target_pairs={{0,4},{1,5},{2,6},{3,7},{4,0},{5,1},{6,2},{7,3},{8,12},{9,13},{10,... | collective-permute-start | bytes 294920 | tf_op jit(solution)/shard_map/ppermute | solution.py:28
  12.9 9.7 %collective-permute-start.5 = (bf16[4,16,768]{2,1,0:T(8,128)(2,1)S(1)}, bf16[4,16,768]{2,1,0:T(8,128)(2,1)S(1)}, u32[]{:S(2)}, u32[]{:S(2)}) collective-permute-start(bf16[4,16,768]{2,1,0:T(8,128)(2,1)S(1)} %get-tuple-element.65), channel_id=1, source_target_pairs={{0,8},{1,9},{2,10},{3,11},{4,12},{5,13},{6,14},{7,15},{8,0},{9,1},... | collective-permute-start | bytes 294920 | tf_op jit(solution)/shard_map/ppermute | solution.py:28
  15.5 7.1 %collective-permute-start.6 = (bf16[4,16,768]{2,1,0:T(8,128)(2,1)S(1)}, bf16[4,16,768]{2,1,0:T(8,128)(2,1)S(1)}, u32[]{:S(2)}, u32[]{:S(2)}) collective-permute-start(bf16[4,16,768]{2,1,0:T(8,128)(2,1)S(1)} %get-tuple-element.66), channel_id=1, source_target_pairs={{0,12},{1,13},{2,14},{3,15},{4,8},{5,9},{6,10},{7,11},{8,4},{9,5},... | collective-permute-start | bytes 294920 | tf_op jit(solution)/shard_map/ppermute | solution.py:28
  22.6 2.2 copy-start.9
  24.8 2.6 copy-start.10
  24.8 3.3 %copy-start.11 = (bf16[4,256,1024]{2,1,0:T(8,128)(2,1)S(1)}, bf16[4,256,1024]{2,1,0:T(8,128)(2,1)}, u32[]{:S(2)}) copy-start(bf16[4,256,1024]{2,1,0:T(8,128)(2,1)} %x_ref.3) | copy-start | bytes 6291460
  31.9 2.1 copy-start
  34.0 2.1 collective-permute-start.7
  36.3 0.7 copy-start.12
  37.0 0.7 copy-start.21
  44.9 31.3 %copy-start.13 = (bf16[4,4,16,640]{3,2,1,0:T(8,128)(2,1)S(1)}, bf16[4,4,16,640]{3,2,1,0:T(8,128)(2,1)}, u32[]{:S(2)}) copy-start(bf16[4,4,16,640]{3,2,1,0:T(8,128)(2,1)} %copy-done.12) | copy-start | bytes 983044
  44.9 35.9 %copy-start.22 = (f32[544]{0:T(1024)S(1)}, f32[544]{0:T(1024)}, u32[]{:S(2)}) copy-start(f32[544]{0:T(1024)} %param.28) | copy-start | bytes 6532
  44.9 71.6 %copy-start.23 = (s32[16]{0:T(128)S(1)}, s32[16]{0:T(128)}, u32[]{:S(2)}) copy-start(s32[16]{0:T(128)} %param.21) | copy-start | bytes 196
  44.9 82.1 %copy-start.2 = (bf16[512,1024]{1,0:T(8,128)(2,1)S(1)}, bf16[512,1024]{1,0:T(8,128)(2,1)}, u32[]{:S(2)}) copy-start(bf16[512,1024]{1,0:T(8,128)(2,1)} %refs_7_.7) | copy-start | bytes 3145732
  44.9 82.1 %copy-start.15 = (f32[16,1024]{1,0:T(8,128)S(1)}, f32[16,1024]{1,0:T(8,128)}, u32[]{:S(2)}) copy-start(f32[16,1024]{1,0:T(8,128)} %refs_9_.7) | copy-start | bytes 196612
  44.9 82.1 %copy-start.17 = (f32[1024]{0:T(1024)S(1)}, f32[1024]{0:T(1024)}, u32[]{:S(2)}) copy-start(f32[1024]{0:T(1024)} %param.30) | copy-start | bytes 12292
  44.9 82.1 %copy-start.18 = (f32[1024]{0:T(1024)S(1)}, f32[1024]{0:T(1024)}, u32[]{:S(2)}) copy-start(f32[1024]{0:T(1024)} %param.32) | copy-start | bytes 12292
  44.9 103.1 %collective-permute-start.19 = (bf16[1024,4096]{1,0:T(8,128)(2,1)}, bf16[1024,4096]{1,0:T(8,128)(2,1)}, u32[]{:S(2)}, u32[]{:S(2)}) collective-permute-start(bf16[1024,4096]{1,0:T(8,128)(2,1)} %weight_half.1), channel_id=1, source_target_pairs={{0,1},{1,0},{2,3},{3,2},{4,5},{5,4},{6,7},{7,6},{8,9},{9,8},{10,11... | collective-permute-start | bytes 25165832 | tf_op jit(solution)/shard_map/ppermute | solution.py:28
  45.1 81.8 %all-to-all-start = ((bf16[16,64,1024]{2,1,0:T(8,128)(2,1)}), bf16[16,64,1024]{2,1,0:T(8,128)(2,1)S(1)}, u32[]{:S(2)}, u32[]{:S(2)}) async-start(bf16[16,64,1024]{2,1,0:T(8,128)(2,1)} %pack_state.1.refs_4_), calls=%async_computation | async-start | bytes 4194304 | tf_op jit(solution)/shard_map/all_to_all | solution.py:551
  49.3 26.9 %collective-permute-start.8 = (bf16[4,4,16,640]{3,2,1,0:T(8,128)(2,1)}, bf16[4,4,16,640]{3,2,1,0:T(8,128)(2,1)S(1)}, u32[]{:S(2)}, u32[]{:S(2)}) collective-permute-start(bf16[4,4,16,640]{3,2,1,0:T(8,128)(2,1)} %copy-done.21), channel_id=1, source_target_pairs={{0,2},{1,3},{2,0},{3,1},{4,6},{5,7},{6,4},{7,5},{8,10},{9,11},{10,... | collective-permute-start | bytes 983048 | tf_op jit(solution)/shard_map/ppermute | solution.py:28
  76.3 9.9 %collective-permute-start.9 = (bf16[4,16,640]{2,1,0:T(8,128)(2,1)S(1)}, bf16[4,16,640]{2,1,0:T(8,128)(2,1)S(1)}, u32[]{:S(2)}, u32[]{:S(2)}) collective-permute-start(bf16[4,16,640]{2,1,0:T(8,128)(2,1)S(1)} %get-tuple-element.73), channel_id=1, source_target_pairs={{0,4},{1,5},{2,6},{3,7},{4,0},{5,1},{6,2},{7,3},{8,12},{9,13},{10,... | collective-permute-start | bytes 245768 | tf_op jit(solution)/shard_map/ppermute | solution.py:28
  76.3 27.7 %collective-permute-start.10 = (bf16[4,16,640]{2,1,0:T(8,128)(2,1)S(1)}, bf16[4,16,640]{2,1,0:T(8,128)(2,1)S(1)}, u32[]{:S(2)}, u32[]{:S(2)}) collective-permute-start(bf16[4,16,640]{2,1,0:T(8,128)(2,1)S(1)} %get-tuple-element.74), channel_id=1, source_target_pairs={{0,8},{1,9},{2,10},{3,11},{4,12},{5,13},{6,14},{7,15},{8,0},{9,1},... | collective-permute-start | bytes 245768 | tf_op jit(solution)/shard_map/ppermute | solution.py:28
  80.3 23.8 %collective-permute-start.11 = (bf16[4,16,640]{2,1,0:T(8,128)(2,1)S(1)}, bf16[4,16,640]{2,1,0:T(8,128)(2,1)S(1)}, u32[]{:S(2)}, u32[]{:S(2)}) collective-permute-start(bf16[4,16,640]{2,1,0:T(8,128)(2,1)S(1)} %get-tuple-element.75), channel_id=1, source_target_pairs={{0,12},{1,13},{2,14},{3,15},{4,8},{5,9},{6,10},{7,11},{8,4},{9,5},... | collective-permute-start | bytes 245768 | tf_op jit(solution)/shard_map/ppermute | solution.py:28
  104.2 7.1 %collective-permute-start.14 = (bf16[4,16,640]{2,1,0:T(8,128)(2,1)S(1)}, bf16[4,16,640]{2,1,0:T(8,128)(2,1)S(1)}, u32[]{:S(2)}, u32[]{:S(2)}) collective-permute-start(bf16[4,16,640]{2,1,0:T(8,128)(2,1)S(1)} %norm.1.refs_0_), channel_id=1, source_target_pairs={{0,12},{1,13},{2,14},{3,15},{4,8},{5,9},{6,10},{7,11},{8,4},{9,5},... | collective-permute-start | bytes 245768 | tf_op jit(solution)/shard_map/ppermute | solution.py:28
  105.9 9.0 %collective-permute-start.13 = (bf16[4,16,640]{2,1,0:T(8,128)(2,1)S(1)}, bf16[4,16,640]{2,1,0:T(8,128)(2,1)S(1)}, u32[]{:S(2)}, u32[]{:S(2)}) collective-permute-start(bf16[4,16,640]{2,1,0:T(8,128)(2,1)S(1)} %norm.1.refs_0_), channel_id=1, source_target_pairs={{0,8},{1,9},{2,10},{3,11},{4,12},{5,13},{6,14},{7,15},{8,0},{9,1},... | collective-permute-start | bytes 245768 | tf_op jit(solution)/shard_map/ppermute | solution.py:28
  107.6 7.2 %collective-permute-start.12 = (bf16[4,16,640]{2,1,0:T(8,128)(2,1)S(1)}, bf16[4,16,640]{2,1,0:T(8,128)(2,1)S(1)}, u32[]{:S(2)}, u32[]{:S(2)}) collective-permute-start(bf16[4,16,640]{2,1,0:T(8,128)(2,1)S(1)} %norm.1.refs_0_), channel_id=1, source_target_pairs={{0,4},{1,5},{2,6},{3,7},{4,0},{5,1},{6,2},{7,3},{8,12},{9,13},{10,... | collective-permute-start | bytes 245768 | tf_op jit(solution)/shard_map/ppermute | solution.py:28
  114.9 9.5 %collective-permute-start.15 = (bf16[4,4,16,640]{3,2,1,0:T(8,128)(2,1)S(1)}, bf16[4,4,16,640]{3,2,1,0:T(8,128)(2,1)}, u32[]{:S(2)}, u32[]{:S(2)}) collective-permute-start(bf16[4,4,16,640]{3,2,1,0:T(8,128)(2,1)S(1)} %merge_z.1.refs_1_), channel_id=1, source_target_pairs={{0,2},{1,3},{2,0},{3,1},{4,6},{5,7},{6,4},{7,5},{8,10},{9,11},{10,... | collective-permute-start | bytes 983048 | tf_op jit(solution)/shard_map/ppermute | solution.py:28
  117.3 7.5 %collective-permute-start.16 = (bf16[4,4,16,640]{3,2,1,0:T(8,128)(2,1)S(1)}, bf16[4,4,16,640]{3,2,1,0:T(8,128)(2,1)S(1)}, u32[]{:S(2)}, u32[]{:S(2)}) collective-permute-start(bf16[4,4,16,640]{3,2,1,0:T(8,128)(2,1)S(1)} %merge_z.1.refs_1_), channel_id=1, source_target_pairs={{0,1},{1,0},{2,3},{3,2},{4,5},{5,4},{6,7},{7,6},{8,9},{9,8},{10,11... | collective-permute-start | bytes 983048 | tf_op jit(solution)/shard_map/ppermute | solution.py:28
  124.4 1.8 collective-permute-start.17
  124.8 0.7 copy-start.3
  126.2 0.7 copy-start.6
  127.0 1.0 copy-start.4
  128.0 1.0 copy-start.7
  146.0 12.4 %copy-start.1 = (bf16[4,256,1024]{2,1,0:T(8,128)(2,1)S(1)}, bf16[4,256,1024]{2,1,0:T(8,128)(2,1)}, u32[]{:S(2)}) copy-start(bf16[4,256,1024]{2,1,0:T(8,128)(2,1)} %refs_6_.7) | copy-start | bytes 6291460
  146.1 12.4 %copy-start.5 = (bf16[4,4,16,640]{3,2,1,0:T(8,128)(2,1)S(1)}, bf16[4,4,16,640]{3,2,1,0:T(8,128)(2,1)}, u32[]{:S(2)}) copy-start(bf16[4,4,16,640]{3,2,1,0:T(8,128)(2,1)} %copy-done.3) | copy-start | bytes 983044
  146.1 12.4 %copy-start.8 = (bf16[4,4,16,640]{3,2,1,0:T(8,128)(2,1)S(1)}, bf16[4,4,16,640]{3,2,1,0:T(8,128)(2,1)}, u32[]{:S(2)}) copy-start(bf16[4,4,16,640]{3,2,1,0:T(8,128)(2,1)} %copy-done.6) | copy-start | bytes 983044
  146.1 2.0 collective-permute-start.18
  156.6 25.3 %collective-permute-start.21 = (bf16[128,4096]{1,0:T(8,128)(2,1)S(1)}, bf16[128,4096]{1,0:T(8,128)(2,1)S(1)}, u32[]{:S(2)}, u32[]{:S(2)}) collective-permute-start(bf16[128,4096]{1,0:T(8,128)(2,1)S(1)} %get-tuple-element.82), channel_id=1, source_target_pairs={{0,2},{1,3},{2,0},{3,1},{4,6},{5,7},{6,4},{7,5},{8,10},{9,11},{10,... | collective-permute-start | bytes 3145736 | tf_op jit(solution)/shard_map/ppermute | solution.py:28
  171.0 1.9 collective-permute-start.20
  181.4 28.9 %collective-permute-start.25 = (bf16[128,4096]{1,0:T(8,128)(2,1)S(1)}, bf16[128,4096]{1,0:T(8,128)(2,1)S(1)}, u32[]{:S(2)}, u32[]{:S(2)}) collective-permute-start(bf16[128,4096]{1,0:T(8,128)(2,1)S(1)} %get-tuple-element.91), channel_id=1, source_target_pairs={{0,2},{1,3},{2,0},{3,1},{4,6},{5,7},{6,4},{7,5},{8,10},{9,11},{10,... | collective-permute-start | bytes 3145736 | tf_op jit(solution)/shard_map/ppermute | solution.py:28
  182.1 13.7 %collective-permute-start.23 = (bf16[2,32,4096]{2,1,0:T(8,128)(2,1)S(1)}, bf16[2,32,4096]{2,1,0:T(8,128)(2,1)S(1)}, u32[]{:S(2)}, u32[]{:S(2)}) collective-permute-start(bf16[2,32,4096]{2,1,0:T(8,128)(2,1)S(1)} %get-tuple-element.86), channel_id=1, source_target_pairs={{0,4},{1,5},{2,6},{3,7},{4,0},{5,1},{6,2},{7,3},{8,12},{9,13},{10,... | collective-permute-start | bytes 1572872 | tf_op jit(solution)/shard_map/ppermute | solution.py:28
  194.8 2.2 collective-permute-start.22
  195.9 14.3 %collective-permute-start.24 = (bf16[1,32,4096]{2,1,0:T(8,128)(2,1)S(1)}, bf16[1,32,4096]{2,1,0:T(8,128)(2,1)S(1)}, u32[]{:S(2)}, u32[]{:S(2)}) collective-permute-start(bf16[1,32,4096]{2,1,0:T(8,128)(2,1)S(1)} %get-tuple-element.89), channel_id=1, source_target_pairs={{0,8},{1,9},{2,10},{3,11},{4,12},{5,13},{6,14},{7,15},{8,0},{9,1},... | collective-permute-start | bytes 786440 | tf_op jit(solution)/shard_map/ppermute | solution.py:28
  205.5 30.9 %collective-permute-start.29 = (bf16[128,4096]{1,0:T(8,128)(2,1)S(1)}, bf16[128,4096]{1,0:T(8,128)(2,1)S(1)}, u32[]{:S(2)}, u32[]{:S(2)}) collective-permute-start(bf16[128,4096]{1,0:T(8,128)(2,1)S(1)} %get-tuple-element.99), channel_id=1, source_target_pairs={{0,2},{1,3},{2,0},{3,1},{4,6},{5,7},{6,4},{7,5},{8,10},{9,11},{10,... | collective-permute-start | bytes 3145736 | tf_op jit(solution)/shard_map/ppermute | solution.py:28
  210.6 12.5 %collective-permute-start.27 = (bf16[2,32,4096]{2,1,0:T(8,128)(2,1)S(1)}, bf16[2,32,4096]{2,1,0:T(8,128)(2,1)S(1)}, u32[]{:S(2)}, u32[]{:S(2)}) collective-permute-start(bf16[2,32,4096]{2,1,0:T(8,128)(2,1)S(1)} %get-tuple-element.94), channel_id=1, source_target_pairs={{0,4},{1,5},{2,6},{3,7},{4,0},{5,1},{6,2},{7,3},{8,12},{9,13},{10,... | collective-permute-start | bytes 1572872 | tf_op jit(solution)/shard_map/ppermute | solution.py:28
  220.9 3.3 %collective-permute-start.26 = (bf16[256,1024]{1,0:T(8,128)(2,1)S(1)}, bf16[256,1024]{1,0:T(8,128)(2,1)S(1)}, u32[]{:S(2)}, u32[]{:S(2)}) collective-permute-start(bf16[256,1024]{1,0:T(8,128)(2,1)S(1)} %state_step.7.after_ref.own_ref), channel_id=1, source_target_pairs={{0,1},{1,0},{2,3},{3,2},{4,5},{5,4},{6,7},{7,6},{8,9},{9,8},{10,11... | collective-permute-start | bytes 1572872 | tf_op jit(solution)/shard_map/ppermute | solution.py:28
  223.2 13.2 %collective-permute-start.28 = (bf16[1,32,4096]{2,1,0:T(8,128)(2,1)S(1)}, bf16[1,32,4096]{2,1,0:T(8,128)(2,1)S(1)}, u32[]{:S(2)}, u32[]{:S(2)}) collective-permute-start(bf16[1,32,4096]{2,1,0:T(8,128)(2,1)S(1)} %get-tuple-element.97), channel_id=1, source_target_pairs={{0,8},{1,9},{2,10},{3,11},{4,12},{5,13},{6,14},{7,15},{8,0},{9,1},... | collective-permute-start | bytes 786440 | tf_op jit(solution)/shard_map/ppermute | solution.py:28
  232.7 28.7 %collective-permute-start.32 = (bf16[128,4096]{1,0:T(8,128)(2,1)S(1)}, bf16[128,4096]{1,0:T(8,128)(2,1)S(1)}, u32[]{:S(2)}, u32[]{:S(2)}) collective-permute-start(bf16[128,4096]{1,0:T(8,128)(2,1)S(1)} %get-tuple-element.105), channel_id=1, source_target_pairs={{0,2},{1,3},{2,0},{3,1},{4,6},{5,7},{6,4},{7,5},{8,10},{9,11},{10,... | collective-permute-start | bytes 3145736 | tf_op jit(solution)/shard_map/ppermute | solution.py:28
  236.7 12.4 %collective-permute-start.30 = (bf16[2,32,4096]{2,1,0:T(8,128)(2,1)S(1)}, bf16[2,32,4096]{2,1,0:T(8,128)(2,1)S(1)}, u32[]{:S(2)}, u32[]{:S(2)}) collective-permute-start(bf16[2,32,4096]{2,1,0:T(8,128)(2,1)S(1)} %get-tuple-element.101), channel_id=1, source_target_pairs={{0,4},{1,5},{2,6},{3,7},{4,0},{5,1},{6,2},{7,3},{8,12},{9,13},{10,... | collective-permute-start | bytes 1572872 | tf_op jit(solution)/shard_map/ppermute | solution.py:28
  249.2 12.0 %collective-permute-start.31 = (bf16[1,32,4096]{2,1,0:T(8,128)(2,1)S(1)}, bf16[1,32,4096]{2,1,0:T(8,128)(2,1)S(1)}, u32[]{:S(2)}, u32[]{:S(2)}) collective-permute-start(bf16[1,32,4096]{2,1,0:T(8,128)(2,1)S(1)} %get-tuple-element.103), channel_id=1, source_target_pairs={{0,8},{1,9},{2,10},{3,11},{4,12},{5,13},{6,14},{7,15},{8,0},{9,1},... | collective-permute-start | bytes 786440 | tf_op jit(solution)/shard_map/ppermute | solution.py:28
  261.6 13.2 %collective-permute-start.33 = (bf16[2,32,4096]{2,1,0:T(8,128)(2,1)S(1)}, bf16[2,32,4096]{2,1,0:T(8,128)(2,1)S(1)}, u32[]{:S(2)}, u32[]{:S(2)}) collective-permute-start(bf16[2,32,4096]{2,1,0:T(8,128)(2,1)S(1)} %get-tuple-element.107), channel_id=1, source_target_pairs={{0,4},{1,5},{2,6},{3,7},{4,0},{5,1},{6,2},{7,3},{8,12},{9,13},{10,... | collective-permute-start | bytes 1572872 | tf_op jit(solution)/shard_map/ppermute | solution.py:28
  274.9 13.2 %collective-permute-start.34 = (bf16[1,32,4096]{2,1,0:T(8,128)(2,1)S(1)}, bf16[1,32,4096]{2,1,0:T(8,128)(2,1)S(1)}, u32[]{:S(2)}, u32[]{:S(2)}) collective-permute-start(bf16[1,32,4096]{2,1,0:T(8,128)(2,1)S(1)} %get-tuple-element.109), channel_id=1, source_target_pairs={{0,8},{1,9},{2,10},{3,11},{4,12},{5,13},{6,14},{7,15},{8,0},{9,1},... | collective-permute-start | bytes 786440 | tf_op jit(solution)/shard_map/ppermute | solution.py:28
  276.4 11.9 %collective-permute-start.35 = (bf16[16,4096]{1,0:T(8,128)(2,1)S(1)}, bf16[16,4096]{1,0:T(8,128)(2,1)S(1)}, u32[]{:S(2)}, u32[]{:S(2)}) collective-permute-start(bf16[16,4096]{1,0:T(8,128)(2,1)S(1)} %get-tuple-element.111), channel_id=1, source_target_pairs={{0,1},{1,0},{2,3},{3,2},{4,5},{5,4},{6,7},{7,6},{8,9},{9,8},{10,11... | collective-permute-start | bytes 393224 | tf_op jit(solution)/shard_map/ppermute | solution.py:28
  276.4 11.9 %collective-permute-start.36 = (bf16[16,4096]{1,0:T(8,128)(2,1)S(1)}, bf16[16,4096]{1,0:T(8,128)(2,1)S(1)}, u32[]{:S(2)}, u32[]{:S(2)}) collective-permute-start(bf16[16,4096]{1,0:T(8,128)(2,1)S(1)} %get-tuple-element.112), channel_id=1, source_target_pairs={{0,1},{1,0},{2,3},{3,2},{4,5},{5,4},{6,7},{7,6},{8,9},{9,8},{10,11... | collective-permute-start | bytes 393224 | tf_op jit(solution)/shard_map/ppermute | solution.py:28
  276.9 11.4 %collective-permute-start.37 = (bf16[16,4096]{1,0:T(8,128)(2,1)S(1)}, bf16[16,4096]{1,0:T(8,128)(2,1)S(1)}, u32[]{:S(2)}, u32[]{:S(2)}) collective-permute-start(bf16[16,4096]{1,0:T(8,128)(2,1)S(1)} %get-tuple-element.113), channel_id=1, source_target_pairs={{0,1},{1,0},{2,3},{3,2},{4,5},{5,4},{6,7},{7,6},{8,9},{9,8},{10,11... | collective-permute-start | bytes 393224 | tf_op jit(solution)/shard_map/ppermute | solution.py:28
  288.2 1.4 collective-permute-start.38

commit v7 on v6

--- a/solution.py
+++ b/solution.py
@@ -235,7 +235,7 @@
         o_ref[...] = (keep_ref[at].astype(F32) + got_ref[at].astype(F32)).astype(BF16)
 
 
-def norm_kernel(me_ref, gain_ref, *refs):
+def norm_kernel(me_ref, after_ref, gain_ref, *refs):
     o_ref = refs[-1]
     total = refs[0][...].astype(F32)
     for ref in refs[1:-1]:
@@ -263,19 +263,19 @@
         o_ref[jnp.bitwise_xor(z, m)] = ref[...]
 
 
-def reduce_projection(send, keep, gain, me, after_y, after_z, n):
+def reduce_projection(send, keep, gain, me, after, n):
     zs = n // 4
     piece = keep.shape[1:]
     got = swap(send, 1, n)
-    send, keep = small(add_y_kernel, me, [keep, got], [(zs,) + piece] * 2, "add_y", after_y)
+    send, keep = small(add_y_kernel, me, [keep, got], [(zs,) + piece] * 2, "add_y")
     got = swap(send, 2, n)
-    cut = small(functools.partial(add_z_kernel, zs), me, [keep, got], [piece] * zs, "add_z", after_z)
+    cut = small(functools.partial(add_z_kernel, zs), me, [keep, got], [piece] * zs, "add_z")
     cut = [cut[0]] + [swap(cut[m], 4 * m, n) for m in range(1, zs)]
-    (low,) = small(norm_kernel, me, [gain] + cut, [piece], "norm")
+    (low,) = small(norm_kernel, me, [gain] + cut, [piece], "norm", after)
     lows = [low] + [swap(low, 4 * m, n) for m in range(1, zs)]
     (mine,) = small(merge_kernel, me, lows, [(zs,) + piece], "merge_z")
     beside = swap(mine, 2, n)
-    return keep, (mine, beside, swap(mine, 1, n), swap(beside, 1, n))
+    return cut[0], (mine, beside, swap(mine, 1, n), swap(beside, 1, n))
 
 
 def assemble_low(lows, index, low_scr, me_ref):
@@ -291,19 +291,39 @@
     return jnp.maximum(pre, 0.0) + jnp.log(1.0 + jnp.exp(-jnp.abs(pre)))
 
 
+def step_kernel(t, me_ref, after_ref, *refs):
+    *lows, dtp_ref, dtb_ref, step_ref, tail_ref, low_scr = refs
+    low = assemble_low(lows, t, low_scr, me_ref)
+    step_ref[...] = step_sizes(low, dtp_ref, dtb_ref)
+    tail_ref[...] = low[:, DT_RANK:].astype(F32)
+
+
+def step_rows(t, me, after, lows, dt_proj, dt_bias, rows, n):
+    return small(
+        functools.partial(step_kernel, t),
+        me,
+        [*lows, dt_proj, dt_bias],
+        [(rows, dt_proj.shape[1]), (rows, 128)],
+        "step_rows",
+        after,
+        F32,
+        [pltpu.VMEM((n // 4, 2, 2, rows // n, WIDE), BF16)],
+        12,
+    )
+
+
 def state_kernel(t, behind, me_ref, live_ref, *refs):
     first, last = t == 0, t == STEPS - 1
     refs = refs[behind:]
     if first:
         moved_ref, *refs = refs
-    lows, refs = refs[:4], refs[4:]
-    conv_ref, z_ref, dtp_ref, dtb_ref, alog_ref, skip_ref, state_ref, *refs = refs
+    step_ref, tail_ref, conv_ref, z_ref, alog_ref, skip_ref, state_ref, *refs = refs
     new_ref = None
     if not last:
         new_ref, *refs = refs
-    gated_ref, low_scr, step_scr, tail_scr, decay_scr, *refs = refs
+    gated_ref, decay_scr, bc_scr, *refs = refs
     block = pl.program_id(0)
-    rows, c = step_scr.shape
+    rows, c = step_ref.shape
     take = conv_ref.shape[0]
     blocks = rows // take
 
@@ -335,10 +355,7 @@
 
     @pl.when(block == 0)
     def _():
-        low = assemble_low(lows, t, low_scr, me_ref)
-        step_scr[...] = step_sizes(low, dtp_ref, dtb_ref)
         decay_scr[...] = -jnp.exp(alog_ref[...])
-        tail_scr[...] = low[:, DT_RANK:].astype(F32)
 
     base = block * take
     if first:
@@ -354,12 +371,14 @@
 
         lax.fori_loop(live_ref[0, block], live_ref[0, block + 1], replace, 0)
 
-    tall, lanes = 16, min(512, c)
+    tall, lanes = 16, min(256, c)
     for r in range(0, take, tall):
-        tail = tail_scr[pl.ds(base + r, tall), :]
+        tail = tail_ref[pl.ds(pl.multiple_of(base + r, tall), tall), :]
+        for s in range(2 * STATE):
+            bc_scr[s] = jnp.broadcast_to(tail[:, s : s + 1], (tall, 128))
         for l in range(0, c, lanes):
             cols = slice(l, l + lanes)
-            step = step_scr[pl.ds(base + r, tall), cols]
+            step = step_ref[pl.ds(pl.multiple_of(base + r, tall), tall), cols]
             conv = conv_ref[r : r + tall, cols]
             drive = step * conv
             total = skip_ref[:, cols] * conv
@@ -370,21 +389,21 @@
                     old = jnp.concatenate([buf[now, k, at, :] for k in tiles], axis=1)
                 else:
                     old = state_ref[s, r : r + tall, cols].astype(F32)
-                state = jnp.exp(step * decay_scr[s : s + 1, cols]) * old + drive * tail[:, s : s + 1]
+                b = jnp.concatenate([bc_scr[s]] * (lanes // 128), axis=1)
+                g = jnp.concatenate([bc_scr[STATE + s]] * (lanes // 128), axis=1)
+                state = jnp.exp(step * decay_scr[s : s + 1, cols]) * old + drive * b
                 if not last:
                     new_ref[s, r : r + tall, cols] = state.astype(BF16)
-                total = total + state * tail[:, STATE + s : STATE + s + 1]
+                total = total + state * g
             z = z_ref[0, r : r + tall, cols].astype(F32)
             gated_ref[r : r + tall, cols] = (total * (z * sigmoid(z))).astype(BF16)
 
 
-def state_step(t, me, live, moved, after, lows, conv, step_z, dt_proj, dt_bias, a_log, d_skip, state, n):
+def state_step(t, me, live, moved, after, steps, conv, step_z, a_log, d_skip, state, n):
     _, rows, c = conv.shape
     take = 2 * rows // n
     blocks = rows // take
     first, last = t == 0, t == STEPS - 1
-    own = rows // n
-    zs = n // 4
 
     def placed(i, me_ref, live_ref):
         z, y = i // 2, i % 2
@@ -392,19 +411,15 @@
         return (mine * (blocks // 2) + z, 0)
 
     vmem = pl.BlockSpec(memory_space=pltpu.VMEM)
-    in_specs = [vmem] * len(moved) + [vmem] * 4 + [
+    in_specs = [vmem] * len(moved) + [vmem] * 2 + [
         pl.BlockSpec((None, take, c), lambda i, *_: (t, i, 0)),
         pl.BlockSpec((1, take, c), lambda i, *_: (t, i, 0)),
-        whole(dt_proj.shape),
-        whole((1, c)),
         whole(a_log.shape),
         whole((1, c)),
     ]
     scratch = [
-        pltpu.VMEM((zs, 2, 2, own, WIDE), BF16),
-        pltpu.VMEM((rows, c), F32),
-        pltpu.VMEM((rows, 128), F32),
         pltpu.VMEM((STATE, c), F32),
+        pltpu.VMEM((2 * STATE, 16, 128), F32),
     ]
     flat = pl.BlockSpec((STATE, take, c), lambda i, *_: (0, i, 0))
     if first:
@@ -435,7 +450,7 @@
         compiler_params=params(48),
         cost_estimate=cost(8 * size, 4 * size, size),
         name="state_step",
-    )(me, live, *after, *moved, *lows, conv, step_z, dt_proj, dt_bias, a_log, d_skip, state)
+    )(me, live, *after, *moved, *steps, conv, step_z, a_log, d_skip, state)
     return (None, out[0]) if last else (out[0], out[1])
 
 
@@ -547,7 +562,7 @@
     me = me_scalar.reshape(1)
 
     moved_conv = exchange_conv(prefilled_conv, me, n)
-    packed = pack_state(tuple(moved_conv[1:]), prefilled_state, n)
+    packed = pack_state((moved_conv[1],), prefilled_state, n)
     moved_state = lax.all_to_all(packed, "dex", 0, 0, tiled=True).reshape(n * slots, STATE, c)
     cols = out_weight.shape[1] // 2
 
@@ -577,7 +592,7 @@
     conv, send, keep = conv_steps(
         tuple(range(STEPS)), n, me, (packed,), spread, old, moved_conv, step_x, conv_weight, bias, proj
     )
-    behind, lows = reduce_projection(send, keep, gain, me, (), (), n)
+    behind, lows = reduce_projection(send, keep, gain, me, (moved_state,), n)
     other_weight = swap(weight_half(me, behind, out_weight), 1, n)
 
     state = resident_state.reshape(rows * STATE, c)
@@ -587,12 +602,20 @@
 
     rate_bias, skip = dt_bias.reshape(1, c), d_skip.reshape(1, c)
 
+    next_steps = None
+
     def s_step(t, after):
-        nonlocal state
-        state, gated[t] = state_step(
-            t, me, live, (moved_state,) if t == 0 else (), after, lows, conv, step_z, dt_proj, rate_bias, a_log, skip, state, n
-        )
-        return gated[t]
+        nonlocal state, next_steps
+        if t == 0:
+            steps = step_rows(0, me, (after,), lows, dt_proj, rate_bias, rows, n)
+        else:
+            steps = next_steps
+        moved = (moved_state,) if t == 0 else ()
+        state, gated[t] = state_step(t, me, live, moved, (after,), steps, conv, step_z, a_log, skip, state, n)
+        if t == STEPS - 1:
+            return gated[t]
+        next_steps = step_rows(t + 1, me, (gated[t],), lows, dt_proj, rate_bias, rows, n)
+        return next_steps[1]
 
     def project(t, after):
         sends[t], keeps[t] = out_project(me, gated[t], swap(gated[t], 1, n), out_weight, other_weight, (after,))
@@ -612,10 +635,10 @@
             sends[t] = swap(sends[t], 1, n)
         return keeps[t]
 
-    last = s_step(0, ())
+    last = s_step(0, moved_state)
     last = project(0, last)
     for t in range(1, STEPS):
-        last = s_step(t, (last,))
+        last = s_step(t, last)
         if t > 1:
             for stage in range(1, stages):
                 last = reduce(t - 2, stage, last)

time: 295 us -> 305 us (1.034)
  waiting for transfers between devices: 136 us -> 150 us
  local copies, waits for them, and re-layouts: 12.7 us -> 7.97 us
  Pallas kernels: 104 us -> 108 us
    ppermute x39, waiting for transfers between devices: 136 us -> 150 us  [swap(): return lax.ppermute(x, 'dex', [(i, i ^ mask) for i in range(n)])]
    pallas_call x18 -> x22, Pallas kernels: 2.34 us -> 9.39 us  [small(): pl.pallas_call(kernel, in_specs=[pl.BlockSpec(memory_space=pltpu.SMEM)] +...]
    unnamed x48 -> x38, local copies, waits for them, and re-layouts: 11.5 us -> 6.79 us
  transfers between devices with their start and end apart: 40 -> 40, of which waited for: 24 -> 23; matrix products, arithmetic and copies ran while one was open for 1% -> 1% of each run, Pallas kernels for 27% -> 28%
where the time goes in v7:
time: 305 us; the launch traced here: 303 us
  waiting for transfers between devices  150 us (49%)
  Pallas kernels  108 us (35%)
  starting transfers between devices  34.8 us (11%)
  local copies, waits for them, and re-layouts  7.97 us (3%)
    ppermute x39, waiting for transfers between devices, swap(): return lax.ppermute(x, 'dex', [(i, i ^ mask) for i in range(n)])  150 us
    pallas_call x4, Pallas kernels, state_step(): pl.pallas_call(functools.partial(state_kernel, t, len(after)), grid_spec=...  50.9 us
    pallas_call x4, Pallas kernels, out_project(): pl.pallas_call(out_kernel, grid_spec=pltpu.PrefetchScalarGridSpec(num_sca...  34.2 us
    ppermute x39, starting transfers between devices, swap(): return lax.ppermute(x, 'dex', [(i, i ^ mask) for i in range(n)])  30.6 us
    pallas_call x22, Pallas kernels, small(): pl.pallas_call(kernel, in_specs=[pl.BlockSpec(memory_space=pltpu.SMEM)] +...  9.39 us
    pallas_call x1, Pallas kernels, weight_half(): pl.pallas_call(half_kernel, grid_spec=pltpu.PrefetchScalarGridSpec(num_sc...  7.16 us
    unnamed x38, local copies, waits for them, and re-layouts  6.79 us
  transfers between devices with their start and end apart: 40, of which 23 were waited for; matrix products, arithmetic and copies ran while one was open for 1% of the time, Pallas kernels for 28%

profile of v7, /device:TPU:0, one launch (start us, length us, event | category | flops | bytes accessed | tf_op | source)
XLA Modules:
  0.0 303.2 jit_solution(3249858932635874660)
XLA Ops:
  0.0 1.2 copy-done.9
  1.3 3.0 collective-permute-start
  4.3 0.5 collective-permute-start.2
  4.9 0.7 reshape.103
  5.6 0.7 broadcast_select_fusion
  7.1 4.1 %collective-permute-done.3.refs_3_ = bf16[4,16,768]{2,1,0:T(8,128)(2,1)S(1)} collective-permute-done((bf16[4,16,768]{2,1,0:T(8,128)(2,1)S(1)}, bf16[4,16,768]{2,1,0:T(8,128)(2,1)S(1)}, u32[]{:S(2)}, u32[]{:S(2)}) %collective-permute-start.3) | collective-permute-done | bytes 98336 | tf_op jit(solution)/shard_map/ppermute | solution.py:28
  11.3 1.6 collective-permute-start.4
  12.9 2.6 collective-permute-start.5
  15.7 1.2 collective-permute-done.4.refs_0_.refs_1_
  16.9 2.2 copy-done.4
  19.1 0.6 pack_state.1.refs_4_
  19.7 2.9 collective-permute-done.5.refs_2_
  22.7 3.9 %conv_project.1 = (f32[4,256,1024]{2,1,0:T(8,128)S(1)}, bf16[8,4,16,640]{3,2,1,0:T(8,128)(2,1)S(1)}, bf16[8,4,16,640]{3,2,1,0:T(8,128)(2,1)S(1)}) custom-call(s32[1]{0:T(128)} %bitcast.me_ref, s32[4,256]{1,0:T(4,128)S(1)} %broadcast_select_fusion.1.target_ref, f32[3,256,1024]{2,1,0:T(8,128)S(1)} %bitcast.28, bf16[4,256,1024]{2,1,0:T(8,128)(2,1)S(1)} %copy-done.6, ...), custom_call_target="tpu_custom_call" | custom-call | flops 1024 | bytes 1024 | tf_op jit(solution)/shard_map/conv_project/pallas_call | solution.py:194
  26.6 2.1 copy-done
  28.6 2.1 collective-permute-done.7.refs_1_
  30.9 0.6 collective-permute-start.8
  31.5 9.2 %collective-permute-done.8.refs_1_ = bf16[4,4,16,640]{3,2,1,0:T(8,128)(2,1)S(1)} collective-permute-done((bf16[4,4,16,640]{3,2,1,0:T(8,128)(2,1)S(1)}, bf16[4,4,16,640]{3,2,1,0:T(8,128)(2,1)S(1)}, u32[]{:S(2)}, u32[]{:S(2)}) %collective-permute-start.8) | collective-permute-done | bytes 327712 | tf_op jit(solution)/shard_map/ppermute | solution.py:28
  40.7 0.7 add_z.1
  41.4 0.6 copy-done.10
  42.0 0.6 copy-done.16
  42.7 7.2 %weight_half.1 = bf16[1024,4096]{1,0:T(8,128)(2,1)} custom-call(s32[1]{0:T(128)} %bitcast.me_ref, bf16[4,16,640]{2,1,0:T(8,128)(2,1)} %copy-done.10, bf16[1024,8192]{1,0:T(8,128)(2,1)} %wown_ref.7), custom_call_target="tpu_custom_call" | custom-call | flops 1024 | bytes 1024 | tf_op jit(solution)/shard_map/weight_half/pallas_call | solution.py:129
  49.9 4.2 %all-to-all-start = ((bf16[16,64,1024]{2,1,0:T(8,128)(2,1)}), bf16[16,64,1024]{2,1,0:T(8,128)(2,1)S(1)}, u32[]{:S(2)}, u32[]{:S(2)}) async-start(bf16[16,64,1024]{2,1,0:T(8,128)(2,1)} %copy-done.2), calls=%async_computation | async-start | bytes 4194304 | tf_op jit(solution)/shard_map/all_to_all | solution.py:566
  54.1 2.0 collective-permute-start.9
  56.1 2.4 collective-permute-start.10
  58.6 32.4 %collective-permute-done.9.refs_1_ = bf16[4,16,640]{2,1,0:T(8,128)(2,1)S(1)} collective-permute-done((bf16[4,16,640]{2,1,0:T(8,128)(2,1)}, bf16[4,16,640]{2,1,0:T(8,128)(2,1)S(1)}, u32[]{:S(2)}, u32[]{:S(2)}) %collective-permute-start.9) | collective-permute-done | bytes 81952 | tf_op jit(solution)/shard_map/ppermute | solution.py:28
  91.0 17.9 %collective-permute-done.10.refs_2_ = bf16[4,16,640]{2,1,0:T(8,128)(2,1)S(1)} collective-permute-done((bf16[4,16,640]{2,1,0:T(8,128)(2,1)}, bf16[4,16,640]{2,1,0:T(8,128)(2,1)S(1)}, u32[]{:S(2)}, u32[]{:S(2)}) %collective-permute-start.10) | collective-permute-done | bytes 81952 | tf_op jit(solution)/shard_map/ppermute | solution.py:28
  109.1 1.5 collective-permute-start.14
  110.6 1.8 collective-permute-start.13
  112.4 1.1 collective-permute-start.12
  113.5 2.7 collective-permute-done.14.refs_3_
  116.2 3.5 %collective-permute-done.13.refs_2_ = bf16[4,16,640]{2,1,0:T(8,128)(2,1)S(1)} collective-permute-done((bf16[4,16,640]{2,1,0:T(8,128)(2,1)S(1)}, bf16[4,16,640]{2,1,0:T(8,128)(2,1)S(1)}, u32[]{:S(2)}, u32[]{:S(2)}) %collective-permute-start.13) | collective-permute-done | bytes 81952 | tf_op jit(solution)/shard_map/ppermute | solution.py:28
  119.7 1.6 collective-permute-start.15
  121.5 0.8 compare_select_fusion
  122.3 7.0 %collective-permute-done.15.refs_1_ = bf16[4,4,16,640]{3,2,1,0:T(8,128)(2,1)} collective-permute-done((bf16[4,4,16,640]{3,2,1,0:T(8,128)(2,1)S(1)}, bf16[4,4,16,640]{3,2,1,0:T(8,128)(2,1)}, u32[]{:S(2)}, u32[]{:S(2)}) %collective-permute-start.15) | collective-permute-done | bytes 327712 | tf_op jit(solution)/shard_map/ppermute | solution.py:28
  129.7 1.4 collective-permute-done.17.refs_3_
  131.1 1.6 step_rows.4
  132.8 17.1 %state_step.4 = (bf16[16,256,1024]{2,1,0:T(8,128)(2,1)}, bf16[256,1024]{1,0:T(8,128)(2,1)S(1)}) custom-call(s32[1]{0:T(128)} %bitcast.me_ref, s32[3,64]{1,0:T(4,128)S(1)} %pad_add_fusion.live_ref, bf16[64,16,1024]{2,1,0:T(8,128)(2,1)S(1)} %bitcast.22, bf16[64,16,1024]{2,1,0:T(8,128)(2,1)S(1)} %bitcast.23, f32[256,1024]{1,0:T(8,128)S(1)} %get-tuple-element.84.refs_2_, ...), custom_call_target="tpu_custom_call" | custom-call | flops 1024 | bytes 1024 | tf_op jit(solution)/shard_map/state_step/pallas_call | solution.py:440
  150.1 1.6 step_rows.5
  151.9 8.6 %out_project.4 = (bf16[128,4096]{1,0:T(8,128)(2,1)S(1)}, bf16[128,4096]{1,0:T(8,128)(2,1)S(1)}) custom-call(s32[1]{0:T(128)} %bitcast.me_ref, bf16[256,1024]{1,0:T(8,128)(2,1)S(1)} %get-tuple-element.87.after_ref.own_ref, bf16[256,1024]{1,0:T(8,128)(2,1)S(1)} %collective-permute-done.18.other_ref, bf16[1024,8192]{1,0:T(8,128)(2,1)} %wown_ref.7, ...), custom_call_target="tpu_custom_call" | custom-call | flops 1024 | bytes 1024 | tf_op jit(solution)/shard_map/out_project/pallas_call | solution.py:472
  160.4 1.7 collective-permute-start.21
  162.1 12.1 %state_step.5 = (bf16[16,256,1024]{2,1,0:T(8,128)(2,1)}, bf16[256,1024]{1,0:T(8,128)(2,1)S(1)}) custom-call(s32[1]{0:T(128)} %bitcast.me_ref, s32[3,64]{1,0:T(4,128)S(1)} %pad_add_fusion.live_ref, bf16[128,4096]{1,0:T(8,128)(2,1)S(1)} %get-tuple-element.89.refs_0_, f32[256,1024]{1,0:T(8,128)S(1)} %get-tuple-element.90.refs_1_, ...), custom_call_target="tpu_custom_call" | custom-call | flops 1024 | bytes 1024 | tf_op jit(solution)/shard_map/state_step/pallas_call | solution.py:440
  174.2 1.6 step_rows.6
  176.1 8.6 %out_project.5 = (bf16[128,4096]{1,0:T(8,128)(2,1)S(1)}, bf16[128,4096]{1,0:T(8,128)(2,1)S(1)}) custom-call(s32[1]{0:T(128)} %bitcast.me_ref, bf16[256,1024]{1,0:T(8,128)(2,1)S(1)} %get-tuple-element.92.after_ref.own_ref, bf16[256,1024]{1,0:T(8,128)(2,1)S(1)} %collective-permute-done.20.other_ref, bf16[1024,8192]{1,0:T(8,128)(2,1)} %wown_ref.7, ...), custom_call_target="tpu_custom_call" | custom-call | flops 1024 | bytes 1024 | tf_op jit(solution)/shard_map/out_project/pallas_call | solution.py:472
  185.1 0.7 collective-permute-done.21
  186.1 12.1 %state_step.6 = (bf16[16,256,1024]{2,1,0:T(8,128)(2,1)}, bf16[256,1024]{1,0:T(8,128)(2,1)S(1)}) custom-call(s32[1]{0:T(128)} %bitcast.me_ref, s32[3,64]{1,0:T(4,128)S(1)} %pad_add_fusion.live_ref, bf16[2,32,4096]{2,1,0:T(8,128)(2,1)S(1)} %get-tuple-element.96.refs_0_.keep_ref, f32[256,1024]{1,0:T(8,128)S(1)} %get-tuple-element.97.refs_1_, ...), custom_call_target="tpu_custom_call" | custom-call | flops 1024 | bytes 1024 | tf_op jit(solution)/shard_map/state_step/pallas_call | solution.py:440
  198.2 1.6 step_rows.7
  200.0 1.9 collective-permute-start.24
  201.9 8.6 %out_project.6 = (bf16[128,4096]{1,0:T(8,128)(2,1)S(1)}, bf16[128,4096]{1,0:T(8,128)(2,1)S(1)}) custom-call(s32[1]{0:T(128)} %bitcast.me_ref, bf16[256,1024]{1,0:T(8,128)(2,1)S(1)} %get-tuple-element.99.after_ref.own_ref, bf16[256,1024]{1,0:T(8,128)(2,1)S(1)} %collective-permute-done.22.other_ref, bf16[1024,8192]{1,0:T(8,128)(2,1)} %wown_ref.7, ...), custom_call_target="tpu_custom_call" | custom-call | flops 1024 | bytes 1024 | tf_op jit(solution)/shard_map/out_project/pallas_call | solution.py:472
  210.4 1.5 collective-permute-start.29
  211.9 3.4 %collective-permute-done.24.got_ref = bf16[1,32,4096]{2,1,0:T(8,128)(2,1)S(1)} collective-permute-done((bf16[1,32,4096]{2,1,0:T(8,128)(2,1)S(1)}, bf16[1,32,4096]{2,1,0:T(8,128)(2,1)S(1)}, u32[]{:S(2)}, u32[]{:S(2)}) %collective-permute-start.24) | collective-permute-done | bytes 262176 | tf_op jit(solution)/shard_map/ppermute | solution.py:28
  215.7 9.6 %state_step.7.after_ref.own_ref = bf16[256,1024]{1,0:T(8,128)(2,1)S(1)} custom-call(s32[1]{0:T(128)} %bitcast.me_ref, s32[3,64]{1,0:T(4,128)S(1)} %pad_add_fusion.live_ref, bf16[2,32,4096]{2,1,0:T(8,128)(2,1)S(1)} %get-tuple-element.107.refs_0_.keep_ref, f32[256,1024]{1,0:T(8,128)S(1)} %get-tuple-element.108.refs_1_, ...), custom_call_target="tpu_custom_call" | custom-call | flops 1024 | bytes 1024 | tf_op jit(solution)/shard_map/state_step/pallas_call | solution.py:440
  225.4 3.8 %collective-permute-done.27.got_ref = bf16[2,32,4096]{2,1,0:T(8,128)(2,1)S(1)} collective-permute-done((bf16[2,32,4096]{2,1,0:T(8,128)(2,1)S(1)}, bf16[2,32,4096]{2,1,0:T(8,128)(2,1)S(1)}, u32[]{:S(2)}, u32[]{:S(2)}) %collective-permute-start.27) | collective-permute-done | bytes 524320 | tf_op jit(solution)/shard_map/ppermute | solution.py:28
  229.4 0.8 collective-permute-start.28
  230.2 8.6 %out_project.7 = (bf16[128,4096]{1,0:T(8,128)(2,1)S(1)}, bf16[128,4096]{1,0:T(8,128)(2,1)S(1)}) custom-call(s32[1]{0:T(128)} %bitcast.me_ref, bf16[256,1024]{1,0:T(8,128)(2,1)S(1)} %state_step.7.after_ref.own_ref, bf16[256,1024]{1,0:T(8,128)(2,1)S(1)} %collective-permute-done.26.other_ref, bf16[1024,8192]{1,0:T(8,128)(2,1)} %wown_ref.7, ...), custom_call_target="tpu_custom_call" | custom-call | flops 1024 | bytes 1024 | tf_op jit(solution)/shard_map/out_project/pallas_call | solution.py:472
  238.8 1.6 collective-permute-start.32
  240.4 2.6 collective-permute-done.28.got_ref
  243.4 13.8 %collective-permute-done.30.got_ref = bf16[2,32,4096]{2,1,0:T(8,128)(2,1)S(1)} collective-permute-done((bf16[2,32,4096]{2,1,0:T(8,128)(2,1)S(1)}, bf16[2,32,4096]{2,1,0:T(8,128)(2,1)S(1)}, u32[]{:S(2)}, u32[]{:S(2)}) %collective-permute-start.30) | collective-permute-done | bytes 524320 | tf_op jit(solution)/shard_map/ppermute | solution.py:28
  257.3 1.1 collective-permute-start.31
  258.4 12.8 %collective-permute-done.31.got_ref = bf16[1,32,4096]{2,1,0:T(8,128)(2,1)S(1)} collective-permute-done((bf16[1,32,4096]{2,1,0:T(8,128)(2,1)S(1)}, bf16[1,32,4096]{2,1,0:T(8,128)(2,1)S(1)}, u32[]{:S(2)}, u32[]{:S(2)}) %collective-permute-start.31) | collective-permute-done | bytes 262176 | tf_op jit(solution)/shard_map/ppermute | solution.py:28
  271.7 13.8 %collective-permute-done.33.got_ref = bf16[2,32,4096]{2,1,0:T(8,128)(2,1)S(1)} collective-permute-done((bf16[2,32,4096]{2,1,0:T(8,128)(2,1)S(1)}, bf16[2,32,4096]{2,1,0:T(8,128)(2,1)S(1)}, u32[]{:S(2)}, u32[]{:S(2)}) %collective-permute-start.33) | collective-permute-done | bytes 524320 | tf_op jit(solution)/shard_map/ppermute | solution.py:28
  285.6 1.1 collective-permute-start.34
  287.2 12.3 %collective-permute-done.34.got_ref = bf16[1,32,4096]{2,1,0:T(8,128)(2,1)S(1)} collective-permute-done((bf16[1,32,4096]{2,1,0:T(8,128)(2,1)S(1)}, bf16[1,32,4096]{2,1,0:T(8,128)(2,1)S(1)}, u32[]{:S(2)}, u32[]{:S(2)}) %collective-permute-start.34) | collective-permute-done | bytes 262176 | tf_op jit(solution)/shard_map/ppermute | solution.py:28
  299.7 1.3 collective-permute-done.38.refs_7_
  301.0 2.2 final_join.1
  (104 shorter events, 6.2 us)
Async XLA Ops:
  0.0 22.6 %copy-start.7 = (bf16[1024,544]{0,1:T(8,128)(2,1)S(1)}, bf16[1024,544]{0,1:T(8,128)(2,1)}, u32[]{:S(2)}) copy-start(bf16[1024,544]{0,1:T(8,128)(2,1)} %param.27) | copy-start | bytes 3342340
  0.0 1.2 copy-start.9
  1.2 21.4 %copy-start.14 = (f32[4,1024]{1,0:T(4,128)S(1)}, f32[4,1024]{1,0:T(4,128)}, u32[]{:S(2)}) copy-start(f32[4,1024]{1,0:T(4,128)} %w_ref.2) | copy-start | bytes 49156
  1.2 21.4 %copy-start.15 = (f32[1024]{0:T(1024)S(1)}, f32[1024]{0:T(1024)}, u32[]{:S(2)}) copy-start(f32[1024]{0:T(1024)} %param.26) | copy-start | bytes 12292
  1.3 5.8 %collective-permute-start = (bf16[4,16,768]{2,1,0:T(8,128)(2,1)S(1)}, bf16[4,16,768]{2,1,0:T(8,128)(2,1)S(1)}, u32[]{:S(2)}, u32[]{:S(2)}) collective-permute-start(bf16[4,16,768]{2,1,0:T(8,128)(2,1)S(1)} %get-tuple-element.69), channel_id=1, source_target_pairs={{0,2},{1,3},{2,0},{3,1},{4,6},{5,7},{6,4},{7,5},{8,10},{9,11},{10,... | collective-permute-start | bytes 294920 | tf_op jit(solution)/shard_map/ppermute | solution.py:28
  4.3 2.8 collective-permute-start.1
  4.3 2.1 collective-permute-start.2
  6.5 4.8 %collective-permute-start.3 = (bf16[4,16,768]{2,1,0:T(8,128)(2,1)S(1)}, bf16[4,16,768]{2,1,0:T(8,128)(2,1)S(1)}, u32[]{:S(2)}, u32[]{:S(2)}) collective-permute-start(bf16[4,16,768]{2,1,0:T(8,128)(2,1)S(1)} %collective-permute-done.2), channel_id=1, source_target_pairs={{0,2},{1,3},{2,0},{3,1},{4,6},{5,7},{6,4},{7,5},{8,10},{9,11},{10,... | collective-permute-start | bytes 294920 | tf_op jit(solution)/shard_map/ppermute | solution.py:28
  11.3 5.7 %collective-permute-start.4 = (bf16[4,16,768]{2,1,0:T(8,128)(2,1)S(1)}, bf16[4,16,768]{2,1,0:T(8,128)(2,1)S(1)}, u32[]{:S(2)}, u32[]{:S(2)}) collective-permute-start(bf16[4,16,768]{2,1,0:T(8,128)(2,1)S(1)} %get-tuple-element.72), channel_id=1, source_target_pairs={{0,4},{1,5},{2,6},{3,7},{4,0},{5,1},{6,2},{7,3},{8,12},{9,13},{10,... | collective-permute-start | bytes 294920 | tf_op jit(solution)/shard_map/ppermute | solution.py:28
  12.9 9.7 %collective-permute-start.5 = (bf16[4,16,768]{2,1,0:T(8,128)(2,1)S(1)}, bf16[4,16,768]{2,1,0:T(8,128)(2,1)S(1)}, u32[]{:S(2)}, u32[]{:S(2)}) collective-permute-start(bf16[4,16,768]{2,1,0:T(8,128)(2,1)S(1)} %get-tuple-element.74), channel_id=1, source_target_pairs={{0,8},{1,9},{2,10},{3,11},{4,12},{5,13},{6,14},{7,15},{8,0},{9,1},... | collective-permute-start | bytes 294920 | tf_op jit(solution)/shard_map/ppermute | solution.py:28
  15.5 7.1 %collective-permute-start.6 = (bf16[4,16,768]{2,1,0:T(8,128)(2,1)S(1)}, bf16[4,16,768]{2,1,0:T(8,128)(2,1)S(1)}, u32[]{:S(2)}, u32[]{:S(2)}) collective-permute-start(bf16[4,16,768]{2,1,0:T(8,128)(2,1)S(1)} %get-tuple-element.75), channel_id=1, source_target_pairs={{0,12},{1,13},{2,14},{3,15},{4,8},{5,9},{6,10},{7,11},{8,4},{9,5},... | collective-permute-start | bytes 294920 | tf_op jit(solution)/shard_map/ppermute | solution.py:28
  16.9 2.2 copy-start.4
  19.1 3.5 %copy-start.5 = (f32[256,3,1024]{2,0,1:T(8,128)S(1)}, f32[256,3,1024]{2,0,1:T(8,128)}, u32[]{:S(2)}) copy-start(f32[256,3,1024]{2,0,1:T(8,128)} %param.18) | copy-start | bytes 9437188
  19.1 3.6 %copy-start.6 = (bf16[4,256,1024]{2,1,0:T(8,128)(2,1)S(1)}, bf16[4,256,1024]{2,1,0:T(8,128)(2,1)}, u32[]{:S(2)}) copy-start(bf16[4,256,1024]{2,1,0:T(8,128)(2,1)} %x_ref.3) | copy-start | bytes 6291460
  19.7 6.9 %copy-start.2 = (bf16[16,64,1024]{2,1,0:T(8,128)(2,1)}, bf16[16,64,1024]{2,1,0:T(8,128)(2,1)S(1)}, u32[]{:S(2)}) copy-start(bf16[16,64,1024]{2,1,0:T(8,128)(2,1)S(1)} %pack_state.1.refs_4_) | copy-start | bytes 6291460
  26.6 2.1 copy-start
  28.6 2.1 collective-permute-start.7
  30.9 9.8 %collective-permute-start.8 = (bf16[4,4,16,640]{3,2,1,0:T(8,128)(2,1)S(1)}, bf16[4,4,16,640]{3,2,1,0:T(8,128)(2,1)S(1)}, u32[]{:S(2)}, u32[]{:S(2)}) collective-permute-start(bf16[4,4,16,640]{3,2,1,0:T(8,128)(2,1)S(1)} %get-tuple-element.79), channel_id=1, source_target_pairs={{0,2},{1,3},{2,0},{3,1},{4,6},{5,7},{6,4},{7,5},{8,10},{9,11},{10,... | collective-permute-start | bytes 983048 | tf_op jit(solution)/shard_map/ppermute | solution.py:28
  41.4 0.6 copy-start.10
  42.0 0.6 copy-start.16
  49.8 8.8 %copy-start.17 = (f32[544]{0:T(1024)S(1)}, f32[544]{0:T(1024)}, u32[]{:S(2)}) copy-start(f32[544]{0:T(1024)} %param.28) | copy-start | bytes 6532
  49.8 59.1 %copy-start.11 = (bf16[4,16,640]{2,1,0:T(8,128)(2,1)S(1)}, bf16[4,16,640]{2,1,0:T(8,128)(2,1)}, u32[]{:S(2)}) copy-start(bf16[4,16,640]{2,1,0:T(8,128)(2,1)} %copy-done.10) | copy-start | bytes 245764
  49.8 71.5 %copy-start.18 = (s32[16]{0:T(128)S(1)}, s32[16]{0:T(128)}, u32[]{:S(2)}) copy-start(s32[16]{0:T(128)} %param.21) | copy-start | bytes 196
  49.8 81.3 %copy-start.3 = (bf16[512,1024]{1,0:T(8,128)(2,1)S(1)}, bf16[512,1024]{1,0:T(8,128)(2,1)}, u32[]{:S(2)}) copy-start(bf16[512,1024]{1,0:T(8,128)(2,1)} %refs_4_.12) | copy-start | bytes 3145732
  49.8 81.3 %copy-start.12 = (f32[1024]{0:T(1024)S(1)}, f32[1024]{0:T(1024)}, u32[]{:S(2)}) copy-start(f32[1024]{0:T(1024)} %param.30) | copy-start | bytes 12292
  49.8 102.0 %collective-permute-start.19 = (bf16[1024,4096]{1,0:T(8,128)(2,1)}, bf16[1024,4096]{1,0:T(8,128)(2,1)}, u32[]{:S(2)}, u32[]{:S(2)}) collective-permute-start(bf16[1024,4096]{1,0:T(8,128)(2,1)} %weight_half.1), channel_id=1, source_target_pairs={{0,1},{1,0},{2,3},{3,2},{4,5},{5,4},{6,7},{7,6},{8,9},{9,8},{10,11... | collective-permute-start | bytes 25165832 | tf_op jit(solution)/shard_map/ppermute | solution.py:28
  49.9 59.0 %all-to-all-start = ((bf16[16,64,1024]{2,1,0:T(8,128)(2,1)}), bf16[16,64,1024]{2,1,0:T(8,128)(2,1)S(1)}, u32[]{:S(2)}, u32[]{:S(2)}) async-start(bf16[16,64,1024]{2,1,0:T(8,128)(2,1)} %copy-done.2), calls=%async_computation | async-start | bytes 4194304 | tf_op jit(solution)/shard_map/all_to_all | solution.py:566
  54.1 78.6 %copy-start.8 = (f32[16,1024]{1,0:T(8,128)S(1)}, f32[16,1024]{1,0:T(8,128)}, u32[]{:S(2)}) copy-start(f32[16,1024]{1,0:T(8,128)} %refs_5_.7) | copy-start | bytes 196612
  54.1 78.6 %copy-start.13 = (f32[1024]{0:T(1024)S(1)}, f32[1024]{0:T(1024)}, u32[]{:S(2)}) copy-start(f32[1024]{0:T(1024)} %param.32) | copy-start | bytes 12292
  54.1 36.9 %collective-permute-start.9 = (bf16[4,16,640]{2,1,0:T(8,128)(2,1)}, bf16[4,16,640]{2,1,0:T(8,128)(2,1)S(1)}, u32[]{:S(2)}, u32[]{:S(2)}) collective-permute-start(bf16[4,16,640]{2,1,0:T(8,128)(2,1)} %get-tuple-element.81), channel_id=1, source_target_pairs={{0,4},{1,5},{2,6},{3,7},{4,0},{5,1},{6,2},{7,3},{8,12},{9,13},{10,... | collective-permute-start | bytes 245768 | tf_op jit(solution)/shard_map/ppermute | solution.py:28
  56.1 52.8 %collective-permute-start.10 = (bf16[4,16,640]{2,1,0:T(8,128)(2,1)}, bf16[4,16,640]{2,1,0:T(8,128)(2,1)S(1)}, u32[]{:S(2)}, u32[]{:S(2)}) collective-permute-start(bf16[4,16,640]{2,1,0:T(8,128)(2,1)} %get-tuple-element.82), channel_id=1, source_target_pairs={{0,8},{1,9},{2,10},{3,11},{4,12},{5,13},{6,14},{7,15},{8,0},{9,1},... | collective-permute-start | bytes 245768 | tf_op jit(solution)/shard_map/ppermute | solution.py:28
  58.5 50.4 %collective-permute-start.11 = (bf16[4,16,640]{2,1,0:T(8,128)(2,1)}, bf16[4,16,640]{2,1,0:T(8,128)(2,1)S(1)}, u32[]{:S(2)}, u32[]{:S(2)}) collective-permute-start(bf16[4,16,640]{2,1,0:T(8,128)(2,1)} %copy-done.16), channel_id=1, source_target_pairs={{0,12},{1,13},{2,14},{3,15},{4,8},{5,9},{6,10},{7,11},{8,4},{9,5},... | collective-permute-start | bytes 245768 | tf_op jit(solution)/shard_map/ppermute | solution.py:28
  109.1 7.1 %collective-permute-start.14 = (bf16[4,16,640]{2,1,0:T(8,128)(2,1)S(1)}, bf16[4,16,640]{2,1,0:T(8,128)(2,1)S(1)}, u32[]{:S(2)}, u32[]{:S(2)}) collective-permute-start(bf16[4,16,640]{2,1,0:T(8,128)(2,1)S(1)} %norm.1.refs_0_), channel_id=1, source_target_pairs={{0,12},{1,13},{2,14},{3,15},{4,8},{5,9},{6,10},{7,11},{8,4},{9,5},... | collective-permute-start | bytes 245768 | tf_op jit(solution)/shard_map/ppermute | solution.py:28
  110.6 9.1 %collective-permute-start.13 = (bf16[4,16,640]{2,1,0:T(8,128)(2,1)S(1)}, bf16[4,16,640]{2,1,0:T(8,128)(2,1)S(1)}, u32[]{:S(2)}, u32[]{:S(2)}) collective-permute-start(bf16[4,16,640]{2,1,0:T(8,128)(2,1)S(1)} %norm.1.refs_0_), channel_id=1, source_target_pairs={{0,8},{1,9},{2,10},{3,11},{4,12},{5,13},{6,14},{7,15},{8,0},{9,1},... | collective-permute-start | bytes 245768 | tf_op jit(solution)/shard_map/ppermute | solution.py:28
  112.4 7.2 %collective-permute-start.12 = (bf16[4,16,640]{2,1,0:T(8,128)(2,1)S(1)}, bf16[4,16,640]{2,1,0:T(8,128)(2,1)S(1)}, u32[]{:S(2)}, u32[]{:S(2)}) collective-permute-start(bf16[4,16,640]{2,1,0:T(8,128)(2,1)S(1)} %norm.1.refs_0_), channel_id=1, source_target_pairs={{0,4},{1,5},{2,6},{3,7},{4,0},{5,1},{6,2},{7,3},{8,12},{9,13},{10,... | collective-permute-start | bytes 245768 | tf_op jit(solution)/shard_map/ppermute | solution.py:28
  119.7 9.6 %collective-permute-start.15 = (bf16[4,4,16,640]{3,2,1,0:T(8,128)(2,1)S(1)}, bf16[4,4,16,640]{3,2,1,0:T(8,128)(2,1)}, u32[]{:S(2)}, u32[]{:S(2)}) collective-permute-start(bf16[4,4,16,640]{3,2,1,0:T(8,128)(2,1)S(1)} %merge_z.1.refs_0_), channel_id=1, source_target_pairs={{0,2},{1,3},{2,0},{3,1},{4,6},{5,7},{6,4},{7,5},{8,10},{9,11},{10,... | collective-permute-start | bytes 983048 | tf_op jit(solution)/shard_map/ppermute | solution.py:28
  121.5 11.3 %copy-start.1 = (bf16[4,256,1024]{2,1,0:T(8,128)(2,1)S(1)}, bf16[4,256,1024]{2,1,0:T(8,128)(2,1)}, u32[]{:S(2)}) copy-start(bf16[4,256,1024]{2,1,0:T(8,128)(2,1)} %refs_4_.13) | copy-start | bytes 6291460
  122.3 7.4 %collective-permute-start.16 = (bf16[4,4,16,640]{3,2,1,0:T(8,128)(2,1)S(1)}, bf16[4,4,16,640]{3,2,1,0:T(8,128)(2,1)S(1)}, u32[]{:S(2)}, u32[]{:S(2)}) collective-permute-start(bf16[4,4,16,640]{3,2,1,0:T(8,128)(2,1)S(1)} %merge_z.1.refs_0_), channel_id=1, source_target_pairs={{0,1},{1,0},{2,3},{3,2},{4,5},{5,4},{6,7},{7,6},{8,9},{9,8},{10,11... | collective-permute-start | bytes 983048 | tf_op jit(solution)/shard_map/ppermute | solution.py:28
  129.3 1.8 collective-permute-start.17
  149.9 2.0 collective-permute-start.18
  160.4 25.4 %collective-permute-start.21 = (bf16[128,4096]{1,0:T(8,128)(2,1)S(1)}, bf16[128,4096]{1,0:T(8,128)(2,1)S(1)}, u32[]{:S(2)}, u32[]{:S(2)}) collective-permute-start(bf16[128,4096]{1,0:T(8,128)(2,1)S(1)} %get-tuple-element.95), channel_id=1, source_target_pairs={{0,2},{1,3},{2,0},{3,1},{4,6},{5,7},{6,4},{7,5},{8,10},{9,11},{10,... | collective-permute-start | bytes 3145736 | tf_op jit(solution)/shard_map/ppermute | solution.py:28
  174.2 1.9 collective-permute-start.20
  184.6 30.7 %collective-permute-start.25 = (bf16[128,4096]{1,0:T(8,128)(2,1)S(1)}, bf16[128,4096]{1,0:T(8,128)(2,1)S(1)}, u32[]{:S(2)}, u32[]{:S(2)}) collective-permute-start(bf16[128,4096]{1,0:T(8,128)(2,1)S(1)} %get-tuple-element.106), channel_id=1, source_target_pairs={{0,2},{1,3},{2,0},{3,1},{4,6},{5,7},{6,4},{7,5},{8,10},{9,11},{10,... | collective-permute-start | bytes 3145736 | tf_op jit(solution)/shard_map/ppermute | solution.py:28
  186.1 13.8 %collective-permute-start.23 = (bf16[2,32,4096]{2,1,0:T(8,128)(2,1)S(1)}, bf16[2,32,4096]{2,1,0:T(8,128)(2,1)S(1)}, u32[]{:S(2)}, u32[]{:S(2)}) collective-permute-start(bf16[2,32,4096]{2,1,0:T(8,128)(2,1)S(1)} %get-tuple-element.101), channel_id=1, source_target_pairs={{0,4},{1,5},{2,6},{3,7},{4,0},{5,1},{6,2},{7,3},{8,12},{9,13},{10,... | collective-permute-start | bytes 1572872 | tf_op jit(solution)/shard_map/ppermute | solution.py:28
  198.2 3.6 %collective-permute-start.22 = (bf16[256,1024]{1,0:T(8,128)(2,1)S(1)}, bf16[256,1024]{1,0:T(8,128)(2,1)S(1)}, u32[]{:S(2)}, u32[]{:S(2)}) collective-permute-start(bf16[256,1024]{1,0:T(8,128)(2,1)S(1)} %get-tuple-element.99.after_ref.own_ref), channel_id=1, source_target_pairs={{0,1},{1,0},{2,3},{3,2},{4,5},{5,4},{6,7},{7,6},{8,9},{9,8},{10,11... | collective-permute-start | bytes 1572872 | tf_op jit(solution)/shard_map/ppermute | solution.py:28
  200.0 15.3 %collective-permute-start.24 = (bf16[1,32,4096]{2,1,0:T(8,128)(2,1)S(1)}, bf16[1,32,4096]{2,1,0:T(8,128)(2,1)S(1)}, u32[]{:S(2)}, u32[]{:S(2)}) collective-permute-start(bf16[1,32,4096]{2,1,0:T(8,128)(2,1)S(1)} %get-tuple-element.104), channel_id=1, source_target_pairs={{0,8},{1,9},{2,10},{3,11},{4,12},{5,13},{6,14},{7,15},{8,0},{9,1},... | collective-permute-start | bytes 786440 | tf_op jit(solution)/shard_map/ppermute | solution.py:28
  210.4 32.7 %collective-permute-start.29 = (bf16[128,4096]{1,0:T(8,128)(2,1)S(1)}, bf16[128,4096]{1,0:T(8,128)(2,1)S(1)}, u32[]{:S(2)}, u32[]{:S(2)}) collective-permute-start(bf16[128,4096]{1,0:T(8,128)(2,1)S(1)} %get-tuple-element.115), channel_id=1, source_target_pairs={{0,2},{1,3},{2,0},{3,1},{4,6},{5,7},{6,4},{7,5},{8,10},{9,11},{10,... | collective-permute-start | bytes 3145736 | tf_op jit(solution)/shard_map/ppermute | solution.py:28
  215.6 13.6 %collective-permute-start.27 = (bf16[2,32,4096]{2,1,0:T(8,128)(2,1)S(1)}, bf16[2,32,4096]{2,1,0:T(8,128)(2,1)S(1)}, u32[]{:S(2)}, u32[]{:S(2)}) collective-permute-start(bf16[2,32,4096]{2,1,0:T(8,128)(2,1)S(1)} %get-tuple-element.110), channel_id=1, source_target_pairs={{0,4},{1,5},{2,6},{3,7},{4,0},{5,1},{6,2},{7,3},{8,12},{9,13},{10,... | collective-permute-start | bytes 1572872 | tf_op jit(solution)/shard_map/ppermute | solution.py:28
  225.3 4.9 %collective-permute-start.26 = (bf16[256,1024]{1,0:T(8,128)(2,1)S(1)}, bf16[256,1024]{1,0:T(8,128)(2,1)S(1)}, u32[]{:S(2)}, u32[]{:S(2)}) collective-permute-start(bf16[256,1024]{1,0:T(8,128)(2,1)S(1)} %state_step.7.after_ref.own_ref), channel_id=1, source_target_pairs={{0,1},{1,0},{2,3},{3,2},{4,5},{5,4},{6,7},{7,6},{8,9},{9,8},{10,11... | collective-permute-start | bytes 1572872 | tf_op jit(solution)/shard_map/ppermute | solution.py:28
  229.4 13.6 %collective-permute-start.28 = (bf16[1,32,4096]{2,1,0:T(8,128)(2,1)S(1)}, bf16[1,32,4096]{2,1,0:T(8,128)(2,1)S(1)}, u32[]{:S(2)}, u32[]{:S(2)}) collective-permute-start(bf16[1,32,4096]{2,1,0:T(8,128)(2,1)S(1)} %get-tuple-element.113), channel_id=1, source_target_pairs={{0,8},{1,9},{2,10},{3,11},{4,12},{5,13},{6,14},{7,15},{8,0},{9,1},... | collective-permute-start | bytes 786440 | tf_op jit(solution)/shard_map/ppermute | solution.py:28
  238.8 32.6 %collective-permute-start.32 = (bf16[128,4096]{1,0:T(8,128)(2,1)S(1)}, bf16[128,4096]{1,0:T(8,128)(2,1)S(1)}, u32[]{:S(2)}, u32[]{:S(2)}) collective-permute-start(bf16[128,4096]{1,0:T(8,128)(2,1)S(1)} %get-tuple-element.121), channel_id=1, source_target_pairs={{0,2},{1,3},{2,0},{3,1},{4,6},{5,7},{6,4},{7,5},{8,10},{9,11},{10,... | collective-permute-start | bytes 3145736 | tf_op jit(solution)/shard_map/ppermute | solution.py:28
  243.3 13.9 %collective-permute-start.30 = (bf16[2,32,4096]{2,1,0:T(8,128)(2,1)S(1)}, bf16[2,32,4096]{2,1,0:T(8,128)(2,1)S(1)}, u32[]{:S(2)}, u32[]{:S(2)}) collective-permute-start(bf16[2,32,4096]{2,1,0:T(8,128)(2,1)S(1)} %get-tuple-element.117), channel_id=1, source_target_pairs={{0,4},{1,5},{2,6},{3,7},{4,0},{5,1},{6,2},{7,3},{8,12},{9,13},{10,... | collective-permute-start | bytes 1572872 | tf_op jit(solution)/shard_map/ppermute | solution.py:28
  257.3 13.9 %collective-permute-start.31 = (bf16[1,32,4096]{2,1,0:T(8,128)(2,1)S(1)}, bf16[1,32,4096]{2,1,0:T(8,128)(2,1)S(1)}, u32[]{:S(2)}, u32[]{:S(2)}) collective-permute-start(bf16[1,32,4096]{2,1,0:T(8,128)(2,1)S(1)} %get-tuple-element.119), channel_id=1, source_target_pairs={{0,8},{1,9},{2,10},{3,11},{4,12},{5,13},{6,14},{7,15},{8,0},{9,1},... | collective-permute-start | bytes 786440 | tf_op jit(solution)/shard_map/ppermute | solution.py:28
  271.6 13.9 %collective-permute-start.33 = (bf16[2,32,4096]{2,1,0:T(8,128)(2,1)S(1)}, bf16[2,32,4096]{2,1,0:T(8,128)(2,1)S(1)}, u32[]{:S(2)}, u32[]{:S(2)}) collective-permute-start(bf16[2,32,4096]{2,1,0:T(8,128)(2,1)S(1)} %get-tuple-element.123), channel_id=1, source_target_pairs={{0,4},{1,5},{2,6},{3,7},{4,0},{5,1},{6,2},{7,3},{8,12},{9,13},{10,... | collective-permute-start | bytes 1572872 | tf_op jit(solution)/shard_map/ppermute | solution.py:28
  285.6 13.9 %collective-permute-start.34 = (bf16[1,32,4096]{2,1,0:T(8,128)(2,1)S(1)}, bf16[1,32,4096]{2,1,0:T(8,128)(2,1)S(1)}, u32[]{:S(2)}, u32[]{:S(2)}) collective-permute-start(bf16[1,32,4096]{2,1,0:T(8,128)(2,1)S(1)} %get-tuple-element.125), channel_id=1, source_target_pairs={{0,8},{1,9},{2,10},{3,11},{4,12},{5,13},{6,14},{7,15},{8,0},{9,1},... | collective-permute-start | bytes 786440 | tf_op jit(solution)/shard_map/ppermute | solution.py:28
  286.7 13.0 %collective-permute-start.35 = (bf16[16,4096]{1,0:T(8,128)(2,1)S(1)}, bf16[16,4096]{1,0:T(8,128)(2,1)S(1)}, u32[]{:S(2)}, u32[]{:S(2)}) collective-permute-start(bf16[16,4096]{1,0:T(8,128)(2,1)S(1)} %get-tuple-element.127), channel_id=1, source_target_pairs={{0,1},{1,0},{2,3},{3,2},{4,5},{5,4},{6,7},{7,6},{8,9},{9,8},{10,11... | collective-permute-start | bytes 393224 | tf_op jit(solution)/shard_map/ppermute | solution.py:28
  286.7 13.0 %collective-permute-start.36 = (bf16[16,4096]{1,0:T(8,128)(2,1)S(1)}, bf16[16,4096]{1,0:T(8,128)(2,1)S(1)}, u32[]{:S(2)}, u32[]{:S(2)}) collective-permute-start(bf16[16,4096]{1,0:T(8,128)(2,1)S(1)} %get-tuple-element.128), channel_id=1, source_target_pairs={{0,1},{1,0},{2,3},{3,2},{4,5},{5,4},{6,7},{7,6},{8,9},{9,8},{10,11... | collective-permute-start | bytes 393224 | tf_op jit(solution)/shard_map/ppermute | solution.py:28
  287.2 12.5 %collective-permute-start.37 = (bf16[16,4096]{1,0:T(8,128)(2,1)S(1)}, bf16[16,4096]{1,0:T(8,128)(2,1)S(1)}, u32[]{:S(2)}, u32[]{:S(2)}) collective-permute-start(bf16[16,4096]{1,0:T(8,128)(2,1)S(1)} %get-tuple-element.129), channel_id=1, source_target_pairs={{0,1},{1,0},{2,3},{3,2},{4,5},{5,4},{6,7},{7,6},{8,9},{9,8},{10,11... | collective-permute-start | bytes 393224 | tf_op jit(solution)/shard_map/ppermute | solution.py:28
  299.6 1.4 collective-permute-start.38

commit v8 on v7

--- a/solution.py
+++ b/solution.py
@@ -116,6 +116,24 @@
         cost_estimate=cost(0, slots * STATE * inner * 6),
         name="pack_state",
     )(prefilled_state, *after)
+
+
+def hold_kernel(x_ref, after_ref, o_ref):
+    pass
+
+
+def hold(x, after):
+    some = pl.BlockSpec(memory_space=pl.ANY)
+    return pl.pallas_call(
+        hold_kernel,
+        in_specs=[some, some],
+        out_specs=some,
+        out_shape=jax.ShapeDtypeStruct(x.shape, x.dtype),
+        input_output_aliases={0: 0},
+        compiler_params=params(8),
+        cost_estimate=cost(0, 0),
+        name="hold",
+    )(x, after)
 
 
 def half_kernel(me_ref, after_ref, w_ref, o_ref):
@@ -235,7 +253,7 @@
         o_ref[...] = (keep_ref[at].astype(F32) + got_ref[at].astype(F32)).astype(BF16)
 
 
-def norm_kernel(me_ref, after_ref, gain_ref, *refs):
+def norm_kernel(me_ref, gain_ref, *refs):
     o_ref = refs[-1]
     total = refs[0][...].astype(F32)
     for ref in refs[1:-1]:
@@ -263,7 +281,7 @@
         o_ref[jnp.bitwise_xor(z, m)] = ref[...]
 
 
-def reduce_projection(send, keep, gain, me, after, n):
+def reduce_projection(send, keep, gain, me, n):
     zs = n // 4
     piece = keep.shape[1:]
     got = swap(send, 1, n)
@@ -271,11 +289,11 @@
     got = swap(send, 2, n)
     cut = small(functools.partial(add_z_kernel, zs), me, [keep, got], [piece] * zs, "add_z")
     cut = [cut[0]] + [swap(cut[m], 4 * m, n) for m in range(1, zs)]
-    (low,) = small(norm_kernel, me, [gain] + cut, [piece], "norm", after)
+    (low,) = small(norm_kernel, me, [gain] + cut, [piece], "norm")
     lows = [low] + [swap(low, 4 * m, n) for m in range(1, zs)]
     (mine,) = small(merge_kernel, me, lows, [(zs,) + piece], "merge_z")
     beside = swap(mine, 2, n)
-    return cut[0], (mine, beside, swap(mine, 1, n), swap(beside, 1, n))
+    return keep, mine, (mine, beside, swap(mine, 1, n), swap(beside, 1, n))
 
 
 def assemble_low(lows, index, low_scr, me_ref):
@@ -312,11 +330,9 @@
     )
 
 
-def state_kernel(t, behind, me_ref, live_ref, *refs):
+def state_kernel(t, behind, me_ref, *refs):
     first, last = t == 0, t == STEPS - 1
     refs = refs[behind:]
-    if first:
-        moved_ref, *refs = refs
     step_ref, tail_ref, conv_ref, z_ref, alog_ref, skip_ref, state_ref, *refs = refs
     new_ref = None
     if not last:
@@ -361,15 +377,6 @@
     if first:
         for copy in fetch(block, now):
             copy.wait()
-
-        def replace(i, carry):
-            at = pl.multiple_of((live_ref[1, i] - base) * STATE, STATE)
-            value = moved_ref[live_ref[2, i]].astype(F32)
-            for l in range(c // 128):
-                buf[now, l, pl.ds(at, STATE), :] = value[:, 128 * l : 128 * (l + 1)]
-            return carry
-
-        lax.fori_loop(live_ref[0, block], live_ref[0, block + 1], replace, 0)
 
     tall, lanes = 16, min(256, c)
     for r in range(0, take, tall):
@@ -399,19 +406,19 @@
             gated_ref[r : r + tall, cols] = (total * (z * sigmoid(z))).astype(BF16)
 
 
-def state_step(t, me, live, moved, after, steps, conv, step_z, a_log, d_skip, state, n):
+def state_step(t, me, after, steps, conv, step_z, a_log, d_skip, state, n):
     _, rows, c = conv.shape
     take = 2 * rows // n
     blocks = rows // take
     first, last = t == 0, t == STEPS - 1
 
-    def placed(i, me_ref, live_ref):
+    def placed(i, me_ref):
         z, y = i // 2, i % 2
         mine = (y == (me_ref[0] // 2) % 2).astype(jnp.int32)
         return (mine * (blocks // 2) + z, 0)
 
     vmem = pl.BlockSpec(memory_space=pltpu.VMEM)
-    in_specs = [vmem] * len(moved) + [vmem] * 2 + [
+    in_specs = [vmem] * 2 + [
         pl.BlockSpec((None, take, c), lambda i, *_: (t, i, 0)),
         pl.BlockSpec((1, take, c), lambda i, *_: (t, i, 0)),
         whole(a_log.shape),
@@ -440,7 +447,7 @@
     out = pl.pallas_call(
         functools.partial(state_kernel, t, len(after)),
         grid_spec=pltpu.PrefetchScalarGridSpec(
-            num_scalar_prefetch=2,
+            num_scalar_prefetch=1,
             grid=(blocks,),
             in_specs=in_specs,
             out_specs=out_specs,
@@ -450,8 +457,114 @@
         compiler_params=params(48),
         cost_estimate=cost(8 * size, 4 * size, size),
         name="state_step",
-    )(me, live, *after, *moved, *steps, conv, step_z, a_log, d_skip, state)
+    )(me, *after, *steps, conv, step_z, a_log, d_skip, state)
     return (None, out[0]) if last else (out[0], out[1])
+
+
+def gather_kernel(me_ref, after_ref, row_ref, *refs):
+    lows, refs = refs[:4], refs[4:]
+    conv_ref, z_ref, dtp_ref, dtb_ref, step_ref, live_conv_ref, gate_ref, tail_ref, low_scr = refs
+    count = step_ref.shape[1]
+    rows = conv_ref.shape[1]
+    hot = (row_ref[:, :1] == lax.broadcasted_iota(jnp.int32, (count, rows), 1)).astype(F32).astype(BF16)
+    for t in range(STEPS):
+        low = jnp.dot(hot, assemble_low(lows, t, low_scr, me_ref), preferred_element_type=F32)
+        step_ref[t] = step_sizes(low.astype(BF16), dtp_ref, dtb_ref)
+        tail_ref[t, :, :128] = low[:, DT_RANK:]
+        conv = conv_ref[t]
+        high = conv.astype(BF16)
+        rest = (conv - high.astype(F32)).astype(BF16)
+        live_conv_ref[t] = jnp.dot(hot, high, preferred_element_type=F32) + jnp.dot(
+            hot, rest, preferred_element_type=F32
+        )
+        z = jnp.dot(hot, z_ref[t], preferred_element_type=F32)
+        gate_ref[t] = z * sigmoid(z)
+
+
+def gather_live(me, after, row_of_live, lows, conv, step_z, dt_proj, dt_bias, n):
+    _, rows, c = conv.shape
+    count = row_of_live.shape[0]
+    wide = (STEPS, count, c)
+    return small(
+        gather_kernel,
+        me,
+        [row_of_live, *lows, conv, step_z, dt_proj, dt_bias],
+        [wide, wide, wide, (STEPS, count, 128)],
+        "gather_live",
+        after,
+        F32,
+        [pltpu.VMEM((n // 4, 2, 2, rows // n, WIDE), BF16)],
+        40,
+    )
+
+
+def live_kernel(slot_ref, after_ref, moved_ref, step_ref, conv_ref, gate_ref, tail_ref, alog_ref, skip_ref, o_ref, buf, state_scr):
+    _, count, c = o_ref.shape
+    def place(i, carry):
+        source, slot = slot_ref[0, i], slot_ref[1, i]
+        at = pl.multiple_of(i * STATE, STATE)
+        from_row = pl.multiple_of(slot * STATE, STATE)
+        value = moved_ref[source, pl.ds(from_row, STATE), :].astype(F32)
+        for l in range(c // 128):
+            buf[l, pl.ds(at, STATE), :] = value[:, 128 * l : 128 * (l + 1)]
+        return carry
+
+    lax.fori_loop(0, count, place, 0)
+    for s in range(STATE):
+        for l in range(c // 128):
+            state_scr[s, :, 128 * l : 128 * (l + 1)] = buf[l, pl.ds(s, count, stride=STATE), :]
+    tall, lanes = 16, min(512, c)
+
+    def step_all(t, carry):
+        for r in range(0, count, tall):
+            tail = tail_ref[t, r : r + tall, :]
+            for l in range(0, c, lanes):
+                cols = slice(l, l + lanes)
+                step = step_ref[t, r : r + tall, cols]
+                conv = conv_ref[t, r : r + tall, cols]
+                drive = step * conv
+                total = skip_ref[:, cols] * conv
+                for s in range(STATE):
+                    rate = -jnp.exp(alog_ref[s : s + 1, cols])
+                    old = state_scr[s, r : r + tall, cols]
+                    state = jnp.exp(step * rate) * old + drive * tail[:, s : s + 1]
+                    state_scr[s, r : r + tall, cols] = state
+                    total = total + state * tail[:, STATE + s : STATE + s + 1]
+                o_ref[t, r : r + tall, cols] = (total * gate_ref[t, r : r + tall, cols]).astype(BF16)
+        return carry
+
+    lax.fori_loop(0, STEPS, step_all, 0)
+
+
+def live_steps(slot_of_live, after, moved, gathered, a_log, d_skip):
+    _, count, c = gathered[0].shape
+    (out,) = small(
+        live_kernel,
+        slot_of_live,
+        [moved, *gathered, a_log, d_skip],
+        [(STEPS, count, c)],
+        "live_steps",
+        after,
+        BF16,
+        [pltpu.VMEM((c // 128, count * STATE, 128), F32), pltpu.VMEM((STATE, count, c), F32)],
+        32,
+    )
+    return out
+
+
+def fix_kernel(t, take, me_ref, after_ref, row_ref, gated_ref, live_ref, o_ref):
+    rows = gated_ref.shape[0]
+    count = live_ref.shape[1]
+    shift = take.bit_length() - 1
+    place = lax.broadcasted_iota(jnp.int32, (rows, count), 0)
+    mine = place >= rows // 2
+    within = place - jnp.where(mine, rows // 2, 0)
+    y = (me_ref[0] // 2) % 2
+    row = ((2 * (within >> shift) + jnp.where(mine, y, 1 - y)) << shift) + (within & (take - 1))
+    hot = (row == row_ref[...]).astype(F32)
+    taken = jnp.max(hot, axis=1, keepdims=True) > 0.0
+    live = jnp.dot(hot.astype(BF16), live_ref[t], preferred_element_type=F32)
+    o_ref[...] = jnp.where(taken, live, gated_ref[...].astype(F32)).astype(BF16)
 
 
 def out_kernel(me_ref, own_ref, other_ref, wown_ref, wother_ref, *refs):
@@ -562,8 +675,8 @@
     me = me_scalar.reshape(1)
 
     moved_conv = exchange_conv(prefilled_conv, me, n)
-    packed = pack_state((moved_conv[1],), prefilled_state, n)
-    moved_state = lax.all_to_all(packed, "dex", 0, 0, tiled=True).reshape(n * slots, STATE, c)
+    half_weight = weight_half(me, moved_conv[1], out_weight)
+    packed = pack_state((half_weight,), prefilled_state, n)
     cols = out_weight.shape[1] // 2
 
     is_live = jnp.arange(slots, dtype=jnp.int32)[None, :] < live_counts[:, None]
@@ -572,19 +685,15 @@
     mine = place[None, None, :, None] == place[:, None, None, None]
     spread = jnp.where(mine, target[None, :, None, :], -1).reshape(TAPS + 1, n * (TAPS + 1) * slots)
     flat = target.reshape(-1)
-    count = n * slots
-    number = jnp.arange(count, dtype=jnp.int32)
-    key = jnp.where(flat < 0, rows + number, flat)
-    before = jnp.sum((key[None, :] < key[:, None]).astype(jnp.int32), axis=1)
-    hit = before[None, :] == number[:, None]
-    bounds = jnp.arange(count, dtype=jnp.int32) * (2 * rows // n)
-    live = jnp.stack(
-        [
-            jnp.sum((key[None, :] < jnp.minimum(bounds, rows)[:, None]).astype(jnp.int32), axis=1),
-            jnp.sum(jnp.where(hit, key[None, :], 0), axis=1),
-            jnp.sum(jnp.where(hit, number[None, :], 0), axis=1),
-        ]
-    )
+    number = jnp.arange(n * slots, dtype=jnp.int32)
+    count = n * slots // 2
+    rank = jnp.sum(((flat >= 0)[None, :] & (number[None, :] < number[:, None])).astype(jnp.int32), axis=1)
+    hit = (rank[None, :] == number[:count, None]) & (flat >= 0)[None, :]
+    live_slot = jnp.sum(jnp.where(hit, number[None, :], 0), axis=1)
+    live_row = jnp.sum(jnp.where(hit, flat[None, :], 0), axis=1)
+    slot_of_live = jnp.stack([live_slot // slots, live_slot % slots])
+    row_of_live = jnp.broadcast_to(live_row[:, None], (count, 128))
+    live_row = live_row.reshape(1, count)
     gain = jnp.concatenate([norm_gain, jnp.zeros((WIDE - norm_gain.shape[0],), F32)]).reshape(1, WIDE)
     old = jnp.transpose(resident_conv, (1, 0, 2))
     proj = x_proj.T
@@ -592,8 +701,10 @@
     conv, send, keep = conv_steps(
         tuple(range(STEPS)), n, me, (packed,), spread, old, moved_conv, step_x, conv_weight, bias, proj
     )
-    behind, lows = reduce_projection(send, keep, gain, me, (moved_state,), n)
-    other_weight = swap(weight_half(me, behind, out_weight), 1, n)
+    behind, merged, lows = reduce_projection(send, keep, gain, me, n)
+    packed = hold(packed, merged)
+    moved_state = lax.all_to_all(packed, "dex", 0, 0, tiled=True)
+    other_weight = swap(hold(half_weight, behind), 1, n)
 
     state = resident_state.reshape(rows * STATE, c)
     sends, keeps, gated = {}, {}, {}
@@ -607,15 +718,19 @@
     def s_step(t, after):
         nonlocal state, next_steps
         if t == 0:
-            steps = step_rows(0, me, (after,), lows, dt_proj, rate_bias, rows, n)
+            steps = step_rows(0, me, after, lows, dt_proj, rate_bias, rows, n)
         else:
             steps = next_steps
-        moved = (moved_state,) if t == 0 else ()
-        state, gated[t] = state_step(t, me, live, moved, (after,), steps, conv, step_z, a_log, skip, state, n)
+        state, gated[t] = state_step(t, me, after, steps, conv, step_z, a_log, skip, state, n)
         if t == STEPS - 1:
             return gated[t]
         next_steps = step_rows(t + 1, me, (gated[t],), lows, dt_proj, rate_bias, rows, n)
         return next_steps[1]
+
+    def fix(t, after):
+        kernel = functools.partial(fix_kernel, t, take)
+        (gated[t],) = small(kernel, me, [live_row, gated[t], live_gated], [(rows, c)], "fix", (after,))
+        return gated[t]
 
     def project(t, after):
         sends[t], keeps[t] = out_project(me, gated[t], swap(gated[t], 1, n), out_weight, other_weight, (after,))
@@ -635,21 +750,25 @@
             sends[t] = swap(sends[t], 1, n)
         return keeps[t]
 
-    last = s_step(0, moved_state)
+    last = s_step(0, (packed,))
+    gathered = gather_live(me, (last,), row_of_live, lows, conv, step_z, dt_proj, rate_bias, n)
+    last = s_step(1, (gathered[0],))
+    live_gated = live_steps(slot_of_live, (last,), moved_state, gathered, a_log, skip)
+    last = fix(0, live_gated)
+    last = fix(1, last)
     last = project(0, last)
-    for t in range(1, STEPS):
-        last = s_step(t, last)
-        if t > 1:
+    last = project(1, last)
+    for t in range(2, STEPS):
+        last = s_step(t, (last,))
+        last = fix(t, last)
+        if t > 2:
             for stage in range(1, stages):
-                last = reduce(t - 2, stage, last)
+                last = reduce(t - 3, stage, last)
+        last = reduce(t - 2, 0, last)
         last = project(t, last)
-        if t > 1:
-            last = reduce(t - 2, stages, last)
-        last = reduce(t - 1, 0, last)
-    for t in (STEPS - 2, STEPS - 1):
-        if t == STEPS - 1:
-            last = reduce(t, 0, last)
-        for stage in range(1, stages + 1):
+    last = reduce(STEPS - 4, stages, last)
+    for t in range(STEPS - 3, STEPS):
+        for stage in range(0 if t > STEPS - 3 else 1, stages + 1):
             last = reduce(t, stage, last)
     return final_join(me, [keeps[t] for t in range(STEPS)], [sends[t] for t in range(STEPS)])
 

time: 305 us -> 296 us (0.970)
  waiting for transfers between devices: 150 us -> 124 us
  starting transfers between devices: 34.8 us -> 43 us
  Pallas kernels: 108 us -> 114 us
  local copies, waits for them, and re-layouts: 7.97 us -> 11.9 us
    ppermute x39, waiting for transfers between devices: 150 us -> 124 us  [swap(): return lax.ppermute(x, 'dex', [(i, i ^ mask) for i in range(n)])]
    ppermute x39, starting transfers between devices: 30.6 us -> 38.1 us  [swap(): return lax.ppermute(x, 'dex', [(i, i ^ mask) for i in range(n)])]
    pallas_call x22 -> x28, Pallas kernels: 9.39 us -> 14.3 us  [small(): pl.pallas_call(kernel, in_specs=[pl.BlockSpec(memory_space=pltpu.SMEM)] +...]
    unnamed x38 -> x82, local copies, waits for them, and re-layouts: 6.79 us -> 10.6 us
  transfers between devices with their start and end apart: 40 -> 40, of which waited for: 23 -> 24; matrix products, arithmetic and copies ran while one was open for 1% -> 1% of each run, Pallas kernels for 28% -> 33%
where the time goes in v8:
time: 296 us; the launch traced here: 295 us
  waiting for transfers between devices  124 us (42%)
  Pallas kernels  114 us (39%)
  starting transfers between devices  43 us (15%)
  local copies, waits for them, and re-layouts  11.9 us (4%)
    ppermute x39, waiting for transfers between devices, swap(): return lax.ppermute(x, 'dex', [(i, i ^ mask) for i in range(n)])  124 us
    pallas_call x4, Pallas kernels, state_step(): pl.pallas_call(functools.partial(state_kernel, t, len(after)), grid_spec=...  49.5 us
    ppermute x39, starting transfers between devices, swap(): return lax.ppermute(x, 'dex', [(i, i ^ mask) for i in range(n)])  38.1 us
    pallas_call x4, Pallas kernels, out_project(): pl.pallas_call(out_kernel, grid_spec=pltpu.PrefetchScalarGridSpec(num_sca...  34.3 us
    pallas_call x28, Pallas kernels, small(): pl.pallas_call(kernel, in_specs=[pl.BlockSpec(memory_space=pltpu.SMEM)] +...  14.3 us
    unnamed x82, local copies, waits for them, and re-layouts  10.6 us
    pallas_call x1, Pallas kernels, weight_half(): pl.pallas_call(half_kernel, grid_spec=pltpu.PrefetchScalarGridSpec(num_sc...  7.18 us
  transfers between devices with their start and end apart: 40, of which 24 were waited for; matrix products, arithmetic and copies ran while one was open for 1% of the time, Pallas kernels for 33%

profile of v8, /device:TPU:0, one launch (start us, length us, event | category | flops | bytes accessed | tf_op | source)
XLA Modules:
  0.0 294.9 jit_solution(17182271536253494363)
XLA Ops:
  0.0 1.1 copy-done.23
  1.2 3.0 %collective-permute-start = (bf16[4,16,768]{2,1,0:T(8,128)(2,1)S(1)}, bf16[4,16,768]{2,1,0:T(8,128)(2,1)S(1)}, u32[]{:S(2)}, u32[]{:S(2)}) collective-permute-start(bf16[4,16,768]{2,1,0:T(8,128)(2,1)S(1)} %get-tuple-element.73), channel_id=1, source_target_pairs={{0,2},{1,3},{2,0},{3,1},{4,6},{5,7},{6,4},{7,5},{8,10},{9,11},{10,... | collective-permute-start | bytes 294920 | tf_op jit(solution)/shard_map/ppermute | solution.py:28
  4.8 0.7 reshape.182
  5.5 0.7 broadcast_select_fusion
  7.0 4.1 %collective-permute-done.3.refs_3_ = bf16[4,16,768]{2,1,0:T(8,128)(2,1)S(1)} collective-permute-done((bf16[4,16,768]{2,1,0:T(8,128)(2,1)S(1)}, bf16[4,16,768]{2,1,0:T(8,128)(2,1)S(1)}, u32[]{:S(2)}, u32[]{:S(2)}) %collective-permute-start.3) | collective-permute-done | bytes 98336 | tf_op jit(solution)/shard_map/ppermute | solution.py:28
  11.2 1.6 collective-permute-start.4
  12.8 2.6 collective-permute-start.5
  15.6 1.2 collective-permute-done.4.after_ref.refs_1_
  17.5 7.2 %weight_half.1.refs_0_.x_ref = bf16[1024,4096]{1,0:T(8,128)(2,1)} custom-call(s32[1]{0:T(128)} %bitcast.me_ref, bf16[4,16,768]{2,1,0:T(8,128)(2,1)} %copy-done.31, bf16[1024,8192]{1,0:T(8,128)(2,1)} %wown_ref.7), custom_call_target="tpu_custom_call" | custom-call | flops 1024 | bytes 1024 | tf_op jit(solution)/shard_map/weight_half/pallas_call | solution.py:147
  24.7 2.1 pack_state.1.refs_4_.x_ref
  27.2 0.8 copy-done.16
  28.2 3.9 %conv_project.1 = (f32[4,256,1024]{2,1,0:T(8,128)S(1)}, bf16[8,4,16,640]{3,2,1,0:T(8,128)(2,1)S(1)}, bf16[8,4,16,640]{3,2,1,0:T(8,128)(2,1)S(1)}) custom-call(s32[1]{0:T(128)} %bitcast.me_ref, s32[4,256]{1,0:T(4,128)S(1)} %broadcast_select_fusion.1.target_ref, f32[3,256,1024]{2,1,0:T(8,128)S(1)} %bitcast.37, bf16[4,256,1024]{2,1,0:T(8,128)(2,1)S(1)} %copy-done.16, ...), custom_call_target="tpu_custom_call" | custom-call | flops 1024 | bytes 1024 | tf_op jit(solution)/shard_map/conv_project/pallas_call | solution.py:212
  32.2 2.1 collective-permute-done.7.refs_1_
  35.0 9.7 %collective-permute-done.8.refs_1_ = bf16[4,4,16,640]{3,2,1,0:T(8,128)(2,1)S(1)} collective-permute-done((bf16[4,4,16,640]{3,2,1,0:T(8,128)(2,1)S(1)}, bf16[4,4,16,640]{3,2,1,0:T(8,128)(2,1)S(1)}, u32[]{:S(2)}, u32[]{:S(2)}) %collective-permute-start.8) | collective-permute-done | bytes 327712 | tf_op jit(solution)/shard_map/ppermute | solution.py:28
  44.8 1.3 collective-permute-start.9
  46.1 2.4 collective-permute-start.10
  48.5 0.8 collective-permute-start.11
  49.8 5.2 %collective-permute-done.10.refs_2_ = bf16[4,16,640]{2,1,0:T(8,128)(2,1)S(1)} collective-permute-done((bf16[4,16,640]{2,1,0:T(8,128)(2,1)S(1)}, bf16[4,16,640]{2,1,0:T(8,128)(2,1)S(1)}, u32[]{:S(2)}, u32[]{:S(2)}) %collective-permute-start.10) | collective-permute-done | bytes 81952 | tf_op jit(solution)/shard_map/ppermute | solution.py:28
  55.2 2.3 collective-permute-start.14
  57.4 0.7 collective-permute-start.13
  58.1 1.5 collective-permute-start.12
  59.6 2.2 collective-permute-done.14.refs_3_
  61.8 2.5 collective-permute-done.13.refs_2_
  64.4 4.9 %all-to-all-start = ((bf16[16,64,1024]{2,1,0:T(8,128)(2,1)}), bf16[16,64,1024]{2,1,0:T(8,128)(2,1)}, u32[]{:S(2)}, u32[]{:S(2)}) async-start(bf16[16,64,1024]{2,1,0:T(8,128)(2,1)} %hold.2.after_ref.refs_0_), calls=%async_computation | async-start | bytes 4194304 | tf_op jit(solution)/shard_map/all_to_all | solution.py:706
  69.5 1.6 collective-permute-start.15
  72.2 23.7 %collective-permute-done.15.refs_1_ = bf16[4,4,16,640]{3,2,1,0:T(8,128)(2,1)S(1)} collective-permute-done((bf16[4,4,16,640]{3,2,1,0:T(8,128)(2,1)S(1)}, bf16[4,4,16,640]{3,2,1,0:T(8,128)(2,1)S(1)}, u32[]{:S(2)}, u32[]{:S(2)}) %collective-permute-start.15) | collective-permute-done | bytes 327712 | tf_op jit(solution)/shard_map/ppermute | solution.py:28
  95.9 1.6 collective-permute-done.17.refs_3_
  98.1 16.7 %state_step.4 = (bf16[16,256,1024]{2,1,0:T(8,128)(2,1)}, bf16[256,1024]{1,0:T(8,128)(2,1)S(1)}) custom-call(s32[1]{0:T(128)} %bitcast.me_ref, bf16[16,64,1024]{2,1,0:T(8,128)(2,1)} %hold.2.after_ref.refs_0_, f32[256,1024]{1,0:T(8,128)S(1)} %get-tuple-element.88.refs_1_, f32[256,128]{1,0:T(8,128)S(1)} %get-tuple-element.89.refs_2_, f32[4,256,1024]{2,1,0:T(8,128)} %copy-done, ...), custom_call_target="tpu_custom_call" | custom-call | flops 1024 | bytes 1024 | tf_op jit(solution)/shard_map/state_step/pallas_call | solution.py:447
  115.6 2.7 gather_live.1
  118.3 12.1 %state_step.5 = (bf16[16,256,1024]{2,1,0:T(8,128)(2,1)}, bf16[256,1024]{1,0:T(8,128)(2,1)S(1)}) custom-call(s32[1]{0:T(128)} %bitcast.me_ref, f32[4,32,1024]{2,1,0:T(8,128)S(1)} %get-tuple-element.93.refs_0_.step_ref, f32[256,1024]{1,0:T(8,128)S(1)} %get-tuple-element.94.refs_1_, f32[256,128]{1,0:T(8,128)S(1)} %get-tuple-element.92.after_ref.refs_2_, ...), custom_call_target="tpu_custom_call" | custom-call | flops 1024 | bytes 1024 | tf_op jit(solution)/shard_map/state_step/pallas_call | solution.py:447
  131.0 0.8 copy-done.12
  131.8 1.0 copy-done.21
  133.4 1.1 copy-done.18
  134.6 0.9 copy-done.25
  135.5 1.0 copy-done.28
  136.5 1.0 copy-done.30
  137.6 0.8 copy-done.36
  138.4 5.7 %live_steps.1.after_ref.live_ref = bf16[4,32,1024]{2,1,0:T(8,128)(2,1)S(1)} custom-call(s32[2,32]{1,0:T(2,128)S(1)} %pad_add_fusion.slot_ref, f32[256,128]{1,0:T(8,128)S(1)} %copy-done.25, bf16[16,64,1024]{2,1,0:T(8,128)(2,1)} %all-to-all-done.moved_ref, f32[4,32,1024]{2,1,0:T(8,128)S(1)} %copy-done.18, f32[4,32,1024]{2,1,0:T(8,128)S(1)} %copy-done.28, ...), custom_call_target="tpu_custom_call" | custom-call | flops 1024 | bytes 1024 | tf_op jit(solution)/shard_map/live_steps/pallas_call | solution.py:47
  144.9 1.5 collective-permute-done.20.other_ref
  146.4 8.6 %out_project.4 = (bf16[128,4096]{1,0:T(8,128)(2,1)S(1)}, bf16[128,4096]{1,0:T(8,128)(2,1)S(1)}) custom-call(s32[1]{0:T(128)} %bitcast.me_ref, bf16[256,1024]{1,0:T(8,128)(2,1)S(1)} %fix.4.after_ref.own_ref, bf16[256,1024]{1,0:T(8,128)(2,1)S(1)} %collective-permute-done.20.other_ref, bf16[1024,8192]{1,0:T(8,128)(2,1)} %wown_ref.7, ...), custom_call_target="tpu_custom_call" | custom-call | flops 1024 | bytes 1024 | tf_op jit(solution)/shard_map/out_project/pallas_call | solution.py:585
  155.2 1.8 collective-permute-done.18.other_ref
  157.0 8.6 %out_project.5 = (bf16[128,4096]{1,0:T(8,128)(2,1)S(1)}, bf16[128,4096]{1,0:T(8,128)(2,1)S(1)}) custom-call(s32[1]{0:T(128)} %bitcast.me_ref, bf16[256,1024]{1,0:T(8,128)(2,1)S(1)} %fix.5.refs_0_.own_ref, bf16[256,1024]{1,0:T(8,128)(2,1)S(1)} %collective-permute-done.18.other_ref, bf16[1024,8192]{1,0:T(8,128)(2,1)} %wown_ref.7, ...), custom_call_target="tpu_custom_call" | custom-call | flops 1024 | bytes 1024 | tf_op jit(solution)/shard_map/out_project/pallas_call | solution.py:585
  165.6 2.0 collective-permute-start.25
  167.7 11.6 %state_step.6 = (bf16[16,256,1024]{2,1,0:T(8,128)(2,1)}, bf16[256,1024]{1,0:T(8,128)(2,1)S(1)}) custom-call(s32[1]{0:T(128)} %bitcast.me_ref, bf16[128,4096]{1,0:T(8,128)(2,1)S(1)} %get-tuple-element.102.refs_0_, f32[256,1024]{1,0:T(8,128)S(1)} %copy-done.22, f32[256,128]{1,0:T(8,128)S(1)} %copy-done.26, f32[4,256,1024]{2,1,0:T(8,128)} %copy-done, ...), custom_call_target="tpu_custom_call" | custom-call | flops 1024 | bytes 1024 | tf_op jit(solution)/shard_map/state_step/pallas_call | solution.py:447
  181.3 0.9 collective-permute-done.21.other_ref
  182.2 8.6 %out_project.6 = (bf16[128,4096]{1,0:T(8,128)(2,1)S(1)}, bf16[128,4096]{1,0:T(8,128)(2,1)S(1)}) custom-call(s32[1]{0:T(128)} %bitcast.me_ref, bf16[256,1024]{1,0:T(8,128)(2,1)S(1)} %fix.6.after_ref.own_ref, bf16[256,1024]{1,0:T(8,128)(2,1)S(1)} %collective-permute-done.21.other_ref, bf16[1024,8192]{1,0:T(8,128)(2,1)} %wown_ref.7, ...), custom_call_target="tpu_custom_call" | custom-call | flops 1024 | bytes 1024 | tf_op jit(solution)/shard_map/out_project/pallas_call | solution.py:585
  190.9 9.1 %state_step.7.after_ref.gated_ref = bf16[256,1024]{1,0:T(8,128)(2,1)S(1)} custom-call(s32[1]{0:T(128)} %bitcast.me_ref, bf16[128,4096]{1,0:T(8,128)(2,1)S(1)} %get-tuple-element.109.refs_0_, f32[256,1024]{1,0:T(8,128)S(1)} %get-tuple-element.110.refs_1_, f32[256,128]{1,0:T(8,128)S(1)} %get-tuple-element.106.after_ref.refs_2_, f32[4,256,1024]{2,1,0:T(8,128)} %copy-done, ...), custom_call_target="tpu_custom_call" | custom-call | flops 1024 | bytes 1024 | tf_op jit(solution)/shard_map/state_step/pallas_call | solution.py:447
  200.6 2.9 collective-permute-done.25
  203.8 4.0 %collective-permute-start.26 = (bf16[1,32,4096]{2,1,0:T(8,128)(2,1)S(1)}, bf16[1,32,4096]{2,1,0:T(8,128)(2,1)S(1)}, u32[]{:S(2)}, u32[]{:S(2)}) collective-permute-start(bf16[1,32,4096]{2,1,0:T(8,128)(2,1)S(1)} %get-tuple-element.117), channel_id=1, source_target_pairs={{0,8},{1,9},{2,10},{3,11},{4,12},{5,13},{6,14},{7,15},{8,0},{9,1},... | collective-permute-start | bytes 786440 | tf_op jit(solution)/shard_map/ppermute | solution.py:28
  207.8 8.5 %out_project.7 = (bf16[128,4096]{1,0:T(8,128)(2,1)S(1)}, bf16[128,4096]{1,0:T(8,128)(2,1)S(1)}) custom-call(s32[1]{0:T(128)} %bitcast.me_ref, bf16[256,1024]{1,0:T(8,128)(2,1)S(1)} %fix.7.after_ref.own_ref, bf16[256,1024]{1,0:T(8,128)(2,1)S(1)} %collective-permute-done.23.other_ref, bf16[1024,8192]{1,0:T(8,128)(2,1)} %wown_ref.7, ...), custom_call_target="tpu_custom_call" | custom-call | flops 1024 | bytes 1024 | tf_op jit(solution)/shard_map/out_project/pallas_call | solution.py:585
  216.4 3.2 %collective-permute-done.26.got_ref = bf16[1,32,4096]{2,1,0:T(8,128)(2,1)S(1)} collective-permute-done((bf16[1,32,4096]{2,1,0:T(8,128)(2,1)S(1)}, bf16[1,32,4096]{2,1,0:T(8,128)(2,1)S(1)}, u32[]{:S(2)}, u32[]{:S(2)}) %collective-permute-start.26) | collective-permute-done | bytes 262176 | tf_op jit(solution)/shard_map/ppermute | solution.py:28
  219.6 2.1 collective-permute-done.27.got_ref
  221.9 1.6 collective-permute-start.28
  223.5 1.6 collective-permute-start.32
  225.0 9.7 %collective-permute-done.28.got_ref = bf16[1,32,4096]{2,1,0:T(8,128)(2,1)S(1)} collective-permute-done((bf16[1,32,4096]{2,1,0:T(8,128)(2,1)S(1)}, bf16[1,32,4096]{2,1,0:T(8,128)(2,1)S(1)}, u32[]{:S(2)}, u32[]{:S(2)}) %collective-permute-start.28) | collective-permute-done | bytes 262176 | tf_op jit(solution)/shard_map/ppermute | solution.py:28
  235.7 12.1 %collective-permute-done.30.got_ref = bf16[2,32,4096]{2,1,0:T(8,128)(2,1)S(1)} collective-permute-done((bf16[2,32,4096]{2,1,0:T(8,128)(2,1)S(1)}, bf16[2,32,4096]{2,1,0:T(8,128)(2,1)S(1)}, u32[]{:S(2)}, u32[]{:S(2)}) %collective-permute-start.30) | collective-permute-done | bytes 524320 | tf_op jit(solution)/shard_map/ppermute | solution.py:28
  247.9 3.4 %collective-permute-start.31 = (bf16[1,32,4096]{2,1,0:T(8,128)(2,1)S(1)}, bf16[1,32,4096]{2,1,0:T(8,128)(2,1)S(1)}, u32[]{:S(2)}, u32[]{:S(2)}) collective-permute-start(bf16[1,32,4096]{2,1,0:T(8,128)(2,1)S(1)} %get-tuple-element.127), channel_id=1, source_target_pairs={{0,8},{1,9},{2,10},{3,11},{4,12},{5,13},{6,14},{7,15},{8,0},{9,1},... | collective-permute-start | bytes 786440 | tf_op jit(solution)/shard_map/ppermute | solution.py:28
  251.3 11.6 %collective-permute-done.31.got_ref = bf16[1,32,4096]{2,1,0:T(8,128)(2,1)S(1)} collective-permute-done((bf16[1,32,4096]{2,1,0:T(8,128)(2,1)S(1)}, bf16[1,32,4096]{2,1,0:T(8,128)(2,1)S(1)}, u32[]{:S(2)}, u32[]{:S(2)}) %collective-permute-start.31) | collective-permute-done | bytes 262176 | tf_op jit(solution)/shard_map/ppermute | solution.py:28
  263.3 0.7 collective-permute-start.33
  264.0 12.3 %collective-permute-done.33.got_ref = bf16[2,32,4096]{2,1,0:T(8,128)(2,1)S(1)} collective-permute-done((bf16[2,32,4096]{2,1,0:T(8,128)(2,1)S(1)}, bf16[2,32,4096]{2,1,0:T(8,128)(2,1)S(1)}, u32[]{:S(2)}, u32[]{:S(2)}) %collective-permute-start.33) | collective-permute-done | bytes 524320 | tf_op jit(solution)/shard_map/ppermute | solution.py:28
  276.4 3.2 %collective-permute-start.34 = (bf16[1,32,4096]{2,1,0:T(8,128)(2,1)S(1)}, bf16[1,32,4096]{2,1,0:T(8,128)(2,1)S(1)}, u32[]{:S(2)}, u32[]{:S(2)}) collective-permute-start(bf16[1,32,4096]{2,1,0:T(8,128)(2,1)S(1)} %get-tuple-element.133), channel_id=1, source_target_pairs={{0,8},{1,9},{2,10},{3,11},{4,12},{5,13},{6,14},{7,15},{8,0},{9,1},... | collective-permute-start | bytes 786440 | tf_op jit(solution)/shard_map/ppermute | solution.py:28
  280.2 11.0 %collective-permute-done.34.got_ref = bf16[1,32,4096]{2,1,0:T(8,128)(2,1)S(1)} collective-permute-done((bf16[1,32,4096]{2,1,0:T(8,128)(2,1)S(1)}, bf16[1,32,4096]{2,1,0:T(8,128)(2,1)S(1)}, u32[]{:S(2)}, u32[]{:S(2)}) %collective-permute-start.34) | collective-permute-done | bytes 262176 | tf_op jit(solution)/shard_map/ppermute | solution.py:28
  291.4 1.3 collective-permute-done.38.refs_7_
  292.7 2.2 final_join.1
  (159 shorter events, 14.7 us)
Async XLA Ops:
  1.2 5.8 %collective-permute-start = (bf16[4,16,768]{2,1,0:T(8,128)(2,1)S(1)}, bf16[4,16,768]{2,1,0:T(8,128)(2,1)S(1)}, u32[]{:S(2)}, u32[]{:S(2)}) collective-permute-start(bf16[4,16,768]{2,1,0:T(8,128)(2,1)S(1)} %get-tuple-element.73), channel_id=1, source_target_pairs={{0,2},{1,3},{2,0},{3,1},{4,6},{5,7},{6,4},{7,5},{8,10},{9,11},{10,... | collective-permute-start | bytes 294920 | tf_op jit(solution)/shard_map/ppermute | solution.py:28
  4.2 2.8 collective-permute-start.1
  4.2 2.1 collective-permute-start.2
  6.4 4.8 %collective-permute-start.3 = (bf16[4,16,768]{2,1,0:T(8,128)(2,1)S(1)}, bf16[4,16,768]{2,1,0:T(8,128)(2,1)S(1)}, u32[]{:S(2)}, u32[]{:S(2)}) collective-permute-start(bf16[4,16,768]{2,1,0:T(8,128)(2,1)S(1)} %collective-permute-done.2), channel_id=1, source_target_pairs={{0,2},{1,3},{2,0},{3,1},{4,6},{5,7},{6,4},{7,5},{8,10},{9,11},{10,... | collective-permute-start | bytes 294920 | tf_op jit(solution)/shard_map/ppermute | solution.py:28
  11.2 5.7 %collective-permute-start.4 = (bf16[4,16,768]{2,1,0:T(8,128)(2,1)S(1)}, bf16[4,16,768]{2,1,0:T(8,128)(2,1)S(1)}, u32[]{:S(2)}, u32[]{:S(2)}) collective-permute-start(bf16[4,16,768]{2,1,0:T(8,128)(2,1)S(1)} %get-tuple-element.76), channel_id=1, source_target_pairs={{0,4},{1,5},{2,6},{3,7},{4,0},{5,1},{6,2},{7,3},{8,12},{9,13},{10,... | collective-permute-start | bytes 294920 | tf_op jit(solution)/shard_map/ppermute | solution.py:28
  12.8 14.0 %collective-permute-start.5 = (bf16[4,16,768]{2,1,0:T(8,128)(2,1)S(1)}, bf16[4,16,768]{2,1,0:T(8,128)(2,1)S(1)}, u32[]{:S(2)}, u32[]{:S(2)}) collective-permute-start(bf16[4,16,768]{2,1,0:T(8,128)(2,1)S(1)} %get-tuple-element.78), channel_id=1, source_target_pairs={{0,8},{1,9},{2,10},{3,11},{4,12},{5,13},{6,14},{7,15},{8,0},{9,1},... | collective-permute-start | bytes 294920 | tf_op jit(solution)/shard_map/ppermute | solution.py:28
  15.4 11.5 %collective-permute-start.6 = (bf16[4,16,768]{2,1,0:T(8,128)(2,1)S(1)}, bf16[4,16,768]{2,1,0:T(8,128)(2,1)S(1)}, u32[]{:S(2)}, u32[]{:S(2)}) collective-permute-start(bf16[4,16,768]{2,1,0:T(8,128)(2,1)S(1)} %get-tuple-element.79), channel_id=1, source_target_pairs={{0,12},{1,13},{2,14},{3,15},{4,8},{5,9},{6,10},{7,11},{8,4},{9,5},... | collective-permute-start | bytes 294920 | tf_op jit(solution)/shard_map/ppermute | solution.py:28
  15.6 9.0 %copy-start.10 = (f32[4,16,16384]{2,1,0:T(8,128)S(1)}, f32[4,16,16384]{2,1,0:T(8,128)}, u32[]{:S(2)}) copy-start(f32[4,16,16384]{2,1,0:T(8,128)} %x_ref.2) | copy-start | bytes 12582916
  24.7 3.6 %copy-start.20 = (bf16[1024,544]{0,1:T(8,128)(2,1)S(1)}, bf16[1024,544]{0,1:T(8,128)(2,1)}, u32[]{:S(2)}) copy-start(bf16[1024,544]{0,1:T(8,128)(2,1)} %param.27) | copy-start | bytes 3342340
  32.1 2.2 collective-permute-start.7
  34.5 14.8 %copy-start.39 = (f32[544]{0:T(1024)S(1)}, f32[544]{0:T(1024)}, u32[]{:S(2)}) copy-start(f32[544]{0:T(1024)} %param.28) | copy-start | bytes 6532
  34.5 111.9 %collective-permute-start.19 = (bf16[1024,4096]{1,0:T(8,128)(2,1)}, bf16[1024,4096]{1,0:T(8,128)(2,1)}, u32[]{:S(2)}, u32[]{:S(2)}) collective-permute-start(bf16[1024,4096]{1,0:T(8,128)(2,1)} %hold.3), channel_id=1, source_target_pairs={{0,1},{1,0},{2,3},{3,2},{4,5},{5,4},{6,7},{7,6},{8,9},{9,8},{10,11... | collective-permute-start | bytes 25165832 | tf_op jit(solution)/shard_map/ppermute | solution.py:28
  34.7 10.0 %collective-permute-start.8 = (bf16[4,4,16,640]{3,2,1,0:T(8,128)(2,1)S(1)}, bf16[4,4,16,640]{3,2,1,0:T(8,128)(2,1)S(1)}, u32[]{:S(2)}, u32[]{:S(2)}) collective-permute-start(bf16[4,4,16,640]{3,2,1,0:T(8,128)(2,1)S(1)} %get-tuple-element.83), channel_id=1, source_target_pairs={{0,2},{1,3},{2,0},{3,1},{4,6},{5,7},{6,4},{7,5},{8,10},{9,11},{10,... | collective-permute-start | bytes 983048 | tf_op jit(solution)/shard_map/ppermute | solution.py:28
  44.8 5.0 %collective-permute-start.9 = (bf16[4,16,640]{2,1,0:T(8,128)(2,1)S(1)}, bf16[4,16,640]{2,1,0:T(8,128)(2,1)S(1)}, u32[]{:S(2)}, u32[]{:S(2)}) collective-permute-start(bf16[4,16,640]{2,1,0:T(8,128)(2,1)S(1)} %get-tuple-element.85), channel_id=1, source_target_pairs={{0,4},{1,5},{2,6},{3,7},{4,0},{5,1},{6,2},{7,3},{8,12},{9,13},{10,... | collective-permute-start | bytes 245768 | tf_op jit(solution)/shard_map/ppermute | solution.py:28
  46.1 8.9 %collective-permute-start.10 = (bf16[4,16,640]{2,1,0:T(8,128)(2,1)S(1)}, bf16[4,16,640]{2,1,0:T(8,128)(2,1)S(1)}, u32[]{:S(2)}, u32[]{:S(2)}) collective-permute-start(bf16[4,16,640]{2,1,0:T(8,128)(2,1)S(1)} %get-tuple-element.86), channel_id=1, source_target_pairs={{0,8},{1,9},{2,10},{3,11},{4,12},{5,13},{6,14},{7,15},{8,0},{9,1},... | collective-permute-start | bytes 245768 | tf_op jit(solution)/shard_map/ppermute | solution.py:28
  48.5 6.5 %collective-permute-start.11 = (bf16[4,16,640]{2,1,0:T(8,128)(2,1)S(1)}, bf16[4,16,640]{2,1,0:T(8,128)(2,1)S(1)}, u32[]{:S(2)}, u32[]{:S(2)}) collective-permute-start(bf16[4,16,640]{2,1,0:T(8,128)(2,1)S(1)} %get-tuple-element.87), channel_id=1, source_target_pairs={{0,12},{1,13},{2,14},{3,15},{4,8},{5,9},{6,10},{7,11},{8,4},{9,5},... | collective-permute-start | bytes 245768 | tf_op jit(solution)/shard_map/ppermute | solution.py:28
  55.2 6.6 %collective-permute-start.14 = (bf16[4,16,640]{2,1,0:T(8,128)(2,1)S(1)}, bf16[4,16,640]{2,1,0:T(8,128)(2,1)S(1)}, u32[]{:S(2)}, u32[]{:S(2)}) collective-permute-start(bf16[4,16,640]{2,1,0:T(8,128)(2,1)S(1)} %norm.1.refs_0_), channel_id=1, source_target_pairs={{0,12},{1,13},{2,14},{3,15},{4,8},{5,9},{6,10},{7,11},{8,4},{9,5},... | collective-permute-start | bytes 245768 | tf_op jit(solution)/shard_map/ppermute | solution.py:28
  57.4 6.9 %collective-permute-start.13 = (bf16[4,16,640]{2,1,0:T(8,128)(2,1)S(1)}, bf16[4,16,640]{2,1,0:T(8,128)(2,1)S(1)}, u32[]{:S(2)}, u32[]{:S(2)}) collective-permute-start(bf16[4,16,640]{2,1,0:T(8,128)(2,1)S(1)} %norm.1.refs_0_), channel_id=1, source_target_pairs={{0,8},{1,9},{2,10},{3,11},{4,12},{5,13},{6,14},{7,15},{8,0},{9,1},... | collective-permute-start | bytes 245768 | tf_op jit(solution)/shard_map/ppermute | solution.py:28
  58.1 6.2 %collective-permute-start.12 = (bf16[4,16,640]{2,1,0:T(8,128)(2,1)S(1)}, bf16[4,16,640]{2,1,0:T(8,128)(2,1)S(1)}, u32[]{:S(2)}, u32[]{:S(2)}) collective-permute-start(bf16[4,16,640]{2,1,0:T(8,128)(2,1)S(1)} %norm.1.refs_0_), channel_id=1, source_target_pairs={{0,4},{1,5},{2,6},{3,7},{4,0},{5,1},{6,2},{7,3},{8,12},{9,13},{10,... | collective-permute-start | bytes 245768 | tf_op jit(solution)/shard_map/ppermute | solution.py:28
  64.3 5.0 %copy-start.40 = (s32[16]{0:T(128)S(1)}, s32[16]{0:T(128)}, u32[]{:S(2)}) copy-start(s32[16]{0:T(128)} %param.21) | copy-start | bytes 196
  64.3 33.1 %copy-start.3 = (bf16[512,1024]{1,0:T(8,128)(2,1)S(1)}, bf16[512,1024]{1,0:T(8,128)(2,1)}, u32[]{:S(2)}) copy-start(bf16[512,1024]{1,0:T(8,128)(2,1)} %refs_4_.14) | copy-start | bytes 3145732
  64.3 33.1 %copy-start.33 = (f32[1024]{0:T(1024)S(1)}, f32[1024]{0:T(1024)}, u32[]{:S(2)}) copy-start(f32[1024]{0:T(1024)} %param.30) | copy-start | bytes 12292
  64.4 33.7 %copy-start.2 = (bf16[4,256,1024]{2,1,0:T(8,128)(2,1)S(1)}, bf16[4,256,1024]{2,1,0:T(8,128)(2,1)}, u32[]{:S(2)}) copy-start(bf16[4,256,1024]{2,1,0:T(8,128)(2,1)} %refs_4_.15) | copy-start | bytes 6291460
  64.4 33.7 %copy-start.19 = (f32[16,1024]{1,0:T(8,128)S(1)}, f32[16,1024]{1,0:T(8,128)}, u32[]{:S(2)}) copy-start(f32[16,1024]{1,0:T(8,128)} %refs_5_.9) | copy-start | bytes 196612
  64.4 33.7 %copy-start.34 = (f32[1024]{0:T(1024)S(1)}, f32[1024]{0:T(1024)}, u32[]{:S(2)}) copy-start(f32[1024]{0:T(1024)} %param.32) | copy-start | bytes 12292
  64.4 69.0 %all-to-all-start = ((bf16[16,64,1024]{2,1,0:T(8,128)(2,1)}), bf16[16,64,1024]{2,1,0:T(8,128)(2,1)}, u32[]{:S(2)}, u32[]{:S(2)}) async-start(bf16[16,64,1024]{2,1,0:T(8,128)(2,1)} %hold.2.after_ref.refs_0_), calls=%async_computation | async-start | bytes 4194304 | tf_op jit(solution)/shard_map/all_to_all | solution.py:706
  69.5 26.3 %collective-permute-start.15 = (bf16[4,4,16,640]{3,2,1,0:T(8,128)(2,1)S(1)}, bf16[4,4,16,640]{3,2,1,0:T(8,128)(2,1)S(1)}, u32[]{:S(2)}, u32[]{:S(2)}) collective-permute-start(bf16[4,4,16,640]{3,2,1,0:T(8,128)(2,1)S(1)} %merge_z.1.after_ref.refs_0_), channel_id=1, source_target_pairs={{0,2},{1,3},{2,0},{3,1},{4,6},{5,7},{6,4},{7,5},{8,10},{9,11},{10,... | collective-permute-start | bytes 983048 | tf_op jit(solution)/shard_map/ppermute | solution.py:28
  72.1 23.8 %collective-permute-start.16 = (bf16[4,4,16,640]{3,2,1,0:T(8,128)(2,1)S(1)}, bf16[4,4,16,640]{3,2,1,0:T(8,128)(2,1)S(1)}, u32[]{:S(2)}, u32[]{:S(2)}) collective-permute-start(bf16[4,4,16,640]{3,2,1,0:T(8,128)(2,1)S(1)} %merge_z.1.after_ref.refs_0_), channel_id=1, source_target_pairs={{0,1},{1,0},{2,3},{3,2},{4,5},{5,4},{6,7},{7,6},{8,9},{9,8},{10,11... | collective-permute-start | bytes 983048 | tf_op jit(solution)/shard_map/ppermute | solution.py:28
  95.8 34.6 %copy-start.4 = (bf16[4,4,16,640]{3,2,1,0:T(8,128)(2,1)}, bf16[4,4,16,640]{3,2,1,0:T(8,128)(2,1)S(1)}, u32[]{:S(2)}) copy-start(bf16[4,4,16,640]{3,2,1,0:T(8,128)(2,1)S(1)} %collective-permute-done.15.refs_1_) | copy-start | bytes 983044
  95.8 1.6 collective-permute-start.17
  95.9 34.5 %copy-start.6 = (bf16[4,4,16,640]{3,2,1,0:T(8,128)(2,1)}, bf16[4,4,16,640]{3,2,1,0:T(8,128)(2,1)S(1)}, u32[]{:S(2)}) copy-start(bf16[4,4,16,640]{3,2,1,0:T(8,128)(2,1)S(1)} %collective-permute-done.16.refs_2_) | copy-start | bytes 983044
  97.5 32.9 %copy-start.8 = (bf16[4,4,16,640]{3,2,1,0:T(8,128)(2,1)}, bf16[4,4,16,640]{3,2,1,0:T(8,128)(2,1)S(1)}, u32[]{:S(2)}) copy-start(bf16[4,4,16,640]{3,2,1,0:T(8,128)(2,1)S(1)} %collective-permute-done.17.refs_3_) | copy-start | bytes 983044
  98.1 17.5 %copy-start.1 = (f32[4,256,1024]{2,1,0:T(8,128)S(1)}, f32[4,256,1024]{2,1,0:T(8,128)}, u32[]{:S(2)}) copy-start(f32[4,256,1024]{2,1,0:T(8,128)} %copy-done) | copy-start | bytes 12582916
  118.3 12.1 %copy-start.17 = (f32[4,32,1024]{2,1,0:T(8,128)}, f32[4,32,1024]{2,1,0:T(8,128)S(1)}, u32[]{:S(2)}) copy-start(f32[4,32,1024]{2,1,0:T(8,128)S(1)} %get-tuple-element.93.refs_0_.step_ref) | copy-start | bytes 1572868
  118.3 12.1 %copy-start.27 = (f32[4,32,1024]{2,1,0:T(8,128)}, f32[4,32,1024]{2,1,0:T(8,128)S(1)}, u32[]{:S(2)}) copy-start(f32[4,32,1024]{2,1,0:T(8,128)S(1)} %get-tuple-element.98.conv_ref) | copy-start | bytes 1572868
  118.3 12.1 %copy-start.29 = (f32[4,32,1024]{2,1,0:T(8,128)}, f32[4,32,1024]{2,1,0:T(8,128)S(1)}, u32[]{:S(2)}) copy-start(f32[4,32,1024]{2,1,0:T(8,128)S(1)} %get-tuple-element.99.gate_ref) | copy-start | bytes 1572868
  118.3 12.1 %copy-start.35 = (f32[4,32,128]{2,1,0:T(8,128)}, f32[4,32,128]{2,1,0:T(8,128)S(1)}, u32[]{:S(2)}) copy-start(f32[4,32,128]{2,1,0:T(8,128)S(1)} %get-tuple-element.100.tail_ref) | copy-start | bytes 196612
  133.4 10.7 %copy-start.15 = (bf16[256,1024]{1,0:T(8,128)(2,1)S(1)}, bf16[256,1024]{1,0:T(8,128)(2,1)}, u32[]{:S(2)}) copy-start(bf16[256,1024]{1,0:T(8,128)(2,1)} %copy-done.14) | copy-start | bytes 1572868
  133.4 11.2 %copy-start.13 = (bf16[256,1024]{1,0:T(8,128)(2,1)S(1)}, bf16[256,1024]{1,0:T(8,128)(2,1)}, u32[]{:S(2)}) copy-start(bf16[256,1024]{1,0:T(8,128)(2,1)} %copy-done.12) | copy-start | bytes 1572868
  144.4 2.0 collective-permute-start.20
  154.9 26.1 %collective-permute-start.22 = (bf16[128,4096]{1,0:T(8,128)(2,1)S(1)}, bf16[128,4096]{1,0:T(8,128)(2,1)S(1)}, u32[]{:S(2)}, u32[]{:S(2)}) collective-permute-start(bf16[128,4096]{1,0:T(8,128)(2,1)S(1)} %get-tuple-element.107), channel_id=1, source_target_pairs={{0,2},{1,3},{2,0},{3,1},{4,6},{5,7},{6,4},{7,5},{8,10},{9,11},{10,... | collective-permute-start | bytes 3145736 | tf_op jit(solution)/shard_map/ppermute | solution.py:28
  155.0 2.0 collective-permute-start.18
  157.0 10.7 %copy-start.22 = (f32[256,1024]{1,0:T(8,128)S(1)}, f32[256,1024]{1,0:T(8,128)}, u32[]{:S(2)}) copy-start(f32[256,1024]{1,0:T(8,128)} %copy-done.21) | copy-start | bytes 3145732
  157.0 10.7 %copy-start.26 = (f32[256,128]{1,0:T(8,128)S(1)}, f32[256,128]{1,0:T(8,128)}, u32[]{:S(2)}) copy-start(f32[256,128]{1,0:T(8,128)} %copy-done.24) | copy-start | bytes 393220
  165.6 37.8 %collective-permute-start.25 = (bf16[128,4096]{1,0:T(8,128)(2,1)S(1)}, bf16[128,4096]{1,0:T(8,128)(2,1)S(1)}, u32[]{:S(2)}, u32[]{:S(2)}) collective-permute-start(bf16[128,4096]{1,0:T(8,128)(2,1)S(1)} %get-tuple-element.114), channel_id=1, source_target_pairs={{0,2},{1,3},{2,0},{3,1},{4,6},{5,7},{6,4},{7,5},{8,10},{9,11},{10,... | collective-permute-start | bytes 3145736 | tf_op jit(solution)/shard_map/ppermute | solution.py:28
  167.7 11.6 %copy-start.5 = (bf16[4,4,16,640]{3,2,1,0:T(8,128)(2,1)S(1)}, bf16[4,4,16,640]{3,2,1,0:T(8,128)(2,1)}, u32[]{:S(2)}) copy-start(bf16[4,4,16,640]{3,2,1,0:T(8,128)(2,1)} %copy-done.4) | copy-start | bytes 983044
  167.7 11.6 %copy-start.7 = (bf16[4,4,16,640]{3,2,1,0:T(8,128)(2,1)S(1)}, bf16[4,4,16,640]{3,2,1,0:T(8,128)(2,1)}, u32[]{:S(2)}) copy-start(bf16[4,4,16,640]{3,2,1,0:T(8,128)(2,1)} %copy-done.6) | copy-start | bytes 983044
  167.7 11.6 %copy-start.9 = (bf16[4,4,16,640]{3,2,1,0:T(8,128)(2,1)S(1)}, bf16[4,4,16,640]{3,2,1,0:T(8,128)(2,1)}, u32[]{:S(2)}) copy-start(bf16[4,4,16,640]{3,2,1,0:T(8,128)(2,1)} %copy-done.8) | copy-start | bytes 983044
  180.2 2.0 collective-permute-start.21
  181.2 19.2 %collective-permute-start.24 = (bf16[2,32,4096]{2,1,0:T(8,128)(2,1)S(1)}, bf16[2,32,4096]{2,1,0:T(8,128)(2,1)S(1)}, u32[]{:S(2)}, u32[]{:S(2)}) collective-permute-start(bf16[2,32,4096]{2,1,0:T(8,128)(2,1)S(1)} %get-tuple-element.112), channel_id=1, source_target_pairs={{0,4},{1,5},{2,6},{3,7},{4,0},{5,1},{6,2},{7,3},{8,12},{9,13},{10,... | collective-permute-start | bytes 1572872 | tf_op jit(solution)/shard_map/ppermute | solution.py:28
  190.8 44.1 %collective-permute-start.29 = (bf16[128,4096]{1,0:T(8,128)(2,1)S(1)}, bf16[128,4096]{1,0:T(8,128)(2,1)S(1)}, u32[]{:S(2)}, u32[]{:S(2)}) collective-permute-start(bf16[128,4096]{1,0:T(8,128)(2,1)S(1)} %get-tuple-element.123), channel_id=1, source_target_pairs={{0,2},{1,3},{2,0},{3,1},{4,6},{5,7},{6,4},{7,5},{8,10},{9,11},{10,... | collective-permute-start | bytes 3145736 | tf_op jit(solution)/shard_map/ppermute | solution.py:28
  200.3 7.5 %collective-permute-start.23 = (bf16[256,1024]{1,0:T(8,128)(2,1)S(1)}, bf16[256,1024]{1,0:T(8,128)(2,1)S(1)}, u32[]{:S(2)}, u32[]{:S(2)}) collective-permute-start(bf16[256,1024]{1,0:T(8,128)(2,1)S(1)} %fix.7.after_ref.own_ref), channel_id=1, source_target_pairs={{0,1},{1,0},{2,3},{3,2},{4,5},{5,4},{6,7},{7,6},{8,9},{9,8},{10,11... | collective-permute-start | bytes 1572872 | tf_op jit(solution)/shard_map/ppermute | solution.py:28
  203.7 18.0 %collective-permute-start.27 = (bf16[2,32,4096]{2,1,0:T(8,128)(2,1)S(1)}, bf16[2,32,4096]{2,1,0:T(8,128)(2,1)S(1)}, u32[]{:S(2)}, u32[]{:S(2)}) collective-permute-start(bf16[2,32,4096]{2,1,0:T(8,128)(2,1)S(1)} %get-tuple-element.119), channel_id=1, source_target_pairs={{0,4},{1,5},{2,6},{3,7},{4,0},{5,1},{6,2},{7,3},{8,12},{9,13},{10,... | collective-permute-start | bytes 1572872 | tf_op jit(solution)/shard_map/ppermute | solution.py:28
  203.8 15.7 %collective-permute-start.26 = (bf16[1,32,4096]{2,1,0:T(8,128)(2,1)S(1)}, bf16[1,32,4096]{2,1,0:T(8,128)(2,1)S(1)}, u32[]{:S(2)}, u32[]{:S(2)}) collective-permute-start(bf16[1,32,4096]{2,1,0:T(8,128)(2,1)S(1)} %get-tuple-element.117), channel_id=1, source_target_pairs={{0,8},{1,9},{2,10},{3,11},{4,12},{5,13},{6,14},{7,15},{8,0},{9,1},... | collective-permute-start | bytes 786440 | tf_op jit(solution)/shard_map/ppermute | solution.py:28
  221.9 12.9 %collective-permute-start.28 = (bf16[1,32,4096]{2,1,0:T(8,128)(2,1)S(1)}, bf16[1,32,4096]{2,1,0:T(8,128)(2,1)S(1)}, u32[]{:S(2)}, u32[]{:S(2)}) collective-permute-start(bf16[1,32,4096]{2,1,0:T(8,128)(2,1)S(1)} %get-tuple-element.121), channel_id=1, source_target_pairs={{0,8},{1,9},{2,10},{3,11},{4,12},{5,13},{6,14},{7,15},{8,0},{9,1},... | collective-permute-start | bytes 786440 | tf_op jit(solution)/shard_map/ppermute | solution.py:28
  223.5 39.5 %collective-permute-start.32 = (bf16[128,4096]{1,0:T(8,128)(2,1)S(1)}, bf16[128,4096]{1,0:T(8,128)(2,1)S(1)}, u32[]{:S(2)}, u32[]{:S(2)}) collective-permute-start(bf16[128,4096]{1,0:T(8,128)(2,1)S(1)} %get-tuple-element.129), channel_id=1, source_target_pairs={{0,2},{1,3},{2,0},{3,1},{4,6},{5,7},{6,4},{7,5},{8,10},{9,11},{10,... | collective-permute-start | bytes 3145736 | tf_op jit(solution)/shard_map/ppermute | solution.py:28
  235.1 12.7 %collective-permute-start.30 = (bf16[2,32,4096]{2,1,0:T(8,128)(2,1)S(1)}, bf16[2,32,4096]{2,1,0:T(8,128)(2,1)S(1)}, u32[]{:S(2)}, u32[]{:S(2)}) collective-permute-start(bf16[2,32,4096]{2,1,0:T(8,128)(2,1)S(1)} %get-tuple-element.125), channel_id=1, source_target_pairs={{0,4},{1,5},{2,6},{3,7},{4,0},{5,1},{6,2},{7,3},{8,12},{9,13},{10,... | collective-permute-start | bytes 1572872 | tf_op jit(solution)/shard_map/ppermute | solution.py:28
  247.9 15.0 %collective-permute-start.31 = (bf16[1,32,4096]{2,1,0:T(8,128)(2,1)S(1)}, bf16[1,32,4096]{2,1,0:T(8,128)(2,1)S(1)}, u32[]{:S(2)}, u32[]{:S(2)}) collective-permute-start(bf16[1,32,4096]{2,1,0:T(8,128)(2,1)S(1)} %get-tuple-element.127), channel_id=1, source_target_pairs={{0,8},{1,9},{2,10},{3,11},{4,12},{5,13},{6,14},{7,15},{8,0},{9,1},... | collective-permute-start | bytes 786440 | tf_op jit(solution)/shard_map/ppermute | solution.py:28
  263.3 13.0 %collective-permute-start.33 = (bf16[2,32,4096]{2,1,0:T(8,128)(2,1)S(1)}, bf16[2,32,4096]{2,1,0:T(8,128)(2,1)S(1)}, u32[]{:S(2)}, u32[]{:S(2)}) collective-permute-start(bf16[2,32,4096]{2,1,0:T(8,128)(2,1)S(1)} %get-tuple-element.131), channel_id=1, source_target_pairs={{0,4},{1,5},{2,6},{3,7},{4,0},{5,1},{6,2},{7,3},{8,12},{9,13},{10,... | collective-permute-start | bytes 1572872 | tf_op jit(solution)/shard_map/ppermute | solution.py:28
  276.4 14.8 %collective-permute-start.34 = (bf16[1,32,4096]{2,1,0:T(8,128)(2,1)S(1)}, bf16[1,32,4096]{2,1,0:T(8,128)(2,1)S(1)}, u32[]{:S(2)}, u32[]{:S(2)}) collective-permute-start(bf16[1,32,4096]{2,1,0:T(8,128)(2,1)S(1)} %get-tuple-element.133), channel_id=1, source_target_pairs={{0,8},{1,9},{2,10},{3,11},{4,12},{5,13},{6,14},{7,15},{8,0},{9,1},... | collective-permute-start | bytes 786440 | tf_op jit(solution)/shard_map/ppermute | solution.py:28
  279.6 11.7 %collective-permute-start.35 = (bf16[16,4096]{1,0:T(8,128)(2,1)S(1)}, bf16[16,4096]{1,0:T(8,128)(2,1)S(1)}, u32[]{:S(2)}, u32[]{:S(2)}) collective-permute-start(bf16[16,4096]{1,0:T(8,128)(2,1)S(1)} %get-tuple-element.135), channel_id=1, source_target_pairs={{0,1},{1,0},{2,3},{3,2},{4,5},{5,4},{6,7},{7,6},{8,9},{9,8},{10,11... | collective-permute-start | bytes 393224 | tf_op jit(solution)/shard_map/ppermute | solution.py:28
  279.7 11.7 %collective-permute-start.36 = (bf16[16,4096]{1,0:T(8,128)(2,1)S(1)}, bf16[16,4096]{1,0:T(8,128)(2,1)S(1)}, u32[]{:S(2)}, u32[]{:S(2)}) collective-permute-start(bf16[16,4096]{1,0:T(8,128)(2,1)S(1)} %get-tuple-element.136), channel_id=1, source_target_pairs={{0,1},{1,0},{2,3},{3,2},{4,5},{5,4},{6,7},{7,6},{8,9},{9,8},{10,11... | collective-permute-start | bytes 393224 | tf_op jit(solution)/shard_map/ppermute | solution.py:28
  280.2 11.2 %collective-permute-start.37 = (bf16[16,4096]{1,0:T(8,128)(2,1)S(1)}, bf16[16,4096]{1,0:T(8,128)(2,1)S(1)}, u32[]{:S(2)}, u32[]{:S(2)}) collective-permute-start(bf16[16,4096]{1,0:T(8,128)(2,1)S(1)} %get-tuple-element.137), channel_id=1, source_target_pairs={{0,1},{1,0},{2,3},{3,2},{4,5},{5,4},{6,7},{7,6},{8,9},{9,8},{10,11... | collective-permute-start | bytes 393224 | tf_op jit(solution)/shard_map/ppermute | solution.py:28
  291.3 1.4 collective-permute-start.38
  (17 other events, 31.3 us)

commit v9 on v8

--- a/solution.py
+++ b/solution.py
@@ -752,24 +752,26 @@
 
     last = s_step(0, (packed,))
     gathered = gather_live(me, (last,), row_of_live, lows, conv, step_z, dt_proj, rate_bias, n)
-    last = s_step(1, (gathered[0],))
     live_gated = live_steps(slot_of_live, (last,), moved_state, gathered, a_log, skip)
     last = fix(0, live_gated)
-    last = fix(1, last)
     last = project(0, last)
-    last = project(1, last)
-    for t in range(2, STEPS):
+    for t in range(1, STEPS):
         last = s_step(t, (last,))
         last = fix(t, last)
-        if t > 2:
+        if t > 1:
             for stage in range(1, stages):
-                last = reduce(t - 3, stage, last)
-        last = reduce(t - 2, 0, last)
+                last = reduce(t - 2, stage, last)
         last = project(t, last)
-    last = reduce(STEPS - 4, stages, last)
-    for t in range(STEPS - 3, STEPS):
-        for stage in range(0 if t > STEPS - 3 else 1, stages + 1):
-            last = reduce(t, stage, last)
+        if 1 < t < STEPS - 1:
+            last = reduce(t - 2, stages, last)
+        last = reduce(t - 1, 0, last)
+    last = reduce(STEPS - 3, stages, last)
+    for stage in range(1, stages):
+        last = reduce(STEPS - 2, stage, last)
+    last = reduce(STEPS - 1, 0, last)
+    last = reduce(STEPS - 2, stages, last)
+    for stage in range(1, stages + 1):
+        last = reduce(STEPS - 1, stage, last)
     return final_join(me, [keeps[t] for t in range(STEPS)], [sends[t] for t in range(STEPS)])
 
 

time: 296 us -> 283 us (0.956)
  waiting for transfers between devices: 124 us -> 116 us
  starting transfers between devices: 43 us -> 35.9 us
    ppermute x39, waiting for transfers between devices: 124 us -> 116 us  [swap(): return lax.ppermute(x, 'dex', [(i, i ^ mask) for i in range(n)])]
    ppermute x39, starting transfers between devices: 38.1 us -> 31 us  [swap(): return lax.ppermute(x, 'dex', [(i, i ^ mask) for i in range(n)])]
    unnamed x82 -> x78, local copies, waits for them, and re-layouts: 10.6 us -> 13.6 us
  transfers between devices with their start and end apart: 40 -> 40, of which waited for: 24 -> 23; matrix products, arithmetic and copies ran while one was open for 1% -> 1% of each run, Pallas kernels for 33% -> 35%
where the time goes in v9:
time: 283 us; the launch traced here: 282 us
  waiting for transfers between devices  116 us (41%)
  Pallas kernels  113 us (40%)
  starting transfers between devices  35.9 us (13%)
  local copies, waits for them, and re-layouts  14.8 us (5%)
    ppermute x39, waiting for transfers between devices, swap(): return lax.ppermute(x, 'dex', [(i, i ^ mask) for i in range(n)])  116 us
    pallas_call x4, Pallas kernels, state_step(): pl.pallas_call(functools.partial(state_kernel, t, len(after)), grid_spec=...  49 us
    pallas_call x4, Pallas kernels, out_project(): pl.pallas_call(out_kernel, grid_spec=pltpu.PrefetchScalarGridSpec(num_sca...  34.2 us
    ppermute x39, starting transfers between devices, swap(): return lax.ppermute(x, 'dex', [(i, i ^ mask) for i in range(n)])  31 us
    pallas_call x28, Pallas kernels, small(): pl.pallas_call(kernel, in_specs=[pl.BlockSpec(memory_space=pltpu.SMEM)] +...  14.3 us
    unnamed x78, local copies, waits for them, and re-layouts  13.6 us
    pallas_call x1, Pallas kernels, weight_half(): pl.pallas_call(half_kernel, grid_spec=pltpu.PrefetchScalarGridSpec(num_sc...  7.14 us
  transfers between devices with their start and end apart: 40, of which 23 were waited for; matrix products, arithmetic and copies ran while one was open for 1% of the time, Pallas kernels for 35%

profile of v9, /device:TPU:0, one launch (start us, length us, event | category | flops | bytes accessed | tf_op | source)
XLA Modules:
  0.0 282.1 jit_solution(10560839431073730737)
XLA Ops:
  0.0 1.1 copy-done.22
  1.2 3.0 %collective-permute-start = (bf16[4,16,768]{2,1,0:T(8,128)(2,1)S(1)}, bf16[4,16,768]{2,1,0:T(8,128)(2,1)S(1)}, u32[]{:S(2)}, u32[]{:S(2)}) collective-permute-start(bf16[4,16,768]{2,1,0:T(8,128)(2,1)S(1)} %get-tuple-element.73), channel_id=1, source_target_pairs={{0,2},{1,3},{2,0},{3,1},{4,6},{5,7},{6,4},{7,5},{8,10},{9,11},{10,... | collective-permute-start | bytes 294920 | tf_op jit(solution)/shard_map/ppermute | solution.py:28
  4.8 0.7 reshape.182
  5.5 0.7 broadcast_select_fusion
  7.0 4.1 %collective-permute-done.3.refs_3_ = bf16[4,16,768]{2,1,0:T(8,128)(2,1)S(1)} collective-permute-done((bf16[4,16,768]{2,1,0:T(8,128)(2,1)S(1)}, bf16[4,16,768]{2,1,0:T(8,128)(2,1)S(1)}, u32[]{:S(2)}, u32[]{:S(2)}) %collective-permute-start.3) | collective-permute-done | bytes 98336 | tf_op jit(solution)/shard_map/ppermute | solution.py:28
  11.2 1.6 collective-permute-start.4
  12.8 2.6 collective-permute-start.5
  15.6 1.2 collective-permute-done.4.after_ref.refs_1_
  17.5 7.1 %weight_half.1.refs_0_.x_ref = bf16[1024,4096]{1,0:T(8,128)(2,1)} custom-call(s32[1]{0:T(128)} %bitcast.me_ref, bf16[4,16,768]{2,1,0:T(8,128)(2,1)} %copy-done.29, bf16[1024,8192]{1,0:T(8,128)(2,1)} %wown_ref.7), custom_call_target="tpu_custom_call" | custom-call | flops 1024 | bytes 1024 | tf_op jit(solution)/shard_map/weight_half/pallas_call | solution.py:147
  24.7 2.1 pack_state.1.refs_4_.x_ref
  27.2 0.7 copy-done.14
  28.2 3.9 %conv_project.1 = (f32[4,256,1024]{2,1,0:T(8,128)S(1)}, bf16[8,4,16,640]{3,2,1,0:T(8,128)(2,1)S(1)}, bf16[8,4,16,640]{3,2,1,0:T(8,128)(2,1)S(1)}) custom-call(s32[1]{0:T(128)} %bitcast.me_ref, s32[4,256]{1,0:T(4,128)S(1)} %broadcast_select_fusion.1.target_ref, f32[3,256,1024]{2,1,0:T(8,128)S(1)} %bitcast.37, bf16[4,256,1024]{2,1,0:T(8,128)(2,1)S(1)} %copy-done.14, ...), custom_call_target="tpu_custom_call" | custom-call | flops 1024 | bytes 1024 | tf_op jit(solution)/shard_map/conv_project/pallas_call | solution.py:212
  32.2 2.1 collective-permute-done.7.refs_1_
  35.0 9.7 %collective-permute-done.8.refs_1_ = bf16[4,4,16,640]{3,2,1,0:T(8,128)(2,1)S(1)} collective-permute-done((bf16[4,4,16,640]{3,2,1,0:T(8,128)(2,1)S(1)}, bf16[4,4,16,640]{3,2,1,0:T(8,128)(2,1)S(1)}, u32[]{:S(2)}, u32[]{:S(2)}) %collective-permute-start.8) | collective-permute-done | bytes 327712 | tf_op jit(solution)/shard_map/ppermute | solution.py:28
  44.8 1.3 collective-permute-start.9
  46.1 2.4 collective-permute-start.10
  48.5 0.8 collective-permute-start.11
  49.7 5.2 %collective-permute-done.10.refs_2_ = bf16[4,16,640]{2,1,0:T(8,128)(2,1)S(1)} collective-permute-done((bf16[4,16,640]{2,1,0:T(8,128)(2,1)S(1)}, bf16[4,16,640]{2,1,0:T(8,128)(2,1)S(1)}, u32[]{:S(2)}, u32[]{:S(2)}) %collective-permute-start.10) | collective-permute-done | bytes 81952 | tf_op jit(solution)/shard_map/ppermute | solution.py:28
  55.1 2.2 collective-permute-start.14
  57.4 0.7 collective-permute-start.13
  58.1 1.5 collective-permute-start.12
  59.6 2.2 collective-permute-done.14.refs_3_
  61.8 2.5 collective-permute-done.13.refs_2_
  64.4 4.9 %all-to-all-start = ((bf16[16,64,1024]{2,1,0:T(8,128)(2,1)}), bf16[16,64,1024]{2,1,0:T(8,128)(2,1)}, u32[]{:S(2)}, u32[]{:S(2)}) async-start(bf16[16,64,1024]{2,1,0:T(8,128)(2,1)} %hold.2.after_ref.refs_0_), calls=%async_computation | async-start | bytes 4194304 | tf_op jit(solution)/shard_map/all_to_all | solution.py:706
  69.5 1.6 collective-permute-start.15
  72.1 23.7 %collective-permute-done.15.refs_1_ = bf16[4,4,16,640]{3,2,1,0:T(8,128)(2,1)S(1)} collective-permute-done((bf16[4,4,16,640]{3,2,1,0:T(8,128)(2,1)S(1)}, bf16[4,4,16,640]{3,2,1,0:T(8,128)(2,1)S(1)}, u32[]{:S(2)}, u32[]{:S(2)}) %collective-permute-start.15) | collective-permute-done | bytes 327712 | tf_op jit(solution)/shard_map/ppermute | solution.py:28
  95.8 1.6 collective-permute-done.17.refs_3_
  98.1 16.7 %state_step.4 = (bf16[16,256,1024]{2,1,0:T(8,128)(2,1)}, bf16[256,1024]{1,0:T(8,128)(2,1)S(1)}) custom-call(s32[1]{0:T(128)} %bitcast.me_ref, bf16[16,64,1024]{2,1,0:T(8,128)(2,1)} %hold.2.after_ref.refs_0_, f32[256,1024]{1,0:T(8,128)S(1)} %get-tuple-element.88.refs_1_, f32[256,128]{1,0:T(8,128)S(1)} %get-tuple-element.89.refs_2_, f32[4,256,1024]{2,1,0:T(8,128)} %copy-done, ...), custom_call_target="tpu_custom_call" | custom-call | flops 1024 | bytes 1024 | tf_op jit(solution)/shard_map/state_step/pallas_call | solution.py:447
  115.5 0.8 copy-done.12
  116.2 1.0 copy-done.20
  117.3 2.7 gather_live.1
  120.6 0.8 copy-done.23
  121.4 0.8 copy-done.25
  122.2 0.8 copy-done.27
  123.6 1.0 copy-done.17
  124.6 1.0 copy-done.24
  125.6 1.0 copy-done.26
  126.7 1.0 copy-done.28
  127.7 0.8 copy-done.34
  128.5 5.7 %live_steps.1.after_ref.live_ref = bf16[4,32,1024]{2,1,0:T(8,128)(2,1)S(1)} custom-call(s32[2,32]{1,0:T(2,128)S(1)} %pad_add_fusion.slot_ref, f32[256,128]{1,0:T(8,128)S(1)} %copy-done.17, bf16[16,64,1024]{2,1,0:T(8,128)(2,1)} %all-to-all-done.moved_ref, f32[4,32,1024]{2,1,0:T(8,128)S(1)} %copy-done.24, f32[4,32,1024]{2,1,0:T(8,128)S(1)} %copy-done.26, ...), custom_call_target="tpu_custom_call" | custom-call | flops 1024 | bytes 1024 | tf_op jit(solution)/shard_map/live_steps/pallas_call | solution.py:47
  134.8 1.8 collective-permute-done.18.other_ref
  136.5 8.6 %out_project.4 = (bf16[128,4096]{1,0:T(8,128)(2,1)S(1)}, bf16[128,4096]{1,0:T(8,128)(2,1)S(1)}) custom-call(s32[1]{0:T(128)} %bitcast.me_ref, bf16[256,1024]{1,0:T(8,128)(2,1)S(1)} %fix.4.own_ref.refs_0_, bf16[256,1024]{1,0:T(8,128)(2,1)S(1)} %collective-permute-done.18.other_ref, bf16[1024,8192]{1,0:T(8,128)(2,1)} %wown_ref.7, ...), custom_call_target="tpu_custom_call" | custom-call | flops 1024 | bytes 1024 | tf_op jit(solution)/shard_map/out_project/pallas_call | solution.py:585
  145.2 11.6 %state_step.5 = (bf16[16,256,1024]{2,1,0:T(8,128)(2,1)}, bf16[256,1024]{1,0:T(8,128)(2,1)S(1)}) custom-call(s32[1]{0:T(128)} %bitcast.me_ref, bf16[128,4096]{1,0:T(8,128)(2,1)S(1)} %get-tuple-element.97.refs_0_, f32[256,1024]{1,0:T(8,128)S(1)} %copy-done.21, f32[256,128]{1,0:T(8,128)S(1)} %copy-done.18, f32[4,256,1024]{2,1,0:T(8,128)} %copy-done, ...), custom_call_target="tpu_custom_call" | custom-call | flops 1024 | bytes 1024 | tf_op jit(solution)/shard_map/state_step/pallas_call | solution.py:447
  158.0 1.8 collective-permute-done.20.other_ref
  159.7 8.5 %out_project.5 = (bf16[128,4096]{1,0:T(8,128)(2,1)S(1)}, bf16[128,4096]{1,0:T(8,128)(2,1)S(1)}) custom-call(s32[1]{0:T(128)} %bitcast.me_ref, bf16[256,1024]{1,0:T(8,128)(2,1)S(1)} %fix.5.own_ref.refs_0_, bf16[256,1024]{1,0:T(8,128)(2,1)S(1)} %collective-permute-done.20.other_ref, bf16[1024,8192]{1,0:T(8,128)(2,1)} %wown_ref.7, ...), custom_call_target="tpu_custom_call" | custom-call | flops 1024 | bytes 1024 | tf_op jit(solution)/shard_map/out_project/pallas_call | solution.py:585
  168.3 2.1 collective-permute-start.25
  170.7 11.5 %state_step.6 = (bf16[16,256,1024]{2,1,0:T(8,128)(2,1)}, bf16[256,1024]{1,0:T(8,128)(2,1)S(1)}) custom-call(s32[1]{0:T(128)} %bitcast.me_ref, bf16[2,32,4096]{2,1,0:T(8,128)(2,1)S(1)} %get-tuple-element.104.refs_0_.keep_ref, f32[256,1024]{1,0:T(8,128)S(1)} %get-tuple-element.105.refs_1_, f32[256,128]{1,0:T(8,128)S(1)} %get-tuple-element.101.after_ref.refs_2_, ...), custom_call_target="tpu_custom_call" | custom-call | flops 1024 | bytes 1024 | tf_op jit(solution)/shard_map/state_step/pallas_call | solution.py:447
  183.2 1.1 collective-permute-done.23.got_ref
  184.5 3.0 %collective-permute-start.24 = (bf16[1,32,4096]{2,1,0:T(8,128)(2,1)S(1)}, bf16[1,32,4096]{2,1,0:T(8,128)(2,1)S(1)}, u32[]{:S(2)}, u32[]{:S(2)}) collective-permute-start(bf16[1,32,4096]{2,1,0:T(8,128)(2,1)S(1)} %get-tuple-element.112), channel_id=1, source_target_pairs={{0,8},{1,9},{2,10},{3,11},{4,12},{5,13},{6,14},{7,15},{8,0},{9,1},... | collective-permute-start | bytes 786440 | tf_op jit(solution)/shard_map/ppermute | solution.py:28
  187.4 8.5 %out_project.6 = (bf16[128,4096]{1,0:T(8,128)(2,1)S(1)}, bf16[128,4096]{1,0:T(8,128)(2,1)S(1)}) custom-call(s32[1]{0:T(128)} %bitcast.me_ref, bf16[256,1024]{1,0:T(8,128)(2,1)S(1)} %fix.6.after_ref.own_ref, bf16[256,1024]{1,0:T(8,128)(2,1)S(1)} %collective-permute-done.22.other_ref, bf16[1024,8192]{1,0:T(8,128)(2,1)} %wown_ref.7, ...), custom_call_target="tpu_custom_call" | custom-call | flops 1024 | bytes 1024 | tf_op jit(solution)/shard_map/out_project/pallas_call | solution.py:585
  196.3 3.7 %collective-permute-done.24.got_ref = bf16[1,32,4096]{2,1,0:T(8,128)(2,1)S(1)} collective-permute-done((bf16[1,32,4096]{2,1,0:T(8,128)(2,1)S(1)}, bf16[1,32,4096]{2,1,0:T(8,128)(2,1)S(1)}, u32[]{:S(2)}, u32[]{:S(2)}) %collective-permute-start.24) | collective-permute-done | bytes 262176 | tf_op jit(solution)/shard_map/ppermute | solution.py:28
  200.4 9.1 %state_step.7.after_ref.gated_ref = bf16[256,1024]{1,0:T(8,128)(2,1)S(1)} custom-call(s32[1]{0:T(128)} %bitcast.me_ref, bf16[2,32,4096]{2,1,0:T(8,128)(2,1)S(1)} %get-tuple-element.115.refs_0_.keep_ref, f32[256,1024]{1,0:T(8,128)S(1)} %get-tuple-element.116.refs_1_, f32[256,128]{1,0:T(8,128)S(1)} %get-tuple-element.108.after_ref.refs_2_, ...), custom_call_target="tpu_custom_call" | custom-call | flops 1024 | bytes 1024 | tf_op jit(solution)/shard_map/state_step/pallas_call | solution.py:447
  209.9 4.3 %collective-permute-done.27.got_ref = bf16[2,32,4096]{2,1,0:T(8,128)(2,1)S(1)} collective-permute-done((bf16[2,32,4096]{2,1,0:T(8,128)(2,1)S(1)}, bf16[2,32,4096]{2,1,0:T(8,128)(2,1)S(1)}, u32[]{:S(2)}, u32[]{:S(2)}) %collective-permute-start.27) | collective-permute-done | bytes 524320 | tf_op jit(solution)/shard_map/ppermute | solution.py:28
  214.3 8.6 %out_project.7 = (bf16[128,4096]{1,0:T(8,128)(2,1)S(1)}, bf16[128,4096]{1,0:T(8,128)(2,1)S(1)}) custom-call(s32[1]{0:T(128)} %bitcast.me_ref, bf16[256,1024]{1,0:T(8,128)(2,1)S(1)} %fix.7.after_ref.own_ref, bf16[256,1024]{1,0:T(8,128)(2,1)S(1)} %collective-permute-done.26.other_ref, bf16[1024,8192]{1,0:T(8,128)(2,1)} %wown_ref.7, ...), custom_call_target="tpu_custom_call" | custom-call | flops 1024 | bytes 1024 | tf_op jit(solution)/shard_map/out_project/pallas_call | solution.py:585
  223.9 1.0 collective-permute-start.29
  224.8 15.2 %collective-permute-done.29.got_ref = bf16[1,32,4096]{2,1,0:T(8,128)(2,1)S(1)} collective-permute-done((bf16[1,32,4096]{2,1,0:T(8,128)(2,1)S(1)}, bf16[1,32,4096]{2,1,0:T(8,128)(2,1)S(1)}, u32[]{:S(2)}, u32[]{:S(2)}) %collective-permute-start.29) | collective-permute-done | bytes 262176 | tf_op jit(solution)/shard_map/ppermute | solution.py:28
  240.1 1.8 collective-permute-done.30.got_ref
  242.0 5.2 %collective-permute-done.31 = bf16[128,4096]{1,0:T(8,128)(2,1)S(1)} collective-permute-done((bf16[128,4096]{1,0:T(8,128)(2,1)S(1)}, bf16[128,4096]{1,0:T(8,128)(2,1)S(1)}, u32[]{:S(2)}, u32[]{:S(2)}) %collective-permute-start.31) | collective-permute-done | bytes 1048608 | tf_op jit(solution)/shard_map/ppermute | solution.py:28
  248.7 14.8 %collective-permute-done.32.got_ref = bf16[1,32,4096]{2,1,0:T(8,128)(2,1)S(1)} collective-permute-done((bf16[1,32,4096]{2,1,0:T(8,128)(2,1)S(1)}, bf16[1,32,4096]{2,1,0:T(8,128)(2,1)S(1)}, u32[]{:S(2)}, u32[]{:S(2)}) %collective-permute-start.32) | collective-permute-done | bytes 262176 | tf_op jit(solution)/shard_map/ppermute | solution.py:28
  263.6 1.5 collective-permute-done.33.got_ref
  265.2 2.0 collective-permute-start.34
  267.7 10.7 %collective-permute-done.34.got_ref = bf16[1,32,4096]{2,1,0:T(8,128)(2,1)S(1)} collective-permute-done((bf16[1,32,4096]{2,1,0:T(8,128)(2,1)S(1)}, bf16[1,32,4096]{2,1,0:T(8,128)(2,1)S(1)}, u32[]{:S(2)}, u32[]{:S(2)}) %collective-permute-start.34) | collective-permute-done | bytes 262176 | tf_op jit(solution)/shard_map/ppermute | solution.py:28
  278.6 1.3 collective-permute-done.38.refs_7_
  279.9 2.2 final_join.1
  (155 shorter events, 16.2 us)
Async XLA Ops:
  1.2 5.8 %collective-permute-start = (bf16[4,16,768]{2,1,0:T(8,128)(2,1)S(1)}, bf16[4,16,768]{2,1,0:T(8,128)(2,1)S(1)}, u32[]{:S(2)}, u32[]{:S(2)}) collective-permute-start(bf16[4,16,768]{2,1,0:T(8,128)(2,1)S(1)} %get-tuple-element.73), channel_id=1, source_target_pairs={{0,2},{1,3},{2,0},{3,1},{4,6},{5,7},{6,4},{7,5},{8,10},{9,11},{10,... | collective-permute-start | bytes 294920 | tf_op jit(solution)/shard_map/ppermute | solution.py:28
  4.2 2.8 collective-permute-start.1
  4.2 2.1 collective-permute-start.2
  6.4 4.8 %collective-permute-start.3 = (bf16[4,16,768]{2,1,0:T(8,128)(2,1)S(1)}, bf16[4,16,768]{2,1,0:T(8,128)(2,1)S(1)}, u32[]{:S(2)}, u32[]{:S(2)}) collective-permute-start(bf16[4,16,768]{2,1,0:T(8,128)(2,1)S(1)} %collective-permute-done.2), channel_id=1, source_target_pairs={{0,2},{1,3},{2,0},{3,1},{4,6},{5,7},{6,4},{7,5},{8,10},{9,11},{10,... | collective-permute-start | bytes 294920 | tf_op jit(solution)/shard_map/ppermute | solution.py:28
  11.2 5.7 %collective-permute-start.4 = (bf16[4,16,768]{2,1,0:T(8,128)(2,1)S(1)}, bf16[4,16,768]{2,1,0:T(8,128)(2,1)S(1)}, u32[]{:S(2)}, u32[]{:S(2)}) collective-permute-start(bf16[4,16,768]{2,1,0:T(8,128)(2,1)S(1)} %get-tuple-element.76), channel_id=1, source_target_pairs={{0,4},{1,5},{2,6},{3,7},{4,0},{5,1},{6,2},{7,3},{8,12},{9,13},{10,... | collective-permute-start | bytes 294920 | tf_op jit(solution)/shard_map/ppermute | solution.py:28
  12.8 14.0 %collective-permute-start.5 = (bf16[4,16,768]{2,1,0:T(8,128)(2,1)S(1)}, bf16[4,16,768]{2,1,0:T(8,128)(2,1)S(1)}, u32[]{:S(2)}, u32[]{:S(2)}) collective-permute-start(bf16[4,16,768]{2,1,0:T(8,128)(2,1)S(1)} %get-tuple-element.78), channel_id=1, source_target_pairs={{0,8},{1,9},{2,10},{3,11},{4,12},{5,13},{6,14},{7,15},{8,0},{9,1},... | collective-permute-start | bytes 294920 | tf_op jit(solution)/shard_map/ppermute | solution.py:28
  15.4 11.4 %collective-permute-start.6 = (bf16[4,16,768]{2,1,0:T(8,128)(2,1)S(1)}, bf16[4,16,768]{2,1,0:T(8,128)(2,1)S(1)}, u32[]{:S(2)}, u32[]{:S(2)}) collective-permute-start(bf16[4,16,768]{2,1,0:T(8,128)(2,1)S(1)} %get-tuple-element.79), channel_id=1, source_target_pairs={{0,12},{1,13},{2,14},{3,15},{4,8},{5,9},{6,10},{7,11},{8,4},{9,5},... | collective-permute-start | bytes 294920 | tf_op jit(solution)/shard_map/ppermute | solution.py:28
  15.6 9.0 %copy-start.10 = (f32[4,16,16384]{2,1,0:T(8,128)S(1)}, f32[4,16,16384]{2,1,0:T(8,128)}, u32[]{:S(2)}) copy-start(f32[4,16,16384]{2,1,0:T(8,128)} %x_ref.2) | copy-start | bytes 12582916
  24.6 2.6 copy-start.11
  24.6 3.3 %copy-start.14 = (bf16[4,256,1024]{2,1,0:T(8,128)(2,1)S(1)}, bf16[4,256,1024]{2,1,0:T(8,128)(2,1)}, u32[]{:S(2)}) copy-start(bf16[4,256,1024]{2,1,0:T(8,128)(2,1)} %x_ref.3) | copy-start | bytes 6291460
  24.6 3.6 %copy-start.19 = (bf16[1024,544]{0,1:T(8,128)(2,1)S(1)}, bf16[1024,544]{0,1:T(8,128)(2,1)}, u32[]{:S(2)}) copy-start(bf16[1024,544]{0,1:T(8,128)(2,1)} %param.27) | copy-start | bytes 3342340
  24.6 3.6 %copy-start.30 = (bf16[4,16,768]{2,1,0:T(8,128)(2,1)S(1)}, bf16[4,16,768]{2,1,0:T(8,128)(2,1)}, u32[]{:S(2)}) copy-start(bf16[4,16,768]{2,1,0:T(8,128)(2,1)} %copy-done.29) | copy-start | bytes 294916
  24.6 3.5 %copy-start.35 = (f32[4,1024]{1,0:T(4,128)S(1)}, f32[4,1024]{1,0:T(4,128)}, u32[]{:S(2)}) copy-start(f32[4,1024]{1,0:T(4,128)} %w_ref.3) | copy-start | bytes 49156
  24.7 3.5 %copy-start.36 = (f32[1024]{0:T(1024)S(1)}, f32[1024]{0:T(1024)}, u32[]{:S(2)}) copy-start(f32[1024]{0:T(1024)} %param.26) | copy-start | bytes 12292
  32.1 2.2 collective-permute-start.7
  34.5 14.8 %copy-start.37 = (f32[544]{0:T(1024)S(1)}, f32[544]{0:T(1024)}, u32[]{:S(2)}) copy-start(f32[544]{0:T(1024)} %param.28) | copy-start | bytes 6532
  34.5 102.1 %collective-permute-start.19 = (bf16[1024,4096]{1,0:T(8,128)(2,1)}, bf16[1024,4096]{1,0:T(8,128)(2,1)}, u32[]{:S(2)}, u32[]{:S(2)}) collective-permute-start(bf16[1024,4096]{1,0:T(8,128)(2,1)} %hold.3), channel_id=1, source_target_pairs={{0,1},{1,0},{2,3},{3,2},{4,5},{5,4},{6,7},{7,6},{8,9},{9,8},{10,11... | collective-permute-start | bytes 25165832 | tf_op jit(solution)/shard_map/ppermute | solution.py:28
  34.7 10.0 %collective-permute-start.8 = (bf16[4,4,16,640]{3,2,1,0:T(8,128)(2,1)S(1)}, bf16[4,4,16,640]{3,2,1,0:T(8,128)(2,1)S(1)}, u32[]{:S(2)}, u32[]{:S(2)}) collective-permute-start(bf16[4,4,16,640]{3,2,1,0:T(8,128)(2,1)S(1)} %get-tuple-element.83), channel_id=1, source_target_pairs={{0,2},{1,3},{2,0},{3,1},{4,6},{5,7},{6,4},{7,5},{8,10},{9,11},{10,... | collective-permute-start | bytes 983048 | tf_op jit(solution)/shard_map/ppermute | solution.py:28
  44.8 5.0 %collective-permute-start.9 = (bf16[4,16,640]{2,1,0:T(8,128)(2,1)S(1)}, bf16[4,16,640]{2,1,0:T(8,128)(2,1)S(1)}, u32[]{:S(2)}, u32[]{:S(2)}) collective-permute-start(bf16[4,16,640]{2,1,0:T(8,128)(2,1)S(1)} %get-tuple-element.85), channel_id=1, source_target_pairs={{0,4},{1,5},{2,6},{3,7},{4,0},{5,1},{6,2},{7,3},{8,12},{9,13},{10,... | collective-permute-start | bytes 245768 | tf_op jit(solution)/shard_map/ppermute | solution.py:28
  46.1 8.9 %collective-permute-start.10 = (bf16[4,16,640]{2,1,0:T(8,128)(2,1)S(1)}, bf16[4,16,640]{2,1,0:T(8,128)(2,1)S(1)}, u32[]{:S(2)}, u32[]{:S(2)}) collective-permute-start(bf16[4,16,640]{2,1,0:T(8,128)(2,1)S(1)} %get-tuple-element.86), channel_id=1, source_target_pairs={{0,8},{1,9},{2,10},{3,11},{4,12},{5,13},{6,14},{7,15},{8,0},{9,1},... | collective-permute-start | bytes 245768 | tf_op jit(solution)/shard_map/ppermute | solution.py:28
  48.5 6.5 %collective-permute-start.11 = (bf16[4,16,640]{2,1,0:T(8,128)(2,1)S(1)}, bf16[4,16,640]{2,1,0:T(8,128)(2,1)S(1)}, u32[]{:S(2)}, u32[]{:S(2)}) collective-permute-start(bf16[4,16,640]{2,1,0:T(8,128)(2,1)S(1)} %get-tuple-element.87), channel_id=1, source_target_pairs={{0,12},{1,13},{2,14},{3,15},{4,8},{5,9},{6,10},{7,11},{8,4},{9,5},... | collective-permute-start | bytes 245768 | tf_op jit(solution)/shard_map/ppermute | solution.py:28
  55.1 6.6 %collective-permute-start.14 = (bf16[4,16,640]{2,1,0:T(8,128)(2,1)S(1)}, bf16[4,16,640]{2,1,0:T(8,128)(2,1)S(1)}, u32[]{:S(2)}, u32[]{:S(2)}) collective-permute-start(bf16[4,16,640]{2,1,0:T(8,128)(2,1)S(1)} %norm.1.refs_0_), channel_id=1, source_target_pairs={{0,12},{1,13},{2,14},{3,15},{4,8},{5,9},{6,10},{7,11},{8,4},{9,5},... | collective-permute-start | bytes 245768 | tf_op jit(solution)/shard_map/ppermute | solution.py:28
  57.4 6.9 %collective-permute-start.13 = (bf16[4,16,640]{2,1,0:T(8,128)(2,1)S(1)}, bf16[4,16,640]{2,1,0:T(8,128)(2,1)S(1)}, u32[]{:S(2)}, u32[]{:S(2)}) collective-permute-start(bf16[4,16,640]{2,1,0:T(8,128)(2,1)S(1)} %norm.1.refs_0_), channel_id=1, source_target_pairs={{0,8},{1,9},{2,10},{3,11},{4,12},{5,13},{6,14},{7,15},{8,0},{9,1},... | collective-permute-start | bytes 245768 | tf_op jit(solution)/shard_map/ppermute | solution.py:28
  58.1 6.2 %collective-permute-start.12 = (bf16[4,16,640]{2,1,0:T(8,128)(2,1)S(1)}, bf16[4,16,640]{2,1,0:T(8,128)(2,1)S(1)}, u32[]{:S(2)}, u32[]{:S(2)}) collective-permute-start(bf16[4,16,640]{2,1,0:T(8,128)(2,1)S(1)} %norm.1.refs_0_), channel_id=1, source_target_pairs={{0,4},{1,5},{2,6},{3,7},{4,0},{5,1},{6,2},{7,3},{8,12},{9,13},{10,... | collective-permute-start | bytes 245768 | tf_op jit(solution)/shard_map/ppermute | solution.py:28
  64.3 5.0 %copy-start.38 = (s32[16]{0:T(128)S(1)}, s32[16]{0:T(128)}, u32[]{:S(2)}) copy-start(s32[16]{0:T(128)} %param.21) | copy-start | bytes 196
  64.3 33.1 %copy-start.3 = (bf16[512,1024]{1,0:T(8,128)(2,1)S(1)}, bf16[512,1024]{1,0:T(8,128)(2,1)}, u32[]{:S(2)}) copy-start(bf16[512,1024]{1,0:T(8,128)(2,1)} %refs_4_.14) | copy-start | bytes 3145732
  64.3 33.1 %copy-start.31 = (f32[1024]{0:T(1024)S(1)}, f32[1024]{0:T(1024)}, u32[]{:S(2)}) copy-start(f32[1024]{0:T(1024)} %param.30) | copy-start | bytes 12292
  64.3 33.7 %copy-start.2 = (bf16[4,256,1024]{2,1,0:T(8,128)(2,1)S(1)}, bf16[4,256,1024]{2,1,0:T(8,128)(2,1)}, u32[]{:S(2)}) copy-start(bf16[4,256,1024]{2,1,0:T(8,128)(2,1)} %refs_4_.15) | copy-start | bytes 6291460
  64.4 33.7 %copy-start.15 = (f32[16,1024]{1,0:T(8,128)S(1)}, f32[16,1024]{1,0:T(8,128)}, u32[]{:S(2)}) copy-start(f32[16,1024]{1,0:T(8,128)} %refs_5_.9) | copy-start | bytes 196612
  64.4 33.7 %copy-start.32 = (f32[1024]{0:T(1024)S(1)}, f32[1024]{0:T(1024)}, u32[]{:S(2)}) copy-start(f32[1024]{0:T(1024)} %param.32) | copy-start | bytes 12292
  64.4 59.2 %all-to-all-start = ((bf16[16,64,1024]{2,1,0:T(8,128)(2,1)}), bf16[16,64,1024]{2,1,0:T(8,128)(2,1)}, u32[]{:S(2)}, u32[]{:S(2)}) async-start(bf16[16,64,1024]{2,1,0:T(8,128)(2,1)} %hold.2.after_ref.refs_0_), calls=%async_computation | async-start | bytes 4194304 | tf_op jit(solution)/shard_map/all_to_all | solution.py:706
  69.5 26.3 %collective-permute-start.15 = (bf16[4,4,16,640]{3,2,1,0:T(8,128)(2,1)S(1)}, bf16[4,4,16,640]{3,2,1,0:T(8,128)(2,1)S(1)}, u32[]{:S(2)}, u32[]{:S(2)}) collective-permute-start(bf16[4,4,16,640]{3,2,1,0:T(8,128)(2,1)S(1)} %merge_z.1.after_ref.refs_0_), channel_id=1, source_target_pairs={{0,2},{1,3},{2,0},{3,1},{4,6},{5,7},{6,4},{7,5},{8,10},{9,11},{10,... | collective-permute-start | bytes 983048 | tf_op jit(solution)/shard_map/ppermute | solution.py:28
  72.1 23.8 %collective-permute-start.16 = (bf16[4,4,16,640]{3,2,1,0:T(8,128)(2,1)S(1)}, bf16[4,4,16,640]{3,2,1,0:T(8,128)(2,1)S(1)}, u32[]{:S(2)}, u32[]{:S(2)}) collective-permute-start(bf16[4,4,16,640]{3,2,1,0:T(8,128)(2,1)S(1)} %merge_z.1.after_ref.refs_0_), channel_id=1, source_target_pairs={{0,1},{1,0},{2,3},{3,2},{4,5},{5,4},{6,7},{7,6},{8,9},{9,8},{10,11... | collective-permute-start | bytes 983048 | tf_op jit(solution)/shard_map/ppermute | solution.py:28
  95.8 21.5 %copy-start.4 = (bf16[4,4,16,640]{3,2,1,0:T(8,128)(2,1)}, bf16[4,4,16,640]{3,2,1,0:T(8,128)(2,1)S(1)}, u32[]{:S(2)}) copy-start(bf16[4,4,16,640]{3,2,1,0:T(8,128)(2,1)S(1)} %collective-permute-done.15.refs_1_) | copy-start | bytes 983044
  95.8 1.6 collective-permute-start.17
  95.8 21.4 %copy-start.6 = (bf16[4,4,16,640]{3,2,1,0:T(8,128)(2,1)}, bf16[4,4,16,640]{3,2,1,0:T(8,128)(2,1)S(1)}, u32[]{:S(2)}) copy-start(bf16[4,4,16,640]{3,2,1,0:T(8,128)(2,1)S(1)} %collective-permute-done.16.refs_2_) | copy-start | bytes 983044
  97.4 19.9 %copy-start.8 = (bf16[4,4,16,640]{3,2,1,0:T(8,128)(2,1)}, bf16[4,4,16,640]{3,2,1,0:T(8,128)(2,1)S(1)}, u32[]{:S(2)}) copy-start(bf16[4,4,16,640]{3,2,1,0:T(8,128)(2,1)S(1)} %collective-permute-done.17.refs_3_) | copy-start | bytes 983044
  98.1 19.2 %copy-start.1 = (f32[4,256,1024]{2,1,0:T(8,128)S(1)}, f32[4,256,1024]{2,1,0:T(8,128)}, u32[]{:S(2)}) copy-start(f32[4,256,1024]{2,1,0:T(8,128)} %copy-done) | copy-start | bytes 12582916
  123.6 10.6 %copy-start.13 = (bf16[256,1024]{1,0:T(8,128)(2,1)S(1)}, bf16[256,1024]{1,0:T(8,128)(2,1)}, u32[]{:S(2)}) copy-start(bf16[256,1024]{1,0:T(8,128)(2,1)} %copy-done.12) | copy-start | bytes 1572868
  134.5 10.6 %copy-start.18 = (f32[256,128]{1,0:T(8,128)S(1)}, f32[256,128]{1,0:T(8,128)}, u32[]{:S(2)}) copy-start(f32[256,128]{1,0:T(8,128)} %copy-done.16) | copy-start | bytes 393220
  134.5 10.6 %copy-start.21 = (f32[256,1024]{1,0:T(8,128)S(1)}, f32[256,1024]{1,0:T(8,128)}, u32[]{:S(2)}) copy-start(f32[256,1024]{1,0:T(8,128)} %copy-done.20) | copy-start | bytes 3145732
  134.6 2.0 collective-permute-start.18
  145.1 25.3 %collective-permute-start.21 = (bf16[128,4096]{1,0:T(8,128)(2,1)S(1)}, bf16[128,4096]{1,0:T(8,128)(2,1)S(1)}, u32[]{:S(2)}, u32[]{:S(2)}) collective-permute-start(bf16[128,4096]{1,0:T(8,128)(2,1)S(1)} %get-tuple-element.103), channel_id=1, source_target_pairs={{0,2},{1,3},{2,0},{3,1},{4,6},{5,7},{6,4},{7,5},{8,10},{9,11},{10,... | collective-permute-start | bytes 3145736 | tf_op jit(solution)/shard_map/ppermute | solution.py:28
  145.2 11.6 %copy-start.5 = (bf16[4,4,16,640]{3,2,1,0:T(8,128)(2,1)S(1)}, bf16[4,4,16,640]{3,2,1,0:T(8,128)(2,1)}, u32[]{:S(2)}) copy-start(bf16[4,4,16,640]{3,2,1,0:T(8,128)(2,1)} %copy-done.4) | copy-start | bytes 983044
  145.2 11.6 %copy-start.7 = (bf16[4,4,16,640]{3,2,1,0:T(8,128)(2,1)S(1)}, bf16[4,4,16,640]{3,2,1,0:T(8,128)(2,1)}, u32[]{:S(2)}) copy-start(bf16[4,4,16,640]{3,2,1,0:T(8,128)(2,1)} %copy-done.6) | copy-start | bytes 983044
  145.2 11.6 %copy-start.9 = (bf16[4,4,16,640]{3,2,1,0:T(8,128)(2,1)S(1)}, bf16[4,4,16,640]{3,2,1,0:T(8,128)(2,1)}, u32[]{:S(2)}) copy-start(bf16[4,4,16,640]{3,2,1,0:T(8,128)(2,1)} %copy-done.8) | copy-start | bytes 983044
  157.7 2.0 collective-permute-start.20
  168.3 31.8 %collective-permute-start.25 = (bf16[128,4096]{1,0:T(8,128)(2,1)S(1)}, bf16[128,4096]{1,0:T(8,128)(2,1)S(1)}, u32[]{:S(2)}, u32[]{:S(2)}) collective-permute-start(bf16[128,4096]{1,0:T(8,128)(2,1)S(1)} %get-tuple-element.114), channel_id=1, source_target_pairs={{0,2},{1,3},{2,0},{3,1},{4,6},{5,7},{6,4},{7,5},{8,10},{9,11},{10,... | collective-permute-start | bytes 3145736 | tf_op jit(solution)/shard_map/ppermute | solution.py:28
  170.6 13.7 %collective-permute-start.23 = (bf16[2,32,4096]{2,1,0:T(8,128)(2,1)S(1)}, bf16[2,32,4096]{2,1,0:T(8,128)(2,1)S(1)}, u32[]{:S(2)}, u32[]{:S(2)}) collective-permute-start(bf16[2,32,4096]{2,1,0:T(8,128)(2,1)S(1)} %get-tuple-element.109), channel_id=1, source_target_pairs={{0,4},{1,5},{2,6},{3,7},{4,0},{5,1},{6,2},{7,3},{8,12},{9,13},{10,... | collective-permute-start | bytes 1572872 | tf_op jit(solution)/shard_map/ppermute | solution.py:28
  183.1 4.3 %collective-permute-start.22 = (bf16[256,1024]{1,0:T(8,128)(2,1)S(1)}, bf16[256,1024]{1,0:T(8,128)(2,1)S(1)}, u32[]{:S(2)}, u32[]{:S(2)}) collective-permute-start(bf16[256,1024]{1,0:T(8,128)(2,1)S(1)} %fix.6.after_ref.own_ref), channel_id=1, source_target_pairs={{0,1},{1,0},{2,3},{3,2},{4,5},{5,4},{6,7},{7,6},{8,9},{9,8},{10,11... | collective-permute-start | bytes 1572872 | tf_op jit(solution)/shard_map/ppermute | solution.py:28
  184.5 15.5 %collective-permute-start.24 = (bf16[1,32,4096]{2,1,0:T(8,128)(2,1)S(1)}, bf16[1,32,4096]{2,1,0:T(8,128)(2,1)S(1)}, u32[]{:S(2)}, u32[]{:S(2)}) collective-permute-start(bf16[1,32,4096]{2,1,0:T(8,128)(2,1)S(1)} %get-tuple-element.112), channel_id=1, source_target_pairs={{0,8},{1,9},{2,10},{3,11},{4,12},{5,13},{6,14},{7,15},{8,0},{9,1},... | collective-permute-start | bytes 786440 | tf_op jit(solution)/shard_map/ppermute | solution.py:28
  196.0 27.3 %collective-permute-start.28 = (bf16[128,4096]{1,0:T(8,128)(2,1)S(1)}, bf16[128,4096]{1,0:T(8,128)(2,1)S(1)}, u32[]{:S(2)}, u32[]{:S(2)}) collective-permute-start(bf16[128,4096]{1,0:T(8,128)(2,1)S(1)} %get-tuple-element.121), channel_id=1, source_target_pairs={{0,2},{1,3},{2,0},{3,1},{4,6},{5,7},{6,4},{7,5},{8,10},{9,11},{10,... | collective-permute-start | bytes 3145736 | tf_op jit(solution)/shard_map/ppermute | solution.py:28
  200.4 13.8 %collective-permute-start.27 = (bf16[2,32,4096]{2,1,0:T(8,128)(2,1)S(1)}, bf16[2,32,4096]{2,1,0:T(8,128)(2,1)S(1)}, u32[]{:S(2)}, u32[]{:S(2)}) collective-permute-start(bf16[2,32,4096]{2,1,0:T(8,128)(2,1)S(1)} %get-tuple-element.118), channel_id=1, source_target_pairs={{0,4},{1,5},{2,6},{3,7},{4,0},{5,1},{6,2},{7,3},{8,12},{9,13},{10,... | collective-permute-start | bytes 1572872 | tf_op jit(solution)/shard_map/ppermute | solution.py:28
  209.8 4.5 %collective-permute-start.26 = (bf16[256,1024]{1,0:T(8,128)(2,1)S(1)}, bf16[256,1024]{1,0:T(8,128)(2,1)S(1)}, u32[]{:S(2)}, u32[]{:S(2)}) collective-permute-start(bf16[256,1024]{1,0:T(8,128)(2,1)S(1)} %fix.7.after_ref.own_ref), channel_id=1, source_target_pairs={{0,1},{1,0},{2,3},{3,2},{4,5},{5,4},{6,7},{7,6},{8,9},{9,8},{10,11... | collective-permute-start | bytes 1572872 | tf_op jit(solution)/shard_map/ppermute | solution.py:28
  222.9 24.2 %collective-permute-start.31 = (bf16[128,4096]{1,0:T(8,128)(2,1)S(1)}, bf16[128,4096]{1,0:T(8,128)(2,1)S(1)}, u32[]{:S(2)}, u32[]{:S(2)}) collective-permute-start(bf16[128,4096]{1,0:T(8,128)(2,1)S(1)} %get-tuple-element.127), channel_id=1, source_target_pairs={{0,2},{1,3},{2,0},{3,1},{4,6},{5,7},{6,4},{7,5},{8,10},{9,11},{10,... | collective-permute-start | bytes 3145736 | tf_op jit(solution)/shard_map/ppermute | solution.py:28
  223.5 18.4 %collective-permute-start.30 = (bf16[2,32,4096]{2,1,0:T(8,128)(2,1)S(1)}, bf16[2,32,4096]{2,1,0:T(8,128)(2,1)S(1)}, u32[]{:S(2)}, u32[]{:S(2)}) collective-permute-start(bf16[2,32,4096]{2,1,0:T(8,128)(2,1)S(1)} %get-tuple-element.125), channel_id=1, source_target_pairs={{0,4},{1,5},{2,6},{3,7},{4,0},{5,1},{6,2},{7,3},{8,12},{9,13},{10,... | collective-permute-start | bytes 1572872 | tf_op jit(solution)/shard_map/ppermute | solution.py:28
  223.9 16.1 %collective-permute-start.29 = (bf16[1,32,4096]{2,1,0:T(8,128)(2,1)S(1)}, bf16[1,32,4096]{2,1,0:T(8,128)(2,1)S(1)}, u32[]{:S(2)}, u32[]{:S(2)}) collective-permute-start(bf16[1,32,4096]{2,1,0:T(8,128)(2,1)S(1)} %get-tuple-element.123), channel_id=1, source_target_pairs={{0,8},{1,9},{2,10},{3,11},{4,12},{5,13},{6,14},{7,15},{8,0},{9,1},... | collective-permute-start | bytes 786440 | tf_op jit(solution)/shard_map/ppermute | solution.py:28
  247.4 17.7 %collective-permute-start.33 = (bf16[2,32,4096]{2,1,0:T(8,128)(2,1)S(1)}, bf16[2,32,4096]{2,1,0:T(8,128)(2,1)S(1)}, u32[]{:S(2)}, u32[]{:S(2)}) collective-permute-start(bf16[2,32,4096]{2,1,0:T(8,128)(2,1)S(1)} %get-tuple-element.131), channel_id=1, source_target_pairs={{0,4},{1,5},{2,6},{3,7},{4,0},{5,1},{6,2},{7,3},{8,12},{9,13},{10,... | collective-permute-start | bytes 1572872 | tf_op jit(solution)/shard_map/ppermute | solution.py:28
  248.1 15.5 %collective-permute-start.32 = (bf16[1,32,4096]{2,1,0:T(8,128)(2,1)S(1)}, bf16[1,32,4096]{2,1,0:T(8,128)(2,1)S(1)}, u32[]{:S(2)}, u32[]{:S(2)}) collective-permute-start(bf16[1,32,4096]{2,1,0:T(8,128)(2,1)S(1)} %get-tuple-element.129), channel_id=1, source_target_pairs={{0,8},{1,9},{2,10},{3,11},{4,12},{5,13},{6,14},{7,15},{8,0},{9,1},... | collective-permute-start | bytes 786440 | tf_op jit(solution)/shard_map/ppermute | solution.py:28
  265.2 13.2 %collective-permute-start.34 = (bf16[1,32,4096]{2,1,0:T(8,128)(2,1)S(1)}, bf16[1,32,4096]{2,1,0:T(8,128)(2,1)S(1)}, u32[]{:S(2)}, u32[]{:S(2)}) collective-permute-start(bf16[1,32,4096]{2,1,0:T(8,128)(2,1)S(1)} %get-tuple-element.133), channel_id=1, source_target_pairs={{0,8},{1,9},{2,10},{3,11},{4,12},{5,13},{6,14},{7,15},{8,0},{9,1},... | collective-permute-start | bytes 786440 | tf_op jit(solution)/shard_map/ppermute | solution.py:28
  267.2 11.4 %collective-permute-start.35 = (bf16[16,4096]{1,0:T(8,128)(2,1)S(1)}, bf16[16,4096]{1,0:T(8,128)(2,1)S(1)}, u32[]{:S(2)}, u32[]{:S(2)}) collective-permute-start(bf16[16,4096]{1,0:T(8,128)(2,1)S(1)} %get-tuple-element.135), channel_id=1, source_target_pairs={{0,1},{1,0},{2,3},{3,2},{4,5},{5,4},{6,7},{7,6},{8,9},{9,8},{10,11... | collective-permute-start | bytes 393224 | tf_op jit(solution)/shard_map/ppermute | solution.py:28
  267.2 11.4 %collective-permute-start.36 = (bf16[16,4096]{1,0:T(8,128)(2,1)S(1)}, bf16[16,4096]{1,0:T(8,128)(2,1)S(1)}, u32[]{:S(2)}, u32[]{:S(2)}) collective-permute-start(bf16[16,4096]{1,0:T(8,128)(2,1)S(1)} %get-tuple-element.136), channel_id=1, source_target_pairs={{0,1},{1,0},{2,3},{3,2},{4,5},{5,4},{6,7},{7,6},{8,9},{9,8},{10,11... | collective-permute-start | bytes 393224 | tf_op jit(solution)/shard_map/ppermute | solution.py:28
  267.7 10.9 %collective-permute-start.37 = (bf16[16,4096]{1,0:T(8,128)(2,1)S(1)}, bf16[16,4096]{1,0:T(8,128)(2,1)S(1)}, u32[]{:S(2)}, u32[]{:S(2)}) collective-permute-start(bf16[16,4096]{1,0:T(8,128)(2,1)S(1)} %get-tuple-element.137), channel_id=1, source_target_pairs={{0,1},{1,0},{2,3},{3,2},{4,5},{5,4},{6,7},{7,6},{8,9},{9,8},{10,11... | collective-permute-start | bytes 393224 | tf_op jit(solution)/shard_map/ppermute | solution.py:28
  278.5 1.4 collective-permute-start.38
  (15 other events, 14.5 us)

commit v10 on v9

--- a/solution.py
+++ b/solution.py
@@ -547,7 +547,7 @@
         after,
         BF16,
         [pltpu.VMEM((c // 128, count * STATE, 128), F32), pltpu.VMEM((STATE, count, c), F32)],
-        32,
+        40,
     )
     return out
 
@@ -576,11 +576,13 @@
     keep_ref[...] = total[half:].astype(BF16)
 
 
-def out_project(me, own, other, out_weight, other_weight, after):
+def out_project(me, own, other, out_weight, other_weight, after, part, parts):
     rows, c = own.shape
-    cols = out_weight.shape[1] // 2
     tile = 1024
-    tiles = cols // tile
+    every = out_weight.shape[1] // 2 // tile
+    tiles = every // parts
+    cols = tiles * tile
+    first = part * tiles
     half = jax.ShapeDtypeStruct((rows // 2, cols), BF16)
     return pl.pallas_call(
         out_kernel,
@@ -590,8 +592,8 @@
             in_specs=[
                 pl.BlockSpec(memory_space=pltpu.VMEM),
                 pl.BlockSpec(memory_space=pltpu.VMEM),
-                pl.BlockSpec((c, tile), lambda j, me_ref: (0, (me_ref[0] % 2) * tiles + j)),
-                pl.BlockSpec((c, tile), lambda j, me_ref: (0, j)),
+                pl.BlockSpec((c, tile), lambda j, me_ref: (0, (me_ref[0] % 2) * every + first + j)),
+                pl.BlockSpec((c, tile), lambda j, me_ref: (0, first + j)),
             ]
             + [pl.BlockSpec(memory_space=pl.ANY)] * len(after),
             out_specs=[pl.BlockSpec((rows // 2, tile), lambda j, me_ref: (0, j))] * 2,
@@ -619,32 +621,46 @@
     left_ref[...] = jnp.where(core == 0, low, high).astype(BF16)
 
 
-def final_kernel(tiles, me_ref, *refs):
+def final_kernel(tiles, counts, me_ref, *refs):
     o_ref = refs[-1]
     own_half = pl.program_id(0) // tiles == me_ref[0] % 2
-    parts = []
-    for t in range(STEPS):
-        value = jnp.where(own_half, refs[t][...].astype(F32), refs[STEPS + t][...].astype(F32))
+    tile = pl.program_id(0) % tiles
+    at = 0
+    for t, count in enumerate(counts):
+        value = None
+        for part in range(count):
+            mine, theirs = refs[at][...].astype(F32), refs[at + 1][...].astype(F32)
+            here = jnp.where(own_half, mine, theirs)
+            value = here if value is None else jnp.where(tile == part, here, value)
+            at += 2
         o_ref[:, t, :] = value.astype(BF16)
 
 
-def final_join(me, keeps, gots):
-    own, cols = keeps[0].shape
-    tile = 2048
-    tiles = cols // tile
+def final_join(me, pieces):
+    own = pieces[0][0][0].shape[0]
+    cols = sum(keep.shape[1] for keep, _ in pieces[0])
+    tiles = max(len(parts) for parts in pieces)
+    tile = cols // tiles
+    args, specs = [], []
+    for parts in pieces:
+        for keep, got in parts:
+            many = keep.shape[1] // tile
+            spec = pl.BlockSpec((own, tile), lambda j, me_ref, many=many: (0, (j % tiles) % many))
+            args += [keep, got]
+            specs += [spec, spec]
     return pl.pallas_call(
-        functools.partial(final_kernel, tiles),
+        functools.partial(final_kernel, tiles, [len(parts) for parts in pieces]),
         grid_spec=pltpu.PrefetchScalarGridSpec(
             num_scalar_prefetch=1,
             grid=(2 * tiles,),
-            in_specs=[pl.BlockSpec((own, tile), lambda j, me_ref: (0, j % tiles))] * (2 * STEPS),
+            in_specs=specs,
             out_specs=pl.BlockSpec((own, STEPS, tile), lambda j, me_ref: (0, 0, j)),
         ),
         out_shape=jax.ShapeDtypeStruct((own, STEPS, 2 * cols), BF16),
         compiler_params=params(16),
         cost_estimate=cost(0, own * cols * 32),
         name="final_join",
-    )(me, *keeps, *gots)
+    )(me, *args)
 
 
 def shards(
@@ -732,47 +748,67 @@
         (gated[t],) = small(kernel, me, [live_row, gated[t], live_gated], [(rows, c)], "fix", (after,))
         return gated[t]
 
-    def project(t, after):
-        sends[t], keeps[t] = out_project(me, gated[t], swap(gated[t], 1, n), out_weight, other_weight, (after,))
-        return keeps[t]
-
-    def reduce(t, stage, after):
+    def project(t, after, parts=1):
+        other = swap(gated[t], 1, n)
+        for part in range(parts):
+            sends[t, part], keeps[t, part] = out_project(
+                me, gated[t], other, out_weight, other_weight, (after,), part, parts
+            )
+            after = keeps[t, part]
+        return after
+
+    def reduce(t, stage, after, part=0):
+        at = t, part
+        width = keeps[at].shape[-1]
         if stage == 0:
-            keep, got = keeps[t].reshape(zs, take, cols), swap(sends[t], 2, n).reshape(zs, take, cols)
+            keep = keeps[at].reshape(zs, take, width)
+            got = swap(sends[at], 2, n).reshape(zs, take, width)
         else:
-            keep, got = keeps[t], swap(sends[t], 2 << stage, n)
+            keep, got = keeps[at], swap(sends[at], 2 << stage, n)
         if stage < stages:
-            kernel, shape = functools.partial(halve_kernel, stage), (keep.shape[0] // 2, take, cols)
+            kernel, shape = functools.partial(halve_kernel, stage), (keep.shape[0] // 2, take, width)
         else:
-            kernel, shape = sum_z_kernel, (take // 2, cols)
-        sends[t], keeps[t] = small(kernel, me, [keep, got], [shape] * 2, "reduce_%d" % stage, (after,))
+            kernel, shape = sum_z_kernel, (take // 2, width)
+        sends[at], keeps[at] = small(kernel, me, [keep, got], [shape] * 2, "reduce_%d" % stage, (after,))
         if stage == stages:
-            sends[t] = swap(sends[t], 1, n)
-        return keeps[t]
+            sends[at] = swap(sends[at], 1, n)
+        return keeps[at]
 
     last = s_step(0, (packed,))
     gathered = gather_live(me, (last,), row_of_live, lows, conv, step_z, dt_proj, rate_bias, n)
     live_gated = live_steps(slot_of_live, (last,), moved_state, gathered, a_log, skip)
     last = fix(0, live_gated)
     last = project(0, last)
-    for t in range(1, STEPS):
+    for t in range(1, STEPS - 1):
         last = s_step(t, (last,))
         last = fix(t, last)
+        last = project(t, last)
         if t > 1:
             for stage in range(1, stages):
                 last = reduce(t - 2, stage, last)
-        last = project(t, last)
-        if 1 < t < STEPS - 1:
-            last = reduce(t - 2, stages, last)
         last = reduce(t - 1, 0, last)
-    last = reduce(STEPS - 3, stages, last)
+    t = STEPS - 1
+    last = s_step(t, (last,))
+    last = fix(t, last)
+    last = project(t, last, 2)
     for stage in range(1, stages):
-        last = reduce(STEPS - 2, stage, last)
-    last = reduce(STEPS - 1, 0, last)
-    last = reduce(STEPS - 2, stages, last)
-    for stage in range(1, stages + 1):
-        last = reduce(STEPS - 1, stage, last)
-    return final_join(me, [keeps[t] for t in range(STEPS)], [sends[t] for t in range(STEPS)])
+        last = reduce(t - 2, stage, last)
+    last = reduce(t - 3, stages, last)
+    last = reduce(t - 1, 0, last)
+    for stage in range(1, stages):
+        last = reduce(t - 1, stage, last)
+    last = reduce(t - 2, stages, last)
+    last = reduce(t, 0, last, 0)
+    for stage in range(1, stages):
+        last = reduce(t, stage, last, 0)
+    last = reduce(t - 1, stages, last)
+    last = reduce(t, 0, last, 1)
+    for stage in range(1, stages):
+        last = reduce(t, stage, last, 1)
+    last = reduce(t, stages, last, 0)
+    last = reduce(t, stages, last, 1)
+    pieces = [[(keeps[t, part], sends[t, part]) for part in range(1 if t < STEPS - 1 else 2)] for t in range(STEPS)]
+    return final_join(me, pieces)
 
 
 def solution(mesh):

time: 283 us -> 283 us (level)
  waiting for transfers between devices: 116 us -> 106 us
  starting transfers between devices: 35.9 us -> 45 us
    ppermute x39 -> x43, waiting for transfers between devices: 116 us -> 106 us  [swap(): return lax.ppermute(x, 'dex', [(i, i ^ mask) for i in range(n)])]
    ppermute x39 -> x43, starting transfers between devices: 31 us -> 40.1 us  [swap(): return lax.ppermute(x, 'dex', [(i, i ^ mask) for i in range(n)])]
    pallas_call x4 -> x5, Pallas kernels: 34.2 us -> 35.4 us  [out_project(): pl.pallas_call(out_kernel, grid_spec=pltpu.PrefetchScalarGridSpec(num_sca...]
    pallas_call x28 -> x31, Pallas kernels: 14.3 us -> 14.3 us  [small(): pl.pallas_call(kernel, in_specs=[pl.BlockSpec(memory_space=pltpu.SMEM)] +...]
  transfers between devices with their start and end apart: 40 -> 44, of which waited for: 23 -> 22; matrix products, arithmetic and copies ran while one was open for 1% -> 1% of each run, Pallas kernels for 35% -> 35%
where the time goes in v10:
time: 283 us; the launch traced here: 282 us
  Pallas kernels  114 us (40%)
  waiting for transfers between devices  106 us (37%)
  starting transfers between devices  45 us (16%)
  local copies, waits for them, and re-layouts  14.9 us (5%)
    ppermute x43, waiting for transfers between devices, swap(): return lax.ppermute(x, 'dex', [(i, i ^ mask) for i in range(n)])  106 us
    pallas_call x4, Pallas kernels, state_step(): pl.pallas_call(functools.partial(state_kernel, t, len(after)), grid_spec=...  49 us
    ppermute x43, starting transfers between devices, swap(): return lax.ppermute(x, 'dex', [(i, i ^ mask) for i in range(n)])  40.1 us
    pallas_call x5, Pallas kernels, out_project(): pl.pallas_call(out_kernel, grid_spec=pltpu.PrefetchScalarGridSpec(num_sca...  35.4 us
    pallas_call x31, Pallas kernels, small(): pl.pallas_call(kernel, in_specs=[pl.BlockSpec(memory_space=pltpu.SMEM)] +...  14.3 us
    unnamed x78, local copies, waits for them, and re-layouts  13.6 us
    pallas_call x1, Pallas kernels, weight_half(): pl.pallas_call(half_kernel, grid_spec=pltpu.PrefetchScalarGridSpec(num_sc...  7.13 us
  transfers between devices with their start and end apart: 44, of which 22 were waited for; matrix products, arithmetic and copies ran while one was open for 1% of the time, Pallas kernels for 35%

profile of v10, /device:TPU:0, one launch (start us, length us, event | category | flops | bytes accessed | tf_op | source)
XLA Modules:
  0.0 282.1 jit_solution(5660273895546880962)
XLA Ops:
  0.0 1.1 copy-done.22
  1.2 3.0 %collective-permute-start = (bf16[4,16,768]{2,1,0:T(8,128)(2,1)S(1)}, bf16[4,16,768]{2,1,0:T(8,128)(2,1)S(1)}, u32[]{:S(2)}, u32[]{:S(2)}) collective-permute-start(bf16[4,16,768]{2,1,0:T(8,128)(2,1)S(1)} %get-tuple-element.81), channel_id=1, source_target_pairs={{0,2},{1,3},{2,0},{3,1},{4,6},{5,7},{6,4},{7,5},{8,10},{9,11},{10,... | collective-permute-start | bytes 294920 | tf_op jit(solution)/shard_map/ppermute | solution.py:28
  7.0 4.1 %collective-permute-done.3.refs_3_ = bf16[4,16,768]{2,1,0:T(8,128)(2,1)S(1)} collective-permute-done((bf16[4,16,768]{2,1,0:T(8,128)(2,1)S(1)}, bf16[4,16,768]{2,1,0:T(8,128)(2,1)S(1)}, u32[]{:S(2)}, u32[]{:S(2)}) %collective-permute-start.3) | collective-permute-done | bytes 98336 | tf_op jit(solution)/shard_map/ppermute | solution.py:28
  11.2 1.6 collective-permute-start.4
  12.8 2.6 collective-permute-start.5
  15.6 1.2 collective-permute-done.4.after_ref.refs_1_
  17.5 7.1 %weight_half.1.refs_0_.x_ref = bf16[1024,4096]{1,0:T(8,128)(2,1)} custom-call(s32[1]{0:T(128)} %bitcast.me_ref, bf16[4,16,768]{2,1,0:T(8,128)(2,1)} %copy-done.29, bf16[1024,8192]{1,0:T(8,128)(2,1)} %wown_ref.9), custom_call_target="tpu_custom_call" | custom-call | flops 1024 | bytes 1024 | tf_op jit(solution)/shard_map/weight_half/pallas_call | solution.py:147
  24.7 2.1 pack_state.1.refs_4_.x_ref
  27.1 0.8 copy-done.14
  28.2 3.9 %conv_project.1 = (f32[4,256,1024]{2,1,0:T(8,128)S(1)}, bf16[8,4,16,640]{3,2,1,0:T(8,128)(2,1)S(1)}, bf16[8,4,16,640]{3,2,1,0:T(8,128)(2,1)S(1)}) custom-call(s32[1]{0:T(128)} %bitcast.me_ref, s32[4,256]{1,0:T(4,128)S(1)} %broadcast_select_fusion.1.target_ref, f32[3,256,1024]{2,1,0:T(8,128)S(1)} %bitcast.38, bf16[4,256,1024]{2,1,0:T(8,128)(2,1)S(1)} %copy-done.14, ...), custom_call_target="tpu_custom_call" | custom-call | flops 1024 | bytes 1024 | tf_op jit(solution)/shard_map/conv_project/pallas_call | solution.py:212
  32.2 2.1 collective-permute-done.7.refs_1_
  35.0 9.7 %collective-permute-done.8.refs_1_ = bf16[4,4,16,640]{3,2,1,0:T(8,128)(2,1)S(1)} collective-permute-done((bf16[4,4,16,640]{3,2,1,0:T(8,128)(2,1)S(1)}, bf16[4,4,16,640]{3,2,1,0:T(8,128)(2,1)S(1)}, u32[]{:S(2)}, u32[]{:S(2)}) %collective-permute-start.8) | collective-permute-done | bytes 327712 | tf_op jit(solution)/shard_map/ppermute | solution.py:28
  44.8 1.3 collective-permute-start.9
  46.1 2.4 collective-permute-start.10
  48.4 0.8 collective-permute-start.11
  49.7 5.2 %collective-permute-done.10.refs_2_ = bf16[4,16,640]{2,1,0:T(8,128)(2,1)S(1)} collective-permute-done((bf16[4,16,640]{2,1,0:T(8,128)(2,1)S(1)}, bf16[4,16,640]{2,1,0:T(8,128)(2,1)S(1)}, u32[]{:S(2)}, u32[]{:S(2)}) %collective-permute-start.10) | collective-permute-done | bytes 81952 | tf_op jit(solution)/shard_map/ppermute | solution.py:28
  55.1 2.2 collective-permute-start.14
  58.1 1.5 collective-permute-start.12
  59.6 2.2 collective-permute-done.14.refs_3_
  61.7 2.5 collective-permute-done.13.refs_2_
  64.4 4.9 %all-to-all-start = ((bf16[16,64,1024]{2,1,0:T(8,128)(2,1)}), bf16[16,64,1024]{2,1,0:T(8,128)(2,1)}, u32[]{:S(2)}, u32[]{:S(2)}) async-start(bf16[16,64,1024]{2,1,0:T(8,128)(2,1)} %hold.2.after_ref.refs_0_), calls=%async_computation | async-start | bytes 4194304 | tf_op jit(solution)/shard_map/all_to_all | solution.py:722
  69.4 1.6 collective-permute-start.15
  72.1 23.7 %collective-permute-done.15.refs_1_ = bf16[4,4,16,640]{3,2,1,0:T(8,128)(2,1)S(1)} collective-permute-done((bf16[4,4,16,640]{3,2,1,0:T(8,128)(2,1)S(1)}, bf16[4,4,16,640]{3,2,1,0:T(8,128)(2,1)S(1)}, u32[]{:S(2)}, u32[]{:S(2)}) %collective-permute-start.15) | collective-permute-done | bytes 327712 | tf_op jit(solution)/shard_map/ppermute | solution.py:28
  95.8 1.6 collective-permute-done.17.refs_3_
  98.1 16.7 %state_step.4 = (bf16[16,256,1024]{2,1,0:T(8,128)(2,1)}, bf16[256,1024]{1,0:T(8,128)(2,1)S(1)}) custom-call(s32[1]{0:T(128)} %bitcast.me_ref, bf16[16,64,1024]{2,1,0:T(8,128)(2,1)} %hold.2.after_ref.refs_0_, f32[256,1024]{1,0:T(8,128)S(1)} %get-tuple-element.96.refs_1_, f32[256,128]{1,0:T(8,128)S(1)} %get-tuple-element.97.refs_2_, f32[4,256,1024]{2,1,0:T(8,128)} %copy-done, ...), custom_call_target="tpu_custom_call" | custom-call | flops 1024 | bytes 1024 | tf_op jit(solution)/shard_map/state_step/pallas_call | solution.py:447
  116.2 1.0 copy-done.20
  117.3 2.7 gather_live.1
  120.6 0.8 copy-done.23
  121.4 0.8 copy-done.25
  122.2 0.8 copy-done.27
  123.6 1.0 copy-done.17
  124.6 1.0 copy-done.24
  125.6 1.0 copy-done.26
  126.7 1.0 copy-done.28
  127.7 0.8 copy-done.34
  128.6 5.7 %live_steps.1.after_ref.live_ref = bf16[4,32,1024]{2,1,0:T(8,128)(2,1)S(1)} custom-call(s32[2,32]{1,0:T(2,128)S(1)} %pad_add_fusion.slot_ref, f32[256,128]{1,0:T(8,128)S(1)} %copy-done.17, bf16[16,64,1024]{2,1,0:T(8,128)(2,1)} %all-to-all-done.moved_ref, f32[4,32,1024]{2,1,0:T(8,128)S(1)} %copy-done.24, f32[4,32,1024]{2,1,0:T(8,128)S(1)} %copy-done.26, ...), custom_call_target="tpu_custom_call" | custom-call | flops 1024 | bytes 1024 | tf_op jit(solution)/shard_map/live_steps/pallas_call | solution.py:47
  134.8 1.8 collective-permute-done.18.other_ref
  136.6 8.6 %out_project.5 = (bf16[128,4096]{1,0:T(8,128)(2,1)S(1)}, bf16[128,4096]{1,0:T(8,128)(2,1)S(1)}) custom-call(s32[1]{0:T(128)} %bitcast.me_ref, bf16[256,1024]{1,0:T(8,128)(2,1)S(1)} %fix.4.own_ref.refs_0_, bf16[256,1024]{1,0:T(8,128)(2,1)S(1)} %collective-permute-done.18.other_ref, bf16[1024,8192]{1,0:T(8,128)(2,1)} %wown_ref.9, ...), custom_call_target="tpu_custom_call" | custom-call | flops 1024 | bytes 1024 | tf_op jit(solution)/shard_map/out_project/pallas_call | solution.py:587
  145.3 11.6 %state_step.5 = (bf16[16,256,1024]{2,1,0:T(8,128)(2,1)}, bf16[256,1024]{1,0:T(8,128)(2,1)S(1)}) custom-call(s32[1]{0:T(128)} %bitcast.me_ref, bf16[128,4096]{1,0:T(8,128)(2,1)S(1)} %get-tuple-element.105.refs_0_, f32[256,1024]{1,0:T(8,128)S(1)} %copy-done.21, f32[256,128]{1,0:T(8,128)S(1)} %copy-done.18, f32[4,256,1024]{2,1,0:T(8,128)} %copy-done, ...), custom_call_target="tpu_custom_call" | custom-call | flops 1024 | bytes 1024 | tf_op jit(solution)/shard_map/state_step/pallas_call | solution.py:447
  158.0 1.8 collective-permute-done.20.other_ref
  159.8 8.6 %out_project.6 = (bf16[128,4096]{1,0:T(8,128)(2,1)S(1)}, bf16[128,4096]{1,0:T(8,128)(2,1)S(1)}) custom-call(s32[1]{0:T(128)} %bitcast.me_ref, bf16[256,1024]{1,0:T(8,128)(2,1)S(1)} %fix.5.own_ref.refs_0_, bf16[256,1024]{1,0:T(8,128)(2,1)S(1)} %collective-permute-done.20.other_ref, bf16[1024,8192]{1,0:T(8,128)(2,1)} %wown_ref.9, ...), custom_call_target="tpu_custom_call" | custom-call | flops 1024 | bytes 1024 | tf_op jit(solution)/shard_map/out_project/pallas_call | solution.py:587
  168.3 2.1 collective-permute-start.24
  170.6 11.5 %state_step.6 = (bf16[16,256,1024]{2,1,0:T(8,128)(2,1)}, bf16[256,1024]{1,0:T(8,128)(2,1)S(1)}) custom-call(s32[1]{0:T(128)} %bitcast.me_ref, bf16[2,32,4096]{2,1,0:T(8,128)(2,1)S(1)} %get-tuple-element.112.refs_0_.keep_ref, f32[256,1024]{1,0:T(8,128)S(1)} %get-tuple-element.113.refs_1_, f32[256,128]{1,0:T(8,128)S(1)} %get-tuple-element.109.after_ref.refs_2_, ...), custom_call_target="tpu_custom_call" | custom-call | flops 1024 | bytes 1024 | tf_op jit(solution)/shard_map/state_step/pallas_call | solution.py:447
  183.3 1.8 collective-permute-done.22.other_ref
  185.1 8.6 %out_project.7 = (bf16[128,4096]{1,0:T(8,128)(2,1)S(1)}, bf16[128,4096]{1,0:T(8,128)(2,1)S(1)}) custom-call(s32[1]{0:T(128)} %bitcast.me_ref, bf16[256,1024]{1,0:T(8,128)(2,1)S(1)} %fix.6.own_ref.refs_0_, bf16[256,1024]{1,0:T(8,128)(2,1)S(1)} %collective-permute-done.22.other_ref, bf16[1024,8192]{1,0:T(8,128)(2,1)} %wown_ref.9, ...), custom_call_target="tpu_custom_call" | custom-call | flops 1024 | bytes 1024 | tf_op jit(solution)/shard_map/out_project/pallas_call | solution.py:587
  194.0 3.5 %collective-permute-done.23.got_ref = bf16[2,32,4096]{2,1,0:T(8,128)(2,1)S(1)} collective-permute-done((bf16[2,32,4096]{2,1,0:T(8,128)(2,1)S(1)}, bf16[2,32,4096]{2,1,0:T(8,128)(2,1)S(1)}, u32[]{:S(2)}, u32[]{:S(2)}) %collective-permute-start.23) | collective-permute-done | bytes 524320 | tf_op jit(solution)/shard_map/ppermute | solution.py:28
  197.9 9.1 %state_step.7.after_ref.gated_ref = bf16[256,1024]{1,0:T(8,128)(2,1)S(1)} custom-call(s32[1]{0:T(128)} %bitcast.me_ref, bf16[2,32,4096]{2,1,0:T(8,128)(2,1)S(1)} %get-tuple-element.121.refs_0_.keep_ref, f32[256,1024]{1,0:T(8,128)S(1)} %get-tuple-element.122.refs_1_, f32[256,128]{1,0:T(8,128)S(1)} %get-tuple-element.116.after_ref.refs_2_, ...), custom_call_target="tpu_custom_call" | custom-call | flops 1024 | bytes 1024 | tf_op jit(solution)/shard_map/state_step/pallas_call | solution.py:447
  207.7 3.8 %collective-permute-start.27 = (bf16[1,32,4096]{2,1,0:T(8,128)(2,1)S(1)}, bf16[1,32,4096]{2,1,0:T(8,128)(2,1)S(1)}, u32[]{:S(2)}, u32[]{:S(2)}) collective-permute-start(bf16[1,32,4096]{2,1,0:T(8,128)(2,1)S(1)} %get-tuple-element.128), channel_id=1, source_target_pairs={{0,8},{1,9},{2,10},{3,11},{4,12},{5,13},{6,14},{7,15},{8,0},{9,1},... | collective-permute-start | bytes 786440 | tf_op jit(solution)/shard_map/ppermute | solution.py:28
  211.5 4.8 %out_project.8 = (bf16[128,2048]{1,0:T(8,128)(2,1)S(1)}, bf16[128,2048]{1,0:T(8,128)(2,1)S(1)}) custom-call(s32[1]{0:T(128)} %bitcast.me_ref, bf16[256,1024]{1,0:T(8,128)(2,1)S(1)} %fix.7.own_ref.refs_0_, bf16[256,1024]{1,0:T(8,128)(2,1)S(1)} %collective-permute-done.25.other_ref, bf16[1024,8192]{1,0:T(8,128)(2,1)} %wown_ref.9, ...), custom_call_target="tpu_custom_call" | custom-call | flops 1024 | bytes 1024 | tf_op jit(solution)/shard_map/out_project/pallas_call | solution.py:587
  216.3 4.9 %out_project.9 = (bf16[128,2048]{1,0:T(8,128)(2,1)S(1)}, bf16[128,2048]{1,0:T(8,128)(2,1)S(1)}) custom-call(s32[1]{0:T(128)} %bitcast.me_ref, bf16[256,1024]{1,0:T(8,128)(2,1)S(1)} %fix.7.own_ref.refs_0_, bf16[256,1024]{1,0:T(8,128)(2,1)S(1)} %collective-permute-done.25.other_ref, bf16[1024,8192]{1,0:T(8,128)(2,1)} %wown_ref.9, ...), custom_call_target="tpu_custom_call" | custom-call | flops 1024 | bytes 1024 | tf_op jit(solution)/shard_map/out_project/pallas_call | solution.py:587
  221.2 6.1 %collective-permute-done.26.got_ref = bf16[2,32,4096]{2,1,0:T(8,128)(2,1)S(1)} collective-permute-done((bf16[2,32,4096]{2,1,0:T(8,128)(2,1)S(1)}, bf16[2,32,4096]{2,1,0:T(8,128)(2,1)S(1)}, u32[]{:S(2)}, u32[]{:S(2)}) %collective-permute-start.26) | collective-permute-done | bytes 524320 | tf_op jit(solution)/shard_map/ppermute | solution.py:28
  227.8 2.2 collective-permute-start.30
  230.3 1.9 collective-permute-start.31
  232.2 1.7 collective-permute-start.37
  234.0 13.4 %collective-permute-done.30.got_ref = bf16[2,32,4096]{2,1,0:T(8,128)(2,1)S(1)} collective-permute-done((bf16[2,32,4096]{2,1,0:T(8,128)(2,1)S(1)}, bf16[2,32,4096]{2,1,0:T(8,128)(2,1)S(1)}, u32[]{:S(2)}, u32[]{:S(2)}) %collective-permute-start.30) | collective-permute-done | bytes 524320 | tf_op jit(solution)/shard_map/ppermute | solution.py:28
  247.8 1.8 collective-permute-start.34
  249.6 1.9 collective-permute-start.35
  251.5 8.6 %collective-permute-done.34.got_ref = bf16[2,32,2048]{2,1,0:T(8,128)(2,1)S(1)} collective-permute-done((bf16[2,32,2048]{2,1,0:T(8,128)(2,1)S(1)}, bf16[2,32,2048]{2,1,0:T(8,128)(2,1)S(1)}, u32[]{:S(2)}, u32[]{:S(2)}) %collective-permute-start.34) | collective-permute-done | bytes 262176 | tf_op jit(solution)/shard_map/ppermute | solution.py:28
  260.1 3.2 %collective-permute-done.35.got_ref = bf16[1,32,4096]{2,1,0:T(8,128)(2,1)S(1)} collective-permute-done((bf16[1,32,4096]{2,1,0:T(8,128)(2,1)S(1)}, bf16[1,32,4096]{2,1,0:T(8,128)(2,1)S(1)}, u32[]{:S(2)}, u32[]{:S(2)}) %collective-permute-start.35) | collective-permute-done | bytes 262176 | tf_op jit(solution)/shard_map/ppermute | solution.py:28
  263.6 2.4 collective-permute-start.39
  266.0 6.1 %collective-permute-done.38.got_ref = bf16[2,32,2048]{2,1,0:T(8,128)(2,1)S(1)} collective-permute-done((bf16[2,32,2048]{2,1,0:T(8,128)(2,1)S(1)}, bf16[2,32,2048]{2,1,0:T(8,128)(2,1)S(1)}, u32[]{:S(2)}, u32[]{:S(2)}) %collective-permute-start.38) | collective-permute-done | bytes 262176 | tf_op jit(solution)/shard_map/ppermute | solution.py:28
  273.4 5.0 %collective-permute-done.41.got_ref = bf16[1,32,2048]{2,1,0:T(8,128)(2,1)S(1)} collective-permute-done((bf16[1,32,2048]{2,1,0:T(8,128)(2,1)S(1)}, bf16[1,32,2048]{2,1,0:T(8,128)(2,1)S(1)}, u32[]{:S(2)}, u32[]{:S(2)}) %collective-permute-start.41) | collective-permute-done | bytes 131104 | tf_op jit(solution)/shard_map/ppermute | solution.py:28
  278.6 1.2 collective-permute-done.42.refs_9_
  279.8 2.3 final_join.1
  (167 shorter events, 18.5 us)
Async XLA Ops:
  1.2 5.8 %collective-permute-start = (bf16[4,16,768]{2,1,0:T(8,128)(2,1)S(1)}, bf16[4,16,768]{2,1,0:T(8,128)(2,1)S(1)}, u32[]{:S(2)}, u32[]{:S(2)}) collective-permute-start(bf16[4,16,768]{2,1,0:T(8,128)(2,1)S(1)} %get-tuple-element.81), channel_id=1, source_target_pairs={{0,2},{1,3},{2,0},{3,1},{4,6},{5,7},{6,4},{7,5},{8,10},{9,11},{10,... | collective-permute-start | bytes 294920 | tf_op jit(solution)/shard_map/ppermute | solution.py:28
  4.2 2.8 collective-permute-start.1
  4.2 2.1 collective-permute-start.2
  6.4 4.8 %collective-permute-start.3 = (bf16[4,16,768]{2,1,0:T(8,128)(2,1)S(1)}, bf16[4,16,768]{2,1,0:T(8,128)(2,1)S(1)}, u32[]{:S(2)}, u32[]{:S(2)}) collective-permute-start(bf16[4,16,768]{2,1,0:T(8,128)(2,1)S(1)} %collective-permute-done.2), channel_id=1, source_target_pairs={{0,2},{1,3},{2,0},{3,1},{4,6},{5,7},{6,4},{7,5},{8,10},{9,11},{10,... | collective-permute-start | bytes 294920 | tf_op jit(solution)/shard_map/ppermute | solution.py:28
  11.2 5.7 %collective-permute-start.4 = (bf16[4,16,768]{2,1,0:T(8,128)(2,1)S(1)}, bf16[4,16,768]{2,1,0:T(8,128)(2,1)S(1)}, u32[]{:S(2)}, u32[]{:S(2)}) collective-permute-start(bf16[4,16,768]{2,1,0:T(8,128)(2,1)S(1)} %get-tuple-element.84), channel_id=1, source_target_pairs={{0,4},{1,5},{2,6},{3,7},{4,0},{5,1},{6,2},{7,3},{8,12},{9,13},{10,... | collective-permute-start | bytes 294920 | tf_op jit(solution)/shard_map/ppermute | solution.py:28
  12.8 14.0 %collective-permute-start.5 = (bf16[4,16,768]{2,1,0:T(8,128)(2,1)S(1)}, bf16[4,16,768]{2,1,0:T(8,128)(2,1)S(1)}, u32[]{:S(2)}, u32[]{:S(2)}) collective-permute-start(bf16[4,16,768]{2,1,0:T(8,128)(2,1)S(1)} %get-tuple-element.86), channel_id=1, source_target_pairs={{0,8},{1,9},{2,10},{3,11},{4,12},{5,13},{6,14},{7,15},{8,0},{9,1},... | collective-permute-start | bytes 294920 | tf_op jit(solution)/shard_map/ppermute | solution.py:28
  15.4 11.4 %collective-permute-start.6 = (bf16[4,16,768]{2,1,0:T(8,128)(2,1)S(1)}, bf16[4,16,768]{2,1,0:T(8,128)(2,1)S(1)}, u32[]{:S(2)}, u32[]{:S(2)}) collective-permute-start(bf16[4,16,768]{2,1,0:T(8,128)(2,1)S(1)} %get-tuple-element.87), channel_id=1, source_target_pairs={{0,12},{1,13},{2,14},{3,15},{4,8},{5,9},{6,10},{7,11},{8,4},{9,5},... | collective-permute-start | bytes 294920 | tf_op jit(solution)/shard_map/ppermute | solution.py:28
  15.6 9.0 %copy-start.10 = (f32[4,16,16384]{2,1,0:T(8,128)S(1)}, f32[4,16,16384]{2,1,0:T(8,128)}, u32[]{:S(2)}) copy-start(f32[4,16,16384]{2,1,0:T(8,128)} %x_ref.2) | copy-start | bytes 12582916
  24.6 3.6 %copy-start.19 = (bf16[1024,544]{0,1:T(8,128)(2,1)S(1)}, bf16[1024,544]{0,1:T(8,128)(2,1)}, u32[]{:S(2)}) copy-start(bf16[1024,544]{0,1:T(8,128)(2,1)} %param.27) | copy-start | bytes 3342340
  24.6 3.6 %copy-start.30 = (bf16[4,16,768]{2,1,0:T(8,128)(2,1)S(1)}, bf16[4,16,768]{2,1,0:T(8,128)(2,1)}, u32[]{:S(2)}) copy-start(bf16[4,16,768]{2,1,0:T(8,128)(2,1)} %copy-done.29) | copy-start | bytes 294916
  32.1 2.2 collective-permute-start.7
  34.4 14.8 %copy-start.37 = (f32[544]{0:T(1024)S(1)}, f32[544]{0:T(1024)}, u32[]{:S(2)}) copy-start(f32[544]{0:T(1024)} %param.28) | copy-start | bytes 6532
  34.5 102.1 %collective-permute-start.19 = (bf16[1024,4096]{1,0:T(8,128)(2,1)}, bf16[1024,4096]{1,0:T(8,128)(2,1)}, u32[]{:S(2)}, u32[]{:S(2)}) collective-permute-start(bf16[1024,4096]{1,0:T(8,128)(2,1)} %hold.3), channel_id=1, source_target_pairs={{0,1},{1,0},{2,3},{3,2},{4,5},{5,4},{6,7},{7,6},{8,9},{9,8},{10,11... | collective-permute-start | bytes 25165832 | tf_op jit(solution)/shard_map/ppermute | solution.py:28
  34.7 10.0 %collective-permute-start.8 = (bf16[4,4,16,640]{3,2,1,0:T(8,128)(2,1)S(1)}, bf16[4,4,16,640]{3,2,1,0:T(8,128)(2,1)S(1)}, u32[]{:S(2)}, u32[]{:S(2)}) collective-permute-start(bf16[4,4,16,640]{3,2,1,0:T(8,128)(2,1)S(1)} %get-tuple-element.91), channel_id=1, source_target_pairs={{0,2},{1,3},{2,0},{3,1},{4,6},{5,7},{6,4},{7,5},{8,10},{9,11},{10,... | collective-permute-start | bytes 983048 | tf_op jit(solution)/shard_map/ppermute | solution.py:28
  44.8 5.0 %collective-permute-start.9 = (bf16[4,16,640]{2,1,0:T(8,128)(2,1)S(1)}, bf16[4,16,640]{2,1,0:T(8,128)(2,1)S(1)}, u32[]{:S(2)}, u32[]{:S(2)}) collective-permute-start(bf16[4,16,640]{2,1,0:T(8,128)(2,1)S(1)} %get-tuple-element.93), channel_id=1, source_target_pairs={{0,4},{1,5},{2,6},{3,7},{4,0},{5,1},{6,2},{7,3},{8,12},{9,13},{10,... | collective-permute-start | bytes 245768 | tf_op jit(solution)/shard_map/ppermute | solution.py:28
  46.1 8.9 %collective-permute-start.10 = (bf16[4,16,640]{2,1,0:T(8,128)(2,1)S(1)}, bf16[4,16,640]{2,1,0:T(8,128)(2,1)S(1)}, u32[]{:S(2)}, u32[]{:S(2)}) collective-permute-start(bf16[4,16,640]{2,1,0:T(8,128)(2,1)S(1)} %get-tuple-element.94), channel_id=1, source_target_pairs={{0,8},{1,9},{2,10},{3,11},{4,12},{5,13},{6,14},{7,15},{8,0},{9,1},... | collective-permute-start | bytes 245768 | tf_op jit(solution)/shard_map/ppermute | solution.py:28
  48.4 6.5 %collective-permute-start.11 = (bf16[4,16,640]{2,1,0:T(8,128)(2,1)S(1)}, bf16[4,16,640]{2,1,0:T(8,128)(2,1)S(1)}, u32[]{:S(2)}, u32[]{:S(2)}) collective-permute-start(bf16[4,16,640]{2,1,0:T(8,128)(2,1)S(1)} %get-tuple-element.95), channel_id=1, source_target_pairs={{0,12},{1,13},{2,14},{3,15},{4,8},{5,9},{6,10},{7,11},{8,4},{9,5},... | collective-permute-start | bytes 245768 | tf_op jit(solution)/shard_map/ppermute | solution.py:28
  55.1 6.6 %collective-permute-start.14 = (bf16[4,16,640]{2,1,0:T(8,128)(2,1)S(1)}, bf16[4,16,640]{2,1,0:T(8,128)(2,1)S(1)}, u32[]{:S(2)}, u32[]{:S(2)}) collective-permute-start(bf16[4,16,640]{2,1,0:T(8,128)(2,1)S(1)} %norm.1.refs_0_), channel_id=1, source_target_pairs={{0,12},{1,13},{2,14},{3,15},{4,8},{5,9},{6,10},{7,11},{8,4},{9,5},... | collective-permute-start | bytes 245768 | tf_op jit(solution)/shard_map/ppermute | solution.py:28
  57.4 6.9 %collective-permute-start.13 = (bf16[4,16,640]{2,1,0:T(8,128)(2,1)S(1)}, bf16[4,16,640]{2,1,0:T(8,128)(2,1)S(1)}, u32[]{:S(2)}, u32[]{:S(2)}) collective-permute-start(bf16[4,16,640]{2,1,0:T(8,128)(2,1)S(1)} %norm.1.refs_0_), channel_id=1, source_target_pairs={{0,8},{1,9},{2,10},{3,11},{4,12},{5,13},{6,14},{7,15},{8,0},{9,1},... | collective-permute-start | bytes 245768 | tf_op jit(solution)/shard_map/ppermute | solution.py:28
  58.1 6.2 %collective-permute-start.12 = (bf16[4,16,640]{2,1,0:T(8,128)(2,1)S(1)}, bf16[4,16,640]{2,1,0:T(8,128)(2,1)S(1)}, u32[]{:S(2)}, u32[]{:S(2)}) collective-permute-start(bf16[4,16,640]{2,1,0:T(8,128)(2,1)S(1)} %norm.1.refs_0_), channel_id=1, source_target_pairs={{0,4},{1,5},{2,6},{3,7},{4,0},{5,1},{6,2},{7,3},{8,12},{9,13},{10,... | collective-permute-start | bytes 245768 | tf_op jit(solution)/shard_map/ppermute | solution.py:28
  64.3 5.0 %copy-start.38 = (s32[16]{0:T(128)S(1)}, s32[16]{0:T(128)}, u32[]{:S(2)}) copy-start(s32[16]{0:T(128)} %param.21) | copy-start | bytes 196
  64.3 33.1 %copy-start.3 = (bf16[512,1024]{1,0:T(8,128)(2,1)S(1)}, bf16[512,1024]{1,0:T(8,128)(2,1)}, u32[]{:S(2)}) copy-start(bf16[512,1024]{1,0:T(8,128)(2,1)} %refs_4_.14) | copy-start | bytes 3145732
  64.3 33.1 %copy-start.31 = (f32[1024]{0:T(1024)S(1)}, f32[1024]{0:T(1024)}, u32[]{:S(2)}) copy-start(f32[1024]{0:T(1024)} %param.30) | copy-start | bytes 12292
  64.3 33.7 %copy-start.2 = (bf16[4,256,1024]{2,1,0:T(8,128)(2,1)S(1)}, bf16[4,256,1024]{2,1,0:T(8,128)(2,1)}, u32[]{:S(2)}) copy-start(bf16[4,256,1024]{2,1,0:T(8,128)(2,1)} %refs_4_.15) | copy-start | bytes 6291460
  64.3 33.7 %copy-start.15 = (f32[16,1024]{1,0:T(8,128)S(1)}, f32[16,1024]{1,0:T(8,128)}, u32[]{:S(2)}) copy-start(f32[16,1024]{1,0:T(8,128)} %refs_5_.9) | copy-start | bytes 196612
  64.3 33.7 %copy-start.32 = (f32[1024]{0:T(1024)S(1)}, f32[1024]{0:T(1024)}, u32[]{:S(2)}) copy-start(f32[1024]{0:T(1024)} %param.32) | copy-start | bytes 12292
  64.4 59.3 %all-to-all-start = ((bf16[16,64,1024]{2,1,0:T(8,128)(2,1)}), bf16[16,64,1024]{2,1,0:T(8,128)(2,1)}, u32[]{:S(2)}, u32[]{:S(2)}) async-start(bf16[16,64,1024]{2,1,0:T(8,128)(2,1)} %hold.2.after_ref.refs_0_), calls=%async_computation | async-start | bytes 4194304 | tf_op jit(solution)/shard_map/all_to_all | solution.py:722
  69.4 26.3 %collective-permute-start.15 = (bf16[4,4,16,640]{3,2,1,0:T(8,128)(2,1)S(1)}, bf16[4,4,16,640]{3,2,1,0:T(8,128)(2,1)S(1)}, u32[]{:S(2)}, u32[]{:S(2)}) collective-permute-start(bf16[4,4,16,640]{3,2,1,0:T(8,128)(2,1)S(1)} %merge_z.1.after_ref.refs_0_), channel_id=1, source_target_pairs={{0,2},{1,3},{2,0},{3,1},{4,6},{5,7},{6,4},{7,5},{8,10},{9,11},{10,... | collective-permute-start | bytes 983048 | tf_op jit(solution)/shard_map/ppermute | solution.py:28
  72.0 23.8 %collective-permute-start.16 = (bf16[4,4,16,640]{3,2,1,0:T(8,128)(2,1)S(1)}, bf16[4,4,16,640]{3,2,1,0:T(8,128)(2,1)S(1)}, u32[]{:S(2)}, u32[]{:S(2)}) collective-permute-start(bf16[4,4,16,640]{3,2,1,0:T(8,128)(2,1)S(1)} %merge_z.1.after_ref.refs_0_), channel_id=1, source_target_pairs={{0,1},{1,0},{2,3},{3,2},{4,5},{5,4},{6,7},{7,6},{8,9},{9,8},{10,11... | collective-permute-start | bytes 983048 | tf_op jit(solution)/shard_map/ppermute | solution.py:28
  95.8 21.5 %copy-start.4 = (bf16[4,4,16,640]{3,2,1,0:T(8,128)(2,1)}, bf16[4,4,16,640]{3,2,1,0:T(8,128)(2,1)S(1)}, u32[]{:S(2)}) copy-start(bf16[4,4,16,640]{3,2,1,0:T(8,128)(2,1)S(1)} %collective-permute-done.15.refs_1_) | copy-start | bytes 983044
  95.8 1.6 collective-permute-start.17
  95.8 21.4 %copy-start.6 = (bf16[4,4,16,640]{3,2,1,0:T(8,128)(2,1)}, bf16[4,4,16,640]{3,2,1,0:T(8,128)(2,1)S(1)}, u32[]{:S(2)}) copy-start(bf16[4,4,16,640]{3,2,1,0:T(8,128)(2,1)S(1)} %collective-permute-done.16.refs_2_) | copy-start | bytes 983044
  97.4 19.8 %copy-start.8 = (bf16[4,4,16,640]{3,2,1,0:T(8,128)(2,1)}, bf16[4,4,16,640]{3,2,1,0:T(8,128)(2,1)S(1)}, u32[]{:S(2)}) copy-start(bf16[4,4,16,640]{3,2,1,0:T(8,128)(2,1)S(1)} %collective-permute-done.17.refs_3_) | copy-start | bytes 983044
  98.1 19.2 %copy-start.1 = (f32[4,256,1024]{2,1,0:T(8,128)S(1)}, f32[4,256,1024]{2,1,0:T(8,128)}, u32[]{:S(2)}) copy-start(f32[4,256,1024]{2,1,0:T(8,128)} %copy-done) | copy-start | bytes 12582916
  123.6 10.6 %copy-start.13 = (bf16[256,1024]{1,0:T(8,128)(2,1)S(1)}, bf16[256,1024]{1,0:T(8,128)(2,1)}, u32[]{:S(2)}) copy-start(bf16[256,1024]{1,0:T(8,128)(2,1)} %copy-done.12) | copy-start | bytes 1572868
  134.6 10.6 %copy-start.18 = (f32[256,128]{1,0:T(8,128)S(1)}, f32[256,128]{1,0:T(8,128)}, u32[]{:S(2)}) copy-start(f32[256,128]{1,0:T(8,128)} %copy-done.16) | copy-start | bytes 393220
  134.6 10.6 %copy-start.21 = (f32[256,1024]{1,0:T(8,128)S(1)}, f32[256,1024]{1,0:T(8,128)}, u32[]{:S(2)}) copy-start(f32[256,1024]{1,0:T(8,128)} %copy-done.20) | copy-start | bytes 3145732
  134.6 2.0 collective-permute-start.18
  145.1 25.3 %collective-permute-start.21 = (bf16[128,4096]{1,0:T(8,128)(2,1)S(1)}, bf16[128,4096]{1,0:T(8,128)(2,1)S(1)}, u32[]{:S(2)}, u32[]{:S(2)}) collective-permute-start(bf16[128,4096]{1,0:T(8,128)(2,1)S(1)} %get-tuple-element.111), channel_id=1, source_target_pairs={{0,2},{1,3},{2,0},{3,1},{4,6},{5,7},{6,4},{7,5},{8,10},{9,11},{10,... | collective-permute-start | bytes 3145736 | tf_op jit(solution)/shard_map/ppermute | solution.py:28
  145.2 11.6 %copy-start.5 = (bf16[4,4,16,640]{3,2,1,0:T(8,128)(2,1)S(1)}, bf16[4,4,16,640]{3,2,1,0:T(8,128)(2,1)}, u32[]{:S(2)}) copy-start(bf16[4,4,16,640]{3,2,1,0:T(8,128)(2,1)} %copy-done.4) | copy-start | bytes 983044
  145.2 11.6 %copy-start.7 = (bf16[4,4,16,640]{3,2,1,0:T(8,128)(2,1)S(1)}, bf16[4,4,16,640]{3,2,1,0:T(8,128)(2,1)}, u32[]{:S(2)}) copy-start(bf16[4,4,16,640]{3,2,1,0:T(8,128)(2,1)} %copy-done.6) | copy-start | bytes 983044
  145.3 11.6 %copy-start.9 = (bf16[4,4,16,640]{3,2,1,0:T(8,128)(2,1)S(1)}, bf16[4,4,16,640]{3,2,1,0:T(8,128)(2,1)}, u32[]{:S(2)}) copy-start(bf16[4,4,16,640]{3,2,1,0:T(8,128)(2,1)} %copy-done.8) | copy-start | bytes 983044
  157.8 2.0 collective-permute-start.20
  168.3 29.3 %collective-permute-start.24 = (bf16[128,4096]{1,0:T(8,128)(2,1)S(1)}, bf16[128,4096]{1,0:T(8,128)(2,1)S(1)}, u32[]{:S(2)}, u32[]{:S(2)}) collective-permute-start(bf16[128,4096]{1,0:T(8,128)(2,1)S(1)} %get-tuple-element.120), channel_id=1, source_target_pairs={{0,2},{1,3},{2,0},{3,1},{4,6},{5,7},{6,4},{7,5},{8,10},{9,11},{10,... | collective-permute-start | bytes 3145736 | tf_op jit(solution)/shard_map/ppermute | solution.py:28
  183.1 2.0 collective-permute-start.22
  183.2 14.3 %collective-permute-start.23 = (bf16[2,32,4096]{2,1,0:T(8,128)(2,1)S(1)}, bf16[2,32,4096]{2,1,0:T(8,128)(2,1)S(1)}, u32[]{:S(2)}, u32[]{:S(2)}) collective-permute-start(bf16[2,32,4096]{2,1,0:T(8,128)(2,1)S(1)} %get-tuple-element.118), channel_id=1, source_target_pairs={{0,4},{1,5},{2,6},{3,7},{4,0},{5,1},{6,2},{7,3},{8,12},{9,13},{10,... | collective-permute-start | bytes 1572872 | tf_op jit(solution)/shard_map/ppermute | solution.py:28
  193.6 33.9 %collective-permute-start.29 = (bf16[128,4096]{1,0:T(8,128)(2,1)S(1)}, bf16[128,4096]{1,0:T(8,128)(2,1)S(1)}, u32[]{:S(2)}, u32[]{:S(2)}) collective-permute-start(bf16[128,4096]{1,0:T(8,128)(2,1)S(1)} %get-tuple-element.131), channel_id=1, source_target_pairs={{0,2},{1,3},{2,0},{3,1},{4,6},{5,7},{6,4},{7,5},{8,10},{9,11},{10,... | collective-permute-start | bytes 3145736 | tf_op jit(solution)/shard_map/ppermute | solution.py:28
  207.3 4.2 %collective-permute-start.25 = (bf16[256,1024]{1,0:T(8,128)(2,1)S(1)}, bf16[256,1024]{1,0:T(8,128)(2,1)S(1)}, u32[]{:S(2)}, u32[]{:S(2)}) collective-permute-start(bf16[256,1024]{1,0:T(8,128)(2,1)S(1)} %fix.7.own_ref.refs_0_), channel_id=1, source_target_pairs={{0,1},{1,0},{2,3},{3,2},{4,5},{5,4},{6,7},{7,6},{8,9},{9,8},{10,11... | collective-permute-start | bytes 1572872 | tf_op jit(solution)/shard_map/ppermute | solution.py:28
  207.4 20.0 %collective-permute-start.26 = (bf16[2,32,4096]{2,1,0:T(8,128)(2,1)S(1)}, bf16[2,32,4096]{2,1,0:T(8,128)(2,1)S(1)}, u32[]{:S(2)}, u32[]{:S(2)}) collective-permute-start(bf16[2,32,4096]{2,1,0:T(8,128)(2,1)S(1)} %get-tuple-element.126), channel_id=1, source_target_pairs={{0,4},{1,5},{2,6},{3,7},{4,0},{5,1},{6,2},{7,3},{8,12},{9,13},{10,... | collective-permute-start | bytes 1572872 | tf_op jit(solution)/shard_map/ppermute | solution.py:28
  207.7 19.8 %collective-permute-start.27 = (bf16[1,32,4096]{2,1,0:T(8,128)(2,1)S(1)}, bf16[1,32,4096]{2,1,0:T(8,128)(2,1)S(1)}, u32[]{:S(2)}, u32[]{:S(2)}) collective-permute-start(bf16[1,32,4096]{2,1,0:T(8,128)(2,1)S(1)} %get-tuple-element.128), channel_id=1, source_target_pairs={{0,8},{1,9},{2,10},{3,11},{4,12},{5,13},{6,14},{7,15},{8,0},{9,1},... | collective-permute-start | bytes 786440 | tf_op jit(solution)/shard_map/ppermute | solution.py:28
  227.8 19.6 %collective-permute-start.30 = (bf16[2,32,4096]{2,1,0:T(8,128)(2,1)S(1)}, bf16[2,32,4096]{2,1,0:T(8,128)(2,1)S(1)}, u32[]{:S(2)}, u32[]{:S(2)}) collective-permute-start(bf16[2,32,4096]{2,1,0:T(8,128)(2,1)S(1)} %get-tuple-element.133), channel_id=1, source_target_pairs={{0,4},{1,5},{2,6},{3,7},{4,0},{5,1},{6,2},{7,3},{8,12},{9,13},{10,... | collective-permute-start | bytes 1572872 | tf_op jit(solution)/shard_map/ppermute | solution.py:28
  230.0 17.6 %collective-permute-start.33 = (bf16[128,2048]{1,0:T(8,128)(2,1)S(1)}, bf16[128,2048]{1,0:T(8,128)(2,1)S(1)}, u32[]{:S(2)}, u32[]{:S(2)}) collective-permute-start(bf16[128,2048]{1,0:T(8,128)(2,1)S(1)} %get-tuple-element.138), channel_id=1, source_target_pairs={{0,2},{1,3},{2,0},{3,1},{4,6},{5,7},{6,4},{7,5},{8,10},{9,11},{10,... | collective-permute-start | bytes 1572872 | tf_op jit(solution)/shard_map/ppermute | solution.py:28
  230.3 17.2 %collective-permute-start.31 = (bf16[1,32,4096]{2,1,0:T(8,128)(2,1)S(1)}, bf16[1,32,4096]{2,1,0:T(8,128)(2,1)S(1)}, u32[]{:S(2)}, u32[]{:S(2)}) collective-permute-start(bf16[1,32,4096]{2,1,0:T(8,128)(2,1)S(1)} %get-tuple-element.135), channel_id=1, source_target_pairs={{0,8},{1,9},{2,10},{3,11},{4,12},{5,13},{6,14},{7,15},{8,0},{9,1},... | collective-permute-start | bytes 786440 | tf_op jit(solution)/shard_map/ppermute | solution.py:28
  232.2 31.1 %collective-permute-start.37 = (bf16[128,2048]{1,0:T(8,128)(2,1)S(1)}, bf16[128,2048]{1,0:T(8,128)(2,1)S(1)}, u32[]{:S(2)}, u32[]{:S(2)}) collective-permute-start(bf16[128,2048]{1,0:T(8,128)(2,1)S(1)} %get-tuple-element.145), channel_id=1, source_target_pairs={{0,2},{1,3},{2,0},{3,1},{4,6},{5,7},{6,4},{7,5},{8,10},{9,11},{10,... | collective-permute-start | bytes 1572872 | tf_op jit(solution)/shard_map/ppermute | solution.py:28
  247.8 12.3 %collective-permute-start.34 = (bf16[2,32,2048]{2,1,0:T(8,128)(2,1)S(1)}, bf16[2,32,2048]{2,1,0:T(8,128)(2,1)S(1)}, u32[]{:S(2)}, u32[]{:S(2)}) collective-permute-start(bf16[2,32,2048]{2,1,0:T(8,128)(2,1)S(1)} %get-tuple-element.140), channel_id=1, source_target_pairs={{0,4},{1,5},{2,6},{3,7},{4,0},{5,1},{6,2},{7,3},{8,12},{9,13},{10,... | collective-permute-start | bytes 786440 | tf_op jit(solution)/shard_map/ppermute | solution.py:28
  249.6 13.7 %collective-permute-start.35 = (bf16[1,32,4096]{2,1,0:T(8,128)(2,1)S(1)}, bf16[1,32,4096]{2,1,0:T(8,128)(2,1)S(1)}, u32[]{:S(2)}, u32[]{:S(2)}) collective-permute-start(bf16[1,32,4096]{2,1,0:T(8,128)(2,1)S(1)} %get-tuple-element.142), channel_id=1, source_target_pairs={{0,8},{1,9},{2,10},{3,11},{4,12},{5,13},{6,14},{7,15},{8,0},{9,1},... | collective-permute-start | bytes 786440 | tf_op jit(solution)/shard_map/ppermute | solution.py:28
  263.5 8.6 %collective-permute-start.38 = (bf16[2,32,2048]{2,1,0:T(8,128)(2,1)S(1)}, bf16[2,32,2048]{2,1,0:T(8,128)(2,1)S(1)}, u32[]{:S(2)}, u32[]{:S(2)}) collective-permute-start(bf16[2,32,2048]{2,1,0:T(8,128)(2,1)S(1)} %get-tuple-element.147), channel_id=1, source_target_pairs={{0,4},{1,5},{2,6},{3,7},{4,0},{5,1},{6,2},{7,3},{8,12},{9,13},{10,... | collective-permute-start | bytes 786440 | tf_op jit(solution)/shard_map/ppermute | solution.py:28
  263.6 9.3 %collective-permute-start.39 = (bf16[1,32,2048]{2,1,0:T(8,128)(2,1)S(1)}, bf16[1,32,2048]{2,1,0:T(8,128)(2,1)S(1)}, u32[]{:S(2)}, u32[]{:S(2)}) collective-permute-start(bf16[1,32,2048]{2,1,0:T(8,128)(2,1)S(1)} %get-tuple-element.149), channel_id=1, source_target_pairs={{0,8},{1,9},{2,10},{3,11},{4,12},{5,13},{6,14},{7,15},{8,0},{9,1},... | collective-permute-start | bytes 393224 | tf_op jit(solution)/shard_map/ppermute | solution.py:28
  272.1 6.3 %collective-permute-start.41 = (bf16[1,32,2048]{2,1,0:T(8,128)(2,1)S(1)}, bf16[1,32,2048]{2,1,0:T(8,128)(2,1)S(1)}, u32[]{:S(2)}, u32[]{:S(2)}) collective-permute-start(bf16[1,32,2048]{2,1,0:T(8,128)(2,1)S(1)} %get-tuple-element.152), channel_id=1, source_target_pairs={{0,8},{1,9},{2,10},{3,11},{4,12},{5,13},{6,14},{7,15},{8,0},{9,1},... | collective-permute-start | bytes 393224 | tf_op jit(solution)/shard_map/ppermute | solution.py:28
  272.2 6.4 %collective-permute-start.28 = (bf16[16,4096]{1,0:T(8,128)(2,1)S(1)}, bf16[16,4096]{1,0:T(8,128)(2,1)S(1)}, u32[]{:S(2)}, u32[]{:S(2)}) collective-permute-start(bf16[16,4096]{1,0:T(8,128)(2,1)S(1)} %get-tuple-element.130), channel_id=1, source_target_pairs={{0,1},{1,0},{2,3},{3,2},{4,5},{5,4},{6,7},{7,6},{8,9},{9,8},{10,11... | collective-permute-start | bytes 393224 | tf_op jit(solution)/shard_map/ppermute | solution.py:28
  272.3 6.3 %collective-permute-start.32 = (bf16[16,4096]{1,0:T(8,128)(2,1)S(1)}, bf16[16,4096]{1,0:T(8,128)(2,1)S(1)}, u32[]{:S(2)}, u32[]{:S(2)}) collective-permute-start(bf16[16,4096]{1,0:T(8,128)(2,1)S(1)} %get-tuple-element.137), channel_id=1, source_target_pairs={{0,1},{1,0},{2,3},{3,2},{4,5},{5,4},{6,7},{7,6},{8,9},{9,8},{10,11... | collective-permute-start | bytes 393224 | tf_op jit(solution)/shard_map/ppermute | solution.py:28
  272.8 5.8 %collective-permute-start.36 = (bf16[16,4096]{1,0:T(8,128)(2,1)S(1)}, bf16[16,4096]{1,0:T(8,128)(2,1)S(1)}, u32[]{:S(2)}, u32[]{:S(2)}) collective-permute-start(bf16[16,4096]{1,0:T(8,128)(2,1)S(1)} %get-tuple-element.144), channel_id=1, source_target_pairs={{0,1},{1,0},{2,3},{3,2},{4,5},{5,4},{6,7},{7,6},{8,9},{9,8},{10,11... | collective-permute-start | bytes 393224 | tf_op jit(solution)/shard_map/ppermute | solution.py:28
  272.9 5.7 %collective-permute-start.40 = (bf16[16,2048]{1,0:T(8,128)(2,1)S(1)}, bf16[16,2048]{1,0:T(8,128)(2,1)S(1)}, u32[]{:S(2)}, u32[]{:S(2)}) collective-permute-start(bf16[16,2048]{1,0:T(8,128)(2,1)S(1)} %get-tuple-element.151), channel_id=1, source_target_pairs={{0,1},{1,0},{2,3},{3,2},{4,5},{5,4},{6,7},{7,6},{8,9},{9,8},{10,11... | collective-permute-start | bytes 196616 | tf_op jit(solution)/shard_map/ppermute | solution.py:28
  278.5 1.3 collective-permute-start.42
  (19 other events, 27.4 us)

commit v11 on v10

--- a/solution.py
+++ b/solution.py
@@ -463,42 +463,42 @@
 
 def gather_kernel(me_ref, after_ref, row_ref, *refs):
     lows, refs = refs[:4], refs[4:]
-    conv_ref, z_ref, dtp_ref, dtb_ref, step_ref, live_conv_ref, gate_ref, tail_ref, low_scr = refs
-    count = step_ref.shape[1]
-    rows = conv_ref.shape[1]
+    conv_ref, z_ref, dtp_ref, dtb_ref, o_ref, low_scr = refs
+    count = o_ref.shape[1]
+    _, rows, c = conv_ref.shape
     hot = (row_ref[:, :1] == lax.broadcasted_iota(jnp.int32, (count, rows), 1)).astype(F32).astype(BF16)
     for t in range(STEPS):
         low = jnp.dot(hot, assemble_low(lows, t, low_scr, me_ref), preferred_element_type=F32)
-        step_ref[t] = step_sizes(low.astype(BF16), dtp_ref, dtb_ref)
-        tail_ref[t, :, :128] = low[:, DT_RANK:]
+        o_ref[t, :, :c] = step_sizes(low.astype(BF16), dtp_ref, dtb_ref)
+        o_ref[t, :, 3 * c :] = low[:, DT_RANK:]
         conv = conv_ref[t]
         high = conv.astype(BF16)
         rest = (conv - high.astype(F32)).astype(BF16)
-        live_conv_ref[t] = jnp.dot(hot, high, preferred_element_type=F32) + jnp.dot(
+        o_ref[t, :, c : 2 * c] = jnp.dot(hot, high, preferred_element_type=F32) + jnp.dot(
             hot, rest, preferred_element_type=F32
         )
         z = jnp.dot(hot, z_ref[t], preferred_element_type=F32)
-        gate_ref[t] = z * sigmoid(z)
+        o_ref[t, :, 2 * c : 3 * c] = z * sigmoid(z)
 
 
 def gather_live(me, after, row_of_live, lows, conv, step_z, dt_proj, dt_bias, n):
     _, rows, c = conv.shape
     count = row_of_live.shape[0]
-    wide = (STEPS, count, c)
-    return small(
+    (out,) = small(
         gather_kernel,
         me,
         [row_of_live, *lows, conv, step_z, dt_proj, dt_bias],
-        [wide, wide, wide, (STEPS, count, 128)],
+        [(STEPS, count, 3 * c + 128)],
         "gather_live",
         after,
         F32,
         [pltpu.VMEM((n // 4, 2, 2, rows // n, WIDE), BF16)],
         40,
     )
-
-
-def live_kernel(slot_ref, after_ref, moved_ref, step_ref, conv_ref, gate_ref, tail_ref, alog_ref, skip_ref, o_ref, buf, state_scr):
+    return out
+
+
+def live_kernel(slot_ref, after_ref, moved_ref, live_ref, alog_ref, skip_ref, o_ref, buf, state_scr):
     _, count, c = o_ref.shape
     def place(i, carry):
         source, slot = slot_ref[0, i], slot_ref[1, i]
@@ -517,11 +517,12 @@
 
     def step_all(t, carry):
         for r in range(0, count, tall):
-            tail = tail_ref[t, r : r + tall, :]
+            tail = live_ref[t, r : r + tall, 3 * c :]
             for l in range(0, c, lanes):
                 cols = slice(l, l + lanes)
-                step = step_ref[t, r : r + tall, cols]
-                conv = conv_ref[t, r : r + tall, cols]
+                step = live_ref[t, r : r + tall, cols]
+                conv = live_ref[t, r : r + tall, c + l : c + l + lanes]
+                gate = live_ref[t, r : r + tall, 2 * c + l : 2 * c + l + lanes]
                 drive = step * conv
                 total = skip_ref[:, cols] * conv
                 for s in range(STATE):
@@ -530,18 +531,18 @@
                     state = jnp.exp(step * rate) * old + drive * tail[:, s : s + 1]
                     state_scr[s, r : r + tall, cols] = state
                     total = total + state * tail[:, STATE + s : STATE + s + 1]
-                o_ref[t, r : r + tall, cols] = (total * gate_ref[t, r : r + tall, cols]).astype(BF16)
+                o_ref[t, r : r + tall, cols] = (total * gate).astype(BF16)
         return carry
 
     lax.fori_loop(0, STEPS, step_all, 0)
 
 
 def live_steps(slot_of_live, after, moved, gathered, a_log, d_skip):
-    _, count, c = gathered[0].shape
+    count, c = gathered.shape[1], a_log.shape[1]
     (out,) = small(
         live_kernel,
         slot_of_live,
-        [moved, *gathered, a_log, d_skip],
+        [moved, gathered, a_log, d_skip],
         [(STEPS, count, c)],
         "live_steps",
         after,
@@ -732,21 +733,22 @@
     next_steps = None
 
     def s_step(t, after):
-        nonlocal state, next_steps
+        nonlocal state
         if t == 0:
             steps = step_rows(0, me, after, lows, dt_proj, rate_bias, rows, n)
         else:
             steps = next_steps
         state, gated[t] = state_step(t, me, after, steps, conv, step_z, a_log, skip, state, n)
-        if t == STEPS - 1:
-            return gated[t]
-        next_steps = step_rows(t + 1, me, (gated[t],), lows, dt_proj, rate_bias, rows, n)
-        return next_steps[1]
+        return gated[t]
 
     def fix(t, after):
         kernel = functools.partial(fix_kernel, t, take)
         (gated[t],) = small(kernel, me, [live_row, gated[t], live_gated], [(rows, c)], "fix", (after,))
-        return gated[t]
+        if t == STEPS - 1:
+            return gated[t]
+        nonlocal next_steps
+        next_steps = step_rows(t + 1, me, (gated[t],), lows, dt_proj, rate_bias, rows, n)
+        return next_steps[1]
 
     def project(t, after, parts=1):
         other = swap(gated[t], 1, n)
@@ -779,30 +781,25 @@
     live_gated = live_steps(slot_of_live, (last,), moved_state, gathered, a_log, skip)
     last = fix(0, live_gated)
     last = project(0, last)
-    for t in range(1, STEPS - 1):
+    for t in range(1, STEPS):
         last = s_step(t, (last,))
         last = fix(t, last)
-        last = project(t, last)
         if t > 1:
             for stage in range(1, stages):
                 last = reduce(t - 2, stage, last)
-        last = reduce(t - 1, 0, last)
-    t = STEPS - 1
-    last = s_step(t, (last,))
-    last = fix(t, last)
-    last = project(t, last, 2)
-    for stage in range(1, stages):
-        last = reduce(t - 2, stage, last)
+        last = project(t, last, 1 if t < STEPS - 1 else 2)
+        if t < STEPS - 1:
+            last = reduce(t - 1, 0, last)
     last = reduce(t - 3, stages, last)
     last = reduce(t - 1, 0, last)
+    last = reduce(t, 0, last, 0)
     for stage in range(1, stages):
         last = reduce(t - 1, stage, last)
     last = reduce(t - 2, stages, last)
-    last = reduce(t, 0, last, 0)
     for stage in range(1, stages):
         last = reduce(t, stage, last, 0)
+    last = reduce(t, 0, last, 1)
     last = reduce(t - 1, stages, last)
-    last = reduce(t, 0, last, 1)
     for stage in range(1, stages):
         last = reduce(t, stage, last, 1)
     last = reduce(t, stages, last, 0)

time: 283 us -> 267 us (0.943)
  waiting for transfers between devices: 106 us -> 92 us
  local copies, waits for them, and re-layouts: 14.9 us -> 8.93 us
  starting transfers between devices: 45 us -> 48.6 us
    ppermute x43, waiting for transfers between devices: 106 us -> 92 us  [swap(): return lax.ppermute(x, 'dex', [(i, i ^ mask) for i in range(n)])]
    unnamed x78 -> x56, local copies, waits for them, and re-layouts: 13.6 us -> 7.68 us
    ppermute x43, starting transfers between devices: 40.1 us -> 43.7 us  [swap(): return lax.ppermute(x, 'dex', [(i, i ^ mask) for i in range(n)])]
  transfers between devices with their start and end apart: 44 -> 44, of which waited for: 22 -> 25; matrix products, arithmetic and copies ran while one was open for 1% -> 1% of each run, Pallas kernels for 35% -> 37%
where the time goes in v11:
time: 267 us; the launch traced here: 266 us
  Pallas kernels  114 us (43%)
  waiting for transfers between devices  92 us (34%)
  starting transfers between devices  48.6 us (18%)
  local copies, waits for them, and re-layouts  8.93 us (3%)
    ppermute x43, waiting for transfers between devices, swap(): return lax.ppermute(x, 'dex', [(i, i ^ mask) for i in range(n)])  92 us
    pallas_call x4, Pallas kernels, state_step(): pl.pallas_call(functools.partial(state_kernel, t, len(after)), grid_spec=...  48.9 us
    ppermute x43, starting transfers between devices, swap(): return lax.ppermute(x, 'dex', [(i, i ^ mask) for i in range(n)])  43.7 us
    pallas_call x5, Pallas kernels, out_project(): pl.pallas_call(out_kernel, grid_spec=pltpu.PrefetchScalarGridSpec(num_sca...  35.4 us
    pallas_call x31, Pallas kernels, small(): pl.pallas_call(kernel, in_specs=[pl.BlockSpec(memory_space=pltpu.SMEM)] +...  14.4 us
    unnamed x56, local copies, waits for them, and re-layouts  7.68 us
    pallas_call x1, Pallas kernels, weight_half(): pl.pallas_call(half_kernel, grid_spec=pltpu.PrefetchScalarGridSpec(num_sc...  7.13 us
  transfers between devices with their start and end apart: 44, of which 25 were waited for; matrix products, arithmetic and copies ran while one was open for 1% of the time, Pallas kernels for 37%

profile of v11, /device:TPU:0, one launch (start us, length us, event | category | flops | bytes accessed | tf_op | source)
XLA Modules:
  0.0 265.9 jit_solution(6410599568867973713)
XLA Ops:
  0.0 1.1 copy-done.19
  1.2 3.0 %collective-permute-start = (bf16[4,16,768]{2,1,0:T(8,128)(2,1)S(1)}, bf16[4,16,768]{2,1,0:T(8,128)(2,1)S(1)}, u32[]{:S(2)}, u32[]{:S(2)}) collective-permute-start(bf16[4,16,768]{2,1,0:T(8,128)(2,1)S(1)} %get-tuple-element.77), channel_id=1, source_target_pairs={{0,2},{1,3},{2,0},{3,1},{4,6},{5,7},{6,4},{7,5},{8,10},{9,11},{10,... | collective-permute-start | bytes 294920 | tf_op jit(solution)/shard_map/ppermute | solution.py:28
  4.8 0.7 reshape.188
  5.5 0.7 broadcast_select_fusion
  7.0 4.1 %collective-permute-done.3.refs_3_ = bf16[4,16,768]{2,1,0:T(8,128)(2,1)S(1)} collective-permute-done((bf16[4,16,768]{2,1,0:T(8,128)(2,1)S(1)}, bf16[4,16,768]{2,1,0:T(8,128)(2,1)S(1)}, u32[]{:S(2)}, u32[]{:S(2)}) %collective-permute-start.3) | collective-permute-done | bytes 98336 | tf_op jit(solution)/shard_map/ppermute | solution.py:28
  11.2 1.6 collective-permute-start.4
  12.8 2.6 collective-permute-start.5
  15.6 1.2 collective-permute-done.4.after_ref.refs_1_
  17.5 7.1 %weight_half.1.refs_0_.x_ref = bf16[1024,4096]{1,0:T(8,128)(2,1)} custom-call(s32[1]{0:T(128)} %bitcast.me_ref, bf16[4,16,768]{2,1,0:T(8,128)(2,1)} %copy-done.20, bf16[1024,8192]{1,0:T(8,128)(2,1)} %wown_ref.9), custom_call_target="tpu_custom_call" | custom-call | flops 1024 | bytes 1024 | tf_op jit(solution)/shard_map/weight_half/pallas_call | solution.py:147
  24.7 2.1 pack_state.1.refs_4_.x_ref
  27.2 0.7 copy-done.16
  28.2 3.9 %conv_project.1 = (f32[4,256,1024]{2,1,0:T(8,128)S(1)}, bf16[8,4,16,640]{3,2,1,0:T(8,128)(2,1)S(1)}, bf16[8,4,16,640]{3,2,1,0:T(8,128)(2,1)S(1)}) custom-call(s32[1]{0:T(128)} %bitcast.me_ref, s32[4,256]{1,0:T(4,128)S(1)} %broadcast_select_fusion.1.target_ref, f32[3,256,1024]{2,1,0:T(8,128)S(1)} %bitcast.38, bf16[4,256,1024]{2,1,0:T(8,128)(2,1)S(1)} %copy-done.16, ...), custom_call_target="tpu_custom_call" | custom-call | flops 1024 | bytes 1024 | tf_op jit(solution)/shard_map/conv_project/pallas_call | solution.py:212
  32.2 2.1 collective-permute-done.7.refs_1_
  35.0 9.7 %collective-permute-done.8.refs_1_ = bf16[4,4,16,640]{3,2,1,0:T(8,128)(2,1)S(1)} collective-permute-done((bf16[4,4,16,640]{3,2,1,0:T(8,128)(2,1)S(1)}, bf16[4,4,16,640]{3,2,1,0:T(8,128)(2,1)S(1)}, u32[]{:S(2)}, u32[]{:S(2)}) %collective-permute-start.8) | collective-permute-done | bytes 327712 | tf_op jit(solution)/shard_map/ppermute | solution.py:28
  44.8 1.3 collective-permute-start.9
  46.1 2.4 collective-permute-start.10
  48.4 0.8 collective-permute-start.11
  49.7 5.2 %collective-permute-done.10.refs_2_ = bf16[4,16,640]{2,1,0:T(8,128)(2,1)S(1)} collective-permute-done((bf16[4,16,640]{2,1,0:T(8,128)(2,1)S(1)}, bf16[4,16,640]{2,1,0:T(8,128)(2,1)S(1)}, u32[]{:S(2)}, u32[]{:S(2)}) %collective-permute-start.10) | collective-permute-done | bytes 81952 | tf_op jit(solution)/shard_map/ppermute | solution.py:28
  55.1 2.2 collective-permute-start.14
  58.1 1.5 collective-permute-start.12
  59.6 2.2 collective-permute-done.14.refs_3_
  61.7 2.5 collective-permute-done.13.refs_2_
  64.4 4.9 %all-to-all-start = ((bf16[16,64,1024]{2,1,0:T(8,128)(2,1)}), bf16[16,64,1024]{2,1,0:T(8,128)(2,1)}, u32[]{:S(2)}, u32[]{:S(2)}) async-start(bf16[16,64,1024]{2,1,0:T(8,128)(2,1)} %hold.2.after_ref.refs_0_), calls=%async_computation | async-start | bytes 4194304 | tf_op jit(solution)/shard_map/all_to_all | solution.py:723
  69.4 1.6 collective-permute-start.15
  72.1 23.7 %collective-permute-done.15.refs_1_ = bf16[4,4,16,640]{3,2,1,0:T(8,128)(2,1)S(1)} collective-permute-done((bf16[4,4,16,640]{3,2,1,0:T(8,128)(2,1)S(1)}, bf16[4,4,16,640]{3,2,1,0:T(8,128)(2,1)S(1)}, u32[]{:S(2)}, u32[]{:S(2)}) %collective-permute-start.15) | collective-permute-done | bytes 327712 | tf_op jit(solution)/shard_map/ppermute | solution.py:28
  95.8 1.6 collective-permute-done.17.refs_3_
  98.1 16.7 %state_step.4 = (bf16[16,256,1024]{2,1,0:T(8,128)(2,1)}, bf16[256,1024]{1,0:T(8,128)(2,1)S(1)}) custom-call(s32[1]{0:T(128)} %bitcast.me_ref, bf16[16,64,1024]{2,1,0:T(8,128)(2,1)} %hold.2.after_ref.refs_0_, f32[256,1024]{1,0:T(8,128)S(1)} %get-tuple-element.92.refs_1_, f32[256,128]{1,0:T(8,128)S(1)} %get-tuple-element.93.refs_2_, f32[4,256,1024]{2,1,0:T(8,128)} %copy-done, ...), custom_call_target="tpu_custom_call" | custom-call | flops 1024 | bytes 1024 | tf_op jit(solution)/shard_map/state_step/pallas_call | solution.py:447
  114.9 2.7 %gather_live.1.live_ref = f32[4,32,3200]{2,1,0:T(8,128)S(1)} custom-call(s32[1]{0:T(128)} %bitcast.me_ref, bf16[256,1024]{1,0:T(8,128)(2,1)S(1)} %get-tuple-element.95.after_ref.gated_ref, s32[32,128]{1,0:T(8,128)S(1)} %broadcast_in_dim.80.row_ref, bf16[4,4,16,640]{3,2,1,0:T(8,128)(2,1)S(1)} %merge_z.1.after_ref.refs_0_, ...), custom_call_target="tpu_custom_call" | custom-call | flops 1024 | bytes 1024 | tf_op jit(solution)/shard_map/gather_live/pallas_call | solution.py:47
  117.6 1.1 copy-done.10
  118.7 0.8 copy-done.12
  119.5 1.4 copy-done.11
  120.9 1.0 copy-done.13
  122.0 5.8 %live_steps.1.after_ref.live_ref = bf16[4,32,1024]{2,1,0:T(8,128)(2,1)S(1)} custom-call(s32[2,32]{1,0:T(2,128)S(1)} %pad_add_fusion.slot_ref, bf16[256,1024]{1,0:T(8,128)(2,1)S(1)} %copy-done.13, bf16[16,64,1024]{2,1,0:T(8,128)(2,1)} %all-to-all-done.moved_ref, f32[4,32,3200]{2,1,0:T(8,128)S(1)} %copy-done.11, f32[16,1024]{1,0:T(8,128)S(1)} %copy-done.17, ...), custom_call_target="tpu_custom_call" | custom-call | flops 1024 | bytes 1024 | tf_op jit(solution)/shard_map/live_steps/pallas_call | solution.py:47
  128.9 1.2 collective-permute-done.18.other_ref
  130.0 8.6 %out_project.5 = (bf16[128,4096]{1,0:T(8,128)(2,1)S(1)}, bf16[128,4096]{1,0:T(8,128)(2,1)S(1)}) custom-call(s32[1]{0:T(128)} %bitcast.me_ref, bf16[256,1024]{1,0:T(8,128)(2,1)S(1)} %fix.4.after_ref.own_ref, bf16[256,1024]{1,0:T(8,128)(2,1)S(1)} %collective-permute-done.18.other_ref, bf16[1024,8192]{1,0:T(8,128)(2,1)} %wown_ref.9, ...), custom_call_target="tpu_custom_call" | custom-call | flops 1024 | bytes 1024 | tf_op jit(solution)/shard_map/out_project/pallas_call | solution.py:588
  138.7 11.5 %state_step.5 = (bf16[16,256,1024]{2,1,0:T(8,128)(2,1)}, bf16[256,1024]{1,0:T(8,128)(2,1)S(1)}) custom-call(s32[1]{0:T(128)} %bitcast.me_ref, bf16[128,4096]{1,0:T(8,128)(2,1)S(1)} %get-tuple-element.97.refs_0_, f32[256,1024]{1,0:T(8,128)S(1)} %get-tuple-element.98.refs_1_, f32[256,128]{1,0:T(8,128)S(1)} %get-tuple-element.96.refs_0_.refs_2_, ...), custom_call_target="tpu_custom_call" | custom-call | flops 1024 | bytes 1024 | tf_op jit(solution)/shard_map/state_step/pallas_call | solution.py:447
  151.3 1.2 collective-permute-done.20.other_ref
  152.5 8.6 %out_project.6 = (bf16[128,4096]{1,0:T(8,128)(2,1)S(1)}, bf16[128,4096]{1,0:T(8,128)(2,1)S(1)}) custom-call(s32[1]{0:T(128)} %bitcast.me_ref, bf16[256,1024]{1,0:T(8,128)(2,1)S(1)} %fix.5.after_ref.own_ref, bf16[256,1024]{1,0:T(8,128)(2,1)S(1)} %collective-permute-done.20.other_ref, bf16[1024,8192]{1,0:T(8,128)(2,1)} %wown_ref.9, ...), custom_call_target="tpu_custom_call" | custom-call | flops 1024 | bytes 1024 | tf_op jit(solution)/shard_map/out_project/pallas_call | solution.py:588
  161.1 2.1 collective-permute-start.24
  163.1 0.8 collective-permute-done.21
  164.2 11.5 %state_step.6 = (bf16[16,256,1024]{2,1,0:T(8,128)(2,1)}, bf16[256,1024]{1,0:T(8,128)(2,1)S(1)}) custom-call(s32[1]{0:T(128)} %bitcast.me_ref, bf16[2,32,4096]{2,1,0:T(8,128)(2,1)S(1)} %get-tuple-element.104.refs_0_.keep_ref, f32[256,1024]{1,0:T(8,128)S(1)} %get-tuple-element.105.refs_1_, f32[256,128]{1,0:T(8,128)S(1)} %get-tuple-element.101.refs_0_.refs_2_, ...), custom_call_target="tpu_custom_call" | custom-call | flops 1024 | bytes 1024 | tf_op jit(solution)/shard_map/state_step/pallas_call | solution.py:447
  178.0 8.6 %out_project.7 = (bf16[128,4096]{1,0:T(8,128)(2,1)S(1)}, bf16[128,4096]{1,0:T(8,128)(2,1)S(1)}) custom-call(s32[1]{0:T(128)} %bitcast.me_ref, bf16[256,1024]{1,0:T(8,128)(2,1)S(1)} %fix.6.after_ref.own_ref, bf16[256,1024]{1,0:T(8,128)(2,1)S(1)} %collective-permute-done.22.other_ref, bf16[1024,8192]{1,0:T(8,128)(2,1)} %wown_ref.9, ...), custom_call_target="tpu_custom_call" | custom-call | flops 1024 | bytes 1024 | tf_op jit(solution)/shard_map/out_project/pallas_call | solution.py:588
  187.2 2.0 collective-permute-start.26
  189.2 9.1 %state_step.7.after_ref.gated_ref = bf16[256,1024]{1,0:T(8,128)(2,1)S(1)} custom-call(s32[1]{0:T(128)} %bitcast.me_ref, bf16[2,32,4096]{2,1,0:T(8,128)(2,1)S(1)} %get-tuple-element.113.refs_0_.keep_ref, f32[256,1024]{1,0:T(8,128)S(1)} %get-tuple-element.114.refs_1_, f32[256,128]{1,0:T(8,128)S(1)} %get-tuple-element.108.after_ref.refs_2_, ...), custom_call_target="tpu_custom_call" | custom-call | flops 1024 | bytes 1024 | tf_op jit(solution)/shard_map/state_step/pallas_call | solution.py:447
  198.6 2.1 collective-permute-start.27
  201.3 4.9 %out_project.8 = (bf16[128,2048]{1,0:T(8,128)(2,1)S(1)}, bf16[128,2048]{1,0:T(8,128)(2,1)S(1)}) custom-call(s32[1]{0:T(128)} %bitcast.me_ref, bf16[256,1024]{1,0:T(8,128)(2,1)S(1)} %fix.7.after_ref.own_ref, bf16[256,1024]{1,0:T(8,128)(2,1)S(1)} %collective-permute-done.25.other_ref, bf16[1024,8192]{1,0:T(8,128)(2,1)} %wown_ref.9, ...), custom_call_target="tpu_custom_call" | custom-call | flops 1024 | bytes 1024 | tf_op jit(solution)/shard_map/out_project/pallas_call | solution.py:588
  206.2 1.8 collective-permute-start.30
  207.9 4.8 %out_project.9 = (bf16[128,2048]{1,0:T(8,128)(2,1)S(1)}, bf16[128,2048]{1,0:T(8,128)(2,1)S(1)}) custom-call(s32[1]{0:T(128)} %bitcast.me_ref, bf16[256,1024]{1,0:T(8,128)(2,1)S(1)} %fix.7.after_ref.own_ref, bf16[256,1024]{1,0:T(8,128)(2,1)S(1)} %collective-permute-done.25.other_ref, bf16[1024,8192]{1,0:T(8,128)(2,1)} %wown_ref.9, ...), custom_call_target="tpu_custom_call" | custom-call | flops 1024 | bytes 1024 | tf_op jit(solution)/shard_map/out_project/pallas_call | solution.py:588
  212.8 1.1 collective-permute-done.27.got_ref
  214.2 0.7 collective-permute-start.31
  215.0 1.2 collective-permute-start.35
  216.2 3.4 %collective-permute-start.32 = (bf16[1,32,4096]{2,1,0:T(8,128)(2,1)S(1)}, bf16[1,32,4096]{2,1,0:T(8,128)(2,1)S(1)}, u32[]{:S(2)}, u32[]{:S(2)}) collective-permute-start(bf16[1,32,4096]{2,1,0:T(8,128)(2,1)S(1)} %get-tuple-element.129), channel_id=1, source_target_pairs={{0,8},{1,9},{2,10},{3,11},{4,12},{5,13},{6,14},{7,15},{8,0},{9,1},... | collective-permute-start | bytes 786440 | tf_op jit(solution)/shard_map/ppermute | solution.py:28
  219.6 4.3 %collective-permute-done.30 = bf16[128,2048]{1,0:T(8,128)(2,1)S(1)} collective-permute-done((bf16[128,2048]{1,0:T(8,128)(2,1)S(1)}, bf16[128,2048]{1,0:T(8,128)(2,1)S(1)}, u32[]{:S(2)}, u32[]{:S(2)}) %collective-permute-start.30) | collective-permute-done | bytes 524320 | tf_op jit(solution)/shard_map/ppermute | solution.py:28
  224.0 2.1 collective-permute-start.34
  226.0 8.7 %collective-permute-done.31.got_ref = bf16[2,32,4096]{2,1,0:T(8,128)(2,1)S(1)} collective-permute-done((bf16[2,32,4096]{2,1,0:T(8,128)(2,1)S(1)}, bf16[2,32,4096]{2,1,0:T(8,128)(2,1)S(1)}, u32[]{:S(2)}, u32[]{:S(2)}) %collective-permute-start.31) | collective-permute-done | bytes 524320 | tf_op jit(solution)/shard_map/ppermute | solution.py:28
  234.9 1.0 collective-permute-start.36
  236.0 6.5 %collective-permute-done.34.got_ref = bf16[2,32,2048]{2,1,0:T(8,128)(2,1)S(1)} collective-permute-done((bf16[2,32,2048]{2,1,0:T(8,128)(2,1)S(1)}, bf16[2,32,2048]{2,1,0:T(8,128)(2,1)S(1)}, u32[]{:S(2)}, u32[]{:S(2)}) %collective-permute-start.34) | collective-permute-done | bytes 262176 | tf_op jit(solution)/shard_map/ppermute | solution.py:28
  242.8 2.5 collective-permute-start.39
  245.2 4.3 %collective-permute-done.36.got_ref = bf16[1,32,4096]{2,1,0:T(8,128)(2,1)S(1)} collective-permute-done((bf16[1,32,4096]{2,1,0:T(8,128)(2,1)S(1)}, bf16[1,32,4096]{2,1,0:T(8,128)(2,1)S(1)}, u32[]{:S(2)}, u32[]{:S(2)}) %collective-permute-start.36) | collective-permute-done | bytes 262176 | tf_op jit(solution)/shard_map/ppermute | solution.py:28
  249.6 3.6 %collective-permute-done.38.got_ref = bf16[2,32,2048]{2,1,0:T(8,128)(2,1)S(1)} collective-permute-done((bf16[2,32,2048]{2,1,0:T(8,128)(2,1)S(1)}, bf16[2,32,2048]{2,1,0:T(8,128)(2,1)S(1)}, u32[]{:S(2)}, u32[]{:S(2)}) %collective-permute-start.38) | collective-permute-done | bytes 262176 | tf_op jit(solution)/shard_map/ppermute | solution.py:28
  253.3 3.3 %collective-permute-start.41 = (bf16[1,32,2048]{2,1,0:T(8,128)(2,1)S(1)}, bf16[1,32,2048]{2,1,0:T(8,128)(2,1)S(1)}, u32[]{:S(2)}, u32[]{:S(2)}) collective-permute-start(bf16[1,32,2048]{2,1,0:T(8,128)(2,1)S(1)} %get-tuple-element.144), channel_id=1, source_target_pairs={{0,8},{1,9},{2,10},{3,11},{4,12},{5,13},{6,14},{7,15},{8,0},{9,1},... | collective-permute-start | bytes 393224 | tf_op jit(solution)/shard_map/ppermute | solution.py:28
  257.7 4.6 %collective-permute-done.41.got_ref = bf16[1,32,2048]{2,1,0:T(8,128)(2,1)S(1)} collective-permute-done((bf16[1,32,2048]{2,1,0:T(8,128)(2,1)S(1)}, bf16[1,32,2048]{2,1,0:T(8,128)(2,1)S(1)}, u32[]{:S(2)}, u32[]{:S(2)}) %collective-permute-start.41) | collective-permute-done | bytes 131104 | tf_op jit(solution)/shard_map/ppermute | solution.py:28
  262.5 1.2 collective-permute-done.42.refs_9_
  263.7 2.3 final_join.1
  (145 shorter events, 15.9 us)
Async XLA Ops:
  1.2 5.8 %collective-permute-start = (bf16[4,16,768]{2,1,0:T(8,128)(2,1)S(1)}, bf16[4,16,768]{2,1,0:T(8,128)(2,1)S(1)}, u32[]{:S(2)}, u32[]{:S(2)}) collective-permute-start(bf16[4,16,768]{2,1,0:T(8,128)(2,1)S(1)} %get-tuple-element.77), channel_id=1, source_target_pairs={{0,2},{1,3},{2,0},{3,1},{4,6},{5,7},{6,4},{7,5},{8,10},{9,11},{10,... | collective-permute-start | bytes 294920 | tf_op jit(solution)/shard_map/ppermute | solution.py:28
  4.2 2.8 %collective-permute-start.1 = (bf16[4,16,768]{2,1,0:T(8,128)(2,1)S(1)}, bf16[4,16,768]{2,1,0:T(8,128)(2,1)S(1)}, u32[]{:S(2)}, u32[]{:S(2)}) collective-permute-start(bf16[4,16,768]{2,1,0:T(8,128)(2,1)S(1)} %get-tuple-element.78), channel_id=1, source_target_pairs={{0,1},{1,0},{2,3},{3,2},{4,5},{5,4},{6,7},{7,6},{8,9},{9,8},{10,11... | collective-permute-start | bytes 294920 | tf_op jit(solution)/shard_map/ppermute | solution.py:28
  4.2 2.1 collective-permute-start.2
  6.4 4.8 %collective-permute-start.3 = (bf16[4,16,768]{2,1,0:T(8,128)(2,1)S(1)}, bf16[4,16,768]{2,1,0:T(8,128)(2,1)S(1)}, u32[]{:S(2)}, u32[]{:S(2)}) collective-permute-start(bf16[4,16,768]{2,1,0:T(8,128)(2,1)S(1)} %collective-permute-done.2), channel_id=1, source_target_pairs={{0,2},{1,3},{2,0},{3,1},{4,6},{5,7},{6,4},{7,5},{8,10},{9,11},{10,... | collective-permute-start | bytes 294920 | tf_op jit(solution)/shard_map/ppermute | solution.py:28
  11.2 5.7 %collective-permute-start.4 = (bf16[4,16,768]{2,1,0:T(8,128)(2,1)S(1)}, bf16[4,16,768]{2,1,0:T(8,128)(2,1)S(1)}, u32[]{:S(2)}, u32[]{:S(2)}) collective-permute-start(bf16[4,16,768]{2,1,0:T(8,128)(2,1)S(1)} %get-tuple-element.80), channel_id=1, source_target_pairs={{0,4},{1,5},{2,6},{3,7},{4,0},{5,1},{6,2},{7,3},{8,12},{9,13},{10,... | collective-permute-start | bytes 294920 | tf_op jit(solution)/shard_map/ppermute | solution.py:28
  12.8 14.0 %collective-permute-start.5 = (bf16[4,16,768]{2,1,0:T(8,128)(2,1)S(1)}, bf16[4,16,768]{2,1,0:T(8,128)(2,1)S(1)}, u32[]{:S(2)}, u32[]{:S(2)}) collective-permute-start(bf16[4,16,768]{2,1,0:T(8,128)(2,1)S(1)} %get-tuple-element.82), channel_id=1, source_target_pairs={{0,8},{1,9},{2,10},{3,11},{4,12},{5,13},{6,14},{7,15},{8,0},{9,1},... | collective-permute-start | bytes 294920 | tf_op jit(solution)/shard_map/ppermute | solution.py:28
  15.4 11.4 %collective-permute-start.6 = (bf16[4,16,768]{2,1,0:T(8,128)(2,1)S(1)}, bf16[4,16,768]{2,1,0:T(8,128)(2,1)S(1)}, u32[]{:S(2)}, u32[]{:S(2)}) collective-permute-start(bf16[4,16,768]{2,1,0:T(8,128)(2,1)S(1)} %get-tuple-element.83), channel_id=1, source_target_pairs={{0,12},{1,13},{2,14},{3,15},{4,8},{5,9},{6,10},{7,11},{8,4},{9,5},... | collective-permute-start | bytes 294920 | tf_op jit(solution)/shard_map/ppermute | solution.py:28
  15.6 9.0 %copy-start.14 = (f32[4,16,16384]{2,1,0:T(8,128)S(1)}, f32[4,16,16384]{2,1,0:T(8,128)}, u32[]{:S(2)}) copy-start(f32[4,16,16384]{2,1,0:T(8,128)} %x_ref.2) | copy-start | bytes 12582916
  24.6 3.3 %copy-start.16 = (bf16[4,256,1024]{2,1,0:T(8,128)(2,1)S(1)}, bf16[4,256,1024]{2,1,0:T(8,128)(2,1)}, u32[]{:S(2)}) copy-start(bf16[4,256,1024]{2,1,0:T(8,128)(2,1)} %x_ref.3) | copy-start | bytes 6291460
  24.6 3.6 %copy-start.18 = (bf16[1024,544]{0,1:T(8,128)(2,1)S(1)}, bf16[1024,544]{0,1:T(8,128)(2,1)}, u32[]{:S(2)}) copy-start(bf16[1024,544]{0,1:T(8,128)(2,1)} %param.27) | copy-start | bytes 3342340
  24.6 3.6 %copy-start.21 = (bf16[4,16,768]{2,1,0:T(8,128)(2,1)S(1)}, bf16[4,16,768]{2,1,0:T(8,128)(2,1)}, u32[]{:S(2)}) copy-start(bf16[4,16,768]{2,1,0:T(8,128)(2,1)} %copy-done.20) | copy-start | bytes 294916
  24.6 3.5 %copy-start.24 = (f32[4,1024]{1,0:T(4,128)S(1)}, f32[4,1024]{1,0:T(4,128)}, u32[]{:S(2)}) copy-start(f32[4,1024]{1,0:T(4,128)} %w_ref.3) | copy-start | bytes 49156
  24.6 3.5 %copy-start.25 = (f32[1024]{0:T(1024)S(1)}, f32[1024]{0:T(1024)}, u32[]{:S(2)}) copy-start(f32[1024]{0:T(1024)} %param.26) | copy-start | bytes 12292
  32.1 2.2 collective-permute-start.7
  34.4 14.8 %copy-start.26 = (f32[544]{0:T(1024)S(1)}, f32[544]{0:T(1024)}, u32[]{:S(2)}) copy-start(f32[544]{0:T(1024)} %param.28) | copy-start | bytes 6532
  34.5 95.6 %collective-permute-start.19 = (bf16[1024,4096]{1,0:T(8,128)(2,1)}, bf16[1024,4096]{1,0:T(8,128)(2,1)}, u32[]{:S(2)}, u32[]{:S(2)}) collective-permute-start(bf16[1024,4096]{1,0:T(8,128)(2,1)} %hold.3), channel_id=1, source_target_pairs={{0,1},{1,0},{2,3},{3,2},{4,5},{5,4},{6,7},{7,6},{8,9},{9,8},{10,11... | collective-permute-start | bytes 25165832 | tf_op jit(solution)/shard_map/ppermute | solution.py:28
  34.7 10.0 %collective-permute-start.8 = (bf16[4,4,16,640]{3,2,1,0:T(8,128)(2,1)S(1)}, bf16[4,4,16,640]{3,2,1,0:T(8,128)(2,1)S(1)}, u32[]{:S(2)}, u32[]{:S(2)}) collective-permute-start(bf16[4,4,16,640]{3,2,1,0:T(8,128)(2,1)S(1)} %get-tuple-element.87), channel_id=1, source_target_pairs={{0,2},{1,3},{2,0},{3,1},{4,6},{5,7},{6,4},{7,5},{8,10},{9,11},{10,... | collective-permute-start | bytes 983048 | tf_op jit(solution)/shard_map/ppermute | solution.py:28
  44.8 5.0 %collective-permute-start.9 = (bf16[4,16,640]{2,1,0:T(8,128)(2,1)S(1)}, bf16[4,16,640]{2,1,0:T(8,128)(2,1)S(1)}, u32[]{:S(2)}, u32[]{:S(2)}) collective-permute-start(bf16[4,16,640]{2,1,0:T(8,128)(2,1)S(1)} %get-tuple-element.89), channel_id=1, source_target_pairs={{0,4},{1,5},{2,6},{3,7},{4,0},{5,1},{6,2},{7,3},{8,12},{9,13},{10,... | collective-permute-start | bytes 245768 | tf_op jit(solution)/shard_map/ppermute | solution.py:28
  46.1 8.9 %collective-permute-start.10 = (bf16[4,16,640]{2,1,0:T(8,128)(2,1)S(1)}, bf16[4,16,640]{2,1,0:T(8,128)(2,1)S(1)}, u32[]{:S(2)}, u32[]{:S(2)}) collective-permute-start(bf16[4,16,640]{2,1,0:T(8,128)(2,1)S(1)} %get-tuple-element.90), channel_id=1, source_target_pairs={{0,8},{1,9},{2,10},{3,11},{4,12},{5,13},{6,14},{7,15},{8,0},{9,1},... | collective-permute-start | bytes 245768 | tf_op jit(solution)/shard_map/ppermute | solution.py:28
  48.4 6.5 %collective-permute-start.11 = (bf16[4,16,640]{2,1,0:T(8,128)(2,1)S(1)}, bf16[4,16,640]{2,1,0:T(8,128)(2,1)S(1)}, u32[]{:S(2)}, u32[]{:S(2)}) collective-permute-start(bf16[4,16,640]{2,1,0:T(8,128)(2,1)S(1)} %get-tuple-element.91), channel_id=1, source_target_pairs={{0,12},{1,13},{2,14},{3,15},{4,8},{5,9},{6,10},{7,11},{8,4},{9,5},... | collective-permute-start | bytes 245768 | tf_op jit(solution)/shard_map/ppermute | solution.py:28
  55.1 6.6 %collective-permute-start.14 = (bf16[4,16,640]{2,1,0:T(8,128)(2,1)S(1)}, bf16[4,16,640]{2,1,0:T(8,128)(2,1)S(1)}, u32[]{:S(2)}, u32[]{:S(2)}) collective-permute-start(bf16[4,16,640]{2,1,0:T(8,128)(2,1)S(1)} %norm.1.refs_0_), channel_id=1, source_target_pairs={{0,12},{1,13},{2,14},{3,15},{4,8},{5,9},{6,10},{7,11},{8,4},{9,5},... | collective-permute-start | bytes 245768 | tf_op jit(solution)/shard_map/ppermute | solution.py:28
  57.4 6.9 %collective-permute-start.13 = (bf16[4,16,640]{2,1,0:T(8,128)(2,1)S(1)}, bf16[4,16,640]{2,1,0:T(8,128)(2,1)S(1)}, u32[]{:S(2)}, u32[]{:S(2)}) collective-permute-start(bf16[4,16,640]{2,1,0:T(8,128)(2,1)S(1)} %norm.1.refs_0_), channel_id=1, source_target_pairs={{0,8},{1,9},{2,10},{3,11},{4,12},{5,13},{6,14},{7,15},{8,0},{9,1},... | collective-permute-start | bytes 245768 | tf_op jit(solution)/shard_map/ppermute | solution.py:28
  58.1 6.2 %collective-permute-start.12 = (bf16[4,16,640]{2,1,0:T(8,128)(2,1)S(1)}, bf16[4,16,640]{2,1,0:T(8,128)(2,1)S(1)}, u32[]{:S(2)}, u32[]{:S(2)}) collective-permute-start(bf16[4,16,640]{2,1,0:T(8,128)(2,1)S(1)} %norm.1.refs_0_), channel_id=1, source_target_pairs={{0,4},{1,5},{2,6},{3,7},{4,0},{5,1},{6,2},{7,3},{8,12},{9,13},{10,... | collective-permute-start | bytes 245768 | tf_op jit(solution)/shard_map/ppermute | solution.py:28
  64.3 5.0 %copy-start.27 = (s32[16]{0:T(128)S(1)}, s32[16]{0:T(128)}, u32[]{:S(2)}) copy-start(s32[16]{0:T(128)} %param.21) | copy-start | bytes 196
  64.3 33.1 %copy-start.3 = (bf16[512,1024]{1,0:T(8,128)(2,1)S(1)}, bf16[512,1024]{1,0:T(8,128)(2,1)}, u32[]{:S(2)}) copy-start(bf16[512,1024]{1,0:T(8,128)(2,1)} %refs_4_.14) | copy-start | bytes 3145732
  64.3 33.1 %copy-start.22 = (f32[1024]{0:T(1024)S(1)}, f32[1024]{0:T(1024)}, u32[]{:S(2)}) copy-start(f32[1024]{0:T(1024)} %param.30) | copy-start | bytes 12292
  64.3 33.7 %copy-start.2 = (bf16[4,256,1024]{2,1,0:T(8,128)(2,1)S(1)}, bf16[4,256,1024]{2,1,0:T(8,128)(2,1)}, u32[]{:S(2)}) copy-start(bf16[4,256,1024]{2,1,0:T(8,128)(2,1)} %refs_4_.15) | copy-start | bytes 6291460
  64.3 33.7 %copy-start.17 = (f32[16,1024]{1,0:T(8,128)S(1)}, f32[16,1024]{1,0:T(8,128)}, u32[]{:S(2)}) copy-start(f32[16,1024]{1,0:T(8,128)} %refs_5_.9) | copy-start | bytes 196612
  64.3 33.7 %copy-start.23 = (f32[1024]{0:T(1024)S(1)}, f32[1024]{0:T(1024)}, u32[]{:S(2)}) copy-start(f32[1024]{0:T(1024)} %param.32) | copy-start | bytes 12292
  64.4 55.1 %all-to-all-start = ((bf16[16,64,1024]{2,1,0:T(8,128)(2,1)}), bf16[16,64,1024]{2,1,0:T(8,128)(2,1)}, u32[]{:S(2)}, u32[]{:S(2)}) async-start(bf16[16,64,1024]{2,1,0:T(8,128)(2,1)} %hold.2.after_ref.refs_0_), calls=%async_computation | async-start | bytes 4194304 | tf_op jit(solution)/shard_map/all_to_all | solution.py:723
  69.4 26.3 %collective-permute-start.15 = (bf16[4,4,16,640]{3,2,1,0:T(8,128)(2,1)S(1)}, bf16[4,4,16,640]{3,2,1,0:T(8,128)(2,1)S(1)}, u32[]{:S(2)}, u32[]{:S(2)}) collective-permute-start(bf16[4,4,16,640]{3,2,1,0:T(8,128)(2,1)S(1)} %merge_z.1.after_ref.refs_0_), channel_id=1, source_target_pairs={{0,2},{1,3},{2,0},{3,1},{4,6},{5,7},{6,4},{7,5},{8,10},{9,11},{10,... | collective-permute-start | bytes 983048 | tf_op jit(solution)/shard_map/ppermute | solution.py:28
  72.0 23.8 %collective-permute-start.16 = (bf16[4,4,16,640]{3,2,1,0:T(8,128)(2,1)S(1)}, bf16[4,4,16,640]{3,2,1,0:T(8,128)(2,1)S(1)}, u32[]{:S(2)}, u32[]{:S(2)}) collective-permute-start(bf16[4,4,16,640]{3,2,1,0:T(8,128)(2,1)S(1)} %merge_z.1.after_ref.refs_0_), channel_id=1, source_target_pairs={{0,1},{1,0},{2,3},{3,2},{4,5},{5,4},{6,7},{7,6},{8,9},{9,8},{10,11... | collective-permute-start | bytes 983048 | tf_op jit(solution)/shard_map/ppermute | solution.py:28
  95.8 19.1 %copy-start.4 = (bf16[4,4,16,640]{3,2,1,0:T(8,128)(2,1)}, bf16[4,4,16,640]{3,2,1,0:T(8,128)(2,1)S(1)}, u32[]{:S(2)}) copy-start(bf16[4,4,16,640]{3,2,1,0:T(8,128)(2,1)S(1)} %collective-permute-done.15.refs_1_) | copy-start | bytes 983044
  95.8 1.6 collective-permute-start.17
  95.8 19.1 %copy-start.6 = (bf16[4,4,16,640]{3,2,1,0:T(8,128)(2,1)}, bf16[4,4,16,640]{3,2,1,0:T(8,128)(2,1)S(1)}, u32[]{:S(2)}) copy-start(bf16[4,4,16,640]{3,2,1,0:T(8,128)(2,1)S(1)} %collective-permute-done.16.refs_2_) | copy-start | bytes 983044
  97.4 17.5 %copy-start.8 = (bf16[4,4,16,640]{3,2,1,0:T(8,128)(2,1)}, bf16[4,4,16,640]{3,2,1,0:T(8,128)(2,1)S(1)}, u32[]{:S(2)}) copy-start(bf16[4,4,16,640]{3,2,1,0:T(8,128)(2,1)S(1)} %collective-permute-done.17.refs_3_) | copy-start | bytes 983044
  98.1 16.8 %copy-start.1 = (f32[4,256,1024]{2,1,0:T(8,128)S(1)}, f32[4,256,1024]{2,1,0:T(8,128)}, u32[]{:S(2)}) copy-start(f32[4,256,1024]{2,1,0:T(8,128)} %copy-done) | copy-start | bytes 12582916
  122.0 6.3 %copy-start.5 = (bf16[4,4,16,640]{3,2,1,0:T(8,128)(2,1)S(1)}, bf16[4,4,16,640]{3,2,1,0:T(8,128)(2,1)}, u32[]{:S(2)}) copy-start(bf16[4,4,16,640]{3,2,1,0:T(8,128)(2,1)} %copy-done.4) | copy-start | bytes 983044
  122.0 6.3 %copy-start.7 = (bf16[4,4,16,640]{3,2,1,0:T(8,128)(2,1)S(1)}, bf16[4,4,16,640]{3,2,1,0:T(8,128)(2,1)}, u32[]{:S(2)}) copy-start(bf16[4,4,16,640]{3,2,1,0:T(8,128)(2,1)} %copy-done.6) | copy-start | bytes 983044
  122.0 6.3 %copy-start.9 = (bf16[4,4,16,640]{3,2,1,0:T(8,128)(2,1)S(1)}, bf16[4,4,16,640]{3,2,1,0:T(8,128)(2,1)}, u32[]{:S(2)}) copy-start(bf16[4,4,16,640]{3,2,1,0:T(8,128)(2,1)} %copy-done.8) | copy-start | bytes 983044
  128.1 2.0 collective-permute-start.18
  138.6 25.3 %collective-permute-start.21 = (bf16[128,4096]{1,0:T(8,128)(2,1)S(1)}, bf16[128,4096]{1,0:T(8,128)(2,1)S(1)}, u32[]{:S(2)}, u32[]{:S(2)}) collective-permute-start(bf16[128,4096]{1,0:T(8,128)(2,1)S(1)} %get-tuple-element.103), channel_id=1, source_target_pairs={{0,2},{1,3},{2,0},{3,1},{4,6},{5,7},{6,4},{7,5},{8,10},{9,11},{10,... | collective-permute-start | bytes 3145736 | tf_op jit(solution)/shard_map/ppermute | solution.py:28
  150.5 2.0 collective-permute-start.20
  161.1 25.9 %collective-permute-start.24 = (bf16[128,4096]{1,0:T(8,128)(2,1)S(1)}, bf16[128,4096]{1,0:T(8,128)(2,1)S(1)}, u32[]{:S(2)}, u32[]{:S(2)}) collective-permute-start(bf16[128,4096]{1,0:T(8,128)(2,1)S(1)} %get-tuple-element.112), channel_id=1, source_target_pairs={{0,2},{1,3},{2,0},{3,1},{4,6},{5,7},{6,4},{7,5},{8,10},{9,11},{10,... | collective-permute-start | bytes 3145736 | tf_op jit(solution)/shard_map/ppermute | solution.py:28
  164.1 13.2 %collective-permute-start.23 = (bf16[2,32,4096]{2,1,0:T(8,128)(2,1)S(1)}, bf16[2,32,4096]{2,1,0:T(8,128)(2,1)S(1)}, u32[]{:S(2)}, u32[]{:S(2)}) collective-permute-start(bf16[2,32,4096]{2,1,0:T(8,128)(2,1)S(1)} %get-tuple-element.109), channel_id=1, source_target_pairs={{0,4},{1,5},{2,6},{3,7},{4,0},{5,1},{6,2},{7,3},{8,12},{9,13},{10,... | collective-permute-start | bytes 1572872 | tf_op jit(solution)/shard_map/ppermute | solution.py:28
  176.0 2.0 collective-permute-start.22
  186.5 27.4 %collective-permute-start.29 = (bf16[128,4096]{1,0:T(8,128)(2,1)S(1)}, bf16[128,4096]{1,0:T(8,128)(2,1)S(1)}, u32[]{:S(2)}, u32[]{:S(2)}) collective-permute-start(bf16[128,4096]{1,0:T(8,128)(2,1)S(1)} %get-tuple-element.123), channel_id=1, source_target_pairs={{0,2},{1,3},{2,0},{3,1},{4,6},{5,7},{6,4},{7,5},{8,10},{9,11},{10,... | collective-permute-start | bytes 3145736 | tf_op jit(solution)/shard_map/ppermute | solution.py:28
  187.2 13.9 %collective-permute-start.26 = (bf16[2,32,4096]{2,1,0:T(8,128)(2,1)S(1)}, bf16[2,32,4096]{2,1,0:T(8,128)(2,1)S(1)}, u32[]{:S(2)}, u32[]{:S(2)}) collective-permute-start(bf16[2,32,4096]{2,1,0:T(8,128)(2,1)S(1)} %get-tuple-element.116), channel_id=1, source_target_pairs={{0,4},{1,5},{2,6},{3,7},{4,0},{5,1},{6,2},{7,3},{8,12},{9,13},{10,... | collective-permute-start | bytes 1572872 | tf_op jit(solution)/shard_map/ppermute | solution.py:28
  198.6 2.7 %collective-permute-start.25 = (bf16[256,1024]{1,0:T(8,128)(2,1)S(1)}, bf16[256,1024]{1,0:T(8,128)(2,1)S(1)}, u32[]{:S(2)}, u32[]{:S(2)}) collective-permute-start(bf16[256,1024]{1,0:T(8,128)(2,1)S(1)} %fix.7.after_ref.own_ref), channel_id=1, source_target_pairs={{0,1},{1,0},{2,3},{3,2},{4,5},{5,4},{6,7},{7,6},{8,9},{9,8},{10,11... | collective-permute-start | bytes 1572872 | tf_op jit(solution)/shard_map/ppermute | solution.py:28
  198.6 15.2 %collective-permute-start.27 = (bf16[1,32,4096]{2,1,0:T(8,128)(2,1)S(1)}, bf16[1,32,4096]{2,1,0:T(8,128)(2,1)S(1)}, u32[]{:S(2)}, u32[]{:S(2)}) collective-permute-start(bf16[1,32,4096]{2,1,0:T(8,128)(2,1)S(1)} %get-tuple-element.120), channel_id=1, source_target_pairs={{0,8},{1,9},{2,10},{3,11},{4,12},{5,13},{6,14},{7,15},{8,0},{9,1},... | collective-permute-start | bytes 786440 | tf_op jit(solution)/shard_map/ppermute | solution.py:28
  206.2 17.7 %collective-permute-start.30 = (bf16[128,2048]{1,0:T(8,128)(2,1)S(1)}, bf16[128,2048]{1,0:T(8,128)(2,1)S(1)}, u32[]{:S(2)}, u32[]{:S(2)}) collective-permute-start(bf16[128,2048]{1,0:T(8,128)(2,1)S(1)} %get-tuple-element.125), channel_id=1, source_target_pairs={{0,2},{1,3},{2,0},{3,1},{4,6},{5,7},{6,4},{7,5},{8,10},{9,11},{10,... | collective-permute-start | bytes 1572872 | tf_op jit(solution)/shard_map/ppermute | solution.py:28
  214.2 20.5 %collective-permute-start.31 = (bf16[2,32,4096]{2,1,0:T(8,128)(2,1)S(1)}, bf16[2,32,4096]{2,1,0:T(8,128)(2,1)S(1)}, u32[]{:S(2)}, u32[]{:S(2)}) collective-permute-start(bf16[2,32,4096]{2,1,0:T(8,128)(2,1)S(1)} %get-tuple-element.127), channel_id=1, source_target_pairs={{0,4},{1,5},{2,6},{3,7},{4,0},{5,1},{6,2},{7,3},{8,12},{9,13},{10,... | collective-permute-start | bytes 1572872 | tf_op jit(solution)/shard_map/ppermute | solution.py:28
  215.0 27.6 %collective-permute-start.35 = (bf16[128,2048]{1,0:T(8,128)(2,1)S(1)}, bf16[128,2048]{1,0:T(8,128)(2,1)S(1)}, u32[]{:S(2)}, u32[]{:S(2)}) collective-permute-start(bf16[128,2048]{1,0:T(8,128)(2,1)S(1)} %get-tuple-element.134), channel_id=1, source_target_pairs={{0,2},{1,3},{2,0},{3,1},{4,6},{5,7},{6,4},{7,5},{8,10},{9,11},{10,... | collective-permute-start | bytes 1572872 | tf_op jit(solution)/shard_map/ppermute | solution.py:28
  216.2 19.7 %collective-permute-start.32 = (bf16[1,32,4096]{2,1,0:T(8,128)(2,1)S(1)}, bf16[1,32,4096]{2,1,0:T(8,128)(2,1)S(1)}, u32[]{:S(2)}, u32[]{:S(2)}) collective-permute-start(bf16[1,32,4096]{2,1,0:T(8,128)(2,1)S(1)} %get-tuple-element.129), channel_id=1, source_target_pairs={{0,8},{1,9},{2,10},{3,11},{4,12},{5,13},{6,14},{7,15},{8,0},{9,1},... | collective-permute-start | bytes 786440 | tf_op jit(solution)/shard_map/ppermute | solution.py:28
  224.0 18.5 %collective-permute-start.34 = (bf16[2,32,2048]{2,1,0:T(8,128)(2,1)S(1)}, bf16[2,32,2048]{2,1,0:T(8,128)(2,1)S(1)}, u32[]{:S(2)}, u32[]{:S(2)}) collective-permute-start(bf16[2,32,2048]{2,1,0:T(8,128)(2,1)S(1)} %get-tuple-element.132), channel_id=1, source_target_pairs={{0,4},{1,5},{2,6},{3,7},{4,0},{5,1},{6,2},{7,3},{8,12},{9,13},{10,... | collective-permute-start | bytes 786440 | tf_op jit(solution)/shard_map/ppermute | solution.py:28
  234.9 14.6 %collective-permute-start.36 = (bf16[1,32,4096]{2,1,0:T(8,128)(2,1)S(1)}, bf16[1,32,4096]{2,1,0:T(8,128)(2,1)S(1)}, u32[]{:S(2)}, u32[]{:S(2)}) collective-permute-start(bf16[1,32,4096]{2,1,0:T(8,128)(2,1)S(1)} %get-tuple-element.136), channel_id=1, source_target_pairs={{0,8},{1,9},{2,10},{3,11},{4,12},{5,13},{6,14},{7,15},{8,0},{9,1},... | collective-permute-start | bytes 786440 | tf_op jit(solution)/shard_map/ppermute | solution.py:28
  242.7 10.5 %collective-permute-start.38 = (bf16[2,32,2048]{2,1,0:T(8,128)(2,1)S(1)}, bf16[2,32,2048]{2,1,0:T(8,128)(2,1)S(1)}, u32[]{:S(2)}, u32[]{:S(2)}) collective-permute-start(bf16[2,32,2048]{2,1,0:T(8,128)(2,1)S(1)} %get-tuple-element.139), channel_id=1, source_target_pairs={{0,4},{1,5},{2,6},{3,7},{4,0},{5,1},{6,2},{7,3},{8,12},{9,13},{10,... | collective-permute-start | bytes 786440 | tf_op jit(solution)/shard_map/ppermute | solution.py:28
  242.8 14.3 %collective-permute-start.39 = (bf16[1,32,2048]{2,1,0:T(8,128)(2,1)S(1)}, bf16[1,32,2048]{2,1,0:T(8,128)(2,1)S(1)}, u32[]{:S(2)}, u32[]{:S(2)}) collective-permute-start(bf16[1,32,2048]{2,1,0:T(8,128)(2,1)S(1)} %get-tuple-element.141), channel_id=1, source_target_pairs={{0,8},{1,9},{2,10},{3,11},{4,12},{5,13},{6,14},{7,15},{8,0},{9,1},... | collective-permute-start | bytes 393224 | tf_op jit(solution)/shard_map/ppermute | solution.py:28
  253.3 9.0 %collective-permute-start.41 = (bf16[1,32,2048]{2,1,0:T(8,128)(2,1)S(1)}, bf16[1,32,2048]{2,1,0:T(8,128)(2,1)S(1)}, u32[]{:S(2)}, u32[]{:S(2)}) collective-permute-start(bf16[1,32,2048]{2,1,0:T(8,128)(2,1)S(1)} %get-tuple-element.144), channel_id=1, source_target_pairs={{0,8},{1,9},{2,10},{3,11},{4,12},{5,13},{6,14},{7,15},{8,0},{9,1},... | collective-permute-start | bytes 393224 | tf_op jit(solution)/shard_map/ppermute | solution.py:28
  256.5 5.9 %collective-permute-start.28 = (bf16[16,4096]{1,0:T(8,128)(2,1)S(1)}, bf16[16,4096]{1,0:T(8,128)(2,1)S(1)}, u32[]{:S(2)}, u32[]{:S(2)}) collective-permute-start(bf16[16,4096]{1,0:T(8,128)(2,1)S(1)} %get-tuple-element.122), channel_id=1, source_target_pairs={{0,1},{1,0},{2,3},{3,2},{4,5},{5,4},{6,7},{7,6},{8,9},{9,8},{10,11... | collective-permute-start | bytes 393224 | tf_op jit(solution)/shard_map/ppermute | solution.py:28
  256.5 5.9 %collective-permute-start.33 = (bf16[16,4096]{1,0:T(8,128)(2,1)S(1)}, bf16[16,4096]{1,0:T(8,128)(2,1)S(1)}, u32[]{:S(2)}, u32[]{:S(2)}) collective-permute-start(bf16[16,4096]{1,0:T(8,128)(2,1)S(1)} %get-tuple-element.131), channel_id=1, source_target_pairs={{0,1},{1,0},{2,3},{3,2},{4,5},{5,4},{6,7},{7,6},{8,9},{9,8},{10,11... | collective-permute-start | bytes 393224 | tf_op jit(solution)/shard_map/ppermute | solution.py:28
  257.1 5.4 %collective-permute-start.37 = (bf16[16,4096]{1,0:T(8,128)(2,1)S(1)}, bf16[16,4096]{1,0:T(8,128)(2,1)S(1)}, u32[]{:S(2)}, u32[]{:S(2)}) collective-permute-start(bf16[16,4096]{1,0:T(8,128)(2,1)S(1)} %get-tuple-element.138), channel_id=1, source_target_pairs={{0,1},{1,0},{2,3},{3,2},{4,5},{5,4},{6,7},{7,6},{8,9},{9,8},{10,11... | collective-permute-start | bytes 393224 | tf_op jit(solution)/shard_map/ppermute | solution.py:28
  257.1 5.3 %collective-permute-start.40 = (bf16[16,2048]{1,0:T(8,128)(2,1)S(1)}, bf16[16,2048]{1,0:T(8,128)(2,1)S(1)}, u32[]{:S(2)}, u32[]{:S(2)}) collective-permute-start(bf16[16,2048]{1,0:T(8,128)(2,1)S(1)} %get-tuple-element.143), channel_id=1, source_target_pairs={{0,1},{1,0},{2,3},{3,2},{4,5},{5,4},{6,7},{7,6},{8,9},{9,8},{10,11... | collective-permute-start | bytes 196616 | tf_op jit(solution)/shard_map/ppermute | solution.py:28
  262.3 1.3 collective-permute-start.42
  (8 other events, 11.1 us)

commit v12 on v11

--- a/solution.py
+++ b/solution.py
@@ -293,7 +293,7 @@
     lows = [low] + [swap(low, 4 * m, n) for m in range(1, zs)]
     (mine,) = small(merge_kernel, me, lows, [(zs,) + piece], "merge_z")
     beside = swap(mine, 2, n)
-    return keep, mine, (mine, beside, swap(mine, 1, n), swap(beside, 1, n))
+    return keep, low, mine, (mine, beside, swap(mine, 1, n), swap(beside, 1, n))
 
 
 def assemble_low(lows, index, low_scr, me_ref):
@@ -692,8 +692,7 @@
     me = me_scalar.reshape(1)
 
     moved_conv = exchange_conv(prefilled_conv, me, n)
-    half_weight = weight_half(me, moved_conv[1], out_weight)
-    packed = pack_state((half_weight,), prefilled_state, n)
+    packed = pack_state((moved_conv[1],), prefilled_state, n)
     cols = out_weight.shape[1] // 2
 
     is_live = jnp.arange(slots, dtype=jnp.int32)[None, :] < live_counts[:, None]
@@ -718,10 +717,11 @@
     conv, send, keep = conv_steps(
         tuple(range(STEPS)), n, me, (packed,), spread, old, moved_conv, step_x, conv_weight, bias, proj
     )
-    behind, merged, lows = reduce_projection(send, keep, gain, me, n)
+    behind, low, merged, lows = reduce_projection(send, keep, gain, me, n)
+    half_weight = weight_half(me, behind, out_weight)
     packed = hold(packed, merged)
     moved_state = lax.all_to_all(packed, "dex", 0, 0, tiled=True)
-    other_weight = swap(hold(half_weight, behind), 1, n)
+    other_weight = swap(hold(half_weight, low), 1, n)
 
     state = resident_state.reshape(rows * STATE, c)
     sends, keeps, gated = {}, {}, {}
@@ -795,13 +795,12 @@
     last = reduce(t, 0, last, 0)
     for stage in range(1, stages):
         last = reduce(t - 1, stage, last)
+    last = reduce(t, 0, last, 1)
     last = reduce(t - 2, stages, last)
-    for stage in range(1, stages):
-        last = reduce(t, stage, last, 0)
-    last = reduce(t, 0, last, 1)
+    for part in range(2):
+        for stage in range(1, stages):
+            last = reduce(t, stage, last, part)
     last = reduce(t - 1, stages, last)
-    for stage in range(1, stages):
-        last = reduce(t, stage, last, 1)
     last = reduce(t, stages, last, 0)
     last = reduce(t, stages, last, 1)
     pieces = [[(keeps[t, part], sends[t, part]) for part in range(1 if t < STEPS - 1 else 2)] for t in range(STEPS)]

time: 267 us -> 265 us (level)
  starting transfers between devices: 48.6 us -> 45.2 us
    ppermute x43, starting transfers between devices: 43.7 us -> 40.3 us  [swap(): return lax.ppermute(x, 'dex', [(i, i ^ mask) for i in range(n)])]
    unnamed x56 -> x54, local copies, waits for them, and re-layouts: 7.68 us -> 10 us
  transfers between devices with their start and end apart: 44 -> 44, of which waited for: 25 -> 24; matrix products, arithmetic and copies ran while one was open for 1% -> 1% of each run, Pallas kernels for 37% -> 37%
where the time goes in v12:
time: 265 us; the launch traced here: 263 us
  Pallas kernels  113 us (43%)
  waiting for transfers between devices  91.4 us (34%)
  starting transfers between devices  45.2 us (17%)
  local copies, waits for them, and re-layouts  11.3 us (4%)
    ppermute x43, waiting for transfers between devices, swap(): return lax.ppermute(x, 'dex', [(i, i ^ mask) for i in range(n)])  91.4 us
    pallas_call x4, Pallas kernels, state_step(): pl.pallas_call(functools.partial(state_kernel, t, len(after)), grid_spec=...  48.1 us
    ppermute x43, starting transfers between devices, swap(): return lax.ppermute(x, 'dex', [(i, i ^ mask) for i in range(n)])  40.3 us
    pallas_call x5, Pallas kernels, out_project(): pl.pallas_call(out_kernel, grid_spec=pltpu.PrefetchScalarGridSpec(num_sca...  35.3 us
    pallas_call x31, Pallas kernels, small(): pl.pallas_call(kernel, in_specs=[pl.BlockSpec(memory_space=pltpu.SMEM)] +...  14.2 us
    unnamed x54, local copies, waits for them, and re-layouts  10 us
    pallas_call x1, Pallas kernels, weight_half(): pl.pallas_call(half_kernel, grid_spec=pltpu.PrefetchScalarGridSpec(num_sc...  7.2 us
  transfers between devices with their start and end apart: 44, of which 24 were waited for; matrix products, arithmetic and copies ran while one was open for 1% of the time, Pallas kernels for 37%

profile of v12, /device:TPU:0, one launch (start us, length us, event | category | flops | bytes accessed | tf_op | source)
XLA Modules:
  0.0 263.3 jit_solution(3644540560489818634)
XLA Ops:
  0.0 1.2 copy-done.20
  1.3 3.0 %collective-permute-start = (bf16[4,16,768]{2,1,0:T(8,128)(2,1)S(1)}, bf16[4,16,768]{2,1,0:T(8,128)(2,1)S(1)}, u32[]{:S(2)}, u32[]{:S(2)}) collective-permute-start(bf16[4,16,768]{2,1,0:T(8,128)(2,1)S(1)} %get-tuple-element.77), channel_id=1, source_target_pairs={{0,2},{1,3},{2,0},{3,1},{4,6},{5,7},{6,4},{7,5},{8,10},{9,11},{10,... | collective-permute-start | bytes 294920 | tf_op jit(solution)/shard_map/ppermute | solution.py:28
  7.1 4.1 %collective-permute-done.3.refs_3_ = bf16[4,16,768]{2,1,0:T(8,128)(2,1)S(1)} collective-permute-done((bf16[4,16,768]{2,1,0:T(8,128)(2,1)S(1)}, bf16[4,16,768]{2,1,0:T(8,128)(2,1)S(1)}, u32[]{:S(2)}, u32[]{:S(2)}) %collective-permute-start.3) | collective-permute-done | bytes 98336 | tf_op jit(solution)/shard_map/ppermute | solution.py:28
  11.3 1.6 collective-permute-start.4
  12.9 2.6 collective-permute-start.5
  15.7 1.2 collective-permute-done.4.refs_0_.refs_1_
  16.9 2.2 copy-done.14
  19.1 2.1 pack_state.1.refs_4_.x_ref
  21.2 1.4 collective-permute-done.5.refs_2_
  22.7 3.8 %conv_project.1 = (f32[4,256,1024]{2,1,0:T(8,128)S(1)}, bf16[8,4,16,640]{3,2,1,0:T(8,128)(2,1)S(1)}, bf16[8,4,16,640]{3,2,1,0:T(8,128)(2,1)S(1)}) custom-call(s32[1]{0:T(128)} %bitcast.me_ref, s32[4,256]{1,0:T(4,128)S(1)} %broadcast_select_fusion.1.target_ref, f32[3,256,1024]{2,1,0:T(8,128)S(1)} %bitcast.38, bf16[4,256,1024]{2,1,0:T(8,128)(2,1)S(1)} %copy-done.16, ...), custom_call_target="tpu_custom_call" | custom-call | flops 1024 | bytes 1024 | tf_op jit(solution)/shard_map/conv_project/pallas_call | solution.py:212
  26.5 2.1 copy-done
  28.6 2.1 collective-permute-done.7.refs_1_
  31.4 9.2 %collective-permute-done.8.refs_1_ = bf16[4,4,16,640]{3,2,1,0:T(8,128)(2,1)S(1)} collective-permute-done((bf16[4,4,16,640]{3,2,1,0:T(8,128)(2,1)S(1)}, bf16[4,4,16,640]{3,2,1,0:T(8,128)(2,1)S(1)}, u32[]{:S(2)}, u32[]{:S(2)}) %collective-permute-start.8) | collective-permute-done | bytes 327712 | tf_op jit(solution)/shard_map/ppermute | solution.py:28
  40.8 1.7 collective-permute-start.9
  42.5 1.6 collective-permute-start.10
  44.1 1.2 collective-permute-start.11
  45.3 7.2 %weight_half.1.x_ref = bf16[1024,4096]{1,0:T(8,128)(2,1)} custom-call(s32[1]{0:T(128)} %bitcast.me_ref, bf16[4,4,16,640]{3,2,1,0:T(8,128)(2,1)} %copy-done.18, bf16[1024,8192]{1,0:T(8,128)(2,1)} %wown_ref.9), custom_call_target="tpu_custom_call" | custom-call | flops 1024 | bytes 1024 | tf_op jit(solution)/shard_map/weight_half/pallas_call | solution.py:147
  52.7 2.7 %collective-permute-start.14 = (bf16[4,16,640]{2,1,0:T(8,128)(2,1)S(1)}, bf16[4,16,640]{2,1,0:T(8,128)(2,1)S(1)}, u32[]{:S(2)}, u32[]{:S(2)}) collective-permute-start(bf16[4,16,640]{2,1,0:T(8,128)(2,1)S(1)} %norm.1.refs_0_.after_ref), channel_id=1, source_target_pairs={{0,12},{1,13},{2,14},{3,15},{4,8},{5,9},{6,10},{7,11},{8,4},{9,5},... | collective-permute-start | bytes 245768 | tf_op jit(solution)/shard_map/ppermute | solution.py:28
  55.4 1.7 collective-permute-start.12
  57.2 2.8 %collective-permute-done.14.refs_3_ = bf16[4,16,640]{2,1,0:T(8,128)(2,1)S(1)} collective-permute-done((bf16[4,16,640]{2,1,0:T(8,128)(2,1)S(1)}, bf16[4,16,640]{2,1,0:T(8,128)(2,1)S(1)}, u32[]{:S(2)}, u32[]{:S(2)}) %collective-permute-start.14) | collective-permute-done | bytes 81952 | tf_op jit(solution)/shard_map/ppermute | solution.py:28
  59.9 3.1 %collective-permute-done.13.refs_2_ = bf16[4,16,640]{2,1,0:T(8,128)(2,1)S(1)} collective-permute-done((bf16[4,16,640]{2,1,0:T(8,128)(2,1)S(1)}, bf16[4,16,640]{2,1,0:T(8,128)(2,1)S(1)}, u32[]{:S(2)}, u32[]{:S(2)}) %collective-permute-start.13) | collective-permute-done | bytes 81952 | tf_op jit(solution)/shard_map/ppermute | solution.py:28
  63.1 4.9 %all-to-all-start = ((bf16[16,64,1024]{2,1,0:T(8,128)(2,1)}), bf16[16,64,1024]{2,1,0:T(8,128)(2,1)}, u32[]{:S(2)}, u32[]{:S(2)}) async-start(bf16[16,64,1024]{2,1,0:T(8,128)(2,1)} %hold.2.after_ref.refs_0_), calls=%async_computation | async-start | bytes 4194304 | tf_op jit(solution)/shard_map/all_to_all | solution.py:723
  68.2 1.6 collective-permute-start.15
  70.9 23.7 %collective-permute-done.15.refs_1_ = bf16[4,4,16,640]{3,2,1,0:T(8,128)(2,1)S(1)} collective-permute-done((bf16[4,4,16,640]{3,2,1,0:T(8,128)(2,1)S(1)}, bf16[4,4,16,640]{3,2,1,0:T(8,128)(2,1)S(1)}, u32[]{:S(2)}, u32[]{:S(2)}) %collective-permute-start.15) | collective-permute-done | bytes 327712 | tf_op jit(solution)/shard_map/ppermute | solution.py:28
  94.6 1.6 collective-permute-done.17.refs_3_
  96.8 16.4 %state_step.4 = (bf16[16,256,1024]{2,1,0:T(8,128)(2,1)}, bf16[256,1024]{1,0:T(8,128)(2,1)S(1)}) custom-call(s32[1]{0:T(128)} %bitcast.me_ref, bf16[16,64,1024]{2,1,0:T(8,128)(2,1)} %hold.2.after_ref.refs_0_, f32[256,1024]{1,0:T(8,128)S(1)} %get-tuple-element.92.refs_1_, f32[256,128]{1,0:T(8,128)S(1)} %get-tuple-element.93.refs_2_, f32[4,256,1024]{2,1,0:T(8,128)} %copy-done, ...), custom_call_target="tpu_custom_call" | custom-call | flops 1024 | bytes 1024 | tf_op jit(solution)/shard_map/state_step/pallas_call | solution.py:447
  113.3 2.6 gather_live.1.live_ref
  115.9 1.1 copy-done.10
  117.1 0.8 copy-done.12
  117.9 1.4 copy-done.11
  119.3 1.0 copy-done.13
  120.4 5.7 %live_steps.1.after_ref.live_ref = bf16[4,32,1024]{2,1,0:T(8,128)(2,1)S(1)} custom-call(s32[2,32]{1,0:T(2,128)S(1)} %pad_add_fusion.slot_ref, bf16[256,1024]{1,0:T(8,128)(2,1)S(1)} %copy-done.13, bf16[16,64,1024]{2,1,0:T(8,128)(2,1)} %all-to-all-done.moved_ref, f32[4,32,3200]{2,1,0:T(8,128)S(1)} %copy-done.11, f32[16,1024]{1,0:T(8,128)S(1)} %copy-done.17, ...), custom_call_target="tpu_custom_call" | custom-call | flops 1024 | bytes 1024 | tf_op jit(solution)/shard_map/live_steps/pallas_call | solution.py:47
  127.2 1.1 collective-permute-done.18.other_ref
  128.3 8.5 %out_project.5 = (bf16[128,4096]{1,0:T(8,128)(2,1)S(1)}, bf16[128,4096]{1,0:T(8,128)(2,1)S(1)}) custom-call(s32[1]{0:T(128)} %bitcast.me_ref, bf16[256,1024]{1,0:T(8,128)(2,1)S(1)} %fix.4.after_ref.own_ref, bf16[256,1024]{1,0:T(8,128)(2,1)S(1)} %collective-permute-done.18.other_ref, bf16[1024,8192]{1,0:T(8,128)(2,1)} %wown_ref.9, ...), custom_call_target="tpu_custom_call" | custom-call | flops 1024 | bytes 1024 | tf_op jit(solution)/shard_map/out_project/pallas_call | solution.py:588
  137.0 11.4 %state_step.5 = (bf16[16,256,1024]{2,1,0:T(8,128)(2,1)}, bf16[256,1024]{1,0:T(8,128)(2,1)S(1)}) custom-call(s32[1]{0:T(128)} %bitcast.me_ref, bf16[128,4096]{1,0:T(8,128)(2,1)S(1)} %get-tuple-element.97.refs_0_, f32[256,1024]{1,0:T(8,128)S(1)} %get-tuple-element.98.refs_1_, f32[256,128]{1,0:T(8,128)S(1)} %get-tuple-element.96.refs_0_.refs_2_, ...), custom_call_target="tpu_custom_call" | custom-call | flops 1024 | bytes 1024 | tf_op jit(solution)/shard_map/state_step/pallas_call | solution.py:447
  149.5 1.2 collective-permute-done.20.other_ref
  150.6 8.5 %out_project.6 = (bf16[128,4096]{1,0:T(8,128)(2,1)S(1)}, bf16[128,4096]{1,0:T(8,128)(2,1)S(1)}) custom-call(s32[1]{0:T(128)} %bitcast.me_ref, bf16[256,1024]{1,0:T(8,128)(2,1)S(1)} %fix.5.after_ref.own_ref, bf16[256,1024]{1,0:T(8,128)(2,1)S(1)} %collective-permute-done.20.other_ref, bf16[1024,8192]{1,0:T(8,128)(2,1)} %wown_ref.9, ...), custom_call_target="tpu_custom_call" | custom-call | flops 1024 | bytes 1024 | tf_op jit(solution)/shard_map/out_project/pallas_call | solution.py:588
  159.2 2.1 collective-permute-start.24
  161.2 0.9 collective-permute-done.21
  162.5 11.4 %state_step.6 = (bf16[16,256,1024]{2,1,0:T(8,128)(2,1)}, bf16[256,1024]{1,0:T(8,128)(2,1)S(1)}) custom-call(s32[1]{0:T(128)} %bitcast.me_ref, bf16[2,32,4096]{2,1,0:T(8,128)(2,1)S(1)} %get-tuple-element.104.refs_0_.keep_ref, f32[256,1024]{1,0:T(8,128)S(1)} %get-tuple-element.105.refs_1_, f32[256,128]{1,0:T(8,128)S(1)} %get-tuple-element.101.refs_0_.refs_2_, ...), custom_call_target="tpu_custom_call" | custom-call | flops 1024 | bytes 1024 | tf_op jit(solution)/shard_map/state_step/pallas_call | solution.py:447
  174.8 0.7 collective-permute-done.23.got_ref
  176.1 8.5 %out_project.7 = (bf16[128,4096]{1,0:T(8,128)(2,1)S(1)}, bf16[128,4096]{1,0:T(8,128)(2,1)S(1)}) custom-call(s32[1]{0:T(128)} %bitcast.me_ref, bf16[256,1024]{1,0:T(8,128)(2,1)S(1)} %fix.6.after_ref.own_ref, bf16[256,1024]{1,0:T(8,128)(2,1)S(1)} %collective-permute-done.22.other_ref, bf16[1024,8192]{1,0:T(8,128)(2,1)} %wown_ref.9, ...), custom_call_target="tpu_custom_call" | custom-call | flops 1024 | bytes 1024 | tf_op jit(solution)/shard_map/out_project/pallas_call | solution.py:588
  184.7 0.8 collective-permute-start.29
  185.8 1.6 collective-permute-start.26
  187.3 9.0 %state_step.7.after_ref.gated_ref = bf16[256,1024]{1,0:T(8,128)(2,1)S(1)} custom-call(s32[1]{0:T(128)} %bitcast.me_ref, bf16[2,32,4096]{2,1,0:T(8,128)(2,1)S(1)} %get-tuple-element.113.refs_0_.keep_ref, f32[256,1024]{1,0:T(8,128)S(1)} %get-tuple-element.114.refs_1_, f32[256,128]{1,0:T(8,128)S(1)} %get-tuple-element.108.after_ref.refs_2_, ...), custom_call_target="tpu_custom_call" | custom-call | flops 1024 | bytes 1024 | tf_op jit(solution)/shard_map/state_step/pallas_call | solution.py:447
  196.7 2.1 collective-permute-start.27
  199.6 4.8 %out_project.8 = (bf16[128,2048]{1,0:T(8,128)(2,1)S(1)}, bf16[128,2048]{1,0:T(8,128)(2,1)S(1)}) custom-call(s32[1]{0:T(128)} %bitcast.me_ref, bf16[256,1024]{1,0:T(8,128)(2,1)S(1)} %fix.7.after_ref.own_ref, bf16[256,1024]{1,0:T(8,128)(2,1)S(1)} %collective-permute-done.25.other_ref, bf16[1024,8192]{1,0:T(8,128)(2,1)} %wown_ref.9, ...), custom_call_target="tpu_custom_call" | custom-call | flops 1024 | bytes 1024 | tf_op jit(solution)/shard_map/out_project/pallas_call | solution.py:588
  204.5 1.6 collective-permute-start.30
  206.1 4.8 %out_project.9 = (bf16[128,2048]{1,0:T(8,128)(2,1)S(1)}, bf16[128,2048]{1,0:T(8,128)(2,1)S(1)}) custom-call(s32[1]{0:T(128)} %bitcast.me_ref, bf16[256,1024]{1,0:T(8,128)(2,1)S(1)} %fix.7.after_ref.own_ref, bf16[256,1024]{1,0:T(8,128)(2,1)S(1)} %collective-permute-done.25.other_ref, bf16[1024,8192]{1,0:T(8,128)(2,1)} %wown_ref.9, ...), custom_call_target="tpu_custom_call" | custom-call | flops 1024 | bytes 1024 | tf_op jit(solution)/shard_map/out_project/pallas_call | solution.py:588
  210.9 1.0 collective-permute-done.27.got_ref
  212.2 0.8 collective-permute-start.31
  213.1 1.1 collective-permute-start.32
  214.2 3.4 %collective-permute-start.33 = (bf16[1,32,4096]{2,1,0:T(8,128)(2,1)S(1)}, bf16[1,32,4096]{2,1,0:T(8,128)(2,1)S(1)}, u32[]{:S(2)}, u32[]{:S(2)}) collective-permute-start(bf16[1,32,4096]{2,1,0:T(8,128)(2,1)S(1)} %get-tuple-element.131), channel_id=1, source_target_pairs={{0,8},{1,9},{2,10},{3,11},{4,12},{5,13},{6,14},{7,15},{8,0},{9,1},... | collective-permute-start | bytes 786440 | tf_op jit(solution)/shard_map/ppermute | solution.py:28
  217.6 4.4 %collective-permute-done.30 = bf16[128,2048]{1,0:T(8,128)(2,1)S(1)} collective-permute-done((bf16[128,2048]{1,0:T(8,128)(2,1)S(1)}, bf16[128,2048]{1,0:T(8,128)(2,1)S(1)}, u32[]{:S(2)}, u32[]{:S(2)}) %collective-permute-start.30) | collective-permute-done | bytes 524320 | tf_op jit(solution)/shard_map/ppermute | solution.py:28
  222.1 2.1 collective-permute-start.35
  224.1 8.6 %collective-permute-done.31.got_ref = bf16[2,32,4096]{2,1,0:T(8,128)(2,1)S(1)} collective-permute-done((bf16[2,32,4096]{2,1,0:T(8,128)(2,1)S(1)}, bf16[2,32,4096]{2,1,0:T(8,128)(2,1)S(1)}, u32[]{:S(2)}, u32[]{:S(2)}) %collective-permute-start.31) | collective-permute-done | bytes 524320 | tf_op jit(solution)/shard_map/ppermute | solution.py:28
  233.0 1.6 collective-permute-start.36
  234.6 2.2 collective-permute-start.37
  236.8 8.5 %collective-permute-done.35.got_ref = bf16[2,32,2048]{2,1,0:T(8,128)(2,1)S(1)} collective-permute-done((bf16[2,32,2048]{2,1,0:T(8,128)(2,1)S(1)}, bf16[2,32,2048]{2,1,0:T(8,128)(2,1)S(1)}, u32[]{:S(2)}, u32[]{:S(2)}) %collective-permute-start.35) | collective-permute-done | bytes 262176 | tf_op jit(solution)/shard_map/ppermute | solution.py:28
  245.5 4.1 %collective-permute-done.36.got_ref = bf16[2,32,2048]{2,1,0:T(8,128)(2,1)S(1)} collective-permute-done((bf16[2,32,2048]{2,1,0:T(8,128)(2,1)S(1)}, bf16[2,32,2048]{2,1,0:T(8,128)(2,1)S(1)}, u32[]{:S(2)}, u32[]{:S(2)}) %collective-permute-start.36) | collective-permute-done | bytes 262176 | tf_op jit(solution)/shard_map/ppermute | solution.py:28
  250.6 7.6 %collective-permute-done.39.got_ref = bf16[1,32,2048]{2,1,0:T(8,128)(2,1)S(1)} collective-permute-done((bf16[1,32,2048]{2,1,0:T(8,128)(2,1)S(1)}, bf16[1,32,2048]{2,1,0:T(8,128)(2,1)S(1)}, u32[]{:S(2)}, u32[]{:S(2)}) %collective-permute-start.39) | collective-permute-done | bytes 131104 | tf_op jit(solution)/shard_map/ppermute | solution.py:28
  258.3 1.4 collective-permute-done.41.got_ref
  259.9 1.2 collective-permute-done.42.refs_9_
  261.1 2.3 final_join.1
  (143 shorter events, 13.9 us)
Async XLA Ops:
  0.0 22.6 %copy-start.19 = (bf16[1024,544]{0,1:T(8,128)(2,1)S(1)}, bf16[1024,544]{0,1:T(8,128)(2,1)}, u32[]{:S(2)}) copy-start(bf16[1024,544]{0,1:T(8,128)(2,1)} %param.27) | copy-start | bytes 3342340
  1.2 21.4 %copy-start.23 = (f32[4,1024]{1,0:T(4,128)S(1)}, f32[4,1024]{1,0:T(4,128)}, u32[]{:S(2)}) copy-start(f32[4,1024]{1,0:T(4,128)} %w_ref.2) | copy-start | bytes 49156
  1.2 21.4 %copy-start.24 = (f32[1024]{0:T(1024)S(1)}, f32[1024]{0:T(1024)}, u32[]{:S(2)}) copy-start(f32[1024]{0:T(1024)} %param.26) | copy-start | bytes 12292
  1.3 5.8 %collective-permute-start = (bf16[4,16,768]{2,1,0:T(8,128)(2,1)S(1)}, bf16[4,16,768]{2,1,0:T(8,128)(2,1)S(1)}, u32[]{:S(2)}, u32[]{:S(2)}) collective-permute-start(bf16[4,16,768]{2,1,0:T(8,128)(2,1)S(1)} %get-tuple-element.77), channel_id=1, source_target_pairs={{0,2},{1,3},{2,0},{3,1},{4,6},{5,7},{6,4},{7,5},{8,10},{9,11},{10,... | collective-permute-start | bytes 294920 | tf_op jit(solution)/shard_map/ppermute | solution.py:28
  4.3 2.8 %collective-permute-start.1 = (bf16[4,16,768]{2,1,0:T(8,128)(2,1)S(1)}, bf16[4,16,768]{2,1,0:T(8,128)(2,1)S(1)}, u32[]{:S(2)}, u32[]{:S(2)}) collective-permute-start(bf16[4,16,768]{2,1,0:T(8,128)(2,1)S(1)} %get-tuple-element.78), channel_id=1, source_target_pairs={{0,1},{1,0},{2,3},{3,2},{4,5},{5,4},{6,7},{7,6},{8,9},{9,8},{10,11... | collective-permute-start | bytes 294920 | tf_op jit(solution)/shard_map/ppermute | solution.py:28
  4.3 2.1 collective-permute-start.2
  6.5 4.8 %collective-permute-start.3 = (bf16[4,16,768]{2,1,0:T(8,128)(2,1)S(1)}, bf16[4,16,768]{2,1,0:T(8,128)(2,1)S(1)}, u32[]{:S(2)}, u32[]{:S(2)}) collective-permute-start(bf16[4,16,768]{2,1,0:T(8,128)(2,1)S(1)} %collective-permute-done.2), channel_id=1, source_target_pairs={{0,2},{1,3},{2,0},{3,1},{4,6},{5,7},{6,4},{7,5},{8,10},{9,11},{10,... | collective-permute-start | bytes 294920 | tf_op jit(solution)/shard_map/ppermute | solution.py:28
  11.3 5.7 %collective-permute-start.4 = (bf16[4,16,768]{2,1,0:T(8,128)(2,1)S(1)}, bf16[4,16,768]{2,1,0:T(8,128)(2,1)S(1)}, u32[]{:S(2)}, u32[]{:S(2)}) collective-permute-start(bf16[4,16,768]{2,1,0:T(8,128)(2,1)S(1)} %get-tuple-element.80), channel_id=1, source_target_pairs={{0,4},{1,5},{2,6},{3,7},{4,0},{5,1},{6,2},{7,3},{8,12},{9,13},{10,... | collective-permute-start | bytes 294920 | tf_op jit(solution)/shard_map/ppermute | solution.py:28
  12.9 9.7 %collective-permute-start.5 = (bf16[4,16,768]{2,1,0:T(8,128)(2,1)S(1)}, bf16[4,16,768]{2,1,0:T(8,128)(2,1)S(1)}, u32[]{:S(2)}, u32[]{:S(2)}) collective-permute-start(bf16[4,16,768]{2,1,0:T(8,128)(2,1)S(1)} %get-tuple-element.82), channel_id=1, source_target_pairs={{0,8},{1,9},{2,10},{3,11},{4,12},{5,13},{6,14},{7,15},{8,0},{9,1},... | collective-permute-start | bytes 294920 | tf_op jit(solution)/shard_map/ppermute | solution.py:28
  15.5 7.1 %collective-permute-start.6 = (bf16[4,16,768]{2,1,0:T(8,128)(2,1)S(1)}, bf16[4,16,768]{2,1,0:T(8,128)(2,1)S(1)}, u32[]{:S(2)}, u32[]{:S(2)}) collective-permute-start(bf16[4,16,768]{2,1,0:T(8,128)(2,1)S(1)} %get-tuple-element.83), channel_id=1, source_target_pairs={{0,12},{1,13},{2,14},{3,15},{4,8},{5,9},{6,10},{7,11},{8,4},{9,5},... | collective-permute-start | bytes 294920 | tf_op jit(solution)/shard_map/ppermute | solution.py:28
  19.1 3.5 %copy-start.15 = (f32[256,3,1024]{2,0,1:T(8,128)S(1)}, f32[256,3,1024]{2,0,1:T(8,128)}, u32[]{:S(2)}) copy-start(f32[256,3,1024]{2,0,1:T(8,128)} %param.18) | copy-start | bytes 9437188
  19.1 3.6 %copy-start.16 = (bf16[4,256,1024]{2,1,0:T(8,128)(2,1)S(1)}, bf16[4,256,1024]{2,1,0:T(8,128)(2,1)}, u32[]{:S(2)}) copy-start(bf16[4,256,1024]{2,1,0:T(8,128)(2,1)} %x_ref.3) | copy-start | bytes 6291460
  22.7 22.6 %copy-start.25 = (f32[544]{0:T(1024)S(1)}, f32[544]{0:T(1024)}, u32[]{:S(2)}) copy-start(f32[544]{0:T(1024)} %param.28) | copy-start | bytes 6532
  28.6 2.1 collective-permute-start.7
  30.9 14.4 %copy-start.18 = (bf16[4,4,16,640]{3,2,1,0:T(8,128)(2,1)}, bf16[4,4,16,640]{3,2,1,0:T(8,128)(2,1)S(1)}, u32[]{:S(2)}) copy-start(bf16[4,4,16,640]{3,2,1,0:T(8,128)(2,1)S(1)} %get-tuple-element.86.refs_0_.after_ref) | copy-start | bytes 983044
  30.9 9.8 %collective-permute-start.8 = (bf16[4,4,16,640]{3,2,1,0:T(8,128)(2,1)S(1)}, bf16[4,4,16,640]{3,2,1,0:T(8,128)(2,1)S(1)}, u32[]{:S(2)}, u32[]{:S(2)}) collective-permute-start(bf16[4,4,16,640]{3,2,1,0:T(8,128)(2,1)S(1)} %get-tuple-element.87), channel_id=1, source_target_pairs={{0,2},{1,3},{2,0},{3,1},{4,6},{5,7},{6,4},{7,5},{8,10},{9,11},{10,... | collective-permute-start | bytes 983048 | tf_op jit(solution)/shard_map/ppermute | solution.py:28
  40.8 11.7 %collective-permute-start.9 = (bf16[4,16,640]{2,1,0:T(8,128)(2,1)S(1)}, bf16[4,16,640]{2,1,0:T(8,128)(2,1)S(1)}, u32[]{:S(2)}, u32[]{:S(2)}) collective-permute-start(bf16[4,16,640]{2,1,0:T(8,128)(2,1)S(1)} %get-tuple-element.89), channel_id=1, source_target_pairs={{0,4},{1,5},{2,6},{3,7},{4,0},{5,1},{6,2},{7,3},{8,12},{9,13},{10,... | collective-permute-start | bytes 245768 | tf_op jit(solution)/shard_map/ppermute | solution.py:28
  42.5 10.0 %collective-permute-start.10 = (bf16[4,16,640]{2,1,0:T(8,128)(2,1)S(1)}, bf16[4,16,640]{2,1,0:T(8,128)(2,1)S(1)}, u32[]{:S(2)}, u32[]{:S(2)}) collective-permute-start(bf16[4,16,640]{2,1,0:T(8,128)(2,1)S(1)} %get-tuple-element.90), channel_id=1, source_target_pairs={{0,8},{1,9},{2,10},{3,11},{4,12},{5,13},{6,14},{7,15},{8,0},{9,1},... | collective-permute-start | bytes 245768 | tf_op jit(solution)/shard_map/ppermute | solution.py:28
  44.1 8.4 %collective-permute-start.11 = (bf16[4,16,640]{2,1,0:T(8,128)(2,1)S(1)}, bf16[4,16,640]{2,1,0:T(8,128)(2,1)S(1)}, u32[]{:S(2)}, u32[]{:S(2)}) collective-permute-start(bf16[4,16,640]{2,1,0:T(8,128)(2,1)S(1)} %get-tuple-element.91), channel_id=1, source_target_pairs={{0,12},{1,13},{2,14},{3,15},{4,8},{5,9},{6,10},{7,11},{8,4},{9,5},... | collective-permute-start | bytes 245768 | tf_op jit(solution)/shard_map/ppermute | solution.py:28
  52.6 75.7 %collective-permute-start.19 = (bf16[1024,4096]{1,0:T(8,128)(2,1)}, bf16[1024,4096]{1,0:T(8,128)(2,1)}, u32[]{:S(2)}, u32[]{:S(2)}) collective-permute-start(bf16[1024,4096]{1,0:T(8,128)(2,1)} %hold.3), channel_id=1, source_target_pairs={{0,1},{1,0},{2,3},{3,2},{4,5},{5,4},{6,7},{7,6},{8,9},{9,8},{10,11... | collective-permute-start | bytes 25165832 | tf_op jit(solution)/shard_map/ppermute | solution.py:28
  52.7 7.2 %collective-permute-start.14 = (bf16[4,16,640]{2,1,0:T(8,128)(2,1)S(1)}, bf16[4,16,640]{2,1,0:T(8,128)(2,1)S(1)}, u32[]{:S(2)}, u32[]{:S(2)}) collective-permute-start(bf16[4,16,640]{2,1,0:T(8,128)(2,1)S(1)} %norm.1.refs_0_.after_ref), channel_id=1, source_target_pairs={{0,12},{1,13},{2,14},{3,15},{4,8},{5,9},{6,10},{7,11},{8,4},{9,5},... | collective-permute-start | bytes 245768 | tf_op jit(solution)/shard_map/ppermute | solution.py:28
  55.4 7.6 %collective-permute-start.13 = (bf16[4,16,640]{2,1,0:T(8,128)(2,1)S(1)}, bf16[4,16,640]{2,1,0:T(8,128)(2,1)S(1)}, u32[]{:S(2)}, u32[]{:S(2)}) collective-permute-start(bf16[4,16,640]{2,1,0:T(8,128)(2,1)S(1)} %norm.1.refs_0_.after_ref), channel_id=1, source_target_pairs={{0,8},{1,9},{2,10},{3,11},{4,12},{5,13},{6,14},{7,15},{8,0},{9,1},... | collective-permute-start | bytes 245768 | tf_op jit(solution)/shard_map/ppermute | solution.py:28
  55.4 7.6 %collective-permute-start.12 = (bf16[4,16,640]{2,1,0:T(8,128)(2,1)S(1)}, bf16[4,16,640]{2,1,0:T(8,128)(2,1)S(1)}, u32[]{:S(2)}, u32[]{:S(2)}) collective-permute-start(bf16[4,16,640]{2,1,0:T(8,128)(2,1)S(1)} %norm.1.refs_0_.after_ref), channel_id=1, source_target_pairs={{0,4},{1,5},{2,6},{3,7},{4,0},{5,1},{6,2},{7,3},{8,12},{9,13},{10,... | collective-permute-start | bytes 245768 | tf_op jit(solution)/shard_map/ppermute | solution.py:28
  63.0 5.0 %copy-start.26 = (s32[16]{0:T(128)S(1)}, s32[16]{0:T(128)}, u32[]{:S(2)}) copy-start(s32[16]{0:T(128)} %param.21) | copy-start | bytes 196
  63.0 33.1 %copy-start.3 = (bf16[512,1024]{1,0:T(8,128)(2,1)S(1)}, bf16[512,1024]{1,0:T(8,128)(2,1)}, u32[]{:S(2)}) copy-start(bf16[512,1024]{1,0:T(8,128)(2,1)} %refs_4_.14) | copy-start | bytes 3145732
  63.0 33.1 %copy-start.21 = (f32[1024]{0:T(1024)S(1)}, f32[1024]{0:T(1024)}, u32[]{:S(2)}) copy-start(f32[1024]{0:T(1024)} %param.30) | copy-start | bytes 12292
  63.1 33.7 %copy-start.2 = (bf16[4,256,1024]{2,1,0:T(8,128)(2,1)S(1)}, bf16[4,256,1024]{2,1,0:T(8,128)(2,1)}, u32[]{:S(2)}) copy-start(bf16[4,256,1024]{2,1,0:T(8,128)(2,1)} %refs_4_.15) | copy-start | bytes 6291460
  63.1 33.7 %copy-start.17 = (f32[16,1024]{1,0:T(8,128)S(1)}, f32[16,1024]{1,0:T(8,128)}, u32[]{:S(2)}) copy-start(f32[16,1024]{1,0:T(8,128)} %refs_5_.9) | copy-start | bytes 196612
  63.1 33.7 %copy-start.22 = (f32[1024]{0:T(1024)S(1)}, f32[1024]{0:T(1024)}, u32[]{:S(2)}) copy-start(f32[1024]{0:T(1024)} %param.32) | copy-start | bytes 12292
  63.1 54.8 %all-to-all-start = ((bf16[16,64,1024]{2,1,0:T(8,128)(2,1)}), bf16[16,64,1024]{2,1,0:T(8,128)(2,1)}, u32[]{:S(2)}, u32[]{:S(2)}) async-start(bf16[16,64,1024]{2,1,0:T(8,128)(2,1)} %hold.2.after_ref.refs_0_), calls=%async_computation | async-start | bytes 4194304 | tf_op jit(solution)/shard_map/all_to_all | solution.py:723
  68.2 26.3 %collective-permute-start.15 = (bf16[4,4,16,640]{3,2,1,0:T(8,128)(2,1)S(1)}, bf16[4,4,16,640]{3,2,1,0:T(8,128)(2,1)S(1)}, u32[]{:S(2)}, u32[]{:S(2)}) collective-permute-start(bf16[4,4,16,640]{3,2,1,0:T(8,128)(2,1)S(1)} %merge_z.1.after_ref.refs_0_), channel_id=1, source_target_pairs={{0,2},{1,3},{2,0},{3,1},{4,6},{5,7},{6,4},{7,5},{8,10},{9,11},{10,... | collective-permute-start | bytes 983048 | tf_op jit(solution)/shard_map/ppermute | solution.py:28
  70.8 23.8 %collective-permute-start.16 = (bf16[4,4,16,640]{3,2,1,0:T(8,128)(2,1)S(1)}, bf16[4,4,16,640]{3,2,1,0:T(8,128)(2,1)S(1)}, u32[]{:S(2)}, u32[]{:S(2)}) collective-permute-start(bf16[4,4,16,640]{3,2,1,0:T(8,128)(2,1)S(1)} %merge_z.1.after_ref.refs_0_), channel_id=1, source_target_pairs={{0,1},{1,0},{2,3},{3,2},{4,5},{5,4},{6,7},{7,6},{8,9},{9,8},{10,11... | collective-permute-start | bytes 983048 | tf_op jit(solution)/shard_map/ppermute | solution.py:28
  94.5 18.8 %copy-start.4 = (bf16[4,4,16,640]{3,2,1,0:T(8,128)(2,1)}, bf16[4,4,16,640]{3,2,1,0:T(8,128)(2,1)S(1)}, u32[]{:S(2)}) copy-start(bf16[4,4,16,640]{3,2,1,0:T(8,128)(2,1)S(1)} %collective-permute-done.15.refs_1_) | copy-start | bytes 983044
  94.5 1.6 collective-permute-start.17
  94.6 18.7 %copy-start.6 = (bf16[4,4,16,640]{3,2,1,0:T(8,128)(2,1)}, bf16[4,4,16,640]{3,2,1,0:T(8,128)(2,1)S(1)}, u32[]{:S(2)}) copy-start(bf16[4,4,16,640]{3,2,1,0:T(8,128)(2,1)S(1)} %collective-permute-done.16.refs_2_) | copy-start | bytes 983044
  96.2 17.2 %copy-start.8 = (bf16[4,4,16,640]{3,2,1,0:T(8,128)(2,1)}, bf16[4,4,16,640]{3,2,1,0:T(8,128)(2,1)S(1)}, u32[]{:S(2)}) copy-start(bf16[4,4,16,640]{3,2,1,0:T(8,128)(2,1)S(1)} %collective-permute-done.17.refs_3_) | copy-start | bytes 983044
  96.8 16.5 %copy-start.1 = (f32[4,256,1024]{2,1,0:T(8,128)S(1)}, f32[4,256,1024]{2,1,0:T(8,128)}, u32[]{:S(2)}) copy-start(f32[4,256,1024]{2,1,0:T(8,128)} %copy-done) | copy-start | bytes 12582916
  120.4 6.2 %copy-start.5 = (bf16[4,4,16,640]{3,2,1,0:T(8,128)(2,1)S(1)}, bf16[4,4,16,640]{3,2,1,0:T(8,128)(2,1)}, u32[]{:S(2)}) copy-start(bf16[4,4,16,640]{3,2,1,0:T(8,128)(2,1)} %copy-done.4) | copy-start | bytes 983044
  120.4 6.2 %copy-start.7 = (bf16[4,4,16,640]{3,2,1,0:T(8,128)(2,1)S(1)}, bf16[4,4,16,640]{3,2,1,0:T(8,128)(2,1)}, u32[]{:S(2)}) copy-start(bf16[4,4,16,640]{3,2,1,0:T(8,128)(2,1)} %copy-done.6) | copy-start | bytes 983044
  120.4 6.2 %copy-start.9 = (bf16[4,4,16,640]{3,2,1,0:T(8,128)(2,1)S(1)}, bf16[4,4,16,640]{3,2,1,0:T(8,128)(2,1)}, u32[]{:S(2)}) copy-start(bf16[4,4,16,640]{3,2,1,0:T(8,128)(2,1)} %copy-done.8) | copy-start | bytes 983044
  126.4 2.0 collective-permute-start.18
  136.9 25.3 %collective-permute-start.21 = (bf16[128,4096]{1,0:T(8,128)(2,1)S(1)}, bf16[128,4096]{1,0:T(8,128)(2,1)S(1)}, u32[]{:S(2)}, u32[]{:S(2)}) collective-permute-start(bf16[128,4096]{1,0:T(8,128)(2,1)S(1)} %get-tuple-element.103), channel_id=1, source_target_pairs={{0,2},{1,3},{2,0},{3,1},{4,6},{5,7},{6,4},{7,5},{8,10},{9,11},{10,... | collective-permute-start | bytes 3145736 | tf_op jit(solution)/shard_map/ppermute | solution.py:28
  148.6 2.0 collective-permute-start.20
  159.2 26.4 %collective-permute-start.24 = (bf16[128,4096]{1,0:T(8,128)(2,1)S(1)}, bf16[128,4096]{1,0:T(8,128)(2,1)S(1)}, u32[]{:S(2)}, u32[]{:S(2)}) collective-permute-start(bf16[128,4096]{1,0:T(8,128)(2,1)S(1)} %get-tuple-element.112), channel_id=1, source_target_pairs={{0,2},{1,3},{2,0},{3,1},{4,6},{5,7},{6,4},{7,5},{8,10},{9,11},{10,... | collective-permute-start | bytes 3145736 | tf_op jit(solution)/shard_map/ppermute | solution.py:28
  162.4 13.2 %collective-permute-start.23 = (bf16[2,32,4096]{2,1,0:T(8,128)(2,1)S(1)}, bf16[2,32,4096]{2,1,0:T(8,128)(2,1)S(1)}, u32[]{:S(2)}, u32[]{:S(2)}) collective-permute-start(bf16[2,32,4096]{2,1,0:T(8,128)(2,1)S(1)} %get-tuple-element.109), channel_id=1, source_target_pairs={{0,4},{1,5},{2,6},{3,7},{4,0},{5,1},{6,2},{7,3},{8,12},{9,13},{10,... | collective-permute-start | bytes 1572872 | tf_op jit(solution)/shard_map/ppermute | solution.py:28
  174.1 2.0 collective-permute-start.22
  184.7 27.3 %collective-permute-start.29 = (bf16[128,4096]{1,0:T(8,128)(2,1)S(1)}, bf16[128,4096]{1,0:T(8,128)(2,1)S(1)}, u32[]{:S(2)}, u32[]{:S(2)}) collective-permute-start(bf16[128,4096]{1,0:T(8,128)(2,1)S(1)} %get-tuple-element.123), channel_id=1, source_target_pairs={{0,2},{1,3},{2,0},{3,1},{4,6},{5,7},{6,4},{7,5},{8,10},{9,11},{10,... | collective-permute-start | bytes 3145736 | tf_op jit(solution)/shard_map/ppermute | solution.py:28
  185.8 13.8 %collective-permute-start.26 = (bf16[2,32,4096]{2,1,0:T(8,128)(2,1)S(1)}, bf16[2,32,4096]{2,1,0:T(8,128)(2,1)S(1)}, u32[]{:S(2)}, u32[]{:S(2)}) collective-permute-start(bf16[2,32,4096]{2,1,0:T(8,128)(2,1)S(1)} %get-tuple-element.116), channel_id=1, source_target_pairs={{0,4},{1,5},{2,6},{3,7},{4,0},{5,1},{6,2},{7,3},{8,12},{9,13},{10,... | collective-permute-start | bytes 1572872 | tf_op jit(solution)/shard_map/ppermute | solution.py:28
  196.6 3.1 %collective-permute-start.25 = (bf16[256,1024]{1,0:T(8,128)(2,1)S(1)}, bf16[256,1024]{1,0:T(8,128)(2,1)S(1)}, u32[]{:S(2)}, u32[]{:S(2)}) collective-permute-start(bf16[256,1024]{1,0:T(8,128)(2,1)S(1)} %fix.7.after_ref.own_ref), channel_id=1, source_target_pairs={{0,1},{1,0},{2,3},{3,2},{4,5},{5,4},{6,7},{7,6},{8,9},{9,8},{10,11... | collective-permute-start | bytes 1572872 | tf_op jit(solution)/shard_map/ppermute | solution.py:28
  196.7 15.2 %collective-permute-start.27 = (bf16[1,32,4096]{2,1,0:T(8,128)(2,1)S(1)}, bf16[1,32,4096]{2,1,0:T(8,128)(2,1)S(1)}, u32[]{:S(2)}, u32[]{:S(2)}) collective-permute-start(bf16[1,32,4096]{2,1,0:T(8,128)(2,1)S(1)} %get-tuple-element.120), channel_id=1, source_target_pairs={{0,8},{1,9},{2,10},{3,11},{4,12},{5,13},{6,14},{7,15},{8,0},{9,1},... | collective-permute-start | bytes 786440 | tf_op jit(solution)/shard_map/ppermute | solution.py:28
  204.5 17.5 %collective-permute-start.30 = (bf16[128,2048]{1,0:T(8,128)(2,1)S(1)}, bf16[128,2048]{1,0:T(8,128)(2,1)S(1)}, u32[]{:S(2)}, u32[]{:S(2)}) collective-permute-start(bf16[128,2048]{1,0:T(8,128)(2,1)S(1)} %get-tuple-element.125), channel_id=1, source_target_pairs={{0,2},{1,3},{2,0},{3,1},{4,6},{5,7},{6,4},{7,5},{8,10},{9,11},{10,... | collective-permute-start | bytes 1572872 | tf_op jit(solution)/shard_map/ppermute | solution.py:28
  212.2 20.5 %collective-permute-start.31 = (bf16[2,32,4096]{2,1,0:T(8,128)(2,1)S(1)}, bf16[2,32,4096]{2,1,0:T(8,128)(2,1)S(1)}, u32[]{:S(2)}, u32[]{:S(2)}) collective-permute-start(bf16[2,32,4096]{2,1,0:T(8,128)(2,1)S(1)} %get-tuple-element.127), channel_id=1, source_target_pairs={{0,4},{1,5},{2,6},{3,7},{4,0},{5,1},{6,2},{7,3},{8,12},{9,13},{10,... | collective-permute-start | bytes 1572872 | tf_op jit(solution)/shard_map/ppermute | solution.py:28
  213.1 19.8 %collective-permute-start.32 = (bf16[128,2048]{1,0:T(8,128)(2,1)S(1)}, bf16[128,2048]{1,0:T(8,128)(2,1)S(1)}, u32[]{:S(2)}, u32[]{:S(2)}) collective-permute-start(bf16[128,2048]{1,0:T(8,128)(2,1)S(1)} %get-tuple-element.129), channel_id=1, source_target_pairs={{0,2},{1,3},{2,0},{3,1},{4,6},{5,7},{6,4},{7,5},{8,10},{9,11},{10,... | collective-permute-start | bytes 1572872 | tf_op jit(solution)/shard_map/ppermute | solution.py:28
  214.2 22.6 %collective-permute-start.33 = (bf16[1,32,4096]{2,1,0:T(8,128)(2,1)S(1)}, bf16[1,32,4096]{2,1,0:T(8,128)(2,1)S(1)}, u32[]{:S(2)}, u32[]{:S(2)}) collective-permute-start(bf16[1,32,4096]{2,1,0:T(8,128)(2,1)S(1)} %get-tuple-element.131), channel_id=1, source_target_pairs={{0,8},{1,9},{2,10},{3,11},{4,12},{5,13},{6,14},{7,15},{8,0},{9,1},... | collective-permute-start | bytes 786440 | tf_op jit(solution)/shard_map/ppermute | solution.py:28
  222.1 23.3 %collective-permute-start.35 = (bf16[2,32,2048]{2,1,0:T(8,128)(2,1)S(1)}, bf16[2,32,2048]{2,1,0:T(8,128)(2,1)S(1)}, u32[]{:S(2)}, u32[]{:S(2)}) collective-permute-start(bf16[2,32,2048]{2,1,0:T(8,128)(2,1)S(1)} %get-tuple-element.134), channel_id=1, source_target_pairs={{0,4},{1,5},{2,6},{3,7},{4,0},{5,1},{6,2},{7,3},{8,12},{9,13},{10,... | collective-permute-start | bytes 786440 | tf_op jit(solution)/shard_map/ppermute | solution.py:28
  233.0 16.6 %collective-permute-start.36 = (bf16[2,32,2048]{2,1,0:T(8,128)(2,1)S(1)}, bf16[2,32,2048]{2,1,0:T(8,128)(2,1)S(1)}, u32[]{:S(2)}, u32[]{:S(2)}) collective-permute-start(bf16[2,32,2048]{2,1,0:T(8,128)(2,1)S(1)} %get-tuple-element.136), channel_id=1, source_target_pairs={{0,4},{1,5},{2,6},{3,7},{4,0},{5,1},{6,2},{7,3},{8,12},{9,13},{10,... | collective-permute-start | bytes 786440 | tf_op jit(solution)/shard_map/ppermute | solution.py:28
  234.6 15.8 %collective-permute-start.37 = (bf16[1,32,4096]{2,1,0:T(8,128)(2,1)S(1)}, bf16[1,32,4096]{2,1,0:T(8,128)(2,1)S(1)}, u32[]{:S(2)}, u32[]{:S(2)}) collective-permute-start(bf16[1,32,4096]{2,1,0:T(8,128)(2,1)S(1)} %get-tuple-element.138), channel_id=1, source_target_pairs={{0,8},{1,9},{2,10},{3,11},{4,12},{5,13},{6,14},{7,15},{8,0},{9,1},... | collective-permute-start | bytes 786440 | tf_op jit(solution)/shard_map/ppermute | solution.py:28
  245.5 12.7 %collective-permute-start.39 = (bf16[1,32,2048]{2,1,0:T(8,128)(2,1)S(1)}, bf16[1,32,2048]{2,1,0:T(8,128)(2,1)S(1)}, u32[]{:S(2)}, u32[]{:S(2)}) collective-permute-start(bf16[1,32,2048]{2,1,0:T(8,128)(2,1)S(1)} %get-tuple-element.141), channel_id=1, source_target_pairs={{0,8},{1,9},{2,10},{3,11},{4,12},{5,13},{6,14},{7,15},{8,0},{9,1},... | collective-permute-start | bytes 393224 | tf_op jit(solution)/shard_map/ppermute | solution.py:28
  249.7 10.0 %collective-permute-start.41 = (bf16[1,32,2048]{2,1,0:T(8,128)(2,1)S(1)}, bf16[1,32,2048]{2,1,0:T(8,128)(2,1)S(1)}, u32[]{:S(2)}, u32[]{:S(2)}) collective-permute-start(bf16[1,32,2048]{2,1,0:T(8,128)(2,1)S(1)} %get-tuple-element.144), channel_id=1, source_target_pairs={{0,8},{1,9},{2,10},{3,11},{4,12},{5,13},{6,14},{7,15},{8,0},{9,1},... | collective-permute-start | bytes 393224 | tf_op jit(solution)/shard_map/ppermute | solution.py:28
  249.8 10.0 %collective-permute-start.28 = (bf16[16,4096]{1,0:T(8,128)(2,1)S(1)}, bf16[16,4096]{1,0:T(8,128)(2,1)S(1)}, u32[]{:S(2)}, u32[]{:S(2)}) collective-permute-start(bf16[16,4096]{1,0:T(8,128)(2,1)S(1)} %get-tuple-element.122), channel_id=1, source_target_pairs={{0,1},{1,0},{2,3},{3,2},{4,5},{5,4},{6,7},{7,6},{8,9},{9,8},{10,11... | collective-permute-start | bytes 393224 | tf_op jit(solution)/shard_map/ppermute | solution.py:28
  249.9 9.9 %collective-permute-start.34 = (bf16[16,4096]{1,0:T(8,128)(2,1)S(1)}, bf16[16,4096]{1,0:T(8,128)(2,1)S(1)}, u32[]{:S(2)}, u32[]{:S(2)}) collective-permute-start(bf16[16,4096]{1,0:T(8,128)(2,1)S(1)} %get-tuple-element.133), channel_id=1, source_target_pairs={{0,1},{1,0},{2,3},{3,2},{4,5},{5,4},{6,7},{7,6},{8,9},{9,8},{10,11... | collective-permute-start | bytes 393224 | tf_op jit(solution)/shard_map/ppermute | solution.py:28
  250.5 9.4 %collective-permute-start.38 = (bf16[16,4096]{1,0:T(8,128)(2,1)S(1)}, bf16[16,4096]{1,0:T(8,128)(2,1)S(1)}, u32[]{:S(2)}, u32[]{:S(2)}) collective-permute-start(bf16[16,4096]{1,0:T(8,128)(2,1)S(1)} %get-tuple-element.140), channel_id=1, source_target_pairs={{0,1},{1,0},{2,3},{3,2},{4,5},{5,4},{6,7},{7,6},{8,9},{9,8},{10,11... | collective-permute-start | bytes 393224 | tf_op jit(solution)/shard_map/ppermute | solution.py:28
  258.2 1.6 collective-permute-start.40
  259.7 1.3 collective-permute-start.42
  (7 other events, 9.9 us)

commit v13 on v12

--- a/solution.py
+++ b/solution.py
@@ -791,12 +791,12 @@
         if t < STEPS - 1:
             last = reduce(t - 1, 0, last)
     last = reduce(t - 3, stages, last)
+    last = reduce(t - 2, stages, last)
     last = reduce(t - 1, 0, last)
     last = reduce(t, 0, last, 0)
     for stage in range(1, stages):
         last = reduce(t - 1, stage, last)
     last = reduce(t, 0, last, 1)
-    last = reduce(t - 2, stages, last)
     for part in range(2):
         for stage in range(1, stages):
             last = reduce(t, stage, last, part)

time: 265 us -> 272 us (1.026)
  waiting for transfers between devices: 91.4 us -> 95.2 us
  starting transfers between devices: 45.2 us -> 48.5 us
    ppermute x43, waiting for transfers between devices: 91.4 us -> 95.2 us  [swap(): return lax.ppermute(x, 'dex', [(i, i ^ mask) for i in range(n)])]
    ppermute x43, starting transfers between devices: 40.3 us -> 43.6 us  [swap(): return lax.ppermute(x, 'dex', [(i, i ^ mask) for i in range(n)])]
  transfers between devices with their start and end apart: 44 -> 44, of which waited for: 24 -> 24; matrix products, arithmetic and copies ran while one was open for 1% -> 1% of each run, Pallas kernels for 37% -> 36%
where the time goes in v13:
time: 272 us; the launch traced here: 270 us
  Pallas kernels  113 us (42%)
  waiting for transfers between devices  95.2 us (35%)
  starting transfers between devices  48.5 us (18%)
  local copies, waits for them, and re-layouts  11.2 us (4%)
    ppermute x43, waiting for transfers between devices, swap(): return lax.ppermute(x, 'dex', [(i, i ^ mask) for i in range(n)])  95.2 us
    pallas_call x4, Pallas kernels, state_step(): pl.pallas_call(functools.partial(state_kernel, t, len(after)), grid_spec=...  48.1 us
    ppermute x43, starting transfers between devices, swap(): return lax.ppermute(x, 'dex', [(i, i ^ mask) for i in range(n)])  43.6 us
    pallas_call x5, Pallas kernels, out_project(): pl.pallas_call(out_kernel, grid_spec=pltpu.PrefetchScalarGridSpec(num_sca...  35.3 us
    pallas_call x31, Pallas kernels, small(): pl.pallas_call(kernel, in_specs=[pl.BlockSpec(memory_space=pltpu.SMEM)] +...  14.2 us
    unnamed x54, local copies, waits for them, and re-layouts  10 us
    pallas_call x1, Pallas kernels, weight_half(): pl.pallas_call(half_kernel, grid_spec=pltpu.PrefetchScalarGridSpec(num_sc...  7.2 us
  transfers between devices with their start and end apart: 44, of which 24 were waited for; matrix products, arithmetic and copies ran while one was open for 1% of the time, Pallas kernels for 36%

profile of v13, /device:TPU:0, one launch (start us, length us, event | category | flops | bytes accessed | tf_op | source)
XLA Modules:
  0.0 270.4 jit_solution(5861625739201210854)
XLA Ops:
  0.0 1.2 copy-done.20
  1.3 3.0 %collective-permute-start = (bf16[4,16,768]{2,1,0:T(8,128)(2,1)S(1)}, bf16[4,16,768]{2,1,0:T(8,128)(2,1)S(1)}, u32[]{:S(2)}, u32[]{:S(2)}) collective-permute-start(bf16[4,16,768]{2,1,0:T(8,128)(2,1)S(1)} %get-tuple-element.77), channel_id=1, source_target_pairs={{0,2},{1,3},{2,0},{3,1},{4,6},{5,7},{6,4},{7,5},{8,10},{9,11},{10,... | collective-permute-start | bytes 294920 | tf_op jit(solution)/shard_map/ppermute | solution.py:28
  7.1 4.1 %collective-permute-done.3.refs_3_ = bf16[4,16,768]{2,1,0:T(8,128)(2,1)S(1)} collective-permute-done((bf16[4,16,768]{2,1,0:T(8,128)(2,1)S(1)}, bf16[4,16,768]{2,1,0:T(8,128)(2,1)S(1)}, u32[]{:S(2)}, u32[]{:S(2)}) %collective-permute-start.3) | collective-permute-done | bytes 98336 | tf_op jit(solution)/shard_map/ppermute | solution.py:28
  11.3 1.6 collective-permute-start.4
  12.9 2.6 collective-permute-start.5
  15.7 1.2 collective-permute-done.4.refs_0_.refs_1_
  16.9 2.2 copy-done.14
  19.1 2.1 pack_state.1.refs_4_.x_ref
  21.2 1.4 collective-permute-done.5.refs_2_
  22.7 3.8 %conv_project.1 = (f32[4,256,1024]{2,1,0:T(8,128)S(1)}, bf16[8,4,16,640]{3,2,1,0:T(8,128)(2,1)S(1)}, bf16[8,4,16,640]{3,2,1,0:T(8,128)(2,1)S(1)}) custom-call(s32[1]{0:T(128)} %bitcast.me_ref, s32[4,256]{1,0:T(4,128)S(1)} %broadcast_select_fusion.1.target_ref, f32[3,256,1024]{2,1,0:T(8,128)S(1)} %bitcast.38, bf16[4,256,1024]{2,1,0:T(8,128)(2,1)S(1)} %copy-done.16, ...), custom_call_target="tpu_custom_call" | custom-call | flops 1024 | bytes 1024 | tf_op jit(solution)/shard_map/conv_project/pallas_call | solution.py:212
  26.5 2.1 copy-done
  28.6 2.1 collective-permute-done.7.refs_1_
  31.4 9.2 %collective-permute-done.8.refs_1_ = bf16[4,4,16,640]{3,2,1,0:T(8,128)(2,1)S(1)} collective-permute-done((bf16[4,4,16,640]{3,2,1,0:T(8,128)(2,1)S(1)}, bf16[4,4,16,640]{3,2,1,0:T(8,128)(2,1)S(1)}, u32[]{:S(2)}, u32[]{:S(2)}) %collective-permute-start.8) | collective-permute-done | bytes 327712 | tf_op jit(solution)/shard_map/ppermute | solution.py:28
  40.8 1.7 collective-permute-start.9
  42.5 1.6 collective-permute-start.10
  44.1 1.2 collective-permute-start.11
  45.3 7.2 %weight_half.1.x_ref = bf16[1024,4096]{1,0:T(8,128)(2,1)} custom-call(s32[1]{0:T(128)} %bitcast.me_ref, bf16[4,4,16,640]{3,2,1,0:T(8,128)(2,1)} %copy-done.18, bf16[1024,8192]{1,0:T(8,128)(2,1)} %wown_ref.9), custom_call_target="tpu_custom_call" | custom-call | flops 1024 | bytes 1024 | tf_op jit(solution)/shard_map/weight_half/pallas_call | solution.py:147
  52.7 2.7 %collective-permute-start.14 = (bf16[4,16,640]{2,1,0:T(8,128)(2,1)S(1)}, bf16[4,16,640]{2,1,0:T(8,128)(2,1)S(1)}, u32[]{:S(2)}, u32[]{:S(2)}) collective-permute-start(bf16[4,16,640]{2,1,0:T(8,128)(2,1)S(1)} %norm.1.refs_0_.after_ref), channel_id=1, source_target_pairs={{0,12},{1,13},{2,14},{3,15},{4,8},{5,9},{6,10},{7,11},{8,4},{9,5},... | collective-permute-start | bytes 245768 | tf_op jit(solution)/shard_map/ppermute | solution.py:28
  55.4 1.7 collective-permute-start.12
  57.2 2.8 %collective-permute-done.14.refs_3_ = bf16[4,16,640]{2,1,0:T(8,128)(2,1)S(1)} collective-permute-done((bf16[4,16,640]{2,1,0:T(8,128)(2,1)S(1)}, bf16[4,16,640]{2,1,0:T(8,128)(2,1)S(1)}, u32[]{:S(2)}, u32[]{:S(2)}) %collective-permute-start.14) | collective-permute-done | bytes 81952 | tf_op jit(solution)/shard_map/ppermute | solution.py:28
  59.9 3.1 %collective-permute-done.13.refs_2_ = bf16[4,16,640]{2,1,0:T(8,128)(2,1)S(1)} collective-permute-done((bf16[4,16,640]{2,1,0:T(8,128)(2,1)S(1)}, bf16[4,16,640]{2,1,0:T(8,128)(2,1)S(1)}, u32[]{:S(2)}, u32[]{:S(2)}) %collective-permute-start.13) | collective-permute-done | bytes 81952 | tf_op jit(solution)/shard_map/ppermute | solution.py:28
  63.1 4.9 %all-to-all-start = ((bf16[16,64,1024]{2,1,0:T(8,128)(2,1)}), bf16[16,64,1024]{2,1,0:T(8,128)(2,1)}, u32[]{:S(2)}, u32[]{:S(2)}) async-start(bf16[16,64,1024]{2,1,0:T(8,128)(2,1)} %hold.2.after_ref.refs_0_), calls=%async_computation | async-start | bytes 4194304 | tf_op jit(solution)/shard_map/all_to_all | solution.py:723
  68.2 1.6 collective-permute-start.15
  70.9 23.7 %collective-permute-done.15.refs_1_ = bf16[4,4,16,640]{3,2,1,0:T(8,128)(2,1)S(1)} collective-permute-done((bf16[4,4,16,640]{3,2,1,0:T(8,128)(2,1)S(1)}, bf16[4,4,16,640]{3,2,1,0:T(8,128)(2,1)S(1)}, u32[]{:S(2)}, u32[]{:S(2)}) %collective-permute-start.15) | collective-permute-done | bytes 327712 | tf_op jit(solution)/shard_map/ppermute | solution.py:28
  94.6 1.6 collective-permute-done.17.refs_3_
  96.8 16.4 %state_step.4 = (bf16[16,256,1024]{2,1,0:T(8,128)(2,1)}, bf16[256,1024]{1,0:T(8,128)(2,1)S(1)}) custom-call(s32[1]{0:T(128)} %bitcast.me_ref, bf16[16,64,1024]{2,1,0:T(8,128)(2,1)} %hold.2.after_ref.refs_0_, f32[256,1024]{1,0:T(8,128)S(1)} %get-tuple-element.92.refs_1_, f32[256,128]{1,0:T(8,128)S(1)} %get-tuple-element.93.refs_2_, f32[4,256,1024]{2,1,0:T(8,128)} %copy-done, ...), custom_call_target="tpu_custom_call" | custom-call | flops 1024 | bytes 1024 | tf_op jit(solution)/shard_map/state_step/pallas_call | solution.py:447
  113.3 2.6 gather_live.1.live_ref
  115.9 1.1 copy-done.10
  117.1 0.8 copy-done.12
  117.9 1.4 copy-done.11
  119.3 1.0 copy-done.13
  120.4 5.7 %live_steps.1.after_ref.live_ref = bf16[4,32,1024]{2,1,0:T(8,128)(2,1)S(1)} custom-call(s32[2,32]{1,0:T(2,128)S(1)} %pad_add_fusion.slot_ref, bf16[256,1024]{1,0:T(8,128)(2,1)S(1)} %copy-done.13, bf16[16,64,1024]{2,1,0:T(8,128)(2,1)} %all-to-all-done.moved_ref, f32[4,32,3200]{2,1,0:T(8,128)S(1)} %copy-done.11, f32[16,1024]{1,0:T(8,128)S(1)} %copy-done.17, ...), custom_call_target="tpu_custom_call" | custom-call | flops 1024 | bytes 1024 | tf_op jit(solution)/shard_map/live_steps/pallas_call | solution.py:47
  127.2 1.1 collective-permute-done.18.other_ref
  128.3 8.5 %out_project.5 = (bf16[128,4096]{1,0:T(8,128)(2,1)S(1)}, bf16[128,4096]{1,0:T(8,128)(2,1)S(1)}) custom-call(s32[1]{0:T(128)} %bitcast.me_ref, bf16[256,1024]{1,0:T(8,128)(2,1)S(1)} %fix.4.after_ref.own_ref, bf16[256,1024]{1,0:T(8,128)(2,1)S(1)} %collective-permute-done.18.other_ref, bf16[1024,8192]{1,0:T(8,128)(2,1)} %wown_ref.9, ...), custom_call_target="tpu_custom_call" | custom-call | flops 1024 | bytes 1024 | tf_op jit(solution)/shard_map/out_project/pallas_call | solution.py:588
  137.0 11.4 %state_step.5 = (bf16[16,256,1024]{2,1,0:T(8,128)(2,1)}, bf16[256,1024]{1,0:T(8,128)(2,1)S(1)}) custom-call(s32[1]{0:T(128)} %bitcast.me_ref, bf16[128,4096]{1,0:T(8,128)(2,1)S(1)} %get-tuple-element.97.refs_0_, f32[256,1024]{1,0:T(8,128)S(1)} %get-tuple-element.98.refs_1_, f32[256,128]{1,0:T(8,128)S(1)} %get-tuple-element.96.refs_0_.refs_2_, ...), custom_call_target="tpu_custom_call" | custom-call | flops 1024 | bytes 1024 | tf_op jit(solution)/shard_map/state_step/pallas_call | solution.py:447
  149.5 1.2 collective-permute-done.20.other_ref
  150.6 8.5 %out_project.6 = (bf16[128,4096]{1,0:T(8,128)(2,1)S(1)}, bf16[128,4096]{1,0:T(8,128)(2,1)S(1)}) custom-call(s32[1]{0:T(128)} %bitcast.me_ref, bf16[256,1024]{1,0:T(8,128)(2,1)S(1)} %fix.5.after_ref.own_ref, bf16[256,1024]{1,0:T(8,128)(2,1)S(1)} %collective-permute-done.20.other_ref, bf16[1024,8192]{1,0:T(8,128)(2,1)} %wown_ref.9, ...), custom_call_target="tpu_custom_call" | custom-call | flops 1024 | bytes 1024 | tf_op jit(solution)/shard_map/out_project/pallas_call | solution.py:588
  159.2 2.1 collective-permute-start.24
  161.2 0.9 collective-permute-done.21
  162.5 11.4 %state_step.6 = (bf16[16,256,1024]{2,1,0:T(8,128)(2,1)}, bf16[256,1024]{1,0:T(8,128)(2,1)S(1)}) custom-call(s32[1]{0:T(128)} %bitcast.me_ref, bf16[2,32,4096]{2,1,0:T(8,128)(2,1)S(1)} %get-tuple-element.104.refs_0_.keep_ref, f32[256,1024]{1,0:T(8,128)S(1)} %get-tuple-element.105.refs_1_, f32[256,128]{1,0:T(8,128)S(1)} %get-tuple-element.101.refs_0_.refs_2_, ...), custom_call_target="tpu_custom_call" | custom-call | flops 1024 | bytes 1024 | tf_op jit(solution)/shard_map/state_step/pallas_call | solution.py:447
  174.8 0.7 collective-permute-done.23.got_ref
  176.1 8.5 %out_project.7 = (bf16[128,4096]{1,0:T(8,128)(2,1)S(1)}, bf16[128,4096]{1,0:T(8,128)(2,1)S(1)}) custom-call(s32[1]{0:T(128)} %bitcast.me_ref, bf16[256,1024]{1,0:T(8,128)(2,1)S(1)} %fix.6.after_ref.own_ref, bf16[256,1024]{1,0:T(8,128)(2,1)S(1)} %collective-permute-done.22.other_ref, bf16[1024,8192]{1,0:T(8,128)(2,1)} %wown_ref.9, ...), custom_call_target="tpu_custom_call" | custom-call | flops 1024 | bytes 1024 | tf_op jit(solution)/shard_map/out_project/pallas_call | solution.py:588
  184.7 0.8 collective-permute-start.31
  185.8 1.6 collective-permute-start.26
  187.3 9.0 %state_step.7.after_ref.gated_ref = bf16[256,1024]{1,0:T(8,128)(2,1)S(1)} custom-call(s32[1]{0:T(128)} %bitcast.me_ref, bf16[2,32,4096]{2,1,0:T(8,128)(2,1)S(1)} %get-tuple-element.113.refs_0_.keep_ref, f32[256,1024]{1,0:T(8,128)S(1)} %get-tuple-element.114.refs_1_, f32[256,128]{1,0:T(8,128)S(1)} %get-tuple-element.108.after_ref.refs_2_, ...), custom_call_target="tpu_custom_call" | custom-call | flops 1024 | bytes 1024 | tf_op jit(solution)/shard_map/state_step/pallas_call | solution.py:447
  196.7 2.1 collective-permute-start.27
  199.6 4.5 %collective-permute-start.29 = (bf16[1,32,4096]{2,1,0:T(8,128)(2,1)S(1)}, bf16[1,32,4096]{2,1,0:T(8,128)(2,1)S(1)}, u32[]{:S(2)}, u32[]{:S(2)}) collective-permute-start(bf16[1,32,4096]{2,1,0:T(8,128)(2,1)S(1)} %get-tuple-element.123), channel_id=1, source_target_pairs={{0,8},{1,9},{2,10},{3,11},{4,12},{5,13},{6,14},{7,15},{8,0},{9,1},... | collective-permute-start | bytes 786440 | tf_op jit(solution)/shard_map/ppermute | solution.py:28
  204.2 4.8 %out_project.8 = (bf16[128,2048]{1,0:T(8,128)(2,1)S(1)}, bf16[128,2048]{1,0:T(8,128)(2,1)S(1)}) custom-call(s32[1]{0:T(128)} %bitcast.me_ref, bf16[256,1024]{1,0:T(8,128)(2,1)S(1)} %fix.7.after_ref.own_ref, bf16[256,1024]{1,0:T(8,128)(2,1)S(1)} %collective-permute-done.25.other_ref, bf16[1024,8192]{1,0:T(8,128)(2,1)} %wown_ref.9, ...), custom_call_target="tpu_custom_call" | custom-call | flops 1024 | bytes 1024 | tf_op jit(solution)/shard_map/out_project/pallas_call | solution.py:588
  209.0 1.8 collective-permute-start.32
  210.8 4.9 %out_project.9 = (bf16[128,2048]{1,0:T(8,128)(2,1)S(1)}, bf16[128,2048]{1,0:T(8,128)(2,1)S(1)}) custom-call(s32[1]{0:T(128)} %bitcast.me_ref, bf16[256,1024]{1,0:T(8,128)(2,1)S(1)} %fix.7.after_ref.own_ref, bf16[256,1024]{1,0:T(8,128)(2,1)S(1)} %collective-permute-done.25.other_ref, bf16[1024,8192]{1,0:T(8,128)(2,1)} %wown_ref.9, ...), custom_call_target="tpu_custom_call" | custom-call | flops 1024 | bytes 1024 | tf_op jit(solution)/shard_map/out_project/pallas_call | solution.py:588
  215.6 2.3 collective-permute-done.27.got_ref
  218.0 5.1 %collective-permute-done.29.got_ref = bf16[1,32,4096]{2,1,0:T(8,128)(2,1)S(1)} collective-permute-done((bf16[1,32,4096]{2,1,0:T(8,128)(2,1)S(1)}, bf16[1,32,4096]{2,1,0:T(8,128)(2,1)S(1)}, u32[]{:S(2)}, u32[]{:S(2)}) %collective-permute-start.29) | collective-permute-done | bytes 262176 | tf_op jit(solution)/shard_map/ppermute | solution.py:28
  223.7 1.7 collective-permute-start.34
  225.6 1.9 collective-permute-start.35
  227.5 10.9 %collective-permute-done.33.got_ref = bf16[2,32,4096]{2,1,0:T(8,128)(2,1)S(1)} collective-permute-done((bf16[2,32,4096]{2,1,0:T(8,128)(2,1)S(1)}, bf16[2,32,4096]{2,1,0:T(8,128)(2,1)S(1)}, u32[]{:S(2)}, u32[]{:S(2)}) %collective-permute-start.33) | collective-permute-done | bytes 524320 | tf_op jit(solution)/shard_map/ppermute | solution.py:28
  239.0 3.2 %collective-permute-start.37 = (bf16[1,32,4096]{2,1,0:T(8,128)(2,1)S(1)}, bf16[1,32,4096]{2,1,0:T(8,128)(2,1)S(1)}, u32[]{:S(2)}, u32[]{:S(2)}) collective-permute-start(bf16[1,32,4096]{2,1,0:T(8,128)(2,1)S(1)} %get-tuple-element.138), channel_id=1, source_target_pairs={{0,8},{1,9},{2,10},{3,11},{4,12},{5,13},{6,14},{7,15},{8,0},{9,1},... | collective-permute-start | bytes 786440 | tf_op jit(solution)/shard_map/ppermute | solution.py:28
  242.2 7.4 %collective-permute-done.35.got_ref = bf16[2,32,2048]{2,1,0:T(8,128)(2,1)S(1)} collective-permute-done((bf16[2,32,2048]{2,1,0:T(8,128)(2,1)S(1)}, bf16[2,32,2048]{2,1,0:T(8,128)(2,1)S(1)}, u32[]{:S(2)}, u32[]{:S(2)}) %collective-permute-start.35) | collective-permute-done | bytes 262176 | tf_op jit(solution)/shard_map/ppermute | solution.py:28
  249.7 1.0 collective-permute-start.39
  250.7 3.3 %collective-permute-done.36.got_ref = bf16[2,32,2048]{2,1,0:T(8,128)(2,1)S(1)} collective-permute-done((bf16[2,32,2048]{2,1,0:T(8,128)(2,1)S(1)}, bf16[2,32,2048]{2,1,0:T(8,128)(2,1)S(1)}, u32[]{:S(2)}, u32[]{:S(2)}) %collective-permute-start.36) | collective-permute-done | bytes 262176 | tf_op jit(solution)/shard_map/ppermute | solution.py:28
  254.0 1.5 collective-permute-start.41
  256.2 7.8 %collective-permute-done.39.got_ref = bf16[1,32,2048]{2,1,0:T(8,128)(2,1)S(1)} collective-permute-done((bf16[1,32,2048]{2,1,0:T(8,128)(2,1)S(1)}, bf16[1,32,2048]{2,1,0:T(8,128)(2,1)S(1)}, u32[]{:S(2)}, u32[]{:S(2)}) %collective-permute-start.39) | collective-permute-done | bytes 131104 | tf_op jit(solution)/shard_map/ppermute | solution.py:28
  264.1 2.6 collective-permute-done.41.got_ref
  266.9 1.2 collective-permute-done.42.refs_9_
  268.1 2.3 final_join.1
  (143 shorter events, 14.1 us)
Async XLA Ops:
  0.0 22.6 %copy-start.19 = (bf16[1024,544]{0,1:T(8,128)(2,1)S(1)}, bf16[1024,544]{0,1:T(8,128)(2,1)}, u32[]{:S(2)}) copy-start(bf16[1024,544]{0,1:T(8,128)(2,1)} %param.27) | copy-start | bytes 3342340
  1.2 21.4 %copy-start.23 = (f32[4,1024]{1,0:T(4,128)S(1)}, f32[4,1024]{1,0:T(4,128)}, u32[]{:S(2)}) copy-start(f32[4,1024]{1,0:T(4,128)} %w_ref.2) | copy-start | bytes 49156
  1.2 21.4 %copy-start.24 = (f32[1024]{0:T(1024)S(1)}, f32[1024]{0:T(1024)}, u32[]{:S(2)}) copy-start(f32[1024]{0:T(1024)} %param.26) | copy-start | bytes 12292
  1.3 5.8 %collective-permute-start = (bf16[4,16,768]{2,1,0:T(8,128)(2,1)S(1)}, bf16[4,16,768]{2,1,0:T(8,128)(2,1)S(1)}, u32[]{:S(2)}, u32[]{:S(2)}) collective-permute-start(bf16[4,16,768]{2,1,0:T(8,128)(2,1)S(1)} %get-tuple-element.77), channel_id=1, source_target_pairs={{0,2},{1,3},{2,0},{3,1},{4,6},{5,7},{6,4},{7,5},{8,10},{9,11},{10,... | collective-permute-start | bytes 294920 | tf_op jit(solution)/shard_map/ppermute | solution.py:28
  4.3 2.8 %collective-permute-start.1 = (bf16[4,16,768]{2,1,0:T(8,128)(2,1)S(1)}, bf16[4,16,768]{2,1,0:T(8,128)(2,1)S(1)}, u32[]{:S(2)}, u32[]{:S(2)}) collective-permute-start(bf16[4,16,768]{2,1,0:T(8,128)(2,1)S(1)} %get-tuple-element.78), channel_id=1, source_target_pairs={{0,1},{1,0},{2,3},{3,2},{4,5},{5,4},{6,7},{7,6},{8,9},{9,8},{10,11... | collective-permute-start | bytes 294920 | tf_op jit(solution)/shard_map/ppermute | solution.py:28
  4.3 2.1 collective-permute-start.2
  6.5 4.8 %collective-permute-start.3 = (bf16[4,16,768]{2,1,0:T(8,128)(2,1)S(1)}, bf16[4,16,768]{2,1,0:T(8,128)(2,1)S(1)}, u32[]{:S(2)}, u32[]{:S(2)}) collective-permute-start(bf16[4,16,768]{2,1,0:T(8,128)(2,1)S(1)} %collective-permute-done.2), channel_id=1, source_target_pairs={{0,2},{1,3},{2,0},{3,1},{4,6},{5,7},{6,4},{7,5},{8,10},{9,11},{10,... | collective-permute-start | bytes 294920 | tf_op jit(solution)/shard_map/ppermute | solution.py:28
  11.3 5.7 %collective-permute-start.4 = (bf16[4,16,768]{2,1,0:T(8,128)(2,1)S(1)}, bf16[4,16,768]{2,1,0:T(8,128)(2,1)S(1)}, u32[]{:S(2)}, u32[]{:S(2)}) collective-permute-start(bf16[4,16,768]{2,1,0:T(8,128)(2,1)S(1)} %get-tuple-element.80), channel_id=1, source_target_pairs={{0,4},{1,5},{2,6},{3,7},{4,0},{5,1},{6,2},{7,3},{8,12},{9,13},{10,... | collective-permute-start | bytes 294920 | tf_op jit(solution)/shard_map/ppermute | solution.py:28
  12.9 9.7 %collective-permute-start.5 = (bf16[4,16,768]{2,1,0:T(8,128)(2,1)S(1)}, bf16[4,16,768]{2,1,0:T(8,128)(2,1)S(1)}, u32[]{:S(2)}, u32[]{:S(2)}) collective-permute-start(bf16[4,16,768]{2,1,0:T(8,128)(2,1)S(1)} %get-tuple-element.82), channel_id=1, source_target_pairs={{0,8},{1,9},{2,10},{3,11},{4,12},{5,13},{6,14},{7,15},{8,0},{9,1},... | collective-permute-start | bytes 294920 | tf_op jit(solution)/shard_map/ppermute | solution.py:28
  15.5 7.1 %collective-permute-start.6 = (bf16[4,16,768]{2,1,0:T(8,128)(2,1)S(1)}, bf16[4,16,768]{2,1,0:T(8,128)(2,1)S(1)}, u32[]{:S(2)}, u32[]{:S(2)}) collective-permute-start(bf16[4,16,768]{2,1,0:T(8,128)(2,1)S(1)} %get-tuple-element.83), channel_id=1, source_target_pairs={{0,12},{1,13},{2,14},{3,15},{4,8},{5,9},{6,10},{7,11},{8,4},{9,5},... | collective-permute-start | bytes 294920 | tf_op jit(solution)/shard_map/ppermute | solution.py:28
  19.1 3.5 %copy-start.15 = (f32[256,3,1024]{2,0,1:T(8,128)S(1)}, f32[256,3,1024]{2,0,1:T(8,128)}, u32[]{:S(2)}) copy-start(f32[256,3,1024]{2,0,1:T(8,128)} %param.18) | copy-start | bytes 9437188
  19.1 3.6 %copy-start.16 = (bf16[4,256,1024]{2,1,0:T(8,128)(2,1)S(1)}, bf16[4,256,1024]{2,1,0:T(8,128)(2,1)}, u32[]{:S(2)}) copy-start(bf16[4,256,1024]{2,1,0:T(8,128)(2,1)} %x_ref.3) | copy-start | bytes 6291460
  22.7 22.6 %copy-start.25 = (f32[544]{0:T(1024)S(1)}, f32[544]{0:T(1024)}, u32[]{:S(2)}) copy-start(f32[544]{0:T(1024)} %param.28) | copy-start | bytes 6532
  28.6 2.1 collective-permute-start.7
  30.9 14.4 %copy-start.18 = (bf16[4,4,16,640]{3,2,1,0:T(8,128)(2,1)}, bf16[4,4,16,640]{3,2,1,0:T(8,128)(2,1)S(1)}, u32[]{:S(2)}) copy-start(bf16[4,4,16,640]{3,2,1,0:T(8,128)(2,1)S(1)} %get-tuple-element.86.refs_0_.after_ref) | copy-start | bytes 983044
  30.9 9.8 %collective-permute-start.8 = (bf16[4,4,16,640]{3,2,1,0:T(8,128)(2,1)S(1)}, bf16[4,4,16,640]{3,2,1,0:T(8,128)(2,1)S(1)}, u32[]{:S(2)}, u32[]{:S(2)}) collective-permute-start(bf16[4,4,16,640]{3,2,1,0:T(8,128)(2,1)S(1)} %get-tuple-element.87), channel_id=1, source_target_pairs={{0,2},{1,3},{2,0},{3,1},{4,6},{5,7},{6,4},{7,5},{8,10},{9,11},{10,... | collective-permute-start | bytes 983048 | tf_op jit(solution)/shard_map/ppermute | solution.py:28
  40.8 11.7 %collective-permute-start.9 = (bf16[4,16,640]{2,1,0:T(8,128)(2,1)S(1)}, bf16[4,16,640]{2,1,0:T(8,128)(2,1)S(1)}, u32[]{:S(2)}, u32[]{:S(2)}) collective-permute-start(bf16[4,16,640]{2,1,0:T(8,128)(2,1)S(1)} %get-tuple-element.89), channel_id=1, source_target_pairs={{0,4},{1,5},{2,6},{3,7},{4,0},{5,1},{6,2},{7,3},{8,12},{9,13},{10,... | collective-permute-start | bytes 245768 | tf_op jit(solution)/shard_map/ppermute | solution.py:28
  42.5 10.0 %collective-permute-start.10 = (bf16[4,16,640]{2,1,0:T(8,128)(2,1)S(1)}, bf16[4,16,640]{2,1,0:T(8,128)(2,1)S(1)}, u32[]{:S(2)}, u32[]{:S(2)}) collective-permute-start(bf16[4,16,640]{2,1,0:T(8,128)(2,1)S(1)} %get-tuple-element.90), channel_id=1, source_target_pairs={{0,8},{1,9},{2,10},{3,11},{4,12},{5,13},{6,14},{7,15},{8,0},{9,1},... | collective-permute-start | bytes 245768 | tf_op jit(solution)/shard_map/ppermute | solution.py:28
  44.1 8.4 %collective-permute-start.11 = (bf16[4,16,640]{2,1,0:T(8,128)(2,1)S(1)}, bf16[4,16,640]{2,1,0:T(8,128)(2,1)S(1)}, u32[]{:S(2)}, u32[]{:S(2)}) collective-permute-start(bf16[4,16,640]{2,1,0:T(8,128)(2,1)S(1)} %get-tuple-element.91), channel_id=1, source_target_pairs={{0,12},{1,13},{2,14},{3,15},{4,8},{5,9},{6,10},{7,11},{8,4},{9,5},... | collective-permute-start | bytes 245768 | tf_op jit(solution)/shard_map/ppermute | solution.py:28
  52.6 75.7 %collective-permute-start.19 = (bf16[1024,4096]{1,0:T(8,128)(2,1)}, bf16[1024,4096]{1,0:T(8,128)(2,1)}, u32[]{:S(2)}, u32[]{:S(2)}) collective-permute-start(bf16[1024,4096]{1,0:T(8,128)(2,1)} %hold.3), channel_id=1, source_target_pairs={{0,1},{1,0},{2,3},{3,2},{4,5},{5,4},{6,7},{7,6},{8,9},{9,8},{10,11... | collective-permute-start | bytes 25165832 | tf_op jit(solution)/shard_map/ppermute | solution.py:28
  52.7 7.2 %collective-permute-start.14 = (bf16[4,16,640]{2,1,0:T(8,128)(2,1)S(1)}, bf16[4,16,640]{2,1,0:T(8,128)(2,1)S(1)}, u32[]{:S(2)}, u32[]{:S(2)}) collective-permute-start(bf16[4,16,640]{2,1,0:T(8,128)(2,1)S(1)} %norm.1.refs_0_.after_ref), channel_id=1, source_target_pairs={{0,12},{1,13},{2,14},{3,15},{4,8},{5,9},{6,10},{7,11},{8,4},{9,5},... | collective-permute-start | bytes 245768 | tf_op jit(solution)/shard_map/ppermute | solution.py:28
  55.4 7.6 %collective-permute-start.13 = (bf16[4,16,640]{2,1,0:T(8,128)(2,1)S(1)}, bf16[4,16,640]{2,1,0:T(8,128)(2,1)S(1)}, u32[]{:S(2)}, u32[]{:S(2)}) collective-permute-start(bf16[4,16,640]{2,1,0:T(8,128)(2,1)S(1)} %norm.1.refs_0_.after_ref), channel_id=1, source_target_pairs={{0,8},{1,9},{2,10},{3,11},{4,12},{5,13},{6,14},{7,15},{8,0},{9,1},... | collective-permute-start | bytes 245768 | tf_op jit(solution)/shard_map/ppermute | solution.py:28
  55.4 7.6 %collective-permute-start.12 = (bf16[4,16,640]{2,1,0:T(8,128)(2,1)S(1)}, bf16[4,16,640]{2,1,0:T(8,128)(2,1)S(1)}, u32[]{:S(2)}, u32[]{:S(2)}) collective-permute-start(bf16[4,16,640]{2,1,0:T(8,128)(2,1)S(1)} %norm.1.refs_0_.after_ref), channel_id=1, source_target_pairs={{0,4},{1,5},{2,6},{3,7},{4,0},{5,1},{6,2},{7,3},{8,12},{9,13},{10,... | collective-permute-start | bytes 245768 | tf_op jit(solution)/shard_map/ppermute | solution.py:28
  63.0 5.0 %copy-start.26 = (s32[16]{0:T(128)S(1)}, s32[16]{0:T(128)}, u32[]{:S(2)}) copy-start(s32[16]{0:T(128)} %param.21) | copy-start | bytes 196
  63.0 33.1 %copy-start.3 = (bf16[512,1024]{1,0:T(8,128)(2,1)S(1)}, bf16[512,1024]{1,0:T(8,128)(2,1)}, u32[]{:S(2)}) copy-start(bf16[512,1024]{1,0:T(8,128)(2,1)} %refs_4_.14) | copy-start | bytes 3145732
  63.0 33.1 %copy-start.21 = (f32[1024]{0:T(1024)S(1)}, f32[1024]{0:T(1024)}, u32[]{:S(2)}) copy-start(f32[1024]{0:T(1024)} %param.30) | copy-start | bytes 12292
  63.1 33.7 %copy-start.2 = (bf16[4,256,1024]{2,1,0:T(8,128)(2,1)S(1)}, bf16[4,256,1024]{2,1,0:T(8,128)(2,1)}, u32[]{:S(2)}) copy-start(bf16[4,256,1024]{2,1,0:T(8,128)(2,1)} %refs_4_.15) | copy-start | bytes 6291460
  63.1 33.7 %copy-start.17 = (f32[16,1024]{1,0:T(8,128)S(1)}, f32[16,1024]{1,0:T(8,128)}, u32[]{:S(2)}) copy-start(f32[16,1024]{1,0:T(8,128)} %refs_5_.9) | copy-start | bytes 196612
  63.1 33.7 %copy-start.22 = (f32[1024]{0:T(1024)S(1)}, f32[1024]{0:T(1024)}, u32[]{:S(2)}) copy-start(f32[1024]{0:T(1024)} %param.32) | copy-start | bytes 12292
  63.1 54.8 %all-to-all-start = ((bf16[16,64,1024]{2,1,0:T(8,128)(2,1)}), bf16[16,64,1024]{2,1,0:T(8,128)(2,1)}, u32[]{:S(2)}, u32[]{:S(2)}) async-start(bf16[16,64,1024]{2,1,0:T(8,128)(2,1)} %hold.2.after_ref.refs_0_), calls=%async_computation | async-start | bytes 4194304 | tf_op jit(solution)/shard_map/all_to_all | solution.py:723
  68.2 26.3 %collective-permute-start.15 = (bf16[4,4,16,640]{3,2,1,0:T(8,128)(2,1)S(1)}, bf16[4,4,16,640]{3,2,1,0:T(8,128)(2,1)S(1)}, u32[]{:S(2)}, u32[]{:S(2)}) collective-permute-start(bf16[4,4,16,640]{3,2,1,0:T(8,128)(2,1)S(1)} %merge_z.1.after_ref.refs_0_), channel_id=1, source_target_pairs={{0,2},{1,3},{2,0},{3,1},{4,6},{5,7},{6,4},{7,5},{8,10},{9,11},{10,... | collective-permute-start | bytes 983048 | tf_op jit(solution)/shard_map/ppermute | solution.py:28
  70.8 23.8 %collective-permute-start.16 = (bf16[4,4,16,640]{3,2,1,0:T(8,128)(2,1)S(1)}, bf16[4,4,16,640]{3,2,1,0:T(8,128)(2,1)S(1)}, u32[]{:S(2)}, u32[]{:S(2)}) collective-permute-start(bf16[4,4,16,640]{3,2,1,0:T(8,128)(2,1)S(1)} %merge_z.1.after_ref.refs_0_), channel_id=1, source_target_pairs={{0,1},{1,0},{2,3},{3,2},{4,5},{5,4},{6,7},{7,6},{8,9},{9,8},{10,11... | collective-permute-start | bytes 983048 | tf_op jit(solution)/shard_map/ppermute | solution.py:28
  94.5 18.8 %copy-start.4 = (bf16[4,4,16,640]{3,2,1,0:T(8,128)(2,1)}, bf16[4,4,16,640]{3,2,1,0:T(8,128)(2,1)S(1)}, u32[]{:S(2)}) copy-start(bf16[4,4,16,640]{3,2,1,0:T(8,128)(2,1)S(1)} %collective-permute-done.15.refs_1_) | copy-start | bytes 983044
  94.5 1.6 collective-permute-start.17
  94.6 18.7 %copy-start.6 = (bf16[4,4,16,640]{3,2,1,0:T(8,128)(2,1)}, bf16[4,4,16,640]{3,2,1,0:T(8,128)(2,1)S(1)}, u32[]{:S(2)}) copy-start(bf16[4,4,16,640]{3,2,1,0:T(8,128)(2,1)S(1)} %collective-permute-done.16.refs_2_) | copy-start | bytes 983044
  96.2 17.2 %copy-start.8 = (bf16[4,4,16,640]{3,2,1,0:T(8,128)(2,1)}, bf16[4,4,16,640]{3,2,1,0:T(8,128)(2,1)S(1)}, u32[]{:S(2)}) copy-start(bf16[4,4,16,640]{3,2,1,0:T(8,128)(2,1)S(1)} %collective-permute-done.17.refs_3_) | copy-start | bytes 983044
  96.8 16.5 %copy-start.1 = (f32[4,256,1024]{2,1,0:T(8,128)S(1)}, f32[4,256,1024]{2,1,0:T(8,128)}, u32[]{:S(2)}) copy-start(f32[4,256,1024]{2,1,0:T(8,128)} %copy-done) | copy-start | bytes 12582916
  120.4 6.2 %copy-start.5 = (bf16[4,4,16,640]{3,2,1,0:T(8,128)(2,1)S(1)}, bf16[4,4,16,640]{3,2,1,0:T(8,128)(2,1)}, u32[]{:S(2)}) copy-start(bf16[4,4,16,640]{3,2,1,0:T(8,128)(2,1)} %copy-done.4) | copy-start | bytes 983044
  120.4 6.2 %copy-start.7 = (bf16[4,4,16,640]{3,2,1,0:T(8,128)(2,1)S(1)}, bf16[4,4,16,640]{3,2,1,0:T(8,128)(2,1)}, u32[]{:S(2)}) copy-start(bf16[4,4,16,640]{3,2,1,0:T(8,128)(2,1)} %copy-done.6) | copy-start | bytes 983044
  120.4 6.2 %copy-start.9 = (bf16[4,4,16,640]{3,2,1,0:T(8,128)(2,1)S(1)}, bf16[4,4,16,640]{3,2,1,0:T(8,128)(2,1)}, u32[]{:S(2)}) copy-start(bf16[4,4,16,640]{3,2,1,0:T(8,128)(2,1)} %copy-done.8) | copy-start | bytes 983044
  126.4 2.0 collective-permute-start.18
  136.9 25.3 %collective-permute-start.21 = (bf16[128,4096]{1,0:T(8,128)(2,1)S(1)}, bf16[128,4096]{1,0:T(8,128)(2,1)S(1)}, u32[]{:S(2)}, u32[]{:S(2)}) collective-permute-start(bf16[128,4096]{1,0:T(8,128)(2,1)S(1)} %get-tuple-element.103), channel_id=1, source_target_pairs={{0,2},{1,3},{2,0},{3,1},{4,6},{5,7},{6,4},{7,5},{8,10},{9,11},{10,... | collective-permute-start | bytes 3145736 | tf_op jit(solution)/shard_map/ppermute | solution.py:28
  148.6 2.0 collective-permute-start.20
  159.2 26.4 %collective-permute-start.24 = (bf16[128,4096]{1,0:T(8,128)(2,1)S(1)}, bf16[128,4096]{1,0:T(8,128)(2,1)S(1)}, u32[]{:S(2)}, u32[]{:S(2)}) collective-permute-start(bf16[128,4096]{1,0:T(8,128)(2,1)S(1)} %get-tuple-element.112), channel_id=1, source_target_pairs={{0,2},{1,3},{2,0},{3,1},{4,6},{5,7},{6,4},{7,5},{8,10},{9,11},{10,... | collective-permute-start | bytes 3145736 | tf_op jit(solution)/shard_map/ppermute | solution.py:28
  162.4 13.2 %collective-permute-start.23 = (bf16[2,32,4096]{2,1,0:T(8,128)(2,1)S(1)}, bf16[2,32,4096]{2,1,0:T(8,128)(2,1)S(1)}, u32[]{:S(2)}, u32[]{:S(2)}) collective-permute-start(bf16[2,32,4096]{2,1,0:T(8,128)(2,1)S(1)} %get-tuple-element.109), channel_id=1, source_target_pairs={{0,4},{1,5},{2,6},{3,7},{4,0},{5,1},{6,2},{7,3},{8,12},{9,13},{10,... | collective-permute-start | bytes 1572872 | tf_op jit(solution)/shard_map/ppermute | solution.py:28
  174.1 2.0 collective-permute-start.22
  184.7 38.6 %collective-permute-start.31 = (bf16[128,4096]{1,0:T(8,128)(2,1)S(1)}, bf16[128,4096]{1,0:T(8,128)(2,1)S(1)}, u32[]{:S(2)}, u32[]{:S(2)}) collective-permute-start(bf16[128,4096]{1,0:T(8,128)(2,1)S(1)} %get-tuple-element.126), channel_id=1, source_target_pairs={{0,2},{1,3},{2,0},{3,1},{4,6},{5,7},{6,4},{7,5},{8,10},{9,11},{10,... | collective-permute-start | bytes 3145736 | tf_op jit(solution)/shard_map/ppermute | solution.py:28
  185.8 13.8 %collective-permute-start.26 = (bf16[2,32,4096]{2,1,0:T(8,128)(2,1)S(1)}, bf16[2,32,4096]{2,1,0:T(8,128)(2,1)S(1)}, u32[]{:S(2)}, u32[]{:S(2)}) collective-permute-start(bf16[2,32,4096]{2,1,0:T(8,128)(2,1)S(1)} %get-tuple-element.116), channel_id=1, source_target_pairs={{0,4},{1,5},{2,6},{3,7},{4,0},{5,1},{6,2},{7,3},{8,12},{9,13},{10,... | collective-permute-start | bytes 1572872 | tf_op jit(solution)/shard_map/ppermute | solution.py:28
  196.6 7.6 %collective-permute-start.25 = (bf16[256,1024]{1,0:T(8,128)(2,1)S(1)}, bf16[256,1024]{1,0:T(8,128)(2,1)S(1)}, u32[]{:S(2)}, u32[]{:S(2)}) collective-permute-start(bf16[256,1024]{1,0:T(8,128)(2,1)S(1)} %fix.7.after_ref.own_ref), channel_id=1, source_target_pairs={{0,1},{1,0},{2,3},{3,2},{4,5},{5,4},{6,7},{7,6},{8,9},{9,8},{10,11... | collective-permute-start | bytes 1572872 | tf_op jit(solution)/shard_map/ppermute | solution.py:28
  196.7 21.3 %collective-permute-start.27 = (bf16[1,32,4096]{2,1,0:T(8,128)(2,1)S(1)}, bf16[1,32,4096]{2,1,0:T(8,128)(2,1)S(1)}, u32[]{:S(2)}, u32[]{:S(2)}) collective-permute-start(bf16[1,32,4096]{2,1,0:T(8,128)(2,1)S(1)} %get-tuple-element.120), channel_id=1, source_target_pairs={{0,8},{1,9},{2,10},{3,11},{4,12},{5,13},{6,14},{7,15},{8,0},{9,1},... | collective-permute-start | bytes 786440 | tf_op jit(solution)/shard_map/ppermute | solution.py:28
  199.6 23.5 %collective-permute-start.29 = (bf16[1,32,4096]{2,1,0:T(8,128)(2,1)S(1)}, bf16[1,32,4096]{2,1,0:T(8,128)(2,1)S(1)}, u32[]{:S(2)}, u32[]{:S(2)}) collective-permute-start(bf16[1,32,4096]{2,1,0:T(8,128)(2,1)S(1)} %get-tuple-element.123), channel_id=1, source_target_pairs={{0,8},{1,9},{2,10},{3,11},{4,12},{5,13},{6,14},{7,15},{8,0},{9,1},... | collective-permute-start | bytes 786440 | tf_op jit(solution)/shard_map/ppermute | solution.py:28
  209.0 16.4 %collective-permute-start.32 = (bf16[128,2048]{1,0:T(8,128)(2,1)S(1)}, bf16[128,2048]{1,0:T(8,128)(2,1)S(1)}, u32[]{:S(2)}, u32[]{:S(2)}) collective-permute-start(bf16[128,2048]{1,0:T(8,128)(2,1)S(1)} %get-tuple-element.128), channel_id=1, source_target_pairs={{0,2},{1,3},{2,0},{3,1},{4,6},{5,7},{6,4},{7,5},{8,10},{9,11},{10,... | collective-permute-start | bytes 1572872 | tf_op jit(solution)/shard_map/ppermute | solution.py:28
  223.5 14.9 %collective-permute-start.33 = (bf16[2,32,4096]{2,1,0:T(8,128)(2,1)S(1)}, bf16[2,32,4096]{2,1,0:T(8,128)(2,1)S(1)}, u32[]{:S(2)}, u32[]{:S(2)}) collective-permute-start(bf16[2,32,4096]{2,1,0:T(8,128)(2,1)S(1)} %get-tuple-element.130), channel_id=1, source_target_pairs={{0,4},{1,5},{2,6},{3,7},{4,0},{5,1},{6,2},{7,3},{8,12},{9,13},{10,... | collective-permute-start | bytes 1572872 | tf_op jit(solution)/shard_map/ppermute | solution.py:28
  223.7 14.8 %collective-permute-start.34 = (bf16[128,2048]{1,0:T(8,128)(2,1)S(1)}, bf16[128,2048]{1,0:T(8,128)(2,1)S(1)}, u32[]{:S(2)}, u32[]{:S(2)}) collective-permute-start(bf16[128,2048]{1,0:T(8,128)(2,1)S(1)} %get-tuple-element.132), channel_id=1, source_target_pairs={{0,2},{1,3},{2,0},{3,1},{4,6},{5,7},{6,4},{7,5},{8,10},{9,11},{10,... | collective-permute-start | bytes 1572872 | tf_op jit(solution)/shard_map/ppermute | solution.py:28
  225.6 24.1 %collective-permute-start.35 = (bf16[2,32,2048]{2,1,0:T(8,128)(2,1)S(1)}, bf16[2,32,2048]{2,1,0:T(8,128)(2,1)S(1)}, u32[]{:S(2)}, u32[]{:S(2)}) collective-permute-start(bf16[2,32,2048]{2,1,0:T(8,128)(2,1)S(1)} %get-tuple-element.134), channel_id=1, source_target_pairs={{0,4},{1,5},{2,6},{3,7},{4,0},{5,1},{6,2},{7,3},{8,12},{9,13},{10,... | collective-permute-start | bytes 786440 | tf_op jit(solution)/shard_map/ppermute | solution.py:28
  238.6 15.3 %collective-permute-start.36 = (bf16[2,32,2048]{2,1,0:T(8,128)(2,1)S(1)}, bf16[2,32,2048]{2,1,0:T(8,128)(2,1)S(1)}, u32[]{:S(2)}, u32[]{:S(2)}) collective-permute-start(bf16[2,32,2048]{2,1,0:T(8,128)(2,1)S(1)} %get-tuple-element.136), channel_id=1, source_target_pairs={{0,4},{1,5},{2,6},{3,7},{4,0},{5,1},{6,2},{7,3},{8,12},{9,13},{10,... | collective-permute-start | bytes 786440 | tf_op jit(solution)/shard_map/ppermute | solution.py:28
  239.0 17.1 %collective-permute-start.37 = (bf16[1,32,4096]{2,1,0:T(8,128)(2,1)S(1)}, bf16[1,32,4096]{2,1,0:T(8,128)(2,1)S(1)}, u32[]{:S(2)}, u32[]{:S(2)}) collective-permute-start(bf16[1,32,4096]{2,1,0:T(8,128)(2,1)S(1)} %get-tuple-element.138), channel_id=1, source_target_pairs={{0,8},{1,9},{2,10},{3,11},{4,12},{5,13},{6,14},{7,15},{8,0},{9,1},... | collective-permute-start | bytes 786440 | tf_op jit(solution)/shard_map/ppermute | solution.py:28
  249.7 14.3 %collective-permute-start.39 = (bf16[1,32,2048]{2,1,0:T(8,128)(2,1)S(1)}, bf16[1,32,2048]{2,1,0:T(8,128)(2,1)S(1)}, u32[]{:S(2)}, u32[]{:S(2)}) collective-permute-start(bf16[1,32,2048]{2,1,0:T(8,128)(2,1)S(1)} %get-tuple-element.141), channel_id=1, source_target_pairs={{0,8},{1,9},{2,10},{3,11},{4,12},{5,13},{6,14},{7,15},{8,0},{9,1},... | collective-permute-start | bytes 393224 | tf_op jit(solution)/shard_map/ppermute | solution.py:28
  254.0 12.7 %collective-permute-start.41 = (bf16[1,32,2048]{2,1,0:T(8,128)(2,1)S(1)}, bf16[1,32,2048]{2,1,0:T(8,128)(2,1)S(1)}, u32[]{:S(2)}, u32[]{:S(2)}) collective-permute-start(bf16[1,32,2048]{2,1,0:T(8,128)(2,1)S(1)} %get-tuple-element.144), channel_id=1, source_target_pairs={{0,8},{1,9},{2,10},{3,11},{4,12},{5,13},{6,14},{7,15},{8,0},{9,1},... | collective-permute-start | bytes 393224 | tf_op jit(solution)/shard_map/ppermute | solution.py:28
  255.5 11.3 %collective-permute-start.28 = (bf16[16,4096]{1,0:T(8,128)(2,1)S(1)}, bf16[16,4096]{1,0:T(8,128)(2,1)S(1)}, u32[]{:S(2)}, u32[]{:S(2)}) collective-permute-start(bf16[16,4096]{1,0:T(8,128)(2,1)S(1)} %get-tuple-element.122), channel_id=1, source_target_pairs={{0,1},{1,0},{2,3},{3,2},{4,5},{5,4},{6,7},{7,6},{8,9},{9,8},{10,11... | collective-permute-start | bytes 393224 | tf_op jit(solution)/shard_map/ppermute | solution.py:28
  255.5 11.3 %collective-permute-start.30 = (bf16[16,4096]{1,0:T(8,128)(2,1)S(1)}, bf16[16,4096]{1,0:T(8,128)(2,1)S(1)}, u32[]{:S(2)}, u32[]{:S(2)}) collective-permute-start(bf16[16,4096]{1,0:T(8,128)(2,1)S(1)} %get-tuple-element.125), channel_id=1, source_target_pairs={{0,1},{1,0},{2,3},{3,2},{4,5},{5,4},{6,7},{7,6},{8,9},{9,8},{10,11... | collective-permute-start | bytes 393224 | tf_op jit(solution)/shard_map/ppermute | solution.py:28
  256.1 10.7 %collective-permute-start.38 = (bf16[16,4096]{1,0:T(8,128)(2,1)S(1)}, bf16[16,4096]{1,0:T(8,128)(2,1)S(1)}, u32[]{:S(2)}, u32[]{:S(2)}) collective-permute-start(bf16[16,4096]{1,0:T(8,128)(2,1)S(1)} %get-tuple-element.140), channel_id=1, source_target_pairs={{0,1},{1,0},{2,3},{3,2},{4,5},{5,4},{6,7},{7,6},{8,9},{9,8},{10,11... | collective-permute-start | bytes 393224 | tf_op jit(solution)/shard_map/ppermute | solution.py:28
  264.1 2.8 %collective-permute-start.40 = (bf16[16,2048]{1,0:T(8,128)(2,1)S(1)}, bf16[16,2048]{1,0:T(8,128)(2,1)S(1)}, u32[]{:S(2)}, u32[]{:S(2)}) collective-permute-start(bf16[16,2048]{1,0:T(8,128)(2,1)S(1)} %get-tuple-element.143), channel_id=1, source_target_pairs={{0,1},{1,0},{2,3},{3,2},{4,5},{5,4},{6,7},{7,6},{8,9},{9,8},{10,11... | collective-permute-start | bytes 196616 | tf_op jit(solution)/shard_map/ppermute | solution.py:28
  266.8 1.3 collective-permute-start.42
  (7 other events, 9.9 us)

commit v14 on v12

--- a/solution.py
+++ b/solution.py
@@ -378,7 +378,7 @@
         for copy in fetch(block, now):
             copy.wait()
 
-    tall, lanes = 16, min(256, c)
+    tall, lanes = 16, min(512, c)
     for r in range(0, take, tall):
         tail = tail_ref[pl.ds(pl.multiple_of(base + r, tall), tall), :]
         for s in range(2 * STATE):

time: 265 us -> 265 us (level)
  no operation moved by 1% of the time
where the time goes in v14:
time: 265 us; the launch traced here: 263 us
  Pallas kernels  113 us (43%)
  waiting for transfers between devices  91.4 us (34%)
  starting transfers between devices  45.2 us (17%)
  local copies, waits for them, and re-layouts  11.3 us (4%)
    ppermute x43, waiting for transfers between devices, swap(): return lax.ppermute(x, 'dex', [(i, i ^ mask) for i in range(n)])  91.4 us
    pallas_call x4, Pallas kernels, state_step(): pl.pallas_call(functools.partial(state_kernel, t, len(after)), grid_spec=...  48.2 us
    ppermute x43, starting transfers between devices, swap(): return lax.ppermute(x, 'dex', [(i, i ^ mask) for i in range(n)])  40.3 us
    pallas_call x5, Pallas kernels, out_project(): pl.pallas_call(out_kernel, grid_spec=pltpu.PrefetchScalarGridSpec(num_sca...  35.3 us
    pallas_call x31, Pallas kernels, small(): pl.pallas_call(kernel, in_specs=[pl.BlockSpec(memory_space=pltpu.SMEM)] +...  14.2 us
    unnamed x54, local copies, waits for them, and re-layouts  10 us
    pallas_call x1, Pallas kernels, weight_half(): pl.pallas_call(half_kernel, grid_spec=pltpu.PrefetchScalarGridSpec(num_sc...  7.2 us
  transfers between devices with their start and end apart: 44, of which 24 were waited for; matrix products, arithmetic and copies ran while one was open for 1% of the time, Pallas kernels for 37%

profile of v14, /device:TPU:0, one launch (start us, length us, event | category | flops | bytes accessed | tf_op | source)
XLA Modules:
  0.0 263.4 jit_solution(828612797184411867)
XLA Ops:
  0.0 1.2 copy-done.20
  1.3 3.0 %collective-permute-start = (bf16[4,16,768]{2,1,0:T(8,128)(2,1)S(1)}, bf16[4,16,768]{2,1,0:T(8,128)(2,1)S(1)}, u32[]{:S(2)}, u32[]{:S(2)}) collective-permute-start(bf16[4,16,768]{2,1,0:T(8,128)(2,1)S(1)} %get-tuple-element.77), channel_id=1, source_target_pairs={{0,2},{1,3},{2,0},{3,1},{4,6},{5,7},{6,4},{7,5},{8,10},{9,11},{10,... | collective-permute-start | bytes 294920 | tf_op jit(solution)/shard_map/ppermute | solution.py:28
  5.6 0.7 broadcast_select_fusion
  7.1 4.1 %collective-permute-done.3.refs_3_ = bf16[4,16,768]{2,1,0:T(8,128)(2,1)S(1)} collective-permute-done((bf16[4,16,768]{2,1,0:T(8,128)(2,1)S(1)}, bf16[4,16,768]{2,1,0:T(8,128)(2,1)S(1)}, u32[]{:S(2)}, u32[]{:S(2)}) %collective-permute-start.3) | collective-permute-done | bytes 98336 | tf_op jit(solution)/shard_map/ppermute | solution.py:28
  11.3 1.6 collective-permute-start.4
  12.9 2.6 collective-permute-start.5
  15.7 1.2 collective-permute-done.4.refs_0_.refs_1_
  16.9 2.2 copy-done.14
  19.1 2.1 pack_state.1.refs_4_.x_ref
  21.2 1.4 collective-permute-done.5.refs_2_
  22.7 3.8 %conv_project.1 = (f32[4,256,1024]{2,1,0:T(8,128)S(1)}, bf16[8,4,16,640]{3,2,1,0:T(8,128)(2,1)S(1)}, bf16[8,4,16,640]{3,2,1,0:T(8,128)(2,1)S(1)}) custom-call(s32[1]{0:T(128)} %bitcast.me_ref, s32[4,256]{1,0:T(4,128)S(1)} %broadcast_select_fusion.1.target_ref, f32[3,256,1024]{2,1,0:T(8,128)S(1)} %bitcast.38, bf16[4,256,1024]{2,1,0:T(8,128)(2,1)S(1)} %copy-done.16, ...), custom_call_target="tpu_custom_call" | custom-call | flops 1024 | bytes 1024 | tf_op jit(solution)/shard_map/conv_project/pallas_call | solution.py:212
  26.5 2.1 copy-done
  28.6 2.1 collective-permute-done.7.refs_1_
  31.4 9.2 %collective-permute-done.8.refs_1_ = bf16[4,4,16,640]{3,2,1,0:T(8,128)(2,1)S(1)} collective-permute-done((bf16[4,4,16,640]{3,2,1,0:T(8,128)(2,1)S(1)}, bf16[4,4,16,640]{3,2,1,0:T(8,128)(2,1)S(1)}, u32[]{:S(2)}, u32[]{:S(2)}) %collective-permute-start.8) | collective-permute-done | bytes 327712 | tf_op jit(solution)/shard_map/ppermute | solution.py:28
  40.8 1.7 collective-permute-start.9
  42.5 1.6 collective-permute-start.10
  44.1 1.2 collective-permute-start.11
  45.3 7.2 %weight_half.1.x_ref = bf16[1024,4096]{1,0:T(8,128)(2,1)} custom-call(s32[1]{0:T(128)} %bitcast.me_ref, bf16[4,4,16,640]{3,2,1,0:T(8,128)(2,1)} %copy-done.18, bf16[1024,8192]{1,0:T(8,128)(2,1)} %wown_ref.9), custom_call_target="tpu_custom_call" | custom-call | flops 1024 | bytes 1024 | tf_op jit(solution)/shard_map/weight_half/pallas_call | solution.py:147
  52.7 2.7 %collective-permute-start.14 = (bf16[4,16,640]{2,1,0:T(8,128)(2,1)S(1)}, bf16[4,16,640]{2,1,0:T(8,128)(2,1)S(1)}, u32[]{:S(2)}, u32[]{:S(2)}) collective-permute-start(bf16[4,16,640]{2,1,0:T(8,128)(2,1)S(1)} %norm.1.refs_0_.after_ref), channel_id=1, source_target_pairs={{0,12},{1,13},{2,14},{3,15},{4,8},{5,9},{6,10},{7,11},{8,4},{9,5},... | collective-permute-start | bytes 245768 | tf_op jit(solution)/shard_map/ppermute | solution.py:28
  55.4 1.7 collective-permute-start.12
  57.2 2.8 %collective-permute-done.14.refs_3_ = bf16[4,16,640]{2,1,0:T(8,128)(2,1)S(1)} collective-permute-done((bf16[4,16,640]{2,1,0:T(8,128)(2,1)S(1)}, bf16[4,16,640]{2,1,0:T(8,128)(2,1)S(1)}, u32[]{:S(2)}, u32[]{:S(2)}) %collective-permute-start.14) | collective-permute-done | bytes 81952 | tf_op jit(solution)/shard_map/ppermute | solution.py:28
  59.9 3.1 %collective-permute-done.13.refs_2_ = bf16[4,16,640]{2,1,0:T(8,128)(2,1)S(1)} collective-permute-done((bf16[4,16,640]{2,1,0:T(8,128)(2,1)S(1)}, bf16[4,16,640]{2,1,0:T(8,128)(2,1)S(1)}, u32[]{:S(2)}, u32[]{:S(2)}) %collective-permute-start.13) | collective-permute-done | bytes 81952 | tf_op jit(solution)/shard_map/ppermute | solution.py:28
  63.1 4.9 %all-to-all-start = ((bf16[16,64,1024]{2,1,0:T(8,128)(2,1)}), bf16[16,64,1024]{2,1,0:T(8,128)(2,1)}, u32[]{:S(2)}, u32[]{:S(2)}) async-start(bf16[16,64,1024]{2,1,0:T(8,128)(2,1)} %hold.2.after_ref.refs_0_), calls=%async_computation | async-start | bytes 4194304 | tf_op jit(solution)/shard_map/all_to_all | solution.py:723
  68.2 1.6 collective-permute-start.15
  70.9 23.7 %collective-permute-done.15.refs_1_ = bf16[4,4,16,640]{3,2,1,0:T(8,128)(2,1)S(1)} collective-permute-done((bf16[4,4,16,640]{3,2,1,0:T(8,128)(2,1)S(1)}, bf16[4,4,16,640]{3,2,1,0:T(8,128)(2,1)S(1)}, u32[]{:S(2)}, u32[]{:S(2)}) %collective-permute-start.15) | collective-permute-done | bytes 327712 | tf_op jit(solution)/shard_map/ppermute | solution.py:28
  94.6 1.6 collective-permute-done.17.refs_3_
  96.8 16.4 %state_step.4 = (bf16[16,256,1024]{2,1,0:T(8,128)(2,1)}, bf16[256,1024]{1,0:T(8,128)(2,1)S(1)}) custom-call(s32[1]{0:T(128)} %bitcast.me_ref, bf16[16,64,1024]{2,1,0:T(8,128)(2,1)} %hold.2.after_ref.refs_0_, f32[256,1024]{1,0:T(8,128)S(1)} %get-tuple-element.92.refs_1_, f32[256,128]{1,0:T(8,128)S(1)} %get-tuple-element.93.refs_2_, f32[4,256,1024]{2,1,0:T(8,128)} %copy-done, ...), custom_call_target="tpu_custom_call" | custom-call | flops 1024 | bytes 1024 | tf_op jit(solution)/shard_map/state_step/pallas_call | solution.py:447
  113.3 2.6 gather_live.1.live_ref
  115.9 1.1 copy-done.10
  117.1 0.8 copy-done.12
  117.9 1.4 copy-done.11
  119.3 1.0 copy-done.13
  120.4 5.7 %live_steps.1.after_ref.live_ref = bf16[4,32,1024]{2,1,0:T(8,128)(2,1)S(1)} custom-call(s32[2,32]{1,0:T(2,128)S(1)} %pad_add_fusion.slot_ref, bf16[256,1024]{1,0:T(8,128)(2,1)S(1)} %copy-done.13, bf16[16,64,1024]{2,1,0:T(8,128)(2,1)} %all-to-all-done.moved_ref, f32[4,32,3200]{2,1,0:T(8,128)S(1)} %copy-done.11, f32[16,1024]{1,0:T(8,128)S(1)} %copy-done.17, ...), custom_call_target="tpu_custom_call" | custom-call | flops 1024 | bytes 1024 | tf_op jit(solution)/shard_map/live_steps/pallas_call | solution.py:47
  127.2 1.1 collective-permute-done.18.other_ref
  128.3 8.5 %out_project.5 = (bf16[128,4096]{1,0:T(8,128)(2,1)S(1)}, bf16[128,4096]{1,0:T(8,128)(2,1)S(1)}) custom-call(s32[1]{0:T(128)} %bitcast.me_ref, bf16[256,1024]{1,0:T(8,128)(2,1)S(1)} %fix.4.after_ref.own_ref, bf16[256,1024]{1,0:T(8,128)(2,1)S(1)} %collective-permute-done.18.other_ref, bf16[1024,8192]{1,0:T(8,128)(2,1)} %wown_ref.9, ...), custom_call_target="tpu_custom_call" | custom-call | flops 1024 | bytes 1024 | tf_op jit(solution)/shard_map/out_project/pallas_call | solution.py:588
  137.0 11.4 %state_step.5 = (bf16[16,256,1024]{2,1,0:T(8,128)(2,1)}, bf16[256,1024]{1,0:T(8,128)(2,1)S(1)}) custom-call(s32[1]{0:T(128)} %bitcast.me_ref, bf16[128,4096]{1,0:T(8,128)(2,1)S(1)} %get-tuple-element.97.refs_0_, f32[256,1024]{1,0:T(8,128)S(1)} %get-tuple-element.98.refs_1_, f32[256,128]{1,0:T(8,128)S(1)} %get-tuple-element.96.refs_0_.refs_2_, ...), custom_call_target="tpu_custom_call" | custom-call | flops 1024 | bytes 1024 | tf_op jit(solution)/shard_map/state_step/pallas_call | solution.py:447
  149.5 1.2 collective-permute-done.20.other_ref
  150.6 8.5 %out_project.6 = (bf16[128,4096]{1,0:T(8,128)(2,1)S(1)}, bf16[128,4096]{1,0:T(8,128)(2,1)S(1)}) custom-call(s32[1]{0:T(128)} %bitcast.me_ref, bf16[256,1024]{1,0:T(8,128)(2,1)S(1)} %fix.5.after_ref.own_ref, bf16[256,1024]{1,0:T(8,128)(2,1)S(1)} %collective-permute-done.20.other_ref, bf16[1024,8192]{1,0:T(8,128)(2,1)} %wown_ref.9, ...), custom_call_target="tpu_custom_call" | custom-call | flops 1024 | bytes 1024 | tf_op jit(solution)/shard_map/out_project/pallas_call | solution.py:588
  159.2 2.1 collective-permute-start.24
  161.2 0.9 collective-permute-done.21
  162.5 11.4 %state_step.6 = (bf16[16,256,1024]{2,1,0:T(8,128)(2,1)}, bf16[256,1024]{1,0:T(8,128)(2,1)S(1)}) custom-call(s32[1]{0:T(128)} %bitcast.me_ref, bf16[2,32,4096]{2,1,0:T(8,128)(2,1)S(1)} %get-tuple-element.104.refs_0_.keep_ref, f32[256,1024]{1,0:T(8,128)S(1)} %get-tuple-element.105.refs_1_, f32[256,128]{1,0:T(8,128)S(1)} %get-tuple-element.101.refs_0_.refs_2_, ...), custom_call_target="tpu_custom_call" | custom-call | flops 1024 | bytes 1024 | tf_op jit(solution)/shard_map/state_step/pallas_call | solution.py:447
  176.1 8.5 %out_project.7 = (bf16[128,4096]{1,0:T(8,128)(2,1)S(1)}, bf16[128,4096]{1,0:T(8,128)(2,1)S(1)}) custom-call(s32[1]{0:T(128)} %bitcast.me_ref, bf16[256,1024]{1,0:T(8,128)(2,1)S(1)} %fix.6.after_ref.own_ref, bf16[256,1024]{1,0:T(8,128)(2,1)S(1)} %collective-permute-done.22.other_ref, bf16[1024,8192]{1,0:T(8,128)(2,1)} %wown_ref.9, ...), custom_call_target="tpu_custom_call" | custom-call | flops 1024 | bytes 1024 | tf_op jit(solution)/shard_map/out_project/pallas_call | solution.py:588
  184.7 0.8 collective-permute-start.29
  185.8 1.6 collective-permute-start.26
  187.3 9.0 %state_step.7.after_ref.gated_ref = bf16[256,1024]{1,0:T(8,128)(2,1)S(1)} custom-call(s32[1]{0:T(128)} %bitcast.me_ref, bf16[2,32,4096]{2,1,0:T(8,128)(2,1)S(1)} %get-tuple-element.113.refs_0_.keep_ref, f32[256,1024]{1,0:T(8,128)S(1)} %get-tuple-element.114.refs_1_, f32[256,128]{1,0:T(8,128)S(1)} %get-tuple-element.108.after_ref.refs_2_, ...), custom_call_target="tpu_custom_call" | custom-call | flops 1024 | bytes 1024 | tf_op jit(solution)/shard_map/state_step/pallas_call | solution.py:447
  196.7 2.1 collective-permute-start.27
  199.6 4.8 %out_project.8 = (bf16[128,2048]{1,0:T(8,128)(2,1)S(1)}, bf16[128,2048]{1,0:T(8,128)(2,1)S(1)}) custom-call(s32[1]{0:T(128)} %bitcast.me_ref, bf16[256,1024]{1,0:T(8,128)(2,1)S(1)} %fix.7.after_ref.own_ref, bf16[256,1024]{1,0:T(8,128)(2,1)S(1)} %collective-permute-done.25.other_ref, bf16[1024,8192]{1,0:T(8,128)(2,1)} %wown_ref.9, ...), custom_call_target="tpu_custom_call" | custom-call | flops 1024 | bytes 1024 | tf_op jit(solution)/shard_map/out_project/pallas_call | solution.py:588
  204.5 1.6 collective-permute-start.30
  206.1 4.8 %out_project.9 = (bf16[128,2048]{1,0:T(8,128)(2,1)S(1)}, bf16[128,2048]{1,0:T(8,128)(2,1)S(1)}) custom-call(s32[1]{0:T(128)} %bitcast.me_ref, bf16[256,1024]{1,0:T(8,128)(2,1)S(1)} %fix.7.after_ref.own_ref, bf16[256,1024]{1,0:T(8,128)(2,1)S(1)} %collective-permute-done.25.other_ref, bf16[1024,8192]{1,0:T(8,128)(2,1)} %wown_ref.9, ...), custom_call_target="tpu_custom_call" | custom-call | flops 1024 | bytes 1024 | tf_op jit(solution)/shard_map/out_project/pallas_call | solution.py:588
  210.9 1.0 collective-permute-done.27.got_ref
  212.3 0.8 collective-permute-start.31
  213.1 1.1 collective-permute-start.32
  214.2 3.4 %collective-permute-start.33 = (bf16[1,32,4096]{2,1,0:T(8,128)(2,1)S(1)}, bf16[1,32,4096]{2,1,0:T(8,128)(2,1)S(1)}, u32[]{:S(2)}, u32[]{:S(2)}) collective-permute-start(bf16[1,32,4096]{2,1,0:T(8,128)(2,1)S(1)} %get-tuple-element.131), channel_id=1, source_target_pairs={{0,8},{1,9},{2,10},{3,11},{4,12},{5,13},{6,14},{7,15},{8,0},{9,1},... | collective-permute-start | bytes 786440 | tf_op jit(solution)/shard_map/ppermute | solution.py:28
  217.6 4.4 %collective-permute-done.30 = bf16[128,2048]{1,0:T(8,128)(2,1)S(1)} collective-permute-done((bf16[128,2048]{1,0:T(8,128)(2,1)S(1)}, bf16[128,2048]{1,0:T(8,128)(2,1)S(1)}, u32[]{:S(2)}, u32[]{:S(2)}) %collective-permute-start.30) | collective-permute-done | bytes 524320 | tf_op jit(solution)/shard_map/ppermute | solution.py:28
  222.1 2.1 collective-permute-start.35
  224.2 8.6 %collective-permute-done.31.got_ref = bf16[2,32,4096]{2,1,0:T(8,128)(2,1)S(1)} collective-permute-done((bf16[2,32,4096]{2,1,0:T(8,128)(2,1)S(1)}, bf16[2,32,4096]{2,1,0:T(8,128)(2,1)S(1)}, u32[]{:S(2)}, u32[]{:S(2)}) %collective-permute-start.31) | collective-permute-done | bytes 524320 | tf_op jit(solution)/shard_map/ppermute | solution.py:28
  233.0 1.5 collective-permute-start.36
  234.6 2.2 collective-permute-start.37
  236.9 8.6 %collective-permute-done.35.got_ref = bf16[2,32,2048]{2,1,0:T(8,128)(2,1)S(1)} collective-permute-done((bf16[2,32,2048]{2,1,0:T(8,128)(2,1)S(1)}, bf16[2,32,2048]{2,1,0:T(8,128)(2,1)S(1)}, u32[]{:S(2)}, u32[]{:S(2)}) %collective-permute-start.35) | collective-permute-done | bytes 262176 | tf_op jit(solution)/shard_map/ppermute | solution.py:28
  245.6 4.1 %collective-permute-done.36.got_ref = bf16[2,32,2048]{2,1,0:T(8,128)(2,1)S(1)} collective-permute-done((bf16[2,32,2048]{2,1,0:T(8,128)(2,1)S(1)}, bf16[2,32,2048]{2,1,0:T(8,128)(2,1)S(1)}, u32[]{:S(2)}, u32[]{:S(2)}) %collective-permute-start.36) | collective-permute-done | bytes 262176 | tf_op jit(solution)/shard_map/ppermute | solution.py:28
  250.6 7.6 %collective-permute-done.39.got_ref = bf16[1,32,2048]{2,1,0:T(8,128)(2,1)S(1)} collective-permute-done((bf16[1,32,2048]{2,1,0:T(8,128)(2,1)S(1)}, bf16[1,32,2048]{2,1,0:T(8,128)(2,1)S(1)}, u32[]{:S(2)}, u32[]{:S(2)}) %collective-permute-start.39) | collective-permute-done | bytes 131104 | tf_op jit(solution)/shard_map/ppermute | solution.py:28
  258.3 1.4 collective-permute-done.41.got_ref
  259.9 1.2 collective-permute-done.42.refs_9_
  261.1 2.3 final_join.1
  (143 shorter events, 13.9 us)
Async XLA Ops:
  0.0 22.6 %copy-start.19 = (bf16[1024,544]{0,1:T(8,128)(2,1)S(1)}, bf16[1024,544]{0,1:T(8,128)(2,1)}, u32[]{:S(2)}) copy-start(bf16[1024,544]{0,1:T(8,128)(2,1)} %param.27) | copy-start | bytes 3342340
  1.2 21.4 %copy-start.23 = (f32[4,1024]{1,0:T(4,128)S(1)}, f32[4,1024]{1,0:T(4,128)}, u32[]{:S(2)}) copy-start(f32[4,1024]{1,0:T(4,128)} %w_ref.2) | copy-start | bytes 49156
  1.2 21.4 %copy-start.24 = (f32[1024]{0:T(1024)S(1)}, f32[1024]{0:T(1024)}, u32[]{:S(2)}) copy-start(f32[1024]{0:T(1024)} %param.26) | copy-start | bytes 12292
  1.3 5.8 %collective-permute-start = (bf16[4,16,768]{2,1,0:T(8,128)(2,1)S(1)}, bf16[4,16,768]{2,1,0:T(8,128)(2,1)S(1)}, u32[]{:S(2)}, u32[]{:S(2)}) collective-permute-start(bf16[4,16,768]{2,1,0:T(8,128)(2,1)S(1)} %get-tuple-element.77), channel_id=1, source_target_pairs={{0,2},{1,3},{2,0},{3,1},{4,6},{5,7},{6,4},{7,5},{8,10},{9,11},{10,... | collective-permute-start | bytes 294920 | tf_op jit(solution)/shard_map/ppermute | solution.py:28
  4.3 2.8 %collective-permute-start.1 = (bf16[4,16,768]{2,1,0:T(8,128)(2,1)S(1)}, bf16[4,16,768]{2,1,0:T(8,128)(2,1)S(1)}, u32[]{:S(2)}, u32[]{:S(2)}) collective-permute-start(bf16[4,16,768]{2,1,0:T(8,128)(2,1)S(1)} %get-tuple-element.78), channel_id=1, source_target_pairs={{0,1},{1,0},{2,3},{3,2},{4,5},{5,4},{6,7},{7,6},{8,9},{9,8},{10,11... | collective-permute-start | bytes 294920 | tf_op jit(solution)/shard_map/ppermute | solution.py:28
  4.3 2.1 collective-permute-start.2
  6.5 4.8 %collective-permute-start.3 = (bf16[4,16,768]{2,1,0:T(8,128)(2,1)S(1)}, bf16[4,16,768]{2,1,0:T(8,128)(2,1)S(1)}, u32[]{:S(2)}, u32[]{:S(2)}) collective-permute-start(bf16[4,16,768]{2,1,0:T(8,128)(2,1)S(1)} %collective-permute-done.2), channel_id=1, source_target_pairs={{0,2},{1,3},{2,0},{3,1},{4,6},{5,7},{6,4},{7,5},{8,10},{9,11},{10,... | collective-permute-start | bytes 294920 | tf_op jit(solution)/shard_map/ppermute | solution.py:28
  11.3 5.7 %collective-permute-start.4 = (bf16[4,16,768]{2,1,0:T(8,128)(2,1)S(1)}, bf16[4,16,768]{2,1,0:T(8,128)(2,1)S(1)}, u32[]{:S(2)}, u32[]{:S(2)}) collective-permute-start(bf16[4,16,768]{2,1,0:T(8,128)(2,1)S(1)} %get-tuple-element.80), channel_id=1, source_target_pairs={{0,4},{1,5},{2,6},{3,7},{4,0},{5,1},{6,2},{7,3},{8,12},{9,13},{10,... | collective-permute-start | bytes 294920 | tf_op jit(solution)/shard_map/ppermute | solution.py:28
  12.9 9.7 %collective-permute-start.5 = (bf16[4,16,768]{2,1,0:T(8,128)(2,1)S(1)}, bf16[4,16,768]{2,1,0:T(8,128)(2,1)S(1)}, u32[]{:S(2)}, u32[]{:S(2)}) collective-permute-start(bf16[4,16,768]{2,1,0:T(8,128)(2,1)S(1)} %get-tuple-element.82), channel_id=1, source_target_pairs={{0,8},{1,9},{2,10},{3,11},{4,12},{5,13},{6,14},{7,15},{8,0},{9,1},... | collective-permute-start | bytes 294920 | tf_op jit(solution)/shard_map/ppermute | solution.py:28
  15.5 7.1 %collective-permute-start.6 = (bf16[4,16,768]{2,1,0:T(8,128)(2,1)S(1)}, bf16[4,16,768]{2,1,0:T(8,128)(2,1)S(1)}, u32[]{:S(2)}, u32[]{:S(2)}) collective-permute-start(bf16[4,16,768]{2,1,0:T(8,128)(2,1)S(1)} %get-tuple-element.83), channel_id=1, source_target_pairs={{0,12},{1,13},{2,14},{3,15},{4,8},{5,9},{6,10},{7,11},{8,4},{9,5},... | collective-permute-start | bytes 294920 | tf_op jit(solution)/shard_map/ppermute | solution.py:28
  19.1 3.5 %copy-start.15 = (f32[256,3,1024]{2,0,1:T(8,128)S(1)}, f32[256,3,1024]{2,0,1:T(8,128)}, u32[]{:S(2)}) copy-start(f32[256,3,1024]{2,0,1:T(8,128)} %param.18) | copy-start | bytes 9437188
  19.1 3.6 %copy-start.16 = (bf16[4,256,1024]{2,1,0:T(8,128)(2,1)S(1)}, bf16[4,256,1024]{2,1,0:T(8,128)(2,1)}, u32[]{:S(2)}) copy-start(bf16[4,256,1024]{2,1,0:T(8,128)(2,1)} %x_ref.3) | copy-start | bytes 6291460
  22.7 22.6 %copy-start.25 = (f32[544]{0:T(1024)S(1)}, f32[544]{0:T(1024)}, u32[]{:S(2)}) copy-start(f32[544]{0:T(1024)} %param.28) | copy-start | bytes 6532
  28.6 2.1 collective-permute-start.7
  30.9 14.4 %copy-start.18 = (bf16[4,4,16,640]{3,2,1,0:T(8,128)(2,1)}, bf16[4,4,16,640]{3,2,1,0:T(8,128)(2,1)S(1)}, u32[]{:S(2)}) copy-start(bf16[4,4,16,640]{3,2,1,0:T(8,128)(2,1)S(1)} %get-tuple-element.86.refs_0_.after_ref) | copy-start | bytes 983044
  30.9 9.8 %collective-permute-start.8 = (bf16[4,4,16,640]{3,2,1,0:T(8,128)(2,1)S(1)}, bf16[4,4,16,640]{3,2,1,0:T(8,128)(2,1)S(1)}, u32[]{:S(2)}, u32[]{:S(2)}) collective-permute-start(bf16[4,4,16,640]{3,2,1,0:T(8,128)(2,1)S(1)} %get-tuple-element.87), channel_id=1, source_target_pairs={{0,2},{1,3},{2,0},{3,1},{4,6},{5,7},{6,4},{7,5},{8,10},{9,11},{10,... | collective-permute-start | bytes 983048 | tf_op jit(solution)/shard_map/ppermute | solution.py:28
  40.8 11.7 %collective-permute-start.9 = (bf16[4,16,640]{2,1,0:T(8,128)(2,1)S(1)}, bf16[4,16,640]{2,1,0:T(8,128)(2,1)S(1)}, u32[]{:S(2)}, u32[]{:S(2)}) collective-permute-start(bf16[4,16,640]{2,1,0:T(8,128)(2,1)S(1)} %get-tuple-element.89), channel_id=1, source_target_pairs={{0,4},{1,5},{2,6},{3,7},{4,0},{5,1},{6,2},{7,3},{8,12},{9,13},{10,... | collective-permute-start | bytes 245768 | tf_op jit(solution)/shard_map/ppermute | solution.py:28
  42.5 10.0 %collective-permute-start.10 = (bf16[4,16,640]{2,1,0:T(8,128)(2,1)S(1)}, bf16[4,16,640]{2,1,0:T(8,128)(2,1)S(1)}, u32[]{:S(2)}, u32[]{:S(2)}) collective-permute-start(bf16[4,16,640]{2,1,0:T(8,128)(2,1)S(1)} %get-tuple-element.90), channel_id=1, source_target_pairs={{0,8},{1,9},{2,10},{3,11},{4,12},{5,13},{6,14},{7,15},{8,0},{9,1},... | collective-permute-start | bytes 245768 | tf_op jit(solution)/shard_map/ppermute | solution.py:28
  44.1 8.4 %collective-permute-start.11 = (bf16[4,16,640]{2,1,0:T(8,128)(2,1)S(1)}, bf16[4,16,640]{2,1,0:T(8,128)(2,1)S(1)}, u32[]{:S(2)}, u32[]{:S(2)}) collective-permute-start(bf16[4,16,640]{2,1,0:T(8,128)(2,1)S(1)} %get-tuple-element.91), channel_id=1, source_target_pairs={{0,12},{1,13},{2,14},{3,15},{4,8},{5,9},{6,10},{7,11},{8,4},{9,5},... | collective-permute-start | bytes 245768 | tf_op jit(solution)/shard_map/ppermute | solution.py:28
  52.6 75.7 %collective-permute-start.19 = (bf16[1024,4096]{1,0:T(8,128)(2,1)}, bf16[1024,4096]{1,0:T(8,128)(2,1)}, u32[]{:S(2)}, u32[]{:S(2)}) collective-permute-start(bf16[1024,4096]{1,0:T(8,128)(2,1)} %hold.3), channel_id=1, source_target_pairs={{0,1},{1,0},{2,3},{3,2},{4,5},{5,4},{6,7},{7,6},{8,9},{9,8},{10,11... | collective-permute-start | bytes 25165832 | tf_op jit(solution)/shard_map/ppermute | solution.py:28
  52.7 7.2 %collective-permute-start.14 = (bf16[4,16,640]{2,1,0:T(8,128)(2,1)S(1)}, bf16[4,16,640]{2,1,0:T(8,128)(2,1)S(1)}, u32[]{:S(2)}, u32[]{:S(2)}) collective-permute-start(bf16[4,16,640]{2,1,0:T(8,128)(2,1)S(1)} %norm.1.refs_0_.after_ref), channel_id=1, source_target_pairs={{0,12},{1,13},{2,14},{3,15},{4,8},{5,9},{6,10},{7,11},{8,4},{9,5},... | collective-permute-start | bytes 245768 | tf_op jit(solution)/shard_map/ppermute | solution.py:28
  55.4 7.6 %collective-permute-start.13 = (bf16[4,16,640]{2,1,0:T(8,128)(2,1)S(1)}, bf16[4,16,640]{2,1,0:T(8,128)(2,1)S(1)}, u32[]{:S(2)}, u32[]{:S(2)}) collective-permute-start(bf16[4,16,640]{2,1,0:T(8,128)(2,1)S(1)} %norm.1.refs_0_.after_ref), channel_id=1, source_target_pairs={{0,8},{1,9},{2,10},{3,11},{4,12},{5,13},{6,14},{7,15},{8,0},{9,1},... | collective-permute-start | bytes 245768 | tf_op jit(solution)/shard_map/ppermute | solution.py:28
  55.4 7.6 %collective-permute-start.12 = (bf16[4,16,640]{2,1,0:T(8,128)(2,1)S(1)}, bf16[4,16,640]{2,1,0:T(8,128)(2,1)S(1)}, u32[]{:S(2)}, u32[]{:S(2)}) collective-permute-start(bf16[4,16,640]{2,1,0:T(8,128)(2,1)S(1)} %norm.1.refs_0_.after_ref), channel_id=1, source_target_pairs={{0,4},{1,5},{2,6},{3,7},{4,0},{5,1},{6,2},{7,3},{8,12},{9,13},{10,... | collective-permute-start | bytes 245768 | tf_op jit(solution)/shard_map/ppermute | solution.py:28
  63.0 5.0 %copy-start.26 = (s32[16]{0:T(128)S(1)}, s32[16]{0:T(128)}, u32[]{:S(2)}) copy-start(s32[16]{0:T(128)} %param.21) | copy-start | bytes 196
  63.0 33.1 %copy-start.3 = (bf16[512,1024]{1,0:T(8,128)(2,1)S(1)}, bf16[512,1024]{1,0:T(8,128)(2,1)}, u32[]{:S(2)}) copy-start(bf16[512,1024]{1,0:T(8,128)(2,1)} %refs_4_.14) | copy-start | bytes 3145732
  63.0 33.1 %copy-start.21 = (f32[1024]{0:T(1024)S(1)}, f32[1024]{0:T(1024)}, u32[]{:S(2)}) copy-start(f32[1024]{0:T(1024)} %param.30) | copy-start | bytes 12292
  63.1 33.7 %copy-start.2 = (bf16[4,256,1024]{2,1,0:T(8,128)(2,1)S(1)}, bf16[4,256,1024]{2,1,0:T(8,128)(2,1)}, u32[]{:S(2)}) copy-start(bf16[4,256,1024]{2,1,0:T(8,128)(2,1)} %refs_4_.15) | copy-start | bytes 6291460
  63.1 33.7 %copy-start.17 = (f32[16,1024]{1,0:T(8,128)S(1)}, f32[16,1024]{1,0:T(8,128)}, u32[]{:S(2)}) copy-start(f32[16,1024]{1,0:T(8,128)} %refs_5_.9) | copy-start | bytes 196612
  63.1 33.7 %copy-start.22 = (f32[1024]{0:T(1024)S(1)}, f32[1024]{0:T(1024)}, u32[]{:S(2)}) copy-start(f32[1024]{0:T(1024)} %param.32) | copy-start | bytes 12292
  63.1 54.8 %all-to-all-start = ((bf16[16,64,1024]{2,1,0:T(8,128)(2,1)}), bf16[16,64,1024]{2,1,0:T(8,128)(2,1)}, u32[]{:S(2)}, u32[]{:S(2)}) async-start(bf16[16,64,1024]{2,1,0:T(8,128)(2,1)} %hold.2.after_ref.refs_0_), calls=%async_computation | async-start | bytes 4194304 | tf_op jit(solution)/shard_map/all_to_all | solution.py:723
  68.2 26.3 %collective-permute-start.15 = (bf16[4,4,16,640]{3,2,1,0:T(8,128)(2,1)S(1)}, bf16[4,4,16,640]{3,2,1,0:T(8,128)(2,1)S(1)}, u32[]{:S(2)}, u32[]{:S(2)}) collective-permute-start(bf16[4,4,16,640]{3,2,1,0:T(8,128)(2,1)S(1)} %merge_z.1.after_ref.refs_0_), channel_id=1, source_target_pairs={{0,2},{1,3},{2,0},{3,1},{4,6},{5,7},{6,4},{7,5},{8,10},{9,11},{10,... | collective-permute-start | bytes 983048 | tf_op jit(solution)/shard_map/ppermute | solution.py:28
  70.8 23.8 %collective-permute-start.16 = (bf16[4,4,16,640]{3,2,1,0:T(8,128)(2,1)S(1)}, bf16[4,4,16,640]{3,2,1,0:T(8,128)(2,1)S(1)}, u32[]{:S(2)}, u32[]{:S(2)}) collective-permute-start(bf16[4,4,16,640]{3,2,1,0:T(8,128)(2,1)S(1)} %merge_z.1.after_ref.refs_0_), channel_id=1, source_target_pairs={{0,1},{1,0},{2,3},{3,2},{4,5},{5,4},{6,7},{7,6},{8,9},{9,8},{10,11... | collective-permute-start | bytes 983048 | tf_op jit(solution)/shard_map/ppermute | solution.py:28
  94.5 18.8 %copy-start.4 = (bf16[4,4,16,640]{3,2,1,0:T(8,128)(2,1)}, bf16[4,4,16,640]{3,2,1,0:T(8,128)(2,1)S(1)}, u32[]{:S(2)}) copy-start(bf16[4,4,16,640]{3,2,1,0:T(8,128)(2,1)S(1)} %collective-permute-done.15.refs_1_) | copy-start | bytes 983044
  94.5 1.6 collective-permute-start.17
  94.6 18.7 %copy-start.6 = (bf16[4,4,16,640]{3,2,1,0:T(8,128)(2,1)}, bf16[4,4,16,640]{3,2,1,0:T(8,128)(2,1)S(1)}, u32[]{:S(2)}) copy-start(bf16[4,4,16,640]{3,2,1,0:T(8,128)(2,1)S(1)} %collective-permute-done.16.refs_2_) | copy-start | bytes 983044
  96.2 17.2 %copy-start.8 = (bf16[4,4,16,640]{3,2,1,0:T(8,128)(2,1)}, bf16[4,4,16,640]{3,2,1,0:T(8,128)(2,1)S(1)}, u32[]{:S(2)}) copy-start(bf16[4,4,16,640]{3,2,1,0:T(8,128)(2,1)S(1)} %collective-permute-done.17.refs_3_) | copy-start | bytes 983044
  96.8 16.5 %copy-start.1 = (f32[4,256,1024]{2,1,0:T(8,128)S(1)}, f32[4,256,1024]{2,1,0:T(8,128)}, u32[]{:S(2)}) copy-start(f32[4,256,1024]{2,1,0:T(8,128)} %copy-done) | copy-start | bytes 12582916
  120.4 6.2 %copy-start.5 = (bf16[4,4,16,640]{3,2,1,0:T(8,128)(2,1)S(1)}, bf16[4,4,16,640]{3,2,1,0:T(8,128)(2,1)}, u32[]{:S(2)}) copy-start(bf16[4,4,16,640]{3,2,1,0:T(8,128)(2,1)} %copy-done.4) | copy-start | bytes 983044
  120.4 6.2 %copy-start.7 = (bf16[4,4,16,640]{3,2,1,0:T(8,128)(2,1)S(1)}, bf16[4,4,16,640]{3,2,1,0:T(8,128)(2,1)}, u32[]{:S(2)}) copy-start(bf16[4,4,16,640]{3,2,1,0:T(8,128)(2,1)} %copy-done.6) | copy-start | bytes 983044
  120.4 6.2 %copy-start.9 = (bf16[4,4,16,640]{3,2,1,0:T(8,128)(2,1)S(1)}, bf16[4,4,16,640]{3,2,1,0:T(8,128)(2,1)}, u32[]{:S(2)}) copy-start(bf16[4,4,16,640]{3,2,1,0:T(8,128)(2,1)} %copy-done.8) | copy-start | bytes 983044
  126.3 2.0 collective-permute-start.18
  136.9 25.3 %collective-permute-start.21 = (bf16[128,4096]{1,0:T(8,128)(2,1)S(1)}, bf16[128,4096]{1,0:T(8,128)(2,1)S(1)}, u32[]{:S(2)}, u32[]{:S(2)}) collective-permute-start(bf16[128,4096]{1,0:T(8,128)(2,1)S(1)} %get-tuple-element.103), channel_id=1, source_target_pairs={{0,2},{1,3},{2,0},{3,1},{4,6},{5,7},{6,4},{7,5},{8,10},{9,11},{10,... | collective-permute-start | bytes 3145736 | tf_op jit(solution)/shard_map/ppermute | solution.py:28
  148.6 2.0 collective-permute-start.20
  159.2 26.3 %collective-permute-start.24 = (bf16[128,4096]{1,0:T(8,128)(2,1)S(1)}, bf16[128,4096]{1,0:T(8,128)(2,1)S(1)}, u32[]{:S(2)}, u32[]{:S(2)}) collective-permute-start(bf16[128,4096]{1,0:T(8,128)(2,1)S(1)} %get-tuple-element.112), channel_id=1, source_target_pairs={{0,2},{1,3},{2,0},{3,1},{4,6},{5,7},{6,4},{7,5},{8,10},{9,11},{10,... | collective-permute-start | bytes 3145736 | tf_op jit(solution)/shard_map/ppermute | solution.py:28
  162.4 13.2 %collective-permute-start.23 = (bf16[2,32,4096]{2,1,0:T(8,128)(2,1)S(1)}, bf16[2,32,4096]{2,1,0:T(8,128)(2,1)S(1)}, u32[]{:S(2)}, u32[]{:S(2)}) collective-permute-start(bf16[2,32,4096]{2,1,0:T(8,128)(2,1)S(1)} %get-tuple-element.109), channel_id=1, source_target_pairs={{0,4},{1,5},{2,6},{3,7},{4,0},{5,1},{6,2},{7,3},{8,12},{9,13},{10,... | collective-permute-start | bytes 1572872 | tf_op jit(solution)/shard_map/ppermute | solution.py:28
  174.2 2.0 collective-permute-start.22
  184.7 27.3 %collective-permute-start.29 = (bf16[128,4096]{1,0:T(8,128)(2,1)S(1)}, bf16[128,4096]{1,0:T(8,128)(2,1)S(1)}, u32[]{:S(2)}, u32[]{:S(2)}) collective-permute-start(bf16[128,4096]{1,0:T(8,128)(2,1)S(1)} %get-tuple-element.123), channel_id=1, source_target_pairs={{0,2},{1,3},{2,0},{3,1},{4,6},{5,7},{6,4},{7,5},{8,10},{9,11},{10,... | collective-permute-start | bytes 3145736 | tf_op jit(solution)/shard_map/ppermute | solution.py:28
  185.8 13.8 %collective-permute-start.26 = (bf16[2,32,4096]{2,1,0:T(8,128)(2,1)S(1)}, bf16[2,32,4096]{2,1,0:T(8,128)(2,1)S(1)}, u32[]{:S(2)}, u32[]{:S(2)}) collective-permute-start(bf16[2,32,4096]{2,1,0:T(8,128)(2,1)S(1)} %get-tuple-element.116), channel_id=1, source_target_pairs={{0,4},{1,5},{2,6},{3,7},{4,0},{5,1},{6,2},{7,3},{8,12},{9,13},{10,... | collective-permute-start | bytes 1572872 | tf_op jit(solution)/shard_map/ppermute | solution.py:28
  196.6 3.0 %collective-permute-start.25 = (bf16[256,1024]{1,0:T(8,128)(2,1)S(1)}, bf16[256,1024]{1,0:T(8,128)(2,1)S(1)}, u32[]{:S(2)}, u32[]{:S(2)}) collective-permute-start(bf16[256,1024]{1,0:T(8,128)(2,1)S(1)} %fix.7.after_ref.own_ref), channel_id=1, source_target_pairs={{0,1},{1,0},{2,3},{3,2},{4,5},{5,4},{6,7},{7,6},{8,9},{9,8},{10,11... | collective-permute-start | bytes 1572872 | tf_op jit(solution)/shard_map/ppermute | solution.py:28
  196.7 15.2 %collective-permute-start.27 = (bf16[1,32,4096]{2,1,0:T(8,128)(2,1)S(1)}, bf16[1,32,4096]{2,1,0:T(8,128)(2,1)S(1)}, u32[]{:S(2)}, u32[]{:S(2)}) collective-permute-start(bf16[1,32,4096]{2,1,0:T(8,128)(2,1)S(1)} %get-tuple-element.120), channel_id=1, source_target_pairs={{0,8},{1,9},{2,10},{3,11},{4,12},{5,13},{6,14},{7,15},{8,0},{9,1},... | collective-permute-start | bytes 786440 | tf_op jit(solution)/shard_map/ppermute | solution.py:28
  204.5 17.5 %collective-permute-start.30 = (bf16[128,2048]{1,0:T(8,128)(2,1)S(1)}, bf16[128,2048]{1,0:T(8,128)(2,1)S(1)}, u32[]{:S(2)}, u32[]{:S(2)}) collective-permute-start(bf16[128,2048]{1,0:T(8,128)(2,1)S(1)} %get-tuple-element.125), channel_id=1, source_target_pairs={{0,2},{1,3},{2,0},{3,1},{4,6},{5,7},{6,4},{7,5},{8,10},{9,11},{10,... | collective-permute-start | bytes 1572872 | tf_op jit(solution)/shard_map/ppermute | solution.py:28
  212.3 20.5 %collective-permute-start.31 = (bf16[2,32,4096]{2,1,0:T(8,128)(2,1)S(1)}, bf16[2,32,4096]{2,1,0:T(8,128)(2,1)S(1)}, u32[]{:S(2)}, u32[]{:S(2)}) collective-permute-start(bf16[2,32,4096]{2,1,0:T(8,128)(2,1)S(1)} %get-tuple-element.127), channel_id=1, source_target_pairs={{0,4},{1,5},{2,6},{3,7},{4,0},{5,1},{6,2},{7,3},{8,12},{9,13},{10,... | collective-permute-start | bytes 1572872 | tf_op jit(solution)/shard_map/ppermute | solution.py:28
  213.1 19.8 %collective-permute-start.32 = (bf16[128,2048]{1,0:T(8,128)(2,1)S(1)}, bf16[128,2048]{1,0:T(8,128)(2,1)S(1)}, u32[]{:S(2)}, u32[]{:S(2)}) collective-permute-start(bf16[128,2048]{1,0:T(8,128)(2,1)S(1)} %get-tuple-element.129), channel_id=1, source_target_pairs={{0,2},{1,3},{2,0},{3,1},{4,6},{5,7},{6,4},{7,5},{8,10},{9,11},{10,... | collective-permute-start | bytes 1572872 | tf_op jit(solution)/shard_map/ppermute | solution.py:28
  214.2 22.6 %collective-permute-start.33 = (bf16[1,32,4096]{2,1,0:T(8,128)(2,1)S(1)}, bf16[1,32,4096]{2,1,0:T(8,128)(2,1)S(1)}, u32[]{:S(2)}, u32[]{:S(2)}) collective-permute-start(bf16[1,32,4096]{2,1,0:T(8,128)(2,1)S(1)} %get-tuple-element.131), channel_id=1, source_target_pairs={{0,8},{1,9},{2,10},{3,11},{4,12},{5,13},{6,14},{7,15},{8,0},{9,1},... | collective-permute-start | bytes 786440 | tf_op jit(solution)/shard_map/ppermute | solution.py:28
  222.1 23.3 %collective-permute-start.35 = (bf16[2,32,2048]{2,1,0:T(8,128)(2,1)S(1)}, bf16[2,32,2048]{2,1,0:T(8,128)(2,1)S(1)}, u32[]{:S(2)}, u32[]{:S(2)}) collective-permute-start(bf16[2,32,2048]{2,1,0:T(8,128)(2,1)S(1)} %get-tuple-element.134), channel_id=1, source_target_pairs={{0,4},{1,5},{2,6},{3,7},{4,0},{5,1},{6,2},{7,3},{8,12},{9,13},{10,... | collective-permute-start | bytes 786440 | tf_op jit(solution)/shard_map/ppermute | solution.py:28
  233.0 16.6 %collective-permute-start.36 = (bf16[2,32,2048]{2,1,0:T(8,128)(2,1)S(1)}, bf16[2,32,2048]{2,1,0:T(8,128)(2,1)S(1)}, u32[]{:S(2)}, u32[]{:S(2)}) collective-permute-start(bf16[2,32,2048]{2,1,0:T(8,128)(2,1)S(1)} %get-tuple-element.136), channel_id=1, source_target_pairs={{0,4},{1,5},{2,6},{3,7},{4,0},{5,1},{6,2},{7,3},{8,12},{9,13},{10,... | collective-permute-start | bytes 786440 | tf_op jit(solution)/shard_map/ppermute | solution.py:28
  234.6 15.8 %collective-permute-start.37 = (bf16[1,32,4096]{2,1,0:T(8,128)(2,1)S(1)}, bf16[1,32,4096]{2,1,0:T(8,128)(2,1)S(1)}, u32[]{:S(2)}, u32[]{:S(2)}) collective-permute-start(bf16[1,32,4096]{2,1,0:T(8,128)(2,1)S(1)} %get-tuple-element.138), channel_id=1, source_target_pairs={{0,8},{1,9},{2,10},{3,11},{4,12},{5,13},{6,14},{7,15},{8,0},{9,1},... | collective-permute-start | bytes 786440 | tf_op jit(solution)/shard_map/ppermute | solution.py:28
  245.5 12.7 %collective-permute-start.39 = (bf16[1,32,2048]{2,1,0:T(8,128)(2,1)S(1)}, bf16[1,32,2048]{2,1,0:T(8,128)(2,1)S(1)}, u32[]{:S(2)}, u32[]{:S(2)}) collective-permute-start(bf16[1,32,2048]{2,1,0:T(8,128)(2,1)S(1)} %get-tuple-element.141), channel_id=1, source_target_pairs={{0,8},{1,9},{2,10},{3,11},{4,12},{5,13},{6,14},{7,15},{8,0},{9,1},... | collective-permute-start | bytes 393224 | tf_op jit(solution)/shard_map/ppermute | solution.py:28
  249.8 10.0 %collective-permute-start.41 = (bf16[1,32,2048]{2,1,0:T(8,128)(2,1)S(1)}, bf16[1,32,2048]{2,1,0:T(8,128)(2,1)S(1)}, u32[]{:S(2)}, u32[]{:S(2)}) collective-permute-start(bf16[1,32,2048]{2,1,0:T(8,128)(2,1)S(1)} %get-tuple-element.144), channel_id=1, source_target_pairs={{0,8},{1,9},{2,10},{3,11},{4,12},{5,13},{6,14},{7,15},{8,0},{9,1},... | collective-permute-start | bytes 393224 | tf_op jit(solution)/shard_map/ppermute | solution.py:28
  249.8 10.0 %collective-permute-start.28 = (bf16[16,4096]{1,0:T(8,128)(2,1)S(1)}, bf16[16,4096]{1,0:T(8,128)(2,1)S(1)}, u32[]{:S(2)}, u32[]{:S(2)}) collective-permute-start(bf16[16,4096]{1,0:T(8,128)(2,1)S(1)} %get-tuple-element.122), channel_id=1, source_target_pairs={{0,1},{1,0},{2,3},{3,2},{4,5},{5,4},{6,7},{7,6},{8,9},{9,8},{10,11... | collective-permute-start | bytes 393224 | tf_op jit(solution)/shard_map/ppermute | solution.py:28
  249.9 9.9 %collective-permute-start.34 = (bf16[16,4096]{1,0:T(8,128)(2,1)S(1)}, bf16[16,4096]{1,0:T(8,128)(2,1)S(1)}, u32[]{:S(2)}, u32[]{:S(2)}) collective-permute-start(bf16[16,4096]{1,0:T(8,128)(2,1)S(1)} %get-tuple-element.133), channel_id=1, source_target_pairs={{0,1},{1,0},{2,3},{3,2},{4,5},{5,4},{6,7},{7,6},{8,9},{9,8},{10,11... | collective-permute-start | bytes 393224 | tf_op jit(solution)/shard_map/ppermute | solution.py:28
  250.5 9.4 %collective-permute-start.38 = (bf16[16,4096]{1,0:T(8,128)(2,1)S(1)}, bf16[16,4096]{1,0:T(8,128)(2,1)S(1)}, u32[]{:S(2)}, u32[]{:S(2)}) collective-permute-start(bf16[16,4096]{1,0:T(8,128)(2,1)S(1)} %get-tuple-element.140), channel_id=1, source_target_pairs={{0,1},{1,0},{2,3},{3,2},{4,5},{5,4},{6,7},{7,6},{8,9},{9,8},{10,11... | collective-permute-start | bytes 393224 | tf_op jit(solution)/shard_map/ppermute | solution.py:28
  258.3 1.6 collective-permute-start.40
  259.8 1.3 collective-permute-start.42
  (7 other events, 9.9 us)
